TPU v7x, 32 devices: a whole 2x2x4 slice. The times are simulated.
32 devices in a mesh: gz: 8 (over z, y), gy: 4 (over x, core).
Axes of the slice: x: 2, y: 2, z: 4, core: 2. Of those that a mesh axis runs over, the one named last changes fastest.
Arguments:
- level_input: bfloat16 [8, 32, 64, 128], P('gz', 'gy'), may hold values from -6 to 6
- pre_activation: bfloat16 [8, 32, 64, 128], P('gz', 'gy'), may hold values from -6 to 6
- conv_weight: bfloat16 [3, 3, 3, 128, 128], replicated, may hold values from -0.109375 to 0.109375
- down_weight: bfloat16 [2, 2, 2, 128, 256], replicated, may hold values from -0.1875 to 0.1875
- skip_cotangent: bfloat16 [8, 32, 64, 128], P('gz', 'gy'), may hold values from -12 to 12
- deep_cotangent: bfloat16 [4, 16, 32, 256], P(None, 'gy', None, 'gz'), may hold values from -12 to 12
Outputs:
- input_grad: bfloat16 [8, 32, 64, 128], P('gz', 'gy')
- conv_weight_grad: bfloat16 [3, 3, 3, 128, 128], replicated
- down_weight_grad: bfloat16 [2, 2, 2, 128, 256], replicated
All inputs are finite; a program needn't handle non-finite values.
Results may differ from a plain program's by a relative error of at most 0.0054.
Values may be sent and summed in bfloat16 or wider, within the bound.
No kernel may reach another device: no remote copies, remote signals or barrier semaphores. Data moves between devices by JAX's collectives and lax.ppermute only.
A program may use at most 64 MiB of HBM per device.

v0:
```python
import math

import jax
import jax.numpy as jnp
from jax import lax
from jax.sharding import PartitionSpec as P


def swapped(array, axis, bit):
    return lax.ppermute(array, axis, [(i, i ^ 1 << bit) for i in range(lax.axis_size(axis))])


def extended(cells, sides, width):
    for axis, dim in sides:
        count = lax.axis_size(axis)
        ends = count - 1
        head = lax.slice_in_dim(cells, 0, width, axis=dim)
        tail = lax.slice_in_dim(cells, cells.shape[dim] - width, cells.shape[dim], axis=dim)
        cells = jnp.concatenate(
            [
                lax.ppermute(tail, axis, [(i, (i + 1) % count) for i in range(ends)]),
                cells,
                lax.ppermute(head, axis, [((i + 1) % count, i) for i in range(ends)]),
            ],
            axis=dim,
        )
    return cells


def per_device(
    level_input, pre_activation, conv_weight, down_weight, skip_cotangent, deep_cotangent
):
    row_count = level_input.shape[1]
    col_count = level_input.shape[2]
    channels = level_input.shape[3]
    plane_count = deep_cotangent.shape[0]
    deep_rows = deep_cotangent.shape[1]
    deep_cols = deep_cotangent.shape[2]
    deep_share = deep_cotangent.shape[3]
    parity = lax.axis_index("gz") % 2
    halved = deep_cotangent.reshape(2 * plane_count, deep_rows // 2, deep_cols, deep_share)
    own_half = lax.all_to_all(halved, "gz", split_axis=0, concat_axis=3, tiled=True)[0]
    pair_half = swapped(own_half, "gz", 0)
    even_plane = parity == 0
    top_half = jnp.where(even_plane, own_half, pair_half)
    low_half = jnp.where(even_plane, pair_half, own_half)
    deep_grad = jnp.concatenate([top_half, low_half], axis=0)
    down_slice = lax.dynamic_index_in_dim(down_weight, parity, 0, keepdims=False)
    down_part = jnp.einsum(
        "yxo,bcio->ybxci", deep_grad, down_slice, preferred_element_type=jnp.float32
    )
    down_part = down_part.reshape(row_count, col_count, channels)
    hidden_grad = down_part + skip_cotangent[0].astype(jnp.float32)
    pre_plane = pre_activation[0]
    masked_grad = jnp.where(pre_plane > 0, hidden_grad, jnp.zeros_like(hidden_grad)).astype(
        jnp.bfloat16
    )
    hidden = jnp.maximum(pre_plane, jnp.zeros_like(pre_plane))
    hidden_blocks = hidden.reshape(row_count // 2, 2, col_count // 2, 2, channels)
    down_local = jnp.einsum(
        "ybxci,yxo->bcio", hidden_blocks, deep_grad, preferred_element_type=jnp.float32
    )
    slot_mask = (jnp.arange(2) == parity).astype(jnp.float32)
    down_terms = slot_mask[:, None, None, None, None] * down_local[None]
    grad_padded = extended(masked_grad[None], (("gz", 0), ("gy", 1)), 1)
    grad_padded = jnp.pad(grad_padded, ((0, 0), (0, 0), (1, 1), (0, 0)))
    input_padded = extended(level_input, (("gz", 0), ("gy", 1)), 1)
    input_padded = jnp.pad(input_padded, ((0, 0), (0, 0), (1, 1), (0, 0)))
    cell_count = row_count * col_count
    grad_flat = masked_grad.reshape(cell_count, channels)
    input_total = jnp.zeros((cell_count, channels), jnp.float32)
    conv_terms = []
    for kernel_z in range(3):
        grad_patches = jnp.concatenate(
            [
                grad_padded[
                    2 - kernel_z,
                    2 - kernel_y : 2 - kernel_y + row_count,
                    2 - kernel_x : 2 - kernel_x + col_count,
                    :,
                ]
                for kernel_y in range(3)
                for kernel_x in range(3)
            ],
            axis=-1,
        )
        grad_patches = grad_patches.reshape(cell_count, 9 * channels)
        conv_matrix = jnp.swapaxes(conv_weight[kernel_z], 2, 3).reshape(9 * channels, channels)
        input_total = input_total + jnp.dot(
            grad_patches, conv_matrix, preferred_element_type=jnp.float32
        )
        input_patches = jnp.concatenate(
            [
                input_padded[
                    kernel_z, kernel_y : kernel_y + row_count, kernel_x : kernel_x + col_count, :
                ]
                for kernel_y in range(3)
                for kernel_x in range(3)
            ],
            axis=-1,
        )
        input_patches = input_patches.reshape(cell_count, 9 * channels)
        slab_grad = lax.dot_general(
            input_patches, grad_flat, (((0,), (0,)), ((), ())), preferred_element_type=jnp.float32
        )
        slab_grad = slab_grad.reshape(3, 3, channels, channels)
        conv_terms.append(slab_grad)
    conv_local = jnp.stack(conv_terms)
    cell_total = lax.axis_size("gz") * lax.axis_size("gy") * cell_count
    conv_scale = math.sqrt(cell_total)
    down_scale = math.sqrt(cell_total // 8)
    conv_total, down_total = lax.psum((conv_local, down_terms), ("gz", "gy"))
    conv_weight_grad = (conv_total / conv_scale).astype(jnp.bfloat16)
    down_weight_grad = (down_total / down_scale).astype(jnp.bfloat16)
    input_grad = input_total.reshape(1, row_count, col_count, channels).astype(jnp.bfloat16)
    return (input_grad, conv_weight_grad, down_weight_grad)


def solution(mesh):
    return jax.shard_map(
        per_device,
        mesh=mesh,
        in_specs=(
            P("gz", "gy", None, None),
            P("gz", "gy", None, None),
            P(),
            P(),
            P("gz", "gy", None, None),
            P(None, "gy", None, "gz"),
        ),
        out_specs=(P("gz", "gy", None, None), P(), P()),
        check_vma=False,
    )
```

profile of v0, /device:TPU:0, one launch (start us, length us, event | category | flops | bytes accessed | tf_op | source)
XLA Modules:
  0.0 245.7 jit_solution(16545257537580352954)
XLA Ops:
  7.2 5.0 %collective-permute-start.5 = (bf16[1,8,64,128]{3,2,1,0:T(8,128)(2,1)}, bf16[1,8,64,128]{3,2,1,0:T(8,128)(2,1)S(1)}, u32[]{:S(2)}, u32[]{:S(2)}) collective-permute-start(bf16[1,8,64,128]{3,2,1,0:T(8,128)(2,1)} %param.6), channel_id=1, source_target_pairs={{0,4},{4,8},{8,12},{12,16},{16,20},{20,24},{24,28},{1,5},{5,9},{9,... | collective-permute-start | bytes 393224 | tf_op jit(solution)/shard_map/ppermute | solution.py:21
  12.2 1.3 collective-permute-start.6
  13.5 1.7 reshape.201
  15.2 7.0 %all-to-all-start = ((bf16[8,2,1024]{2,1,0:T(2,128)(2,1)}), bf16[8,2,1024]{2,1,0:T(2,128)(2,1)S(1)}, u32[]{:S(2)}, u32[]{:S(2)}) async-start(bf16[8,2,1024]{2,1,0:T(2,128)(2,1)} %reshape.201), calls=%async_computation | async-start | bytes 65536 | tf_op jit(solution)/shard_map/all_to_all | solution.py:42
  22.2 1.2 fusion.13
  23.5 5.4 %all-to-all-done = bf16[8,2,1024]{2,1,0:T(2,128)(2,1)S(1)} async-done(((bf16[8,2,1024]{2,1,0:T(2,128)(2,1)}), bf16[8,2,1024]{2,1,0:T(2,128)(2,1)S(1)}, u32[]{:S(2)}, u32[]{:S(2)}) %all-to-all-start) | async-done | bytes 32800 | tf_op jit(solution)/shard_map/all_to_all | solution.py:42
  29.2 0.5 collective-permute-start
  29.8 0.9 copy.108
  30.6 0.9 copy.109
  31.5 0.9 copy.110
  32.4 0.8 copy.89
  33.8 1.3 collective-permute-start.2
  35.1 4.6 %collective-permute-start.1 = (bf16[1,8,64,128]{3,2,1,0:T(8,128)(2,1)S(1)}, bf16[1,8,64,128]{3,2,1,0:T(8,128)(2,1)S(1)}, u32[]{:S(2)}, u32[]{:S(2)}) collective-permute-start(bf16[1,8,64,128]{3,2,1,0:T(8,128)(2,1)S(1)} %select_convert_fusion), channel_id=1, source_target_pairs={{0,4},{4,8},{8,12},{12,16},{16,20},{20,24},{24,28},{1,5},{5,9},{9,... | collective-permute-start | bytes 393224 | tf_op jit(solution)/shard_map/ppermute | solution.py:21
  40.0 1.3 collective-permute-start.8
  41.3 3.0 %collective-permute-start.7 = (bf16[3,1,64,128]{3,2,1,0:T(8,128)(2,1)S(1)}, bf16[3,1,64,128]{3,2,1,0:T(8,128)(2,1)S(1)}, u32[]{:S(2)}, u32[]{:S(2)}) collective-permute-start(bf16[3,1,64,128]{3,2,1,0:T(8,128)(2,1)S(1)} %get-tuple-element.59), channel_id=1, source_target_pairs={{0,1},{1,2},{2,3},{4,5},{5,6},{6,7},{8,9},{9,10},{10,11},{12,13},{... | collective-permute-start | bytes 147464 | tf_op jit(solution)/shard_map/ppermute | solution.py:21
  44.4 1.1 broadcast_multiply_fusion
  45.5 0.8 copy.98
  46.3 0.8 copy.80
  47.0 0.6 copy-done.24
  47.9 1.2 fusion.14
  49.1 0.8 copy.94
  49.8 0.9 constant_dynamic-update-slice_fusion.56
  50.8 1.7 pad_maximum_fusion.5
  52.4 1.7 copy.95
  54.1 1.7 copy.96
  55.8 1.7 copy.97
  57.5 1.7 copy.99
  59.1 1.7 copy.100
  60.8 1.7 copy.101
  62.5 0.8 copy.102
  63.4 0.7 constant_dynamic-update-slice_fusion.47
  64.0 1.7 copy.86
  65.7 0.8 copy.87
  66.5 0.8 copy.88
  67.3 0.8 copy.90
  68.0 0.8 copy.91
  68.8 1.0 copy.92
  70.0 0.9 constant_dynamic-update-slice_fusion.55
  70.9 0.9 constant_dynamic-update-slice_fusion.54
  71.8 0.9 constant_dynamic-update-slice_fusion.53
  72.8 0.9 constant_dynamic-update-slice_fusion.51
  73.7 0.9 constant_dynamic-update-slice_fusion.50
  75.2 0.7 copy-done.1
  76.6 0.8 copy.76
  77.4 0.9 constant_dynamic-update-slice_fusion.38
  78.3 1.7 copy.77
  79.9 1.7 copy.78
  81.6 1.7 copy.79
  83.3 1.7 copy.81
  85.0 0.8 copy.82
  85.7 1.7 copy.83
  87.4 0.8 copy.84
  88.2 1.0 constant_dynamic-update-slice_fusion.37
  89.2 0.9 constant_dynamic-update-slice_fusion.36
  90.1 0.9 constant_dynamic-update-slice_fusion.35
  91.0 0.9 constant_dynamic-update-slice_fusion.33
  92.6 1.3 collective-permute-start.4
  93.9 3.6 %collective-permute-start.3 = (bf16[3,1,64,128]{3,2,1,0:T(8,128)(2,1)S(1)}, bf16[3,1,64,128]{3,2,1,0:T(8,128)(2,1)S(1)}, u32[]{:S(2)}, u32[]{:S(2)}) collective-permute-start(bf16[3,1,64,128]{3,2,1,0:T(8,128)(2,1)S(1)} %get-tuple-element.61), channel_id=1, source_target_pairs={{0,1},{1,2},{2,3},{4,5},{5,6},{6,7},{8,9},{9,10},{10,11},{12,13},{... | collective-permute-start | bytes 147464 | tf_op jit(solution)/shard_map/ppermute | solution.py:21
  97.5 1.4 pad_maximum_fusion
  100.9 0.6 copy-done.4
  102.9 1.1 fusion
  104.0 131.3 %all-reduce.5.cloned.1.call-done = (f32[3,3,3,128,128]{4,3,2,1,0:T(8,128)}, f32[2,2,2,128,256]{4,3,2,1,0:T(8,128)}) async-done(((f32[3,3,3,128,128]{4,3,2,1,0:T(8,128)}, f32[2,2,2,128,256]{4,3,2,1,0:T(8,128)}), (f32[3,3,3,128,128]{4,3,2,1,0:T(8,128)}, f32[2,2,2,128,256]{4,3,2,1,0:T(8,128)})) %all-reduce.5.cloned.1.call-update) | async-done | bytes 2818064 | tf_op jit(solution)/shard_map/psum | solution.py:112
  235.3 2.7 %multiply_convert_fusion = bf16[3,3,3,128,128]{4,3,2,1,0:T(8,128)(2,1)} fusion(f32[3,3,3,128,128]{4,3,2,1,0:T(8,128)} %get-tuple-element.3), kind=kLoop, calls=%fused_computation.1 | loop fusion | flops 884736 | bytes 2654208 | tf_op jit(solution)/shard_map/convert_element_type | solution.py:113
  238.0 0.9 multiply_convert_fusion.1
  (129 shorter events, 6.6 us)
Async XLA Ops:
  7.2 26.1 %copy-start = (bf16[2,2,2,128,256]{4,3,2,1,0:T(8,128)(2,1)S(1)}, bf16[2,2,2,128,256]{4,3,2,1,0:T(8,128)(2,1)}, u32[]{:S(2)}) copy-start(bf16[2,2,2,128,256]{4,3,2,1,0:T(8,128)(2,1)} %param.9) | copy-start | bytes 1572868
  7.2 16.2 %copy-start.6 = (bf16[1,8,64,128]{3,2,1,0:T(8,128)(2,1)S(1)}, bf16[1,8,64,128]{3,2,1,0:T(8,128)(2,1)}, u32[]{:S(2)}) copy-start(bf16[1,8,64,128]{3,2,1,0:T(8,128)(2,1)} %param.7) | copy-start | bytes 393220
  7.2 32.7 %collective-permute-start.5 = (bf16[1,8,64,128]{3,2,1,0:T(8,128)(2,1)}, bf16[1,8,64,128]{3,2,1,0:T(8,128)(2,1)S(1)}, u32[]{:S(2)}, u32[]{:S(2)}) collective-permute-start(bf16[1,8,64,128]{3,2,1,0:T(8,128)(2,1)} %param.6), channel_id=1, source_target_pairs={{0,4},{4,8},{8,12},{12,16},{16,20},{20,24},{24,28},{1,5},{5,9},{9,... | collective-permute-start | bytes 393224 | tf_op jit(solution)/shard_map/ppermute | solution.py:21
  12.2 27.8 %collective-permute-start.6 = (bf16[1,8,64,128]{3,2,1,0:T(8,128)(2,1)}, bf16[1,8,64,128]{3,2,1,0:T(8,128)(2,1)S(1)}, u32[]{:S(2)}, u32[]{:S(2)}) collective-permute-start(bf16[1,8,64,128]{3,2,1,0:T(8,128)(2,1)} %param.6), channel_id=1, source_target_pairs={{4,0},{8,4},{12,8},{16,12},{20,16},{24,20},{28,24},{5,1},{9,5},{13... | collective-permute-start | bytes 393224 | tf_op jit(solution)/shard_map/ppermute | solution.py:23
  15.2 13.6 %all-to-all-start = ((bf16[8,2,1024]{2,1,0:T(2,128)(2,1)}), bf16[8,2,1024]{2,1,0:T(2,128)(2,1)S(1)}, u32[]{:S(2)}, u32[]{:S(2)}) async-start(bf16[8,2,1024]{2,1,0:T(2,128)(2,1)} %reshape.201), calls=%async_computation | async-start | bytes 65536 | tf_op jit(solution)/shard_map/all_to_all | solution.py:42
  22.2 213.1 %all-reduce.5.cloned.1.call-start = ((), (), s32[]{:S(2)}) async-start(), calls=%async_computation.1 | async-start | bytes 5636096 | tf_op jit(solution)/shard_map/psum | solution.py:112
  23.4 9.0 %copy-start.10 = (bf16[1,8,64,128]{3,2,1,0:T(8,128)(2,1)S(1)}, bf16[1,8,64,128]{3,2,1,0:T(8,128)(2,1)}, u32[]{:S(2)}) copy-start(bf16[1,8,64,128]{3,2,1,0:T(8,128)(2,1)} %param.6) | copy-start | bytes 393220
  29.2 4.0 %collective-permute-start = (bf16[2,32,256]{2,1,0:T(8,128)(2,1)S(1)}, bf16[2,32,256]{2,1,0:T(8,128)(2,1)S(1)}, u32[]{:S(2)}, u32[]{:S(2)}) collective-permute-start(bf16[2,32,256]{2,1,0:T(8,128)(2,1)S(1)} %squeeze.13), channel_id=1, source_target_pairs={{0,4},{4,0},{8,12},{12,8},{16,20},{20,16},{24,28},{28,24},{1,5},{5... | collective-permute-start | bytes 98312 | tf_op jit(solution)/shard_map/ppermute | solution.py:10
  31.5 2.2 copy-start.25
  33.8 58.7 %collective-permute-start.2 = (bf16[1,8,64,128]{3,2,1,0:T(8,128)(2,1)S(1)}, bf16[1,8,64,128]{3,2,1,0:T(8,128)(2,1)S(1)}, u32[]{:S(2)}, u32[]{:S(2)}) collective-permute-start(bf16[1,8,64,128]{3,2,1,0:T(8,128)(2,1)S(1)} %select_convert_fusion), channel_id=1, source_target_pairs={{4,0},{8,4},{12,8},{16,12},{20,16},{24,20},{28,24},{5,1},{9,5},{13... | collective-permute-start | bytes 393224 | tf_op jit(solution)/shard_map/ppermute | solution.py:23
  35.1 57.4 %collective-permute-start.1 = (bf16[1,8,64,128]{3,2,1,0:T(8,128)(2,1)S(1)}, bf16[1,8,64,128]{3,2,1,0:T(8,128)(2,1)S(1)}, u32[]{:S(2)}, u32[]{:S(2)}) collective-permute-start(bf16[1,8,64,128]{3,2,1,0:T(8,128)(2,1)S(1)} %select_convert_fusion), channel_id=1, source_target_pairs={{0,4},{4,8},{8,12},{12,16},{16,20},{20,24},{24,28},{1,5},{5,9},{9,... | collective-permute-start | bytes 393224 | tf_op jit(solution)/shard_map/ppermute | solution.py:21
  40.0 7.0 %collective-permute-start.8 = (bf16[3,1,64,128]{3,2,1,0:T(8,128)(2,1)S(1)}, bf16[3,1,64,128]{3,2,1,0:T(8,128)(2,1)S(1)}, u32[]{:S(2)}, u32[]{:S(2)}) collective-permute-start(bf16[3,1,64,128]{3,2,1,0:T(8,128)(2,1)S(1)} %get-tuple-element.60), channel_id=1, source_target_pairs={{1,0},{2,1},{3,2},{5,4},{6,5},{7,6},{9,8},{10,9},{11,10},{13,12},{... | collective-permute-start | bytes 147464 | tf_op jit(solution)/shard_map/ppermute | solution.py:23
  41.3 5.7 %collective-permute-start.7 = (bf16[3,1,64,128]{3,2,1,0:T(8,128)(2,1)S(1)}, bf16[3,1,64,128]{3,2,1,0:T(8,128)(2,1)S(1)}, u32[]{:S(2)}, u32[]{:S(2)}) collective-permute-start(bf16[3,1,64,128]{3,2,1,0:T(8,128)(2,1)S(1)} %get-tuple-element.59), channel_id=1, source_target_pairs={{0,1},{1,2},{2,3},{4,5},{5,6},{6,7},{8,9},{9,10},{10,11},{12,13},{... | collective-permute-start | bytes 147464 | tf_op jit(solution)/shard_map/ppermute | solution.py:21
  47.0 0.6 copy-start.24
  52.4 10.0 %copy-start.9 = (bf16[1,8,64,128]{3,2,1,0:T(8,128)(2,1)S(1)}, bf16[1,8,64,128]{3,2,1,0:T(8,128)(2,1)}, u32[]{:S(2)}) copy-start(bf16[1,8,64,128]{3,2,1,0:T(8,128)(2,1)} %get-tuple-element.25) | copy-start | bytes 393220
  52.4 10.8 %copy-start.8 = (bf16[1,8,64,128]{3,2,1,0:T(8,128)(2,1)S(1)}, bf16[1,8,64,128]{3,2,1,0:T(8,128)(2,1)}, u32[]{:S(2)}) copy-start(bf16[1,8,64,128]{3,2,1,0:T(8,128)(2,1)} %get-tuple-element.19) | copy-start | bytes 393220
  54.1 11.6 %copy-start.7 = (bf16[1,8,64,128]{3,2,1,0:T(8,128)(2,1)S(1)}, bf16[1,8,64,128]{3,2,1,0:T(8,128)(2,1)}, u32[]{:S(2)}) copy-start(bf16[1,8,64,128]{3,2,1,0:T(8,128)(2,1)} %get-tuple-element.18) | copy-start | bytes 393220
  65.7 7.0 %copy-start.13 = (bf16[512,128]{0,1:T(8,128)(2,1)S(1)}, bf16[512,128]{0,1:T(8,128)(2,1)}, u32[]{:S(2)}) copy-start(bf16[512,128]{0,1:T(8,128)(2,1)} %copy.98) | copy-start | bytes 393220
  68.0 6.6 %copy-start.20 = (bf16[512,128]{0,1:T(8,128)(2,1)S(1)}, bf16[512,128]{0,1:T(8,128)(2,1)}, u32[]{:S(2)}) copy-start(bf16[512,128]{0,1:T(8,128)(2,1)} %copy.101) | copy-start | bytes 393220
  68.8 5.8 %copy-start.17 = (bf16[512,128]{0,1:T(8,128)(2,1)S(1)}, bf16[512,128]{0,1:T(8,128)(2,1)}, u32[]{:S(2)}) copy-start(bf16[512,128]{0,1:T(8,128)(2,1)} %copy.102) | copy-start | bytes 393220
  74.6 1.3 copy-start.1
  74.6 1.3 copy-start.18
  74.6 1.2 copy-start.19
  74.7 1.3 copy-start.16
  74.7 1.3 copy-start.11
  74.7 1.3 copy-start.15
  74.7 1.4 copy-start.14
  85.7 5.3 %copy-start.12 = (bf16[512,128]{0,1:T(8,128)(2,1)S(1)}, bf16[512,128]{0,1:T(8,128)(2,1)}, u32[]{:S(2)}) copy-start(bf16[512,128]{0,1:T(8,128)(2,1)} %copy.80) | copy-start | bytes 393220
  88.2 3.8 %copy-start.21 = (bf16[512,128]{0,1:T(8,128)(2,1)S(1)}, bf16[512,128]{0,1:T(8,128)(2,1)}, u32[]{:S(2)}) copy-start(bf16[512,128]{0,1:T(8,128)(2,1)} %copy.82) | copy-start | bytes 393220
  88.2 3.8 %copy-start.22 = (bf16[512,128]{0,1:T(8,128)(2,1)S(1)}, bf16[512,128]{0,1:T(8,128)(2,1)}, u32[]{:S(2)}) copy-start(bf16[512,128]{0,1:T(8,128)(2,1)} %copy.83) | copy-start | bytes 393220
  88.2 3.8 %copy-start.23 = (bf16[512,128]{0,1:T(8,128)(2,1)S(1)}, bf16[512,128]{0,1:T(8,128)(2,1)}, u32[]{:S(2)}) copy-start(bf16[512,128]{0,1:T(8,128)(2,1)} %copy.84) | copy-start | bytes 393220
  92.6 6.3 %collective-permute-start.4 = (bf16[3,1,64,128]{3,2,1,0:T(8,128)(2,1)S(1)}, bf16[3,1,64,128]{3,2,1,0:T(8,128)(2,1)S(1)}, u32[]{:S(2)}, u32[]{:S(2)}) collective-permute-start(bf16[3,1,64,128]{3,2,1,0:T(8,128)(2,1)S(1)} %get-tuple-element.62), channel_id=1, source_target_pairs={{1,0},{2,1},{3,2},{5,4},{6,5},{7,6},{9,8},{10,9},{11,10},{13,12},{... | collective-permute-start | bytes 147464 | tf_op jit(solution)/shard_map/ppermute | solution.py:23
  93.9 5.0 %collective-permute-start.3 = (bf16[3,1,64,128]{3,2,1,0:T(8,128)(2,1)S(1)}, bf16[3,1,64,128]{3,2,1,0:T(8,128)(2,1)S(1)}, u32[]{:S(2)}, u32[]{:S(2)}) collective-permute-start(bf16[3,1,64,128]{3,2,1,0:T(8,128)(2,1)S(1)} %get-tuple-element.61), channel_id=1, source_target_pairs={{0,1},{1,2},{2,3},{4,5},{5,6},{6,7},{8,9},{9,10},{10,11},{12,13},{... | collective-permute-start | bytes 147464 | tf_op jit(solution)/shard_map/ppermute | solution.py:21
  100.5 1.0 copy-start.4
  100.8 1.2 copy-start.3
  101.9 1.0 copy-start.2
  235.3 2.7 %copy-start.5 = (f32[2,2,2,128,256]{4,3,2,1,0:T(8,128)S(1)}, f32[2,2,2,128,256]{4,3,2,1,0:T(8,128)}, u32[]{:S(2)}) copy-start(f32[2,2,2,128,256]{4,3,2,1,0:T(8,128)} %get-tuple-element.4) | copy-start | bytes 3145732
Sparse Core Ops, SparseCore 0:
  99.0 136.2 all-reduce.4
where the time goes:
time: 247 us; the launch traced here: 246 us
  waiting for transfers between devices  137 us (55%)
  local copies, waits for them, and re-layouts  52.9 us (21%)
  starting transfers between devices  28.9 us (12%)
  between operations  14.9 us (6%)
  other arithmetic  8.36 us (3%)
  matrix products  3.96 us (2%)
    psum x1, waiting for transfers between devices, per_device(): conv_total, down_total = lax.psum((conv_local, down_terms), ('gz', 'gy'))  131 us
    concatenate x30, local copies, waits for them, and re-layouts, per_device(): jnp.concatenate([input_padded[kernel_z, kernel_y:kernel_y + row_count, ke...  30.7 us
    unnamed x107, local copies, waits for them, and re-layouts  18.8 us
    ppermute x4, starting transfers between devices, extended(): lax.ppermute(tail, axis, [(i, (i + 1) % count) for i in range(ends)])  16.2 us
    all_to_all x1, starting transfers between devices, per_device(): lax.all_to_all(halved, 'gz', split_axis=0, concat_axis=3, tiled=True)[0]  6.96 us
    all_to_all x1, waiting for transfers between devices, per_device(): lax.all_to_all(halved, 'gz', split_axis=0, concat_axis=3, tiled=True)[0]  5.38 us
    ppermute x4, starting transfers between devices, extended(): lax.ppermute(head, axis, [((i + 1) % count, i) for i in range(ends)])  5.17 us
  transfers between devices with their start and end apart: 11, of which 2 were waited for; matrix products, arithmetic and copies ran while one was open for 24% of the time, Pallas kernels for 0%

commit v1 on v0

v1 whole, which is shorter than its diff:
```python
import math

import jax
import jax.numpy as jnp
from jax import lax
from jax.experimental import pallas as pl
from jax.experimental.pallas import tpu as pltpu
from jax.sharding import PartitionSpec as P

F32 = jnp.float32
BF16 = jnp.bfloat16
VMEM_LIMIT = 40 * 1024 * 1024


def call(kernel, out_shape, *operands, scratch=()):
    return pl.pallas_call(
        kernel,
        out_shape=out_shape,
        scratch_shapes=list(scratch),
        compiler_params=pltpu.CompilerParams(vmem_limit_bytes=VMEM_LIMIT),
    )(*operands)


def shifted(cells, step):
    if step == 0:
        return cells
    cols = cells.shape[1]
    moved = pltpu.roll(cells, step % cols, 1)
    col = lax.broadcasted_iota(jnp.int32, cells.shape, 1)
    keep = col >= step if step > 0 else col < cols + step
    return jnp.where(keep, moved, 0.0)


def fill_padded(padded, own, z_low, z_high, y_low, y_high):
    rows = own.shape[0]
    for plane, ref in enumerate((z_low, own, z_high)):
        padded[plane, pl.ds(1, rows)] = ref[...]
        padded[plane, 0] = y_low[plane]
        padded[plane, rows + 1] = y_high[plane]


def mask_kernel(pre, skip, deep_t, weight, grad, down):
    rows, cols, channels = pre.shape
    half = rows // 2
    deep_cols = cols // 2
    cells = half * cols
    deep_cells = half * deep_cols
    wide = lax.broadcasted_iota(jnp.int32, (deep_cells, cells), 1) // 2
    deep = lax.broadcasted_iota(jnp.int32, (deep_cells, cells), 0)
    repeat = (wide == deep).astype(BF16)
    spread = jnp.dot(deep_t[...], repeat, preferred_element_type=F32).astype(BF16)
    col = lax.broadcasted_iota(jnp.int32, (cells, channels), 0) % 2
    for b in range(2):
        parts = [
            lax.dot_general(
                spread, weight[b, c], (((0,), (1,)), ((), ())), preferred_element_type=F32
            )
            for c in range(2)
        ]
        part = jnp.where(col == 0, parts[0], parts[1]).reshape(half, cols, channels)
        for y in range(half):
            row = 2 * y + b
            pre_row = pre[row].astype(F32)
            total = part[y] + skip[row].astype(F32)
            grad[row] = jnp.where(pre_row > 0, total, 0.0).astype(BF16)
        hidden = jnp.concatenate(
            [jnp.maximum(pre[2 * y + b].astype(F32), 0.0) for y in range(half)], axis=0
        )
        for c in range(2):
            one = jnp.where(col == c, hidden, 0.0).astype(BF16)
            down[b, c] = lax.dot_general(
                one, spread, (((0,), (1,)), ((), ())), preferred_element_type=F32
            ).astype(BF16)


def weight_kernel(n_gy, n_gz, conv_rows, down_rows, own, z_low, z_high, y_low, y_high, grad, down, out, padded):
    rows, cols, channels = own.shape
    fill_padded(padded, own, z_low, z_high, y_low, y_high)
    grads = grad[...].astype(F32)
    shifts = jnp.concatenate(
        [shifted(grads, kx - 1).astype(BF16).reshape(rows * cols, channels) for kx in range(3)],
        axis=1,
    )

    def store(base, piece, row, value):
        done = 0
        while done < value.shape[0]:
            owner, inner = divmod(row + done, piece)
            take = min(piece - inner, value.shape[0] - done)
            out[owner // n_gz, owner % n_gz, pl.ds(base + inner, take)] = value[done : done + take]
            done += take

    for kz in range(3):
        for ky in range(3):
            slab = padded[kz, pl.ds(ky, rows)].reshape(rows * cols, channels)
            total = lax.dot_general(
                slab, shifts, (((0,), (0,)), ((), ())), preferred_element_type=F32
            ).astype(BF16)
            for kx in range(3):
                index = (kz * 3 + ky) * 3 + kx
                store(0, conv_rows, index * channels, total[:, kx * channels : (kx + 1) * channels])
    blank = n_gy * n_gz * conv_rows - 27 * channels
    if blank:
        store(0, conv_rows, 27 * channels, jnp.zeros((blank, channels), BF16))
    wide = down.shape[3] // channels
    count = 4 * channels
    for part in range(wide):
        for b in range(2):
            for c in range(2):
                row = part * count + (b * 2 + c) * channels
                store(conv_rows, down_rows, row, down[b, c, :, part * channels : (part + 1) * channels])
    blank = n_gy * n_gz * down_rows - wide * count
    if blank:
        store(conv_rows, down_rows, wide * count, jnp.zeros((blank, channels), BF16))


def input_kernel(own, z_low, z_high, y_low, y_high, weight, out, padded):
    rows, cols, channels = own.shape
    fill_padded(padded, own, z_low, z_high, y_low, y_high)
    total = None
    for kz in range(3):
        for ky in range(3):
            slab = padded[2 - kz, pl.ds(2 - ky, rows)].reshape(rows * cols, channels)
            term = lax.dot_general(
                slab,
                weight[kz, ky].reshape(3 * channels, channels),
                (((1,), (1,)), ((), ())),
                preferred_element_type=F32,
            )
            total = term if total is None else total + term
    answer = None
    for kx in range(3):
        part = total[:, kx * channels : (kx + 1) * channels].reshape(rows, cols, channels)
        part = shifted(part, kx - 1)
        answer = part if answer is None else answer + part
    out[...] = answer.astype(BF16)


def spread_kernel(n_gy, n_gz, conv_rows, down_rows, gathered, conv, down):
    rows, channels = conv.shape
    wide = down.shape[2] // channels
    for owner in range(n_gy * n_gz):
        piece = gathered.at[owner]
        first = owner * conv_rows
        take = min(conv_rows, rows - first)
        if take > 0:
            conv[pl.ds(first, take)] = piece[pl.ds(0, take)]
        first = owner * down_rows
        count = down.shape[1]
        done = 0
        while done < down_rows and first + done < wide * count:
            part, row = divmod(first + done, count)
            take = min(count - row, down_rows - done)
            for a in range(2):
                down[a, pl.ds(row, take), pl.ds(part * channels, channels)] = piece[
                    pl.ds(conv_rows + a * down_rows + done, take)
                ]
            done += take


def sides(cells, gz, gy):
    def moved(value, axis, count, up):
        pairs = [(i, i + 1) if up else (i + 1, i) for i in range(count - 1)]
        return lax.ppermute(value, axis, pairs)

    z_low = moved(cells, "gz", gz, True)
    z_high = moved(cells, "gz", gz, False)
    planes = (z_low, cells, z_high)
    y_low = moved(jnp.stack([plane[-1] for plane in planes]), "gy", gy, True)
    y_high = moved(jnp.stack([plane[0] for plane in planes]), "gy", gy, False)
    return cells, z_low, z_high, y_low, y_high


def per_device(
    level_input, pre_activation, conv_weight, down_weight, skip_cotangent, deep_cotangent
):
    n_gz = lax.axis_size("gz")
    n_gy = lax.axis_size("gy")
    _, rows, cols, channels = level_input.shape
    planes, deep_rows, deep_cols, share = deep_cotangent.shape
    deep_channels = down_weight.shape[4]
    parity = lax.axis_index("gz") % 2
    devices = n_gz * n_gy
    conv_rows = -(-27 * channels // (devices * 16)) * 16
    down_count = 4 * channels * deep_channels // channels
    down_rows = -(-down_count // (devices * 16)) * 16

    deep_t = jnp.swapaxes(deep_cotangent.reshape(planes, deep_rows * deep_cols, share), 1, 2)
    deep_t = jnp.broadcast_to(deep_t[:, None], (planes, 2) + deep_t.shape[1:])
    deep_t = deep_t.reshape(2 * planes, share, deep_rows * deep_cols)
    deep_t = lax.all_to_all(deep_t, "gz", split_axis=0, concat_axis=0, tiled=True)
    deep_t = deep_t.reshape(deep_channels, deep_rows * deep_cols)
    level = sides(level_input[0], n_gz, n_gy)
    down_slice = lax.dynamic_index_in_dim(down_weight, parity, 0, keepdims=False)

    shape = jax.ShapeDtypeStruct
    grad, down = call(
        mask_kernel,
        (
            shape((rows, cols, channels), BF16),
            shape((2, 2, channels, deep_channels), BF16),
        ),
        pre_activation[0],
        skip_cotangent[0],
        deep_t,
        down_slice,
    )

    piece = conv_rows + down_rows
    parts = call(
        lambda *refs: weight_kernel(n_gy, n_gz, conv_rows, down_rows, *refs),
        shape((n_gy, n_gz, piece, channels), BF16),
        *level,
        grad,
        down,
        scratch=[pltpu.VMEM((3, rows + 2, cols, channels), BF16)],
    )
    parts = lax.all_to_all(parts, "gy", split_axis=0, concat_axis=0, tiled=True)
    parts = jnp.sum(parts.astype(F32), axis=0).astype(BF16)
    parts = lax.all_to_all(parts, "gz", split_axis=0, concat_axis=0, tiled=True)
    parts = parts.astype(F32)
    cell_total = devices * rows * cols
    conv_sum = jnp.sum(parts[:, :conv_rows], axis=0) / math.sqrt(cell_total)
    slots = parts[:, conv_rows:].reshape(n_gz // 2, 2, down_rows, channels)
    down_sum = jnp.sum(slots, axis=0) / math.sqrt(cell_total // 8)
    final = jnp.concatenate([conv_sum, down_sum.reshape(2 * down_rows, channels)], axis=0)
    final = final.astype(BF16)
    gathered = lax.all_gather(final, ("gy", "gz"), axis=0, tiled=False)
    conv_grad, down_grad = call(
        lambda *refs: spread_kernel(n_gy, n_gz, conv_rows, down_rows, *refs),
        (
            shape((27 * channels, channels), BF16),
            shape((2, 4 * channels, deep_channels), BF16),
        ),
        gathered,
    )

    halo = sides(grad, n_gz, n_gy)
    input_grad = call(
        input_kernel,
        shape((rows, cols, channels), BF16),
        *halo,
        conv_weight,
        scratch=[pltpu.VMEM((3, rows + 2, cols, channels), BF16)],
    )
    return (
        input_grad[None],
        conv_grad.reshape(conv_weight.shape),
        down_grad.reshape(down_weight.shape),
    )


def solution(mesh):
    return jax.shard_map(
        per_device,
        mesh=mesh,
        in_specs=(
            P("gz", "gy", None, None),
            P("gz", "gy", None, None),
            P(),
            P(),
            P("gz", "gy", None, None),
            P(None, "gy", None, "gz"),
        ),
        out_specs=(P("gz", "gy", None, None), P(), P()),
        check_vma=False,
    )
```

time: 247 us -> 129 us (0.52)
  waiting for transfers between devices: 137 us -> 45.8 us
  local copies, waits for them, and re-layouts: 52.9 us -> 3.82 us
  blocking collectives: 0 us -> 35 us
  other arithmetic: 8.36 us -> 0.95 us
  starting transfers between devices: 28.9 us -> 24.2 us
  Pallas kernels: 0 us -> 4.41 us
  matrix products: 3.96 us -> 0 us
    psum x1 -> x0, waiting for transfers between devices: 131 us -> none  [per_device(): conv_total, down_total = lax.psum((conv_local, down_terms), ('gz', 'gy'))]
    all_gather x0 -> x1, waiting for transfers between devices: none -> 36.8 us  [per_device(): gathered = lax.all_gather(final, ('gy', 'gz'), axis=0, tiled=False)]
    all_to_all x0 -> x2, blocking collectives: none -> 35 us  [the longest x1 19.2 us: per_device(): parts = lax.all_to_all(parts, 'gy', split_axis=0, concat_axis=0, tiled=True)]
    concatenate x34 -> x0, local copies, waits for them, and re-layouts: 30.8 us -> none  [the longest x30 30.7 us: per_device(): jnp.concatenate([input_padded[kernel_z, kernel_y:kernel_y + row_count, ke...]
    unnamed x107 -> x12, local copies, waits for them, and re-layouts: 18.8 us -> 1.39 us
    ppermute x9 -> x8, waiting for transfers between devices: 0.02 us -> 5.63 us  [moved(): return lax.ppermute(value, axis, pairs)]
    pallas_call x0 -> x4, Pallas kernels: none -> 4.41 us  [call(): pl.pallas_call(kernel, out_shape=out_shape, scratch_shapes=list(scratch),...]
    ppermute x9 -> x8, starting transfers between devices: 21.9 us -> 17.9 us  [moved(): return lax.ppermute(value, axis, pairs)]
  transfers between devices with their start and end apart: 11 -> 10, of which waited for: 2 -> 5; matrix products, arithmetic and copies ran while one was open for 24% -> 2% of each run, Pallas kernels for 0% -> 2%
where the time goes in v1:
time: 129 us; the launch traced here: 128 us
  waiting for transfers between devices  45.8 us (36%)
  blocking collectives  35 us (27%)
  starting transfers between devices  24.2 us (19%)
  between operations  14.3 us (11%)
  Pallas kernels  4.41 us (3%)
  local copies, waits for them, and re-layouts  3.82 us (3%)
    all_gather x1, waiting for transfers between devices, per_device(): gathered = lax.all_gather(final, ('gy', 'gz'), axis=0, tiled=False)  36.8 us
    all_to_all x1, blocking collectives, per_device(): parts = lax.all_to_all(parts, 'gy', split_axis=0, concat_axis=0, tiled=True)  19.2 us
    ppermute x8, starting transfers between devices, moved(): return lax.ppermute(value, axis, pairs)  17.9 us
    all_to_all x1, blocking collectives, per_device(): parts = lax.all_to_all(parts, 'gz', split_axis=0, concat_axis=0, tiled=True)  15.7 us
    all_to_all x1, starting transfers between devices, per_device(): lax.all_to_all(deep_t, 'gz', split_axis=0, concat_axis=0, tiled=True)  6.21 us
    ppermute x8, waiting for transfers between devices, moved(): return lax.ppermute(value, axis, pairs)  5.63 us
    pallas_call x4, Pallas kernels, call(): pl.pallas_call(kernel, out_shape=out_shape, scratch_shapes=list(scratch),...  4.41 us
    all_to_all x1, waiting for transfers between devices, per_device(): lax.all_to_all(deep_t, 'gz', split_axis=0, concat_axis=0, tiled=True)  3.39 us
  transfers between devices with their start and end apart: 10, of which 5 were waited for; matrix products, arithmetic and copies ran while one was open for 2% of the time, Pallas kernels for 2%

profile of v1, /device:TPU:0, one launch (start us, length us, event | category | flops | bytes accessed | tf_op | source)
XLA Modules:
  0.0 128.4 jit_solution(7259495352392537317)
XLA Ops:
  7.2 0.0 copy-start
  7.2 0.0 copy-start.3
  7.2 0.0 copy-start.5
  7.2 0.0 copy-start.4
  7.2 1.4 %collective-permute-start.5 = (bf16[8,64,128]{2,1,0:T(8,128)(2,1)}, bf16[8,64,128]{2,1,0:T(8,128)(2,1)S(1)}, u32[]{:S(2)}, u32[]{:S(2)}) collective-permute-start(bf16[8,64,128]{2,1,0:T(8,128)(2,1)} %bitcast.22), channel_id=1, source_target_pairs={{4,0},{8,4},{12,8},{16,12},{20,16},{24,20},{28,24},{5,1},{9,5},{13... | collective-permute-start | bytes 393224 | tf_op jit(solution)/shard_map/ppermute | solution.py:164
  8.6 5.5 %collective-permute-start.4 = (bf16[8,64,128]{2,1,0:T(8,128)(2,1)}, bf16[8,64,128]{2,1,0:T(8,128)(2,1)S(1)}, u32[]{:S(2)}, u32[]{:S(2)}) collective-permute-start(bf16[8,64,128]{2,1,0:T(8,128)(2,1)} %bitcast.23), channel_id=1, source_target_pairs={{0,4},{4,8},{8,12},{12,16},{16,20},{20,24},{24,28},{1,5},{5,9},{9,... | collective-permute-start | bytes 393224 | tf_op jit(solution)/shard_map/ppermute | solution.py:164
  14.2 1.0 copy.11
  15.2 0.6 broadcast_in_dim.4
  15.8 6.2 %all-to-all-start = ((bf16[8,32,128]{2,1,0:T(8,128)(2,1)}), bf16[8,32,128]{2,1,0:T(8,128)(2,1)S(1)}, u32[]{:S(2)}, u32[]{:S(2)}) async-start(bf16[8,32,128]{2,1,0:T(8,128)(2,1)} %bitcast.4), calls=%async_computation | async-start | bytes 131072 | tf_op jit(solution)/shard_map/all_to_all | solution.py:191
  22.0 0.0 all-gather.2.cloned.1.call-start
  22.1 0.7 slice_bitcast_fusion
  22.8 0.0 collective-permute-done.5.refs_2_
  22.8 0.0 collective-permute-done.4.refs_1_
  22.9 1.3 %collective-permute-start.6 = (bf16[3,64,128]{2,1,0:T(8,128)(2,1)S(1)}, bf16[3,64,128]{2,1,0:T(8,128)(2,1)S(1)}, u32[]{:S(2)}, u32[]{:S(2)}) collective-permute-start(bf16[3,64,128]{2,1,0:T(8,128)(2,1)S(1)} %pad_maximum_fusion.2), channel_id=1, source_target_pairs={{0,1},{1,2},{2,3},{4,5},{5,6},{6,7},{8,9},{9,10},{10,11},{12,13},{... | collective-permute-start | bytes 147464 | tf_op jit(solution)/shard_map/ppermute | solution.py:164
  24.2 1.3 %collective-permute-start.7 = (bf16[3,64,128]{2,1,0:T(8,128)(2,1)S(1)}, bf16[3,64,128]{2,1,0:T(8,128)(2,1)S(1)}, u32[]{:S(2)}, u32[]{:S(2)}) collective-permute-start(bf16[3,64,128]{2,1,0:T(8,128)(2,1)S(1)} %pad_maximum_fusion.3), channel_id=1, source_target_pairs={{1,0},{2,1},{3,2},{5,4},{6,5},{7,6},{9,8},{10,9},{11,10},{13,12},{... | collective-permute-start | bytes 147464 | tf_op jit(solution)/shard_map/ppermute | solution.py:164
  25.5 0.0 copy-done
  25.5 3.4 %all-to-all-done = bf16[8,32,128]{2,1,0:T(8,128)(2,1)S(1)} async-done(((bf16[8,32,128]{2,1,0:T(8,128)(2,1)}), bf16[8,32,128]{2,1,0:T(8,128)(2,1)S(1)}, u32[]{:S(2)}, u32[]{:S(2)}) %all-to-all-start) | async-done | bytes 65568 | tf_op jit(solution)/shard_map/all_to_all | solution.py:191
  28.9 0.0 copy-done.5
  28.9 0.0 copy-done.4
  28.9 0.6 shard_map.85
  29.5 0.0 collective-permute-done.6.refs_3_
  29.5 0.0 collective-permute-done.7.refs_4_
  29.5 0.0 copy-done.3
  29.5 0.9 shard_map.87
  30.4 19.2 %all_to_all.15 = bf16[4,8,144,128]{3,2,1,0:T(8,128)(2,1)S(1)} all-to-all(bf16[4,8,144,128]{3,2,1,0:T(8,128)(2,1)S(1)} %shard_map.87), channel_id=1, replica_groups=mesh['gz'=8,'gy'=4] {'gy'}, dimensions={0} | all-to-all | bytes 2359296 | tf_op jit(solution)/shard_map/all_to_all | solution.py:218
  49.6 0.2 reduce_sum.30
  49.8 15.7 %all_to_all.16 = bf16[8,144,128]{2,1,0:T(8,128)(2,1)S(1)} all-to-all(bf16[8,144,128]{2,1,0:T(8,128)(2,1)S(1)} %reduce_sum.30), channel_id=1, replica_groups=mesh['gz'=8,'gy'=4] {'gz'}, dimensions={0} | all-to-all | bytes 589824 | tf_op jit(solution)/shard_map/all_to_all | solution.py:220
  65.6 0.0 copy-start.2
  65.7 0.6 pad_maximum_fusion.4
  66.3 0.0 all-gather.2.cloned.1.call-update
  66.4 1.3 %collective-permute-start.1 = (bf16[8,64,128]{2,1,0:T(8,128)(2,1)S(1)}, bf16[8,64,128]{2,1,0:T(8,128)(2,1)S(1)}, u32[]{:S(2)}, u32[]{:S(2)}) collective-permute-start(bf16[8,64,128]{2,1,0:T(8,128)(2,1)S(1)} %get-tuple-element.7.own.refs_5_), channel_id=1, source_target_pairs={{4,0},{8,4},{12,8},{16,12},{20,16},{24,20},{28,24},{5,1},{9,5},{13... | collective-permute-start | bytes 393224 | tf_op jit(solution)/shard_map/ppermute | solution.py:164
  67.7 4.6 %collective-permute-start = (bf16[8,64,128]{2,1,0:T(8,128)(2,1)S(1)}, bf16[8,64,128]{2,1,0:T(8,128)(2,1)S(1)}, u32[]{:S(2)}, u32[]{:S(2)}) collective-permute-start(bf16[8,64,128]{2,1,0:T(8,128)(2,1)S(1)} %get-tuple-element.7.own.refs_5_), channel_id=1, source_target_pairs={{0,4},{4,8},{8,12},{12,16},{16,20},{20,24},{24,28},{1,5},{5,9},{9,... | collective-permute-start | bytes 393224 | tf_op jit(solution)/shard_map/ppermute | solution.py:164
  72.2 1.0 collective-permute-done.1.z_high
  73.2 1.7 %collective-permute-done.z_low = bf16[8,64,128]{2,1,0:T(8,128)(2,1)S(1)} collective-permute-done((bf16[8,64,128]{2,1,0:T(8,128)(2,1)S(1)}, bf16[8,64,128]{2,1,0:T(8,128)(2,1)S(1)}, u32[]{:S(2)}, u32[]{:S(2)}) %collective-permute-start) | collective-permute-done | bytes 131104 | tf_op jit(solution)/shard_map/ppermute | solution.py:164
  75.0 1.3 %collective-permute-start.2 = (bf16[3,64,128]{2,1,0:T(8,128)(2,1)S(1)}, bf16[3,64,128]{2,1,0:T(8,128)(2,1)S(1)}, u32[]{:S(2)}, u32[]{:S(2)}) collective-permute-start(bf16[3,64,128]{2,1,0:T(8,128)(2,1)S(1)} %pad_maximum_fusion), channel_id=1, source_target_pairs={{0,1},{1,2},{2,3},{4,5},{5,6},{6,7},{8,9},{9,10},{10,11},{12,13},{... | collective-permute-start | bytes 147464 | tf_op jit(solution)/shard_map/ppermute | solution.py:164
  76.3 1.3 %collective-permute-start.3 = (bf16[3,64,128]{2,1,0:T(8,128)(2,1)S(1)}, bf16[3,64,128]{2,1,0:T(8,128)(2,1)S(1)}, u32[]{:S(2)}, u32[]{:S(2)}) collective-permute-start(bf16[3,64,128]{2,1,0:T(8,128)(2,1)S(1)} %pad_maximum_fusion.1), channel_id=1, source_target_pairs={{1,0},{2,1},{3,2},{5,4},{6,5},{7,6},{9,8},{10,9},{11,10},{13,12},{... | collective-permute-start | bytes 147464 | tf_op jit(solution)/shard_map/ppermute | solution.py:164
  77.6 0.0 collective-permute-done.2.y_low
  77.6 2.9 %collective-permute-done.3.y_high = bf16[3,64,128]{2,1,0:T(8,128)(2,1)S(1)} collective-permute-done((bf16[3,64,128]{2,1,0:T(8,128)(2,1)S(1)}, bf16[3,64,128]{2,1,0:T(8,128)(2,1)S(1)}, u32[]{:S(2)}, u32[]{:S(2)}) %collective-permute-start.3) | collective-permute-done | bytes 49184 | tf_op jit(solution)/shard_map/ppermute | solution.py:164
  80.5 0.0 copy-done.2
  80.5 1.8 %shard_map.86 = bf16[8,64,128]{2,1,0:T(8,128)(2,1)} custom-call(bf16[8,64,128]{2,1,0:T(8,128)(2,1)S(1)} %get-tuple-element.7.own.refs_5_, bf16[8,64,128]{2,1,0:T(8,128)(2,1)S(1)} %collective-permute-done.z_low, bf16[8,64,128]{2,1,0:T(8,128)(2,1)S(1)} %collective-permute-done.1.z_high, bf16[3,64,128]{2,1,0:T(8,128)(2,1)S(1)} %collective-permute-done.2.y_low, ...), custom_call_target="tpu_custom_call" | custom-call | tf_op jit(solution)/shard_map/pallas_call | solution.py:16
  82.3 36.8 %all-gather.2.cloned.1.call-done.refs_0_ = bf16[32,176,128]{2,1,0:T(8,128)(2,1)} async-done(((bf16[1,176,128]{2,1,0:T(8,128)(2,1)}), bf16[32,176,128]{2,1,0:T(8,128)(2,1)}) %all-gather.2.cloned.1.call-update) | async-done | bytes 1441808 | tf_op jit(solution)/shard_map/all_gather | solution.py:228
  119.0 0.0 copy-start.1
  119.0 1.4 %copy-done.1 = bf16[32,176,128]{2,1,0:T(8,128)(2,1)S(1)} copy-done((bf16[32,176,128]{2,1,0:T(8,128)(2,1)S(1)}, bf16[32,176,128]{2,1,0:T(8,128)(2,1)}, u32[]{:S(2)}) %copy-start.1) | copy-done | bytes 1441816
  120.4 1.2 shard_map.88
  (16 shorter events, 0.2 us)
Async XLA Ops:
  7.2 18.3 %copy-start = (bf16[2,2,2,128,256]{4,3,2,1,0:T(8,128)(2,1)S(1)}, bf16[2,2,2,128,256]{4,3,2,1,0:T(8,128)(2,1)}, u32[]{:S(2)}) copy-start(bf16[2,2,2,128,256]{4,3,2,1,0:T(8,128)(2,1)} %param.9) | copy-start | bytes 1572868
  7.2 22.3 %copy-start.3 = (bf16[1,8,64,128]{3,2,1,0:T(8,128)(2,1)S(1)}, bf16[1,8,64,128]{3,2,1,0:T(8,128)(2,1)}, u32[]{:S(2)}) copy-start(bf16[1,8,64,128]{3,2,1,0:T(8,128)(2,1)} %param.6) | copy-start | bytes 393220
  7.2 21.7 %copy-start.5 = (bf16[1,8,64,128]{3,2,1,0:T(8,128)(2,1)S(1)}, bf16[1,8,64,128]{3,2,1,0:T(8,128)(2,1)}, u32[]{:S(2)}) copy-start(bf16[1,8,64,128]{3,2,1,0:T(8,128)(2,1)} %param.10) | copy-start | bytes 393220
  7.2 21.7 %copy-start.4 = (bf16[1,8,64,128]{3,2,1,0:T(8,128)(2,1)S(1)}, bf16[1,8,64,128]{3,2,1,0:T(8,128)(2,1)}, u32[]{:S(2)}) copy-start(bf16[1,8,64,128]{3,2,1,0:T(8,128)(2,1)} %param.7) | copy-start | bytes 393220
  7.2 15.6 %collective-permute-start.5 = (bf16[8,64,128]{2,1,0:T(8,128)(2,1)}, bf16[8,64,128]{2,1,0:T(8,128)(2,1)S(1)}, u32[]{:S(2)}, u32[]{:S(2)}) collective-permute-start(bf16[8,64,128]{2,1,0:T(8,128)(2,1)} %bitcast.22), channel_id=1, source_target_pairs={{4,0},{8,4},{12,8},{16,12},{20,16},{24,20},{28,24},{5,1},{9,5},{13... | collective-permute-start | bytes 393224 | tf_op jit(solution)/shard_map/ppermute | solution.py:164
  8.6 14.2 %collective-permute-start.4 = (bf16[8,64,128]{2,1,0:T(8,128)(2,1)}, bf16[8,64,128]{2,1,0:T(8,128)(2,1)S(1)}, u32[]{:S(2)}, u32[]{:S(2)}) collective-permute-start(bf16[8,64,128]{2,1,0:T(8,128)(2,1)} %bitcast.23), channel_id=1, source_target_pairs={{0,4},{4,8},{8,12},{12,16},{16,20},{20,24},{24,28},{1,5},{5,9},{9,... | collective-permute-start | bytes 393224 | tf_op jit(solution)/shard_map/ppermute | solution.py:164
  15.8 13.1 %all-to-all-start = ((bf16[8,32,128]{2,1,0:T(8,128)(2,1)}), bf16[8,32,128]{2,1,0:T(8,128)(2,1)S(1)}, u32[]{:S(2)}, u32[]{:S(2)}) async-start(bf16[8,32,128]{2,1,0:T(8,128)(2,1)} %bitcast.4), calls=%async_computation | async-start | bytes 131072 | tf_op jit(solution)/shard_map/all_to_all | solution.py:191
  22.0 97.0 %all-gather.2.cloned.1.call-start = ((), (), s32[]{:S(2)}) async-start(), calls=%async_computation.3 | async-start | bytes 1486848 | tf_op jit(solution)/shard_map/all_gather | solution.py:228
  22.9 6.6 %collective-permute-start.6 = (bf16[3,64,128]{2,1,0:T(8,128)(2,1)S(1)}, bf16[3,64,128]{2,1,0:T(8,128)(2,1)S(1)}, u32[]{:S(2)}, u32[]{:S(2)}) collective-permute-start(bf16[3,64,128]{2,1,0:T(8,128)(2,1)S(1)} %pad_maximum_fusion.2), channel_id=1, source_target_pairs={{0,1},{1,2},{2,3},{4,5},{5,6},{6,7},{8,9},{9,10},{10,11},{12,13},{... | collective-permute-start | bytes 147464 | tf_op jit(solution)/shard_map/ppermute | solution.py:164
  24.2 5.3 %collective-permute-start.7 = (bf16[3,64,128]{2,1,0:T(8,128)(2,1)S(1)}, bf16[3,64,128]{2,1,0:T(8,128)(2,1)S(1)}, u32[]{:S(2)}, u32[]{:S(2)}) collective-permute-start(bf16[3,64,128]{2,1,0:T(8,128)(2,1)S(1)} %pad_maximum_fusion.3), channel_id=1, source_target_pairs={{1,0},{2,1},{3,2},{5,4},{6,5},{7,6},{9,8},{10,9},{11,10},{13,12},{... | collective-permute-start | bytes 147464 | tf_op jit(solution)/shard_map/ppermute | solution.py:164
  65.6 14.9 %copy-start.2 = (bf16[3,3,3,128,128]{4,3,2,1,0:T(8,128)(2,1)S(1)}, bf16[3,3,3,128,128]{4,3,2,1,0:T(8,128)(2,1)}, u32[]{:S(2)}) copy-start(bf16[3,3,3,128,128]{4,3,2,1,0:T(8,128)(2,1)} %weight.1) | copy-start | bytes 2654212
  66.4 6.9 %collective-permute-start.1 = (bf16[8,64,128]{2,1,0:T(8,128)(2,1)S(1)}, bf16[8,64,128]{2,1,0:T(8,128)(2,1)S(1)}, u32[]{:S(2)}, u32[]{:S(2)}) collective-permute-start(bf16[8,64,128]{2,1,0:T(8,128)(2,1)S(1)} %get-tuple-element.7.own.refs_5_), channel_id=1, source_target_pairs={{4,0},{8,4},{12,8},{16,12},{20,16},{24,20},{28,24},{5,1},{9,5},{13... | collective-permute-start | bytes 393224 | tf_op jit(solution)/shard_map/ppermute | solution.py:164
  67.7 7.3 %collective-permute-start = (bf16[8,64,128]{2,1,0:T(8,128)(2,1)S(1)}, bf16[8,64,128]{2,1,0:T(8,128)(2,1)S(1)}, u32[]{:S(2)}, u32[]{:S(2)}) collective-permute-start(bf16[8,64,128]{2,1,0:T(8,128)(2,1)S(1)} %get-tuple-element.7.own.refs_5_), channel_id=1, source_target_pairs={{0,4},{4,8},{8,12},{12,16},{16,20},{20,24},{24,28},{1,5},{5,9},{9,... | collective-permute-start | bytes 393224 | tf_op jit(solution)/shard_map/ppermute | solution.py:164
  75.0 2.6 %collective-permute-start.2 = (bf16[3,64,128]{2,1,0:T(8,128)(2,1)S(1)}, bf16[3,64,128]{2,1,0:T(8,128)(2,1)S(1)}, u32[]{:S(2)}, u32[]{:S(2)}) collective-permute-start(bf16[3,64,128]{2,1,0:T(8,128)(2,1)S(1)} %pad_maximum_fusion), channel_id=1, source_target_pairs={{0,1},{1,2},{2,3},{4,5},{5,6},{6,7},{8,9},{9,10},{10,11},{12,13},{... | collective-permute-start | bytes 147464 | tf_op jit(solution)/shard_map/ppermute | solution.py:164
  76.3 4.2 %collective-permute-start.3 = (bf16[3,64,128]{2,1,0:T(8,128)(2,1)S(1)}, bf16[3,64,128]{2,1,0:T(8,128)(2,1)S(1)}, u32[]{:S(2)}, u32[]{:S(2)}) collective-permute-start(bf16[3,64,128]{2,1,0:T(8,128)(2,1)S(1)} %pad_maximum_fusion.1), channel_id=1, source_target_pairs={{1,0},{2,1},{3,2},{5,4},{6,5},{7,6},{9,8},{10,9},{11,10},{13,12},{... | collective-permute-start | bytes 147464 | tf_op jit(solution)/shard_map/ppermute | solution.py:164
  119.0 1.4 %copy-start.1 = (bf16[32,176,128]{2,1,0:T(8,128)(2,1)S(1)}, bf16[32,176,128]{2,1,0:T(8,128)(2,1)}, u32[]{:S(2)}) copy-start(bf16[32,176,128]{2,1,0:T(8,128)(2,1)} %all-gather.2.cloned.1.call-done.refs_0_) | copy-start | bytes 4325380
Sparse Core Ops, SparseCore 0:
  66.5 52.4 all-gather.1

commit v2 on v1

--- a/solution.py
+++ b/solution.py
@@ -29,14 +29,6 @@
     col = lax.broadcasted_iota(jnp.int32, cells.shape, 1)
     keep = col >= step if step > 0 else col < cols + step
     return jnp.where(keep, moved, 0.0)
-
-
-def fill_padded(padded, own, z_low, z_high, y_low, y_high):
-    rows = own.shape[0]
-    for plane, ref in enumerate((z_low, own, z_high)):
-        padded[plane, pl.ds(1, rows)] = ref[...]
-        padded[plane, 0] = y_low[plane]
-        padded[plane, rows + 1] = y_high[plane]
 
 
 def mask_kernel(pre, skip, deep_t, weight, grad, down):
@@ -73,14 +65,22 @@
             ).astype(BF16)
 
 
-def weight_kernel(n_gy, n_gz, conv_rows, down_rows, own, z_low, z_high, y_low, y_high, grad, down, out, padded):
-    rows, cols, channels = own.shape
-    fill_padded(padded, own, z_low, z_high, y_low, y_high)
-    grads = grad[...].astype(F32)
+def slabs(planes, rows):
+    cols, channels = planes[0].shape[1:]
+    pieces = [
+        planes[2 - kz][pl.ds(2 - ky, rows)].reshape(rows * cols, channels)
+        for kz in range(3)
+        for ky in range(3)
+    ]
+    return jnp.concatenate(pieces, axis=1)
+
+
+def weight_kernel(n_gy, n_gz, conv_rows, down_rows, level, z_low, own, z_high, down, out):
+    rows, cols, channels = level.shape
+    cells = level[...].astype(F32)
     shifts = jnp.concatenate(
-        [shifted(grads, kx - 1).astype(BF16).reshape(rows * cols, channels) for kx in range(3)],
-        axis=1,
-    )
+        [shifted(cells, 1 - kx).reshape(rows * cols, channels) for kx in range(3)], axis=1
+    ).T.astype(BF16)
 
     def store(base, piece, row, value):
         done = 0
@@ -90,15 +90,15 @@
             out[owner // n_gz, owner % n_gz, pl.ds(base + inner, take)] = value[done : done + take]
             done += take
 
-    for kz in range(3):
-        for ky in range(3):
-            slab = padded[kz, pl.ds(ky, rows)].reshape(rows * cols, channels)
-            total = lax.dot_general(
-                slab, shifts, (((0,), (0,)), ((), ())), preferred_element_type=F32
-            ).astype(BF16)
-            for kx in range(3):
-                index = (kz * 3 + ky) * 3 + kx
-                store(0, conv_rows, index * channels, total[:, kx * channels : (kx + 1) * channels])
+    total = jnp.dot(shifts, slabs((z_low, own, z_high), rows), preferred_element_type=F32)
+    total = total.astype(BF16)
+    for index in range(9):
+        store(
+            0,
+            conv_rows,
+            index * 3 * channels,
+            total[:, index * channels : (index + 1) * channels],
+        )
     blank = n_gy * n_gz * conv_rows - 27 * channels
     if blank:
         store(0, conv_rows, 27 * channels, jnp.zeros((blank, channels), BF16))
@@ -114,20 +114,18 @@
         store(conv_rows, down_rows, wide * count, jnp.zeros((blank, channels), BF16))
 
 
-def input_kernel(own, z_low, z_high, y_low, y_high, weight, out, padded):
-    rows, cols, channels = own.shape
-    fill_padded(padded, own, z_low, z_high, y_low, y_high)
+def input_kernel(z_low, own, z_high, weight, out):
+    rows, cols, channels = out.shape
+    stacked = slabs((z_low, own, z_high), rows)
     total = None
-    for kz in range(3):
-        for ky in range(3):
-            slab = padded[2 - kz, pl.ds(2 - ky, rows)].reshape(rows * cols, channels)
-            term = lax.dot_general(
-                slab,
-                weight[kz, ky].reshape(3 * channels, channels),
-                (((1,), (1,)), ((), ())),
-                preferred_element_type=F32,
-            )
-            total = term if total is None else total + term
+    for index in range(9):
+        term = lax.dot_general(
+            stacked[:, index * channels : (index + 1) * channels],
+            weight[index // 3, index % 3].reshape(3 * channels, channels),
+            (((1,), (1,)), ((), ())),
+            preferred_element_type=F32,
+        )
+        total = term if total is None else total + term
     answer = None
     for kx in range(3):
         part = total[:, kx * channels : (kx + 1) * channels].reshape(rows, cols, channels)
@@ -158,17 +156,15 @@
             done += take
 
 
-def sides(cells, gz, gy):
+def padded(cells, gz, gy):
     def moved(value, axis, count, up):
         pairs = [(i, i + 1) if up else (i + 1, i) for i in range(count - 1)]
         return lax.ppermute(value, axis, pairs)
 
-    z_low = moved(cells, "gz", gz, True)
-    z_high = moved(cells, "gz", gz, False)
-    planes = (z_low, cells, z_high)
-    y_low = moved(jnp.stack([plane[-1] for plane in planes]), "gy", gy, True)
-    y_high = moved(jnp.stack([plane[0] for plane in planes]), "gy", gy, False)
-    return cells, z_low, z_high, y_low, y_high
+    y_low = moved(cells[-1:], "gy", gy, True)
+    y_high = moved(cells[:1], "gy", gy, False)
+    own = jnp.concatenate([y_low, cells, y_high], axis=0)
+    return moved(own, "gz", gz, True), own, moved(own, "gz", gz, False)
 
 
 def per_device(
@@ -190,7 +186,6 @@
     deep_t = deep_t.reshape(2 * planes, share, deep_rows * deep_cols)
     deep_t = lax.all_to_all(deep_t, "gz", split_axis=0, concat_axis=0, tiled=True)
     deep_t = deep_t.reshape(deep_channels, deep_rows * deep_cols)
-    level = sides(level_input[0], n_gz, n_gy)
     down_slice = lax.dynamic_index_in_dim(down_weight, parity, 0, keepdims=False)
 
     shape = jax.ShapeDtypeStruct
@@ -206,14 +201,14 @@
         down_slice,
     )
 
+    planes_near = padded(grad, n_gz, n_gy)
     piece = conv_rows + down_rows
     parts = call(
         lambda *refs: weight_kernel(n_gy, n_gz, conv_rows, down_rows, *refs),
         shape((n_gy, n_gz, piece, channels), BF16),
-        *level,
-        grad,
+        level_input[0],
+        *planes_near,
         down,
-        scratch=[pltpu.VMEM((3, rows + 2, cols, channels), BF16)],
     )
     parts = lax.all_to_all(parts, "gy", split_axis=0, concat_axis=0, tiled=True)
     parts = jnp.sum(parts.astype(F32), axis=0).astype(BF16)
@@ -225,7 +220,9 @@
     down_sum = jnp.sum(slots, axis=0) / math.sqrt(cell_total // 8)
     final = jnp.concatenate([conv_sum, down_sum.reshape(2 * down_rows, channels)], axis=0)
     final = final.astype(BF16)
-    gathered = lax.all_gather(final, ("gy", "gz"), axis=0, tiled=False)
+    gathered = lax.all_gather(final, "gz", axis=0, tiled=False)
+    gathered = lax.all_gather(gathered, "gy", axis=0, tiled=False)
+    gathered = gathered.reshape((devices,) + final.shape)
     conv_grad, down_grad = call(
         lambda *refs: spread_kernel(n_gy, n_gz, conv_rows, down_rows, *refs),
         (
@@ -235,13 +232,11 @@
         gathered,
     )
 
-    halo = sides(grad, n_gz, n_gy)
     input_grad = call(
         input_kernel,
         shape((rows, cols, channels), BF16),
-        *halo,
+        *planes_near,
         conv_weight,
-        scratch=[pltpu.VMEM((3, rows + 2, cols, channels), BF16)],
     )
     return (
         input_grad[None],

time: 129 us -> 136 us (1.054)
  blocking collectives: 35 us -> 65.5 us
  waiting for transfers between devices: 45.8 us -> 30.2 us
  starting transfers between devices: 24.2 us -> 15.7 us
    all_gather x0 -> x1, blocking collectives: none -> 33.1 us  [per_device(): gathered = lax.all_gather(final, 'gz', axis=0, tiled=False)]
    all_gather x1, waiting for transfers between devices: 36.8 us -> 14.9 us  [per_device(): gathered = lax.all_gather(gathered, 'gy', axis=0, tiled=False)]
    ppermute x8 -> x4, starting transfers between devices: 17.9 us -> 8.42 us  [moved(): return lax.ppermute(value, axis, pairs)]
    all_to_all x1, waiting for transfers between devices: 3.39 us -> 6.8 us  [per_device(): lax.all_to_all(deep_t, 'gz', split_axis=0, concat_axis=0, tiled=True)]
    ppermute x8 -> x4, waiting for transfers between devices: 5.63 us -> 8.48 us  [moved(): return lax.ppermute(value, axis, pairs)]
    unnamed x12 -> x14, local copies, waits for them, and re-layouts: 1.39 us -> 3.21 us
    all_to_all x1, blocking collectives: 15.7 us -> 14.1 us  [per_device(): parts = lax.all_to_all(parts, 'gz', split_axis=0, concat_axis=0, tiled=True)]
  transfers between devices with their start and end apart: 10 -> 6, of which waited for: 5 -> 5; matrix products, arithmetic and copies ran while one was open for 2% -> 0% of each run, Pallas kernels for 2% -> 1%
where the time goes in v2:
time: 136 us; the launch traced here: 135 us
  blocking collectives  65.5 us (48%)
  waiting for transfers between devices  30.2 us (22%)
  starting transfers between devices  15.7 us (12%)
  between operations  14.2 us (10%)
  local copies, waits for them, and re-layouts  4.95 us (4%)
  Pallas kernels  4.25 us (3%)
    all_gather x1, blocking collectives, per_device(): gathered = lax.all_gather(final, 'gz', axis=0, tiled=False)  33.1 us
    all_to_all x1, blocking collectives, per_device(): parts = lax.all_to_all(parts, 'gy', split_axis=0, concat_axis=0, tiled=True)  18.3 us
    all_gather x1, waiting for transfers between devices, per_device(): gathered = lax.all_gather(gathered, 'gy', axis=0, tiled=False)  14.9 us
    all_to_all x1, blocking collectives, per_device(): parts = lax.all_to_all(parts, 'gz', split_axis=0, concat_axis=0, tiled=True)  14.1 us
    ppermute x4, waiting for transfers between devices, moved(): return lax.ppermute(value, axis, pairs)  8.48 us
    ppermute x4, starting transfers between devices, moved(): return lax.ppermute(value, axis, pairs)  8.42 us
    all_to_all x1, starting transfers between devices, per_device(): lax.all_to_all(deep_t, 'gz', split_axis=0, concat_axis=0, tiled=True)  7.28 us
    all_to_all x1, waiting for transfers between devices, per_device(): lax.all_to_all(deep_t, 'gz', split_axis=0, concat_axis=0, tiled=True)  6.8 us
  transfers between devices with their start and end apart: 6, of which 5 were waited for; matrix products, arithmetic and copies ran while one was open for 0% of the time, Pallas kernels for 1%

profile of v2, /device:TPU:0, one launch (start us, length us, event | category | flops | bytes accessed | tf_op | source)
XLA Modules:
  0.0 135.2 jit_solution(8091856912736672688)
XLA Ops:
  7.2 0.0 copy-start
  7.2 0.0 copy-start.3
  7.2 1.1 copy.11
  8.2 0.6 broadcast_in_dim.4
  8.9 7.3 %all-to-all-start = ((bf16[8,32,128]{2,1,0:T(8,128)(2,1)}), bf16[8,32,128]{2,1,0:T(8,128)(2,1)S(1)}, u32[]{:S(2)}, u32[]{:S(2)}) async-start(bf16[8,32,128]{2,1,0:T(8,128)(2,1)} %bitcast.4), calls=%async_computation | async-start | bytes 131072 | tf_op jit(solution)/shard_map/all_to_all | solution.py:187
  16.2 0.0 all-gather.3.cloned.1.call-start
  16.2 0.0 copy-done
  16.3 6.8 %all-to-all-done = bf16[8,32,128]{2,1,0:T(8,128)(2,1)S(1)} async-done(((bf16[8,32,128]{2,1,0:T(8,128)(2,1)}), bf16[8,32,128]{2,1,0:T(8,128)(2,1)S(1)}, u32[]{:S(2)}, u32[]{:S(2)}) %all-to-all-start) | async-done | bytes 65568 | tf_op jit(solution)/shard_map/all_to_all | solution.py:187
  23.1 0.0 copy-start.4
  23.1 0.9 copy-done.4
  24.0 0.0 copy-start.5
  24.0 0.9 copy-done.5
  24.9 0.6 shard_map.85
  25.5 1.3 collective-permute-start
  26.8 1.3 collective-permute-start.1
  28.1 0.0 collective-permute-done
  28.1 3.5 %collective-permute-done.1 = bf16[1,64,128]{2,1,0:T(8,128)(2,1)S(1)} collective-permute-done((bf16[1,64,128]{2,1,0:T(8,128)(2,1)S(1)}, bf16[1,64,128]{2,1,0:T(8,128)(2,1)S(1)}, u32[]{:S(2)}, u32[]{:S(2)}) %collective-permute-start.1) | collective-permute-done | bytes 16416 | tf_op jit(solution)/shard_map/ppermute | solution.py:162
  31.6 1.3 collective-permute-start.3
  32.9 4.6 %collective-permute-start.2 = (bf16[10,64,128]{2,1,0:T(8,128)(2,1)S(1)}, bf16[10,64,128]{2,1,0:T(8,128)(2,1)S(1)}, u32[]{:S(2)}, u32[]{:S(2)}) collective-permute-start(bf16[10,64,128]{2,1,0:T(8,128)(2,1)S(1)} %constant_dynamic-update-slice_fusion.own.refs_2_), channel_id=1, source_target_pairs={{0,4},{4,8},{8,12},{12,16},{16,20},{20,24},{24,28},{1,5},{5,9},{9,... | collective-permute-start | bytes 491528 | tf_op jit(solution)/shard_map/ppermute | solution.py:162
  37.4 1.5 %collective-permute-done.3.z_high.refs_3_ = bf16[10,64,128]{2,1,0:T(8,128)(2,1)S(1)} collective-permute-done((bf16[10,64,128]{2,1,0:T(8,128)(2,1)S(1)}, bf16[10,64,128]{2,1,0:T(8,128)(2,1)S(1)}, u32[]{:S(2)}, u32[]{:S(2)}) %collective-permute-start.3) | collective-permute-done | bytes 163872 | tf_op jit(solution)/shard_map/ppermute | solution.py:162
  39.0 3.5 %collective-permute-done.2.z_low.refs_1_ = bf16[10,64,128]{2,1,0:T(8,128)(2,1)S(1)} collective-permute-done((bf16[10,64,128]{2,1,0:T(8,128)(2,1)S(1)}, bf16[10,64,128]{2,1,0:T(8,128)(2,1)S(1)}, u32[]{:S(2)}, u32[]{:S(2)}) %collective-permute-start.2) | collective-permute-done | bytes 163872 | tf_op jit(solution)/shard_map/ppermute | solution.py:162
  42.4 0.0 copy-done.3
  42.5 0.7 shard_map.87
  43.2 18.3 %all_to_all.15 = bf16[4,8,144,128]{3,2,1,0:T(8,128)(2,1)S(1)} all-to-all(bf16[4,8,144,128]{3,2,1,0:T(8,128)(2,1)S(1)} %shard_map.87), channel_id=1, replica_groups=mesh['gz'=8,'gy'=4] {'gy'}, dimensions={0} | all-to-all | bytes 2359296 | tf_op jit(solution)/shard_map/all_to_all | solution.py:213
  61.5 0.2 reduce_sum.30
  61.7 14.1 %all_to_all.16 = bf16[8,144,128]{2,1,0:T(8,128)(2,1)S(1)} all-to-all(bf16[8,144,128]{2,1,0:T(8,128)(2,1)S(1)} %reduce_sum.30), channel_id=1, replica_groups=mesh['gz'=8,'gy'=4] {'gz'}, dimensions={0} | all-to-all | bytes 589824 | tf_op jit(solution)/shard_map/all_to_all | solution.py:215
  75.8 0.0 copy-start.2
  76.0 33.1 %all_gather.10 = bf16[8,176,128]{2,1,0:T(8,128)(2,1)} all-gather(bf16[1,176,128]{2,1,0:T(8,128)(2,1)S(1)} %pad_maximum_fusion), channel_id=1, replica_groups=mesh['gz'=8,'gy'=4] {'gz'}, dimensions={0}, use_global_device_ids=true | all-gather | bytes 405504 | tf_op jit(solution)/shard_map/all_gather | solution.py:223
  109.1 0.0 all-gather.3.cloned.1.call-update
  109.1 0.0 copy-done.2
  109.1 1.7 %shard_map.86 = bf16[8,64,128]{2,1,0:T(8,128)(2,1)} custom-call(bf16[10,64,128]{2,1,0:T(8,128)(2,1)S(1)} %collective-permute-done.2.z_low.refs_1_, bf16[10,64,128]{2,1,0:T(8,128)(2,1)S(1)} %constant_dynamic-update-slice_fusion.own.refs_2_, bf16[10,64,128]{2,1,0:T(8,128)(2,1)S(1)} %collective-permute-done.3.z_high.refs_3_, ...), custom_call_target="tpu_custom_call" | custom-call | tf_op jit(solution)/shard_map/pallas_call | solution.py:16
  110.8 14.9 %all-gather.3.cloned.1.call-done.refs_0_ = bf16[32,176,128]{2,1,0:T(8,128)(2,1)} async-done(((bf16[8,176,128]{2,1,0:T(8,128)(2,1)}), bf16[32,176,128]{2,1,0:T(8,128)(2,1)}) %all-gather.3.cloned.1.call-update) | async-done | bytes 1441808 | tf_op jit(solution)/shard_map/all_gather | solution.py:224
  125.8 0.0 copy-start.1
  125.8 1.4 %copy-done.1 = bf16[32,176,128]{2,1,0:T(8,128)(2,1)S(1)} copy-done((bf16[32,176,128]{2,1,0:T(8,128)(2,1)S(1)}, bf16[32,176,128]{2,1,0:T(8,128)(2,1)}, u32[]{:S(2)}) %copy-start.1) | copy-done | bytes 1441816
  127.1 1.2 shard_map.88
  (12 shorter events, 0.2 us)
Async XLA Ops:
  7.2 9.1 %copy-start = (bf16[2,2,2,128,256]{4,3,2,1,0:T(8,128)(2,1)S(1)}, bf16[2,2,2,128,256]{4,3,2,1,0:T(8,128)(2,1)}, u32[]{:S(2)}) copy-start(bf16[2,2,2,128,256]{4,3,2,1,0:T(8,128)(2,1)} %param.9) | copy-start | bytes 1572868
  7.2 35.3 %copy-start.3 = (bf16[1,8,64,128]{3,2,1,0:T(8,128)(2,1)S(1)}, bf16[1,8,64,128]{3,2,1,0:T(8,128)(2,1)}, u32[]{:S(2)}) copy-start(bf16[1,8,64,128]{3,2,1,0:T(8,128)(2,1)} %param.6) | copy-start | bytes 393220
  8.9 14.2 %all-to-all-start = ((bf16[8,32,128]{2,1,0:T(8,128)(2,1)}), bf16[8,32,128]{2,1,0:T(8,128)(2,1)S(1)}, u32[]{:S(2)}, u32[]{:S(2)}) async-start(bf16[8,32,128]{2,1,0:T(8,128)(2,1)} %bitcast.4), calls=%async_computation | async-start | bytes 131072 | tf_op jit(solution)/shard_map/all_to_all | solution.py:187
  16.2 109.6 %all-gather.3.cloned.1.call-start = ((), (), s32[]{:S(2)}) async-start(), calls=%async_computation.3 | async-start | bytes 1802240 | tf_op jit(solution)/shard_map/all_gather | solution.py:224
  23.1 0.9 copy-start.4
  24.0 0.9 copy-start.5
  25.5 2.6 %collective-permute-start = (bf16[1,64,128]{2,1,0:T(8,128)(2,1)S(1)}, bf16[1,64,128]{2,1,0:T(8,128)(2,1)S(1)}, u32[]{:S(2)}, u32[]{:S(2)}) collective-permute-start(bf16[1,64,128]{2,1,0:T(8,128)(2,1)S(1)} %get-tuple-element.12), channel_id=1, source_target_pairs={{0,1},{1,2},{2,3},{4,5},{5,6},{6,7},{8,9},{9,10},{10,11},{12,13},{... | collective-permute-start | bytes 49160 | tf_op jit(solution)/shard_map/ppermute | solution.py:162
  26.8 4.8 %collective-permute-start.1 = (bf16[1,64,128]{2,1,0:T(8,128)(2,1)S(1)}, bf16[1,64,128]{2,1,0:T(8,128)(2,1)S(1)}, u32[]{:S(2)}, u32[]{:S(2)}) collective-permute-start(bf16[1,64,128]{2,1,0:T(8,128)(2,1)S(1)} %get-tuple-element.11), channel_id=1, source_target_pairs={{1,0},{2,1},{3,2},{5,4},{6,5},{7,6},{9,8},{10,9},{11,10},{13,12},{... | collective-permute-start | bytes 49160 | tf_op jit(solution)/shard_map/ppermute | solution.py:162
  31.6 7.4 %collective-permute-start.3 = (bf16[10,64,128]{2,1,0:T(8,128)(2,1)S(1)}, bf16[10,64,128]{2,1,0:T(8,128)(2,1)S(1)}, u32[]{:S(2)}, u32[]{:S(2)}) collective-permute-start(bf16[10,64,128]{2,1,0:T(8,128)(2,1)S(1)} %constant_dynamic-update-slice_fusion.own.refs_2_), channel_id=1, source_target_pairs={{4,0},{8,4},{12,8},{16,12},{20,16},{24,20},{28,24},{5,1},{9,5},{13... | collective-permute-start | bytes 491528 | tf_op jit(solution)/shard_map/ppermute | solution.py:162
  32.9 9.6 %collective-permute-start.2 = (bf16[10,64,128]{2,1,0:T(8,128)(2,1)S(1)}, bf16[10,64,128]{2,1,0:T(8,128)(2,1)S(1)}, u32[]{:S(2)}, u32[]{:S(2)}) collective-permute-start(bf16[10,64,128]{2,1,0:T(8,128)(2,1)S(1)} %constant_dynamic-update-slice_fusion.own.refs_2_), channel_id=1, source_target_pairs={{0,4},{4,8},{8,12},{12,16},{16,20},{20,24},{24,28},{1,5},{5,9},{9,... | collective-permute-start | bytes 491528 | tf_op jit(solution)/shard_map/ppermute | solution.py:162
  75.8 33.3 %copy-start.2 = (bf16[3,3,3,128,128]{4,3,2,1,0:T(8,128)(2,1)S(1)}, bf16[3,3,3,128,128]{4,3,2,1,0:T(8,128)(2,1)}, u32[]{:S(2)}) copy-start(bf16[3,3,3,128,128]{4,3,2,1,0:T(8,128)(2,1)} %weight.1) | copy-start | bytes 2654212
  125.8 1.4 %copy-start.1 = (bf16[32,176,128]{2,1,0:T(8,128)(2,1)S(1)}, bf16[32,176,128]{2,1,0:T(8,128)(2,1)}, u32[]{:S(2)}) copy-start(bf16[32,176,128]{2,1,0:T(8,128)(2,1)} %all-gather.3.cloned.1.call-done.refs_0_) | copy-start | bytes 4325380
Sparse Core Ops, SparseCore 0:
  109.2 16.5 all-gather.2

commit v3 on v1

--- a/solution.py
+++ b/solution.py
@@ -171,6 +171,11 @@
     return cells, z_low, z_high, y_low, y_high
 
 
+def everywhere(value, axis):
+    copies = jnp.broadcast_to(value[None], (lax.axis_size(axis),) + value.shape)
+    return lax.all_to_all(copies, axis, split_axis=0, concat_axis=0, tiled=True)
+
+
 def per_device(
     level_input, pre_activation, conv_weight, down_weight, skip_cotangent, deep_cotangent
 ):
@@ -225,7 +230,7 @@
     down_sum = jnp.sum(slots, axis=0) / math.sqrt(cell_total // 8)
     final = jnp.concatenate([conv_sum, down_sum.reshape(2 * down_rows, channels)], axis=0)
     final = final.astype(BF16)
-    gathered = lax.all_gather(final, ("gy", "gz"), axis=0, tiled=False)
+    gathered = everywhere(everywhere(final, "gz"), "gy").reshape((devices,) + final.shape)
     conv_grad, down_grad = call(
         lambda *refs: spread_kernel(n_gy, n_gz, conv_rows, down_rows, *refs),
         (

time: 129 us -> 101 us (0.78)
  the two profiles are of different devices: /device:TPU:0 before, /device:TPU:9 now
where the time goes in v3:
time: 101 us; the launch traced here: 99.9 us
  blocking collectives  42.6 us (42%)
  starting transfers between devices  36 us (36%)
  waiting for transfers between devices  11.8 us (12%)
  Pallas kernels  4.42 us (4%)
  local copies, waits for them, and re-layouts  3.79 us (4%)
    ppermute x8, starting transfers between devices, moved(): return lax.ppermute(value, axis, pairs)  23.7 us
    all_to_all x1, blocking collectives, per_device(): parts = lax.all_to_all(parts, 'gy', split_axis=0, concat_axis=0, tiled=True)  16.4 us
    all_to_all x1, blocking collectives, everywhere(): return lax.all_to_all(copies, axis, split_axis=0, concat_axis=0, tiled=True)  14 us
    all_to_all x1, blocking collectives, per_device(): parts = lax.all_to_all(parts, 'gz', split_axis=0, concat_axis=0, tiled=True)  12.2 us
    ppermute x8, waiting for transfers between devices, moved(): return lax.ppermute(value, axis, pairs)  11.8 us
    all_to_all x1, starting transfers between devices, everywhere(): return lax.all_to_all(copies, axis, split_axis=0, concat_axis=0, tiled=True)  6.73 us
    all_to_all x1, starting transfers between devices, per_device(): lax.all_to_all(deep_t, 'gz', split_axis=0, concat_axis=0, tiled=True)  5.61 us
    pallas_call x4, Pallas kernels, call(): pl.pallas_call(kernel, out_shape=out_shape, scratch_shapes=list(scratch),...  4.42 us
  transfers between devices with their start and end apart: 10, of which 4 were waited for; matrix products, arithmetic and copies ran while one was open for 2% of the time, Pallas kernels for 2%

profile of v3, /device:TPU:9, one launch (start us, length us, event | category | flops | bytes accessed | tf_op | source)
XLA Modules:
  0.0 99.9 jit_solution(11427515953420768658)
XLA Ops:
  0.6 0.0 copy-start
  0.6 0.0 copy-start.2
  0.7 0.0 copy-start.4
  0.7 0.0 copy-start.3
  0.7 3.2 %collective-permute-start.5 = (bf16[8,64,128]{2,1,0:T(8,128)(2,1)}, bf16[8,64,128]{2,1,0:T(8,128)(2,1)S(1)}, u32[]{:S(2)}, u32[]{:S(2)}) collective-permute-start(bf16[8,64,128]{2,1,0:T(8,128)(2,1)} %bitcast.22), channel_id=1, source_target_pairs={{4,0},{8,4},{12,8},{16,12},{20,16},{24,20},{28,24},{5,1},{9,5},{13... | collective-permute-start | bytes 393224 | tf_op jit(solution)/shard_map/ppermute | solution.py:164
  3.9 2.3 %collective-permute-start.4 = (bf16[8,64,128]{2,1,0:T(8,128)(2,1)}, bf16[8,64,128]{2,1,0:T(8,128)(2,1)S(1)}, u32[]{:S(2)}, u32[]{:S(2)}) collective-permute-start(bf16[8,64,128]{2,1,0:T(8,128)(2,1)} %bitcast.23), channel_id=1, source_target_pairs={{0,4},{4,8},{8,12},{12,16},{16,20},{20,24},{24,28},{1,5},{5,9},{9,... | collective-permute-start | bytes 393224 | tf_op jit(solution)/shard_map/ppermute | solution.py:164
  6.1 1.0 copy.10
  7.1 0.6 broadcast_in_dim.8
  7.7 5.6 %all-to-all-start = ((bf16[8,32,128]{2,1,0:T(8,128)(2,1)}), bf16[8,32,128]{2,1,0:T(8,128)(2,1)S(1)}, u32[]{:S(2)}, u32[]{:S(2)}) async-start(bf16[8,32,128]{2,1,0:T(8,128)(2,1)} %bitcast.4), calls=%async_computation | async-start | bytes 131072 | tf_op jit(solution)/shard_map/all_to_all | solution.py:196
  13.4 0.7 slice_bitcast_fusion
  14.1 0.0 collective-permute-done.5.refs_2_
  14.1 0.0 collective-permute-done.4.refs_1_
  14.1 4.8 %collective-permute-start.6 = (bf16[3,64,128]{2,1,0:T(8,128)(2,1)S(1)}, bf16[3,64,128]{2,1,0:T(8,128)(2,1)S(1)}, u32[]{:S(2)}, u32[]{:S(2)}) collective-permute-start(bf16[3,64,128]{2,1,0:T(8,128)(2,1)S(1)} %pad_maximum_fusion.2), channel_id=1, source_target_pairs={{0,1},{1,2},{2,3},{4,5},{5,6},{6,7},{8,9},{9,10},{10,11},{12,13},{... | collective-permute-start | bytes 147464 | tf_op jit(solution)/shard_map/ppermute | solution.py:164
  19.0 1.9 %collective-permute-start.7 = (bf16[3,64,128]{2,1,0:T(8,128)(2,1)S(1)}, bf16[3,64,128]{2,1,0:T(8,128)(2,1)S(1)}, u32[]{:S(2)}, u32[]{:S(2)}) collective-permute-start(bf16[3,64,128]{2,1,0:T(8,128)(2,1)S(1)} %pad_maximum_fusion.3), channel_id=1, source_target_pairs={{1,0},{2,1},{3,2},{5,4},{6,5},{7,6},{9,8},{10,9},{11,10},{13,12},{... | collective-permute-start | bytes 147464 | tf_op jit(solution)/shard_map/ppermute | solution.py:164
  20.9 0.0 copy-done
  20.9 0.0 all-to-all-done
  20.9 0.0 copy-done.4
  21.0 0.0 copy-done.3
  21.0 0.6 shard_map.85
  21.5 0.0 collective-permute-done.6.refs_3_
  21.5 2.8 %collective-permute-done.7.refs_4_ = bf16[3,64,128]{2,1,0:T(8,128)(2,1)S(1)} collective-permute-done((bf16[3,64,128]{2,1,0:T(8,128)(2,1)S(1)}, bf16[3,64,128]{2,1,0:T(8,128)(2,1)S(1)}, u32[]{:S(2)}, u32[]{:S(2)}) %collective-permute-start.7) | collective-permute-done | bytes 49184 | tf_op jit(solution)/shard_map/ppermute | solution.py:164
  24.4 0.0 copy-done.2
  24.4 0.9 shard_map.87
  25.2 16.4 %all_to_all.25 = bf16[4,8,144,128]{3,2,1,0:T(8,128)(2,1)S(1)} all-to-all(bf16[4,8,144,128]{3,2,1,0:T(8,128)(2,1)S(1)} %shard_map.87), channel_id=1, replica_groups=mesh['gz'=8,'gy'=4] {'gy'}, dimensions={0} | all-to-all | bytes 2359296 | tf_op jit(solution)/shard_map/all_to_all | solution.py:223
  41.7 0.2 reduce_sum.30
  41.9 12.2 %all_to_all.26 = bf16[8,144,128]{2,1,0:T(8,128)(2,1)S(1)} all-to-all(bf16[8,144,128]{2,1,0:T(8,128)(2,1)S(1)} %reduce_sum.30), channel_id=1, replica_groups=mesh['gz'=8,'gy'=4] {'gz'}, dimensions={0} | all-to-all | bytes 589824 | tf_op jit(solution)/shard_map/all_to_all | solution.py:225
  54.3 14.0 %all_to_all.27 = bf16[8,176,128]{2,1,0:T(8,128)(2,1)S(1)} all-to-all(bf16[8,176,128]{2,1,0:T(8,128)(2,1)S(1)} %broadcast_in_dim.10), channel_id=1, replica_groups=mesh['gz'=8,'gy'=4] {'gz'}, dimensions={0} | all-to-all | bytes 720896 | tf_op jit(solution)/shard_map/all_to_all | solution.py:176
  68.3 1.3 %broadcast_in_dim.11 = bf16[4,8,176,128]{3,2,1,0:T(8,128)(2,1)} broadcast(bf16[8,176,128]{2,1,0:T(8,128)(2,1)S(1)} %all_to_all.27), dimensions={1,2,3} | broadcast | bytes 1802240 | tf_op jit(solution)/shard_map/broadcast_in_dim | solution.py:175
  69.6 0.0 copy-start.1
  69.6 6.7 %all-to-all-start.4 = ((bf16[4,8,176,128]{3,2,1,0:T(8,128)(2,1)}), bf16[4,8,176,128]{3,2,1,0:T(8,128)(2,1)S(1)}, u32[]{:S(2)}, u32[]{:S(2)}) async-start(bf16[4,8,176,128]{3,2,1,0:T(8,128)(2,1)} %broadcast_in_dim.11), calls=%async_computation.4 | async-start | bytes 2883584 | tf_op jit(solution)/shard_map/all_to_all | solution.py:176
  76.3 3.2 %collective-permute-start.1 = (bf16[8,64,128]{2,1,0:T(8,128)(2,1)S(1)}, bf16[8,64,128]{2,1,0:T(8,128)(2,1)S(1)}, u32[]{:S(2)}, u32[]{:S(2)}) collective-permute-start(bf16[8,64,128]{2,1,0:T(8,128)(2,1)S(1)} %get-tuple-element.7.own.refs_5_), channel_id=1, source_target_pairs={{4,0},{8,4},{12,8},{16,12},{20,16},{24,20},{28,24},{5,1},{9,5},{13... | collective-permute-start | bytes 393224 | tf_op jit(solution)/shard_map/ppermute | solution.py:164
  79.5 2.1 %collective-permute-start = (bf16[8,64,128]{2,1,0:T(8,128)(2,1)S(1)}, bf16[8,64,128]{2,1,0:T(8,128)(2,1)S(1)}, u32[]{:S(2)}, u32[]{:S(2)}) collective-permute-start(bf16[8,64,128]{2,1,0:T(8,128)(2,1)S(1)} %get-tuple-element.7.own.refs_5_), channel_id=1, source_target_pairs={{0,4},{4,8},{8,12},{12,16},{16,20},{20,24},{24,28},{1,5},{5,9},{9,... | collective-permute-start | bytes 393224 | tf_op jit(solution)/shard_map/ppermute | solution.py:164
  81.6 1.7 %collective-permute-done.1.z_high = bf16[8,64,128]{2,1,0:T(8,128)(2,1)S(1)} collective-permute-done((bf16[8,64,128]{2,1,0:T(8,128)(2,1)S(1)}, bf16[8,64,128]{2,1,0:T(8,128)(2,1)S(1)}, u32[]{:S(2)}, u32[]{:S(2)}) %collective-permute-start.1) | collective-permute-done | bytes 131104 | tf_op jit(solution)/shard_map/ppermute | solution.py:164
  83.3 3.8 %collective-permute-done.z_low = bf16[8,64,128]{2,1,0:T(8,128)(2,1)S(1)} collective-permute-done((bf16[8,64,128]{2,1,0:T(8,128)(2,1)S(1)}, bf16[8,64,128]{2,1,0:T(8,128)(2,1)S(1)}, u32[]{:S(2)}, u32[]{:S(2)}) %collective-permute-start) | collective-permute-done | bytes 131104 | tf_op jit(solution)/shard_map/ppermute | solution.py:164
  87.1 4.3 %collective-permute-start.2 = (bf16[3,64,128]{2,1,0:T(8,128)(2,1)S(1)}, bf16[3,64,128]{2,1,0:T(8,128)(2,1)S(1)}, u32[]{:S(2)}, u32[]{:S(2)}) collective-permute-start(bf16[3,64,128]{2,1,0:T(8,128)(2,1)S(1)} %pad_maximum_fusion), channel_id=1, source_target_pairs={{0,1},{1,2},{2,3},{4,5},{5,6},{6,7},{8,9},{9,10},{10,11},{12,13},{... | collective-permute-start | bytes 147464 | tf_op jit(solution)/shard_map/ppermute | solution.py:164
  91.5 1.9 %collective-permute-start.3 = (bf16[3,64,128]{2,1,0:T(8,128)(2,1)S(1)}, bf16[3,64,128]{2,1,0:T(8,128)(2,1)S(1)}, u32[]{:S(2)}, u32[]{:S(2)}) collective-permute-start(bf16[3,64,128]{2,1,0:T(8,128)(2,1)S(1)} %pad_maximum_fusion.1), channel_id=1, source_target_pairs={{1,0},{2,1},{3,2},{5,4},{6,5},{7,6},{9,8},{10,9},{11,10},{13,12},{... | collective-permute-start | bytes 147464 | tf_op jit(solution)/shard_map/ppermute | solution.py:164
  93.4 0.0 collective-permute-done.2.y_low
  93.4 3.5 %collective-permute-done.3.y_high = bf16[3,64,128]{2,1,0:T(8,128)(2,1)S(1)} collective-permute-done((bf16[3,64,128]{2,1,0:T(8,128)(2,1)S(1)}, bf16[3,64,128]{2,1,0:T(8,128)(2,1)S(1)}, u32[]{:S(2)}, u32[]{:S(2)}) %collective-permute-start.3) | collective-permute-done | bytes 49184 | tf_op jit(solution)/shard_map/ppermute | solution.py:164
  96.9 0.0 copy-done.1
  96.9 1.8 %shard_map.86 = bf16[8,64,128]{2,1,0:T(8,128)(2,1)} custom-call(bf16[8,64,128]{2,1,0:T(8,128)(2,1)S(1)} %get-tuple-element.7.own.refs_5_, bf16[8,64,128]{2,1,0:T(8,128)(2,1)S(1)} %collective-permute-done.z_low, bf16[8,64,128]{2,1,0:T(8,128)(2,1)S(1)} %collective-permute-done.1.z_high, bf16[3,64,128]{2,1,0:T(8,128)(2,1)S(1)} %collective-permute-done.2.y_low, ...), custom_call_target="tpu_custom_call" | custom-call | tf_op jit(solution)/shard_map/pallas_call | solution.py:16
  98.6 0.0 all-to-all-done.4
  98.6 1.2 %shard_map.88 = (bf16[3456,128]{1,0:T(8,128)(2,1)}, bf16[2,512,256]{2,1,0:T(8,128)(2,1)}) custom-call(bf16[32,176,128]{2,1,0:T(8,128)(2,1)S(1)} %bitcast.20), custom_call_target="tpu_custom_call" | custom-call | tf_op jit(solution)/shard_map/pallas_call | solution.py:16
  (18 shorter events, 0.2 us)
Async XLA Ops:
  0.6 20.3 %copy-start = (bf16[2,2,2,128,256]{4,3,2,1,0:T(8,128)(2,1)S(1)}, bf16[2,2,2,128,256]{4,3,2,1,0:T(8,128)(2,1)}, u32[]{:S(2)}) copy-start(bf16[2,2,2,128,256]{4,3,2,1,0:T(8,128)(2,1)} %param.9) | copy-start | bytes 1572868
  0.6 23.7 %copy-start.2 = (bf16[1,8,64,128]{3,2,1,0:T(8,128)(2,1)S(1)}, bf16[1,8,64,128]{3,2,1,0:T(8,128)(2,1)}, u32[]{:S(2)}) copy-start(bf16[1,8,64,128]{3,2,1,0:T(8,128)(2,1)} %param.6) | copy-start | bytes 393220
  0.7 20.3 %copy-start.4 = (bf16[1,8,64,128]{3,2,1,0:T(8,128)(2,1)S(1)}, bf16[1,8,64,128]{3,2,1,0:T(8,128)(2,1)}, u32[]{:S(2)}) copy-start(bf16[1,8,64,128]{3,2,1,0:T(8,128)(2,1)} %param.10) | copy-start | bytes 393220
  0.7 20.3 %copy-start.3 = (bf16[1,8,64,128]{3,2,1,0:T(8,128)(2,1)S(1)}, bf16[1,8,64,128]{3,2,1,0:T(8,128)(2,1)}, u32[]{:S(2)}) copy-start(bf16[1,8,64,128]{3,2,1,0:T(8,128)(2,1)} %param.7) | copy-start | bytes 393220
  0.7 13.4 %collective-permute-start.5 = (bf16[8,64,128]{2,1,0:T(8,128)(2,1)}, bf16[8,64,128]{2,1,0:T(8,128)(2,1)S(1)}, u32[]{:S(2)}, u32[]{:S(2)}) collective-permute-start(bf16[8,64,128]{2,1,0:T(8,128)(2,1)} %bitcast.22), channel_id=1, source_target_pairs={{4,0},{8,4},{12,8},{16,12},{20,16},{24,20},{28,24},{5,1},{9,5},{13... | collective-permute-start | bytes 393224 | tf_op jit(solution)/shard_map/ppermute | solution.py:164
  3.9 10.2 %collective-permute-start.4 = (bf16[8,64,128]{2,1,0:T(8,128)(2,1)}, bf16[8,64,128]{2,1,0:T(8,128)(2,1)S(1)}, u32[]{:S(2)}, u32[]{:S(2)}) collective-permute-start(bf16[8,64,128]{2,1,0:T(8,128)(2,1)} %bitcast.23), channel_id=1, source_target_pairs={{0,4},{4,8},{8,12},{12,16},{16,20},{20,24},{24,28},{1,5},{5,9},{9,... | collective-permute-start | bytes 393224 | tf_op jit(solution)/shard_map/ppermute | solution.py:164
  7.7 13.2 %all-to-all-start = ((bf16[8,32,128]{2,1,0:T(8,128)(2,1)}), bf16[8,32,128]{2,1,0:T(8,128)(2,1)S(1)}, u32[]{:S(2)}, u32[]{:S(2)}) async-start(bf16[8,32,128]{2,1,0:T(8,128)(2,1)} %bitcast.4), calls=%async_computation | async-start | bytes 131072 | tf_op jit(solution)/shard_map/all_to_all | solution.py:196
  14.1 7.4 %collective-permute-start.6 = (bf16[3,64,128]{2,1,0:T(8,128)(2,1)S(1)}, bf16[3,64,128]{2,1,0:T(8,128)(2,1)S(1)}, u32[]{:S(2)}, u32[]{:S(2)}) collective-permute-start(bf16[3,64,128]{2,1,0:T(8,128)(2,1)S(1)} %pad_maximum_fusion.2), channel_id=1, source_target_pairs={{0,1},{1,2},{2,3},{4,5},{5,6},{6,7},{8,9},{9,10},{10,11},{12,13},{... | collective-permute-start | bytes 147464 | tf_op jit(solution)/shard_map/ppermute | solution.py:164
  19.0 5.4 %collective-permute-start.7 = (bf16[3,64,128]{2,1,0:T(8,128)(2,1)S(1)}, bf16[3,64,128]{2,1,0:T(8,128)(2,1)S(1)}, u32[]{:S(2)}, u32[]{:S(2)}) collective-permute-start(bf16[3,64,128]{2,1,0:T(8,128)(2,1)S(1)} %pad_maximum_fusion.3), channel_id=1, source_target_pairs={{1,0},{2,1},{3,2},{5,4},{6,5},{7,6},{9,8},{10,9},{11,10},{13,12},{... | collective-permute-start | bytes 147464 | tf_op jit(solution)/shard_map/ppermute | solution.py:164
  69.6 27.3 %copy-start.1 = (bf16[3,3,3,128,128]{4,3,2,1,0:T(8,128)(2,1)S(1)}, bf16[3,3,3,128,128]{4,3,2,1,0:T(8,128)(2,1)}, u32[]{:S(2)}) copy-start(bf16[3,3,3,128,128]{4,3,2,1,0:T(8,128)(2,1)} %weight.1) | copy-start | bytes 2654212
  69.6 29.0 %all-to-all-start.4 = ((bf16[4,8,176,128]{3,2,1,0:T(8,128)(2,1)}), bf16[4,8,176,128]{3,2,1,0:T(8,128)(2,1)S(1)}, u32[]{:S(2)}, u32[]{:S(2)}) async-start(bf16[4,8,176,128]{3,2,1,0:T(8,128)(2,1)} %broadcast_in_dim.11), calls=%async_computation.4 | async-start | bytes 2883584 | tf_op jit(solution)/shard_map/all_to_all | solution.py:176
  76.3 7.0 %collective-permute-start.1 = (bf16[8,64,128]{2,1,0:T(8,128)(2,1)S(1)}, bf16[8,64,128]{2,1,0:T(8,128)(2,1)S(1)}, u32[]{:S(2)}, u32[]{:S(2)}) collective-permute-start(bf16[8,64,128]{2,1,0:T(8,128)(2,1)S(1)} %get-tuple-element.7.own.refs_5_), channel_id=1, source_target_pairs={{4,0},{8,4},{12,8},{16,12},{20,16},{24,20},{28,24},{5,1},{9,5},{13... | collective-permute-start | bytes 393224 | tf_op jit(solution)/shard_map/ppermute | solution.py:164
  79.5 7.5 %collective-permute-start = (bf16[8,64,128]{2,1,0:T(8,128)(2,1)S(1)}, bf16[8,64,128]{2,1,0:T(8,128)(2,1)S(1)}, u32[]{:S(2)}, u32[]{:S(2)}) collective-permute-start(bf16[8,64,128]{2,1,0:T(8,128)(2,1)S(1)} %get-tuple-element.7.own.refs_5_), channel_id=1, source_target_pairs={{0,4},{4,8},{8,12},{12,16},{16,20},{20,24},{24,28},{1,5},{5,9},{9,... | collective-permute-start | bytes 393224 | tf_op jit(solution)/shard_map/ppermute | solution.py:164
  87.1 6.3 %collective-permute-start.2 = (bf16[3,64,128]{2,1,0:T(8,128)(2,1)S(1)}, bf16[3,64,128]{2,1,0:T(8,128)(2,1)S(1)}, u32[]{:S(2)}, u32[]{:S(2)}) collective-permute-start(bf16[3,64,128]{2,1,0:T(8,128)(2,1)S(1)} %pad_maximum_fusion), channel_id=1, source_target_pairs={{0,1},{1,2},{2,3},{4,5},{5,6},{6,7},{8,9},{9,10},{10,11},{12,13},{... | collective-permute-start | bytes 147464 | tf_op jit(solution)/shard_map/ppermute | solution.py:164
  91.5 5.4 %collective-permute-start.3 = (bf16[3,64,128]{2,1,0:T(8,128)(2,1)S(1)}, bf16[3,64,128]{2,1,0:T(8,128)(2,1)S(1)}, u32[]{:S(2)}, u32[]{:S(2)}) collective-permute-start(bf16[3,64,128]{2,1,0:T(8,128)(2,1)S(1)} %pad_maximum_fusion.1), channel_id=1, source_target_pairs={{1,0},{2,1},{3,2},{5,4},{6,5},{7,6},{9,8},{10,9},{11,10},{13,12},{... | collective-permute-start | bytes 147464 | tf_op jit(solution)/shard_map/ppermute | solution.py:164

commit v4 on v3

v4 whole, which is shorter than its diff:
```python
import math

import jax
import jax.numpy as jnp
from jax import lax
from jax.experimental import pallas as pl
from jax.experimental.pallas import tpu as pltpu
from jax.sharding import PartitionSpec as P

F32 = jnp.float32
BF16 = jnp.bfloat16
VMEM_LIMIT = 40 * 1024 * 1024


def call(kernel, out_shape, *operands, scratch=()):
    return pl.pallas_call(
        kernel,
        out_shape=out_shape,
        scratch_shapes=list(scratch),
        compiler_params=pltpu.CompilerParams(vmem_limit_bytes=VMEM_LIMIT),
    )(*operands)


def shifted(cells, step):
    if step == 0:
        return cells
    cols = cells.shape[1]
    moved = pltpu.roll(cells, step % cols, 1)
    col = lax.broadcasted_iota(jnp.int32, cells.shape, 1)
    keep = col >= step if step > 0 else col < cols + step
    return jnp.where(keep, moved, 0.0)


def pack_kernel(n_gy, deep, level, deep_out, level_out):
    planes, cells, share = deep.shape
    for plane in range(planes):
        turned = deep[plane].astype(F32).T.astype(BF16)
        deep_out[2 * plane] = turned
        deep_out[2 * plane + 1] = turned
    turned = level[...].astype(F32).T.astype(BF16)
    part = turned.shape[0] // n_gy
    for owner in range(n_gy):
        level_out[owner] = turned[owner * part : (owner + 1) * part]


def mask_kernel(n_gy, pre, skip, deep_t, weight, out):
    rows, cols, channels = pre.shape
    half = rows // 2
    deep_cols = cols // 2
    cells = half * cols
    deep_cells = half * deep_cols
    wide = lax.broadcasted_iota(jnp.int32, (deep_cells, cells), 1) // 2
    deep = lax.broadcasted_iota(jnp.int32, (deep_cells, cells), 0)
    repeat = (wide == deep).astype(BF16)
    spread = jnp.dot(deep_t[...], repeat, preferred_element_type=F32).astype(BF16)
    col = lax.broadcasted_iota(jnp.int32, (cells, channels), 0) % 2
    down = []
    for b in range(2):
        parts = [
            lax.dot_general(
                spread, weight[b, c], (((0,), (1,)), ((), ())), preferred_element_type=F32
            )
            for c in range(2)
        ]
        part = jnp.where(col == 0, parts[0], parts[1]).reshape(half, cols, channels)
        for y in range(half):
            row = 2 * y + b
            pre_row = pre[row].astype(F32)
            total = part[y] + skip[row].astype(F32)
            grad = jnp.where(pre_row > 0, total, 0.0).astype(BF16)
            for owner in range(n_gy):
                out[owner, pl.ds(row * cols, cols)] = grad
        hidden = jnp.concatenate(
            [jnp.maximum(pre[2 * y + b].astype(F32), 0.0) for y in range(half)], axis=0
        )
        for c in range(2):
            one = jnp.where(col == c, hidden, 0.0).astype(BF16)
            down.append(
                lax.dot_general(
                    one, spread, (((0,), (1,)), ((), ())), preferred_element_type=F32
                ).astype(BF16)
            )
    down = jnp.concatenate(down, axis=0)
    count = down.shape[0] // n_gy
    for owner in range(n_gy):
        for half_part in range(down.shape[1] // channels):
            out[owner, pl.ds(rows * cols + half_part * count, count)] = down[
                owner * count : (owner + 1) * count,
                half_part * channels : (half_part + 1) * channels,
            ]


def segments(rows, piece, unit):
    row = 0
    while row < rows:
        take = min(rows - row, unit - row % unit, piece - row % piece)
        yield row, row // piece, row % piece, take
        row += take


def weight_kernel(conv_rows, down_rows, shape, z_low, own, z_high, shared, out, near, wide):
    rows, cols, channels = shape
    n_gy, part, cells = own.shape
    n_gz = out.shape[0]
    rows_all = n_gy * rows
    for edge in (0, rows_all + 1):
        wide[edge] = jnp.zeros(wide.shape[1:], BF16)
    for owner in range(n_gy):
        grads = shared[owner, pl.ds(0, cells)].reshape(rows, cols, channels)
        grads = grads.astype(F32)
        for kx in range(3):
            wide[pl.ds(1 + owner * rows, rows), :, pl.ds(kx * channels, channels)] = shifted(
                grads, kx - 1
            ).astype(BF16)
    mine = lax.axis_index("gy") * rows
    near[...] = wide[pl.ds(mine, rows + 2), :, pl.ds(channels, channels)]
    level = jnp.concatenate(
        [
            jnp.concatenate([ref[owner] for owner in range(n_gy)], axis=1)
            for ref in (z_low, own, z_high)
        ],
        axis=0,
    )
    for ky in range(3):
        slab = wide[pl.ds(2 - ky, rows_all)].reshape(rows_all * cols, 3 * channels)
        total = jnp.dot(level, slab, preferred_element_type=F32).astype(BF16)
        for kz in range(3):
            for kx in range(3):
                first = ((kz * 3 + ky) * 3 + kx) * part
                value = total[kz * part : (kz + 1) * part, kx * channels : (kx + 1) * channels]
                for row in range(0, part, 16):
                    owner, inner = divmod(first + row, conv_rows)
                    out[owner, pl.ds(inner, 16)] = value[row : row + 16]
    for row in range(27 * part, n_gz * conv_rows, 16):
        owner, inner = divmod(row, conv_rows)
        out[owner, pl.ds(inner, 16)] = jnp.zeros((16, channels), BF16)
    down = shared[0, pl.ds(cells, shared.shape[1] - cells)].astype(F32)
    for owner in range(1, n_gy):
        down = down + shared[owner, pl.ds(cells, shared.shape[1] - cells)].astype(F32)
    down = down.astype(BF16)
    for row in range(0, n_gz * down_rows, 16):
        owner, inner = divmod(row, down_rows)
        value = down[row : row + 16] if row < down.shape[0] else jnp.zeros((16, channels), BF16)
        out[owner, pl.ds(conv_rows + inner, 16)] = value


def input_kernel(z_low, own, z_high, weight, out):
    rows, cols, channels = out.shape
    planes = (z_low, own, z_high)
    total = None
    for kz in range(3):
        for ky in range(3):
            slab = planes[2 - kz][pl.ds(2 - ky, rows)].reshape(rows * cols, channels)
            term = lax.dot_general(
                slab,
                weight[kz, ky].reshape(3 * channels, channels),
                (((1,), (1,)), ((), ())),
                preferred_element_type=F32,
            )
            total = term if total is None else total + term
    answer = None
    for kx in range(3):
        part = total[:, kx * channels : (kx + 1) * channels].reshape(rows, cols, channels)
        part = shifted(part, kx - 1)
        answer = part if answer is None else answer + part
    out[...] = answer.astype(BF16)


def place_kernel(conv_rows, down_rows, blocks, conv, down):
    me = lax.axis_index("gy")
    part = conv.shape[2]
    count, deep_channels = down.shape[2:]
    channels = conv.shape[3]
    for code, block in blocks:
        column = jnp.bitwise_xor(me, code)
        for row, owner, inner, take in segments(27 * part, conv_rows, part):
            conv[row // part, column, pl.ds(row % part, take)] = block[owner, pl.ds(inner, take)]
        for a in range(2):
            base = conv_rows + a * down_rows
            for half in range(deep_channels // channels):
                for row, _, _, take in segments(count, down_rows, down_rows):
                    owner, inner = divmod(half * count + row, down_rows)
                    down[a, column, pl.ds(row, take), pl.ds(half * channels, channels)] = block[
                        owner, pl.ds(base + inner, take)
                    ]


def along(value, axis, up):
    pairs = [(i, i + 1) if up else (i + 1, i) for i in range(lax.axis_size(axis) - 1)]
    return lax.ppermute(value, axis, pairs)


def swapped(value, axis, code):
    return lax.ppermute(value, axis, [(i, i ^ code) for i in range(lax.axis_size(axis))])


def everywhere(value, axis):
    copies = jnp.broadcast_to(value[None], (lax.axis_size(axis),) + value.shape)
    return exchanged(copies, axis)


def exchanged(value, axis):
    return lax.all_to_all(value, axis, split_axis=0, concat_axis=0, tiled=True)


def per_device(
    level_input, pre_activation, conv_weight, down_weight, skip_cotangent, deep_cotangent
):
    n_gz = lax.axis_size("gz")
    n_gy = lax.axis_size("gy")
    _, rows, cols, channels = level_input.shape
    planes, deep_rows, deep_cols, share = deep_cotangent.shape
    deep_channels = down_weight.shape[4]
    parity = lax.axis_index("gz") % 2
    devices = n_gz * n_gy
    part = channels // n_gy
    cells = rows * cols
    deep_cells = deep_rows * deep_cols
    conv_rows = -(-27 * part // (n_gz * 16)) * 16
    down_count = 4 * deep_channels // n_gy
    down_rows = -(-down_count // (n_gz * 16)) * 16
    shape = jax.ShapeDtypeStruct

    level = level_input.reshape(cells, channels)
    deep = deep_cotangent.reshape(planes, deep_cells, share)
    if share % 16 == 0:
        deep_t, level_t = call(
            lambda *refs: pack_kernel(n_gy, *refs),
            (
                shape((2 * planes, share, deep_cells), BF16),
                shape((n_gy, part, cells), BF16),
            ),
            deep,
            level,
        )
    else:
        deep_t = jnp.repeat(jnp.swapaxes(deep, 1, 2), 2, axis=0)
        level_t = level.T.reshape(n_gy, part, cells)
    deep_t = exchanged(deep_t, "gz").reshape(deep_channels, deep_cells)
    level_t = exchanged(level_t, "gy")
    down_slice = lax.dynamic_index_in_dim(down_weight, parity, 0, keepdims=False)
    shared = call(
        lambda *refs: mask_kernel(n_gy, *refs),
        shape((n_gy, cells + down_count, channels), BF16),
        pre_activation[0],
        skip_cotangent[0],
        deep_t,
        down_slice,
    )
    shared = exchanged(shared, "gy")
    parts, near = call(
        lambda *refs: weight_kernel(conv_rows, down_rows, (rows, cols, channels), *refs),
        (
            shape((n_gz, conv_rows + down_rows, channels), BF16),
            shape((rows + 2, cols, channels), BF16),
        ),
        along(level_t, "gz", True),
        level_t,
        along(level_t, "gz", False),
        shared,
        scratch=[pltpu.VMEM((n_gy * rows + 2, cols, 3 * channels), BF16)],
    )
    parts = exchanged(parts, "gz").astype(F32)
    cell_total = devices * cells
    conv_sum = jnp.sum(parts[:, :conv_rows], axis=0) / math.sqrt(cell_total)
    slots = parts[:, conv_rows:].reshape(n_gz // 2, 2, down_rows, channels)
    down_sum = jnp.sum(slots, axis=0) / math.sqrt(cell_total // 8)
    final = jnp.concatenate([conv_sum, down_sum.reshape(2 * down_rows, channels)], axis=0)
    block = everywhere(final.astype(BF16), "gz")
    if n_gy == 4:
        across = swapped(block, "gy", 2)
        blocks = {0: block, 1: swapped(block, "gy", 1), 2: across, 3: swapped(across, "gy", 1)}
    else:
        blocks = {code: swapped(block, "gy", code) for code in range(n_gy)}
    conv_grad, down_grad = call(
        lambda *refs: place_kernel(conv_rows, down_rows, list(zip(blocks, refs)), *refs[n_gy:]),
        (
            shape((27, n_gy, part, channels), BF16),
            shape((2, n_gy, 4 * channels // n_gy, deep_channels), BF16),
        ),
        *blocks.values(),
    )
    input_grad = call(
        input_kernel,
        shape((rows, cols, channels), BF16),
        along(near, "gz", True),
        near,
        along(near, "gz", False),
        conv_weight,
    )
    return (
        input_grad[None],
        conv_grad.reshape(conv_weight.shape),
        down_grad.reshape(down_weight.shape),
    )


def solution(mesh):
    return jax.shard_map(
        per_device,
        mesh=mesh,
        in_specs=(
            P("gz", "gy", None, None),
            P("gz", "gy", None, None),
            P(),
            P(),
            P("gz", "gy", None, None),
            P(None, "gy", None, "gz"),
        ),
        out_specs=(P("gz", "gy", None, None), P(), P()),
        check_vma=False,
    )
```

time: 101 us -> 92.7 us (0.918)
  the two profiles are of different devices: /device:TPU:9 before, /device:TPU:0 now
where the time goes in v4:
time: 92.7 us; the launch traced here: 92.1 us
  waiting for transfers between devices  28.2 us (30%)
  blocking collectives  27 us (29%)
  starting transfers between devices  26.8 us (29%)
  Pallas kernels  6.41 us (7%)
  local copies, waits for them, and re-layouts  2.88 us (3%)
    all_to_all x2, blocking collectives, exchanged(): return lax.all_to_all(value, axis, split_axis=0, concat_axis=0, tiled=True)  27 us
    all_to_all x3, starting transfers between devices, exchanged(): return lax.all_to_all(value, axis, split_axis=0, concat_axis=0, tiled=True)  14.1 us
    ppermute x4, starting transfers between devices, along(): return lax.ppermute(value, axis, pairs)  11.8 us
    all_to_all x3, waiting for transfers between devices, exchanged(): return lax.all_to_all(value, axis, split_axis=0, concat_axis=0, tiled=True)  11.3 us
    ppermute x4, waiting for transfers between devices, along(): return lax.ppermute(value, axis, pairs)  10.1 us
    ppermute x3, waiting for transfers between devices, swapped(): lax.ppermute(value, axis, [(i, i ^ code) for i in range(lax.axis_size(axi...  6.72 us
    pallas_call x5, Pallas kernels, call(): pl.pallas_call(kernel, out_shape=out_shape, scratch_shapes=list(scratch),...  6.41 us
    unnamed x12, local copies, waits for them, and re-layouts  2.8 us
  transfers between devices with their start and end apart: 10, of which 8 were waited for; matrix products, arithmetic and copies ran while one was open for 0% of the time, Pallas kernels for 3%

profile of v4, /device:TPU:0, one launch (start us, length us, event | category | flops | bytes accessed | tf_op | source)
XLA Modules:
  0.0 92.1 jit_solution(18371769224049758150)
XLA Ops:
  0.6 0.0 copy-start
  0.6 0.0 copy-start.2
  0.7 1.0 %copy-done.2 = bf16[4,4,32,32]{3,2,1,0:T(8,128)(2,1)S(1)} copy-done((bf16[4,4,32,32]{3,2,1,0:T(8,128)(2,1)S(1)}, bf16[4,4,32,32]{3,2,1,0:T(8,128)(2,1)}, u32[]{:S(2)}) %copy-start.2) | copy-done | bytes 32792
  1.6 0.0 copy-start.3
  1.6 0.9 copy-done.3
  2.5 0.8 shard_map.85
  3.3 7.3 %all-to-all-start.1 = ((bf16[8,32,128]{2,1,0:T(8,128)(2,1)}), bf16[8,32,128]{2,1,0:T(8,128)(2,1)S(1)}, u32[]{:S(2)}, u32[]{:S(2)}) async-start(bf16[8,32,128]{2,1,0:T(8,128)(2,1)} %get-tuple-element.10), calls=%async_computation.1 | async-start | bytes 131072 | tf_op jit(solution)/shard_map/all_to_all | solution.py:203
  10.6 6.9 %all-to-all-done.1 = bf16[8,32,128]{2,1,0:T(8,128)(2,1)S(1)} async-done(((bf16[8,32,128]{2,1,0:T(8,128)(2,1)}), bf16[8,32,128]{2,1,0:T(8,128)(2,1)S(1)}, u32[]{:S(2)}, u32[]{:S(2)}) %all-to-all-start.1) | async-done | bytes 65568 | tf_op jit(solution)/shard_map/all_to_all | solution.py:203
  17.5 3.3 %all-to-all-start = ((bf16[4,32,512]{2,1,0:T(8,128)(2,1)}), bf16[4,32,512]{2,1,0:T(8,128)(2,1)S(1)}, u32[]{:S(2)}, u32[]{:S(2)}) async-start(bf16[4,32,512]{2,1,0:T(8,128)(2,1)} %get-tuple-element.9), calls=%async_computation | async-start | bytes 262144 | tf_op jit(solution)/shard_map/all_to_all | solution.py:203
  20.8 0.0 copy-done
  20.8 0.0 copy-start.4
  20.9 0.0 copy-start.5
  20.9 0.9 copy-done.4
  21.7 0.1 copy-done.5
  21.8 1.4 %shard_map.86 = bf16[4,768,128]{2,1,0:T(8,128)(2,1)} custom-call(bf16[8,64,128]{2,1,0:T(8,128)(2,1)S(1)} %bitcast.15, bf16[8,64,128]{2,1,0:T(8,128)(2,1)S(1)} %bitcast.16, bf16[256,128]{1,0:T(8,128)(2,1)S(1)} %bitcast.12, bf16[2,2,128,256]{3,2,1,0:T(8,128)(2,1)S(1)} %dynamic-slice_bitcast_fusion.refs_3_), custom_call_target="tpu_custom_call" | custom-call | tf_op jit(solution)/shard_map/pallas_call | solution.py:16
  23.3 2.2 %all-to-all-done.refs_1_ = bf16[4,32,512]{2,1,0:T(8,128)(2,1)S(1)} async-done(((bf16[4,32,512]{2,1,0:T(8,128)(2,1)}), bf16[4,32,512]{2,1,0:T(8,128)(2,1)S(1)}, u32[]{:S(2)}, u32[]{:S(2)}) %all-to-all-start) | async-done | bytes 131104 | tf_op jit(solution)/shard_map/all_to_all | solution.py:203
  25.4 3.5 %all-to-all-start.2 = ((bf16[4,768,128]{2,1,0:T(8,128)(2,1)}), bf16[4,768,128]{2,1,0:T(8,128)(2,1)S(1)}, u32[]{:S(2)}, u32[]{:S(2)}) async-start(bf16[4,768,128]{2,1,0:T(8,128)(2,1)} %shard_map.86), calls=%async_computation.2 | async-start | bytes 1572864 | tf_op jit(solution)/shard_map/all_to_all | solution.py:203
  28.9 1.3 %collective-permute-start.1 = (bf16[4,32,512]{2,1,0:T(8,128)(2,1)S(1)}, bf16[4,32,512]{2,1,0:T(8,128)(2,1)S(1)}, u32[]{:S(2)}, u32[]{:S(2)}) collective-permute-start(bf16[4,32,512]{2,1,0:T(8,128)(2,1)S(1)} %all-to-all-done.refs_1_), channel_id=1, source_target_pairs={{4,0},{8,4},{12,8},{16,12},{20,16},{24,20},{28,24},{5,1},{9,5},{13... | collective-permute-start | bytes 393224 | tf_op jit(solution)/shard_map/ppermute | solution.py:190
  30.2 4.6 %collective-permute-start = (bf16[4,32,512]{2,1,0:T(8,128)(2,1)S(1)}, bf16[4,32,512]{2,1,0:T(8,128)(2,1)S(1)}, u32[]{:S(2)}, u32[]{:S(2)}) collective-permute-start(bf16[4,32,512]{2,1,0:T(8,128)(2,1)S(1)} %all-to-all-done.refs_1_), channel_id=1, source_target_pairs={{0,4},{4,8},{8,12},{12,16},{16,20},{20,24},{24,28},{1,5},{5,9},{9,... | collective-permute-start | bytes 393224 | tf_op jit(solution)/shard_map/ppermute | solution.py:190
  34.8 1.9 %collective-permute-done.1.refs_2_ = bf16[4,32,512]{2,1,0:T(8,128)(2,1)S(1)} collective-permute-done((bf16[4,32,512]{2,1,0:T(8,128)(2,1)S(1)}, bf16[4,32,512]{2,1,0:T(8,128)(2,1)S(1)}, u32[]{:S(2)}, u32[]{:S(2)}) %collective-permute-start.1) | collective-permute-done | bytes 131104 | tf_op jit(solution)/shard_map/ppermute | solution.py:190
  36.7 1.6 %collective-permute-done.refs_0_ = bf16[4,32,512]{2,1,0:T(8,128)(2,1)S(1)} collective-permute-done((bf16[4,32,512]{2,1,0:T(8,128)(2,1)S(1)}, bf16[4,32,512]{2,1,0:T(8,128)(2,1)S(1)}, u32[]{:S(2)}, u32[]{:S(2)}) %collective-permute-start) | collective-permute-done | bytes 131104 | tf_op jit(solution)/shard_map/ppermute | solution.py:190
  38.3 2.3 %all-to-all-done.2.refs_3_ = bf16[4,768,128]{2,1,0:T(8,128)(2,1)S(1)} async-done(((bf16[4,768,128]{2,1,0:T(8,128)(2,1)}), bf16[4,768,128]{2,1,0:T(8,128)(2,1)S(1)}, u32[]{:S(2)}, u32[]{:S(2)}) %all-to-all-start.2) | async-done | bytes 786464 | tf_op jit(solution)/shard_map/all_to_all | solution.py:203
  40.5 1.2 %shard_map.87 = (bf16[8,144,128]{2,1,0:T(8,128)(2,1)S(1)}, bf16[10,64,128]{2,1,0:T(8,128)(2,1)S(1)}) custom-call(bf16[4,32,512]{2,1,0:T(8,128)(2,1)S(1)} %collective-permute-done.refs_0_, bf16[4,32,512]{2,1,0:T(8,128)(2,1)S(1)} %all-to-all-done.refs_1_, bf16[4,32,512]{2,1,0:T(8,128)(2,1)S(1)} %collective-permute-done.1.refs_2_, ...), custom_call_target="tpu_custom_call" | custom-call | tf_op jit(solution)/shard_map/pallas_call | solution.py:16
  41.8 12.8 %all_to_all.25 = bf16[8,144,128]{2,1,0:T(8,128)(2,1)S(1)} all-to-all(bf16[8,144,128]{2,1,0:T(8,128)(2,1)S(1)} %get-tuple-element.12), channel_id=1, replica_groups=mesh['gz'=8,'gy'=4] {'gz'}, dimensions={0} | all-to-all | bytes 589824 | tf_op jit(solution)/shard_map/all_to_all | solution.py:203
  54.7 0.0 copy-start.1
  54.8 14.2 %all_to_all.26.refs_0_ = bf16[8,176,128]{2,1,0:T(8,128)(2,1)S(1)} all-to-all(bf16[8,176,128]{2,1,0:T(8,128)(2,1)S(1)} %broadcast_in_dim.10), channel_id=1, replica_groups=mesh['gz'=8,'gy'=4] {'gz'}, dimensions={0} | all-to-all | bytes 720896 | tf_op jit(solution)/shard_map/all_to_all | solution.py:203
  69.0 0.8 collective-permute-start.5
  69.8 0.0 collective-permute-start.4
  69.8 6.7 %collective-permute-done.5.refs_2_ = bf16[8,176,128]{2,1,0:T(8,128)(2,1)S(1)} collective-permute-done((bf16[8,176,128]{2,1,0:T(8,128)(2,1)S(1)}, bf16[8,176,128]{2,1,0:T(8,128)(2,1)S(1)}, u32[]{:S(2)}, u32[]{:S(2)}) %collective-permute-start.5) | collective-permute-done | bytes 360480 | tf_op jit(solution)/shard_map/ppermute | solution.py:194
  76.5 0.0 collective-permute-start.6
  76.5 1.3 %collective-permute-start.3 = (bf16[10,64,128]{2,1,0:T(8,128)(2,1)S(1)}, bf16[10,64,128]{2,1,0:T(8,128)(2,1)S(1)}, u32[]{:S(2)}, u32[]{:S(2)}) collective-permute-start(bf16[10,64,128]{2,1,0:T(8,128)(2,1)S(1)} %get-tuple-element.11.own), channel_id=1, source_target_pairs={{4,0},{8,4},{12,8},{16,12},{20,16},{24,20},{28,24},{5,1},{9,5},{13... | collective-permute-start | bytes 491528 | tf_op jit(solution)/shard_map/ppermute | solution.py:190
  77.8 4.7 %collective-permute-start.2 = (bf16[10,64,128]{2,1,0:T(8,128)(2,1)S(1)}, bf16[10,64,128]{2,1,0:T(8,128)(2,1)S(1)}, u32[]{:S(2)}, u32[]{:S(2)}) collective-permute-start(bf16[10,64,128]{2,1,0:T(8,128)(2,1)S(1)} %get-tuple-element.11.own), channel_id=1, source_target_pairs={{0,4},{4,8},{8,12},{12,16},{16,20},{20,24},{24,28},{1,5},{5,9},{9,... | collective-permute-start | bytes 491528 | tf_op jit(solution)/shard_map/ppermute | solution.py:190
  82.5 2.9 %collective-permute-done.3.z_high = bf16[10,64,128]{2,1,0:T(8,128)(2,1)S(1)} collective-permute-done((bf16[10,64,128]{2,1,0:T(8,128)(2,1)S(1)}, bf16[10,64,128]{2,1,0:T(8,128)(2,1)S(1)}, u32[]{:S(2)}, u32[]{:S(2)}) %collective-permute-start.3) | collective-permute-done | bytes 163872 | tf_op jit(solution)/shard_map/ppermute | solution.py:190
  85.4 3.7 %collective-permute-done.2.z_low = bf16[10,64,128]{2,1,0:T(8,128)(2,1)S(1)} collective-permute-done((bf16[10,64,128]{2,1,0:T(8,128)(2,1)S(1)}, bf16[10,64,128]{2,1,0:T(8,128)(2,1)S(1)}, u32[]{:S(2)}, u32[]{:S(2)}) %collective-permute-start.2) | collective-permute-done | bytes 163872 | tf_op jit(solution)/shard_map/ppermute | solution.py:190
  89.1 0.0 copy-done.1
  89.1 1.7 %shard_map.88 = bf16[8,64,128]{2,1,0:T(8,128)(2,1)} custom-call(bf16[10,64,128]{2,1,0:T(8,128)(2,1)S(1)} %collective-permute-done.2.z_low, bf16[10,64,128]{2,1,0:T(8,128)(2,1)S(1)} %get-tuple-element.11.own, bf16[10,64,128]{2,1,0:T(8,128)(2,1)S(1)} %collective-permute-done.3.z_high, bf16[3,3,3,128,128]{4,3,2,1,0:T(8,128)(2,1)S(1)} %copy-done.1), custom_call_target="tpu_custom_call" | custom-call | tf_op jit(solution)/shard_map/pallas_call | solution.py:16
  90.9 0.0 collective-permute-done.4.refs_1_
  90.9 0.0 collective-permute-done.6.refs_3_
  90.9 1.2 %shard_map.89 = (bf16[27,4,32,128]{3,2,1,0:T(8,128)(2,1)}, bf16[2,4,128,256]{3,2,1,0:T(8,128)(2,1)}) custom-call(bf16[8,176,128]{2,1,0:T(8,128)(2,1)S(1)} %all_to_all.26.refs_0_, bf16[8,176,128]{2,1,0:T(8,128)(2,1)S(1)} %collective-permute-done.4.refs_1_, bf16[8,176,128]{2,1,0:T(8,128)(2,1)S(1)} %collective-permute-done.5.refs_2_, ...), custom_call_target="tpu_custom_call" | custom-call | tf_op jit(solution)/shard_map/pallas_call | solution.py:16
  (9 shorter events, 0.2 us)
Async XLA Ops:
  0.6 20.2 %copy-start = (bf16[2,2,2,128,256]{4,3,2,1,0:T(8,128)(2,1)S(1)}, bf16[2,2,2,128,256]{4,3,2,1,0:T(8,128)(2,1)}, u32[]{:S(2)}) copy-start(bf16[2,2,2,128,256]{4,3,2,1,0:T(8,128)(2,1)} %param.9) | copy-start | bytes 1572868
  0.6 1.0 %copy-start.2 = (bf16[4,4,32,32]{3,2,1,0:T(8,128)(2,1)S(1)}, bf16[4,4,32,32]{3,2,1,0:T(8,128)(2,1)}, u32[]{:S(2)}) copy-start(bf16[4,4,32,32]{3,2,1,0:T(8,128)(2,1)} %param.11) | copy-start | bytes 98308
  1.6 0.9 copy-start.3
  3.3 14.2 %all-to-all-start.1 = ((bf16[8,32,128]{2,1,0:T(8,128)(2,1)}), bf16[8,32,128]{2,1,0:T(8,128)(2,1)S(1)}, u32[]{:S(2)}, u32[]{:S(2)}) async-start(bf16[8,32,128]{2,1,0:T(8,128)(2,1)} %get-tuple-element.10), calls=%async_computation.1 | async-start | bytes 131072 | tf_op jit(solution)/shard_map/all_to_all | solution.py:203
  17.5 7.9 %all-to-all-start = ((bf16[4,32,512]{2,1,0:T(8,128)(2,1)}), bf16[4,32,512]{2,1,0:T(8,128)(2,1)S(1)}, u32[]{:S(2)}, u32[]{:S(2)}) async-start(bf16[4,32,512]{2,1,0:T(8,128)(2,1)} %get-tuple-element.9), calls=%async_computation | async-start | bytes 262144 | tf_op jit(solution)/shard_map/all_to_all | solution.py:203
  20.8 0.9 copy-start.4
  20.9 1.0 %copy-start.5 = (bf16[1,8,64,128]{3,2,1,0:T(8,128)(2,1)S(1)}, bf16[1,8,64,128]{3,2,1,0:T(8,128)(2,1)}, u32[]{:S(2)}) copy-start(bf16[1,8,64,128]{3,2,1,0:T(8,128)(2,1)} %param.10) | copy-start | bytes 393220
  25.4 15.1 %all-to-all-start.2 = ((bf16[4,768,128]{2,1,0:T(8,128)(2,1)}), bf16[4,768,128]{2,1,0:T(8,128)(2,1)S(1)}, u32[]{:S(2)}, u32[]{:S(2)}) async-start(bf16[4,768,128]{2,1,0:T(8,128)(2,1)} %shard_map.86), calls=%async_computation.2 | async-start | bytes 1572864 | tf_op jit(solution)/shard_map/all_to_all | solution.py:203
  28.9 7.8 %collective-permute-start.1 = (bf16[4,32,512]{2,1,0:T(8,128)(2,1)S(1)}, bf16[4,32,512]{2,1,0:T(8,128)(2,1)S(1)}, u32[]{:S(2)}, u32[]{:S(2)}) collective-permute-start(bf16[4,32,512]{2,1,0:T(8,128)(2,1)S(1)} %all-to-all-done.refs_1_), channel_id=1, source_target_pairs={{4,0},{8,4},{12,8},{16,12},{20,16},{24,20},{28,24},{5,1},{9,5},{13... | collective-permute-start | bytes 393224 | tf_op jit(solution)/shard_map/ppermute | solution.py:190
  30.2 8.1 %collective-permute-start = (bf16[4,32,512]{2,1,0:T(8,128)(2,1)S(1)}, bf16[4,32,512]{2,1,0:T(8,128)(2,1)S(1)}, u32[]{:S(2)}, u32[]{:S(2)}) collective-permute-start(bf16[4,32,512]{2,1,0:T(8,128)(2,1)S(1)} %all-to-all-done.refs_1_), channel_id=1, source_target_pairs={{0,4},{4,8},{8,12},{12,16},{16,20},{20,24},{24,28},{1,5},{5,9},{9,... | collective-permute-start | bytes 393224 | tf_op jit(solution)/shard_map/ppermute | solution.py:190
  54.7 34.5 %copy-start.1 = (bf16[3,3,3,128,128]{4,3,2,1,0:T(8,128)(2,1)S(1)}, bf16[3,3,3,128,128]{4,3,2,1,0:T(8,128)(2,1)}, u32[]{:S(2)}) copy-start(bf16[3,3,3,128,128]{4,3,2,1,0:T(8,128)(2,1)} %weight.1) | copy-start | bytes 2654212
  69.0 7.6 %collective-permute-start.5 = (bf16[8,176,128]{2,1,0:T(8,128)(2,1)S(1)}, bf16[8,176,128]{2,1,0:T(8,128)(2,1)S(1)}, u32[]{:S(2)}, u32[]{:S(2)}) collective-permute-start(bf16[8,176,128]{2,1,0:T(8,128)(2,1)S(1)} %all_to_all.26.refs_0_), channel_id=1, source_target_pairs={{0,2},{1,3},{2,0},{3,1},{4,6},{5,7},{6,4},{7,5},{8,10},{9,11},{10,... | collective-permute-start | bytes 1081352 | tf_op jit(solution)/shard_map/ppermute | solution.py:194
  69.8 21.1 %collective-permute-start.4 = (bf16[8,176,128]{2,1,0:T(8,128)(2,1)S(1)}, bf16[8,176,128]{2,1,0:T(8,128)(2,1)S(1)}, u32[]{:S(2)}, u32[]{:S(2)}) collective-permute-start(bf16[8,176,128]{2,1,0:T(8,128)(2,1)S(1)} %all_to_all.26.refs_0_), channel_id=1, source_target_pairs={{0,1},{1,0},{2,3},{3,2},{4,5},{5,4},{6,7},{7,6},{8,9},{9,8},{10,11... | collective-permute-start | bytes 1081352 | tf_op jit(solution)/shard_map/ppermute | solution.py:194
  76.5 14.3 %collective-permute-start.6 = (bf16[8,176,128]{2,1,0:T(8,128)(2,1)S(1)}, bf16[8,176,128]{2,1,0:T(8,128)(2,1)S(1)}, u32[]{:S(2)}, u32[]{:S(2)}) collective-permute-start(bf16[8,176,128]{2,1,0:T(8,128)(2,1)S(1)} %collective-permute-done.5.refs_2_), channel_id=1, source_target_pairs={{0,1},{1,0},{2,3},{3,2},{4,5},{5,4},{6,7},{7,6},{8,9},{9,8},{10,11... | collective-permute-start | bytes 1081352 | tf_op jit(solution)/shard_map/ppermute | solution.py:194
  76.5 8.9 %collective-permute-start.3 = (bf16[10,64,128]{2,1,0:T(8,128)(2,1)S(1)}, bf16[10,64,128]{2,1,0:T(8,128)(2,1)S(1)}, u32[]{:S(2)}, u32[]{:S(2)}) collective-permute-start(bf16[10,64,128]{2,1,0:T(8,128)(2,1)S(1)} %get-tuple-element.11.own), channel_id=1, source_target_pairs={{4,0},{8,4},{12,8},{16,12},{20,16},{24,20},{28,24},{5,1},{9,5},{13... | collective-permute-start | bytes 491528 | tf_op jit(solution)/shard_map/ppermute | solution.py:190
  77.8 11.3 %collective-permute-start.2 = (bf16[10,64,128]{2,1,0:T(8,128)(2,1)S(1)}, bf16[10,64,128]{2,1,0:T(8,128)(2,1)S(1)}, u32[]{:S(2)}, u32[]{:S(2)}) collective-permute-start(bf16[10,64,128]{2,1,0:T(8,128)(2,1)S(1)} %get-tuple-element.11.own), channel_id=1, source_target_pairs={{0,4},{4,8},{8,12},{12,16},{16,20},{20,24},{24,28},{1,5},{5,9},{9,... | collective-permute-start | bytes 491528 | tf_op jit(solution)/shard_map/ppermute | solution.py:190

commit v5 on v4

v5 whole, which is shorter than its diff:
```python
import math

import jax
import jax.numpy as jnp
from jax import lax
from jax.experimental import pallas as pl
from jax.experimental.pallas import tpu as pltpu
from jax.sharding import PartitionSpec as P

F32 = jnp.float32
BF16 = jnp.bfloat16
VMEM_LIMIT = 40 * 1024 * 1024


def call(kernel, out_shape, *operands, scratch=()):
    return pl.pallas_call(
        kernel,
        out_shape=out_shape,
        scratch_shapes=list(scratch),
        compiler_params=pltpu.CompilerParams(vmem_limit_bytes=VMEM_LIMIT),
    )(*operands)


def shifted(cells, step):
    if step == 0:
        return cells
    cols = cells.shape[1]
    moved = pltpu.roll(cells, step % cols, 1)
    col = lax.broadcasted_iota(jnp.int32, cells.shape, 1)
    keep = col >= step if step > 0 else col < cols + step
    return jnp.where(keep, moved, 0.0)


def pack_kernel(n_gy, turn_deep, deep, level, *rest):
    level_outs, rest = rest[:n_gy], rest[n_gy:]
    turned = level[...].astype(F32).T.astype(BF16)
    part = turned.shape[0] // n_gy
    level_t = rest[-1]
    for owner in range(n_gy):
        level_t[owner] = turned[owner * part : (owner + 1) * part]
    me = lax.axis_index("gy")
    for code in range(n_gy):
        level_outs[code][...] = level_t[jnp.bitwise_xor(me, code)]
    if turn_deep:
        deep_outs, deep_t = rest[:-2], rest[-2]
        for plane in range(deep.shape[0]):
            deep_t[plane] = deep[plane].astype(F32).T.astype(BF16)
        me = lax.axis_index("gz")
        for code in range(len(deep_outs)):
            deep_outs[code][...] = deep_t[jnp.bitwise_xor(me, code) // 2]


def mask_kernel(n_gy, pre, skip, weight, *rest):
    deeps, outs = rest[: -n_gy - 2], rest[-n_gy - 2 : -2]
    deep_t, down_all = rest[-2:]
    share = deeps[0].shape[0]
    if len(deeps) > 1:
        source = lax.axis_index("gz")
        for code, ref in enumerate(deeps):
            first = pl.multiple_of(jnp.bitwise_xor(source, code) * share, share)
            deep_t[pl.ds(first, share)] = ref[...]
    else:
        deep_t[...] = deeps[0][...]
    rows, cols, channels = pre.shape
    half = rows // 2
    deep_cols = cols // 2
    cells = half * cols
    deep_cells = half * deep_cols
    wide = lax.broadcasted_iota(jnp.int32, (deep_cells, cells), 1) // 2
    deep = lax.broadcasted_iota(jnp.int32, (deep_cells, cells), 0)
    repeat = (wide == deep).astype(BF16)
    spread = jnp.dot(deep_t[...], repeat, preferred_element_type=F32).astype(BF16)
    col = lax.broadcasted_iota(jnp.int32, (cells, channels), 0) % 2
    count = down_all.shape[1]
    for b in range(2):
        parts = [
            lax.dot_general(
                spread, weight[b, c], (((0,), (1,)), ((), ())), preferred_element_type=F32
            )
            for c in range(2)
        ]
        part = jnp.where(col == 0, parts[0], parts[1]).reshape(half, cols, channels)
        for y in range(half):
            row = 2 * y + b
            pre_row = pre[row].astype(F32)
            total = part[y] + skip[row].astype(F32)
            grad = jnp.where(pre_row > 0, total, 0.0).astype(BF16)
            for out in outs:
                out[pl.ds(row * cols, cols)] = grad
        hidden = jnp.concatenate(
            [jnp.maximum(pre[2 * y + b].astype(F32), 0.0) for y in range(half)], axis=0
        )
        for c in range(2):
            one = jnp.where(col == c, hidden, 0.0).astype(BF16)
            down = lax.dot_general(
                one, spread, (((0,), (1,)), ((), ())), preferred_element_type=F32
            ).astype(BF16)
            for first, owner, inner, take in segments(channels, count, channels, (b * 2 + c) * channels):
                down_all[owner, pl.ds(inner, take)] = down[first : first + take]
    me = lax.axis_index("gy")
    for code, out in enumerate(outs):
        owner = jnp.bitwise_xor(me, code)
        for side in range(down_all.shape[2] // channels):
            out[pl.ds(rows * cols + side * count, count)] = down_all[
                owner, :, pl.ds(side * channels, channels)
            ]


def segments(rows, piece, unit, base=0):
    row = 0
    while row < rows:
        take = min(rows - row, unit - row % unit, piece - (base + row) % piece)
        yield row, (base + row) // piece, (base + row) % piece, take
        row += take


def sides(even, odd):
    upper = lax.axis_index("gz") % 2 == 0
    low = jnp.where(upper, odd[...].astype(F32), even[...].astype(F32)).astype(BF16)
    high = jnp.where(upper, even[...].astype(F32), odd[...].astype(F32)).astype(BF16)
    return low, high


def weight_kernel(n_gy, conv_rows, down_rows, shape, *refs):
    even, own, odd = refs[:3]
    shared = refs[3 : 3 + n_gy]
    near, wide, level, parts = refs[-4:]
    outs = refs[3 + n_gy : -4]
    rows, cols, channels = shape
    part = own.shape[1]
    cells = rows * cols
    n_gz = parts.shape[0]
    rows_all = n_gy * rows
    me = lax.axis_index("gy")
    low, high = sides(even, odd)
    for edge in (0, rows_all + 1):
        wide[edge] = jnp.zeros(wide.shape[1:], BF16)
    for code in range(n_gy):
        owner = jnp.bitwise_xor(me, code)
        grads = shared[code][pl.ds(0, cells)].reshape(rows, cols, channels).astype(F32)
        for kx in range(3):
            wide[pl.ds(1 + owner * rows, rows), :, pl.ds(kx * channels, channels)] = shifted(
                grads, kx - 1
            ).astype(BF16)
        for kz, plane in enumerate((low[code], own[code], high[code])):
            level[owner, pl.ds(kz * part, part)] = plane
    near[...] = wide[pl.ds(me * rows, rows + 2), :, pl.ds(channels, channels)]
    for ky in range(3):
        total = None
        for owner in range(n_gy):
            slab = wide[pl.ds(2 - ky + owner * rows, rows)].reshape(cells, 3 * channels)
            term = jnp.dot(level[owner], slab, preferred_element_type=F32)
            total = term if total is None else total + term
        total = total.astype(BF16)
        for kz in range(3):
            for kx in range(3):
                value = total[kz * part : (kz + 1) * part, kx * channels : (kx + 1) * channels]
                first = ((kz * 3 + ky) * 3 + kx) * part
                for row, owner, inner, take in segments(part, conv_rows, part, first):
                    parts[owner, pl.ds(inner, take)] = value[row : row + take]
    blank = n_gz * conv_rows - 27 * part
    for row, owner, inner, take in segments(blank, conv_rows, conv_rows, 27 * part):
        parts[owner, pl.ds(inner, take)] = jnp.zeros((take, channels), BF16)
    count = shared[0].shape[0] - cells
    down = shared[0][pl.ds(cells, count)].astype(F32)
    for code in range(1, n_gy):
        down = down + shared[code][pl.ds(cells, count)].astype(F32)
    down = down.astype(BF16)
    for row, owner, inner, take in segments(count, down_rows, count):
        parts[owner, pl.ds(conv_rows + inner, take)] = down[row : row + take]
    blank = n_gz * down_rows - count
    for row, owner, inner, take in segments(blank, down_rows, down_rows, count):
        parts[owner, pl.ds(conv_rows + inner, take)] = jnp.zeros((take, channels), BF16)
    if len(outs) > 1:
        me = lax.axis_index("gz")
        for code, out in enumerate(outs):
            out[...] = parts[jnp.bitwise_xor(me, code)]
    else:
        outs[0][...] = parts[...]


def input_kernel(even, own, odd, weight, out):
    rows, cols, channels = out.shape
    low, high = sides(even, odd)
    planes = (low, own, high)
    total = None
    for kz in range(3):
        for ky in range(3):
            slab = planes[2 - kz][2 - ky : 2 - ky + rows].reshape(rows * cols, channels)
            term = lax.dot_general(
                slab,
                weight[kz, ky].reshape(3 * channels, channels),
                (((1,), (1,)), ((), ())),
                preferred_element_type=F32,
            )
            total = term if total is None else total + term
    answer = None
    for kx in range(3):
        part = total[:, kx * channels : (kx + 1) * channels].reshape(rows, cols, channels)
        part = shifted(part, kx - 1)
        answer = part if answer is None else answer + part
    out[...] = answer.astype(BF16)


def reversed_bits(code, count):
    place, bit = 0, 1
    while bit < count:
        place = place * 2 + code // bit % 2
        bit *= 2
    return place


def place_kernel(n_gy, conv_rows, down_rows, *refs):
    blocks, (conv, down) = refs[:n_gy], refs[n_gy:]
    me = lax.axis_index("gy")
    line = lax.axis_index("gz")
    part = conv.shape[2]
    count, deep_channels = down.shape[2:]
    channels = conv.shape[3]
    n_gz = blocks[0].shape[0]
    places = [reversed_bits(jnp.bitwise_xor(line, owner), n_gz) for owner in range(n_gz)]
    for code, block in enumerate(blocks):
        column = jnp.bitwise_xor(me, code)
        for row, owner, inner, take in segments(27 * part, conv_rows, part):
            conv[row // part, column, pl.ds(row % part, take)] = block[
                places[owner], pl.ds(inner, take)
            ]
        for a in range(2):
            base = conv_rows + a * down_rows
            for side in range(deep_channels // channels):
                for row, owner, inner, take in segments(count, down_rows, count, side * count):
                    down[a, column, pl.ds(row, take), pl.ds(side * channels, channels)] = block[
                        places[owner], pl.ds(base + inner, take)
                    ]


def swapped(value, axis, code):
    return lax.ppermute(value, axis, [(i, i ^ code) for i in range(lax.axis_size(axis))])


def neighbours(value):
    last = lax.axis_size("gz") - 1
    odd = [(i + d, i + 1 - d) for i in range(1, last, 2) for d in range(2)]
    return swapped(value, "gz", 1), lax.ppermute(value, "gz", odd)


def exchanged(value, axis):
    return lax.all_to_all(value, axis, split_axis=0, concat_axis=0, tiled=True)


def per_device(
    level_input, pre_activation, conv_weight, down_weight, skip_cotangent, deep_cotangent
):
    n_gz = lax.axis_size("gz")
    n_gy = lax.axis_size("gy")
    _, rows, cols, channels = level_input.shape
    planes, deep_rows, deep_cols, share = deep_cotangent.shape
    deep_channels = down_weight.shape[4]
    parity = lax.axis_index("gz") % 2
    devices = n_gz * n_gy
    part = channels // n_gy
    cells = rows * cols
    deep_cells = deep_rows * deep_cols
    conv_rows = -(-27 * part // (n_gz * 16)) * 16
    down_count = 4 * deep_channels // n_gy
    down_rows = -(-down_count // (n_gz * 16)) * 16
    piece = conv_rows + down_rows
    direct = n_gz <= 8
    shape = jax.ShapeDtypeStruct

    level = level_input.reshape(cells, channels)
    deep = deep_cotangent.reshape(planes, deep_cells, share)
    packed = call(
        lambda *refs: pack_kernel(n_gy, direct, *refs),
        [shape((part, cells), BF16)] * n_gy
        + ([shape((share, deep_cells), BF16)] * n_gz if direct else []),
        deep,
        level,
        scratch=([pltpu.VMEM((planes, share, deep_cells), BF16)] if direct else [])
        + [pltpu.VMEM((n_gy, part, cells), BF16)],
    )
    level_t, deep_t = packed[:n_gy], packed[n_gy:]
    if direct:
        deep_t = [swapped(value, "gz", code) if code else value for code, value in enumerate(deep_t)]
    else:
        turned = jnp.repeat(jnp.swapaxes(deep, 1, 2), 2, axis=0)
        deep_t = [exchanged(turned, "gz").reshape(deep_channels, deep_cells)]
    level_t = jnp.stack(
        [swapped(value, "gy", code) if code else value for code, value in enumerate(level_t)]
    )
    down_slice = lax.dynamic_index_in_dim(down_weight, parity, 0, keepdims=False)
    shared = call(
        lambda *refs: mask_kernel(n_gy, *refs),
        [shape((cells + down_count, channels), BF16)] * n_gy,
        pre_activation[0],
        skip_cotangent[0],
        down_slice,
        *deep_t,
        scratch=[
            pltpu.VMEM((deep_channels, deep_cells), BF16),
            pltpu.VMEM((n_gy, 4 * channels // n_gy, deep_channels), BF16),
        ],
    )
    shared = [swapped(value, "gy", code) if code else value for code, value in enumerate(shared)]
    even, odd = neighbours(level_t)
    *parts, near = call(
        lambda *refs: weight_kernel(n_gy, conv_rows, down_rows, (rows, cols, channels), *refs),
        (
            [shape((piece, channels), BF16)] * n_gz
            if direct
            else [shape((n_gz, piece, channels), BF16)]
        )
        + [shape((rows + 2, cols, channels), BF16)],
        even,
        level_t,
        odd,
        *shared,
        scratch=[
            pltpu.VMEM((n_gy * rows + 2, cols, 3 * channels), BF16),
            pltpu.VMEM((n_gy, 3 * part, cells), BF16),
            pltpu.VMEM((n_gz, piece, channels), BF16),
        ],
    )
    cell_total = devices * cells
    if direct:
        parts = [swapped(value, "gz", code) if code else value for code, value in enumerate(parts)]
        same = sum(value.astype(F32) for value in parts[0::2])
        other = sum(value.astype(F32) for value in parts[1::2])
        first = jnp.where(parity == 0, same[conv_rows:], other[conv_rows:])
        second = jnp.where(parity == 0, other[conv_rows:], same[conv_rows:])
    else:
        parts = exchanged(parts[0], "gz").astype(F32)
        same, other = jnp.sum(parts[0::2], axis=0), jnp.sum(parts[1::2], axis=0)
        first, second = same[conv_rows:], other[conv_rows:]
    conv_sum = (same[:conv_rows] + other[:conv_rows]) / math.sqrt(cell_total)
    down_sum = jnp.concatenate([first, second], axis=0) / math.sqrt(cell_total // 8)
    block = jnp.concatenate([conv_sum, down_sum], axis=0).astype(BF16)[None]
    code = n_gz // 2
    while code:
        block = jnp.concatenate([block, swapped(block, "gz", code)], axis=0)
        code //= 2
    blocks = [block]
    code = n_gy // 2
    while code:
        blocks = blocks + [swapped(value, "gy", code) for value in blocks]
        code //= 2
    order = [reversed_bits(place, n_gy) for place in range(n_gy)]
    blocks = [blocks[order[place]] for place in range(n_gy)]
    conv_grad, down_grad = call(
        lambda *refs: place_kernel(n_gy, conv_rows, down_rows, *refs),
        (
            shape((27, n_gy, part, channels), BF16),
            shape((2, n_gy, 4 * channels // n_gy, deep_channels), BF16),
        ),
        *blocks,
    )
    even, odd = neighbours(near)
    input_grad = call(
        input_kernel,
        shape((rows, cols, channels), BF16),
        even,
        near,
        odd,
        conv_weight,
    )
    return (
        input_grad[None],
        conv_grad.reshape(conv_weight.shape),
        down_grad.reshape(down_weight.shape),
    )


def solution(mesh):
    return jax.shard_map(
        per_device,
        mesh=mesh,
        in_specs=(
            P("gz", "gy", None, None),
            P("gz", "gy", None, None),
            P(),
            P(),
            P("gz", "gy", None, None),
            P(None, "gy", None, "gz"),
        ),
        out_specs=(P("gz", "gy", None, None), P(), P()),
        check_vma=False,
    )
```

time: 92.7 us -> 87.6 us (0.945)
  blocking collectives: 27 us -> 0 us
  starting transfers between devices: 26.8 us -> 41.2 us
  waiting for transfers between devices: 28.2 us -> 38.1 us
  Pallas kernels: 6.41 us -> 5.29 us
  local copies, waits for them, and re-layouts: 2.88 us -> 1.9 us
    ppermute x3 -> x28, starting transfers between devices: 0.85 us -> 39.9 us  [swapped(): lax.ppermute(value, axis, [(i, i ^ code) for i in range(lax.axis_size(axi...]
    ppermute x3 -> x28, waiting for transfers between devices: 6.72 us -> 38.1 us  [swapped(): lax.ppermute(value, axis, [(i, i ^ code) for i in range(lax.axis_size(axi...]
    all_to_all x2 -> x0, blocking collectives: 27 us -> none  [exchanged(): return lax.all_to_all(value, axis, split_axis=0, concat_axis=0, tiled=True)]
    all_to_all x3 -> x0, starting transfers between devices: 14.1 us -> none  [exchanged(): return lax.all_to_all(value, axis, split_axis=0, concat_axis=0, tiled=True)]
    all_to_all x3 -> x0, waiting for transfers between devices: 11.3 us -> none  [exchanged(): return lax.all_to_all(value, axis, split_axis=0, concat_axis=0, tiled=True)]
    ppermute x4 -> x2, starting transfers between devices: 11.8 us -> 1.33 us  [neighbours(): return (swapped(value, 'gz', 1), lax.ppermute(value, 'gz', odd))]
    ppermute x4 -> x2, waiting for transfers between devices: 10.1 us -> 0.01 us  [neighbours(): return (swapped(value, 'gz', 1), lax.ppermute(value, 'gz', odd))]
    pallas_call x5, Pallas kernels: 6.41 us -> 5.29 us  [call(): pl.pallas_call(kernel, out_shape=out_shape, scratch_shapes=list(scratch),...]
  transfers between devices with their start and end apart: 10 -> 30, of which waited for: 8 -> 10; matrix products, arithmetic and copies ran while one was open for 0% -> 0% of each run, Pallas kernels for 3% -> 3%
where the time goes in v5:
time: 87.6 us; the launch traced here: 87.4 us
  starting transfers between devices  41.2 us (47%)
  waiting for transfers between devices  38.1 us (43%)
  Pallas kernels  5.29 us (6%)
  local copies, waits for them, and re-layouts  1.9 us (2%)
    ppermute x28, starting transfers between devices, swapped(): lax.ppermute(value, axis, [(i, i ^ code) for i in range(lax.axis_size(axi...  39.9 us
    ppermute x28, waiting for transfers between devices, swapped(): lax.ppermute(value, axis, [(i, i ^ code) for i in range(lax.axis_size(axi...  38.1 us
    pallas_call x5, Pallas kernels, call(): pl.pallas_call(kernel, out_shape=out_shape, scratch_shapes=list(scratch),...  5.29 us
    unnamed x12, local copies, waits for them, and re-layouts  1.88 us
  transfers between devices with their start and end apart: 30, of which 10 were waited for; matrix products, arithmetic and copies ran while one was open for 0% of the time, Pallas kernels for 3%

profile of v5, /device:TPU:0, one launch (start us, length us, event | category | flops | bytes accessed | tf_op | source)
XLA Modules:
  0.0 87.4 jit_solution(12692323106301015305)
XLA Ops:
  0.6 0.0 copy-start
  0.7 1.0 %copy-done.2 = bf16[4,4,32,32]{3,2,1,0:T(8,128)(2,1)S(1)} copy-done((bf16[4,4,32,32]{3,2,1,0:T(8,128)(2,1)S(1)}, bf16[4,4,32,32]{3,2,1,0:T(8,128)(2,1)}, u32[]{:S(2)}) %copy-start.2) | copy-done | bytes 32792
  1.6 0.9 %copy-done.3 = bf16[1,8,64,128]{3,2,1,0:T(8,128)(2,1)S(1)} copy-done((bf16[1,8,64,128]{3,2,1,0:T(8,128)(2,1)S(1)}, bf16[1,8,64,128]{3,2,1,0:T(8,128)(2,1)}, u32[]{:S(2)}) %copy-start.3) | copy-done | bytes 131096
  2.5 0.1 shard_map.85
  2.6 3.0 %collective-permute-start.5 = (bf16[32,128]{1,0:T(8,128)(2,1)S(1)}, bf16[32,128]{1,0:T(8,128)(2,1)S(1)}, u32[]{:S(2)}, u32[]{:S(2)}) collective-permute-start(bf16[32,128]{1,0:T(8,128)(2,1)S(1)} %get-tuple-element.35), channel_id=1, source_target_pairs={{0,4},{4,0},{8,12},{12,8},{16,20},{20,16},{24,28},{28,24},{1,5},{5... | collective-permute-start | bytes 24584 | tf_op jit(solution)/shard_map/ppermute | solution.py:238
  5.7 1.6 %collective-permute-start.6 = (bf16[32,128]{1,0:T(8,128)(2,1)S(1)}, bf16[32,128]{1,0:T(8,128)(2,1)S(1)}, u32[]{:S(2)}, u32[]{:S(2)}) collective-permute-start(bf16[32,128]{1,0:T(8,128)(2,1)S(1)} %get-tuple-element.36), channel_id=1, source_target_pairs={{0,8},{4,12},{8,0},{12,4},{16,24},{20,28},{24,16},{28,20},{1,9},{5... | collective-permute-start | bytes 24584 | tf_op jit(solution)/shard_map/ppermute | solution.py:238
  7.3 0.0 collective-permute-start.7
  7.3 3.0 %collective-permute-start.8 = (bf16[32,128]{1,0:T(8,128)(2,1)S(1)}, bf16[32,128]{1,0:T(8,128)(2,1)S(1)}, u32[]{:S(2)}, u32[]{:S(2)}) collective-permute-start(bf16[32,128]{1,0:T(8,128)(2,1)S(1)} %get-tuple-element.38), channel_id=1, source_target_pairs={{0,16},{4,20},{8,24},{12,28},{16,0},{20,4},{24,8},{28,12},{1,17},{... | collective-permute-start | bytes 24584 | tf_op jit(solution)/shard_map/ppermute | solution.py:238
  10.2 1.3 %collective-permute-start.9 = (bf16[32,128]{1,0:T(8,128)(2,1)S(1)}, bf16[32,128]{1,0:T(8,128)(2,1)S(1)}, u32[]{:S(2)}, u32[]{:S(2)}) collective-permute-start(bf16[32,128]{1,0:T(8,128)(2,1)S(1)} %get-tuple-element.39), channel_id=1, source_target_pairs={{0,20},{4,16},{8,28},{12,24},{16,4},{20,0},{24,12},{28,8},{1,21},{... | collective-permute-start | bytes 24584 | tf_op jit(solution)/shard_map/ppermute | solution.py:238
  11.5 0.0 collective-permute-done.5.refs_4_
  11.5 3.6 %collective-permute-start.10 = (bf16[32,128]{1,0:T(8,128)(2,1)S(1)}, bf16[32,128]{1,0:T(8,128)(2,1)S(1)}, u32[]{:S(2)}, u32[]{:S(2)}) collective-permute-start(bf16[32,128]{1,0:T(8,128)(2,1)S(1)} %get-tuple-element.40), channel_id=1, source_target_pairs={{0,24},{4,28},{8,16},{12,20},{16,8},{20,12},{24,0},{28,4},{1,25},{... | collective-permute-start | bytes 24584 | tf_op jit(solution)/shard_map/ppermute | solution.py:238
  15.1 0.0 collective-permute-done.6.refs_5_
  15.1 0.0 collective-permute-start.11
  15.1 0.0 collective-permute-done.7.refs_6_
  15.2 0.1 collective-permute-start
  15.2 0.0 collective-permute-done.8.refs_7_
  15.2 1.6 %collective-permute-start.1 = (bf16[32,512]{1,0:T(8,128)(2,1)S(1)}, bf16[32,512]{1,0:T(8,128)(2,1)S(1)}, u32[]{:S(2)}, u32[]{:S(2)}) collective-permute-start(bf16[32,512]{1,0:T(8,128)(2,1)S(1)} %get-tuple-element.32), channel_id=1, source_target_pairs={{0,2},{1,3},{2,0},{3,1},{4,6},{5,7},{6,4},{7,5},{8,10},{9,11},{10,... | collective-permute-start | bytes 98312 | tf_op jit(solution)/shard_map/ppermute | solution.py:238
  16.9 0.0 collective-permute-done.9.refs_8_
  16.9 0.2 collective-permute-start.2
  17.1 0.0 collective-permute-done.10.refs_9_
  17.2 4.3 %collective-permute-done.11.refs_10_ = bf16[32,128]{1,0:T(8,128)(2,1)S(1)} collective-permute-done((bf16[32,128]{1,0:T(8,128)(2,1)S(1)}, bf16[32,128]{1,0:T(8,128)(2,1)S(1)}, u32[]{:S(2)}, u32[]{:S(2)}) %collective-permute-start.11) | collective-permute-done | bytes 8224 | tf_op jit(solution)/shard_map/ppermute | solution.py:238
  21.5 0.6 shard_map.86
  22.1 0.1 collective-permute-start.12
  22.2 1.6 %collective-permute-start.13 = (bf16[768,128]{1,0:T(8,128)(2,1)S(1)}, bf16[768,128]{1,0:T(8,128)(2,1)S(1)}, u32[]{:S(2)}, u32[]{:S(2)}) collective-permute-start(bf16[768,128]{1,0:T(8,128)(2,1)S(1)} %get-tuple-element.44), channel_id=1, source_target_pairs={{0,2},{1,3},{2,0},{3,1},{4,6},{5,7},{6,4},{7,5},{8,10},{9,11},{10,... | collective-permute-start | bytes 589832 | tf_op jit(solution)/shard_map/ppermute | solution.py:238
  23.8 0.0 collective-permute-done
  23.8 0.3 collective-permute-start.14
  24.1 0.0 collective-permute-done.1
  24.1 0.0 collective-permute-done.2
  24.1 0.7 collective-permute-start.4
  24.8 1.8 %collective-permute-start.3 = (bf16[4,32,512]{2,1,0:T(8,128)(2,1)S(1)}, bf16[4,32,512]{2,1,0:T(8,128)(2,1)S(1)}, u32[]{:S(2)}, u32[]{:S(2)}) collective-permute-start(bf16[4,32,512]{2,1,0:T(8,128)(2,1)S(1)} %pad_maximum_fusion.2.refs_1_), channel_id=1, source_target_pairs={{0,4},{4,0},{8,12},{12,8},{16,20},{20,16},{24,28},{28,24},{1,5},{5... | collective-permute-start | bytes 393224 | tf_op jit(solution)/shard_map/ppermute | solution.py:238
  26.6 0.0 collective-permute-done.4.refs_2_
  26.6 6.1 %collective-permute-done.3.refs_0_ = bf16[4,32,512]{2,1,0:T(8,128)(2,1)S(1)} collective-permute-done((bf16[4,32,512]{2,1,0:T(8,128)(2,1)S(1)}, bf16[4,32,512]{2,1,0:T(8,128)(2,1)S(1)}, u32[]{:S(2)}, u32[]{:S(2)}) %collective-permute-start.3) | collective-permute-done | bytes 131104 | tf_op jit(solution)/shard_map/ppermute | solution.py:238
  32.7 0.0 collective-permute-done.12.refs_4_
  32.7 0.0 collective-permute-done.13.refs_5_
  32.7 0.6 collective-permute-done.14.refs_6_
  33.3 1.5 %shard_map.87 = (bf16[144,128]{1,0:T(8,128)(2,1)S(1)}, bf16[144,128]{1,0:T(8,128)(2,1)S(1)}, bf16[144,128]{1,0:T(8,128)(2,1)S(1)}, bf16[144,128]{1,0:T(8,128)(2,...) custom-call(bf16[4,32,512]{2,1,0:T(8,128)(2,1)S(1)} %collective-perm, ...), custom_call_target="tpu_custom_call" | custom-call | tf_op jit(solution)/shard_map/pallas_call | solution.py:16
  34.7 1.6 %collective-permute-start.17 = (bf16[144,128]{1,0:T(8,128)(2,1)S(1)}, bf16[144,128]{1,0:T(8,128)(2,1)S(1)}, u32[]{:S(2)}, u32[]{:S(2)}) collective-permute-start(bf16[144,128]{1,0:T(8,128)(2,1)S(1)} %get-tuple-element.48), channel_id=1, source_target_pairs={{0,8},{4,12},{8,0},{12,4},{16,24},{20,28},{24,16},{28,20},{1,9},{5... | collective-permute-start | bytes 110600 | tf_op jit(solution)/shard_map/ppermute | solution.py:238
  36.3 0.7 collective-permute-start.18
  37.0 2.2 %collective-permute-start.19 = (bf16[144,128]{1,0:T(8,128)(2,1)S(1)}, bf16[144,128]{1,0:T(8,128)(2,1)S(1)}, u32[]{:S(2)}, u32[]{:S(2)}) collective-permute-start(bf16[144,128]{1,0:T(8,128)(2,1)S(1)} %get-tuple-element.50), channel_id=1, source_target_pairs={{0,24},{4,28},{8,16},{12,20},{16,8},{20,12},{24,0},{28,4},{1,25},{... | collective-permute-start | bytes 110600 | tf_op jit(solution)/shard_map/ppermute | solution.py:238
  39.2 1.9 %collective-permute-start.20 = (bf16[144,128]{1,0:T(8,128)(2,1)S(1)}, bf16[144,128]{1,0:T(8,128)(2,1)S(1)}, u32[]{:S(2)}, u32[]{:S(2)}) collective-permute-start(bf16[144,128]{1,0:T(8,128)(2,1)S(1)} %get-tuple-element.51), channel_id=1, source_target_pairs={{0,4},{4,0},{8,12},{12,8},{16,20},{20,16},{24,28},{28,24},{1,5},{5... | collective-permute-start | bytes 110600 | tf_op jit(solution)/shard_map/ppermute | solution.py:238
  41.1 0.2 collective-permute-start.21
  41.3 0.0 collective-permute-done.17
  41.3 1.3 %collective-permute-start.22 = (bf16[144,128]{1,0:T(8,128)(2,1)S(1)}, bf16[144,128]{1,0:T(8,128)(2,1)S(1)}, u32[]{:S(2)}, u32[]{:S(2)}) collective-permute-start(bf16[144,128]{1,0:T(8,128)(2,1)S(1)} %get-tuple-element.53), channel_id=1, source_target_pairs={{0,20},{4,16},{8,28},{12,24},{16,4},{20,0},{24,12},{28,8},{1,21},{... | collective-permute-start | bytes 110600 | tf_op jit(solution)/shard_map/ppermute | solution.py:238
  42.5 0.0 collective-permute-done.18
  42.6 3.4 %collective-permute-start.23 = (bf16[144,128]{1,0:T(8,128)(2,1)S(1)}, bf16[144,128]{1,0:T(8,128)(2,1)S(1)}, u32[]{:S(2)}, u32[]{:S(2)}) collective-permute-start(bf16[144,128]{1,0:T(8,128)(2,1)S(1)} %get-tuple-element.54), channel_id=1, source_target_pairs={{0,28},{4,24},{8,20},{12,16},{16,12},{20,8},{24,4},{28,0},{1,29},{... | collective-permute-start | bytes 110600 | tf_op jit(solution)/shard_map/ppermute | solution.py:238
  46.0 0.0 copy-start.1
  46.0 0.0 collective-permute-done.21
  46.0 1.0 %collective-permute-done.22 = bf16[144,128]{1,0:T(8,128)(2,1)S(1)} collective-permute-done((bf16[144,128]{1,0:T(8,128)(2,1)S(1)}, bf16[144,128]{1,0:T(8,128)(2,1)S(1)}, u32[]{:S(2)}, u32[]{:S(2)}) %collective-permute-start.22) | collective-permute-done | bytes 36896 | tf_op jit(solution)/shard_map/ppermute | solution.py:238
  47.0 2.2 %collective-permute-done.23 = bf16[144,128]{1,0:T(8,128)(2,1)S(1)} collective-permute-done((bf16[144,128]{1,0:T(8,128)(2,1)S(1)}, bf16[144,128]{1,0:T(8,128)(2,1)S(1)}, u32[]{:S(2)}, u32[]{:S(2)}) %collective-permute-start.23) | collective-permute-done | bytes 36896 | tf_op jit(solution)/shard_map/ppermute | solution.py:238
  49.3 0.2 collective-permute-start.24
  49.5 4.8 %collective-permute-done.24 = bf16[1,176,128]{2,1,0:T(8,128)(2,1)S(1)} collective-permute-done((bf16[1,176,128]{2,1,0:T(8,128)(2,1)S(1)}, bf16[1,176,128]{2,1,0:T(8,128)(2,1)S(1)}, u32[]{:S(2)}, u32[]{:S(2)}) %collective-permute-start.24) | collective-permute-done | bytes 45088 | tf_op jit(solution)/shard_map/ppermute | solution.py:238
  54.3 2.0 %collective-permute-start.25 = (bf16[2,176,128]{2,1,0:T(8,128)(2,1)S(1)}, bf16[2,176,128]{2,1,0:T(8,128)(2,1)S(1)}, u32[]{:S(2)}, u32[]{:S(2)}) collective-permute-start(bf16[2,176,128]{2,1,0:T(8,128)(2,1)S(1)} %pad_maximum_fusion.3), channel_id=1, source_target_pairs={{0,8},{4,12},{8,0},{12,4},{16,24},{20,28},{24,16},{28,20},{1,9},{5... | collective-permute-start | bytes 270344 | tf_op jit(solution)/shard_map/ppermute | solution.py:238
  56.3 2.6 %collective-permute-done.25 = bf16[2,176,128]{2,1,0:T(8,128)(2,1)S(1)} collective-permute-done((bf16[2,176,128]{2,1,0:T(8,128)(2,1)S(1)}, bf16[2,176,128]{2,1,0:T(8,128)(2,1)S(1)}, u32[]{:S(2)}, u32[]{:S(2)}) %collective-permute-start.25) | collective-permute-done | bytes 90144 | tf_op jit(solution)/shard_map/ppermute | solution.py:238
  58.9 2.0 %collective-permute-start.26 = (bf16[4,176,128]{2,1,0:T(8,128)(2,1)S(1)}, bf16[4,176,128]{2,1,0:T(8,128)(2,1)S(1)}, u32[]{:S(2)}, u32[]{:S(2)}) collective-permute-start(bf16[4,176,128]{2,1,0:T(8,128)(2,1)S(1)} %pad_maximum_fusion.1), channel_id=1, source_target_pairs={{0,4},{4,0},{8,12},{12,8},{16,20},{20,16},{24,28},{28,24},{1,5},{5... | collective-permute-start | bytes 540680 | tf_op jit(solution)/shard_map/ppermute | solution.py:238
  60.9 3.6 %collective-permute-done.26 = bf16[4,176,128]{2,1,0:T(8,128)(2,1)S(1)} collective-permute-done((bf16[4,176,128]{2,1,0:T(8,128)(2,1)S(1)}, bf16[4,176,128]{2,1,0:T(8,128)(2,1)S(1)}, u32[]{:S(2)}, u32[]{:S(2)}) %collective-permute-start.26) | collective-permute-done | bytes 180256 | tf_op jit(solution)/shard_map/ppermute | solution.py:238
  64.5 1.6 %collective-permute-start.28 = (bf16[8,176,128]{2,1,0:T(8,128)(2,1)S(1)}, bf16[8,176,128]{2,1,0:T(8,128)(2,1)S(1)}, u32[]{:S(2)}, u32[]{:S(2)}) collective-permute-start(bf16[8,176,128]{2,1,0:T(8,128)(2,1)S(1)} %pad_maximum_fusion.refs_0_), channel_id=1, source_target_pairs={{0,2},{1,3},{2,0},{3,1},{4,6},{5,7},{6,4},{7,5},{8,10},{9,11},{10,... | collective-permute-start | bytes 1081352 | tf_op jit(solution)/shard_map/ppermute | solution.py:238
  66.1 0.0 collective-permute-start.27
  66.1 5.9 %collective-permute-done.28.refs_2_ = bf16[8,176,128]{2,1,0:T(8,128)(2,1)S(1)} collective-permute-done((bf16[8,176,128]{2,1,0:T(8,128)(2,1)S(1)}, bf16[8,176,128]{2,1,0:T(8,128)(2,1)S(1)}, u32[]{:S(2)}, u32[]{:S(2)}) %collective-permute-start.28) | collective-permute-done | bytes 360480 | tf_op jit(solution)/shard_map/ppermute | solution.py:238
  72.0 0.7 collective-permute-start.16
  72.7 4.7 %collective-permute-start.15 = (bf16[10,64,128]{2,1,0:T(8,128)(2,1)S(1)}, bf16[10,64,128]{2,1,0:T(8,128)(2,1)S(1)}, u32[]{:S(2)}, u32[]{:S(2)}) collective-permute-start(bf16[10,64,128]{2,1,0:T(8,128)(2,1)S(1)} %get-tuple-element.46.own), channel_id=1, source_target_pairs={{0,4},{4,0},{8,12},{12,8},{16,20},{20,16},{24,28},{28,24},{1,5},{5... | collective-permute-start | bytes 491528 | tf_op jit(solution)/shard_map/ppermute | solution.py:238
  77.4 6.9 %collective-permute-done.15.even = bf16[10,64,128]{2,1,0:T(8,128)(2,1)S(1)} collective-permute-done((bf16[10,64,128]{2,1,0:T(8,128)(2,1)S(1)}, bf16[10,64,128]{2,1,0:T(8,128)(2,1)S(1)}, u32[]{:S(2)}, u32[]{:S(2)}) %collective-permute-start.15) | collective-permute-done | bytes 163872 | tf_op jit(solution)/shard_map/ppermute | solution.py:238
  84.3 1.7 %shard_map.88 = bf16[8,64,128]{2,1,0:T(8,128)(2,1)} custom-call(bf16[10,64,128]{2,1,0:T(8,128)(2,1)S(1)} %collective-permute-done.15.even, bf16[10,64,128]{2,1,0:T(8,128)(2,1)S(1)} %get-tuple-element.46.own, bf16[10,64,128]{2,1,0:T(8,128)(2,1)S(1)} %collective-permute-done.16.odd, bf16[3,3,3,128,128]{4,3,2,1,0:T(8,128)(2,1)S(1)} %copy-done.1), custom_call_target="tpu_custom_call" | custom-call | tf_op jit(solution)/shard_map/pallas_call | solution.py:16
  86.1 0.0 collective-permute-done.27.refs_1_
  86.1 1.4 %shard_map.89 = (bf16[27,4,32,128]{3,2,1,0:T(8,128)(2,1)}, bf16[2,4,128,256]{3,2,1,0:T(8,128)(2,1)}) custom-call(bf16[8,176,128]{2,1,0:T(8,128)(2,1)S(1)} %pad_maximum_fusion.refs_0_, bf16[8,176,128]{2,1,0:T(8,128)(2,1)S(1)} %collective-permute-done.27.refs_1_, bf16[8,176,128]{2,1,0:T(8,128)(2,1)S(1)} %collective-permute-done.28.refs_2_, ...), custom_call_target="tpu_custom_call" | custom-call | tf_op jit(solution)/shard_map/pallas_call | solution.py:16
  (24 shorter events, 0.2 us)
Async XLA Ops:
  0.6 16.5 %copy-start = (bf16[2,2,2,128,256]{4,3,2,1,0:T(8,128)(2,1)S(1)}, bf16[2,2,2,128,256]{4,3,2,1,0:T(8,128)(2,1)}, u32[]{:S(2)}) copy-start(bf16[2,2,2,128,256]{4,3,2,1,0:T(8,128)(2,1)} %param.9) | copy-start | bytes 1572868
  0.6 1.0 %copy-start.2 = (bf16[4,4,32,32]{3,2,1,0:T(8,128)(2,1)S(1)}, bf16[4,4,32,32]{3,2,1,0:T(8,128)(2,1)}, u32[]{:S(2)}) copy-start(bf16[4,4,32,32]{3,2,1,0:T(8,128)(2,1)} %param.11) | copy-start | bytes 98308
  1.6 0.9 %copy-start.3 = (bf16[1,8,64,128]{3,2,1,0:T(8,128)(2,1)S(1)}, bf16[1,8,64,128]{3,2,1,0:T(8,128)(2,1)}, u32[]{:S(2)}) copy-start(bf16[1,8,64,128]{3,2,1,0:T(8,128)(2,1)} %param.6) | copy-start | bytes 393220
  2.6 8.9 %collective-permute-start.5 = (bf16[32,128]{1,0:T(8,128)(2,1)S(1)}, bf16[32,128]{1,0:T(8,128)(2,1)S(1)}, u32[]{:S(2)}, u32[]{:S(2)}) collective-permute-start(bf16[32,128]{1,0:T(8,128)(2,1)S(1)} %get-tuple-element.35), channel_id=1, source_target_pairs={{0,4},{4,0},{8,12},{12,8},{16,20},{20,16},{24,28},{28,24},{1,5},{5... | collective-permute-start | bytes 24584 | tf_op jit(solution)/shard_map/ppermute | solution.py:238
  5.7 9.5 %collective-permute-start.6 = (bf16[32,128]{1,0:T(8,128)(2,1)S(1)}, bf16[32,128]{1,0:T(8,128)(2,1)S(1)}, u32[]{:S(2)}, u32[]{:S(2)}) collective-permute-start(bf16[32,128]{1,0:T(8,128)(2,1)S(1)} %get-tuple-element.36), channel_id=1, source_target_pairs={{0,8},{4,12},{8,0},{12,4},{16,24},{20,28},{24,16},{28,20},{1,9},{5... | collective-permute-start | bytes 24584 | tf_op jit(solution)/shard_map/ppermute | solution.py:238
  7.3 7.9 %collective-permute-start.7 = (bf16[32,128]{1,0:T(8,128)(2,1)S(1)}, bf16[32,128]{1,0:T(8,128)(2,1)S(1)}, u32[]{:S(2)}, u32[]{:S(2)}) collective-permute-start(bf16[32,128]{1,0:T(8,128)(2,1)S(1)} %get-tuple-element.37), channel_id=1, source_target_pairs={{0,12},{4,8},{8,4},{12,0},{16,28},{20,24},{24,20},{28,16},{1,13},{... | collective-permute-start | bytes 24584 | tf_op jit(solution)/shard_map/ppermute | solution.py:238
  7.3 8.0 %collective-permute-start.8 = (bf16[32,128]{1,0:T(8,128)(2,1)S(1)}, bf16[32,128]{1,0:T(8,128)(2,1)S(1)}, u32[]{:S(2)}, u32[]{:S(2)}) collective-permute-start(bf16[32,128]{1,0:T(8,128)(2,1)S(1)} %get-tuple-element.38), channel_id=1, source_target_pairs={{0,16},{4,20},{8,24},{12,28},{16,0},{20,4},{24,8},{28,12},{1,17},{... | collective-permute-start | bytes 24584 | tf_op jit(solution)/shard_map/ppermute | solution.py:238
  10.2 6.6 %collective-permute-start.9 = (bf16[32,128]{1,0:T(8,128)(2,1)S(1)}, bf16[32,128]{1,0:T(8,128)(2,1)S(1)}, u32[]{:S(2)}, u32[]{:S(2)}) collective-permute-start(bf16[32,128]{1,0:T(8,128)(2,1)S(1)} %get-tuple-element.39), channel_id=1, source_target_pairs={{0,20},{4,16},{8,28},{12,24},{16,4},{20,0},{24,12},{28,8},{1,21},{... | collective-permute-start | bytes 24584 | tf_op jit(solution)/shard_map/ppermute | solution.py:238
  11.5 5.6 %collective-permute-start.10 = (bf16[32,128]{1,0:T(8,128)(2,1)S(1)}, bf16[32,128]{1,0:T(8,128)(2,1)S(1)}, u32[]{:S(2)}, u32[]{:S(2)}) collective-permute-start(bf16[32,128]{1,0:T(8,128)(2,1)S(1)} %get-tuple-element.40), channel_id=1, source_target_pairs={{0,24},{4,28},{8,16},{12,20},{16,8},{20,12},{24,0},{28,4},{1,25},{... | collective-permute-start | bytes 24584 | tf_op jit(solution)/shard_map/ppermute | solution.py:238
  15.1 6.3 %collective-permute-start.11 = (bf16[32,128]{1,0:T(8,128)(2,1)S(1)}, bf16[32,128]{1,0:T(8,128)(2,1)S(1)}, u32[]{:S(2)}, u32[]{:S(2)}) collective-permute-start(bf16[32,128]{1,0:T(8,128)(2,1)S(1)} %get-tuple-element.41), channel_id=1, source_target_pairs={{0,28},{4,24},{8,20},{12,16},{16,12},{20,8},{24,4},{28,0},{1,29},{... | collective-permute-start | bytes 24584 | tf_op jit(solution)/shard_map/ppermute | solution.py:238
  15.2 8.6 %collective-permute-start = (bf16[32,512]{1,0:T(8,128)(2,1)S(1)}, bf16[32,512]{1,0:T(8,128)(2,1)S(1)}, u32[]{:S(2)}, u32[]{:S(2)}) collective-permute-start(bf16[32,512]{1,0:T(8,128)(2,1)S(1)} %get-tuple-element.31), channel_id=1, source_target_pairs={{0,1},{1,0},{2,3},{3,2},{4,5},{5,4},{6,7},{7,6},{8,9},{9,8},{10,11... | collective-permute-start | bytes 98312 | tf_op jit(solution)/shard_map/ppermute | solution.py:238
  15.2 8.8 %collective-permute-start.1 = (bf16[32,512]{1,0:T(8,128)(2,1)S(1)}, bf16[32,512]{1,0:T(8,128)(2,1)S(1)}, u32[]{:S(2)}, u32[]{:S(2)}) collective-permute-start(bf16[32,512]{1,0:T(8,128)(2,1)S(1)} %get-tuple-element.32), channel_id=1, source_target_pairs={{0,2},{1,3},{2,0},{3,1},{4,6},{5,7},{6,4},{7,5},{8,10},{9,11},{10,... | collective-permute-start | bytes 98312 | tf_op jit(solution)/shard_map/ppermute | solution.py:238
  16.9 4.6 %copy-start.4 = (bf16[1,8,64,128]{3,2,1,0:T(8,128)(2,1)S(1)}, bf16[1,8,64,128]{3,2,1,0:T(8,128)(2,1)}, u32[]{:S(2)}) copy-start(bf16[1,8,64,128]{3,2,1,0:T(8,128)(2,1)} %param.7) | copy-start | bytes 393220
  16.9 4.6 %copy-start.5 = (bf16[1,8,64,128]{3,2,1,0:T(8,128)(2,1)S(1)}, bf16[1,8,64,128]{3,2,1,0:T(8,128)(2,1)}, u32[]{:S(2)}) copy-start(bf16[1,8,64,128]{3,2,1,0:T(8,128)(2,1)} %param.10) | copy-start | bytes 393220
  16.9 7.2 %collective-permute-start.2 = (bf16[32,512]{1,0:T(8,128)(2,1)S(1)}, bf16[32,512]{1,0:T(8,128)(2,1)S(1)}, u32[]{:S(2)}, u32[]{:S(2)}) collective-permute-start(bf16[32,512]{1,0:T(8,128)(2,1)S(1)} %get-tuple-element.33), channel_id=1, source_target_pairs={{0,3},{1,2},{2,1},{3,0},{4,7},{5,6},{6,5},{7,4},{8,11},{9,10},{10,... | collective-permute-start | bytes 98312 | tf_op jit(solution)/shard_map/ppermute | solution.py:238
  22.1 10.6 %collective-permute-start.12 = (bf16[768,128]{1,0:T(8,128)(2,1)S(1)}, bf16[768,128]{1,0:T(8,128)(2,1)S(1)}, u32[]{:S(2)}, u32[]{:S(2)}) collective-permute-start(bf16[768,128]{1,0:T(8,128)(2,1)S(1)} %get-tuple-element.43), channel_id=1, source_target_pairs={{0,1},{1,0},{2,3},{3,2},{4,5},{5,4},{6,7},{7,6},{8,9},{9,8},{10,11... | collective-permute-start | bytes 589832 | tf_op jit(solution)/shard_map/ppermute | solution.py:238
  22.2 10.5 %collective-permute-start.13 = (bf16[768,128]{1,0:T(8,128)(2,1)S(1)}, bf16[768,128]{1,0:T(8,128)(2,1)S(1)}, u32[]{:S(2)}, u32[]{:S(2)}) collective-permute-start(bf16[768,128]{1,0:T(8,128)(2,1)S(1)} %get-tuple-element.44), channel_id=1, source_target_pairs={{0,2},{1,3},{2,0},{3,1},{4,6},{5,7},{6,4},{7,5},{8,10},{9,11},{10,... | collective-permute-start | bytes 589832 | tf_op jit(solution)/shard_map/ppermute | solution.py:238
  23.8 9.5 %collective-permute-start.14 = (bf16[768,128]{1,0:T(8,128)(2,1)S(1)}, bf16[768,128]{1,0:T(8,128)(2,1)S(1)}, u32[]{:S(2)}, u32[]{:S(2)}) collective-permute-start(bf16[768,128]{1,0:T(8,128)(2,1)S(1)} %get-tuple-element.45), channel_id=1, source_target_pairs={{0,3},{1,2},{2,1},{3,0},{4,7},{5,6},{6,5},{7,4},{8,11},{9,10},{10,... | collective-permute-start | bytes 589832 | tf_op jit(solution)/shard_map/ppermute | solution.py:238
  24.1 2.5 %collective-permute-start.4 = (bf16[4,32,512]{2,1,0:T(8,128)(2,1)S(1)}, bf16[4,32,512]{2,1,0:T(8,128)(2,1)S(1)}, u32[]{:S(2)}, u32[]{:S(2)}) collective-permute-start(bf16[4,32,512]{2,1,0:T(8,128)(2,1)S(1)} %pad_maximum_fusion.2.refs_1_), channel_id=1, source_target_pairs={{4,8},{8,4},{12,16},{16,12},{20,24},{24,20},{5,9},{9,5},{13,17},{1... | collective-permute-start | bytes 393224 | tf_op jit(solution)/shard_map/ppermute | solution.py:244
  24.8 7.9 %collective-permute-start.3 = (bf16[4,32,512]{2,1,0:T(8,128)(2,1)S(1)}, bf16[4,32,512]{2,1,0:T(8,128)(2,1)S(1)}, u32[]{:S(2)}, u32[]{:S(2)}) collective-permute-start(bf16[4,32,512]{2,1,0:T(8,128)(2,1)S(1)} %pad_maximum_fusion.2.refs_1_), channel_id=1, source_target_pairs={{0,4},{4,0},{8,12},{12,8},{16,20},{20,16},{24,28},{28,24},{1,5},{5... | collective-permute-start | bytes 393224 | tf_op jit(solution)/shard_map/ppermute | solution.py:238
  34.7 6.5 %collective-permute-start.17 = (bf16[144,128]{1,0:T(8,128)(2,1)S(1)}, bf16[144,128]{1,0:T(8,128)(2,1)S(1)}, u32[]{:S(2)}, u32[]{:S(2)}) collective-permute-start(bf16[144,128]{1,0:T(8,128)(2,1)S(1)} %get-tuple-element.48), channel_id=1, source_target_pairs={{0,8},{4,12},{8,0},{12,4},{16,24},{20,28},{24,16},{28,20},{1,9},{5... | collective-permute-start | bytes 110600 | tf_op jit(solution)/shard_map/ppermute | solution.py:238
  36.3 6.2 %collective-permute-start.18 = (bf16[144,128]{1,0:T(8,128)(2,1)S(1)}, bf16[144,128]{1,0:T(8,128)(2,1)S(1)}, u32[]{:S(2)}, u32[]{:S(2)}) collective-permute-start(bf16[144,128]{1,0:T(8,128)(2,1)S(1)} %get-tuple-element.49), channel_id=1, source_target_pairs={{0,16},{4,20},{8,24},{12,28},{16,0},{20,4},{24,8},{28,12},{1,17},{... | collective-permute-start | bytes 110600 | tf_op jit(solution)/shard_map/ppermute | solution.py:238
  37.0 9.0 %collective-permute-start.19 = (bf16[144,128]{1,0:T(8,128)(2,1)S(1)}, bf16[144,128]{1,0:T(8,128)(2,1)S(1)}, u32[]{:S(2)}, u32[]{:S(2)}) collective-permute-start(bf16[144,128]{1,0:T(8,128)(2,1)S(1)} %get-tuple-element.50), channel_id=1, source_target_pairs={{0,24},{4,28},{8,16},{12,20},{16,8},{20,12},{24,0},{28,4},{1,25},{... | collective-permute-start | bytes 110600 | tf_op jit(solution)/shard_map/ppermute | solution.py:238
  39.2 6.8 %collective-permute-start.20 = (bf16[144,128]{1,0:T(8,128)(2,1)S(1)}, bf16[144,128]{1,0:T(8,128)(2,1)S(1)}, u32[]{:S(2)}, u32[]{:S(2)}) collective-permute-start(bf16[144,128]{1,0:T(8,128)(2,1)S(1)} %get-tuple-element.51), channel_id=1, source_target_pairs={{0,4},{4,0},{8,12},{12,8},{16,20},{20,16},{24,28},{28,24},{1,5},{5... | collective-permute-start | bytes 110600 | tf_op jit(solution)/shard_map/ppermute | solution.py:238
  41.1 4.9 %collective-permute-start.21 = (bf16[144,128]{1,0:T(8,128)(2,1)S(1)}, bf16[144,128]{1,0:T(8,128)(2,1)S(1)}, u32[]{:S(2)}, u32[]{:S(2)}) collective-permute-start(bf16[144,128]{1,0:T(8,128)(2,1)S(1)} %get-tuple-element.52), channel_id=1, source_target_pairs={{0,12},{4,8},{8,4},{12,0},{16,28},{20,24},{24,20},{28,16},{1,13},{... | collective-permute-start | bytes 110600 | tf_op jit(solution)/shard_map/ppermute | solution.py:238
  41.3 5.8 %collective-permute-start.22 = (bf16[144,128]{1,0:T(8,128)(2,1)S(1)}, bf16[144,128]{1,0:T(8,128)(2,1)S(1)}, u32[]{:S(2)}, u32[]{:S(2)}) collective-permute-start(bf16[144,128]{1,0:T(8,128)(2,1)S(1)} %get-tuple-element.53), channel_id=1, source_target_pairs={{0,20},{4,16},{8,28},{12,24},{16,4},{20,0},{24,12},{28,8},{1,21},{... | collective-permute-start | bytes 110600 | tf_op jit(solution)/shard_map/ppermute | solution.py:238
  42.6 6.7 %collective-permute-start.23 = (bf16[144,128]{1,0:T(8,128)(2,1)S(1)}, bf16[144,128]{1,0:T(8,128)(2,1)S(1)}, u32[]{:S(2)}, u32[]{:S(2)}) collective-permute-start(bf16[144,128]{1,0:T(8,128)(2,1)S(1)} %get-tuple-element.54), channel_id=1, source_target_pairs={{0,28},{4,24},{8,20},{12,16},{16,12},{20,8},{24,4},{28,0},{1,29},{... | collective-permute-start | bytes 110600 | tf_op jit(solution)/shard_map/ppermute | solution.py:238
  46.0 38.4 %copy-start.1 = (bf16[3,3,3,128,128]{4,3,2,1,0:T(8,128)(2,1)S(1)}, bf16[3,3,3,128,128]{4,3,2,1,0:T(8,128)(2,1)}, u32[]{:S(2)}) copy-start(bf16[3,3,3,128,128]{4,3,2,1,0:T(8,128)(2,1)} %weight.1) | copy-start | bytes 2654212
  49.3 5.0 %collective-permute-start.24 = (bf16[1,176,128]{2,1,0:T(8,128)(2,1)S(1)}, bf16[1,176,128]{2,1,0:T(8,128)(2,1)S(1)}, u32[]{:S(2)}, u32[]{:S(2)}) collective-permute-start(bf16[1,176,128]{2,1,0:T(8,128)(2,1)S(1)} %pad_maximum_fusion.4), channel_id=1, source_target_pairs={{0,16},{4,20},{8,24},{12,28},{16,0},{20,4},{24,8},{28,12},{1,17},{... | collective-permute-start | bytes 135176 | tf_op jit(solution)/shard_map/ppermute | solution.py:238
  54.3 4.6 %collective-permute-start.25 = (bf16[2,176,128]{2,1,0:T(8,128)(2,1)S(1)}, bf16[2,176,128]{2,1,0:T(8,128)(2,1)S(1)}, u32[]{:S(2)}, u32[]{:S(2)}) collective-permute-start(bf16[2,176,128]{2,1,0:T(8,128)(2,1)S(1)} %pad_maximum_fusion.3), channel_id=1, source_target_pairs={{0,8},{4,12},{8,0},{12,4},{16,24},{20,28},{24,16},{28,20},{1,9},{5... | collective-permute-start | bytes 270344 | tf_op jit(solution)/shard_map/ppermute | solution.py:238
  58.9 5.6 %collective-permute-start.26 = (bf16[4,176,128]{2,1,0:T(8,128)(2,1)S(1)}, bf16[4,176,128]{2,1,0:T(8,128)(2,1)S(1)}, u32[]{:S(2)}, u32[]{:S(2)}) collective-permute-start(bf16[4,176,128]{2,1,0:T(8,128)(2,1)S(1)} %pad_maximum_fusion.1), channel_id=1, source_target_pairs={{0,4},{4,0},{8,12},{12,8},{16,20},{20,16},{24,28},{28,24},{1,5},{5... | collective-permute-start | bytes 540680 | tf_op jit(solution)/shard_map/ppermute | solution.py:238
  64.5 7.5 %collective-permute-start.28 = (bf16[8,176,128]{2,1,0:T(8,128)(2,1)S(1)}, bf16[8,176,128]{2,1,0:T(8,128)(2,1)S(1)}, u32[]{:S(2)}, u32[]{:S(2)}) collective-permute-start(bf16[8,176,128]{2,1,0:T(8,128)(2,1)S(1)} %pad_maximum_fusion.refs_0_), channel_id=1, source_target_pairs={{0,2},{1,3},{2,0},{3,1},{4,6},{5,7},{6,4},{7,5},{8,10},{9,11},{10,... | collective-permute-start | bytes 1081352 | tf_op jit(solution)/shard_map/ppermute | solution.py:238
  66.1 20.0 %collective-permute-start.27 = (bf16[8,176,128]{2,1,0:T(8,128)(2,1)S(1)}, bf16[8,176,128]{2,1,0:T(8,128)(2,1)S(1)}, u32[]{:S(2)}, u32[]{:S(2)}) collective-permute-start(bf16[8,176,128]{2,1,0:T(8,128)(2,1)S(1)} %pad_maximum_fusion.refs_0_), channel_id=1, source_target_pairs={{0,1},{1,0},{2,3},{3,2},{4,5},{5,4},{6,7},{7,6},{8,9},{9,8},{10,11... | collective-permute-start | bytes 1081352 | tf_op jit(solution)/shard_map/ppermute | solution.py:238
  72.0 14.1 %collective-permute-start.29 = (bf16[8,176,128]{2,1,0:T(8,128)(2,1)S(1)}, bf16[8,176,128]{2,1,0:T(8,128)(2,1)S(1)}, u32[]{:S(2)}, u32[]{:S(2)}) collective-permute-start(bf16[8,176,128]{2,1,0:T(8,128)(2,1)S(1)} %collective-permute-done.28.refs_2_), channel_id=1, source_target_pairs={{0,1},{1,0},{2,3},{3,2},{4,5},{5,4},{6,7},{7,6},{8,9},{9,8},{10,11... | collective-permute-start | bytes 1081352 | tf_op jit(solution)/shard_map/ppermute | solution.py:238
  72.0 5.4 %collective-permute-start.16 = (bf16[10,64,128]{2,1,0:T(8,128)(2,1)S(1)}, bf16[10,64,128]{2,1,0:T(8,128)(2,1)S(1)}, u32[]{:S(2)}, u32[]{:S(2)}) collective-permute-start(bf16[10,64,128]{2,1,0:T(8,128)(2,1)S(1)} %get-tuple-element.46.own), channel_id=1, source_target_pairs={{4,8},{8,4},{12,16},{16,12},{20,24},{24,20},{5,9},{9,5},{13,17},{1... | collective-permute-start | bytes 491528 | tf_op jit(solution)/shard_map/ppermute | solution.py:244
  72.7 11.7 %collective-permute-start.15 = (bf16[10,64,128]{2,1,0:T(8,128)(2,1)S(1)}, bf16[10,64,128]{2,1,0:T(8,128)(2,1)S(1)}, u32[]{:S(2)}, u32[]{:S(2)}) collective-permute-start(bf16[10,64,128]{2,1,0:T(8,128)(2,1)S(1)} %get-tuple-element.46.own), channel_id=1, source_target_pairs={{0,4},{4,0},{8,12},{12,8},{16,20},{20,16},{24,28},{28,24},{1,5},{5... | collective-permute-start | bytes 491528 | tf_op jit(solution)/shard_map/ppermute | solution.py:238

commit v6 on v5

--- a/solution.py
+++ b/solution.py
@@ -32,35 +32,24 @@
 
 
 def pack_kernel(n_gy, turn_deep, deep, level, *rest):
-    level_outs, rest = rest[:n_gy], rest[n_gy:]
+    level_outs, level_t = rest[:n_gy], rest[-1]
     turned = level[...].astype(F32).T.astype(BF16)
     part = turned.shape[0] // n_gy
-    level_t = rest[-1]
     for owner in range(n_gy):
         level_t[owner] = turned[owner * part : (owner + 1) * part]
     me = lax.axis_index("gy")
     for code in range(n_gy):
         level_outs[code][...] = level_t[jnp.bitwise_xor(me, code)]
     if turn_deep:
-        deep_outs, deep_t = rest[:-2], rest[-2]
+        deep_out = rest[n_gy]
         for plane in range(deep.shape[0]):
-            deep_t[plane] = deep[plane].astype(F32).T.astype(BF16)
-        me = lax.axis_index("gz")
-        for code in range(len(deep_outs)):
-            deep_outs[code][...] = deep_t[jnp.bitwise_xor(me, code) // 2]
-
-
-def mask_kernel(n_gy, pre, skip, weight, *rest):
-    deeps, outs = rest[: -n_gy - 2], rest[-n_gy - 2 : -2]
-    deep_t, down_all = rest[-2:]
-    share = deeps[0].shape[0]
-    if len(deeps) > 1:
-        source = lax.axis_index("gz")
-        for code, ref in enumerate(deeps):
-            first = pl.multiple_of(jnp.bitwise_xor(source, code) * share, share)
-            deep_t[pl.ds(first, share)] = ref[...]
-    else:
-        deep_t[...] = deeps[0][...]
+            turned = deep[plane].astype(F32).T.astype(BF16)
+            deep_out[2 * plane] = turned
+            deep_out[2 * plane + 1] = turned
+
+
+def mask_kernel(n_gy, pre, skip, weight, deep_t, *rest):
+    outs, down_all = rest[:-1], rest[-1]
     rows, cols, channels = pre.shape
     half = rows // 2
     deep_cols = cols // 2
@@ -124,8 +113,7 @@
 def weight_kernel(n_gy, conv_rows, down_rows, shape, *refs):
     even, own, odd = refs[:3]
     shared = refs[3 : 3 + n_gy]
-    near, wide, level, parts = refs[-4:]
-    outs = refs[3 + n_gy : -4]
+    parts, near, wide, level = refs[3 + n_gy :]
     rows, cols, channels = shape
     part = own.shape[1]
     cells = rows * cols
@@ -171,12 +159,6 @@
     blank = n_gz * down_rows - count
     for row, owner, inner, take in segments(blank, down_rows, down_rows, count):
         parts[owner, pl.ds(conv_rows + inner, take)] = jnp.zeros((take, channels), BF16)
-    if len(outs) > 1:
-        me = lax.axis_index("gz")
-        for code, out in enumerate(outs):
-            out[...] = parts[jnp.bitwise_xor(me, code)]
-    else:
-        outs[0][...] = parts[...]
 
 
 def input_kernel(even, own, odd, weight, out):
@@ -213,24 +195,21 @@
 def place_kernel(n_gy, conv_rows, down_rows, *refs):
     blocks, (conv, down) = refs[:n_gy], refs[n_gy:]
     me = lax.axis_index("gy")
-    line = lax.axis_index("gz")
     part = conv.shape[2]
     count, deep_channels = down.shape[2:]
     channels = conv.shape[3]
-    n_gz = blocks[0].shape[0]
-    places = [reversed_bits(jnp.bitwise_xor(line, owner), n_gz) for owner in range(n_gz)]
     for code, block in enumerate(blocks):
         column = jnp.bitwise_xor(me, code)
         for row, owner, inner, take in segments(27 * part, conv_rows, part):
             conv[row // part, column, pl.ds(row % part, take)] = block[
-                places[owner], pl.ds(inner, take)
+                owner, pl.ds(inner, take)
             ]
         for a in range(2):
             base = conv_rows + a * down_rows
             for side in range(deep_channels // channels):
                 for row, owner, inner, take in segments(count, down_rows, count, side * count):
                     down[a, column, pl.ds(row, take), pl.ds(side * channels, channels)] = block[
-                        places[owner], pl.ds(base + inner, take)
+                        owner, pl.ds(base + inner, take)
                     ]
 
 
@@ -265,29 +244,24 @@
     down_count = 4 * deep_channels // n_gy
     down_rows = -(-down_count // (n_gz * 16)) * 16
     piece = conv_rows + down_rows
-    direct = n_gz <= 8
+    turn_deep = share % 16 == 0
     shape = jax.ShapeDtypeStruct
 
     level = level_input.reshape(cells, channels)
     deep = deep_cotangent.reshape(planes, deep_cells, share)
     packed = call(
-        lambda *refs: pack_kernel(n_gy, direct, *refs),
+        lambda *refs: pack_kernel(n_gy, turn_deep, *refs),
         [shape((part, cells), BF16)] * n_gy
-        + ([shape((share, deep_cells), BF16)] * n_gz if direct else []),
+        + [shape((2 * planes, share, deep_cells), BF16)] * turn_deep,
         deep,
         level,
-        scratch=([pltpu.VMEM((planes, share, deep_cells), BF16)] if direct else [])
-        + [pltpu.VMEM((n_gy, part, cells), BF16)],
-    )
-    level_t, deep_t = packed[:n_gy], packed[n_gy:]
-    if direct:
-        deep_t = [swapped(value, "gz", code) if code else value for code, value in enumerate(deep_t)]
-    else:
-        turned = jnp.repeat(jnp.swapaxes(deep, 1, 2), 2, axis=0)
-        deep_t = [exchanged(turned, "gz").reshape(deep_channels, deep_cells)]
-    level_t = jnp.stack(
-        [swapped(value, "gy", code) if code else value for code, value in enumerate(level_t)]
-    )
+        scratch=[pltpu.VMEM((n_gy, part, cells), BF16)],
+    )
+    level_t = packed[:n_gy]
+    deep_t = packed[n_gy] if turn_deep else jnp.repeat(jnp.swapaxes(deep, 1, 2), 2, axis=0)
+    deep_t = exchanged(deep_t, "gz").reshape(deep_channels, deep_cells)
+    level_t = [swapped(value, "gy", code) if code else value for code, value in enumerate(level_t)]
+    deep_t, level_t = lax.optimization_barrier((deep_t, jnp.stack(level_t)))
     down_slice = lax.dynamic_index_in_dim(down_weight, parity, 0, keepdims=False)
     shared = call(
         lambda *refs: mask_kernel(n_gy, *refs),
@@ -295,22 +269,17 @@
         pre_activation[0],
         skip_cotangent[0],
         down_slice,
-        *deep_t,
-        scratch=[
-            pltpu.VMEM((deep_channels, deep_cells), BF16),
-            pltpu.VMEM((n_gy, 4 * channels // n_gy, deep_channels), BF16),
-        ],
+        deep_t,
+        scratch=[pltpu.VMEM((n_gy, 4 * channels // n_gy, deep_channels), BF16)],
     )
     shared = [swapped(value, "gy", code) if code else value for code, value in enumerate(shared)]
     even, odd = neighbours(level_t)
-    *parts, near = call(
+    parts, near = call(
         lambda *refs: weight_kernel(n_gy, conv_rows, down_rows, (rows, cols, channels), *refs),
         (
-            [shape((piece, channels), BF16)] * n_gz
-            if direct
-            else [shape((n_gz, piece, channels), BF16)]
-        )
-        + [shape((rows + 2, cols, channels), BF16)],
+            shape((n_gz, piece, channels), BF16),
+            shape((rows + 2, cols, channels), BF16),
+        ),
         even,
         level_t,
         odd,
@@ -318,30 +287,30 @@
         scratch=[
             pltpu.VMEM((n_gy * rows + 2, cols, 3 * channels), BF16),
             pltpu.VMEM((n_gy, 3 * part, cells), BF16),
-            pltpu.VMEM((n_gz, piece, channels), BF16),
         ],
     )
+    parts = exchanged(parts, "gz").astype(F32)
     cell_total = devices * cells
-    if direct:
-        parts = [swapped(value, "gz", code) if code else value for code, value in enumerate(parts)]
-        same = sum(value.astype(F32) for value in parts[0::2])
-        other = sum(value.astype(F32) for value in parts[1::2])
-        first = jnp.where(parity == 0, same[conv_rows:], other[conv_rows:])
-        second = jnp.where(parity == 0, other[conv_rows:], same[conv_rows:])
-    else:
-        parts = exchanged(parts[0], "gz").astype(F32)
-        same, other = jnp.sum(parts[0::2], axis=0), jnp.sum(parts[1::2], axis=0)
-        first, second = same[conv_rows:], other[conv_rows:]
-    conv_sum = (same[:conv_rows] + other[:conv_rows]) / math.sqrt(cell_total)
-    down_sum = jnp.concatenate([first, second], axis=0) / math.sqrt(cell_total // 8)
-    block = jnp.concatenate([conv_sum, down_sum], axis=0).astype(BF16)[None]
-    code = n_gz // 2
-    while code:
-        block = jnp.concatenate([block, swapped(block, "gz", code)], axis=0)
-        code //= 2
+    conv_sum = jnp.sum(parts[:, :conv_rows], axis=0) / math.sqrt(cell_total)
+    slots = parts[:, conv_rows:].reshape(n_gz // 2, 2, down_rows, channels)
+    down_sum = jnp.sum(slots, axis=0) / math.sqrt(cell_total // 8)
+    final = jnp.concatenate([conv_sum, down_sum.reshape(2 * down_rows, channels)], axis=0)
+    final = final.astype(BF16)[None]
+    block = exchanged(jnp.broadcast_to(final, (n_gz,) + final.shape[1:]), "gz")
+    even, odd = neighbours(near)
+    input_grad = call(
+        input_kernel,
+        shape((rows, cols, channels), BF16),
+        even,
+        near,
+        odd,
+        conv_weight,
+    )
     blocks = [block]
     code = n_gy // 2
     while code:
+        if code == 1:
+            input_grad, *blocks = lax.optimization_barrier((input_grad, *blocks))
         blocks = blocks + [swapped(value, "gy", code) for value in blocks]
         code //= 2
     order = [reversed_bits(place, n_gy) for place in range(n_gy)]
@@ -353,15 +322,6 @@
             shape((2, n_gy, 4 * channels // n_gy, deep_channels), BF16),
         ),
         *blocks,
-    )
-    even, odd = neighbours(near)
-    input_grad = call(
-        input_kernel,
-        shape((rows, cols, channels), BF16),
-        even,
-        near,
-        odd,
-        conv_weight,
     )
     return (
         input_grad[None],

time: 87.6 us -> 76.4 us (0.87)
  blocking collectives: 0 us -> 29.8 us
  waiting for transfers between devices: 38.1 us -> 16.6 us
  starting transfers between devices: 41.2 us -> 21 us
    all_to_all x0 -> x2, blocking collectives: none -> 29.8 us  [exchanged(): return lax.all_to_all(value, axis, split_axis=0, concat_axis=0, tiled=True)]
    ppermute x28 -> x11, starting transfers between devices: 39.9 us -> 12.4 us  [swapped(): lax.ppermute(value, axis, [(i, i ^ code) for i in range(lax.axis_size(axi...]
    ppermute x28 -> x11, waiting for transfers between devices: 38.1 us -> 14.7 us  [swapped(): lax.ppermute(value, axis, [(i, i ^ code) for i in range(lax.axis_size(axi...]
    all_to_all x0 -> x1, starting transfers between devices: none -> 7.28 us  [exchanged(): return lax.all_to_all(value, axis, split_axis=0, concat_axis=0, tiled=True)]
    all_to_all x0 -> x1, waiting for transfers between devices: none -> 1.96 us  [exchanged(): return lax.all_to_all(value, axis, split_axis=0, concat_axis=0, tiled=True)]
  transfers between devices with their start and end apart: 30 -> 14, of which waited for: 10 -> 7; matrix products, arithmetic and copies ran while one was open for 0% -> 0% of each run, Pallas kernels for 3% -> 2%
where the time goes in v6:
time: 76.4 us; the launch traced here: 76.1 us
  blocking collectives  29.8 us (39%)
  starting transfers between devices  21 us (27%)
  waiting for transfers between devices  16.6 us (22%)
  Pallas kernels  5.76 us (8%)
  local copies, waits for them, and re-layouts  1.96 us (3%)
  between operations  0.79 us (1%)
    all_to_all x2, blocking collectives, exchanged(): return lax.all_to_all(value, axis, split_axis=0, concat_axis=0, tiled=True)  29.8 us
    ppermute x11, waiting for transfers between devices, swapped(): lax.ppermute(value, axis, [(i, i ^ code) for i in range(lax.axis_size(axi...  14.7 us
    ppermute x11, starting transfers between devices, swapped(): lax.ppermute(value, axis, [(i, i ^ code) for i in range(lax.axis_size(axi...  12.4 us
    all_to_all x1, starting transfers between devices, exchanged(): return lax.all_to_all(value, axis, split_axis=0, concat_axis=0, tiled=True)  7.28 us
    pallas_call x5, Pallas kernels, call(): pl.pallas_call(kernel, out_shape=out_shape, scratch_shapes=list(scratch),...  5.76 us
    all_to_all x1, waiting for transfers between devices, exchanged(): return lax.all_to_all(value, axis, split_axis=0, concat_axis=0, tiled=True)  1.96 us
    unnamed x12, local copies, waits for them, and re-layouts  1.88 us
  transfers between devices with their start and end apart: 14, of which 7 were waited for; matrix products, arithmetic and copies ran while one was open for 0% of the time, Pallas kernels for 2%

profile of v6, /device:TPU:0, one launch (start us, length us, event | category | flops | bytes accessed | tf_op | source)
XLA Modules:
  0.0 76.1 jit_solution(9892590617632269409)
XLA Ops:
  0.6 0.0 copy-start
  0.6 0.0 copy-start.2
  0.7 1.0 %copy-done.2 = bf16[4,4,32,32]{3,2,1,0:T(8,128)(2,1)S(1)} copy-done((bf16[4,4,32,32]{3,2,1,0:T(8,128)(2,1)S(1)}, bf16[4,4,32,32]{3,2,1,0:T(8,128)(2,1)}, u32[]{:S(2)}) %copy-start.2) | copy-done | bytes 32792
  1.6 0.0 copy-start.3
  1.6 0.9 %copy-done.3 = bf16[1,8,64,128]{3,2,1,0:T(8,128)(2,1)S(1)} copy-done((bf16[1,8,64,128]{3,2,1,0:T(8,128)(2,1)S(1)}, bf16[1,8,64,128]{3,2,1,0:T(8,128)(2,1)}, u32[]{:S(2)}) %copy-start.3) | copy-done | bytes 131096
  2.5 0.8 shard_map.85
  3.3 7.3 %all-to-all-start = ((bf16[8,32,128]{2,1,0:T(8,128)(2,1)}), bf16[8,32,128]{2,1,0:T(8,128)(2,1)S(1)}, u32[]{:S(2)}, u32[]{:S(2)}) async-start(bf16[8,32,128]{2,1,0:T(8,128)(2,1)} %get-tuple-element.21), calls=%async_computation | async-start | bytes 131072 | tf_op jit(solution)/shard_map/all_to_all | solution.py:227
  10.5 0.0 collective-permute-start
  10.6 1.6 %collective-permute-start.1 = (bf16[32,512]{1,0:T(8,128)(2,1)S(1)}, bf16[32,512]{1,0:T(8,128)(2,1)S(1)}, u32[]{:S(2)}, u32[]{:S(2)}) collective-permute-start(bf16[32,512]{1,0:T(8,128)(2,1)S(1)} %get-tuple-element.24), channel_id=1, source_target_pairs={{0,2},{1,3},{2,0},{3,1},{4,6},{5,7},{6,4},{7,5},{8,10},{9,11},{10,... | collective-permute-start | bytes 98312 | tf_op jit(solution)/shard_map/ppermute | solution.py:217
  12.1 0.3 collective-permute-start.2
  12.4 0.0 copy-done
  12.4 0.0 collective-permute-done
  12.4 2.1 %collective-permute-done.1 = bf16[32,512]{1,0:T(8,128)(2,1)S(1)} collective-permute-done((bf16[32,512]{1,0:T(8,128)(2,1)S(1)}, bf16[32,512]{1,0:T(8,128)(2,1)S(1)}, u32[]{:S(2)}, u32[]{:S(2)}) %collective-permute-start.1) | collective-permute-done | bytes 32800 | tf_op jit(solution)/shard_map/ppermute | solution.py:217
  14.5 0.9 %collective-permute-done.2 = bf16[32,512]{1,0:T(8,128)(2,1)S(1)} collective-permute-done((bf16[32,512]{1,0:T(8,128)(2,1)S(1)}, bf16[32,512]{1,0:T(8,128)(2,1)S(1)}, u32[]{:S(2)}, u32[]{:S(2)}) %collective-permute-start.2) | collective-permute-done | bytes 32800 | tf_op jit(solution)/shard_map/ppermute | solution.py:217
  15.5 0.0 copy-start.4
  15.5 0.0 copy-start.5
  15.5 2.0 %all-to-all-done = bf16[8,32,128]{2,1,0:T(8,128)(2,1)S(1)} async-done(((bf16[8,32,128]{2,1,0:T(8,128)(2,1)}), bf16[8,32,128]{2,1,0:T(8,128)(2,1)S(1)}, u32[]{:S(2)}, u32[]{:S(2)}) %all-to-all-start) | async-done | bytes 65568 | tf_op jit(solution)/shard_map/all_to_all | solution.py:227
  17.5 0.0 copy-done.4
  17.5 0.0 copy-done.5
  17.5 0.6 shard_map.86
  18.1 0.1 collective-permute-start.5
  18.2 1.6 %collective-permute-start.6 = (bf16[768,128]{1,0:T(8,128)(2,1)S(1)}, bf16[768,128]{1,0:T(8,128)(2,1)S(1)}, u32[]{:S(2)}, u32[]{:S(2)}) collective-permute-start(bf16[768,128]{1,0:T(8,128)(2,1)S(1)} %get-tuple-element.30), channel_id=1, source_target_pairs={{0,2},{1,3},{2,0},{3,1},{4,6},{5,7},{6,4},{7,5},{8,10},{9,11},{10,... | collective-permute-start | bytes 589832 | tf_op jit(solution)/shard_map/ppermute | solution.py:217
  19.7 0.3 collective-permute-start.7
  20.0 0.7 collective-permute-start.4
  20.7 3.7 %collective-permute-start.3 = (bf16[4,32,512]{2,1,0:T(8,128)(2,1)S(1)}, bf16[4,32,512]{2,1,0:T(8,128)(2,1)S(1)}, u32[]{:S(2)}, u32[]{:S(2)}) collective-permute-start(bf16[4,32,512]{2,1,0:T(8,128)(2,1)S(1)} %pad_maximum_fusion.refs_1_), channel_id=1, source_target_pairs={{0,4},{4,0},{8,12},{12,8},{16,20},{20,16},{24,28},{28,24},{1,5},{5... | collective-permute-start | bytes 393224 | tf_op jit(solution)/shard_map/ppermute | solution.py:217
  24.4 0.0 collective-permute-done.4.refs_2_
  24.4 5.9 %collective-permute-done.3.refs_0_ = bf16[4,32,512]{2,1,0:T(8,128)(2,1)S(1)} collective-permute-done((bf16[4,32,512]{2,1,0:T(8,128)(2,1)S(1)}, bf16[4,32,512]{2,1,0:T(8,128)(2,1)S(1)}, u32[]{:S(2)}, u32[]{:S(2)}) %collective-permute-start.3) | collective-permute-done | bytes 131104 | tf_op jit(solution)/shard_map/ppermute | solution.py:217
  30.3 0.0 collective-permute-done.5.refs_4_
  30.3 0.0 collective-permute-done.6.refs_5_
  30.3 0.0 collective-permute-done.7.refs_6_
  30.3 1.4 %shard_map.87 = (bf16[8,144,128]{2,1,0:T(8,128)(2,1)S(1)}, bf16[10,64,128]{2,1,0:T(8,128)(2,1)S(1)}) custom-call(bf16[4,32,512]{2,1,0:T(8,128)(2,1)S(1)} %collective-permute-done.3.refs_0_, bf16[4,32,512]{2,1,0:T(8,128)(2,1)S(1)} %pad_maximum_fusion.refs_1_, bf16[4,32,512]{2,1,0:T(8,128)(2,1)S(1)} %collective-permute-done.4.refs_2_, ...), custom_call_target="tpu_custom_call" | custom-call | tf_op jit(solution)/shard_map/pallas_call | solution.py:16
  31.7 15.6 %all_to_all.15 = bf16[8,144,128]{2,1,0:T(8,128)(2,1)S(1)} all-to-all(bf16[8,144,128]{2,1,0:T(8,128)(2,1)S(1)} %get-tuple-element.33), channel_id=1, replica_groups=mesh['gz'=8,'gy'=4] {'gz'}, dimensions={0} | all-to-all | bytes 589824 | tf_op jit(solution)/shard_map/all_to_all | solution.py:227
  47.4 0.0 copy-start.1
  47.5 14.2 %all_to_all.16.refs_0_ = bf16[8,176,128]{2,1,0:T(8,128)(2,1)S(1)} all-to-all(bf16[8,176,128]{2,1,0:T(8,128)(2,1)S(1)} %broadcast_in_dim.4), channel_id=1, replica_groups=mesh['gz'=8,'gy'=4] {'gz'}, dimensions={0} | all-to-all | bytes 720896 | tf_op jit(solution)/shard_map/all_to_all | solution.py:227
  61.7 0.8 %collective-permute-start.10 = (bf16[8,176,128]{2,1,0:T(8,128)(2,1)S(1)}, bf16[8,176,128]{2,1,0:T(8,128)(2,1)S(1)}, u32[]{:S(2)}, u32[]{:S(2)}) collective-permute-start(bf16[8,176,128]{2,1,0:T(8,128)(2,1)S(1)} %all_to_all.16.refs_0_), channel_id=1, source_target_pairs={{0,2},{1,3},{2,0},{3,1},{4,6},{5,7},{6,4},{7,5},{8,10},{9,11},{10,... | collective-permute-start | bytes 1081352 | tf_op jit(solution)/shard_map/ppermute | solution.py:217
  62.6 0.7 collective-permute-start.9
  63.3 3.6 %collective-permute-start.8 = (bf16[10,64,128]{2,1,0:T(8,128)(2,1)S(1)}, bf16[10,64,128]{2,1,0:T(8,128)(2,1)S(1)}, u32[]{:S(2)}, u32[]{:S(2)}) collective-permute-start(bf16[10,64,128]{2,1,0:T(8,128)(2,1)S(1)} %get-tuple-element.32.own), channel_id=1, source_target_pairs={{0,4},{4,0},{8,12},{12,8},{16,20},{20,16},{24,28},{28,24},{1,5},{5... | collective-permute-start | bytes 491528 | tf_op jit(solution)/shard_map/ppermute | solution.py:217
  66.8 0.0 collective-permute-done.9.odd
  66.9 4.1 %collective-permute-done.8.even = bf16[10,64,128]{2,1,0:T(8,128)(2,1)S(1)} collective-permute-done((bf16[10,64,128]{2,1,0:T(8,128)(2,1)S(1)}, bf16[10,64,128]{2,1,0:T(8,128)(2,1)S(1)}, u32[]{:S(2)}, u32[]{:S(2)}) %collective-permute-start.8) | collective-permute-done | bytes 163872 | tf_op jit(solution)/shard_map/ppermute | solution.py:217
  70.9 0.0 copy-done.1
  70.9 1.7 %shard_map.88 = bf16[8,64,128]{2,1,0:T(8,128)(2,1)} custom-call(bf16[10,64,128]{2,1,0:T(8,128)(2,1)S(1)} %collective-permute-done.8.even, bf16[10,64,128]{2,1,0:T(8,128)(2,1)S(1)} %get-tuple-element.32.own, bf16[10,64,128]{2,1,0:T(8,128)(2,1)S(1)} %collective-permute-done.9.odd, bf16[3,3,3,128,128]{4,3,2,1,0:T(8,128)(2,1)S(1)} %copy-done.1), custom_call_target="tpu_custom_call" | custom-call | tf_op jit(solution)/shard_map/pallas_call | solution.py:16
  72.7 0.0 collective-permute-done.10.refs_2_
  72.7 0.0 collective-permute-start.11
  72.7 0.5 collective-permute-start.12
  73.2 1.2 %collective-permute-done.11.refs_1_ = bf16[8,176,128]{2,1,0:T(8,128)(2,1)S(1)} collective-permute-done((bf16[8,176,128]{2,1,0:T(8,128)(2,1)S(1)}, bf16[8,176,128]{2,1,0:T(8,128)(2,1)S(1)}, u32[]{:S(2)}, u32[]{:S(2)}) %collective-permute-start.11) | collective-permute-done | bytes 360480 | tf_op jit(solution)/shard_map/ppermute | solution.py:217
  74.4 0.5 collective-permute-done.12.refs_3_
  74.9 1.2 %shard_map.89 = (bf16[27,4,32,128]{3,2,1,0:T(8,128)(2,1)}, bf16[2,4,128,256]{3,2,1,0:T(8,128)(2,1)}) custom-call(bf16[8,176,128]{2,1,0:T(8,128)(2,1)S(1)} %all_to_all.16.refs_0_, bf16[8,176,128]{2,1,0:T(8,128)(2,1)S(1)} %collective-permute-done.11.refs_1_, bf16[8,176,128]{2,1,0:T(8,128)(2,1)S(1)} %collective-permute-done.10.refs_2_, ...), custom_call_target="tpu_custom_call" | custom-call | tf_op jit(solution)/shard_map/pallas_call | solution.py:16
  (10 shorter events, 0.2 us)
Async XLA Ops:
  0.6 11.8 %copy-start = (bf16[2,2,2,128,256]{4,3,2,1,0:T(8,128)(2,1)S(1)}, bf16[2,2,2,128,256]{4,3,2,1,0:T(8,128)(2,1)}, u32[]{:S(2)}) copy-start(bf16[2,2,2,128,256]{4,3,2,1,0:T(8,128)(2,1)} %param.9) | copy-start | bytes 1572868
  0.6 1.0 %copy-start.2 = (bf16[4,4,32,32]{3,2,1,0:T(8,128)(2,1)S(1)}, bf16[4,4,32,32]{3,2,1,0:T(8,128)(2,1)}, u32[]{:S(2)}) copy-start(bf16[4,4,32,32]{3,2,1,0:T(8,128)(2,1)} %param.11) | copy-start | bytes 98308
  1.6 0.9 %copy-start.3 = (bf16[1,8,64,128]{3,2,1,0:T(8,128)(2,1)S(1)}, bf16[1,8,64,128]{3,2,1,0:T(8,128)(2,1)}, u32[]{:S(2)}) copy-start(bf16[1,8,64,128]{3,2,1,0:T(8,128)(2,1)} %param.6) | copy-start | bytes 393220
  3.3 14.2 %all-to-all-start = ((bf16[8,32,128]{2,1,0:T(8,128)(2,1)}), bf16[8,32,128]{2,1,0:T(8,128)(2,1)S(1)}, u32[]{:S(2)}, u32[]{:S(2)}) async-start(bf16[8,32,128]{2,1,0:T(8,128)(2,1)} %get-tuple-element.21), calls=%async_computation | async-start | bytes 131072 | tf_op jit(solution)/shard_map/all_to_all | solution.py:227
  10.5 1.9 %collective-permute-start = (bf16[32,512]{1,0:T(8,128)(2,1)S(1)}, bf16[32,512]{1,0:T(8,128)(2,1)S(1)}, u32[]{:S(2)}, u32[]{:S(2)}) collective-permute-start(bf16[32,512]{1,0:T(8,128)(2,1)S(1)} %get-tuple-element.23), channel_id=1, source_target_pairs={{0,1},{1,0},{2,3},{3,2},{4,5},{5,4},{6,7},{7,6},{8,9},{9,8},{10,11... | collective-permute-start | bytes 98312 | tf_op jit(solution)/shard_map/ppermute | solution.py:217
  10.6 4.0 %collective-permute-start.1 = (bf16[32,512]{1,0:T(8,128)(2,1)S(1)}, bf16[32,512]{1,0:T(8,128)(2,1)S(1)}, u32[]{:S(2)}, u32[]{:S(2)}) collective-permute-start(bf16[32,512]{1,0:T(8,128)(2,1)S(1)} %get-tuple-element.24), channel_id=1, source_target_pairs={{0,2},{1,3},{2,0},{3,1},{4,6},{5,7},{6,4},{7,5},{8,10},{9,11},{10,... | collective-permute-start | bytes 98312 | tf_op jit(solution)/shard_map/ppermute | solution.py:217
  12.1 3.4 %collective-permute-start.2 = (bf16[32,512]{1,0:T(8,128)(2,1)S(1)}, bf16[32,512]{1,0:T(8,128)(2,1)S(1)}, u32[]{:S(2)}, u32[]{:S(2)}) collective-permute-start(bf16[32,512]{1,0:T(8,128)(2,1)S(1)} %get-tuple-element.25), channel_id=1, source_target_pairs={{0,3},{1,2},{2,1},{3,0},{4,7},{5,6},{6,5},{7,4},{8,11},{9,10},{10,... | collective-permute-start | bytes 98312 | tf_op jit(solution)/shard_map/ppermute | solution.py:217
  15.5 2.0 %copy-start.4 = (bf16[1,8,64,128]{3,2,1,0:T(8,128)(2,1)S(1)}, bf16[1,8,64,128]{3,2,1,0:T(8,128)(2,1)}, u32[]{:S(2)}) copy-start(bf16[1,8,64,128]{3,2,1,0:T(8,128)(2,1)} %param.7) | copy-start | bytes 393220
  15.5 2.0 %copy-start.5 = (bf16[1,8,64,128]{3,2,1,0:T(8,128)(2,1)S(1)}, bf16[1,8,64,128]{3,2,1,0:T(8,128)(2,1)}, u32[]{:S(2)}) copy-start(bf16[1,8,64,128]{3,2,1,0:T(8,128)(2,1)} %param.10) | copy-start | bytes 393220
  18.1 12.2 %collective-permute-start.5 = (bf16[768,128]{1,0:T(8,128)(2,1)S(1)}, bf16[768,128]{1,0:T(8,128)(2,1)S(1)}, u32[]{:S(2)}, u32[]{:S(2)}) collective-permute-start(bf16[768,128]{1,0:T(8,128)(2,1)S(1)} %get-tuple-element.29), channel_id=1, source_target_pairs={{0,1},{1,0},{2,3},{3,2},{4,5},{5,4},{6,7},{7,6},{8,9},{9,8},{10,11... | collective-permute-start | bytes 589832 | tf_op jit(solution)/shard_map/ppermute | solution.py:217
  18.2 12.1 %collective-permute-start.6 = (bf16[768,128]{1,0:T(8,128)(2,1)S(1)}, bf16[768,128]{1,0:T(8,128)(2,1)S(1)}, u32[]{:S(2)}, u32[]{:S(2)}) collective-permute-start(bf16[768,128]{1,0:T(8,128)(2,1)S(1)} %get-tuple-element.30), channel_id=1, source_target_pairs={{0,2},{1,3},{2,0},{3,1},{4,6},{5,7},{6,4},{7,5},{8,10},{9,11},{10,... | collective-permute-start | bytes 589832 | tf_op jit(solution)/shard_map/ppermute | solution.py:217
  19.7 10.5 %collective-permute-start.7 = (bf16[768,128]{1,0:T(8,128)(2,1)S(1)}, bf16[768,128]{1,0:T(8,128)(2,1)S(1)}, u32[]{:S(2)}, u32[]{:S(2)}) collective-permute-start(bf16[768,128]{1,0:T(8,128)(2,1)S(1)} %get-tuple-element.31), channel_id=1, source_target_pairs={{0,3},{1,2},{2,1},{3,0},{4,7},{5,6},{6,5},{7,4},{8,11},{9,10},{10,... | collective-permute-start | bytes 589832 | tf_op jit(solution)/shard_map/ppermute | solution.py:217
  20.0 4.3 %collective-permute-start.4 = (bf16[4,32,512]{2,1,0:T(8,128)(2,1)S(1)}, bf16[4,32,512]{2,1,0:T(8,128)(2,1)S(1)}, u32[]{:S(2)}, u32[]{:S(2)}) collective-permute-start(bf16[4,32,512]{2,1,0:T(8,128)(2,1)S(1)} %pad_maximum_fusion.refs_1_), channel_id=1, source_target_pairs={{4,8},{8,4},{12,16},{16,12},{20,24},{24,20},{5,9},{9,5},{13,17},{1... | collective-permute-start | bytes 393224 | tf_op jit(solution)/shard_map/ppermute | solution.py:223
  20.7 9.6 %collective-permute-start.3 = (bf16[4,32,512]{2,1,0:T(8,128)(2,1)S(1)}, bf16[4,32,512]{2,1,0:T(8,128)(2,1)S(1)}, u32[]{:S(2)}, u32[]{:S(2)}) collective-permute-start(bf16[4,32,512]{2,1,0:T(8,128)(2,1)S(1)} %pad_maximum_fusion.refs_1_), channel_id=1, source_target_pairs={{0,4},{4,0},{8,12},{12,8},{16,20},{20,16},{24,28},{28,24},{1,5},{5... | collective-permute-start | bytes 393224 | tf_op jit(solution)/shard_map/ppermute | solution.py:217
  47.4 23.5 %copy-start.1 = (bf16[3,3,3,128,128]{4,3,2,1,0:T(8,128)(2,1)S(1)}, bf16[3,3,3,128,128]{4,3,2,1,0:T(8,128)(2,1)}, u32[]{:S(2)}) copy-start(bf16[3,3,3,128,128]{4,3,2,1,0:T(8,128)(2,1)} %weight.1) | copy-start | bytes 2654212
  61.7 10.9 %collective-permute-start.10 = (bf16[8,176,128]{2,1,0:T(8,128)(2,1)S(1)}, bf16[8,176,128]{2,1,0:T(8,128)(2,1)S(1)}, u32[]{:S(2)}, u32[]{:S(2)}) collective-permute-start(bf16[8,176,128]{2,1,0:T(8,128)(2,1)S(1)} %all_to_all.16.refs_0_), channel_id=1, source_target_pairs={{0,2},{1,3},{2,0},{3,1},{4,6},{5,7},{6,4},{7,5},{8,10},{9,11},{10,... | collective-permute-start | bytes 1081352 | tf_op jit(solution)/shard_map/ppermute | solution.py:217
  62.6 4.3 %collective-permute-start.9 = (bf16[10,64,128]{2,1,0:T(8,128)(2,1)S(1)}, bf16[10,64,128]{2,1,0:T(8,128)(2,1)S(1)}, u32[]{:S(2)}, u32[]{:S(2)}) collective-permute-start(bf16[10,64,128]{2,1,0:T(8,128)(2,1)S(1)} %get-tuple-element.32.own), channel_id=1, source_target_pairs={{4,8},{8,4},{12,16},{16,12},{20,24},{24,20},{5,9},{9,5},{13,17},{1... | collective-permute-start | bytes 491528 | tf_op jit(solution)/shard_map/ppermute | solution.py:223
  63.3 7.7 %collective-permute-start.8 = (bf16[10,64,128]{2,1,0:T(8,128)(2,1)S(1)}, bf16[10,64,128]{2,1,0:T(8,128)(2,1)S(1)}, u32[]{:S(2)}, u32[]{:S(2)}) collective-permute-start(bf16[10,64,128]{2,1,0:T(8,128)(2,1)S(1)} %get-tuple-element.32.own), channel_id=1, source_target_pairs={{0,4},{4,0},{8,12},{12,8},{16,20},{20,16},{24,28},{28,24},{1,5},{5... | collective-permute-start | bytes 491528 | tf_op jit(solution)/shard_map/ppermute | solution.py:217
  72.7 1.7 %collective-permute-start.11 = (bf16[8,176,128]{2,1,0:T(8,128)(2,1)S(1)}, bf16[8,176,128]{2,1,0:T(8,128)(2,1)S(1)}, u32[]{:S(2)}, u32[]{:S(2)}) collective-permute-start(bf16[8,176,128]{2,1,0:T(8,128)(2,1)S(1)} %all_to_all.16.refs_0_), channel_id=1, source_target_pairs={{0,1},{1,0},{2,3},{3,2},{4,5},{5,4},{6,7},{7,6},{8,9},{9,8},{10,11... | collective-permute-start | bytes 1081352 | tf_op jit(solution)/shard_map/ppermute | solution.py:217
  72.7 2.2 %collective-permute-start.12 = (bf16[8,176,128]{2,1,0:T(8,128)(2,1)S(1)}, bf16[8,176,128]{2,1,0:T(8,128)(2,1)S(1)}, u32[]{:S(2)}, u32[]{:S(2)}) collective-permute-start(bf16[8,176,128]{2,1,0:T(8,128)(2,1)S(1)} %collective-permute-done.10.refs_2_), channel_id=1, source_target_pairs={{0,1},{1,0},{2,3},{3,2},{4,5},{5,4},{6,7},{7,6},{8,9},{9,8},{10,11... | collective-permute-start | bytes 1081352 | tf_op jit(solution)/shard_map/ppermute | solution.py:217

commit v7 on v6

--- a/solution.py
+++ b/solution.py
@@ -31,21 +31,22 @@
     return jnp.where(keep, moved, 0.0)
 
 
-def pack_kernel(n_gy, turn_deep, deep, level, *rest):
-    level_outs, level_t = rest[:n_gy], rest[-1]
+def deep_kernel(deep, out):
+    for plane in range(deep.shape[0]):
+        turned = deep[plane].astype(F32).T.astype(BF16)
+        out[2 * plane] = turned
+        out[2 * plane + 1] = turned
+
+
+def level_kernel(level, *rest):
+    outs, level_t = rest[:-1], rest[-1]
     turned = level[...].astype(F32).T.astype(BF16)
-    part = turned.shape[0] // n_gy
-    for owner in range(n_gy):
+    part = level_t.shape[1]
+    for owner in range(len(outs)):
         level_t[owner] = turned[owner * part : (owner + 1) * part]
     me = lax.axis_index("gy")
-    for code in range(n_gy):
-        level_outs[code][...] = level_t[jnp.bitwise_xor(me, code)]
-    if turn_deep:
-        deep_out = rest[n_gy]
-        for plane in range(deep.shape[0]):
-            turned = deep[plane].astype(F32).T.astype(BF16)
-            deep_out[2 * plane] = turned
-            deep_out[2 * plane + 1] = turned
+    for code, out in enumerate(outs):
+        out[...] = level_t[jnp.bitwise_xor(me, code)]
 
 
 def mask_kernel(n_gy, pre, skip, weight, deep_t, *rest):
@@ -244,24 +245,25 @@
     down_count = 4 * deep_channels // n_gy
     down_rows = -(-down_count // (n_gz * 16)) * 16
     piece = conv_rows + down_rows
-    turn_deep = share % 16 == 0
     shape = jax.ShapeDtypeStruct
 
     level = level_input.reshape(cells, channels)
     deep = deep_cotangent.reshape(planes, deep_cells, share)
-    packed = call(
-        lambda *refs: pack_kernel(n_gy, turn_deep, *refs),
-        [shape((part, cells), BF16)] * n_gy
-        + [shape((2 * planes, share, deep_cells), BF16)] * turn_deep,
-        deep,
+    if share % 16 == 0:
+        deep_t = call(deep_kernel, shape((2 * planes, share, deep_cells), BF16), deep)
+    else:
+        deep_t = jnp.repeat(jnp.swapaxes(deep, 1, 2), 2, axis=0)
+    deep_t = exchanged(deep_t, "gz").reshape(deep_channels, deep_cells)
+    level_t = call(
+        level_kernel,
+        [shape((part, cells), BF16)] * n_gy,
         level,
         scratch=[pltpu.VMEM((n_gy, part, cells), BF16)],
     )
-    level_t = packed[:n_gy]
-    deep_t = packed[n_gy] if turn_deep else jnp.repeat(jnp.swapaxes(deep, 1, 2), 2, axis=0)
-    deep_t = exchanged(deep_t, "gz").reshape(deep_channels, deep_cells)
     level_t = [swapped(value, "gy", code) if code else value for code, value in enumerate(level_t)]
-    deep_t, level_t = lax.optimization_barrier((deep_t, jnp.stack(level_t)))
+    level_t = jnp.stack(level_t)
+    even, odd = neighbours(level_t)
+    deep_t, level_t = lax.optimization_barrier((deep_t, level_t))
     down_slice = lax.dynamic_index_in_dim(down_weight, parity, 0, keepdims=False)
     shared = call(
         lambda *refs: mask_kernel(n_gy, *refs),
@@ -273,7 +275,6 @@
         scratch=[pltpu.VMEM((n_gy, 4 * channels // n_gy, deep_channels), BF16)],
     )
     shared = [swapped(value, "gy", code) if code else value for code, value in enumerate(shared)]
-    even, odd = neighbours(level_t)
     parts, near = call(
         lambda *refs: weight_kernel(n_gy, conv_rows, down_rows, (rows, cols, channels), *refs),
         (
@@ -289,7 +290,9 @@
             pltpu.VMEM((n_gy, 3 * part, cells), BF16),
         ],
     )
-    parts = exchanged(parts, "gz").astype(F32)
+    near_even, near_odd = neighbours(near)
+    parts, near_even = lax.optimization_barrier((exchanged(parts, "gz"), near_even))
+    parts = parts.astype(F32)
     cell_total = devices * cells
     conv_sum = jnp.sum(parts[:, :conv_rows], axis=0) / math.sqrt(cell_total)
     slots = parts[:, conv_rows:].reshape(n_gz // 2, 2, down_rows, channels)
@@ -297,13 +300,13 @@
     final = jnp.concatenate([conv_sum, down_sum.reshape(2 * down_rows, channels)], axis=0)
     final = final.astype(BF16)[None]
     block = exchanged(jnp.broadcast_to(final, (n_gz,) + final.shape[1:]), "gz")
-    even, odd = neighbours(near)
+    block, near_odd = lax.optimization_barrier((block, near_odd))
     input_grad = call(
         input_kernel,
         shape((rows, cols, channels), BF16),
-        even,
+        near_even,
         near,
-        odd,
+        near_odd,
         conv_weight,
     )
     blocks = [block]

time: 76.4 us -> 77.1 us (level)
  the two profiles are of different devices: /device:TPU:0 before, /device:TPU:17 now
where the time goes in v7:
time: 77.1 us; the launch traced here: 76.7 us
  waiting for transfers between devices  35.2 us (46%)
  starting transfers between devices  31.3 us (41%)
  Pallas kernels  6.55 us (8%)
  local copies, waits for them, and re-layouts  2.72 us (4%)
  between operations  0.78 us (1%)
    ppermute x11, waiting for transfers between devices, swapped(): lax.ppermute(value, axis, [(i, i ^ code) for i in range(lax.axis_size(axi...  21.5 us
    all_to_all x3, starting transfers between devices, exchanged(): return lax.all_to_all(value, axis, split_axis=0, concat_axis=0, tiled=True)  14.9 us
    ppermute x2, waiting for transfers between devices, neighbours(): return (swapped(value, 'gz', 1), lax.ppermute(value, 'gz', odd))  13.7 us
    ppermute x11, starting transfers between devices, swapped(): lax.ppermute(value, axis, [(i, i ^ code) for i in range(lax.axis_size(axi...  10.2 us
    pallas_call x6, Pallas kernels, call(): pl.pallas_call(kernel, out_shape=out_shape, scratch_shapes=list(scratch),...  6.55 us
    ppermute x2, starting transfers between devices, neighbours(): return (swapped(value, 'gz', 1), lax.ppermute(value, 'gz', odd))  6.16 us
    unnamed x12, local copies, waits for them, and re-layouts  1.91 us
  transfers between devices with their start and end apart: 16, of which 9 were waited for; matrix products, arithmetic and copies ran while one was open for 0% of the time, Pallas kernels for 2%

profile of v7, /device:TPU:17, one launch (start us, length us, event | category | flops | bytes accessed | tf_op | source)
XLA Modules:
  0.0 76.7 jit_solution(16370278618756625225)
XLA Ops:
  0.6 0.0 copy-start
  0.6 0.0 copy-start.2
  0.7 1.0 %copy-done.2 = bf16[4,4,32,32]{3,2,1,0:T(8,128)(2,1)S(1)} copy-done((bf16[4,4,32,32]{3,2,1,0:T(8,128)(2,1)S(1)}, bf16[4,4,32,32]{3,2,1,0:T(8,128)(2,1)}, u32[]{:S(2)}) %copy-start.2) | copy-done | bytes 32792
  1.6 0.0 copy-start.3
  1.6 0.7 shard_map.86
  2.3 5.6 %all-to-all-start = ((bf16[8,32,128]{2,1,0:T(8,128)(2,1)}), bf16[8,32,128]{2,1,0:T(8,128)(2,1)S(1)}, u32[]{:S(2)}, u32[]{:S(2)}) async-start(bf16[8,32,128]{2,1,0:T(8,128)(2,1)} %shard_map.86), calls=%async_computation | async-start | bytes 131072 | tf_op jit(solution)/shard_map/all_to_all | solution.py:228
  7.9 0.0 copy-done.3
  7.9 0.1 shard_map.85
  8.1 1.3 %collective-permute-start = (bf16[32,512]{1,0:T(8,128)(2,1)S(1)}, bf16[32,512]{1,0:T(8,128)(2,1)S(1)}, u32[]{:S(2)}, u32[]{:S(2)}) collective-permute-start(bf16[32,512]{1,0:T(8,128)(2,1)S(1)} %get-tuple-element.25), channel_id=1, source_target_pairs={{0,1},{1,0},{2,3},{3,2},{4,5},{5,4},{6,7},{7,6},{8,9},{9,8},{10,11... | collective-permute-start | bytes 98312 | tf_op jit(solution)/shard_map/ppermute | solution.py:218
  9.4 1.2 %collective-permute-start.1 = (bf16[32,512]{1,0:T(8,128)(2,1)S(1)}, bf16[32,512]{1,0:T(8,128)(2,1)S(1)}, u32[]{:S(2)}, u32[]{:S(2)}) collective-permute-start(bf16[32,512]{1,0:T(8,128)(2,1)S(1)} %get-tuple-element.26), channel_id=1, source_target_pairs={{0,2},{1,3},{2,0},{3,1},{4,6},{5,7},{6,4},{7,5},{8,10},{9,11},{10,... | collective-permute-start | bytes 98312 | tf_op jit(solution)/shard_map/ppermute | solution.py:218
  10.6 0.5 collective-permute-start.2
  11.1 0.0 copy-done
  11.1 0.0 collective-permute-done
  11.1 1.3 %collective-permute-done.1 = bf16[32,512]{1,0:T(8,128)(2,1)S(1)} collective-permute-done((bf16[32,512]{1,0:T(8,128)(2,1)S(1)}, bf16[32,512]{1,0:T(8,128)(2,1)S(1)}, u32[]{:S(2)}, u32[]{:S(2)}) %collective-permute-start.1) | collective-permute-done | bytes 32800 | tf_op jit(solution)/shard_map/ppermute | solution.py:218
  12.4 1.5 %collective-permute-done.2 = bf16[32,512]{1,0:T(8,128)(2,1)S(1)} collective-permute-done((bf16[32,512]{1,0:T(8,128)(2,1)S(1)}, bf16[32,512]{1,0:T(8,128)(2,1)S(1)}, u32[]{:S(2)}, u32[]{:S(2)}) %collective-permute-start.2) | collective-permute-done | bytes 32800 | tf_op jit(solution)/shard_map/ppermute | solution.py:218
  13.9 0.0 copy-start.4
  13.9 0.0 copy-start.5
  13.9 0.0 all-to-all-done
  14.0 0.9 %copy-done.4 = bf16[1,8,64,128]{3,2,1,0:T(8,128)(2,1)S(1)} copy-done((bf16[1,8,64,128]{3,2,1,0:T(8,128)(2,1)S(1)}, bf16[1,8,64,128]{3,2,1,0:T(8,128)(2,1)}, u32[]{:S(2)}) %copy-start.4) | copy-done | bytes 131096
  14.8 0.1 copy-done.5
  14.9 0.6 shard_map.87
  15.5 0.4 collective-permute-start.5
  15.9 0.6 collective-permute-start.6
  16.5 1.2 %collective-permute-start.7 = (bf16[768,128]{1,0:T(8,128)(2,1)S(1)}, bf16[768,128]{1,0:T(8,128)(2,1)S(1)}, u32[]{:S(2)}, u32[]{:S(2)}) collective-permute-start(bf16[768,128]{1,0:T(8,128)(2,1)S(1)} %get-tuple-element.33), channel_id=1, source_target_pairs={{0,3},{1,2},{2,1},{3,0},{4,7},{5,6},{6,5},{7,4},{8,11},{9,10},{10,... | collective-permute-start | bytes 589832 | tf_op jit(solution)/shard_map/ppermute | solution.py:218
  17.7 3.1 %collective-permute-start.4 = (bf16[4,32,512]{2,1,0:T(8,128)(2,1)S(1)}, bf16[4,32,512]{2,1,0:T(8,128)(2,1)S(1)}, u32[]{:S(2)}, u32[]{:S(2)}) collective-permute-start(bf16[4,32,512]{2,1,0:T(8,128)(2,1)S(1)} %pad_maximum_fusion.refs_1_), channel_id=1, source_target_pairs={{4,8},{8,4},{12,16},{16,12},{20,24},{24,20},{5,9},{9,5},{13,17},{1... | collective-permute-start | bytes 393224 | tf_op jit(solution)/shard_map/ppermute | solution.py:224
  20.8 1.2 %collective-permute-start.3 = (bf16[4,32,512]{2,1,0:T(8,128)(2,1)S(1)}, bf16[4,32,512]{2,1,0:T(8,128)(2,1)S(1)}, u32[]{:S(2)}, u32[]{:S(2)}) collective-permute-start(bf16[4,32,512]{2,1,0:T(8,128)(2,1)S(1)} %pad_maximum_fusion.refs_1_), channel_id=1, source_target_pairs={{0,4},{4,0},{8,12},{12,8},{16,20},{20,16},{24,28},{28,24},{1,5},{5... | collective-permute-start | bytes 393224 | tf_op jit(solution)/shard_map/ppermute | solution.py:218
  22.1 3.5 %collective-permute-done.4.refs_2_ = bf16[4,32,512]{2,1,0:T(8,128)(2,1)S(1)} collective-permute-done((bf16[4,32,512]{2,1,0:T(8,128)(2,1)S(1)}, bf16[4,32,512]{2,1,0:T(8,128)(2,1)S(1)}, u32[]{:S(2)}, u32[]{:S(2)}) %collective-permute-start.4) | collective-permute-done | bytes 131104 | tf_op jit(solution)/shard_map/ppermute | solution.py:224
  25.6 3.1 %collective-permute-done.3.refs_0_ = bf16[4,32,512]{2,1,0:T(8,128)(2,1)S(1)} collective-permute-done((bf16[4,32,512]{2,1,0:T(8,128)(2,1)S(1)}, bf16[4,32,512]{2,1,0:T(8,128)(2,1)S(1)}, u32[]{:S(2)}, u32[]{:S(2)}) %collective-permute-start.3) | collective-permute-done | bytes 131104 | tf_op jit(solution)/shard_map/ppermute | solution.py:218
  28.8 0.0 collective-permute-done.5.refs_4_
  28.8 0.0 collective-permute-done.6.refs_5_
  28.8 0.0 collective-permute-done.7.refs_6_
  28.8 2.1 %shard_map.88 = (bf16[8,144,128]{2,1,0:T(8,128)(2,1)}, bf16[10,64,128]{2,1,0:T(8,128)(2,1)S(1)}) custom-call(bf16[4,32,512]{2,1,0:T(8,128)(2,1)S(1)} %collective-permute-done.3.refs_0_, bf16[4,32,512]{2,1,0:T(8,128)(2,1)S(1)} %pad_maximum_fusion.refs_1_, bf16[4,32,512]{2,1,0:T(8,128)(2,1)S(1)} %collective-permute-done.4.refs_2_, ...), custom_call_target="tpu_custom_call" | custom-call | tf_op jit(solution)/shard_map/pallas_call | solution.py:16
  30.9 4.6 %all-to-all-start.1 = ((bf16[8,144,128]{2,1,0:T(8,128)(2,1)}), bf16[8,144,128]{2,1,0:T(8,128)(2,1)S(1)}, u32[]{:S(2)}, u32[]{:S(2)}) async-start(bf16[8,144,128]{2,1,0:T(8,128)(2,1)} %get-tuple-element.34), calls=%async_computation.1 | async-start | bytes 589824 | tf_op jit(solution)/shard_map/all_to_all | solution.py:228
  35.5 1.2 %collective-permute-start.8 = (bf16[10,64,128]{2,1,0:T(8,128)(2,1)S(1)}, bf16[10,64,128]{2,1,0:T(8,128)(2,1)S(1)}, u32[]{:S(2)}, u32[]{:S(2)}) collective-permute-start(bf16[10,64,128]{2,1,0:T(8,128)(2,1)S(1)} %get-tuple-element.35.own), channel_id=1, source_target_pairs={{0,4},{4,0},{8,12},{12,8},{16,20},{20,16},{24,28},{28,24},{1,5},{5... | collective-permute-start | bytes 491528 | tf_op jit(solution)/shard_map/ppermute | solution.py:218
  36.6 7.1 %collective-permute-done.8.even = bf16[10,64,128]{2,1,0:T(8,128)(2,1)S(1)} collective-permute-done((bf16[10,64,128]{2,1,0:T(8,128)(2,1)S(1)}, bf16[10,64,128]{2,1,0:T(8,128)(2,1)S(1)}, u32[]{:S(2)}, u32[]{:S(2)}) %collective-permute-start.8) | collective-permute-done | bytes 163872 | tf_op jit(solution)/shard_map/ppermute | solution.py:218
  43.8 0.0 all-to-all-done.1
  43.9 0.0 copy-start.1
  44.0 0.8 %broadcast_in_dim.4 = bf16[8,176,128]{2,1,0:T(8,128)(2,1)} broadcast(bf16[176,128]{1,0:T(8,128)(2,1)S(1)} %pad_maximum_fusion.1), dimensions={1,2} | broadcast | bytes 405504 | tf_op jit(solution)/shard_map/broadcast_in_dim | solution.py:302
  44.7 4.8 %all-to-all-start.2 = ((bf16[8,176,128]{2,1,0:T(8,128)(2,1)}), bf16[8,176,128]{2,1,0:T(8,128)(2,1)S(1)}, u32[]{:S(2)}, u32[]{:S(2)}) async-start(bf16[8,176,128]{2,1,0:T(8,128)(2,1)} %broadcast_in_dim.4), calls=%async_computation.2 | async-start | bytes 720896 | tf_op jit(solution)/shard_map/all_to_all | solution.py:228
  49.5 3.1 %collective-permute-start.9 = (bf16[10,64,128]{2,1,0:T(8,128)(2,1)S(1)}, bf16[10,64,128]{2,1,0:T(8,128)(2,1)S(1)}, u32[]{:S(2)}, u32[]{:S(2)}) collective-permute-start(bf16[10,64,128]{2,1,0:T(8,128)(2,1)S(1)} %get-tuple-element.35.own), channel_id=1, source_target_pairs={{4,8},{8,4},{12,16},{16,12},{20,24},{24,20},{5,9},{9,5},{13,17},{1... | collective-permute-start | bytes 491528 | tf_op jit(solution)/shard_map/ppermute | solution.py:224
  52.6 10.2 %collective-permute-done.9.odd = bf16[10,64,128]{2,1,0:T(8,128)(2,1)S(1)} collective-permute-done((bf16[10,64,128]{2,1,0:T(8,128)(2,1)S(1)}, bf16[10,64,128]{2,1,0:T(8,128)(2,1)S(1)}, u32[]{:S(2)}, u32[]{:S(2)}) %collective-permute-start.9) | collective-permute-done | bytes 163872 | tf_op jit(solution)/shard_map/ppermute | solution.py:224
  62.8 0.0 all-to-all-done.2.refs_0_
  62.8 0.6 collective-permute-start.10
  63.4 0.0 copy-done.1
  63.4 1.7 %shard_map.89 = bf16[8,64,128]{2,1,0:T(8,128)(2,1)} custom-call(bf16[10,64,128]{2,1,0:T(8,128)(2,1)S(1)} %collective-permute-done.8.even, bf16[10,64,128]{2,1,0:T(8,128)(2,1)S(1)} %get-tuple-element.35.own, bf16[10,64,128]{2,1,0:T(8,128)(2,1)S(1)} %collective-permute-done.9.odd, bf16[3,3,3,128,128]{4,3,2,1,0:T(8,128)(2,1)S(1)} %copy-done.1), custom_call_target="tpu_custom_call" | custom-call | tf_op jit(solution)/shard_map/pallas_call | solution.py:16
  65.1 6.5 %collective-permute-done.10.refs_2_ = bf16[8,176,128]{2,1,0:T(8,128)(2,1)S(1)} collective-permute-done((bf16[8,176,128]{2,1,0:T(8,128)(2,1)S(1)}, bf16[8,176,128]{2,1,0:T(8,128)(2,1)S(1)}, u32[]{:S(2)}, u32[]{:S(2)}) %collective-permute-start.10) | collective-permute-done | bytes 360480 | tf_op jit(solution)/shard_map/ppermute | solution.py:218
  71.7 1.9 %collective-permute-start.11 = (bf16[8,176,128]{2,1,0:T(8,128)(2,1)S(1)}, bf16[8,176,128]{2,1,0:T(8,128)(2,1)S(1)}, u32[]{:S(2)}, u32[]{:S(2)}) collective-permute-start(bf16[8,176,128]{2,1,0:T(8,128)(2,1)S(1)} %all-to-all-done.2.refs_0_), channel_id=1, source_target_pairs={{0,1},{1,0},{2,3},{3,2},{4,5},{5,4},{6,7},{7,6},{8,9},{9,8},{10,11... | collective-permute-start | bytes 1081352 | tf_op jit(solution)/shard_map/ppermute | solution.py:218
  73.6 0.0 collective-permute-start.12
  73.6 1.3 %collective-permute-done.11.refs_1_ = bf16[8,176,128]{2,1,0:T(8,128)(2,1)S(1)} collective-permute-done((bf16[8,176,128]{2,1,0:T(8,128)(2,1)S(1)}, bf16[8,176,128]{2,1,0:T(8,128)(2,1)S(1)}, u32[]{:S(2)}, u32[]{:S(2)}) %collective-permute-start.11) | collective-permute-done | bytes 360480 | tf_op jit(solution)/shard_map/ppermute | solution.py:218
  74.9 0.5 collective-permute-done.12.refs_3_
  75.4 1.2 %shard_map.90 = (bf16[27,4,32,128]{3,2,1,0:T(8,128)(2,1)}, bf16[2,4,128,256]{3,2,1,0:T(8,128)(2,1)}) custom-call(bf16[8,176,128]{2,1,0:T(8,128)(2,1)S(1)} %all-to-all-done.2.refs_0_, bf16[8,176,128]{2,1,0:T(8,128)(2,1)S(1)} %collective-permute-done.11.refs_1_, bf16[8,176,128]{2,1,0:T(8,128)(2,1)S(1)} %collective-permute-done.10.refs_2_, ...), custom_call_target="tpu_custom_call" | custom-call | tf_op jit(solution)/shard_map/pallas_call | solution.py:16
  (9 shorter events, 0.1 us)
Async XLA Ops:
  0.6 10.4 %copy-start = (bf16[2,2,2,128,256]{4,3,2,1,0:T(8,128)(2,1)S(1)}, bf16[2,2,2,128,256]{4,3,2,1,0:T(8,128)(2,1)}, u32[]{:S(2)}) copy-start(bf16[2,2,2,128,256]{4,3,2,1,0:T(8,128)(2,1)} %param.9) | copy-start | bytes 1572868
  0.6 1.0 %copy-start.2 = (bf16[4,4,32,32]{3,2,1,0:T(8,128)(2,1)S(1)}, bf16[4,4,32,32]{3,2,1,0:T(8,128)(2,1)}, u32[]{:S(2)}) copy-start(bf16[4,4,32,32]{3,2,1,0:T(8,128)(2,1)} %param.11) | copy-start | bytes 98308
  1.6 6.3 %copy-start.3 = (bf16[1,8,64,128]{3,2,1,0:T(8,128)(2,1)S(1)}, bf16[1,8,64,128]{3,2,1,0:T(8,128)(2,1)}, u32[]{:S(2)}) copy-start(bf16[1,8,64,128]{3,2,1,0:T(8,128)(2,1)} %param.6) | copy-start | bytes 393220
  2.3 11.6 %all-to-all-start = ((bf16[8,32,128]{2,1,0:T(8,128)(2,1)}), bf16[8,32,128]{2,1,0:T(8,128)(2,1)S(1)}, u32[]{:S(2)}, u32[]{:S(2)}) async-start(bf16[8,32,128]{2,1,0:T(8,128)(2,1)} %shard_map.86), calls=%async_computation | async-start | bytes 131072 | tf_op jit(solution)/shard_map/all_to_all | solution.py:228
  8.1 3.0 %collective-permute-start = (bf16[32,512]{1,0:T(8,128)(2,1)S(1)}, bf16[32,512]{1,0:T(8,128)(2,1)S(1)}, u32[]{:S(2)}, u32[]{:S(2)}) collective-permute-start(bf16[32,512]{1,0:T(8,128)(2,1)S(1)} %get-tuple-element.25), channel_id=1, source_target_pairs={{0,1},{1,0},{2,3},{3,2},{4,5},{5,4},{6,7},{7,6},{8,9},{9,8},{10,11... | collective-permute-start | bytes 98312 | tf_op jit(solution)/shard_map/ppermute | solution.py:218
  9.4 3.1 %collective-permute-start.1 = (bf16[32,512]{1,0:T(8,128)(2,1)S(1)}, bf16[32,512]{1,0:T(8,128)(2,1)S(1)}, u32[]{:S(2)}, u32[]{:S(2)}) collective-permute-start(bf16[32,512]{1,0:T(8,128)(2,1)S(1)} %get-tuple-element.26), channel_id=1, source_target_pairs={{0,2},{1,3},{2,0},{3,1},{4,6},{5,7},{6,4},{7,5},{8,10},{9,11},{10,... | collective-permute-start | bytes 98312 | tf_op jit(solution)/shard_map/ppermute | solution.py:218
  10.6 3.3 %collective-permute-start.2 = (bf16[32,512]{1,0:T(8,128)(2,1)S(1)}, bf16[32,512]{1,0:T(8,128)(2,1)S(1)}, u32[]{:S(2)}, u32[]{:S(2)}) collective-permute-start(bf16[32,512]{1,0:T(8,128)(2,1)S(1)} %get-tuple-element.27), channel_id=1, source_target_pairs={{0,3},{1,2},{2,1},{3,0},{4,7},{5,6},{6,5},{7,4},{8,11},{9,10},{10,... | collective-permute-start | bytes 98312 | tf_op jit(solution)/shard_map/ppermute | solution.py:218
  13.9 0.9 %copy-start.4 = (bf16[1,8,64,128]{3,2,1,0:T(8,128)(2,1)S(1)}, bf16[1,8,64,128]{3,2,1,0:T(8,128)(2,1)}, u32[]{:S(2)}) copy-start(bf16[1,8,64,128]{3,2,1,0:T(8,128)(2,1)} %param.7) | copy-start | bytes 393220
  13.9 1.0 %copy-start.5 = (bf16[1,8,64,128]{3,2,1,0:T(8,128)(2,1)S(1)}, bf16[1,8,64,128]{3,2,1,0:T(8,128)(2,1)}, u32[]{:S(2)}) copy-start(bf16[1,8,64,128]{3,2,1,0:T(8,128)(2,1)} %param.10) | copy-start | bytes 393220
  15.5 13.2 %collective-permute-start.5 = (bf16[768,128]{1,0:T(8,128)(2,1)S(1)}, bf16[768,128]{1,0:T(8,128)(2,1)S(1)}, u32[]{:S(2)}, u32[]{:S(2)}) collective-permute-start(bf16[768,128]{1,0:T(8,128)(2,1)S(1)} %get-tuple-element.31), channel_id=1, source_target_pairs={{0,1},{1,0},{2,3},{3,2},{4,5},{5,4},{6,7},{7,6},{8,9},{9,8},{10,11... | collective-permute-start | bytes 589832 | tf_op jit(solution)/shard_map/ppermute | solution.py:218
  15.9 12.8 %collective-permute-start.6 = (bf16[768,128]{1,0:T(8,128)(2,1)S(1)}, bf16[768,128]{1,0:T(8,128)(2,1)S(1)}, u32[]{:S(2)}, u32[]{:S(2)}) collective-permute-start(bf16[768,128]{1,0:T(8,128)(2,1)S(1)} %get-tuple-element.32), channel_id=1, source_target_pairs={{0,2},{1,3},{2,0},{3,1},{4,6},{5,7},{6,4},{7,5},{8,10},{9,11},{10,... | collective-permute-start | bytes 589832 | tf_op jit(solution)/shard_map/ppermute | solution.py:218
  16.5 12.2 %collective-permute-start.7 = (bf16[768,128]{1,0:T(8,128)(2,1)S(1)}, bf16[768,128]{1,0:T(8,128)(2,1)S(1)}, u32[]{:S(2)}, u32[]{:S(2)}) collective-permute-start(bf16[768,128]{1,0:T(8,128)(2,1)S(1)} %get-tuple-element.33), channel_id=1, source_target_pairs={{0,3},{1,2},{2,1},{3,0},{4,7},{5,6},{6,5},{7,4},{8,11},{9,10},{10,... | collective-permute-start | bytes 589832 | tf_op jit(solution)/shard_map/ppermute | solution.py:218
  17.7 7.9 %collective-permute-start.4 = (bf16[4,32,512]{2,1,0:T(8,128)(2,1)S(1)}, bf16[4,32,512]{2,1,0:T(8,128)(2,1)S(1)}, u32[]{:S(2)}, u32[]{:S(2)}) collective-permute-start(bf16[4,32,512]{2,1,0:T(8,128)(2,1)S(1)} %pad_maximum_fusion.refs_1_), channel_id=1, source_target_pairs={{4,8},{8,4},{12,16},{16,12},{20,24},{24,20},{5,9},{9,5},{13,17},{1... | collective-permute-start | bytes 393224 | tf_op jit(solution)/shard_map/ppermute | solution.py:224
  20.8 7.9 %collective-permute-start.3 = (bf16[4,32,512]{2,1,0:T(8,128)(2,1)S(1)}, bf16[4,32,512]{2,1,0:T(8,128)(2,1)S(1)}, u32[]{:S(2)}, u32[]{:S(2)}) collective-permute-start(bf16[4,32,512]{2,1,0:T(8,128)(2,1)S(1)} %pad_maximum_fusion.refs_1_), channel_id=1, source_target_pairs={{0,4},{4,0},{8,12},{12,8},{16,20},{20,16},{24,28},{28,24},{1,5},{5... | collective-permute-start | bytes 393224 | tf_op jit(solution)/shard_map/ppermute | solution.py:218
  30.9 12.9 %all-to-all-start.1 = ((bf16[8,144,128]{2,1,0:T(8,128)(2,1)}), bf16[8,144,128]{2,1,0:T(8,128)(2,1)S(1)}, u32[]{:S(2)}, u32[]{:S(2)}) async-start(bf16[8,144,128]{2,1,0:T(8,128)(2,1)} %get-tuple-element.34), calls=%async_computation.1 | async-start | bytes 589824 | tf_op jit(solution)/shard_map/all_to_all | solution.py:228
  35.5 8.3 %collective-permute-start.8 = (bf16[10,64,128]{2,1,0:T(8,128)(2,1)S(1)}, bf16[10,64,128]{2,1,0:T(8,128)(2,1)S(1)}, u32[]{:S(2)}, u32[]{:S(2)}) collective-permute-start(bf16[10,64,128]{2,1,0:T(8,128)(2,1)S(1)} %get-tuple-element.35.own), channel_id=1, source_target_pairs={{0,4},{4,0},{8,12},{12,8},{16,20},{20,16},{24,28},{28,24},{1,5},{5... | collective-permute-start | bytes 491528 | tf_op jit(solution)/shard_map/ppermute | solution.py:218
  43.9 19.5 %copy-start.1 = (bf16[3,3,3,128,128]{4,3,2,1,0:T(8,128)(2,1)S(1)}, bf16[3,3,3,128,128]{4,3,2,1,0:T(8,128)(2,1)}, u32[]{:S(2)}) copy-start(bf16[3,3,3,128,128]{4,3,2,1,0:T(8,128)(2,1)} %weight.1) | copy-start | bytes 2654212
  44.7 18.0 %all-to-all-start.2 = ((bf16[8,176,128]{2,1,0:T(8,128)(2,1)}), bf16[8,176,128]{2,1,0:T(8,128)(2,1)S(1)}, u32[]{:S(2)}, u32[]{:S(2)}) async-start(bf16[8,176,128]{2,1,0:T(8,128)(2,1)} %broadcast_in_dim.4), calls=%async_computation.2 | async-start | bytes 720896 | tf_op jit(solution)/shard_map/all_to_all | solution.py:228
  49.5 13.3 %collective-permute-start.9 = (bf16[10,64,128]{2,1,0:T(8,128)(2,1)S(1)}, bf16[10,64,128]{2,1,0:T(8,128)(2,1)S(1)}, u32[]{:S(2)}, u32[]{:S(2)}) collective-permute-start(bf16[10,64,128]{2,1,0:T(8,128)(2,1)S(1)} %get-tuple-element.35.own), channel_id=1, source_target_pairs={{4,8},{8,4},{12,16},{16,12},{20,24},{24,20},{5,9},{9,5},{13,17},{1... | collective-permute-start | bytes 491528 | tf_op jit(solution)/shard_map/ppermute | solution.py:224
  62.8 8.9 %collective-permute-start.10 = (bf16[8,176,128]{2,1,0:T(8,128)(2,1)S(1)}, bf16[8,176,128]{2,1,0:T(8,128)(2,1)S(1)}, u32[]{:S(2)}, u32[]{:S(2)}) collective-permute-start(bf16[8,176,128]{2,1,0:T(8,128)(2,1)S(1)} %all-to-all-done.2.refs_0_), channel_id=1, source_target_pairs={{0,2},{1,3},{2,0},{3,1},{4,6},{5,7},{6,4},{7,5},{8,10},{9,11},{10,... | collective-permute-start | bytes 1081352 | tf_op jit(solution)/shard_map/ppermute | solution.py:218
  71.7 3.2 %collective-permute-start.11 = (bf16[8,176,128]{2,1,0:T(8,128)(2,1)S(1)}, bf16[8,176,128]{2,1,0:T(8,128)(2,1)S(1)}, u32[]{:S(2)}, u32[]{:S(2)}) collective-permute-start(bf16[8,176,128]{2,1,0:T(8,128)(2,1)S(1)} %all-to-all-done.2.refs_0_), channel_id=1, source_target_pairs={{0,1},{1,0},{2,3},{3,2},{4,5},{5,4},{6,7},{7,6},{8,9},{9,8},{10,11... | collective-permute-start | bytes 1081352 | tf_op jit(solution)/shard_map/ppermute | solution.py:218
  73.6 1.8 %collective-permute-start.12 = (bf16[8,176,128]{2,1,0:T(8,128)(2,1)S(1)}, bf16[8,176,128]{2,1,0:T(8,128)(2,1)S(1)}, u32[]{:S(2)}, u32[]{:S(2)}) collective-permute-start(bf16[8,176,128]{2,1,0:T(8,128)(2,1)S(1)} %collective-permute-done.10.refs_2_), channel_id=1, source_target_pairs={{0,1},{1,0},{2,3},{3,2},{4,5},{5,4},{6,7},{7,6},{8,9},{9,8},{10,11... | collective-permute-start | bytes 1081352 | tf_op jit(solution)/shard_map/ppermute | solution.py:218

commit v8 on v7

--- a/solution.py
+++ b/solution.py
@@ -31,11 +31,14 @@
     return jnp.where(keep, moved, 0.0)
 
 
-def deep_kernel(deep, out):
-    for plane in range(deep.shape[0]):
-        turned = deep[plane].astype(F32).T.astype(BF16)
-        out[2 * plane] = turned
-        out[2 * plane + 1] = turned
+def deep_kernel(deep, keep, send, turned):
+    planes = deep.shape[0]
+    half = planes // 2
+    for plane in range(planes):
+        turned[plane] = deep[plane].astype(F32).T.astype(BF16)
+    upper = lax.axis_index("gz") // planes
+    keep[...] = turned[pl.ds(upper * half, half)]
+    send[...] = turned[pl.ds((1 - upper) * half, half)]
 
 
 def level_kernel(level, *rest):
@@ -49,8 +52,17 @@
         out[...] = level_t[jnp.bitwise_xor(me, code)]
 
 
-def mask_kernel(n_gy, pre, skip, weight, deep_t, *rest):
-    outs, down_all = rest[:-1], rest[-1]
+def mask_kernel(n_gy, pre, skip, weight, *rest):
+    deeps, outs, (deep_t, down_all) = rest[: -n_gy - 2], rest[-n_gy - 2 : -2], rest[-2:]
+    if len(deeps) > 1:
+        count, share = deeps[0].shape[:2]
+        me = lax.axis_index("gz")
+        for place in range(2 * count):
+            owner = jnp.bitwise_xor(me, reversed_bits(place, 2 * count))
+            first = pl.multiple_of(owner * share, share)
+            deep_t[pl.ds(first, share)] = deeps[place // count][place % count]
+    else:
+        deep_t[...] = deeps[0][...]
     rows, cols, channels = pre.shape
     half = rows // 2
     deep_cols = cols // 2
@@ -111,14 +123,14 @@
     return low, high
 
 
-def weight_kernel(n_gy, conv_rows, down_rows, shape, *refs):
+def weight_kernel(n_gy, shape, *refs):
     even, own, odd = refs[:3]
     shared = refs[3 : 3 + n_gy]
-    parts, near, wide, level = refs[3 + n_gy :]
+    keep, send, down_out, near, wide, level, halves = refs[3 + n_gy :]
     rows, cols, channels = shape
     part = own.shape[1]
     cells = rows * cols
-    n_gz = parts.shape[0]
+    half = part // 2
     rows_all = n_gy * rows
     me = lax.axis_index("gy")
     low, high = sides(even, odd)
@@ -140,26 +152,20 @@
             slab = wide[pl.ds(2 - ky + owner * rows, rows)].reshape(cells, 3 * channels)
             term = jnp.dot(level[owner], slab, preferred_element_type=F32)
             total = term if total is None else total + term
-        total = total.astype(BF16)
         for kz in range(3):
             for kx in range(3):
                 value = total[kz * part : (kz + 1) * part, kx * channels : (kx + 1) * channels]
-                first = ((kz * 3 + ky) * 3 + kx) * part
-                for row, owner, inner, take in segments(part, conv_rows, part, first):
-                    parts[owner, pl.ds(inner, take)] = value[row : row + take]
-    blank = n_gz * conv_rows - 27 * part
-    for row, owner, inner, take in segments(blank, conv_rows, conv_rows, 27 * part):
-        parts[owner, pl.ds(inner, take)] = jnp.zeros((take, channels), BF16)
+                index = (kz * 3 + ky) * 3 + kx
+                for side in range(2):
+                    halves[side, pl.ds(index * half, half)] = value[side * half : (side + 1) * half]
+    side = lax.axis_index("gz") % 2
+    keep[...] = halves[side]
+    send[...] = halves[1 - side].astype(send.dtype)
     count = shared[0].shape[0] - cells
     down = shared[0][pl.ds(cells, count)].astype(F32)
     for code in range(1, n_gy):
         down = down + shared[code][pl.ds(cells, count)].astype(F32)
-    down = down.astype(BF16)
-    for row, owner, inner, take in segments(count, down_rows, count):
-        parts[owner, pl.ds(conv_rows + inner, take)] = down[row : row + take]
-    blank = n_gz * down_rows - count
-    for row, owner, inner, take in segments(blank, down_rows, down_rows, count):
-        parts[owner, pl.ds(conv_rows + inner, take)] = jnp.zeros((take, channels), BF16)
+    down_out[...] = down.astype(down_out.dtype)
 
 
 def input_kernel(even, own, odd, weight, out):
@@ -193,25 +199,21 @@
     return place
 
 
-def place_kernel(n_gy, conv_rows, down_rows, *refs):
-    blocks, (conv, down) = refs[:n_gy], refs[n_gy:]
+def place_kernel(n_gy, *refs):
+    blocks, (conv, down) = refs[: 2 * n_gy], refs[2 * n_gy :]
     me = lax.axis_index("gy")
-    part = conv.shape[2]
+    parity = lax.axis_index("gz") % 2
+    half, channels = conv.shape[3:]
     count, deep_channels = down.shape[2:]
-    channels = conv.shape[3]
-    for code, block in enumerate(blocks):
-        column = jnp.bitwise_xor(me, code)
-        for row, owner, inner, take in segments(27 * part, conv_rows, part):
-            conv[row // part, column, pl.ds(row % part, take)] = block[
-                owner, pl.ds(inner, take)
+    for index, block in enumerate(blocks):
+        side = jnp.bitwise_xor(parity, index // n_gy)
+        column = jnp.bitwise_xor(me, index % n_gy)
+        for k in range(27):
+            conv[k, column, side] = block[pl.ds(k * half, half)]
+        for wide in range(deep_channels // channels):
+            down[side, column, :, pl.ds(wide * channels, channels)] = block[
+                pl.ds(27 * half + wide * count, count)
             ]
-        for a in range(2):
-            base = conv_rows + a * down_rows
-            for side in range(deep_channels // channels):
-                for row, owner, inner, take in segments(count, down_rows, count, side * count):
-                    down[a, column, pl.ds(row, take), pl.ds(side * channels, channels)] = block[
-                        owner, pl.ds(base + inner, take)
-                    ]
 
 
 def swapped(value, axis, code):
@@ -241,19 +243,33 @@
     part = channels // n_gy
     cells = rows * cols
     deep_cells = deep_rows * deep_cols
-    conv_rows = -(-27 * part // (n_gz * 16)) * 16
+    half = part // 2
     down_count = 4 * deep_channels // n_gy
-    down_rows = -(-down_count // (n_gz * 16)) * 16
-    piece = conv_rows + down_rows
+    wire = BF16 if n_gz <= 8 else F32
     shape = jax.ShapeDtypeStruct
 
     level = level_input.reshape(cells, channels)
     deep = deep_cotangent.reshape(planes, deep_cells, share)
     if share % 16 == 0:
-        deep_t = call(deep_kernel, shape((2 * planes, share, deep_cells), BF16), deep)
+        keep, send = call(
+            deep_kernel,
+            [shape((planes // 2, share, deep_cells), BF16)] * 2,
+            deep,
+            scratch=[pltpu.VMEM((planes, share, deep_cells), BF16)],
+        )
+        code = planes
+        held = jnp.stack([keep, swapped(send, "gz", code)], axis=1)
+        while code > 2:
+            code //= 2
+            count = code // 2
+            upper = lax.axis_index("gz") // code % 2
+            keep = lax.dynamic_slice_in_dim(held, upper * count, count, axis=0)
+            send = lax.dynamic_slice_in_dim(held, (1 - upper) * count, count, axis=0)
+            held = jnp.concatenate([keep, swapped(send, "gz", code)], axis=1)
+        deep_t = [held[0], swapped(held[0], "gz", 1)]
     else:
         deep_t = jnp.repeat(jnp.swapaxes(deep, 1, 2), 2, axis=0)
-    deep_t = exchanged(deep_t, "gz").reshape(deep_channels, deep_cells)
+        deep_t = [exchanged(deep_t, "gz").reshape(deep_channels, deep_cells)]
     level_t = call(
         level_kernel,
         [shape((part, cells), BF16)] * n_gy,
@@ -263,7 +279,7 @@
     level_t = [swapped(value, "gy", code) if code else value for code, value in enumerate(level_t)]
     level_t = jnp.stack(level_t)
     even, odd = neighbours(level_t)
-    deep_t, level_t = lax.optimization_barrier((deep_t, level_t))
+    *deep_t, level_t = lax.optimization_barrier((*deep_t, level_t))
     down_slice = lax.dynamic_index_in_dim(down_weight, parity, 0, keepdims=False)
     shared = call(
         lambda *refs: mask_kernel(n_gy, *refs),
@@ -271,14 +287,19 @@
         pre_activation[0],
         skip_cotangent[0],
         down_slice,
-        deep_t,
-        scratch=[pltpu.VMEM((n_gy, 4 * channels // n_gy, deep_channels), BF16)],
+        *deep_t,
+        scratch=[
+            pltpu.VMEM((deep_channels, deep_cells), BF16),
+            pltpu.VMEM((n_gy, 4 * channels // n_gy, deep_channels), BF16),
+        ],
     )
     shared = [swapped(value, "gy", code) if code else value for code, value in enumerate(shared)]
-    parts, near = call(
-        lambda *refs: weight_kernel(n_gy, conv_rows, down_rows, (rows, cols, channels), *refs),
+    keep, send, down, near = call(
+        lambda *refs: weight_kernel(n_gy, (rows, cols, channels), *refs),
         (
-            shape((n_gz, piece, channels), BF16),
+            shape((27 * half, channels), F32),
+            shape((27 * half, channels), wire),
+            shape((down_count, channels), wire),
             shape((rows + 2, cols, channels), BF16),
         ),
         even,
@@ -288,19 +309,28 @@
         scratch=[
             pltpu.VMEM((n_gy * rows + 2, cols, 3 * channels), BF16),
             pltpu.VMEM((n_gy, 3 * part, cells), BF16),
+            pltpu.VMEM((2, 27 * half, channels), F32),
         ],
     )
     near_even, near_odd = neighbours(near)
-    parts, near_even = lax.optimization_barrier((exchanged(parts, "gz"), near_even))
-    parts = parts.astype(F32)
+    conv = (keep + swapped(send, "gz", 1).astype(F32)).astype(wire)
+    total = lax.optimization_barrier(jnp.concatenate([conv, down], axis=0))
+    code = n_gz // 2
+    while code > 1:
+        other = swapped(total, "gz", code)
+        if code == 4:
+            other, near_even = lax.optimization_barrier((other, near_even))
+        total = total.astype(F32) + other.astype(F32)
+        if code > 2:
+            total = lax.optimization_barrier(total.astype(wire))
+        code //= 2
     cell_total = devices * cells
-    conv_sum = jnp.sum(parts[:, :conv_rows], axis=0) / math.sqrt(cell_total)
-    slots = parts[:, conv_rows:].reshape(n_gz // 2, 2, down_rows, channels)
-    down_sum = jnp.sum(slots, axis=0) / math.sqrt(cell_total // 8)
-    final = jnp.concatenate([conv_sum, down_sum.reshape(2 * down_rows, channels)], axis=0)
-    final = final.astype(BF16)[None]
-    block = exchanged(jnp.broadcast_to(final, (n_gz,) + final.shape[1:]), "gz")
-    block, near_odd = lax.optimization_barrier((block, near_odd))
+    row = lax.broadcasted_iota(jnp.int32, total.shape, 0)
+    scale = jnp.where(
+        row < 27 * half, 1 / math.sqrt(cell_total), 1 / math.sqrt(cell_total // 8)
+    )
+    total = (total * scale).astype(BF16)
+    pair = [total, swapped(total, "gz", 1)]
     input_grad = call(
         input_kernel,
         shape((rows, cols, channels), BF16),
@@ -309,19 +339,20 @@
         near_odd,
         conv_weight,
     )
-    blocks = [block]
-    code = n_gy // 2
-    while code:
-        if code == 1:
-            input_grad, *blocks = lax.optimization_barrier((input_grad, *blocks))
-        blocks = blocks + [swapped(value, "gy", code) for value in blocks]
-        code //= 2
-    order = [reversed_bits(place, n_gy) for place in range(n_gy)]
-    blocks = [blocks[order[place]] for place in range(n_gy)]
+    blocks = []
+    for index, block in enumerate(pair):
+        line = [block]
+        code = n_gy // 2
+        while code:
+            if code == 1 and index == 1:
+                input_grad, *line = lax.optimization_barrier((input_grad, *line))
+            line = line + [swapped(value, "gy", code) for value in line]
+            code //= 2
+        blocks += [line[reversed_bits(place, n_gy)] for place in range(n_gy)]
     conv_grad, down_grad = call(
-        lambda *refs: place_kernel(n_gy, conv_rows, down_rows, *refs),
+        lambda *refs: place_kernel(n_gy, *refs),
         (
-            shape((27, n_gy, part, channels), BF16),
+            shape((27, n_gy, 2, half, channels), BF16),
             shape((2, n_gy, 4 * channels // n_gy, deep_channels), BF16),
         ),
         *blocks,

time: 77.1 us -> 72.6 us (0.942)
  waiting for transfers between devices: 35.2 us -> 32.5 us
  Pallas kernels: 6.55 us -> 5.35 us
  local copies, waits for them, and re-layouts: 2.72 us -> 1.74 us
    ppermute x11 -> x21, starting transfers between devices: 10.2 us -> 26.8 us  [swapped(): lax.ppermute(value, axis, [(i, i ^ code) for i in range(lax.axis_size(axi...]
    all_to_all x3 -> x0, starting transfers between devices: 14.9 us -> none  [exchanged(): return lax.all_to_all(value, axis, split_axis=0, concat_axis=0, tiled=True)]
    ppermute x2, waiting for transfers between devices: 13.7 us -> 8.29 us  [neighbours(): return (swapped(value, 'gz', 1), lax.ppermute(value, 'gz', odd))]
    ppermute x11 -> x21, waiting for transfers between devices: 21.5 us -> 24.2 us  [swapped(): lax.ppermute(value, axis, [(i, i ^ code) for i in range(lax.axis_size(axi...]
    pallas_call x6, Pallas kernels: 6.55 us -> 5.35 us  [call(): pl.pallas_call(kernel, out_shape=out_shape, scratch_shapes=list(scratch),...]
    ppermute x2, starting transfers between devices: 6.16 us -> 5.01 us  [neighbours(): return (swapped(value, 'gz', 1), lax.ppermute(value, 'gz', odd))]
    broadcast_in_dim x1 -> x0, local copies, waits for them, and re-layouts: 0.78 us -> none  [per_device(): block = exchanged(jnp.broadcast_to(final, (n_gz,) + final.shape[1:]), 'gz')]
  transfers between devices with their start and end apart: 16 -> 23, of which waited for: 9 -> 15; matrix products, arithmetic and copies ran while one was open for 0% -> 0% of each run, Pallas kernels for 2% -> 3%
where the time goes in v8:
time: 72.6 us; the launch traced here: 72.5 us
  waiting for transfers between devices  32.5 us (45%)
  starting transfers between devices  31.8 us (44%)
  Pallas kernels  5.35 us (7%)
  local copies, waits for them, and re-layouts  1.74 us (2%)
  between operations  0.79 us (1%)
    ppermute x21, starting transfers between devices, swapped(): lax.ppermute(value, axis, [(i, i ^ code) for i in range(lax.axis_size(axi...  26.8 us
    ppermute x21, waiting for transfers between devices, swapped(): lax.ppermute(value, axis, [(i, i ^ code) for i in range(lax.axis_size(axi...  24.2 us
    ppermute x2, waiting for transfers between devices, neighbours(): return (swapped(value, 'gz', 1), lax.ppermute(value, 'gz', odd))  8.29 us
    pallas_call x6, Pallas kernels, call(): pl.pallas_call(kernel, out_shape=out_shape, scratch_shapes=list(scratch),...  5.35 us
    ppermute x2, starting transfers between devices, neighbours(): return (swapped(value, 'gz', 1), lax.ppermute(value, 'gz', odd))  5.01 us
    unnamed x12, local copies, waits for them, and re-layouts  1.72 us
  transfers between devices with their start and end apart: 23, of which 15 were waited for; matrix products, arithmetic and copies ran while one was open for 0% of the time, Pallas kernels for 3%

profile of v8, /device:TPU:17, one launch (start us, length us, event | category | flops | bytes accessed | tf_op | source)
XLA Modules:
  0.0 72.5 jit_solution(11215048973942403944)
XLA Ops:
  0.6 0.0 copy-start
  0.6 0.0 copy-start.2
  0.7 1.0 %copy-done.2 = bf16[4,4,32,32]{3,2,1,0:T(8,128)(2,1)S(1)} copy-done((bf16[4,4,32,32]{3,2,1,0:T(8,128)(2,1)S(1)}, bf16[4,4,32,32]{3,2,1,0:T(8,128)(2,1)}, u32[]{:S(2)}) %copy-start.2) | copy-done | bytes 32792
  1.6 0.0 copy-start.3
  1.6 0.1 shard_map.86
  1.7 0.1 collective-permute-start.4
  1.8 0.7 %copy-done.3 = bf16[1,8,64,128]{3,2,1,0:T(8,128)(2,1)S(1)} copy-done((bf16[1,8,64,128]{3,2,1,0:T(8,128)(2,1)S(1)}, bf16[1,8,64,128]{3,2,1,0:T(8,128)(2,1)}, u32[]{:S(2)}) %copy-start.3) | copy-done | bytes 131096
  2.5 0.1 shard_map.85
  2.6 0.7 %collective-permute-start = (bf16[32,512]{1,0:T(8,128)(2,1)S(1)}, bf16[32,512]{1,0:T(8,128)(2,1)S(1)}, u32[]{:S(2)}, u32[]{:S(2)}) collective-permute-start(bf16[32,512]{1,0:T(8,128)(2,1)S(1)} %get-tuple-element.28), channel_id=1, source_target_pairs={{0,1},{1,0},{2,3},{3,2},{4,5},{5,4},{6,7},{7,6},{8,9},{9,8},{10,11... | collective-permute-start | bytes 98312 | tf_op jit(solution)/shard_map/ppermute | solution.py:220
  3.4 1.2 %collective-permute-start.1 = (bf16[32,512]{1,0:T(8,128)(2,1)S(1)}, bf16[32,512]{1,0:T(8,128)(2,1)S(1)}, u32[]{:S(2)}, u32[]{:S(2)}) collective-permute-start(bf16[32,512]{1,0:T(8,128)(2,1)S(1)} %get-tuple-element.29), channel_id=1, source_target_pairs={{0,2},{1,3},{2,0},{3,1},{4,6},{5,7},{6,4},{7,5},{8,10},{9,11},{10,... | collective-permute-start | bytes 98312 | tf_op jit(solution)/shard_map/ppermute | solution.py:220
  4.6 0.5 collective-permute-start.2
  5.1 0.2 collective-permute-done.4
  5.3 1.4 %collective-permute-start.5 = (bf16[1,2,32,128]{3,2,1,0:T(8,128)(2,1)S(1)}, bf16[1,2,32,128]{3,2,1,0:T(8,128)(2,1)S(1)}, u32[]{:S(2)}, u32[]{:S(2)}) collective-permute-start(bf16[1,2,32,128]{3,2,1,0:T(8,128)(2,1)S(1)} %get-tuple-element.52), channel_id=1, source_target_pairs={{0,8},{4,12},{8,0},{12,4},{16,24},{20,28},{24,16},{28,20},{1,9},{5... | collective-permute-start | bytes 49160 | tf_op jit(solution)/shard_map/ppermute | solution.py:220
  6.6 0.0 copy-done
  6.6 1.3 %collective-permute-done.5 = bf16[1,2,32,128]{3,2,1,0:T(8,128)(2,1)S(1)} collective-permute-done((bf16[1,2,32,128]{3,2,1,0:T(8,128)(2,1)S(1)}, bf16[1,2,32,128]{3,2,1,0:T(8,128)(2,1)S(1)}, u32[]{:S(2)}, u32[]{:S(2)}) %collective-permute-start.5) | collective-permute-done | bytes 16416 | tf_op jit(solution)/shard_map/ppermute | solution.py:220
  7.9 1.2 %collective-permute-start.6 = (bf16[4,32,128]{2,1,0:T(8,128)(2,1)S(1)}, bf16[4,32,128]{2,1,0:T(8,128)(2,1)S(1)}, u32[]{:S(2)}, u32[]{:S(2)}) collective-permute-start(bf16[4,32,128]{2,1,0:T(8,128)(2,1)S(1)} %maximum_bitcast_fusion.refs_3_), channel_id=1, source_target_pairs={{0,4},{4,0},{8,12},{12,8},{16,20},{20,16},{24,28},{28,24},{1,5},{5... | collective-permute-start | bytes 98312 | tf_op jit(solution)/shard_map/ppermute | solution.py:220
  9.1 0.0 collective-permute-done
  9.1 0.0 collective-permute-done.1
  9.1 0.0 collective-permute-done.2
  9.2 0.0 copy-start.4
  9.2 0.0 copy-start.5
  9.2 1.5 %collective-permute-done.6.refs_4_ = bf16[4,32,128]{2,1,0:T(8,128)(2,1)S(1)} collective-permute-done((bf16[4,32,128]{2,1,0:T(8,128)(2,1)S(1)}, bf16[4,32,128]{2,1,0:T(8,128)(2,1)S(1)}, u32[]{:S(2)}, u32[]{:S(2)}) %collective-permute-start.6) | collective-permute-done | bytes 32800 | tf_op jit(solution)/shard_map/ppermute | solution.py:220
  10.7 0.0 copy-done.4
  10.7 0.0 copy-done.5
  10.7 0.6 shard_map.87
  11.3 4.1 %collective-permute-start.8 = (bf16[768,128]{1,0:T(8,128)(2,1)S(1)}, bf16[768,128]{1,0:T(8,128)(2,1)S(1)}, u32[]{:S(2)}, u32[]{:S(2)}) collective-permute-start(bf16[768,128]{1,0:T(8,128)(2,1)S(1)} %get-tuple-element.37), channel_id=1, source_target_pairs={{0,1},{1,0},{2,3},{3,2},{4,5},{5,4},{6,7},{7,6},{8,9},{9,8},{10,11... | collective-permute-start | bytes 589832 | tf_op jit(solution)/shard_map/ppermute | solution.py:220
  15.4 1.2 %collective-permute-start.9 = (bf16[768,128]{1,0:T(8,128)(2,1)S(1)}, bf16[768,128]{1,0:T(8,128)(2,1)S(1)}, u32[]{:S(2)}, u32[]{:S(2)}) collective-permute-start(bf16[768,128]{1,0:T(8,128)(2,1)S(1)} %get-tuple-element.38), channel_id=1, source_target_pairs={{0,2},{1,3},{2,0},{3,1},{4,6},{5,7},{6,4},{7,5},{8,10},{9,11},{10,... | collective-permute-start | bytes 589832 | tf_op jit(solution)/shard_map/ppermute | solution.py:220
  16.7 0.5 collective-permute-start.10
  17.1 3.1 %collective-permute-start.7 = (bf16[4,32,512]{2,1,0:T(8,128)(2,1)S(1)}, bf16[4,32,512]{2,1,0:T(8,128)(2,1)S(1)}, u32[]{:S(2)}, u32[]{:S(2)}) collective-permute-start(bf16[4,32,512]{2,1,0:T(8,128)(2,1)S(1)} %pad_maximum_fusion.1.refs_1_), channel_id=1, source_target_pairs={{4,8},{8,4},{12,16},{16,12},{20,24},{24,20},{5,9},{9,5},{13,17},{1... | collective-permute-start | bytes 393224 | tf_op jit(solution)/shard_map/ppermute | solution.py:226
  20.3 1.4 %collective-permute-start.3 = (bf16[4,32,512]{2,1,0:T(8,128)(2,1)S(1)}, bf16[4,32,512]{2,1,0:T(8,128)(2,1)S(1)}, u32[]{:S(2)}, u32[]{:S(2)}) collective-permute-start(bf16[4,32,512]{2,1,0:T(8,128)(2,1)S(1)} %pad_maximum_fusion.1.refs_1_), channel_id=1, source_target_pairs={{0,4},{4,0},{8,12},{12,8},{16,20},{20,16},{24,28},{28,24},{1,5},{5... | collective-permute-start | bytes 393224 | tf_op jit(solution)/shard_map/ppermute | solution.py:220
  21.7 3.3 %collective-permute-done.7.refs_2_ = bf16[4,32,512]{2,1,0:T(8,128)(2,1)S(1)} collective-permute-done((bf16[4,32,512]{2,1,0:T(8,128)(2,1)S(1)}, bf16[4,32,512]{2,1,0:T(8,128)(2,1)S(1)}, u32[]{:S(2)}, u32[]{:S(2)}) %collective-permute-start.7) | collective-permute-done | bytes 131104 | tf_op jit(solution)/shard_map/ppermute | solution.py:226
  24.9 3.3 %collective-permute-done.3.refs_0_ = bf16[4,32,512]{2,1,0:T(8,128)(2,1)S(1)} collective-permute-done((bf16[4,32,512]{2,1,0:T(8,128)(2,1)S(1)}, bf16[4,32,512]{2,1,0:T(8,128)(2,1)S(1)}, u32[]{:S(2)}, u32[]{:S(2)}) %collective-permute-start.3) | collective-permute-done | bytes 131104 | tf_op jit(solution)/shard_map/ppermute | solution.py:220
  28.2 0.0 collective-permute-done.8.refs_4_
  28.2 0.0 collective-permute-done.9.refs_5_
  28.2 0.0 collective-permute-done.10.refs_6_
  28.2 1.5 %shard_map.88 = (f32[432,128]{1,0:T(8,128)S(1)}, bf16[432,128]{1,0:T(8,128)(2,1)S(1)}, bf16[256,128]{1,0:T(8,128)(2,1)S(1)}, bf16[10,64,128]{2,1,0:T(8,128)(2,1)S(1)}) custom-call(bf16[4,32,512]{2,1,0:T(8,128)(2,1)S(1)} %collective-permute-done.3.refs_0_, bf16[4,32,512]{2,1,0:T(8,128)(2,1)S(1)} %pad_maximum_fusion.1.refs_1_, ...), custom_call_target="tpu_custom_call" | custom-call | tf_op jit(solution)/shard_map/pallas_call | solution.py:16
  29.7 1.3 %collective-permute-start.11 = (bf16[432,128]{1,0:T(8,128)(2,1)S(1)}, bf16[432,128]{1,0:T(8,128)(2,1)S(1)}, u32[]{:S(2)}, u32[]{:S(2)}) collective-permute-start(bf16[432,128]{1,0:T(8,128)(2,1)S(1)} %get-tuple-element.41), channel_id=1, source_target_pairs={{0,4},{4,0},{8,12},{12,8},{16,20},{20,16},{24,28},{28,24},{1,5},{5... | collective-permute-start | bytes 331784 | tf_op jit(solution)/shard_map/ppermute | solution.py:220
  31.0 2.9 %collective-permute-done.11 = bf16[432,128]{1,0:T(8,128)(2,1)S(1)} collective-permute-done((bf16[432,128]{1,0:T(8,128)(2,1)S(1)}, bf16[432,128]{1,0:T(8,128)(2,1)S(1)}, u32[]{:S(2)}, u32[]{:S(2)}) %collective-permute-start.11) | collective-permute-done | bytes 110624 | tf_op jit(solution)/shard_map/ppermute | solution.py:220
  34.0 0.3 collective-permute-start.12
  34.2 1.1 %collective-permute-start.13 = (bf16[10,64,128]{2,1,0:T(8,128)(2,1)S(1)}, bf16[10,64,128]{2,1,0:T(8,128)(2,1)S(1)}, u32[]{:S(2)}, u32[]{:S(2)}) collective-permute-start(bf16[10,64,128]{2,1,0:T(8,128)(2,1)S(1)} %get-tuple-element.43.own), channel_id=1, source_target_pairs={{0,4},{4,0},{8,12},{12,8},{16,20},{20,16},{24,28},{28,24},{1,5},{5... | collective-permute-start | bytes 491528 | tf_op jit(solution)/shard_map/ppermute | solution.py:220
  35.4 3.0 %collective-permute-done.13.even = bf16[10,64,128]{2,1,0:T(8,128)(2,1)S(1)} collective-permute-done((bf16[10,64,128]{2,1,0:T(8,128)(2,1)S(1)}, bf16[10,64,128]{2,1,0:T(8,128)(2,1)S(1)}, u32[]{:S(2)}, u32[]{:S(2)}) %collective-permute-start.13) | collective-permute-done | bytes 163872 | tf_op jit(solution)/shard_map/ppermute | solution.py:220
  38.4 2.8 %collective-permute-done.12 = bf16[688,128]{1,0:T(8,128)(2,1)S(1)} collective-permute-done((bf16[688,128]{1,0:T(8,128)(2,1)S(1)}, bf16[688,128]{1,0:T(8,128)(2,1)S(1)}, u32[]{:S(2)}, u32[]{:S(2)}) %collective-permute-start.12) | collective-permute-done | bytes 176160 | tf_op jit(solution)/shard_map/ppermute | solution.py:220
  41.2 5.2 %collective-permute-start.15 = (bf16[688,128]{1,0:T(8,128)(2,1)S(1)}, bf16[688,128]{1,0:T(8,128)(2,1)S(1)}, u32[]{:S(2)}, u32[]{:S(2)}) collective-permute-start(bf16[688,128]{1,0:T(8,128)(2,1)S(1)} %add_convert_fusion), channel_id=1, source_target_pairs={{0,8},{4,12},{8,0},{12,4},{16,24},{20,28},{24,16},{28,20},{1,9},{5... | collective-permute-start | bytes 528392 | tf_op jit(solution)/shard_map/ppermute | solution.py:220
  46.4 4.4 %collective-permute-done.15 = bf16[688,128]{1,0:T(8,128)(2,1)S(1)} collective-permute-done((bf16[688,128]{1,0:T(8,128)(2,1)S(1)}, bf16[688,128]{1,0:T(8,128)(2,1)S(1)}, u32[]{:S(2)}, u32[]{:S(2)}) %collective-permute-start.15) | collective-permute-done | bytes 176160 | tf_op jit(solution)/shard_map/ppermute | solution.py:220
  50.8 0.2 multiply_convert_fusion.refs_0_
  51.0 0.1 collective-permute-start.16
  51.1 1.3 %collective-permute-start.19 = (bf16[688,128]{1,0:T(8,128)(2,1)S(1)}, bf16[688,128]{1,0:T(8,128)(2,1)S(1)}, u32[]{:S(2)}, u32[]{:S(2)}) collective-permute-start(bf16[688,128]{1,0:T(8,128)(2,1)S(1)} %multiply_convert_fusion.refs_0_), channel_id=1, source_target_pairs={{0,2},{1,3},{2,0},{3,1},{4,6},{5,7},{6,4},{7,5},{8,10},{9,11},{10,... | collective-permute-start | bytes 528392 | tf_op jit(solution)/shard_map/ppermute | solution.py:220
  52.3 3.6 %collective-permute-done.16.refs_4_ = bf16[688,128]{1,0:T(8,128)(2,1)S(1)} collective-permute-done((bf16[688,128]{1,0:T(8,128)(2,1)S(1)}, bf16[688,128]{1,0:T(8,128)(2,1)S(1)}, u32[]{:S(2)}, u32[]{:S(2)}) %collective-permute-start.16) | collective-permute-done | bytes 176160 | tf_op jit(solution)/shard_map/ppermute | solution.py:220
  56.0 1.2 %collective-permute-start.17 = (bf16[688,128]{1,0:T(8,128)(2,1)S(1)}, bf16[688,128]{1,0:T(8,128)(2,1)S(1)}, u32[]{:S(2)}, u32[]{:S(2)}) collective-permute-start(bf16[688,128]{1,0:T(8,128)(2,1)S(1)} %collective-permute-done.16.refs_4_), channel_id=1, source_target_pairs={{0,2},{1,3},{2,0},{3,1},{4,6},{5,7},{6,4},{7,5},{8,10},{9,11},{10,... | collective-permute-start | bytes 528392 | tf_op jit(solution)/shard_map/ppermute | solution.py:220
  57.2 1.9 %collective-permute-start.14 = (bf16[10,64,128]{2,1,0:T(8,128)(2,1)S(1)}, bf16[10,64,128]{2,1,0:T(8,128)(2,1)S(1)}, u32[]{:S(2)}, u32[]{:S(2)}) collective-permute-start(bf16[10,64,128]{2,1,0:T(8,128)(2,1)S(1)} %get-tuple-element.43.own), channel_id=1, source_target_pairs={{4,8},{8,4},{12,16},{16,12},{20,24},{24,20},{5,9},{9,5},{13,17},{1... | collective-permute-start | bytes 491528 | tf_op jit(solution)/shard_map/ppermute | solution.py:226
  59.1 5.0 %collective-permute-done.14.odd = bf16[10,64,128]{2,1,0:T(8,128)(2,1)S(1)} collective-permute-done((bf16[10,64,128]{2,1,0:T(8,128)(2,1)S(1)}, bf16[10,64,128]{2,1,0:T(8,128)(2,1)S(1)}, u32[]{:S(2)}, u32[]{:S(2)}) %collective-permute-start.14) | collective-permute-done | bytes 163872 | tf_op jit(solution)/shard_map/ppermute | solution.py:226
  64.1 0.0 copy-done.1
  64.2 1.7 %shard_map.89 = bf16[8,64,128]{2,1,0:T(8,128)(2,1)} custom-call(bf16[10,64,128]{2,1,0:T(8,128)(2,1)S(1)} %collective-permute-done.13.even, bf16[10,64,128]{2,1,0:T(8,128)(2,1)S(1)} %get-tuple-element.43.own, bf16[10,64,128]{2,1,0:T(8,128)(2,1)S(1)} %collective-permute-done.14.odd, bf16[3,3,3,128,128]{4,3,2,1,0:T(8,128)(2,1)S(1)} %copy-done.1), custom_call_target="tpu_custom_call" | custom-call | tf_op jit(solution)/shard_map/pallas_call | solution.py:16
  65.9 3.4 %collective-permute-start.18 = (bf16[688,128]{1,0:T(8,128)(2,1)S(1)}, bf16[688,128]{1,0:T(8,128)(2,1)S(1)}, u32[]{:S(2)}, u32[]{:S(2)}) collective-permute-start(bf16[688,128]{1,0:T(8,128)(2,1)S(1)} %multiply_convert_fusion.refs_0_), channel_id=1, source_target_pairs={{0,1},{1,0},{2,3},{3,2},{4,5},{5,4},{6,7},{7,6},{8,9},{9,8},{10,11... | collective-permute-start | bytes 528392 | tf_op jit(solution)/shard_map/ppermute | solution.py:220
  69.3 0.0 collective-permute-done.19.refs_2_
  69.3 0.0 collective-permute-start.20
  69.3 0.0 collective-permute-done.17.refs_6_
  69.3 0.5 collective-permute-start.21
  69.8 0.1 collective-permute-start.22
  69.9 0.5 collective-permute-done.18.refs_1_
  70.3 0.4 collective-permute-done.20.refs_3_
  70.7 0.3 collective-permute-done.21.refs_5_
  70.9 0.3 collective-permute-done.22.refs_7_
  71.2 1.3 %shard_map.90 = (bf16[27,4,2,16,128]{4,3,2,1,0:T(8,128)(2,1)}, bf16[2,4,128,256]{3,2,1,0:T(8,128)(2,1)}) custom-call(bf16[688,128]{1,0:T(8,128)(2,1)S(1)} %multiply_convert_fusion.refs_0_, bf16[688,128]{1,0:T(8,128)(2,1)S(1)} %collective-permute-done.18.refs_1_, bf16[688,128]{1,0:T(8,128)(2,1)S(1)} %collective-permute-done.19.refs_2_, ...), custom_call_target="tpu_custom_call" | custom-call | tf_op jit(solution)/shard_map/pallas_call | solution.py:16
  (9 shorter events, 0.2 us)
Async XLA Ops:
  0.6 6.0 %copy-start = (bf16[2,2,2,128,256]{4,3,2,1,0:T(8,128)(2,1)S(1)}, bf16[2,2,2,128,256]{4,3,2,1,0:T(8,128)(2,1)}, u32[]{:S(2)}) copy-start(bf16[2,2,2,128,256]{4,3,2,1,0:T(8,128)(2,1)} %param.9) | copy-start | bytes 1572868
  0.6 1.0 %copy-start.2 = (bf16[4,4,32,32]{3,2,1,0:T(8,128)(2,1)S(1)}, bf16[4,4,32,32]{3,2,1,0:T(8,128)(2,1)}, u32[]{:S(2)}) copy-start(bf16[4,4,32,32]{3,2,1,0:T(8,128)(2,1)} %param.11) | copy-start | bytes 98308
  1.6 0.9 %copy-start.3 = (bf16[1,8,64,128]{3,2,1,0:T(8,128)(2,1)S(1)}, bf16[1,8,64,128]{3,2,1,0:T(8,128)(2,1)}, u32[]{:S(2)}) copy-start(bf16[1,8,64,128]{3,2,1,0:T(8,128)(2,1)} %param.6) | copy-start | bytes 393220
  1.7 3.6 %collective-permute-start.4 = (bf16[2,32,128]{2,1,0:T(8,128)(2,1)S(1)}, bf16[2,32,128]{2,1,0:T(8,128)(2,1)S(1)}, u32[]{:S(2)}, u32[]{:S(2)}) collective-permute-start(bf16[2,32,128]{2,1,0:T(8,128)(2,1)S(1)} %get-tuple-element.32), channel_id=1, source_target_pairs={{0,16},{4,20},{8,24},{12,28},{16,0},{20,4},{24,8},{28,12},{1,17},{... | collective-permute-start | bytes 49160 | tf_op jit(solution)/shard_map/ppermute | solution.py:220
  2.6 6.5 %collective-permute-start = (bf16[32,512]{1,0:T(8,128)(2,1)S(1)}, bf16[32,512]{1,0:T(8,128)(2,1)S(1)}, u32[]{:S(2)}, u32[]{:S(2)}) collective-permute-start(bf16[32,512]{1,0:T(8,128)(2,1)S(1)} %get-tuple-element.28), channel_id=1, source_target_pairs={{0,1},{1,0},{2,3},{3,2},{4,5},{5,4},{6,7},{7,6},{8,9},{9,8},{10,11... | collective-permute-start | bytes 98312 | tf_op jit(solution)/shard_map/ppermute | solution.py:220
  3.4 5.8 %collective-permute-start.1 = (bf16[32,512]{1,0:T(8,128)(2,1)S(1)}, bf16[32,512]{1,0:T(8,128)(2,1)S(1)}, u32[]{:S(2)}, u32[]{:S(2)}) collective-permute-start(bf16[32,512]{1,0:T(8,128)(2,1)S(1)} %get-tuple-element.29), channel_id=1, source_target_pairs={{0,2},{1,3},{2,0},{3,1},{4,6},{5,7},{6,4},{7,5},{8,10},{9,11},{10,... | collective-permute-start | bytes 98312 | tf_op jit(solution)/shard_map/ppermute | solution.py:220
  4.6 4.5 %collective-permute-start.2 = (bf16[32,512]{1,0:T(8,128)(2,1)S(1)}, bf16[32,512]{1,0:T(8,128)(2,1)S(1)}, u32[]{:S(2)}, u32[]{:S(2)}) collective-permute-start(bf16[32,512]{1,0:T(8,128)(2,1)S(1)} %get-tuple-element.30), channel_id=1, source_target_pairs={{0,3},{1,2},{2,1},{3,0},{4,7},{5,6},{6,5},{7,4},{8,11},{9,10},{10,... | collective-permute-start | bytes 98312 | tf_op jit(solution)/shard_map/ppermute | solution.py:220
  5.3 2.6 %collective-permute-start.5 = (bf16[1,2,32,128]{3,2,1,0:T(8,128)(2,1)S(1)}, bf16[1,2,32,128]{3,2,1,0:T(8,128)(2,1)S(1)}, u32[]{:S(2)}, u32[]{:S(2)}) collective-permute-start(bf16[1,2,32,128]{3,2,1,0:T(8,128)(2,1)S(1)} %get-tuple-element.52), channel_id=1, source_target_pairs={{0,8},{4,12},{8,0},{12,4},{16,24},{20,28},{24,16},{28,20},{1,9},{5... | collective-permute-start | bytes 49160 | tf_op jit(solution)/shard_map/ppermute | solution.py:220
  7.9 2.8 %collective-permute-start.6 = (bf16[4,32,128]{2,1,0:T(8,128)(2,1)S(1)}, bf16[4,32,128]{2,1,0:T(8,128)(2,1)S(1)}, u32[]{:S(2)}, u32[]{:S(2)}) collective-permute-start(bf16[4,32,128]{2,1,0:T(8,128)(2,1)S(1)} %maximum_bitcast_fusion.refs_3_), channel_id=1, source_target_pairs={{0,4},{4,0},{8,12},{12,8},{16,20},{20,16},{24,28},{28,24},{1,5},{5... | collective-permute-start | bytes 98312 | tf_op jit(solution)/shard_map/ppermute | solution.py:220
  9.2 1.5 %copy-start.4 = (bf16[1,8,64,128]{3,2,1,0:T(8,128)(2,1)S(1)}, bf16[1,8,64,128]{3,2,1,0:T(8,128)(2,1)}, u32[]{:S(2)}) copy-start(bf16[1,8,64,128]{3,2,1,0:T(8,128)(2,1)} %param.7) | copy-start | bytes 393220
  9.2 1.5 %copy-start.5 = (bf16[1,8,64,128]{3,2,1,0:T(8,128)(2,1)S(1)}, bf16[1,8,64,128]{3,2,1,0:T(8,128)(2,1)}, u32[]{:S(2)}) copy-start(bf16[1,8,64,128]{3,2,1,0:T(8,128)(2,1)} %param.10) | copy-start | bytes 393220
  11.3 16.9 %collective-permute-start.8 = (bf16[768,128]{1,0:T(8,128)(2,1)S(1)}, bf16[768,128]{1,0:T(8,128)(2,1)S(1)}, u32[]{:S(2)}, u32[]{:S(2)}) collective-permute-start(bf16[768,128]{1,0:T(8,128)(2,1)S(1)} %get-tuple-element.37), channel_id=1, source_target_pairs={{0,1},{1,0},{2,3},{3,2},{4,5},{5,4},{6,7},{7,6},{8,9},{9,8},{10,11... | collective-permute-start | bytes 589832 | tf_op jit(solution)/shard_map/ppermute | solution.py:220
  15.4 12.7 %collective-permute-start.9 = (bf16[768,128]{1,0:T(8,128)(2,1)S(1)}, bf16[768,128]{1,0:T(8,128)(2,1)S(1)}, u32[]{:S(2)}, u32[]{:S(2)}) collective-permute-start(bf16[768,128]{1,0:T(8,128)(2,1)S(1)} %get-tuple-element.38), channel_id=1, source_target_pairs={{0,2},{1,3},{2,0},{3,1},{4,6},{5,7},{6,4},{7,5},{8,10},{9,11},{10,... | collective-permute-start | bytes 589832 | tf_op jit(solution)/shard_map/ppermute | solution.py:220
  16.7 11.5 %collective-permute-start.10 = (bf16[768,128]{1,0:T(8,128)(2,1)S(1)}, bf16[768,128]{1,0:T(8,128)(2,1)S(1)}, u32[]{:S(2)}, u32[]{:S(2)}) collective-permute-start(bf16[768,128]{1,0:T(8,128)(2,1)S(1)} %get-tuple-element.39), channel_id=1, source_target_pairs={{0,3},{1,2},{2,1},{3,0},{4,7},{5,6},{6,5},{7,4},{8,11},{9,10},{10,... | collective-permute-start | bytes 589832 | tf_op jit(solution)/shard_map/ppermute | solution.py:220
  17.1 7.8 %collective-permute-start.7 = (bf16[4,32,512]{2,1,0:T(8,128)(2,1)S(1)}, bf16[4,32,512]{2,1,0:T(8,128)(2,1)S(1)}, u32[]{:S(2)}, u32[]{:S(2)}) collective-permute-start(bf16[4,32,512]{2,1,0:T(8,128)(2,1)S(1)} %pad_maximum_fusion.1.refs_1_), channel_id=1, source_target_pairs={{4,8},{8,4},{12,16},{16,12},{20,24},{24,20},{5,9},{9,5},{13,17},{1... | collective-permute-start | bytes 393224 | tf_op jit(solution)/shard_map/ppermute | solution.py:226
  20.3 7.9 %collective-permute-start.3 = (bf16[4,32,512]{2,1,0:T(8,128)(2,1)S(1)}, bf16[4,32,512]{2,1,0:T(8,128)(2,1)S(1)}, u32[]{:S(2)}, u32[]{:S(2)}) collective-permute-start(bf16[4,32,512]{2,1,0:T(8,128)(2,1)S(1)} %pad_maximum_fusion.1.refs_1_), channel_id=1, source_target_pairs={{0,4},{4,0},{8,12},{12,8},{16,20},{20,16},{24,28},{28,24},{1,5},{5... | collective-permute-start | bytes 393224 | tf_op jit(solution)/shard_map/ppermute | solution.py:220
  29.7 4.2 %collective-permute-start.11 = (bf16[432,128]{1,0:T(8,128)(2,1)S(1)}, bf16[432,128]{1,0:T(8,128)(2,1)S(1)}, u32[]{:S(2)}, u32[]{:S(2)}) collective-permute-start(bf16[432,128]{1,0:T(8,128)(2,1)S(1)} %get-tuple-element.41), channel_id=1, source_target_pairs={{0,4},{4,0},{8,12},{12,8},{16,20},{20,16},{24,28},{28,24},{1,5},{5... | collective-permute-start | bytes 331784 | tf_op jit(solution)/shard_map/ppermute | solution.py:220
  33.9 30.2 %copy-start.1 = (bf16[3,3,3,128,128]{4,3,2,1,0:T(8,128)(2,1)S(1)}, bf16[3,3,3,128,128]{4,3,2,1,0:T(8,128)(2,1)}, u32[]{:S(2)}) copy-start(bf16[3,3,3,128,128]{4,3,2,1,0:T(8,128)(2,1)} %weight.1) | copy-start | bytes 2654212
  34.0 7.2 %collective-permute-start.12 = (bf16[688,128]{1,0:T(8,128)(2,1)S(1)}, bf16[688,128]{1,0:T(8,128)(2,1)S(1)}, u32[]{:S(2)}, u32[]{:S(2)}) collective-permute-start(bf16[688,128]{1,0:T(8,128)(2,1)S(1)} %pad_maximum_fusion), channel_id=1, source_target_pairs={{0,16},{4,20},{8,24},{12,28},{16,0},{20,4},{24,8},{28,12},{1,17},{... | collective-permute-start | bytes 528392 | tf_op jit(solution)/shard_map/ppermute | solution.py:220
  34.2 4.2 %collective-permute-start.13 = (bf16[10,64,128]{2,1,0:T(8,128)(2,1)S(1)}, bf16[10,64,128]{2,1,0:T(8,128)(2,1)S(1)}, u32[]{:S(2)}, u32[]{:S(2)}) collective-permute-start(bf16[10,64,128]{2,1,0:T(8,128)(2,1)S(1)} %get-tuple-element.43.own), channel_id=1, source_target_pairs={{0,4},{4,0},{8,12},{12,8},{16,20},{20,16},{24,28},{28,24},{1,5},{5... | collective-permute-start | bytes 491528 | tf_op jit(solution)/shard_map/ppermute | solution.py:220
  41.2 9.6 %collective-permute-start.15 = (bf16[688,128]{1,0:T(8,128)(2,1)S(1)}, bf16[688,128]{1,0:T(8,128)(2,1)S(1)}, u32[]{:S(2)}, u32[]{:S(2)}) collective-permute-start(bf16[688,128]{1,0:T(8,128)(2,1)S(1)} %add_convert_fusion), channel_id=1, source_target_pairs={{0,8},{4,12},{8,0},{12,4},{16,24},{20,28},{24,16},{28,20},{1,9},{5... | collective-permute-start | bytes 528392 | tf_op jit(solution)/shard_map/ppermute | solution.py:220
  51.0 5.0 %collective-permute-start.16 = (bf16[688,128]{1,0:T(8,128)(2,1)S(1)}, bf16[688,128]{1,0:T(8,128)(2,1)S(1)}, u32[]{:S(2)}, u32[]{:S(2)}) collective-permute-start(bf16[688,128]{1,0:T(8,128)(2,1)S(1)} %multiply_convert_fusion.refs_0_), channel_id=1, source_target_pairs={{0,4},{4,0},{8,12},{12,8},{16,20},{20,16},{24,28},{28,24},{1,5},{5... | collective-permute-start | bytes 528392 | tf_op jit(solution)/shard_map/ppermute | solution.py:220
  51.1 18.2 %collective-permute-start.19 = (bf16[688,128]{1,0:T(8,128)(2,1)S(1)}, bf16[688,128]{1,0:T(8,128)(2,1)S(1)}, u32[]{:S(2)}, u32[]{:S(2)}) collective-permute-start(bf16[688,128]{1,0:T(8,128)(2,1)S(1)} %multiply_convert_fusion.refs_0_), channel_id=1, source_target_pairs={{0,2},{1,3},{2,0},{3,1},{4,6},{5,7},{6,4},{7,5},{8,10},{9,11},{10,... | collective-permute-start | bytes 528392 | tf_op jit(solution)/shard_map/ppermute | solution.py:220
  56.0 13.3 %collective-permute-start.17 = (bf16[688,128]{1,0:T(8,128)(2,1)S(1)}, bf16[688,128]{1,0:T(8,128)(2,1)S(1)}, u32[]{:S(2)}, u32[]{:S(2)}) collective-permute-start(bf16[688,128]{1,0:T(8,128)(2,1)S(1)} %collective-permute-done.16.refs_4_), channel_id=1, source_target_pairs={{0,2},{1,3},{2,0},{3,1},{4,6},{5,7},{6,4},{7,5},{8,10},{9,11},{10,... | collective-permute-start | bytes 528392 | tf_op jit(solution)/shard_map/ppermute | solution.py:220
  57.2 7.0 %collective-permute-start.14 = (bf16[10,64,128]{2,1,0:T(8,128)(2,1)S(1)}, bf16[10,64,128]{2,1,0:T(8,128)(2,1)S(1)}, u32[]{:S(2)}, u32[]{:S(2)}) collective-permute-start(bf16[10,64,128]{2,1,0:T(8,128)(2,1)S(1)} %get-tuple-element.43.own), channel_id=1, source_target_pairs={{4,8},{8,4},{12,16},{16,12},{20,24},{24,20},{5,9},{9,5},{13,17},{1... | collective-permute-start | bytes 491528 | tf_op jit(solution)/shard_map/ppermute | solution.py:226
  65.9 4.4 %collective-permute-start.18 = (bf16[688,128]{1,0:T(8,128)(2,1)S(1)}, bf16[688,128]{1,0:T(8,128)(2,1)S(1)}, u32[]{:S(2)}, u32[]{:S(2)}) collective-permute-start(bf16[688,128]{1,0:T(8,128)(2,1)S(1)} %multiply_convert_fusion.refs_0_), channel_id=1, source_target_pairs={{0,1},{1,0},{2,3},{3,2},{4,5},{5,4},{6,7},{7,6},{8,9},{9,8},{10,11... | collective-permute-start | bytes 528392 | tf_op jit(solution)/shard_map/ppermute | solution.py:220
  69.3 1.4 %collective-permute-start.20 = (bf16[688,128]{1,0:T(8,128)(2,1)S(1)}, bf16[688,128]{1,0:T(8,128)(2,1)S(1)}, u32[]{:S(2)}, u32[]{:S(2)}) collective-permute-start(bf16[688,128]{1,0:T(8,128)(2,1)S(1)} %collective-permute-done.19.refs_2_), channel_id=1, source_target_pairs={{0,1},{1,0},{2,3},{3,2},{4,5},{5,4},{6,7},{7,6},{8,9},{9,8},{10,11... | collective-permute-start | bytes 528392 | tf_op jit(solution)/shard_map/ppermute | solution.py:220
  69.3 1.7 %collective-permute-start.21 = (bf16[688,128]{1,0:T(8,128)(2,1)S(1)}, bf16[688,128]{1,0:T(8,128)(2,1)S(1)}, u32[]{:S(2)}, u32[]{:S(2)}) collective-permute-start(bf16[688,128]{1,0:T(8,128)(2,1)S(1)} %collective-permute-done.16.refs_4_), channel_id=1, source_target_pairs={{0,1},{1,0},{2,3},{3,2},{4,5},{5,4},{6,7},{7,6},{8,9},{9,8},{10,11... | collective-permute-start | bytes 528392 | tf_op jit(solution)/shard_map/ppermute | solution.py:220
  69.8 1.4 %collective-permute-start.22 = (bf16[688,128]{1,0:T(8,128)(2,1)S(1)}, bf16[688,128]{1,0:T(8,128)(2,1)S(1)}, u32[]{:S(2)}, u32[]{:S(2)}) collective-permute-start(bf16[688,128]{1,0:T(8,128)(2,1)S(1)} %collective-permute-done.17.refs_6_), channel_id=1, source_target_pairs={{0,1},{1,0},{2,3},{3,2},{4,5},{5,4},{6,7},{7,6},{8,9},{9,8},{10,11... | collective-permute-start | bytes 528392 | tf_op jit(solution)/shard_map/ppermute | solution.py:220

commit v9 on v8

--- a/solution.py
+++ b/solution.py
@@ -41,19 +41,21 @@
     send[...] = turned[pl.ds((1 - upper) * half, half)]
 
 
-def level_kernel(level, *rest):
+def level_kernel(even, level, odd, *rest):
     outs, level_t = rest[:-1], rest[-1]
-    turned = level[...].astype(F32).T.astype(BF16)
-    part = level_t.shape[1]
-    for owner in range(len(outs)):
-        level_t[owner] = turned[owner * part : (owner + 1) * part]
+    low, high = sides(even, odd)
+    part = level.shape[1] // len(outs)
+    for kz, plane in enumerate((low, level[...], high)):
+        turned = plane.astype(F32).T.astype(BF16)
+        for owner in range(len(outs)):
+            level_t[owner, pl.ds(kz * part, part)] = turned[owner * part : (owner + 1) * part]
     me = lax.axis_index("gy")
     for code, out in enumerate(outs):
         out[...] = level_t[jnp.bitwise_xor(me, code)]
 
 
-def mask_kernel(n_gy, pre, skip, weight, *rest):
-    deeps, outs, (deep_t, down_all) = rest[: -n_gy - 2], rest[-n_gy - 2 : -2], rest[-2:]
+def mask_kernel(pre, skip, weight, *rest):
+    deeps, (grad_out, pair_out, kept, deep_t, down_all) = rest[:-5], rest[-5:]
     if len(deeps) > 1:
         count, share = deeps[0].shape[:2]
         me = lax.axis_index("gz")
@@ -87,7 +89,7 @@
             pre_row = pre[row].astype(F32)
             total = part[y] + skip[row].astype(F32)
             grad = jnp.where(pre_row > 0, total, 0.0).astype(BF16)
-            for out in outs:
+            for out in (grad_out, pair_out):
                 out[pl.ds(row * cols, cols)] = grad
         hidden = jnp.concatenate(
             [jnp.maximum(pre[2 * y + b].astype(F32), 0.0) for y in range(half)], axis=0
@@ -96,16 +98,19 @@
             one = jnp.where(col == c, hidden, 0.0).astype(BF16)
             down = lax.dot_general(
                 one, spread, (((0,), (1,)), ((), ())), preferred_element_type=F32
-            ).astype(BF16)
+            )
             for first, owner, inner, take in segments(channels, count, channels, (b * 2 + c) * channels):
                 down_all[owner, pl.ds(inner, take)] = down[first : first + take]
     me = lax.axis_index("gy")
-    for code, out in enumerate(outs):
-        owner = jnp.bitwise_xor(me, code)
-        for side in range(down_all.shape[2] // channels):
-            out[pl.ds(rows * cols + side * count, count)] = down_all[
-                owner, :, pl.ds(side * channels, channels)
+    for side in range(down_all.shape[2] // channels):
+        for far in range(2):
+            kept[far, pl.ds(side * count, count)] = down_all[
+                jnp.bitwise_xor(me, 2 * far), :, pl.ds(side * channels, channels)
             ]
+            first = rows * cols + far * kept.shape[1] + side * count
+            pair_out[pl.ds(first, count)] = down_all[
+                jnp.bitwise_xor(me, 2 * far + 1), :, pl.ds(side * channels, channels)
+            ].astype(BF16)
 
 
 def segments(rows, piece, unit, base=0):
@@ -124,16 +129,14 @@
 
 
 def weight_kernel(n_gy, shape, *refs):
-    even, own, odd = refs[:3]
-    shared = refs[3 : 3 + n_gy]
-    keep, send, down_out, near, wide, level, halves = refs[3 + n_gy :]
+    levels, shared = refs[:n_gy], refs[n_gy : 2 * n_gy]
+    kept, other, keep, send, down_out, near, wide, level, halves = refs[2 * n_gy :]
     rows, cols, channels = shape
-    part = own.shape[1]
+    part = levels[0].shape[0] // 3
     cells = rows * cols
     half = part // 2
     rows_all = n_gy * rows
     me = lax.axis_index("gy")
-    low, high = sides(even, odd)
     for edge in (0, rows_all + 1):
         wide[edge] = jnp.zeros(wide.shape[1:], BF16)
     for code in range(n_gy):
@@ -143,8 +146,7 @@
             wide[pl.ds(1 + owner * rows, rows), :, pl.ds(kx * channels, channels)] = shifted(
                 grads, kx - 1
             ).astype(BF16)
-        for kz, plane in enumerate((low[code], own[code], high[code])):
-            level[owner, pl.ds(kz * part, part)] = plane
+        level[owner] = levels[code][...]
     near[...] = wide[pl.ds(me * rows, rows + 2), :, pl.ds(channels, channels)]
     for ky in range(3):
         total = None
@@ -161,10 +163,8 @@
     side = lax.axis_index("gz") % 2
     keep[...] = halves[side]
     send[...] = halves[1 - side].astype(send.dtype)
-    count = shared[0].shape[0] - cells
-    down = shared[0][pl.ds(cells, count)].astype(F32)
-    for code in range(1, n_gy):
-        down = down + shared[code][pl.ds(cells, count)].astype(F32)
+    count = other.shape[0]
+    down = kept[0] + shared[1][pl.ds(cells, count)].astype(F32) + other[...].astype(F32)
     down_out[...] = down.astype(down_out.dtype)
 
 
@@ -270,30 +270,40 @@
     else:
         deep_t = jnp.repeat(jnp.swapaxes(deep, 1, 2), 2, axis=0)
         deep_t = [exchanged(deep_t, "gz").reshape(deep_channels, deep_cells)]
+    even, odd = neighbours(level)
     level_t = call(
         level_kernel,
-        [shape((part, cells), BF16)] * n_gy,
+        [shape((3 * part, cells), BF16)] * n_gy,
+        even,
         level,
-        scratch=[pltpu.VMEM((n_gy, part, cells), BF16)],
+        odd,
+        scratch=[pltpu.VMEM((n_gy, 3 * part, cells), BF16)],
     )
     level_t = [swapped(value, "gy", code) if code else value for code, value in enumerate(level_t)]
-    level_t = jnp.stack(level_t)
-    even, odd = neighbours(level_t)
-    *deep_t, level_t = lax.optimization_barrier((*deep_t, level_t))
+    tied = lax.optimization_barrier((*deep_t, *level_t))
+    deep_t, level_t = tied[:-n_gy], tied[-n_gy:]
     down_slice = lax.dynamic_index_in_dim(down_weight, parity, 0, keepdims=False)
-    shared = call(
-        lambda *refs: mask_kernel(n_gy, *refs),
-        [shape((cells + down_count, channels), BF16)] * n_gy,
+    grad, pair, kept = call(
+        mask_kernel,
+        [
+            shape((cells, channels), BF16),
+            shape((cells + 2 * down_count, channels), BF16),
+            shape((2, down_count, channels), F32),
+        ],
         pre_activation[0],
         skip_cotangent[0],
         down_slice,
         *deep_t,
         scratch=[
             pltpu.VMEM((deep_channels, deep_cells), BF16),
-            pltpu.VMEM((n_gy, 4 * channels // n_gy, deep_channels), BF16),
+            pltpu.VMEM((n_gy, 4 * channels // n_gy, deep_channels), F32),
         ],
     )
-    shared = [swapped(value, "gy", code) if code else value for code, value in enumerate(shared)]
+    across = swapped(grad, "gy", 2)
+    pair = swapped(pair, "gy", 1)
+    other = (kept[1] + pair[cells + down_count :].astype(F32)).astype(BF16)
+    other = swapped(other, "gy", 2)
+    shared = [grad, pair, across, swapped(across, "gy", 1)]
     keep, send, down, near = call(
         lambda *refs: weight_kernel(n_gy, (rows, cols, channels), *refs),
         (
@@ -302,10 +312,10 @@
             shape((down_count, channels), wire),
             shape((rows + 2, cols, channels), BF16),
         ),
-        even,
-        level_t,
-        odd,
+        *level_t,
         *shared,
+        kept,
+        other,
         scratch=[
             pltpu.VMEM((n_gy * rows + 2, cols, 3 * channels), BF16),
             pltpu.VMEM((n_gy, 3 * part, cells), BF16),
@@ -320,6 +330,8 @@
         other = swapped(total, "gz", code)
         if code == 4:
             other, near_even = lax.optimization_barrier((other, near_even))
+        if code == 2:
+            other, near_odd = lax.optimization_barrier((other, near_odd))
         total = total.astype(F32) + other.astype(F32)
         if code > 2:
             total = lax.optimization_barrier(total.astype(wire))

time: 72.6 us -> 74.6 us (1.028)
  the two profiles are of different devices: /device:TPU:17 before, /device:TPU:0 now
where the time goes in v9:
time: 74.6 us; the launch traced here: 74.4 us
  waiting for transfers between devices  38.7 us (52%)
  starting transfers between devices  28.2 us (38%)
  Pallas kernels  5.38 us (7%)
  local copies, waits for them, and re-layouts  1.01 us (1%)
  between operations  0.79 us (1%)
    ppermute x22, waiting for transfers between devices, swapped(): lax.ppermute(value, axis, [(i, i ^ code) for i in range(lax.axis_size(axi...  38.7 us
    ppermute x22, starting transfers between devices, swapped(): lax.ppermute(value, axis, [(i, i ^ code) for i in range(lax.axis_size(axi...  26.9 us
    pallas_call x6, Pallas kernels, call(): pl.pallas_call(kernel, out_shape=out_shape, scratch_shapes=list(scratch),...  5.38 us
  transfers between devices with their start and end apart: 24, of which 15 were waited for; matrix products, arithmetic and copies ran while one was open for 0% of the time, Pallas kernels for 3%

profile of v9, /device:TPU:0, one launch (start us, length us, event | category | flops | bytes accessed | tf_op | source)
XLA Modules:
  0.0 74.4 jit_solution(13128501094795840328)
XLA Ops:
  0.6 0.0 copy-start
  0.6 0.0 copy-start.2
  0.7 0.0 copy-start.3
  0.7 1.0 %copy-done.3 = bf16[4,4,32,32]{3,2,1,0:T(8,128)(2,1)S(1)} copy-done((bf16[4,4,32,32]{3,2,1,0:T(8,128)(2,1)S(1)}, bf16[4,4,32,32]{3,2,1,0:T(8,128)(2,1)}, u32[]{:S(2)}) %copy-start.3) | copy-done | bytes 32792
  1.6 0.1 shard_map.85
  1.7 4.1 %collective-permute-start = (bf16[2,32,128]{2,1,0:T(8,128)(2,1)S(1)}, bf16[2,32,128]{2,1,0:T(8,128)(2,1)S(1)}, u32[]{:S(2)}, u32[]{:S(2)}) collective-permute-start(bf16[2,32,128]{2,1,0:T(8,128)(2,1)S(1)} %get-tuple-element.32), channel_id=1, source_target_pairs={{0,16},{4,20},{8,24},{12,28},{16,0},{20,4},{24,8},{28,12},{1,17},{... | collective-permute-start | bytes 49160 | tf_op jit(solution)/shard_map/ppermute | solution.py:220
  5.8 0.0 copy-done.2
  5.8 0.7 collective-permute-start.4
  6.5 4.3 %collective-permute-start.3 = (bf16[512,128]{1,0:T(8,128)(2,1)S(1)}, bf16[512,128]{1,0:T(8,128)(2,1)S(1)}, u32[]{:S(2)}, u32[]{:S(2)}) collective-permute-start(bf16[512,128]{1,0:T(8,128)(2,1)S(1)} %bitcast.18), channel_id=1, source_target_pairs={{0,4},{4,0},{8,12},{12,8},{16,20},{20,16},{24,28},{28,24},{1,5},{5... | collective-permute-start | bytes 393224 | tf_op jit(solution)/shard_map/ppermute | solution.py:220
  10.8 0.0 collective-permute-done
  10.8 0.1 collective-permute-start.1
  11.0 3.7 %collective-permute-done.1 = bf16[1,2,32,128]{3,2,1,0:T(8,128)(2,1)S(1)} collective-permute-done((bf16[1,2,32,128]{3,2,1,0:T(8,128)(2,1)S(1)}, bf16[1,2,32,128]{3,2,1,0:T(8,128)(2,1)S(1)}, u32[]{:S(2)}, u32[]{:S(2)}) %collective-permute-start.1) | collective-permute-done | bytes 16416 | tf_op jit(solution)/shard_map/ppermute | solution.py:220
  14.7 0.1 collective-permute-start.2
  14.7 0.0 collective-permute-done.4.odd
  14.7 0.9 %collective-permute-done.3.even = bf16[512,128]{1,0:T(8,128)(2,1)S(1)} collective-permute-done((bf16[512,128]{1,0:T(8,128)(2,1)S(1)}, bf16[512,128]{1,0:T(8,128)(2,1)S(1)}, u32[]{:S(2)}, u32[]{:S(2)}) %collective-permute-start.3) | collective-permute-done | bytes 131104 | tf_op jit(solution)/shard_map/ppermute | solution.py:220
  15.6 0.2 shard_map.86
  15.8 0.1 collective-permute-start.5
  15.9 1.6 %collective-permute-start.6 = (bf16[96,512]{1,0:T(8,128)(2,1)S(1)}, bf16[96,512]{1,0:T(8,128)(2,1)S(1)}, u32[]{:S(2)}, u32[]{:S(2)}) collective-permute-start(bf16[96,512]{1,0:T(8,128)(2,1)S(1)} %get-tuple-element.35), channel_id=1, source_target_pairs={{0,2},{1,3},{2,0},{3,1},{4,6},{5,7},{6,4},{7,5},{8,10},{9,11},{10,... | collective-permute-start | bytes 294920 | tf_op jit(solution)/shard_map/ppermute | solution.py:220
  17.5 0.3 collective-permute-start.7
  17.8 0.0 copy-done
  17.8 0.8 %collective-permute-done.2.rest_1_ = bf16[4,32,128]{2,1,0:T(8,128)(2,1)S(1)} collective-permute-done((bf16[4,32,128]{2,1,0:T(8,128)(2,1)S(1)}, bf16[4,32,128]{2,1,0:T(8,128)(2,1)S(1)}, u32[]{:S(2)}, u32[]{:S(2)}) %collective-permute-start.2) | collective-permute-done | bytes 32800 | tf_op jit(solution)/shard_map/ppermute | solution.py:220
  18.6 0.0 collective-permute-done.5.refs_1_
  18.6 3.0 %collective-permute-done.6.refs_2_ = bf16[96,512]{1,0:T(8,128)(2,1)S(1)} collective-permute-done((bf16[96,512]{1,0:T(8,128)(2,1)S(1)}, bf16[96,512]{1,0:T(8,128)(2,1)S(1)}, u32[]{:S(2)}, u32[]{:S(2)}) %collective-permute-start.6) | collective-permute-done | bytes 98336 | tf_op jit(solution)/shard_map/ppermute | solution.py:220
  21.6 1.2 %collective-permute-done.7.refs_3_ = bf16[96,512]{1,0:T(8,128)(2,1)S(1)} collective-permute-done((bf16[96,512]{1,0:T(8,128)(2,1)S(1)}, bf16[96,512]{1,0:T(8,128)(2,1)S(1)}, u32[]{:S(2)}, u32[]{:S(2)}) %collective-permute-start.7) | collective-permute-done | bytes 98336 | tf_op jit(solution)/shard_map/ppermute | solution.py:220
  22.8 0.0 copy-done.4
  22.8 0.0 copy-done.5
  22.8 0.6 shard_map.87
  23.4 0.3 collective-permute-start.8
  23.7 1.5 %collective-permute-start.9 = (bf16[512,128]{1,0:T(8,128)(2,1)S(1)}, bf16[512,128]{1,0:T(8,128)(2,1)S(1)}, u32[]{:S(2)}, u32[]{:S(2)}) collective-permute-start(bf16[512,128]{1,0:T(8,128)(2,1)S(1)} %get-tuple-element.43.refs_4_), channel_id=1, source_target_pairs={{0,2},{1,3},{2,0},{3,1},{4,6},{5,7},{6,4},{7,5},{8,10},{9,11},{10,... | collective-permute-start | bytes 393224 | tf_op jit(solution)/shard_map/ppermute | solution.py:220
  25.2 4.1 %collective-permute-done.9.refs_6_ = bf16[512,128]{1,0:T(8,128)(2,1)S(1)} collective-permute-done((bf16[512,128]{1,0:T(8,128)(2,1)S(1)}, bf16[512,128]{1,0:T(8,128)(2,1)S(1)}, u32[]{:S(2)}, u32[]{:S(2)}) %collective-permute-start.9) | collective-permute-done | bytes 131104 | tf_op jit(solution)/shard_map/ppermute | solution.py:220
  29.4 0.0 collective-permute-start.10
  29.4 0.0 collective-permute-done.8.refs_5_
  29.4 1.6 %collective-permute-start.11 = (bf16[256,128]{1,0:T(8,128)(2,1)S(1)}, bf16[256,128]{1,0:T(8,128)(2,1)S(1)}, u32[]{:S(2)}, u32[]{:S(2)}) collective-permute-start(bf16[256,128]{1,0:T(8,128)(2,1)S(1)} %fusion), channel_id=1, source_target_pairs={{0,2},{1,3},{2,0},{3,1},{4,6},{5,7},{6,4},{7,5},{8,10},{9,11},{10,... | collective-permute-start | bytes 196616 | tf_op jit(solution)/shard_map/ppermute | solution.py:220
  31.0 0.0 collective-permute-done.10.refs_7_
  31.0 3.0 %collective-permute-done.11.refs_9_ = bf16[256,128]{1,0:T(8,128)(2,1)S(1)} collective-permute-done((bf16[256,128]{1,0:T(8,128)(2,1)S(1)}, bf16[256,128]{1,0:T(8,128)(2,1)S(1)}, u32[]{:S(2)}, u32[]{:S(2)}) %collective-permute-start.11) | collective-permute-done | bytes 65568 | tf_op jit(solution)/shard_map/ppermute | solution.py:220
  34.0 1.4 %shard_map.88 = (f32[432,128]{1,0:T(8,128)S(1)}, bf16[432,128]{1,0:T(8,128)(2,1)S(1)}, bf16[256,128]{1,0:T(8,128)(2,1)S(1)}, bf16[10,64,128]{2,1,0:T(8,128)(2,1)S(1)}) custom-call(bf16[96,512]{1,0:T(8,128)(2,1)S(1)} %get-tuple-element.37.refs_0_, bf16[96,512]{1,0:T(8,128)(2,1)S(1)} %collective-permute-done.5.refs_1_, ...), custom_call_target="tpu_custom_call" | custom-call | tf_op jit(solution)/shard_map/pallas_call | solution.py:16
  35.4 2.6 %collective-permute-start.12 = (bf16[432,128]{1,0:T(8,128)(2,1)S(1)}, bf16[432,128]{1,0:T(8,128)(2,1)S(1)}, u32[]{:S(2)}, u32[]{:S(2)}) collective-permute-start(bf16[432,128]{1,0:T(8,128)(2,1)S(1)} %get-tuple-element.47), channel_id=1, source_target_pairs={{0,4},{4,0},{8,12},{12,8},{16,20},{20,16},{24,28},{28,24},{1,5},{5... | collective-permute-start | bytes 331784 | tf_op jit(solution)/shard_map/ppermute | solution.py:220
  38.0 2.9 %collective-permute-done.12 = bf16[432,128]{1,0:T(8,128)(2,1)S(1)} collective-permute-done((bf16[432,128]{1,0:T(8,128)(2,1)S(1)}, bf16[432,128]{1,0:T(8,128)(2,1)S(1)}, u32[]{:S(2)}, u32[]{:S(2)}) %collective-permute-start.12) | collective-permute-done | bytes 110624 | tf_op jit(solution)/shard_map/ppermute | solution.py:220
  41.0 1.9 %collective-permute-start.13 = (bf16[688,128]{1,0:T(8,128)(2,1)S(1)}, bf16[688,128]{1,0:T(8,128)(2,1)S(1)}, u32[]{:S(2)}, u32[]{:S(2)}) collective-permute-start(bf16[688,128]{1,0:T(8,128)(2,1)S(1)} %pad_maximum_fusion), channel_id=1, source_target_pairs={{0,16},{4,20},{8,24},{12,28},{16,0},{20,4},{24,8},{28,12},{1,17},{... | collective-permute-start | bytes 528392 | tf_op jit(solution)/shard_map/ppermute | solution.py:220
  42.8 0.2 collective-permute-start.14
  43.1 5.1 %collective-permute-done.14.even = bf16[10,64,128]{2,1,0:T(8,128)(2,1)S(1)} collective-permute-done((bf16[10,64,128]{2,1,0:T(8,128)(2,1)S(1)}, bf16[10,64,128]{2,1,0:T(8,128)(2,1)S(1)}, u32[]{:S(2)}, u32[]{:S(2)}) %collective-permute-start.14) | collective-permute-done | bytes 163872 | tf_op jit(solution)/shard_map/ppermute | solution.py:220
  48.2 3.1 %collective-permute-done.13 = bf16[688,128]{1,0:T(8,128)(2,1)S(1)} collective-permute-done((bf16[688,128]{1,0:T(8,128)(2,1)S(1)}, bf16[688,128]{1,0:T(8,128)(2,1)S(1)}, u32[]{:S(2)}, u32[]{:S(2)}) %collective-permute-start.13) | collective-permute-done | bytes 176160 | tf_op jit(solution)/shard_map/ppermute | solution.py:220
  51.3 0.1 collective-permute-start.15
  51.4 0.7 collective-permute-start.16
  52.1 0.0 collective-permute-done.16.odd
  52.1 5.8 %collective-permute-done.15 = bf16[688,128]{1,0:T(8,128)(2,1)S(1)} collective-permute-done((bf16[688,128]{1,0:T(8,128)(2,1)S(1)}, bf16[688,128]{1,0:T(8,128)(2,1)S(1)}, u32[]{:S(2)}, u32[]{:S(2)}) %collective-permute-start.15) | collective-permute-done | bytes 176160 | tf_op jit(solution)/shard_map/ppermute | solution.py:220
  57.8 0.2 multiply_convert_fusion.refs_0_
  58.0 4.2 %collective-permute-start.17 = (bf16[688,128]{1,0:T(8,128)(2,1)S(1)}, bf16[688,128]{1,0:T(8,128)(2,1)S(1)}, u32[]{:S(2)}, u32[]{:S(2)}) collective-permute-start(bf16[688,128]{1,0:T(8,128)(2,1)S(1)} %multiply_convert_fusion.refs_0_), channel_id=1, source_target_pairs={{0,4},{4,0},{8,12},{12,8},{16,20},{20,16},{24,28},{28,24},{1,5},{5... | collective-permute-start | bytes 528392 | tf_op jit(solution)/shard_map/ppermute | solution.py:220
  62.2 1.5 %collective-permute-start.20 = (bf16[688,128]{1,0:T(8,128)(2,1)S(1)}, bf16[688,128]{1,0:T(8,128)(2,1)S(1)}, u32[]{:S(2)}, u32[]{:S(2)}) collective-permute-start(bf16[688,128]{1,0:T(8,128)(2,1)S(1)} %multiply_convert_fusion.refs_0_), channel_id=1, source_target_pairs={{0,2},{1,3},{2,0},{3,1},{4,6},{5,7},{6,4},{7,5},{8,10},{9,11},{10,... | collective-permute-start | bytes 528392 | tf_op jit(solution)/shard_map/ppermute | solution.py:220
  63.7 2.3 %collective-permute-done.17.refs_4_ = bf16[688,128]{1,0:T(8,128)(2,1)S(1)} collective-permute-done((bf16[688,128]{1,0:T(8,128)(2,1)S(1)}, bf16[688,128]{1,0:T(8,128)(2,1)S(1)}, u32[]{:S(2)}, u32[]{:S(2)}) %collective-permute-start.17) | collective-permute-done | bytes 176160 | tf_op jit(solution)/shard_map/ppermute | solution.py:220
  66.0 1.5 %collective-permute-start.18 = (bf16[688,128]{1,0:T(8,128)(2,1)S(1)}, bf16[688,128]{1,0:T(8,128)(2,1)S(1)}, u32[]{:S(2)}, u32[]{:S(2)}) collective-permute-start(bf16[688,128]{1,0:T(8,128)(2,1)S(1)} %collective-permute-done.17.refs_4_), channel_id=1, source_target_pairs={{0,2},{1,3},{2,0},{3,1},{4,6},{5,7},{6,4},{7,5},{8,10},{9,11},{10,... | collective-permute-start | bytes 528392 | tf_op jit(solution)/shard_map/ppermute | solution.py:220
  67.5 0.0 collective-permute-start.19
  67.5 0.0 copy-done.1
  67.5 1.7 %shard_map.89 = bf16[8,64,128]{2,1,0:T(8,128)(2,1)} custom-call(bf16[10,64,128]{2,1,0:T(8,128)(2,1)S(1)} %collective-permute-done.14.even, bf16[10,64,128]{2,1,0:T(8,128)(2,1)S(1)} %get-tuple-element.49.own, bf16[10,64,128]{2,1,0:T(8,128)(2,1)S(1)} %collective-permute-done.16.odd, bf16[3,3,3,128,128]{4,3,2,1,0:T(8,128)(2,1)S(1)} %copy-done.1), custom_call_target="tpu_custom_call" | custom-call | tf_op jit(solution)/shard_map/pallas_call | solution.py:16
  69.3 0.0 collective-permute-done.20.refs_2_
  69.3 0.5 collective-permute-start.21
  69.8 1.7 %collective-permute-done.18.refs_6_ = bf16[688,128]{1,0:T(8,128)(2,1)S(1)} collective-permute-done((bf16[688,128]{1,0:T(8,128)(2,1)S(1)}, bf16[688,128]{1,0:T(8,128)(2,1)S(1)}, u32[]{:S(2)}, u32[]{:S(2)}) %collective-permute-start.18) | collective-permute-done | bytes 176160 | tf_op jit(solution)/shard_map/ppermute | solution.py:220
  71.5 0.0 collective-permute-start.22
  71.5 0.5 collective-permute-start.23
  72.0 0.0 collective-permute-done.19.refs_1_
  72.0 0.0 collective-permute-done.21.refs_3_
  72.0 0.9 %collective-permute-done.22.refs_5_ = bf16[688,128]{1,0:T(8,128)(2,1)S(1)} collective-permute-done((bf16[688,128]{1,0:T(8,128)(2,1)S(1)}, bf16[688,128]{1,0:T(8,128)(2,1)S(1)}, u32[]{:S(2)}, u32[]{:S(2)}) %collective-permute-start.22) | collective-permute-done | bytes 176160 | tf_op jit(solution)/shard_map/ppermute | solution.py:220
  72.9 0.3 collective-permute-done.23.refs_7_
  73.1 1.3 %shard_map.90 = (bf16[27,4,2,16,128]{4,3,2,1,0:T(8,128)(2,1)}, bf16[2,4,128,256]{3,2,1,0:T(8,128)(2,1)}) custom-call(bf16[688,128]{1,0:T(8,128)(2,1)S(1)} %multiply_convert_fusion.refs_0_, bf16[688,128]{1,0:T(8,128)(2,1)S(1)} %collective-permute-done.19.refs_1_, bf16[688,128]{1,0:T(8,128)(2,1)S(1)} %collective-permute-done.20.refs_2_, ...), custom_call_target="tpu_custom_call" | custom-call | tf_op jit(solution)/shard_map/pallas_call | solution.py:16
  (11 shorter events, 0.1 us)
Async XLA Ops:
  0.6 17.1 %copy-start = (bf16[2,2,2,128,256]{4,3,2,1,0:T(8,128)(2,1)S(1)}, bf16[2,2,2,128,256]{4,3,2,1,0:T(8,128)(2,1)}, u32[]{:S(2)}) copy-start(bf16[2,2,2,128,256]{4,3,2,1,0:T(8,128)(2,1)} %param.9) | copy-start | bytes 1572868
  0.6 5.2 %copy-start.2 = (bf16[1,8,64,128]{3,2,1,0:T(8,128)(2,1)S(1)}, bf16[1,8,64,128]{3,2,1,0:T(8,128)(2,1)}, u32[]{:S(2)}) copy-start(bf16[1,8,64,128]{3,2,1,0:T(8,128)(2,1)} %param.6) | copy-start | bytes 393220
  0.7 1.0 %copy-start.3 = (bf16[4,4,32,32]{3,2,1,0:T(8,128)(2,1)S(1)}, bf16[4,4,32,32]{3,2,1,0:T(8,128)(2,1)}, u32[]{:S(2)}) copy-start(bf16[4,4,32,32]{3,2,1,0:T(8,128)(2,1)} %param.11) | copy-start | bytes 98308
  1.7 9.1 %collective-permute-start = (bf16[2,32,128]{2,1,0:T(8,128)(2,1)S(1)}, bf16[2,32,128]{2,1,0:T(8,128)(2,1)S(1)}, u32[]{:S(2)}, u32[]{:S(2)}) collective-permute-start(bf16[2,32,128]{2,1,0:T(8,128)(2,1)S(1)} %get-tuple-element.32), channel_id=1, source_target_pairs={{0,16},{4,20},{8,24},{12,28},{16,0},{20,4},{24,8},{28,12},{1,17},{... | collective-permute-start | bytes 49160 | tf_op jit(solution)/shard_map/ppermute | solution.py:220
  5.8 8.9 %collective-permute-start.4 = (bf16[512,128]{1,0:T(8,128)(2,1)S(1)}, bf16[512,128]{1,0:T(8,128)(2,1)S(1)}, u32[]{:S(2)}, u32[]{:S(2)}) collective-permute-start(bf16[512,128]{1,0:T(8,128)(2,1)S(1)} %bitcast.17), channel_id=1, source_target_pairs={{4,8},{8,4},{12,16},{16,12},{20,24},{24,20},{5,9},{9,5},{13,17},{1... | collective-permute-start | bytes 393224 | tf_op jit(solution)/shard_map/ppermute | solution.py:226
  6.5 9.1 %collective-permute-start.3 = (bf16[512,128]{1,0:T(8,128)(2,1)S(1)}, bf16[512,128]{1,0:T(8,128)(2,1)S(1)}, u32[]{:S(2)}, u32[]{:S(2)}) collective-permute-start(bf16[512,128]{1,0:T(8,128)(2,1)S(1)} %bitcast.18), channel_id=1, source_target_pairs={{0,4},{4,0},{8,12},{12,8},{16,20},{20,16},{24,28},{28,24},{1,5},{5... | collective-permute-start | bytes 393224 | tf_op jit(solution)/shard_map/ppermute | solution.py:220
  10.8 3.8 %collective-permute-start.1 = (bf16[1,2,32,128]{3,2,1,0:T(8,128)(2,1)S(1)}, bf16[1,2,32,128]{3,2,1,0:T(8,128)(2,1)S(1)}, u32[]{:S(2)}, u32[]{:S(2)}) collective-permute-start(bf16[1,2,32,128]{3,2,1,0:T(8,128)(2,1)S(1)} %get-tuple-element.60), channel_id=1, source_target_pairs={{0,8},{4,12},{8,0},{12,4},{16,24},{20,28},{24,16},{28,20},{1,9},{5... | collective-permute-start | bytes 49160 | tf_op jit(solution)/shard_map/ppermute | solution.py:220
  14.7 3.9 %collective-permute-start.2 = (bf16[4,32,128]{2,1,0:T(8,128)(2,1)S(1)}, bf16[4,32,128]{2,1,0:T(8,128)(2,1)S(1)}, u32[]{:S(2)}, u32[]{:S(2)}) collective-permute-start(bf16[4,32,128]{2,1,0:T(8,128)(2,1)S(1)} %maximum_bitcast_fusion.rest_0_), channel_id=1, source_target_pairs={{0,4},{4,0},{8,12},{12,8},{16,20},{20,16},{24,28},{28,24},{1,5},{5... | collective-permute-start | bytes 98312 | tf_op jit(solution)/shard_map/ppermute | solution.py:220
  15.8 2.7 %collective-permute-start.5 = (bf16[96,512]{1,0:T(8,128)(2,1)S(1)}, bf16[96,512]{1,0:T(8,128)(2,1)S(1)}, u32[]{:S(2)}, u32[]{:S(2)}) collective-permute-start(bf16[96,512]{1,0:T(8,128)(2,1)S(1)} %get-tuple-element.34), channel_id=1, source_target_pairs={{0,1},{1,0},{2,3},{3,2},{4,5},{5,4},{6,7},{7,6},{8,9},{9,8},{10,11... | collective-permute-start | bytes 294920 | tf_op jit(solution)/shard_map/ppermute | solution.py:220
  15.9 5.7 %collective-permute-start.6 = (bf16[96,512]{1,0:T(8,128)(2,1)S(1)}, bf16[96,512]{1,0:T(8,128)(2,1)S(1)}, u32[]{:S(2)}, u32[]{:S(2)}) collective-permute-start(bf16[96,512]{1,0:T(8,128)(2,1)S(1)} %get-tuple-element.35), channel_id=1, source_target_pairs={{0,2},{1,3},{2,0},{3,1},{4,6},{5,7},{6,4},{7,5},{8,10},{9,11},{10,... | collective-permute-start | bytes 294920 | tf_op jit(solution)/shard_map/ppermute | solution.py:220
  17.5 5.3 %copy-start.4 = (bf16[1,8,64,128]{3,2,1,0:T(8,128)(2,1)S(1)}, bf16[1,8,64,128]{3,2,1,0:T(8,128)(2,1)}, u32[]{:S(2)}) copy-start(bf16[1,8,64,128]{3,2,1,0:T(8,128)(2,1)} %param.7) | copy-start | bytes 393220
  17.5 5.3 %copy-start.5 = (bf16[1,8,64,128]{3,2,1,0:T(8,128)(2,1)S(1)}, bf16[1,8,64,128]{3,2,1,0:T(8,128)(2,1)}, u32[]{:S(2)}) copy-start(bf16[1,8,64,128]{3,2,1,0:T(8,128)(2,1)} %param.10) | copy-start | bytes 393220
  17.5 5.3 %collective-permute-start.7 = (bf16[96,512]{1,0:T(8,128)(2,1)S(1)}, bf16[96,512]{1,0:T(8,128)(2,1)S(1)}, u32[]{:S(2)}, u32[]{:S(2)}) collective-permute-start(bf16[96,512]{1,0:T(8,128)(2,1)S(1)} %get-tuple-element.36), channel_id=1, source_target_pairs={{0,3},{1,2},{2,1},{3,0},{4,7},{5,6},{6,5},{7,4},{8,11},{9,10},{10,... | collective-permute-start | bytes 294920 | tf_op jit(solution)/shard_map/ppermute | solution.py:220
  23.4 6.0 %collective-permute-start.8 = (bf16[1024,128]{1,0:T(8,128)(2,1)S(1)}, bf16[1024,128]{1,0:T(8,128)(2,1)S(1)}, u32[]{:S(2)}, u32[]{:S(2)}) collective-permute-start(bf16[1024,128]{1,0:T(8,128)(2,1)S(1)} %get-tuple-element.44), channel_id=1, source_target_pairs={{0,1},{1,0},{2,3},{3,2},{4,5},{5,4},{6,7},{7,6},{8,9},{9,8},{10,11... | collective-permute-start | bytes 786440 | tf_op jit(solution)/shard_map/ppermute | solution.py:220
  23.7 5.6 %collective-permute-start.9 = (bf16[512,128]{1,0:T(8,128)(2,1)S(1)}, bf16[512,128]{1,0:T(8,128)(2,1)S(1)}, u32[]{:S(2)}, u32[]{:S(2)}) collective-permute-start(bf16[512,128]{1,0:T(8,128)(2,1)S(1)} %get-tuple-element.43.refs_4_), channel_id=1, source_target_pairs={{0,2},{1,3},{2,0},{3,1},{4,6},{5,7},{6,4},{7,5},{8,10},{9,11},{10,... | collective-permute-start | bytes 393224 | tf_op jit(solution)/shard_map/ppermute | solution.py:220
  29.4 1.6 %collective-permute-start.10 = (bf16[512,128]{1,0:T(8,128)(2,1)S(1)}, bf16[512,128]{1,0:T(8,128)(2,1)S(1)}, u32[]{:S(2)}, u32[]{:S(2)}) collective-permute-start(bf16[512,128]{1,0:T(8,128)(2,1)S(1)} %collective-permute-done.9.refs_6_), channel_id=1, source_target_pairs={{0,1},{1,0},{2,3},{3,2},{4,5},{5,4},{6,7},{7,6},{8,9},{9,8},{10,11... | collective-permute-start | bytes 393224 | tf_op jit(solution)/shard_map/ppermute | solution.py:220
  29.4 4.6 %collective-permute-start.11 = (bf16[256,128]{1,0:T(8,128)(2,1)S(1)}, bf16[256,128]{1,0:T(8,128)(2,1)S(1)}, u32[]{:S(2)}, u32[]{:S(2)}) collective-permute-start(bf16[256,128]{1,0:T(8,128)(2,1)S(1)} %fusion), channel_id=1, source_target_pairs={{0,2},{1,3},{2,0},{3,1},{4,6},{5,7},{6,4},{7,5},{8,10},{9,11},{10,... | collective-permute-start | bytes 196616 | tf_op jit(solution)/shard_map/ppermute | solution.py:220
  35.4 5.5 %collective-permute-start.12 = (bf16[432,128]{1,0:T(8,128)(2,1)S(1)}, bf16[432,128]{1,0:T(8,128)(2,1)S(1)}, u32[]{:S(2)}, u32[]{:S(2)}) collective-permute-start(bf16[432,128]{1,0:T(8,128)(2,1)S(1)} %get-tuple-element.47), channel_id=1, source_target_pairs={{0,4},{4,0},{8,12},{12,8},{16,20},{20,16},{24,28},{28,24},{1,5},{5... | collective-permute-start | bytes 331784 | tf_op jit(solution)/shard_map/ppermute | solution.py:220
  40.9 26.6 %copy-start.1 = (bf16[3,3,3,128,128]{4,3,2,1,0:T(8,128)(2,1)S(1)}, bf16[3,3,3,128,128]{4,3,2,1,0:T(8,128)(2,1)}, u32[]{:S(2)}) copy-start(bf16[3,3,3,128,128]{4,3,2,1,0:T(8,128)(2,1)} %weight.1) | copy-start | bytes 2654212
  41.0 10.3 %collective-permute-start.13 = (bf16[688,128]{1,0:T(8,128)(2,1)S(1)}, bf16[688,128]{1,0:T(8,128)(2,1)S(1)}, u32[]{:S(2)}, u32[]{:S(2)}) collective-permute-start(bf16[688,128]{1,0:T(8,128)(2,1)S(1)} %pad_maximum_fusion), channel_id=1, source_target_pairs={{0,16},{4,20},{8,24},{12,28},{16,0},{20,4},{24,8},{28,12},{1,17},{... | collective-permute-start | bytes 528392 | tf_op jit(solution)/shard_map/ppermute | solution.py:220
  42.8 5.3 %collective-permute-start.14 = (bf16[10,64,128]{2,1,0:T(8,128)(2,1)S(1)}, bf16[10,64,128]{2,1,0:T(8,128)(2,1)S(1)}, u32[]{:S(2)}, u32[]{:S(2)}) collective-permute-start(bf16[10,64,128]{2,1,0:T(8,128)(2,1)S(1)} %get-tuple-element.49.own), channel_id=1, source_target_pairs={{0,4},{4,0},{8,12},{12,8},{16,20},{20,16},{24,28},{28,24},{1,5},{5... | collective-permute-start | bytes 491528 | tf_op jit(solution)/shard_map/ppermute | solution.py:220
  51.3 6.5 %collective-permute-start.15 = (bf16[688,128]{1,0:T(8,128)(2,1)S(1)}, bf16[688,128]{1,0:T(8,128)(2,1)S(1)}, u32[]{:S(2)}, u32[]{:S(2)}) collective-permute-start(bf16[688,128]{1,0:T(8,128)(2,1)S(1)} %add_convert_fusion), channel_id=1, source_target_pairs={{0,8},{4,12},{8,0},{12,4},{16,24},{20,28},{24,16},{28,20},{1,9},{5... | collective-permute-start | bytes 528392 | tf_op jit(solution)/shard_map/ppermute | solution.py:220
  51.4 0.7 collective-permute-start.16
  58.0 8.0 %collective-permute-start.17 = (bf16[688,128]{1,0:T(8,128)(2,1)S(1)}, bf16[688,128]{1,0:T(8,128)(2,1)S(1)}, u32[]{:S(2)}, u32[]{:S(2)}) collective-permute-start(bf16[688,128]{1,0:T(8,128)(2,1)S(1)} %multiply_convert_fusion.refs_0_), channel_id=1, source_target_pairs={{0,4},{4,0},{8,12},{12,8},{16,20},{20,16},{24,28},{28,24},{1,5},{5... | collective-permute-start | bytes 528392 | tf_op jit(solution)/shard_map/ppermute | solution.py:220
  62.2 7.1 %collective-permute-start.20 = (bf16[688,128]{1,0:T(8,128)(2,1)S(1)}, bf16[688,128]{1,0:T(8,128)(2,1)S(1)}, u32[]{:S(2)}, u32[]{:S(2)}) collective-permute-start(bf16[688,128]{1,0:T(8,128)(2,1)S(1)} %multiply_convert_fusion.refs_0_), channel_id=1, source_target_pairs={{0,2},{1,3},{2,0},{3,1},{4,6},{5,7},{6,4},{7,5},{8,10},{9,11},{10,... | collective-permute-start | bytes 528392 | tf_op jit(solution)/shard_map/ppermute | solution.py:220
  66.0 5.5 %collective-permute-start.18 = (bf16[688,128]{1,0:T(8,128)(2,1)S(1)}, bf16[688,128]{1,0:T(8,128)(2,1)S(1)}, u32[]{:S(2)}, u32[]{:S(2)}) collective-permute-start(bf16[688,128]{1,0:T(8,128)(2,1)S(1)} %collective-permute-done.17.refs_4_), channel_id=1, source_target_pairs={{0,2},{1,3},{2,0},{3,1},{4,6},{5,7},{6,4},{7,5},{8,10},{9,11},{10,... | collective-permute-start | bytes 528392 | tf_op jit(solution)/shard_map/ppermute | solution.py:220
  67.5 4.5 %collective-permute-start.19 = (bf16[688,128]{1,0:T(8,128)(2,1)S(1)}, bf16[688,128]{1,0:T(8,128)(2,1)S(1)}, u32[]{:S(2)}, u32[]{:S(2)}) collective-permute-start(bf16[688,128]{1,0:T(8,128)(2,1)S(1)} %multiply_convert_fusion.refs_0_), channel_id=1, source_target_pairs={{0,1},{1,0},{2,3},{3,2},{4,5},{5,4},{6,7},{7,6},{8,9},{9,8},{10,11... | collective-permute-start | bytes 528392 | tf_op jit(solution)/shard_map/ppermute | solution.py:220
  69.3 2.7 %collective-permute-start.21 = (bf16[688,128]{1,0:T(8,128)(2,1)S(1)}, bf16[688,128]{1,0:T(8,128)(2,1)S(1)}, u32[]{:S(2)}, u32[]{:S(2)}) collective-permute-start(bf16[688,128]{1,0:T(8,128)(2,1)S(1)} %collective-permute-done.20.refs_2_), channel_id=1, source_target_pairs={{0,1},{1,0},{2,3},{3,2},{4,5},{5,4},{6,7},{7,6},{8,9},{9,8},{10,11... | collective-permute-start | bytes 528392 | tf_op jit(solution)/shard_map/ppermute | solution.py:220
  71.5 1.4 %collective-permute-start.22 = (bf16[688,128]{1,0:T(8,128)(2,1)S(1)}, bf16[688,128]{1,0:T(8,128)(2,1)S(1)}, u32[]{:S(2)}, u32[]{:S(2)}) collective-permute-start(bf16[688,128]{1,0:T(8,128)(2,1)S(1)} %collective-permute-done.17.refs_4_), channel_id=1, source_target_pairs={{0,1},{1,0},{2,3},{3,2},{4,5},{5,4},{6,7},{7,6},{8,9},{9,8},{10,11... | collective-permute-start | bytes 528392 | tf_op jit(solution)/shard_map/ppermute | solution.py:220
  71.5 1.7 %collective-permute-start.23 = (bf16[688,128]{1,0:T(8,128)(2,1)S(1)}, bf16[688,128]{1,0:T(8,128)(2,1)S(1)}, u32[]{:S(2)}, u32[]{:S(2)}) collective-permute-start(bf16[688,128]{1,0:T(8,128)(2,1)S(1)} %collective-permute-done.18.refs_6_), channel_id=1, source_target_pairs={{0,1},{1,0},{2,3},{3,2},{4,5},{5,4},{6,7},{7,6},{8,9},{9,8},{10,11... | collective-permute-start | bytes 528392 | tf_op jit(solution)/shard_map/ppermute | solution.py:220

commit v10 on v8

--- a/solution.py
+++ b/solution.py
@@ -53,7 +53,8 @@
 
 
 def mask_kernel(n_gy, pre, skip, weight, *rest):
-    deeps, outs, (deep_t, down_all) = rest[: -n_gy - 2], rest[-n_gy - 2 : -2], rest[-2:]
+    deeps, rest = rest[: -n_gy - 3], rest[-n_gy - 3 :]
+    grad_out, kept, *outs, deep_t, down_all = rest
     if len(deeps) > 1:
         count, share = deeps[0].shape[:2]
         me = lax.axis_index("gz")
@@ -87,8 +88,7 @@
             pre_row = pre[row].astype(F32)
             total = part[y] + skip[row].astype(F32)
             grad = jnp.where(pre_row > 0, total, 0.0).astype(BF16)
-            for out in outs:
-                out[pl.ds(row * cols, cols)] = grad
+            grad_out[pl.ds(row * cols, cols)] = grad
         hidden = jnp.concatenate(
             [jnp.maximum(pre[2 * y + b].astype(F32), 0.0) for y in range(half)], axis=0
         )
@@ -96,16 +96,16 @@
             one = jnp.where(col == c, hidden, 0.0).astype(BF16)
             down = lax.dot_general(
                 one, spread, (((0,), (1,)), ((), ())), preferred_element_type=F32
-            ).astype(BF16)
+            )
             for first, owner, inner, take in segments(channels, count, channels, (b * 2 + c) * channels):
                 down_all[owner, pl.ds(inner, take)] = down[first : first + take]
     me = lax.axis_index("gy")
-    for code, out in enumerate(outs):
+    for code, out in enumerate([kept, *outs]):
         owner = jnp.bitwise_xor(me, code)
         for side in range(down_all.shape[2] // channels):
-            out[pl.ds(rows * cols + side * count, count)] = down_all[
+            out[pl.ds(side * count, count)] = down_all[
                 owner, :, pl.ds(side * channels, channels)
-            ]
+            ].astype(out.dtype)
 
 
 def segments(rows, piece, unit, base=0):
@@ -126,7 +126,7 @@
 def weight_kernel(n_gy, shape, *refs):
     even, own, odd = refs[:3]
     shared = refs[3 : 3 + n_gy]
-    keep, send, down_out, near, wide, level, halves = refs[3 + n_gy :]
+    keep, send, near, wide, level, halves = refs[3 + n_gy :]
     rows, cols, channels = shape
     part = own.shape[1]
     cells = rows * cols
@@ -161,11 +161,6 @@
     side = lax.axis_index("gz") % 2
     keep[...] = halves[side]
     send[...] = halves[1 - side].astype(send.dtype)
-    count = shared[0].shape[0] - cells
-    down = shared[0][pl.ds(cells, count)].astype(F32)
-    for code in range(1, n_gy):
-        down = down + shared[code][pl.ds(cells, count)].astype(F32)
-    down_out[...] = down.astype(down_out.dtype)
 
 
 def input_kernel(even, own, odd, weight, out):
@@ -279,27 +274,29 @@
     level_t = [swapped(value, "gy", code) if code else value for code, value in enumerate(level_t)]
     level_t = jnp.stack(level_t)
     even, odd = neighbours(level_t)
-    *deep_t, level_t = lax.optimization_barrier((*deep_t, level_t))
+    *deep_t, even, odd = lax.optimization_barrier((*deep_t, even, odd))
     down_slice = lax.dynamic_index_in_dim(down_weight, parity, 0, keepdims=False)
-    shared = call(
+    grad, down, *others = call(
         lambda *refs: mask_kernel(n_gy, *refs),
-        [shape((cells + down_count, channels), BF16)] * n_gy,
+        [shape((cells, channels), BF16), shape((down_count, channels), F32)]
+        + [shape((down_count, channels), BF16)] * (n_gy - 1),
         pre_activation[0],
         skip_cotangent[0],
         down_slice,
         *deep_t,
         scratch=[
             pltpu.VMEM((deep_channels, deep_cells), BF16),
-            pltpu.VMEM((n_gy, 4 * channels // n_gy, deep_channels), BF16),
+            pltpu.VMEM((n_gy, 4 * channels // n_gy, deep_channels), F32),
         ],
     )
-    shared = [swapped(value, "gy", code) if code else value for code, value in enumerate(shared)]
-    keep, send, down, near = call(
+    shared = [swapped(grad, "gy", code) if code else grad for code in range(n_gy)]
+    for code, value in enumerate(others):
+        down = down + swapped(value, "gy", code + 1).astype(F32)
+    keep, send, near = call(
         lambda *refs: weight_kernel(n_gy, (rows, cols, channels), *refs),
         (
             shape((27 * half, channels), F32),
             shape((27 * half, channels), wire),
-            shape((down_count, channels), wire),
             shape((rows + 2, cols, channels), BF16),
         ),
         even,
@@ -314,7 +311,8 @@
     )
     near_even, near_odd = neighbours(near)
     conv = (keep + swapped(send, "gz", 1).astype(F32)).astype(wire)
-    total = lax.optimization_barrier(jnp.concatenate([conv, down], axis=0))
+    total = jnp.concatenate([conv, down.astype(wire)], axis=0)
+    total = lax.optimization_barrier(total)
     code = n_gz // 2
     while code > 1:
         other = swapped(total, "gz", code)
@@ -331,6 +329,7 @@
     )
     total = (total * scale).astype(BF16)
     pair = [total, swapped(total, "gz", 1)]
+    pair[1], near_odd = lax.optimization_barrier((pair[1], near_odd))
     input_grad = call(
         input_kernel,
         shape((rows, cols, channels), BF16),

time: 72.6 us -> 70.8 us (0.975)
  the two profiles are of different devices: /device:TPU:17 before, /device:TPU:5 now
where the time goes in v10:
time: 70.8 us; the launch traced here: 70.6 us
  waiting for transfers between devices  35 us (49%)
  starting transfers between devices  28.1 us (40%)
  Pallas kernels  5.35 us (8%)
  local copies, waits for them, and re-layouts  1 us (1%)
  between operations  0.83 us (1%)
    ppermute x24, waiting for transfers between devices, swapped(): lax.ppermute(value, axis, [(i, i ^ code) for i in range(lax.axis_size(axi...  30.4 us
    ppermute x24, starting transfers between devices, swapped(): lax.ppermute(value, axis, [(i, i ^ code) for i in range(lax.axis_size(axi...  23 us
    pallas_call x6, Pallas kernels, call(): pl.pallas_call(kernel, out_shape=out_shape, scratch_shapes=list(scratch),...  5.35 us
    ppermute x2, starting transfers between devices, neighbours(): return (swapped(value, 'gz', 1), lax.ppermute(value, 'gz', odd))  5.07 us
    ppermute x2, waiting for transfers between devices, neighbours(): return (swapped(value, 'gz', 1), lax.ppermute(value, 'gz', odd))  4.55 us
  transfers between devices with their start and end apart: 26, of which 12 were waited for; matrix products, arithmetic and copies ran while one was open for 0% of the time, Pallas kernels for 5%

profile of v10, /device:TPU:5, one launch (start us, length us, event | category | flops | bytes accessed | tf_op | source)
XLA Modules:
  0.0 70.6 jit_solution(6674589782909929254)
XLA Ops:
  0.6 0.0 copy-start
  0.6 0.0 copy-start.2
  0.7 1.0 %copy-done.2 = bf16[4,4,32,32]{3,2,1,0:T(8,128)(2,1)S(1)} copy-done((bf16[4,4,32,32]{3,2,1,0:T(8,128)(2,1)S(1)}, bf16[4,4,32,32]{3,2,1,0:T(8,128)(2,1)}, u32[]{:S(2)}) %copy-start.2) | copy-done | bytes 32792
  1.6 0.1 shard_map.85
  1.7 2.4 %collective-permute-start = (bf16[2,32,128]{2,1,0:T(8,128)(2,1)S(1)}, bf16[2,32,128]{2,1,0:T(8,128)(2,1)S(1)}, u32[]{:S(2)}, u32[]{:S(2)}) collective-permute-start(bf16[2,32,128]{2,1,0:T(8,128)(2,1)S(1)} %get-tuple-element.31), channel_id=1, source_target_pairs={{0,16},{4,20},{8,24},{12,28},{16,0},{20,4},{24,8},{28,12},{1,17},{... | collective-permute-start | bytes 49160 | tf_op jit(solution)/shard_map/ppermute | solution.py:215
  4.1 0.1 shard_map.86
  4.2 1.0 %collective-permute-start.3 = (bf16[32,512]{1,0:T(8,128)(2,1)S(1)}, bf16[32,512]{1,0:T(8,128)(2,1)S(1)}, u32[]{:S(2)}, u32[]{:S(2)}) collective-permute-start(bf16[32,512]{1,0:T(8,128)(2,1)S(1)} %get-tuple-element.33), channel_id=1, source_target_pairs={{0,1},{1,0},{2,3},{3,2},{4,5},{5,4},{6,7},{7,6},{8,9},{9,8},{10,11... | collective-permute-start | bytes 98312 | tf_op jit(solution)/shard_map/ppermute | solution.py:215
  5.2 1.2 %collective-permute-start.4 = (bf16[32,512]{1,0:T(8,128)(2,1)S(1)}, bf16[32,512]{1,0:T(8,128)(2,1)S(1)}, u32[]{:S(2)}, u32[]{:S(2)}) collective-permute-start(bf16[32,512]{1,0:T(8,128)(2,1)S(1)} %get-tuple-element.34), channel_id=1, source_target_pairs={{0,2},{1,3},{2,0},{3,1},{4,6},{5,7},{6,4},{7,5},{8,10},{9,11},{10,... | collective-permute-start | bytes 98312 | tf_op jit(solution)/shard_map/ppermute | solution.py:215
  6.4 0.5 collective-permute-start.5
  6.9 0.0 collective-permute-done
  6.9 1.4 %collective-permute-start.1 = (bf16[1,2,32,128]{3,2,1,0:T(8,128)(2,1)S(1)}, bf16[1,2,32,128]{3,2,1,0:T(8,128)(2,1)S(1)}, u32[]{:S(2)}, u32[]{:S(2)}) collective-permute-start(bf16[1,2,32,128]{3,2,1,0:T(8,128)(2,1)S(1)} %get-tuple-element.58), channel_id=1, source_target_pairs={{0,8},{4,12},{8,0},{12,4},{16,24},{20,28},{24,16},{28,20},{1,9},{5... | collective-permute-start | bytes 49160 | tf_op jit(solution)/shard_map/ppermute | solution.py:215
  8.3 0.0 collective-permute-done.3
  8.3 0.0 collective-permute-done.4
  8.3 1.5 %collective-permute-done.5 = bf16[32,512]{1,0:T(8,128)(2,1)S(1)} collective-permute-done((bf16[32,512]{1,0:T(8,128)(2,1)S(1)}, bf16[32,512]{1,0:T(8,128)(2,1)S(1)}, u32[]{:S(2)}, u32[]{:S(2)}) %collective-permute-start.5) | collective-permute-done | bytes 32800 | tf_op jit(solution)/shard_map/ppermute | solution.py:215
  9.8 3.1 %collective-permute-start.7 = (bf16[4,32,512]{2,1,0:T(8,128)(2,1)S(1)}, bf16[4,32,512]{2,1,0:T(8,128)(2,1)S(1)}, u32[]{:S(2)}, u32[]{:S(2)}) collective-permute-start(bf16[4,32,512]{2,1,0:T(8,128)(2,1)S(1)} %pad_maximum_fusion.1.refs_1_), channel_id=1, source_target_pairs={{4,8},{8,4},{12,16},{16,12},{20,24},{24,20},{5,9},{9,5},{13,17},{1... | collective-permute-start | bytes 393224 | tf_op jit(solution)/shard_map/ppermute | solution.py:221
  13.0 0.1 collective-permute-start.6
  13.0 0.0 collective-permute-done.1
  13.1 0.0 copy-start.4
  13.1 0.0 copy-start.5
  13.1 1.5 %collective-permute-start.2 = (bf16[4,32,128]{2,1,0:T(8,128)(2,1)S(1)}, bf16[4,32,128]{2,1,0:T(8,128)(2,1)S(1)}, u32[]{:S(2)}, u32[]{:S(2)}) collective-permute-start(bf16[4,32,128]{2,1,0:T(8,128)(2,1)S(1)} %maximum_bitcast_fusion.refs_3_), channel_id=1, source_target_pairs={{0,4},{4,0},{8,12},{12,8},{16,20},{20,16},{24,28},{28,24},{1,5},{5... | collective-permute-start | bytes 98312 | tf_op jit(solution)/shard_map/ppermute | solution.py:215
  14.6 6.9 %collective-permute-done.2.refs_4_ = bf16[4,32,128]{2,1,0:T(8,128)(2,1)S(1)} collective-permute-done((bf16[4,32,128]{2,1,0:T(8,128)(2,1)S(1)}, bf16[4,32,128]{2,1,0:T(8,128)(2,1)S(1)}, u32[]{:S(2)}, u32[]{:S(2)}) %collective-permute-start.2) | collective-permute-done | bytes 32800 | tf_op jit(solution)/shard_map/ppermute | solution.py:215
  21.5 0.0 collective-permute-done.7.refs_2_
  21.5 0.0 collective-permute-done.6.refs_0_
  21.6 0.6 shard_map.87
  22.2 1.1 %collective-permute-start.10 = (bf16[512,128]{1,0:T(8,128)(2,1)S(1)}, bf16[512,128]{1,0:T(8,128)(2,1)S(1)}, u32[]{:S(2)}, u32[]{:S(2)}) collective-permute-start(bf16[512,128]{1,0:T(8,128)(2,1)S(1)} %get-tuple-element.40.refs_3_), channel_id=1, source_target_pairs={{0,3},{1,2},{2,1},{3,0},{4,7},{5,6},{6,5},{7,4},{8,11},{9,10},{10,... | collective-permute-start | bytes 393224 | tf_op jit(solution)/shard_map/ppermute | solution.py:215
  23.2 0.8 %collective-permute-start.9 = (bf16[512,128]{1,0:T(8,128)(2,1)S(1)}, bf16[512,128]{1,0:T(8,128)(2,1)S(1)}, u32[]{:S(2)}, u32[]{:S(2)}) collective-permute-start(bf16[512,128]{1,0:T(8,128)(2,1)S(1)} %get-tuple-element.40.refs_3_), channel_id=1, source_target_pairs={{0,2},{1,3},{2,0},{3,1},{4,6},{5,7},{6,4},{7,5},{8,10},{9,11},{10,... | collective-permute-start | bytes 393224 | tf_op jit(solution)/shard_map/ppermute | solution.py:215
  24.1 0.3 collective-permute-start.8
  24.4 0.2 collective-permute-start.12
  24.6 0.6 collective-permute-start.13
  25.2 2.8 %collective-permute-done.10.refs_6_ = bf16[512,128]{1,0:T(8,128)(2,1)S(1)} collective-permute-done((bf16[512,128]{1,0:T(8,128)(2,1)S(1)}, bf16[512,128]{1,0:T(8,128)(2,1)S(1)}, u32[]{:S(2)}, u32[]{:S(2)}) %collective-permute-start.10) | collective-permute-done | bytes 131104 | tf_op jit(solution)/shard_map/ppermute | solution.py:215
  28.0 0.8 %collective-permute-start.14 = (bf16[256,128]{1,0:T(8,128)(2,1)S(1)}, bf16[256,128]{1,0:T(8,128)(2,1)S(1)}, u32[]{:S(2)}, u32[]{:S(2)}) collective-permute-start(bf16[256,128]{1,0:T(8,128)(2,1)S(1)} %get-tuple-element.46), channel_id=1, source_target_pairs={{0,3},{1,2},{2,1},{3,0},{4,7},{5,6},{6,5},{7,4},{8,11},{9,10},{10,... | collective-permute-start | bytes 196616 | tf_op jit(solution)/shard_map/ppermute | solution.py:215
  28.8 1.9 %collective-permute-done.9.refs_5_ = bf16[512,128]{1,0:T(8,128)(2,1)S(1)} collective-permute-done((bf16[512,128]{1,0:T(8,128)(2,1)S(1)}, bf16[512,128]{1,0:T(8,128)(2,1)S(1)}, u32[]{:S(2)}, u32[]{:S(2)}) %collective-permute-start.9) | collective-permute-done | bytes 131104 | tf_op jit(solution)/shard_map/ppermute | solution.py:215
  30.7 0.0 collective-permute-done.8.refs_4_
  30.8 1.5 %shard_map.88 = (f32[432,128]{1,0:T(8,128)S(1)}, bf16[432,128]{1,0:T(8,128)(2,1)S(1)}, bf16[10,64,128]{2,1,0:T(8,128)(2,1)S(1)}) custom-call(bf16[4,32,512]{2,1,0:T(8,128)(2,1)S(1)} %collective-permute-done.6.refs_0_, bf16[4,32,512]{2,1,0:T(8,128)(2,1)S(1)} %pad_maximum_fusion.1.refs_1_, bf16[4,32,512]{2,1,0:T(8,128)(2,1)S(1)} %collective-permute-done.7.refs_2_, ...), custom_call_target="tpu_custom_call" | custom-call | tf_op jit(solution)/shard_map/pallas_call | solution.py:16
  32.3 0.1 collective-permute-start.11
  32.4 0.0 collective-permute-done.12
  32.4 0.0 collective-permute-done.13
  32.4 1.2 %collective-permute-done.14 = bf16[256,128]{1,0:T(8,128)(2,1)S(1)} collective-permute-done((bf16[256,128]{1,0:T(8,128)(2,1)S(1)}, bf16[256,128]{1,0:T(8,128)(2,1)S(1)}, u32[]{:S(2)}, u32[]{:S(2)}) %collective-permute-start.14) | collective-permute-done | bytes 65568 | tf_op jit(solution)/shard_map/ppermute | solution.py:215
  33.6 2.3 %collective-permute-done.11 = bf16[432,128]{1,0:T(8,128)(2,1)S(1)} collective-permute-done((bf16[432,128]{1,0:T(8,128)(2,1)S(1)}, bf16[432,128]{1,0:T(8,128)(2,1)S(1)}, u32[]{:S(2)}, u32[]{:S(2)}) %collective-permute-start.11) | collective-permute-done | bytes 110624 | tf_op jit(solution)/shard_map/ppermute | solution.py:215
  36.0 0.5 collective-permute-start.15
  36.5 0.9 %collective-permute-start.16 = (bf16[10,64,128]{2,1,0:T(8,128)(2,1)S(1)}, bf16[10,64,128]{2,1,0:T(8,128)(2,1)S(1)}, u32[]{:S(2)}, u32[]{:S(2)}) collective-permute-start(bf16[10,64,128]{2,1,0:T(8,128)(2,1)S(1)} %get-tuple-element.47.own), channel_id=1, source_target_pairs={{0,4},{4,0},{8,12},{12,8},{16,20},{20,16},{24,28},{28,24},{1,5},{5... | collective-permute-start | bytes 491528 | tf_op jit(solution)/shard_map/ppermute | solution.py:215
  37.4 3.3 %collective-permute-done.16.even = bf16[10,64,128]{2,1,0:T(8,128)(2,1)S(1)} collective-permute-done((bf16[10,64,128]{2,1,0:T(8,128)(2,1)S(1)}, bf16[10,64,128]{2,1,0:T(8,128)(2,1)S(1)}, u32[]{:S(2)}, u32[]{:S(2)}) %collective-permute-start.16) | collective-permute-done | bytes 163872 | tf_op jit(solution)/shard_map/ppermute | solution.py:215
  40.7 4.9 %collective-permute-done.15 = bf16[688,128]{1,0:T(8,128)(2,1)S(1)} collective-permute-done((bf16[688,128]{1,0:T(8,128)(2,1)S(1)}, bf16[688,128]{1,0:T(8,128)(2,1)S(1)}, u32[]{:S(2)}, u32[]{:S(2)}) %collective-permute-start.15) | collective-permute-done | bytes 176160 | tf_op jit(solution)/shard_map/ppermute | solution.py:215
  45.6 0.2 collective-permute-start.17
  45.8 4.2 %collective-permute-done.17 = bf16[688,128]{1,0:T(8,128)(2,1)S(1)} collective-permute-done((bf16[688,128]{1,0:T(8,128)(2,1)S(1)}, bf16[688,128]{1,0:T(8,128)(2,1)S(1)}, u32[]{:S(2)}, u32[]{:S(2)}) %collective-permute-start.17) | collective-permute-done | bytes 176160 | tf_op jit(solution)/shard_map/ppermute | solution.py:215
  50.0 0.2 multiply_convert_fusion.refs_0_
  50.1 1.7 %collective-permute-start.18 = (bf16[688,128]{1,0:T(8,128)(2,1)S(1)}, bf16[688,128]{1,0:T(8,128)(2,1)S(1)}, u32[]{:S(2)}, u32[]{:S(2)}) collective-permute-start(bf16[688,128]{1,0:T(8,128)(2,1)S(1)} %multiply_convert_fusion.refs_0_), channel_id=1, source_target_pairs={{0,4},{4,0},{8,12},{12,8},{16,20},{20,16},{24,28},{28,24},{1,5},{5... | collective-permute-start | bytes 528392 | tf_op jit(solution)/shard_map/ppermute | solution.py:215
  51.9 1.9 %collective-permute-start.19 = (bf16[10,64,128]{2,1,0:T(8,128)(2,1)S(1)}, bf16[10,64,128]{2,1,0:T(8,128)(2,1)S(1)}, u32[]{:S(2)}, u32[]{:S(2)}) collective-permute-start(bf16[10,64,128]{2,1,0:T(8,128)(2,1)S(1)} %get-tuple-element.47.own), channel_id=1, source_target_pairs={{4,8},{8,4},{12,16},{16,12},{20,24},{24,20},{5,9},{9,5},{13,17},{1... | collective-permute-start | bytes 491528 | tf_op jit(solution)/shard_map/ppermute | solution.py:221
  53.8 0.6 collective-permute-start.22
  54.4 4.6 %collective-permute-done.19.odd = bf16[10,64,128]{2,1,0:T(8,128)(2,1)S(1)} collective-permute-done((bf16[10,64,128]{2,1,0:T(8,128)(2,1)S(1)}, bf16[10,64,128]{2,1,0:T(8,128)(2,1)S(1)}, u32[]{:S(2)}, u32[]{:S(2)}) %collective-permute-start.19) | collective-permute-done | bytes 163872 | tf_op jit(solution)/shard_map/ppermute | solution.py:221
  58.9 0.0 collective-permute-done.18.refs_4_
  58.9 0.5 collective-permute-start.20
  59.4 3.8 %collective-permute-start.21 = (bf16[688,128]{1,0:T(8,128)(2,1)S(1)}, bf16[688,128]{1,0:T(8,128)(2,1)S(1)}, u32[]{:S(2)}, u32[]{:S(2)}) collective-permute-start(bf16[688,128]{1,0:T(8,128)(2,1)S(1)} %multiply_convert_fusion.refs_0_), channel_id=1, source_target_pairs={{0,1},{1,0},{2,3},{3,2},{4,5},{5,4},{6,7},{7,6},{8,9},{9,8},{10,11... | collective-permute-start | bytes 528392 | tf_op jit(solution)/shard_map/ppermute | solution.py:215
  63.3 1.7 %shard_map.89 = bf16[8,64,128]{2,1,0:T(8,128)(2,1)} custom-call(bf16[10,64,128]{2,1,0:T(8,128)(2,1)S(1)} %collective-permute-done.16.even, bf16[10,64,128]{2,1,0:T(8,128)(2,1)S(1)} %get-tuple-element.47.own, bf16[10,64,128]{2,1,0:T(8,128)(2,1)S(1)} %collective-permute-done.19.odd, bf16[3,3,3,128,128]{4,3,2,1,0:T(8,128)(2,1)S(1)} %copy-done.1), custom_call_target="tpu_custom_call" | custom-call | tf_op jit(solution)/shard_map/pallas_call | solution.py:16
  65.0 0.0 collective-permute-done.22.refs_2_
  65.0 0.0 collective-permute-start.23
  65.0 0.0 collective-permute-done.20.refs_6_
  65.1 2.9 %collective-permute-start.24 = (bf16[688,128]{1,0:T(8,128)(2,1)S(1)}, bf16[688,128]{1,0:T(8,128)(2,1)S(1)}, u32[]{:S(2)}, u32[]{:S(2)}) collective-permute-start(bf16[688,128]{1,0:T(8,128)(2,1)S(1)} %collective-permute-done.18.refs_4_), channel_id=1, source_target_pairs={{0,1},{1,0},{2,3},{3,2},{4,5},{5,4},{6,7},{7,6},{8,9},{9,8},{10,11... | collective-permute-start | bytes 528392 | tf_op jit(solution)/shard_map/ppermute | solution.py:215
  67.9 0.0 collective-permute-start.25
  67.9 0.0 collective-permute-done.21.refs_1_
  67.9 0.0 collective-permute-done.23.refs_3_
  67.9 1.0 %collective-permute-done.24.refs_5_ = bf16[688,128]{1,0:T(8,128)(2,1)S(1)} collective-permute-done((bf16[688,128]{1,0:T(8,128)(2,1)S(1)}, bf16[688,128]{1,0:T(8,128)(2,1)S(1)}, u32[]{:S(2)}, u32[]{:S(2)}) %collective-permute-start.24) | collective-permute-done | bytes 176160 | tf_op jit(solution)/shard_map/ppermute | solution.py:215
  69.0 0.4 collective-permute-done.25.refs_7_
  69.3 1.3 %shard_map.90 = (bf16[27,4,2,16,128]{4,3,2,1,0:T(8,128)(2,1)}, bf16[2,4,128,256]{3,2,1,0:T(8,128)(2,1)}) custom-call(bf16[688,128]{1,0:T(8,128)(2,1)S(1)} %multiply_convert_fusion.refs_0_, bf16[688,128]{1,0:T(8,128)(2,1)S(1)} %collective-permute-done.21.refs_1_, bf16[688,128]{1,0:T(8,128)(2,1)S(1)} %collective-permute-done.22.refs_2_, ...), custom_call_target="tpu_custom_call" | custom-call | tf_op jit(solution)/shard_map/pallas_call | solution.py:16
  (16 shorter events, 0.2 us)
Async XLA Ops:
  0.6 14.0 %copy-start = (bf16[2,2,2,128,256]{4,3,2,1,0:T(8,128)(2,1)S(1)}, bf16[2,2,2,128,256]{4,3,2,1,0:T(8,128)(2,1)}, u32[]{:S(2)}) copy-start(bf16[2,2,2,128,256]{4,3,2,1,0:T(8,128)(2,1)} %param.9) | copy-start | bytes 1572868
  0.6 1.0 %copy-start.2 = (bf16[4,4,32,32]{3,2,1,0:T(8,128)(2,1)S(1)}, bf16[4,4,32,32]{3,2,1,0:T(8,128)(2,1)}, u32[]{:S(2)}) copy-start(bf16[4,4,32,32]{3,2,1,0:T(8,128)(2,1)} %param.11) | copy-start | bytes 98308
  1.6 2.5 %copy-start.3 = (bf16[1,8,64,128]{3,2,1,0:T(8,128)(2,1)S(1)}, bf16[1,8,64,128]{3,2,1,0:T(8,128)(2,1)}, u32[]{:S(2)}) copy-start(bf16[1,8,64,128]{3,2,1,0:T(8,128)(2,1)} %param.6) | copy-start | bytes 393220
  1.7 5.2 %collective-permute-start = (bf16[2,32,128]{2,1,0:T(8,128)(2,1)S(1)}, bf16[2,32,128]{2,1,0:T(8,128)(2,1)S(1)}, u32[]{:S(2)}, u32[]{:S(2)}) collective-permute-start(bf16[2,32,128]{2,1,0:T(8,128)(2,1)S(1)} %get-tuple-element.31), channel_id=1, source_target_pairs={{0,16},{4,20},{8,24},{12,28},{16,0},{20,4},{24,8},{28,12},{1,17},{... | collective-permute-start | bytes 49160 | tf_op jit(solution)/shard_map/ppermute | solution.py:215
  4.2 4.1 %collective-permute-start.3 = (bf16[32,512]{1,0:T(8,128)(2,1)S(1)}, bf16[32,512]{1,0:T(8,128)(2,1)S(1)}, u32[]{:S(2)}, u32[]{:S(2)}) collective-permute-start(bf16[32,512]{1,0:T(8,128)(2,1)S(1)} %get-tuple-element.33), channel_id=1, source_target_pairs={{0,1},{1,0},{2,3},{3,2},{4,5},{5,4},{6,7},{7,6},{8,9},{9,8},{10,11... | collective-permute-start | bytes 98312 | tf_op jit(solution)/shard_map/ppermute | solution.py:215
  5.2 3.1 %collective-permute-start.4 = (bf16[32,512]{1,0:T(8,128)(2,1)S(1)}, bf16[32,512]{1,0:T(8,128)(2,1)S(1)}, u32[]{:S(2)}, u32[]{:S(2)}) collective-permute-start(bf16[32,512]{1,0:T(8,128)(2,1)S(1)} %get-tuple-element.34), channel_id=1, source_target_pairs={{0,2},{1,3},{2,0},{3,1},{4,6},{5,7},{6,4},{7,5},{8,10},{9,11},{10,... | collective-permute-start | bytes 98312 | tf_op jit(solution)/shard_map/ppermute | solution.py:215
  6.4 3.3 %collective-permute-start.5 = (bf16[32,512]{1,0:T(8,128)(2,1)S(1)}, bf16[32,512]{1,0:T(8,128)(2,1)S(1)}, u32[]{:S(2)}, u32[]{:S(2)}) collective-permute-start(bf16[32,512]{1,0:T(8,128)(2,1)S(1)} %get-tuple-element.35), channel_id=1, source_target_pairs={{0,3},{1,2},{2,1},{3,0},{4,7},{5,6},{6,5},{7,4},{8,11},{9,10},{10,... | collective-permute-start | bytes 98312 | tf_op jit(solution)/shard_map/ppermute | solution.py:215
  6.9 6.1 %collective-permute-start.1 = (bf16[1,2,32,128]{3,2,1,0:T(8,128)(2,1)S(1)}, bf16[1,2,32,128]{3,2,1,0:T(8,128)(2,1)S(1)}, u32[]{:S(2)}, u32[]{:S(2)}) collective-permute-start(bf16[1,2,32,128]{3,2,1,0:T(8,128)(2,1)S(1)} %get-tuple-element.58), channel_id=1, source_target_pairs={{0,8},{4,12},{8,0},{12,4},{16,24},{20,28},{24,16},{28,20},{1,9},{5... | collective-permute-start | bytes 49160 | tf_op jit(solution)/shard_map/ppermute | solution.py:215
  9.8 11.7 %collective-permute-start.7 = (bf16[4,32,512]{2,1,0:T(8,128)(2,1)S(1)}, bf16[4,32,512]{2,1,0:T(8,128)(2,1)S(1)}, u32[]{:S(2)}, u32[]{:S(2)}) collective-permute-start(bf16[4,32,512]{2,1,0:T(8,128)(2,1)S(1)} %pad_maximum_fusion.1.refs_1_), channel_id=1, source_target_pairs={{4,8},{8,4},{12,16},{16,12},{20,24},{24,20},{5,9},{9,5},{13,17},{1... | collective-permute-start | bytes 393224 | tf_op jit(solution)/shard_map/ppermute | solution.py:221
  13.0 8.6 %collective-permute-start.6 = (bf16[4,32,512]{2,1,0:T(8,128)(2,1)S(1)}, bf16[4,32,512]{2,1,0:T(8,128)(2,1)S(1)}, u32[]{:S(2)}, u32[]{:S(2)}) collective-permute-start(bf16[4,32,512]{2,1,0:T(8,128)(2,1)S(1)} %pad_maximum_fusion.1.refs_1_), channel_id=1, source_target_pairs={{0,4},{4,0},{8,12},{12,8},{16,20},{20,16},{24,28},{28,24},{1,5},{5... | collective-permute-start | bytes 393224 | tf_op jit(solution)/shard_map/ppermute | solution.py:215
  13.1 8.5 %copy-start.4 = (bf16[1,8,64,128]{3,2,1,0:T(8,128)(2,1)S(1)}, bf16[1,8,64,128]{3,2,1,0:T(8,128)(2,1)}, u32[]{:S(2)}) copy-start(bf16[1,8,64,128]{3,2,1,0:T(8,128)(2,1)} %param.7) | copy-start | bytes 393220
  13.1 8.5 %copy-start.5 = (bf16[1,8,64,128]{3,2,1,0:T(8,128)(2,1)S(1)}, bf16[1,8,64,128]{3,2,1,0:T(8,128)(2,1)}, u32[]{:S(2)}) copy-start(bf16[1,8,64,128]{3,2,1,0:T(8,128)(2,1)} %param.10) | copy-start | bytes 393220
  13.1 8.4 %collective-permute-start.2 = (bf16[4,32,128]{2,1,0:T(8,128)(2,1)S(1)}, bf16[4,32,128]{2,1,0:T(8,128)(2,1)S(1)}, u32[]{:S(2)}, u32[]{:S(2)}) collective-permute-start(bf16[4,32,128]{2,1,0:T(8,128)(2,1)S(1)} %maximum_bitcast_fusion.refs_3_), channel_id=1, source_target_pairs={{0,4},{4,0},{8,12},{12,8},{16,20},{20,16},{24,28},{28,24},{1,5},{5... | collective-permute-start | bytes 98312 | tf_op jit(solution)/shard_map/ppermute | solution.py:215
  22.2 5.9 %collective-permute-start.10 = (bf16[512,128]{1,0:T(8,128)(2,1)S(1)}, bf16[512,128]{1,0:T(8,128)(2,1)S(1)}, u32[]{:S(2)}, u32[]{:S(2)}) collective-permute-start(bf16[512,128]{1,0:T(8,128)(2,1)S(1)} %get-tuple-element.40.refs_3_), channel_id=1, source_target_pairs={{0,3},{1,2},{2,1},{3,0},{4,7},{5,6},{6,5},{7,4},{8,11},{9,10},{10,... | collective-permute-start | bytes 393224 | tf_op jit(solution)/shard_map/ppermute | solution.py:215
  23.2 7.5 %collective-permute-start.9 = (bf16[512,128]{1,0:T(8,128)(2,1)S(1)}, bf16[512,128]{1,0:T(8,128)(2,1)S(1)}, u32[]{:S(2)}, u32[]{:S(2)}) collective-permute-start(bf16[512,128]{1,0:T(8,128)(2,1)S(1)} %get-tuple-element.40.refs_3_), channel_id=1, source_target_pairs={{0,2},{1,3},{2,0},{3,1},{4,6},{5,7},{6,4},{7,5},{8,10},{9,11},{10,... | collective-permute-start | bytes 393224 | tf_op jit(solution)/shard_map/ppermute | solution.py:215
  24.1 6.7 %collective-permute-start.8 = (bf16[512,128]{1,0:T(8,128)(2,1)S(1)}, bf16[512,128]{1,0:T(8,128)(2,1)S(1)}, u32[]{:S(2)}, u32[]{:S(2)}) collective-permute-start(bf16[512,128]{1,0:T(8,128)(2,1)S(1)} %get-tuple-element.40.refs_3_), channel_id=1, source_target_pairs={{0,1},{1,0},{2,3},{3,2},{4,5},{5,4},{6,7},{7,6},{8,9},{9,8},{10,11... | collective-permute-start | bytes 393224 | tf_op jit(solution)/shard_map/ppermute | solution.py:215
  24.4 8.0 %collective-permute-start.12 = (bf16[256,128]{1,0:T(8,128)(2,1)S(1)}, bf16[256,128]{1,0:T(8,128)(2,1)S(1)}, u32[]{:S(2)}, u32[]{:S(2)}) collective-permute-start(bf16[256,128]{1,0:T(8,128)(2,1)S(1)} %get-tuple-element.44), channel_id=1, source_target_pairs={{0,1},{1,0},{2,3},{3,2},{4,5},{5,4},{6,7},{7,6},{8,9},{9,8},{10,11... | collective-permute-start | bytes 196616 | tf_op jit(solution)/shard_map/ppermute | solution.py:215
  24.6 7.8 %collective-permute-start.13 = (bf16[256,128]{1,0:T(8,128)(2,1)S(1)}, bf16[256,128]{1,0:T(8,128)(2,1)S(1)}, u32[]{:S(2)}, u32[]{:S(2)}) collective-permute-start(bf16[256,128]{1,0:T(8,128)(2,1)S(1)} %get-tuple-element.45), channel_id=1, source_target_pairs={{0,2},{1,3},{2,0},{3,1},{4,6},{5,7},{6,4},{7,5},{8,10},{9,11},{10,... | collective-permute-start | bytes 196616 | tf_op jit(solution)/shard_map/ppermute | solution.py:215
  28.0 5.5 %collective-permute-start.14 = (bf16[256,128]{1,0:T(8,128)(2,1)S(1)}, bf16[256,128]{1,0:T(8,128)(2,1)S(1)}, u32[]{:S(2)}, u32[]{:S(2)}) collective-permute-start(bf16[256,128]{1,0:T(8,128)(2,1)S(1)} %get-tuple-element.46), channel_id=1, source_target_pairs={{0,3},{1,2},{2,1},{3,0},{4,7},{5,6},{6,5},{7,4},{8,11},{9,10},{10,... | collective-permute-start | bytes 196616 | tf_op jit(solution)/shard_map/ppermute | solution.py:215
  32.3 3.7 %collective-permute-start.11 = (bf16[432,128]{1,0:T(8,128)(2,1)S(1)}, bf16[432,128]{1,0:T(8,128)(2,1)S(1)}, u32[]{:S(2)}, u32[]{:S(2)}) collective-permute-start(bf16[432,128]{1,0:T(8,128)(2,1)S(1)} %get-tuple-element.42), channel_id=1, source_target_pairs={{0,4},{4,0},{8,12},{12,8},{16,20},{20,16},{24,28},{28,24},{1,5},{5... | collective-permute-start | bytes 331784 | tf_op jit(solution)/shard_map/ppermute | solution.py:215
  35.9 27.4 %copy-start.1 = (bf16[3,3,3,128,128]{4,3,2,1,0:T(8,128)(2,1)S(1)}, bf16[3,3,3,128,128]{4,3,2,1,0:T(8,128)(2,1)}, u32[]{:S(2)}) copy-start(bf16[3,3,3,128,128]{4,3,2,1,0:T(8,128)(2,1)} %weight.1) | copy-start | bytes 2654212
  36.0 9.5 %collective-permute-start.15 = (bf16[688,128]{1,0:T(8,128)(2,1)S(1)}, bf16[688,128]{1,0:T(8,128)(2,1)S(1)}, u32[]{:S(2)}, u32[]{:S(2)}) collective-permute-start(bf16[688,128]{1,0:T(8,128)(2,1)S(1)} %pad_maximum_fusion), channel_id=1, source_target_pairs={{0,16},{4,20},{8,24},{12,28},{16,0},{20,4},{24,8},{28,12},{1,17},{... | collective-permute-start | bytes 528392 | tf_op jit(solution)/shard_map/ppermute | solution.py:215
  36.5 4.2 %collective-permute-start.16 = (bf16[10,64,128]{2,1,0:T(8,128)(2,1)S(1)}, bf16[10,64,128]{2,1,0:T(8,128)(2,1)S(1)}, u32[]{:S(2)}, u32[]{:S(2)}) collective-permute-start(bf16[10,64,128]{2,1,0:T(8,128)(2,1)S(1)} %get-tuple-element.47.own), channel_id=1, source_target_pairs={{0,4},{4,0},{8,12},{12,8},{16,20},{20,16},{24,28},{28,24},{1,5},{5... | collective-permute-start | bytes 491528 | tf_op jit(solution)/shard_map/ppermute | solution.py:215
  45.6 4.4 %collective-permute-start.17 = (bf16[688,128]{1,0:T(8,128)(2,1)S(1)}, bf16[688,128]{1,0:T(8,128)(2,1)S(1)}, u32[]{:S(2)}, u32[]{:S(2)}) collective-permute-start(bf16[688,128]{1,0:T(8,128)(2,1)S(1)} %add_convert_fusion), channel_id=1, source_target_pairs={{0,8},{4,12},{8,0},{12,4},{16,24},{20,28},{24,16},{28,20},{1,9},{5... | collective-permute-start | bytes 528392 | tf_op jit(solution)/shard_map/ppermute | solution.py:215
  50.1 8.8 %collective-permute-start.18 = (bf16[688,128]{1,0:T(8,128)(2,1)S(1)}, bf16[688,128]{1,0:T(8,128)(2,1)S(1)}, u32[]{:S(2)}, u32[]{:S(2)}) collective-permute-start(bf16[688,128]{1,0:T(8,128)(2,1)S(1)} %multiply_convert_fusion.refs_0_), channel_id=1, source_target_pairs={{0,4},{4,0},{8,12},{12,8},{16,20},{20,16},{24,28},{28,24},{1,5},{5... | collective-permute-start | bytes 528392 | tf_op jit(solution)/shard_map/ppermute | solution.py:215
  51.9 7.1 %collective-permute-start.19 = (bf16[10,64,128]{2,1,0:T(8,128)(2,1)S(1)}, bf16[10,64,128]{2,1,0:T(8,128)(2,1)S(1)}, u32[]{:S(2)}, u32[]{:S(2)}) collective-permute-start(bf16[10,64,128]{2,1,0:T(8,128)(2,1)S(1)} %get-tuple-element.47.own), channel_id=1, source_target_pairs={{4,8},{8,4},{12,16},{16,12},{20,24},{24,20},{5,9},{9,5},{13,17},{1... | collective-permute-start | bytes 491528 | tf_op jit(solution)/shard_map/ppermute | solution.py:221
  53.8 11.2 %collective-permute-start.22 = (bf16[688,128]{1,0:T(8,128)(2,1)S(1)}, bf16[688,128]{1,0:T(8,128)(2,1)S(1)}, u32[]{:S(2)}, u32[]{:S(2)}) collective-permute-start(bf16[688,128]{1,0:T(8,128)(2,1)S(1)} %multiply_convert_fusion.refs_0_), channel_id=1, source_target_pairs={{0,2},{1,3},{2,0},{3,1},{4,6},{5,7},{6,4},{7,5},{8,10},{9,11},{10,... | collective-permute-start | bytes 528392 | tf_op jit(solution)/shard_map/ppermute | solution.py:215
  58.9 6.1 %collective-permute-start.20 = (bf16[688,128]{1,0:T(8,128)(2,1)S(1)}, bf16[688,128]{1,0:T(8,128)(2,1)S(1)}, u32[]{:S(2)}, u32[]{:S(2)}) collective-permute-start(bf16[688,128]{1,0:T(8,128)(2,1)S(1)} %collective-permute-done.18.refs_4_), channel_id=1, source_target_pairs={{0,2},{1,3},{2,0},{3,1},{4,6},{5,7},{6,4},{7,5},{8,10},{9,11},{10,... | collective-permute-start | bytes 528392 | tf_op jit(solution)/shard_map/ppermute | solution.py:215
  59.4 8.5 %collective-permute-start.21 = (bf16[688,128]{1,0:T(8,128)(2,1)S(1)}, bf16[688,128]{1,0:T(8,128)(2,1)S(1)}, u32[]{:S(2)}, u32[]{:S(2)}) collective-permute-start(bf16[688,128]{1,0:T(8,128)(2,1)S(1)} %multiply_convert_fusion.refs_0_), channel_id=1, source_target_pairs={{0,1},{1,0},{2,3},{3,2},{4,5},{5,4},{6,7},{7,6},{8,9},{9,8},{10,11... | collective-permute-start | bytes 528392 | tf_op jit(solution)/shard_map/ppermute | solution.py:215
  65.0 2.9 %collective-permute-start.23 = (bf16[688,128]{1,0:T(8,128)(2,1)S(1)}, bf16[688,128]{1,0:T(8,128)(2,1)S(1)}, u32[]{:S(2)}, u32[]{:S(2)}) collective-permute-start(bf16[688,128]{1,0:T(8,128)(2,1)S(1)} %collective-permute-done.22.refs_2_), channel_id=1, source_target_pairs={{0,1},{1,0},{2,3},{3,2},{4,5},{5,4},{6,7},{7,6},{8,9},{9,8},{10,11... | collective-permute-start | bytes 528392 | tf_op jit(solution)/shard_map/ppermute | solution.py:215
  65.1 3.9 %collective-permute-start.24 = (bf16[688,128]{1,0:T(8,128)(2,1)S(1)}, bf16[688,128]{1,0:T(8,128)(2,1)S(1)}, u32[]{:S(2)}, u32[]{:S(2)}) collective-permute-start(bf16[688,128]{1,0:T(8,128)(2,1)S(1)} %collective-permute-done.18.refs_4_), channel_id=1, source_target_pairs={{0,1},{1,0},{2,3},{3,2},{4,5},{5,4},{6,7},{7,6},{8,9},{9,8},{10,11... | collective-permute-start | bytes 528392 | tf_op jit(solution)/shard_map/ppermute | solution.py:215
  67.9 1.4 %collective-permute-start.25 = (bf16[688,128]{1,0:T(8,128)(2,1)S(1)}, bf16[688,128]{1,0:T(8,128)(2,1)S(1)}, u32[]{:S(2)}, u32[]{:S(2)}) collective-permute-start(bf16[688,128]{1,0:T(8,128)(2,1)S(1)} %collective-permute-done.20.refs_6_), channel_id=1, source_target_pairs={{0,1},{1,0},{2,3},{3,2},{4,5},{5,4},{6,7},{7,6},{8,9},{9,8},{10,11... | collective-permute-start | bytes 528392 | tf_op jit(solution)/shard_map/ppermute | solution.py:215

commit v11 on v10

--- a/solution.py
+++ b/solution.py
@@ -274,7 +274,7 @@
     level_t = [swapped(value, "gy", code) if code else value for code, value in enumerate(level_t)]
     level_t = jnp.stack(level_t)
     even, odd = neighbours(level_t)
-    *deep_t, even, odd = lax.optimization_barrier((*deep_t, even, odd))
+    *deep_t, level_t = lax.optimization_barrier((*deep_t, level_t))
     down_slice = lax.dynamic_index_in_dim(down_weight, parity, 0, keepdims=False)
     grad, down, *others = call(
         lambda *refs: mask_kernel(n_gy, *refs),
@@ -290,6 +290,7 @@
         ],
     )
     shared = [swapped(grad, "gy", code) if code else grad for code in range(n_gy)]
+    even, odd, *others = lax.optimization_barrier((even, odd, *others))
     for code, value in enumerate(others):
         down = down + swapped(value, "gy", code + 1).astype(F32)
     keep, send, near = call(
@@ -317,7 +318,17 @@
     while code > 1:
         other = swapped(total, "gz", code)
         if code == 4:
-            other, near_even = lax.optimization_barrier((other, near_even))
+            other, near_even, near_odd = lax.optimization_barrier((other, near_even, near_odd))
+        if code == 2:
+            input_grad = call(
+                input_kernel,
+                shape((rows, cols, channels), BF16),
+                near_even,
+                near,
+                near_odd,
+                conv_weight,
+            )
+            other, input_grad = lax.optimization_barrier((other, input_grad))
         total = total.astype(F32) + other.astype(F32)
         if code > 2:
             total = lax.optimization_barrier(total.astype(wire))
@@ -329,22 +340,11 @@
     )
     total = (total * scale).astype(BF16)
     pair = [total, swapped(total, "gz", 1)]
-    pair[1], near_odd = lax.optimization_barrier((pair[1], near_odd))
-    input_grad = call(
-        input_kernel,
-        shape((rows, cols, channels), BF16),
-        near_even,
-        near,
-        near_odd,
-        conv_weight,
-    )
     blocks = []
     for index, block in enumerate(pair):
         line = [block]
         code = n_gy // 2
         while code:
-            if code == 1 and index == 1:
-                input_grad, *line = lax.optimization_barrier((input_grad, *line))
             line = line + [swapped(value, "gy", code) for value in line]
             code //= 2
         blocks += [line[reversed_bits(place, n_gy)] for place in range(n_gy)]

time: 70.8 us -> 66.5 us (0.939)
  the two profiles are of different devices: /device:TPU:5 before, /device:TPU:0 now
where the time goes in v11:
time: 66.5 us; the launch traced here: 66.3 us
  starting transfers between devices  32.3 us (49%)
  waiting for transfers between devices  26.5 us (40%)
  Pallas kernels  5.36 us (8%)
  local copies, waits for them, and re-layouts  1 us (2%)
  between operations  0.83 us (1%)
    ppermute x24, starting transfers between devices, swapped(): lax.ppermute(value, axis, [(i, i ^ code) for i in range(lax.axis_size(axi...  30.8 us
    ppermute x24, waiting for transfers between devices, swapped(): lax.ppermute(value, axis, [(i, i ^ code) for i in range(lax.axis_size(axi...  26.5 us
    pallas_call x6, Pallas kernels, call(): pl.pallas_call(kernel, out_shape=out_shape, scratch_shapes=list(scratch),...  5.36 us
    ppermute x2, starting transfers between devices, neighbours(): return (swapped(value, 'gz', 1), lax.ppermute(value, 'gz', odd))  1.46 us
  transfers between devices with their start and end apart: 26, of which 12 were waited for; matrix products, arithmetic and copies ran while one was open for 0% of the time, Pallas kernels for 6%

profile of v11, /device:TPU:0, one launch (start us, length us, event | category | flops | bytes accessed | tf_op | source)
XLA Modules:
  0.0 66.3 jit_solution(13754355288807764862)
XLA Ops:
  0.6 0.0 copy-start
  0.7 1.0 %copy-done.2 = bf16[4,4,32,32]{3,2,1,0:T(8,128)(2,1)S(1)} copy-done((bf16[4,4,32,32]{3,2,1,0:T(8,128)(2,1)S(1)}, bf16[4,4,32,32]{3,2,1,0:T(8,128)(2,1)}, u32[]{:S(2)}) %copy-start.2) | copy-done | bytes 32792
  1.6 0.1 shard_map.86
  1.7 4.1 %collective-permute-start.5 = (bf16[2,32,128]{2,1,0:T(8,128)(2,1)S(1)}, bf16[2,32,128]{2,1,0:T(8,128)(2,1)S(1)}, u32[]{:S(2)}, u32[]{:S(2)}) collective-permute-start(bf16[2,32,128]{2,1,0:T(8,128)(2,1)S(1)} %get-tuple-element.37), channel_id=1, source_target_pairs={{0,16},{4,20},{8,24},{12,28},{16,0},{20,4},{24,8},{28,12},{1,17},{... | collective-permute-start | bytes 49160 | tf_op jit(solution)/shard_map/ppermute | solution.py:215
  5.8 0.1 shard_map.85
  5.9 0.1 collective-permute-start
  6.0 1.6 %collective-permute-start.1 = (bf16[32,512]{1,0:T(8,128)(2,1)S(1)}, bf16[32,512]{1,0:T(8,128)(2,1)S(1)}, u32[]{:S(2)}, u32[]{:S(2)}) collective-permute-start(bf16[32,512]{1,0:T(8,128)(2,1)S(1)} %get-tuple-element.34), channel_id=1, source_target_pairs={{0,2},{1,3},{2,0},{3,1},{4,6},{5,7},{6,4},{7,5},{8,10},{9,11},{10,... | collective-permute-start | bytes 98312 | tf_op jit(solution)/shard_map/ppermute | solution.py:215
  7.6 0.3 collective-permute-start.2
  7.9 0.0 collective-permute-done.5
  7.9 1.6 %collective-permute-start.6 = (bf16[1,2,32,128]{3,2,1,0:T(8,128)(2,1)S(1)}, bf16[1,2,32,128]{3,2,1,0:T(8,128)(2,1)S(1)}, u32[]{:S(2)}, u32[]{:S(2)}) collective-permute-start(bf16[1,2,32,128]{3,2,1,0:T(8,128)(2,1)S(1)} %get-tuple-element.62), channel_id=1, source_target_pairs={{0,8},{4,12},{8,0},{12,4},{16,24},{20,28},{24,16},{28,20},{1,9},{5... | collective-permute-start | bytes 49160 | tf_op jit(solution)/shard_map/ppermute | solution.py:215
  9.5 2.1 %collective-permute-done.6 = bf16[1,2,32,128]{3,2,1,0:T(8,128)(2,1)S(1)} collective-permute-done((bf16[1,2,32,128]{3,2,1,0:T(8,128)(2,1)S(1)}, bf16[1,2,32,128]{3,2,1,0:T(8,128)(2,1)S(1)}, u32[]{:S(2)}, u32[]{:S(2)}) %collective-permute-start.6) | collective-permute-done | bytes 16416 | tf_op jit(solution)/shard_map/ppermute | solution.py:215
  11.7 1.5 %collective-permute-start.7 = (bf16[4,32,128]{2,1,0:T(8,128)(2,1)S(1)}, bf16[4,32,128]{2,1,0:T(8,128)(2,1)S(1)}, u32[]{:S(2)}, u32[]{:S(2)}) collective-permute-start(bf16[4,32,128]{2,1,0:T(8,128)(2,1)S(1)} %maximum_bitcast_fusion.refs_3_), channel_id=1, source_target_pairs={{0,4},{4,0},{8,12},{12,8},{16,20},{20,16},{24,28},{28,24},{1,5},{5... | collective-permute-start | bytes 98312 | tf_op jit(solution)/shard_map/ppermute | solution.py:215
  13.2 0.0 collective-permute-done
  13.2 0.0 collective-permute-done.1
  13.2 0.0 collective-permute-done.2
  13.2 0.0 copy-start.4
  13.2 0.0 copy-start.5
  13.3 0.8 %collective-permute-start.4 = (bf16[4,32,512]{2,1,0:T(8,128)(2,1)S(1)}, bf16[4,32,512]{2,1,0:T(8,128)(2,1)S(1)}, u32[]{:S(2)}, u32[]{:S(2)}) collective-permute-start(bf16[4,32,512]{2,1,0:T(8,128)(2,1)S(1)} %pad_maximum_fusion.1.refs_1_), channel_id=1, source_target_pairs={{4,8},{8,4},{12,16},{16,12},{20,24},{24,20},{5,9},{9,5},{13,17},{1... | collective-permute-start | bytes 393224 | tf_op jit(solution)/shard_map/ppermute | solution.py:221
  14.1 4.3 %collective-permute-start.3 = (bf16[4,32,512]{2,1,0:T(8,128)(2,1)S(1)}, bf16[4,32,512]{2,1,0:T(8,128)(2,1)S(1)}, u32[]{:S(2)}, u32[]{:S(2)}) collective-permute-start(bf16[4,32,512]{2,1,0:T(8,128)(2,1)S(1)} %pad_maximum_fusion.1.refs_1_), channel_id=1, source_target_pairs={{0,4},{4,0},{8,12},{12,8},{16,20},{20,16},{24,28},{28,24},{1,5},{5... | collective-permute-start | bytes 393224 | tf_op jit(solution)/shard_map/ppermute | solution.py:215
  18.4 0.0 collective-permute-done.7.refs_4_
  18.4 0.6 shard_map.87
  19.1 0.1 collective-permute-start.10
  19.1 1.6 %collective-permute-start.9 = (bf16[512,128]{1,0:T(8,128)(2,1)S(1)}, bf16[512,128]{1,0:T(8,128)(2,1)S(1)}, u32[]{:S(2)}, u32[]{:S(2)}) collective-permute-start(bf16[512,128]{1,0:T(8,128)(2,1)S(1)} %get-tuple-element.46.refs_3_), channel_id=1, source_target_pairs={{0,2},{1,3},{2,0},{3,1},{4,6},{5,7},{6,4},{7,5},{8,10},{9,11},{10,... | collective-permute-start | bytes 393224 | tf_op jit(solution)/shard_map/ppermute | solution.py:215
  20.7 0.3 collective-permute-start.8
  21.0 0.0 collective-permute-done.4.refs_2_
  21.0 0.5 collective-permute-done.3.refs_0_
  21.5 0.0 collective-permute-start.12
  21.5 1.3 %collective-permute-start.13 = (bf16[256,128]{1,0:T(8,128)(2,1)S(1)}, bf16[256,128]{1,0:T(8,128)(2,1)S(1)}, u32[]{:S(2)}, u32[]{:S(2)}) collective-permute-start(bf16[256,128]{1,0:T(8,128)(2,1)S(1)} %get-tuple-element.51), channel_id=1, source_target_pairs={{0,2},{1,3},{2,0},{3,1},{4,6},{5,7},{6,4},{7,5},{8,10},{9,11},{10,... | collective-permute-start | bytes 196616 | tf_op jit(solution)/shard_map/ppermute | solution.py:215
  22.9 2.0 %collective-permute-done.10.refs_6_ = bf16[512,128]{1,0:T(8,128)(2,1)S(1)} collective-permute-done((bf16[512,128]{1,0:T(8,128)(2,1)S(1)}, bf16[512,128]{1,0:T(8,128)(2,1)S(1)}, u32[]{:S(2)}, u32[]{:S(2)}) %collective-permute-start.10) | collective-permute-done | bytes 131104 | tf_op jit(solution)/shard_map/ppermute | solution.py:215
  24.9 0.0 collective-permute-start.14
  24.9 2.9 %collective-permute-done.9.refs_5_ = bf16[512,128]{1,0:T(8,128)(2,1)S(1)} collective-permute-done((bf16[512,128]{1,0:T(8,128)(2,1)S(1)}, bf16[512,128]{1,0:T(8,128)(2,1)S(1)}, u32[]{:S(2)}, u32[]{:S(2)}) %collective-permute-start.9) | collective-permute-done | bytes 131104 | tf_op jit(solution)/shard_map/ppermute | solution.py:215
  27.8 0.0 collective-permute-done.8.refs_4_
  27.8 1.5 %shard_map.88 = (f32[432,128]{1,0:T(8,128)S(1)}, bf16[432,128]{1,0:T(8,128)(2,1)S(1)}, bf16[10,64,128]{2,1,0:T(8,128)(2,1)S(1)}) custom-call(bf16[4,32,512]{2,1,0:T(8,128)(2,1)S(1)} %collective-permute-done.3.refs_0_, bf16[4,32,512]{2,1,0:T(8,128)(2,1)S(1)} %pad_maximum_fusion.1.refs_1_, bf16[4,32,512]{2,1,0:T(8,128)(2,1)S(1)} %collective-permute-done.4.refs_2_, ...), custom_call_target="tpu_custom_call" | custom-call | tf_op jit(solution)/shard_map/pallas_call | solution.py:16
  29.3 0.0 copy-start.1
  29.3 0.1 collective-permute-start.11
  29.4 0.0 collective-permute-done.12
  29.4 0.0 collective-permute-done.13
  29.4 1.0 %collective-permute-done.14 = bf16[256,128]{1,0:T(8,128)(2,1)S(1)} collective-permute-done((bf16[256,128]{1,0:T(8,128)(2,1)S(1)}, bf16[256,128]{1,0:T(8,128)(2,1)S(1)}, u32[]{:S(2)}, u32[]{:S(2)}) %collective-permute-start.14) | collective-permute-done | bytes 65568 | tf_op jit(solution)/shard_map/ppermute | solution.py:215
  30.5 3.8 %collective-permute-done.11 = bf16[432,128]{1,0:T(8,128)(2,1)S(1)} collective-permute-done((bf16[432,128]{1,0:T(8,128)(2,1)S(1)}, bf16[432,128]{1,0:T(8,128)(2,1)S(1)}, u32[]{:S(2)}, u32[]{:S(2)}) %collective-permute-start.11) | collective-permute-done | bytes 110624 | tf_op jit(solution)/shard_map/ppermute | solution.py:215
  34.4 2.6 %collective-permute-start.15 = (bf16[688,128]{1,0:T(8,128)(2,1)S(1)}, bf16[688,128]{1,0:T(8,128)(2,1)S(1)}, u32[]{:S(2)}, u32[]{:S(2)}) collective-permute-start(bf16[688,128]{1,0:T(8,128)(2,1)S(1)} %pad_maximum_fusion), channel_id=1, source_target_pairs={{0,16},{4,20},{8,24},{12,28},{16,0},{20,4},{24,8},{28,12},{1,17},{... | collective-permute-start | bytes 528392 | tf_op jit(solution)/shard_map/ppermute | solution.py:215
  37.0 0.7 collective-permute-start.17
  37.7 1.9 %collective-permute-start.16 = (bf16[10,64,128]{2,1,0:T(8,128)(2,1)S(1)}, bf16[10,64,128]{2,1,0:T(8,128)(2,1)S(1)}, u32[]{:S(2)}, u32[]{:S(2)}) collective-permute-start(bf16[10,64,128]{2,1,0:T(8,128)(2,1)S(1)} %get-tuple-element.53.own), channel_id=1, source_target_pairs={{0,4},{4,0},{8,12},{12,8},{16,20},{20,16},{24,28},{28,24},{1,5},{5... | collective-permute-start | bytes 491528 | tf_op jit(solution)/shard_map/ppermute | solution.py:215
  39.6 0.0 collective-permute-done.17.odd
  39.6 5.0 %collective-permute-done.16.even = bf16[10,64,128]{2,1,0:T(8,128)(2,1)S(1)} collective-permute-done((bf16[10,64,128]{2,1,0:T(8,128)(2,1)S(1)}, bf16[10,64,128]{2,1,0:T(8,128)(2,1)S(1)}, u32[]{:S(2)}, u32[]{:S(2)}) %collective-permute-start.16) | collective-permute-done | bytes 163872 | tf_op jit(solution)/shard_map/ppermute | solution.py:215
  44.7 1.1 %collective-permute-done.15 = bf16[688,128]{1,0:T(8,128)(2,1)S(1)} collective-permute-done((bf16[688,128]{1,0:T(8,128)(2,1)S(1)}, bf16[688,128]{1,0:T(8,128)(2,1)S(1)}, u32[]{:S(2)}, u32[]{:S(2)}) %collective-permute-start.15) | collective-permute-done | bytes 176160 | tf_op jit(solution)/shard_map/ppermute | solution.py:215
  45.8 2.9 %collective-permute-start.18 = (bf16[688,128]{1,0:T(8,128)(2,1)S(1)}, bf16[688,128]{1,0:T(8,128)(2,1)S(1)}, u32[]{:S(2)}, u32[]{:S(2)}) collective-permute-start(bf16[688,128]{1,0:T(8,128)(2,1)S(1)} %add_convert_fusion), channel_id=1, source_target_pairs={{0,8},{4,12},{8,0},{12,4},{16,24},{20,28},{24,16},{28,20},{1,9},{5... | collective-permute-start | bytes 528392 | tf_op jit(solution)/shard_map/ppermute | solution.py:215
  48.7 1.7 %shard_map.89 = bf16[8,64,128]{2,1,0:T(8,128)(2,1)} custom-call(bf16[10,64,128]{2,1,0:T(8,128)(2,1)S(1)} %collective-permute-done.16.even, bf16[10,64,128]{2,1,0:T(8,128)(2,1)S(1)} %get-tuple-element.53.own, bf16[10,64,128]{2,1,0:T(8,128)(2,1)S(1)} %collective-permute-done.17.odd, bf16[3,3,3,128,128]{4,3,2,1,0:T(8,128)(2,1)S(1)} %copy-done.1), custom_call_target="tpu_custom_call" | custom-call | tf_op jit(solution)/shard_map/pallas_call | solution.py:16
  50.5 1.8 %collective-permute-done.18 = bf16[688,128]{1,0:T(8,128)(2,1)S(1)} collective-permute-done((bf16[688,128]{1,0:T(8,128)(2,1)S(1)}, bf16[688,128]{1,0:T(8,128)(2,1)S(1)}, u32[]{:S(2)}, u32[]{:S(2)}) %collective-permute-start.18) | collective-permute-done | bytes 176160 | tf_op jit(solution)/shard_map/ppermute | solution.py:215
  52.3 0.2 multiply_convert_fusion.refs_0_
  52.5 1.7 %collective-permute-start.22 = (bf16[688,128]{1,0:T(8,128)(2,1)S(1)}, bf16[688,128]{1,0:T(8,128)(2,1)S(1)}, u32[]{:S(2)}, u32[]{:S(2)}) collective-permute-start(bf16[688,128]{1,0:T(8,128)(2,1)S(1)} %multiply_convert_fusion.refs_0_), channel_id=1, source_target_pairs={{0,4},{4,0},{8,12},{12,8},{16,20},{20,16},{24,28},{28,24},{1,5},{5... | collective-permute-start | bytes 528392 | tf_op jit(solution)/shard_map/ppermute | solution.py:215
  54.2 2.1 %collective-permute-start.20 = (bf16[688,128]{1,0:T(8,128)(2,1)S(1)}, bf16[688,128]{1,0:T(8,128)(2,1)S(1)}, u32[]{:S(2)}, u32[]{:S(2)}) collective-permute-start(bf16[688,128]{1,0:T(8,128)(2,1)S(1)} %multiply_convert_fusion.refs_0_), channel_id=1, source_target_pairs={{0,2},{1,3},{2,0},{3,1},{4,6},{5,7},{6,4},{7,5},{8,10},{9,11},{10,... | collective-permute-start | bytes 528392 | tf_op jit(solution)/shard_map/ppermute | solution.py:215
  56.3 1.7 %collective-permute-done.22.refs_4_ = bf16[688,128]{1,0:T(8,128)(2,1)S(1)} collective-permute-done((bf16[688,128]{1,0:T(8,128)(2,1)S(1)}, bf16[688,128]{1,0:T(8,128)(2,1)S(1)}, u32[]{:S(2)}, u32[]{:S(2)}) %collective-permute-start.22) | collective-permute-done | bytes 176160 | tf_op jit(solution)/shard_map/ppermute | solution.py:215
  58.0 2.2 %collective-permute-start.24 = (bf16[688,128]{1,0:T(8,128)(2,1)S(1)}, bf16[688,128]{1,0:T(8,128)(2,1)S(1)}, u32[]{:S(2)}, u32[]{:S(2)}) collective-permute-start(bf16[688,128]{1,0:T(8,128)(2,1)S(1)} %collective-permute-done.22.refs_4_), channel_id=1, source_target_pairs={{0,2},{1,3},{2,0},{3,1},{4,6},{5,7},{6,4},{7,5},{8,10},{9,11},{10,... | collective-permute-start | bytes 528392 | tf_op jit(solution)/shard_map/ppermute | solution.py:215
  60.2 0.0 collective-permute-start.19
  60.2 0.5 collective-permute-start.23
  60.7 0.0 collective-permute-done.20.refs_2_
  60.7 0.0 collective-permute-start.21
  60.7 2.9 %collective-permute-done.24.refs_6_ = bf16[688,128]{1,0:T(8,128)(2,1)S(1)} collective-permute-done((bf16[688,128]{1,0:T(8,128)(2,1)S(1)}, bf16[688,128]{1,0:T(8,128)(2,1)S(1)}, u32[]{:S(2)}, u32[]{:S(2)}) %collective-permute-start.24) | collective-permute-done | bytes 176160 | tf_op jit(solution)/shard_map/ppermute | solution.py:215
  63.6 0.0 collective-permute-start.25
  63.6 0.0 collective-permute-done.19.refs_1_
  63.6 0.0 collective-permute-done.23.refs_5_
  63.6 0.0 collective-permute-done.21.refs_3_
  63.6 1.4 %collective-permute-done.25.refs_7_ = bf16[688,128]{1,0:T(8,128)(2,1)S(1)} collective-permute-done((bf16[688,128]{1,0:T(8,128)(2,1)S(1)}, bf16[688,128]{1,0:T(8,128)(2,1)S(1)}, u32[]{:S(2)}, u32[]{:S(2)}) %collective-permute-start.25) | collective-permute-done | bytes 176160 | tf_op jit(solution)/shard_map/ppermute | solution.py:215
  65.0 1.3 %shard_map.90 = (bf16[27,4,2,16,128]{4,3,2,1,0:T(8,128)(2,1)}, bf16[2,4,128,256]{3,2,1,0:T(8,128)(2,1)}) custom-call(bf16[688,128]{1,0:T(8,128)(2,1)S(1)} %multiply_convert_fusion.refs_0_, bf16[688,128]{1,0:T(8,128)(2,1)S(1)} %collective-permute-done.19.refs_1_, bf16[688,128]{1,0:T(8,128)(2,1)S(1)} %collective-permute-done.20.refs_2_, ...), custom_call_target="tpu_custom_call" | custom-call | tf_op jit(solution)/shard_map/pallas_call | solution.py:16
  (16 shorter events, 0.2 us)
Async XLA Ops:
  0.6 8.9 %copy-start = (bf16[2,2,2,128,256]{4,3,2,1,0:T(8,128)(2,1)S(1)}, bf16[2,2,2,128,256]{4,3,2,1,0:T(8,128)(2,1)}, u32[]{:S(2)}) copy-start(bf16[2,2,2,128,256]{4,3,2,1,0:T(8,128)(2,1)} %param.9) | copy-start | bytes 1572868
  0.6 1.0 %copy-start.2 = (bf16[4,4,32,32]{3,2,1,0:T(8,128)(2,1)S(1)}, bf16[4,4,32,32]{3,2,1,0:T(8,128)(2,1)}, u32[]{:S(2)}) copy-start(bf16[4,4,32,32]{3,2,1,0:T(8,128)(2,1)} %param.11) | copy-start | bytes 98308
  1.6 4.2 %copy-start.3 = (bf16[1,8,64,128]{3,2,1,0:T(8,128)(2,1)S(1)}, bf16[1,8,64,128]{3,2,1,0:T(8,128)(2,1)}, u32[]{:S(2)}) copy-start(bf16[1,8,64,128]{3,2,1,0:T(8,128)(2,1)} %param.6) | copy-start | bytes 393220
  1.7 6.2 %collective-permute-start.5 = (bf16[2,32,128]{2,1,0:T(8,128)(2,1)S(1)}, bf16[2,32,128]{2,1,0:T(8,128)(2,1)S(1)}, u32[]{:S(2)}, u32[]{:S(2)}) collective-permute-start(bf16[2,32,128]{2,1,0:T(8,128)(2,1)S(1)} %get-tuple-element.37), channel_id=1, source_target_pairs={{0,16},{4,20},{8,24},{12,28},{16,0},{20,4},{24,8},{28,12},{1,17},{... | collective-permute-start | bytes 49160 | tf_op jit(solution)/shard_map/ppermute | solution.py:215
  5.9 7.3 %collective-permute-start = (bf16[32,512]{1,0:T(8,128)(2,1)S(1)}, bf16[32,512]{1,0:T(8,128)(2,1)S(1)}, u32[]{:S(2)}, u32[]{:S(2)}) collective-permute-start(bf16[32,512]{1,0:T(8,128)(2,1)S(1)} %get-tuple-element.33), channel_id=1, source_target_pairs={{0,1},{1,0},{2,3},{3,2},{4,5},{5,4},{6,7},{7,6},{8,9},{9,8},{10,11... | collective-permute-start | bytes 98312 | tf_op jit(solution)/shard_map/ppermute | solution.py:215
  6.0 7.2 %collective-permute-start.1 = (bf16[32,512]{1,0:T(8,128)(2,1)S(1)}, bf16[32,512]{1,0:T(8,128)(2,1)S(1)}, u32[]{:S(2)}, u32[]{:S(2)}) collective-permute-start(bf16[32,512]{1,0:T(8,128)(2,1)S(1)} %get-tuple-element.34), channel_id=1, source_target_pairs={{0,2},{1,3},{2,0},{3,1},{4,6},{5,7},{6,4},{7,5},{8,10},{9,11},{10,... | collective-permute-start | bytes 98312 | tf_op jit(solution)/shard_map/ppermute | solution.py:215
  7.6 5.7 %collective-permute-start.2 = (bf16[32,512]{1,0:T(8,128)(2,1)S(1)}, bf16[32,512]{1,0:T(8,128)(2,1)S(1)}, u32[]{:S(2)}, u32[]{:S(2)}) collective-permute-start(bf16[32,512]{1,0:T(8,128)(2,1)S(1)} %get-tuple-element.35), channel_id=1, source_target_pairs={{0,3},{1,2},{2,1},{3,0},{4,7},{5,6},{6,5},{7,4},{8,11},{9,10},{10,... | collective-permute-start | bytes 98312 | tf_op jit(solution)/shard_map/ppermute | solution.py:215
  7.9 3.8 %collective-permute-start.6 = (bf16[1,2,32,128]{3,2,1,0:T(8,128)(2,1)S(1)}, bf16[1,2,32,128]{3,2,1,0:T(8,128)(2,1)S(1)}, u32[]{:S(2)}, u32[]{:S(2)}) collective-permute-start(bf16[1,2,32,128]{3,2,1,0:T(8,128)(2,1)S(1)} %get-tuple-element.62), channel_id=1, source_target_pairs={{0,8},{4,12},{8,0},{12,4},{16,24},{20,28},{24,16},{28,20},{1,9},{5... | collective-permute-start | bytes 49160 | tf_op jit(solution)/shard_map/ppermute | solution.py:215
  11.7 6.7 %collective-permute-start.7 = (bf16[4,32,128]{2,1,0:T(8,128)(2,1)S(1)}, bf16[4,32,128]{2,1,0:T(8,128)(2,1)S(1)}, u32[]{:S(2)}, u32[]{:S(2)}) collective-permute-start(bf16[4,32,128]{2,1,0:T(8,128)(2,1)S(1)} %maximum_bitcast_fusion.refs_3_), channel_id=1, source_target_pairs={{0,4},{4,0},{8,12},{12,8},{16,20},{20,16},{24,28},{28,24},{1,5},{5... | collective-permute-start | bytes 98312 | tf_op jit(solution)/shard_map/ppermute | solution.py:215
  13.2 5.2 %copy-start.4 = (bf16[1,8,64,128]{3,2,1,0:T(8,128)(2,1)S(1)}, bf16[1,8,64,128]{3,2,1,0:T(8,128)(2,1)}, u32[]{:S(2)}) copy-start(bf16[1,8,64,128]{3,2,1,0:T(8,128)(2,1)} %param.7) | copy-start | bytes 393220
  13.2 5.2 %copy-start.5 = (bf16[1,8,64,128]{3,2,1,0:T(8,128)(2,1)S(1)}, bf16[1,8,64,128]{3,2,1,0:T(8,128)(2,1)}, u32[]{:S(2)}) copy-start(bf16[1,8,64,128]{3,2,1,0:T(8,128)(2,1)} %param.10) | copy-start | bytes 393220
  13.3 7.7 %collective-permute-start.4 = (bf16[4,32,512]{2,1,0:T(8,128)(2,1)S(1)}, bf16[4,32,512]{2,1,0:T(8,128)(2,1)S(1)}, u32[]{:S(2)}, u32[]{:S(2)}) collective-permute-start(bf16[4,32,512]{2,1,0:T(8,128)(2,1)S(1)} %pad_maximum_fusion.1.refs_1_), channel_id=1, source_target_pairs={{4,8},{8,4},{12,16},{16,12},{20,24},{24,20},{5,9},{9,5},{13,17},{1... | collective-permute-start | bytes 393224 | tf_op jit(solution)/shard_map/ppermute | solution.py:221
  14.1 7.4 %collective-permute-start.3 = (bf16[4,32,512]{2,1,0:T(8,128)(2,1)S(1)}, bf16[4,32,512]{2,1,0:T(8,128)(2,1)S(1)}, u32[]{:S(2)}, u32[]{:S(2)}) collective-permute-start(bf16[4,32,512]{2,1,0:T(8,128)(2,1)S(1)} %pad_maximum_fusion.1.refs_1_), channel_id=1, source_target_pairs={{0,4},{4,0},{8,12},{12,8},{16,20},{20,16},{24,28},{28,24},{1,5},{5... | collective-permute-start | bytes 393224 | tf_op jit(solution)/shard_map/ppermute | solution.py:215
  19.1 5.8 %collective-permute-start.10 = (bf16[512,128]{1,0:T(8,128)(2,1)S(1)}, bf16[512,128]{1,0:T(8,128)(2,1)S(1)}, u32[]{:S(2)}, u32[]{:S(2)}) collective-permute-start(bf16[512,128]{1,0:T(8,128)(2,1)S(1)} %get-tuple-element.46.refs_3_), channel_id=1, source_target_pairs={{0,3},{1,2},{2,1},{3,0},{4,7},{5,6},{6,5},{7,4},{8,11},{9,10},{10,... | collective-permute-start | bytes 393224 | tf_op jit(solution)/shard_map/ppermute | solution.py:215
  19.1 8.6 %collective-permute-start.9 = (bf16[512,128]{1,0:T(8,128)(2,1)S(1)}, bf16[512,128]{1,0:T(8,128)(2,1)S(1)}, u32[]{:S(2)}, u32[]{:S(2)}) collective-permute-start(bf16[512,128]{1,0:T(8,128)(2,1)S(1)} %get-tuple-element.46.refs_3_), channel_id=1, source_target_pairs={{0,2},{1,3},{2,0},{3,1},{4,6},{5,7},{6,4},{7,5},{8,10},{9,11},{10,... | collective-permute-start | bytes 393224 | tf_op jit(solution)/shard_map/ppermute | solution.py:215
  20.7 7.1 %collective-permute-start.8 = (bf16[512,128]{1,0:T(8,128)(2,1)S(1)}, bf16[512,128]{1,0:T(8,128)(2,1)S(1)}, u32[]{:S(2)}, u32[]{:S(2)}) collective-permute-start(bf16[512,128]{1,0:T(8,128)(2,1)S(1)} %get-tuple-element.46.refs_3_), channel_id=1, source_target_pairs={{0,1},{1,0},{2,3},{3,2},{4,5},{5,4},{6,7},{7,6},{8,9},{9,8},{10,11... | collective-permute-start | bytes 393224 | tf_op jit(solution)/shard_map/ppermute | solution.py:215
  21.5 7.9 %collective-permute-start.12 = (bf16[256,128]{1,0:T(8,128)(2,1)S(1)}, bf16[256,128]{1,0:T(8,128)(2,1)S(1)}, u32[]{:S(2)}, u32[]{:S(2)}) collective-permute-start(bf16[256,128]{1,0:T(8,128)(2,1)S(1)} %get-tuple-element.50), channel_id=1, source_target_pairs={{0,1},{1,0},{2,3},{3,2},{4,5},{5,4},{6,7},{7,6},{8,9},{9,8},{10,11... | collective-permute-start | bytes 196616 | tf_op jit(solution)/shard_map/ppermute | solution.py:215
  21.5 7.9 %collective-permute-start.13 = (bf16[256,128]{1,0:T(8,128)(2,1)S(1)}, bf16[256,128]{1,0:T(8,128)(2,1)S(1)}, u32[]{:S(2)}, u32[]{:S(2)}) collective-permute-start(bf16[256,128]{1,0:T(8,128)(2,1)S(1)} %get-tuple-element.51), channel_id=1, source_target_pairs={{0,2},{1,3},{2,0},{3,1},{4,6},{5,7},{6,4},{7,5},{8,10},{9,11},{10,... | collective-permute-start | bytes 196616 | tf_op jit(solution)/shard_map/ppermute | solution.py:215
  24.9 5.6 %collective-permute-start.14 = (bf16[256,128]{1,0:T(8,128)(2,1)S(1)}, bf16[256,128]{1,0:T(8,128)(2,1)S(1)}, u32[]{:S(2)}, u32[]{:S(2)}) collective-permute-start(bf16[256,128]{1,0:T(8,128)(2,1)S(1)} %get-tuple-element.52), channel_id=1, source_target_pairs={{0,3},{1,2},{2,1},{3,0},{4,7},{5,6},{6,5},{7,4},{8,11},{9,10},{10,... | collective-permute-start | bytes 196616 | tf_op jit(solution)/shard_map/ppermute | solution.py:215
  29.3 19.4 %copy-start.1 = (bf16[3,3,3,128,128]{4,3,2,1,0:T(8,128)(2,1)S(1)}, bf16[3,3,3,128,128]{4,3,2,1,0:T(8,128)(2,1)}, u32[]{:S(2)}) copy-start(bf16[3,3,3,128,128]{4,3,2,1,0:T(8,128)(2,1)} %weight.1) | copy-start | bytes 2654212
  29.3 5.0 %collective-permute-start.11 = (bf16[432,128]{1,0:T(8,128)(2,1)S(1)}, bf16[432,128]{1,0:T(8,128)(2,1)S(1)}, u32[]{:S(2)}, u32[]{:S(2)}) collective-permute-start(bf16[432,128]{1,0:T(8,128)(2,1)S(1)} %get-tuple-element.48), channel_id=1, source_target_pairs={{0,4},{4,0},{8,12},{12,8},{16,20},{20,16},{24,28},{28,24},{1,5},{5... | collective-permute-start | bytes 331784 | tf_op jit(solution)/shard_map/ppermute | solution.py:215
  34.4 11.4 %collective-permute-start.15 = (bf16[688,128]{1,0:T(8,128)(2,1)S(1)}, bf16[688,128]{1,0:T(8,128)(2,1)S(1)}, u32[]{:S(2)}, u32[]{:S(2)}) collective-permute-start(bf16[688,128]{1,0:T(8,128)(2,1)S(1)} %pad_maximum_fusion), channel_id=1, source_target_pairs={{0,16},{4,20},{8,24},{12,28},{16,0},{20,4},{24,8},{28,12},{1,17},{... | collective-permute-start | bytes 528392 | tf_op jit(solution)/shard_map/ppermute | solution.py:215
  37.0 2.6 %collective-permute-start.17 = (bf16[10,64,128]{2,1,0:T(8,128)(2,1)S(1)}, bf16[10,64,128]{2,1,0:T(8,128)(2,1)S(1)}, u32[]{:S(2)}, u32[]{:S(2)}) collective-permute-start(bf16[10,64,128]{2,1,0:T(8,128)(2,1)S(1)} %get-tuple-element.53.own), channel_id=1, source_target_pairs={{4,8},{8,4},{12,16},{16,12},{20,24},{24,20},{5,9},{9,5},{13,17},{1... | collective-permute-start | bytes 491528 | tf_op jit(solution)/shard_map/ppermute | solution.py:221
  37.7 7.0 %collective-permute-start.16 = (bf16[10,64,128]{2,1,0:T(8,128)(2,1)S(1)}, bf16[10,64,128]{2,1,0:T(8,128)(2,1)S(1)}, u32[]{:S(2)}, u32[]{:S(2)}) collective-permute-start(bf16[10,64,128]{2,1,0:T(8,128)(2,1)S(1)} %get-tuple-element.53.own), channel_id=1, source_target_pairs={{0,4},{4,0},{8,12},{12,8},{16,20},{20,16},{24,28},{28,24},{1,5},{5... | collective-permute-start | bytes 491528 | tf_op jit(solution)/shard_map/ppermute | solution.py:215
  45.8 6.5 %collective-permute-start.18 = (bf16[688,128]{1,0:T(8,128)(2,1)S(1)}, bf16[688,128]{1,0:T(8,128)(2,1)S(1)}, u32[]{:S(2)}, u32[]{:S(2)}) collective-permute-start(bf16[688,128]{1,0:T(8,128)(2,1)S(1)} %add_convert_fusion), channel_id=1, source_target_pairs={{0,8},{4,12},{8,0},{12,4},{16,24},{20,28},{24,16},{28,20},{1,9},{5... | collective-permute-start | bytes 528392 | tf_op jit(solution)/shard_map/ppermute | solution.py:215
  52.5 5.5 %collective-permute-start.22 = (bf16[688,128]{1,0:T(8,128)(2,1)S(1)}, bf16[688,128]{1,0:T(8,128)(2,1)S(1)}, u32[]{:S(2)}, u32[]{:S(2)}) collective-permute-start(bf16[688,128]{1,0:T(8,128)(2,1)S(1)} %multiply_convert_fusion.refs_0_), channel_id=1, source_target_pairs={{0,4},{4,0},{8,12},{12,8},{16,20},{20,16},{24,28},{28,24},{1,5},{5... | collective-permute-start | bytes 528392 | tf_op jit(solution)/shard_map/ppermute | solution.py:215
  54.2 6.5 %collective-permute-start.20 = (bf16[688,128]{1,0:T(8,128)(2,1)S(1)}, bf16[688,128]{1,0:T(8,128)(2,1)S(1)}, u32[]{:S(2)}, u32[]{:S(2)}) collective-permute-start(bf16[688,128]{1,0:T(8,128)(2,1)S(1)} %multiply_convert_fusion.refs_0_), channel_id=1, source_target_pairs={{0,2},{1,3},{2,0},{3,1},{4,6},{5,7},{6,4},{7,5},{8,10},{9,11},{10,... | collective-permute-start | bytes 528392 | tf_op jit(solution)/shard_map/ppermute | solution.py:215
  58.0 5.6 %collective-permute-start.24 = (bf16[688,128]{1,0:T(8,128)(2,1)S(1)}, bf16[688,128]{1,0:T(8,128)(2,1)S(1)}, u32[]{:S(2)}, u32[]{:S(2)}) collective-permute-start(bf16[688,128]{1,0:T(8,128)(2,1)S(1)} %collective-permute-done.22.refs_4_), channel_id=1, source_target_pairs={{0,2},{1,3},{2,0},{3,1},{4,6},{5,7},{6,4},{7,5},{8,10},{9,11},{10,... | collective-permute-start | bytes 528392 | tf_op jit(solution)/shard_map/ppermute | solution.py:215
  60.2 3.4 %collective-permute-start.19 = (bf16[688,128]{1,0:T(8,128)(2,1)S(1)}, bf16[688,128]{1,0:T(8,128)(2,1)S(1)}, u32[]{:S(2)}, u32[]{:S(2)}) collective-permute-start(bf16[688,128]{1,0:T(8,128)(2,1)S(1)} %multiply_convert_fusion.refs_0_), channel_id=1, source_target_pairs={{0,1},{1,0},{2,3},{3,2},{4,5},{5,4},{6,7},{7,6},{8,9},{9,8},{10,11... | collective-permute-start | bytes 528392 | tf_op jit(solution)/shard_map/ppermute | solution.py:215
  60.2 3.4 %collective-permute-start.23 = (bf16[688,128]{1,0:T(8,128)(2,1)S(1)}, bf16[688,128]{1,0:T(8,128)(2,1)S(1)}, u32[]{:S(2)}, u32[]{:S(2)}) collective-permute-start(bf16[688,128]{1,0:T(8,128)(2,1)S(1)} %collective-permute-done.22.refs_4_), channel_id=1, source_target_pairs={{0,1},{1,0},{2,3},{3,2},{4,5},{5,4},{6,7},{7,6},{8,9},{9,8},{10,11... | collective-permute-start | bytes 528392 | tf_op jit(solution)/shard_map/ppermute | solution.py:215
  60.7 2.9 %collective-permute-start.21 = (bf16[688,128]{1,0:T(8,128)(2,1)S(1)}, bf16[688,128]{1,0:T(8,128)(2,1)S(1)}, u32[]{:S(2)}, u32[]{:S(2)}) collective-permute-start(bf16[688,128]{1,0:T(8,128)(2,1)S(1)} %collective-permute-done.20.refs_2_), channel_id=1, source_target_pairs={{0,1},{1,0},{2,3},{3,2},{4,5},{5,4},{6,7},{7,6},{8,9},{9,8},{10,11... | collective-permute-start | bytes 528392 | tf_op jit(solution)/shard_map/ppermute | solution.py:215
  63.6 1.4 %collective-permute-start.25 = (bf16[688,128]{1,0:T(8,128)(2,1)S(1)}, bf16[688,128]{1,0:T(8,128)(2,1)S(1)}, u32[]{:S(2)}, u32[]{:S(2)}) collective-permute-start(bf16[688,128]{1,0:T(8,128)(2,1)S(1)} %collective-permute-done.24.refs_6_), channel_id=1, source_target_pairs={{0,1},{1,0},{2,3},{3,2},{4,5},{5,4},{6,7},{7,6},{8,9},{9,8},{10,11... | collective-permute-start | bytes 528392 | tf_op jit(solution)/shard_map/ppermute | solution.py:215

commit v12 on v11

--- a/solution.py
+++ b/solution.py
@@ -194,21 +194,46 @@
     return place
 
 
+def cut_kernel(keep, other, *rest):
+    downs, (own, *outs, pieces) = rest[: -len(rest) // 2], rest[-len(rest) // 2 :]
+    me = lax.axis_index("gz") // 2
+    rows = own.shape[0]
+    down = sum(ref[...].astype(F32) for ref in downs)
+    values = (keep[...] + other[...].astype(F32), down)
+    first = 0
+    for value in values:
+        for row, owner, inner, take in segments(value.shape[0], rows, value.shape[0], first):
+            pieces[owner, pl.ds(inner, take)] = value[row : row + take]
+        first += value.shape[0]
+    blank = pieces.shape[0] * rows - first
+    for row, owner, inner, take in segments(blank, rows, rows, first):
+        pieces[owner, pl.ds(inner, take)] = jnp.zeros((take, own.shape[1]), F32)
+    own[...] = pieces[me]
+    for code, out in enumerate(outs):
+        out[...] = pieces[jnp.bitwise_xor(me, code + 1)].astype(BF16)
+
+
 def place_kernel(n_gy, *refs):
     blocks, (conv, down) = refs[: 2 * n_gy], refs[2 * n_gy :]
     me = lax.axis_index("gy")
+    line = lax.axis_index("gz") // 2
     parity = lax.axis_index("gz") % 2
     half, channels = conv.shape[3:]
     count, deep_channels = down.shape[2:]
+    parts, rows = blocks[0].shape[:2]
+    places = [jnp.bitwise_xor(line, owner) if parts > 1 else 0 for owner in range(parts)]
     for index, block in enumerate(blocks):
         side = jnp.bitwise_xor(parity, index // n_gy)
         column = jnp.bitwise_xor(me, index % n_gy)
         for k in range(27):
-            conv[k, column, side] = block[pl.ds(k * half, half)]
+            for row, owner, inner, take in segments(half, rows, half, k * half):
+                conv[k, column, side, pl.ds(row, take)] = block[places[owner], pl.ds(inner, take)]
         for wide in range(deep_channels // channels):
-            down[side, column, :, pl.ds(wide * channels, channels)] = block[
-                pl.ds(27 * half + wide * count, count)
-            ]
+            first = 27 * half + wide * count
+            for row, owner, inner, take in segments(count, rows, count, first):
+                down[side, column, pl.ds(row, take), pl.ds(wide * channels, channels)] = block[
+                    places[owner], pl.ds(inner, take)
+                ]
 
 
 def swapped(value, axis, code):
@@ -273,7 +298,6 @@
     )
     level_t = [swapped(value, "gy", code) if code else value for code, value in enumerate(level_t)]
     level_t = jnp.stack(level_t)
-    even, odd = neighbours(level_t)
     *deep_t, level_t = lax.optimization_barrier((*deep_t, level_t))
     down_slice = lax.dynamic_index_in_dim(down_weight, parity, 0, keepdims=False)
     grad, down, *others = call(
@@ -289,10 +313,11 @@
             pltpu.VMEM((n_gy, 4 * channels // n_gy, deep_channels), F32),
         ],
     )
+    grad, level_t = lax.optimization_barrier((grad, level_t))
+    even, odd = neighbours(level_t)
     shared = [swapped(grad, "gy", code) if code else grad for code in range(n_gy)]
     even, odd, *others = lax.optimization_barrier((even, odd, *others))
-    for code, value in enumerate(others):
-        down = down + swapped(value, "gy", code + 1).astype(F32)
+    downs = [down] + [swapped(value, "gy", code + 1) for code, value in enumerate(others)]
     keep, send, near = call(
         lambda *refs: weight_kernel(n_gy, (rows, cols, channels), *refs),
         (
@@ -311,34 +336,55 @@
         ],
     )
     near_even, near_odd = neighbours(near)
-    conv = (keep + swapped(send, "gz", 1).astype(F32)).astype(wire)
-    total = jnp.concatenate([conv, down.astype(wire)], axis=0)
-    total = lax.optimization_barrier(total)
-    code = n_gz // 2
-    while code > 1:
-        other = swapped(total, "gz", code)
-        if code == 4:
-            other, near_even, near_odd = lax.optimization_barrier((other, near_even, near_odd))
-        if code == 2:
-            input_grad = call(
-                input_kernel,
-                shape((rows, cols, channels), BF16),
-                near_even,
-                near,
-                near_odd,
-                conv_weight,
-            )
-            other, input_grad = lax.optimization_barrier((other, input_grad))
-        total = total.astype(F32) + other.astype(F32)
-        if code > 2:
-            total = lax.optimization_barrier(total.astype(wire))
-        code //= 2
+    send = swapped(send, "gz", 1)
+
+    def input_part(near_even, near_odd):
+        return call(
+            input_kernel,
+            shape((rows, cols, channels), BF16),
+            near_even,
+            near,
+            near_odd,
+            conv_weight,
+        )
+
     cell_total = devices * cells
-    row = lax.broadcasted_iota(jnp.int32, total.shape, 0)
+    n_z = n_gz // 2
+    total_rows = 27 * half + down_count
+    piece = -(-total_rows // (16 * n_z)) * 16
+    if n_z <= 4:
+        own, *pieces = call(
+            cut_kernel,
+            [shape((piece, channels), F32)] + [shape((piece, channels), BF16)] * (n_z - 1),
+            keep,
+            send,
+            *downs,
+            scratch=[pltpu.VMEM((n_z, piece, channels), F32)],
+        )
+        pieces = [swapped(value, "gz", 2 * code + 2) for code, value in enumerate(pieces)]
+        *pieces, near_even, near_odd = lax.optimization_barrier((*pieces, near_even, near_odd))
+        total = own + sum(value.astype(F32) for value in pieces)
+        first = lax.axis_index("gz") // 2 * piece
+    else:
+        down = sum(value.astype(F32) for value in downs)
+        total = jnp.concatenate([keep + send.astype(F32), down], axis=0)
+        code = n_gz // 2
+        while code > 1:
+            total = total + swapped(total, "gz", code)
+            code //= 2
+        first = 0
+    row = first + lax.broadcasted_iota(jnp.int32, total.shape, 0)
     scale = jnp.where(
         row < 27 * half, 1 / math.sqrt(cell_total), 1 / math.sqrt(cell_total // 8)
     )
     total = (total * scale).astype(BF16)
+    input_grad = input_part(near_even, near_odd)
+    if n_z <= 4:
+        pieces = [swapped(total, "gz", 2 * code) if code else total for code in range(n_z)]
+        *pieces, input_grad = lax.optimization_barrier((*pieces, input_grad))
+        total = jnp.stack(pieces)
+    else:
+        total = total[None]
     pair = [total, swapped(total, "gz", 1)]
     blocks = []
     for index, block in enumerate(pair):

time: 66.5 us -> 70.6 us (1.062)
  waiting for transfers between devices: 26.5 us -> 29.9 us
  starting transfers between devices: 32.3 us -> 33.1 us
    ppermute x24 -> x28, waiting for transfers between devices: 26.5 us -> 29.9 us  [swapped(): lax.ppermute(value, axis, [(i, i ^ code) for i in range(lax.axis_size(axi...]
    ppermute x24 -> x28, starting transfers between devices: 30.8 us -> 31.8 us  [swapped(): lax.ppermute(value, axis, [(i, i ^ code) for i in range(lax.axis_size(axi...]
    pallas_call x6 -> x7, Pallas kernels: 5.36 us -> 5.43 us  [call(): pl.pallas_call(kernel, out_shape=out_shape, scratch_shapes=list(scratch),...]
  transfers between devices with their start and end apart: 26 -> 30, of which waited for: 12 -> 12; matrix products, arithmetic and copies ran while one was open for 0% -> 0% of each run, Pallas kernels for 6% -> 5%
where the time goes in v12:
time: 70.6 us; the launch traced here: 70.4 us
  starting transfers between devices  33.1 us (47%)
  waiting for transfers between devices  29.9 us (42%)
  Pallas kernels  5.43 us (8%)
  local copies, waits for them, and re-layouts  1 us (1%)
  between operations  0.81 us (1%)
    ppermute x28, starting transfers between devices, swapped(): lax.ppermute(value, axis, [(i, i ^ code) for i in range(lax.axis_size(axi...  31.8 us
    ppermute x28, waiting for transfers between devices, swapped(): lax.ppermute(value, axis, [(i, i ^ code) for i in range(lax.axis_size(axi...  29.9 us
    pallas_call x7, Pallas kernels, call(): pl.pallas_call(kernel, out_shape=out_shape, scratch_shapes=list(scratch),...  5.43 us
  transfers between devices with their start and end apart: 30, of which 12 were waited for; matrix products, arithmetic and copies ran while one was open for 0% of the time, Pallas kernels for 5%

profile of v12, /device:TPU:0, one launch (start us, length us, event | category | flops | bytes accessed | tf_op | source)
XLA Modules:
  0.0 70.4 jit_solution(16941242899919253056)
XLA Ops:
  0.6 0.0 copy-start
  0.7 1.0 %copy-done.2 = bf16[4,4,32,32]{3,2,1,0:T(8,128)(2,1)S(1)} copy-done((bf16[4,4,32,32]{3,2,1,0:T(8,128)(2,1)S(1)}, bf16[4,4,32,32]{3,2,1,0:T(8,128)(2,1)}, u32[]{:S(2)}) %copy-start.2) | copy-done | bytes 32792
  1.6 0.1 shard_map.85
  1.7 4.1 %collective-permute-start = (bf16[2,32,128]{2,1,0:T(8,128)(2,1)S(1)}, bf16[2,32,128]{2,1,0:T(8,128)(2,1)S(1)}, u32[]{:S(2)}, u32[]{:S(2)}) collective-permute-start(bf16[2,32,128]{2,1,0:T(8,128)(2,1)S(1)} %get-tuple-element.44), channel_id=1, source_target_pairs={{0,16},{4,20},{8,24},{12,28},{16,0},{20,4},{24,8},{28,12},{1,17},{... | collective-permute-start | bytes 49160 | tf_op jit(solution)/shard_map/ppermute | solution.py:240
  5.8 0.1 shard_map.86
  5.9 0.1 collective-permute-start.3
  6.0 1.6 %collective-permute-start.4 = (bf16[32,512]{1,0:T(8,128)(2,1)S(1)}, bf16[32,512]{1,0:T(8,128)(2,1)S(1)}, u32[]{:S(2)}, u32[]{:S(2)}) collective-permute-start(bf16[32,512]{1,0:T(8,128)(2,1)S(1)} %get-tuple-element.47), channel_id=1, source_target_pairs={{0,2},{1,3},{2,0},{3,1},{4,6},{5,7},{6,4},{7,5},{8,10},{9,11},{10,... | collective-permute-start | bytes 98312 | tf_op jit(solution)/shard_map/ppermute | solution.py:240
  7.6 0.3 collective-permute-start.5
  7.9 0.0 collective-permute-done
  7.9 1.6 %collective-permute-start.1 = (bf16[1,2,32,128]{3,2,1,0:T(8,128)(2,1)S(1)}, bf16[1,2,32,128]{3,2,1,0:T(8,128)(2,1)S(1)}, u32[]{:S(2)}, u32[]{:S(2)}) collective-permute-start(bf16[1,2,32,128]{3,2,1,0:T(8,128)(2,1)S(1)} %get-tuple-element.84), channel_id=1, source_target_pairs={{0,8},{4,12},{8,0},{12,4},{16,24},{20,28},{24,16},{28,20},{1,9},{5... | collective-permute-start | bytes 49160 | tf_op jit(solution)/shard_map/ppermute | solution.py:240
  9.5 2.1 %collective-permute-done.1 = bf16[1,2,32,128]{3,2,1,0:T(8,128)(2,1)S(1)} collective-permute-done((bf16[1,2,32,128]{3,2,1,0:T(8,128)(2,1)S(1)}, bf16[1,2,32,128]{3,2,1,0:T(8,128)(2,1)S(1)}, u32[]{:S(2)}, u32[]{:S(2)}) %collective-permute-start.1) | collective-permute-done | bytes 16416 | tf_op jit(solution)/shard_map/ppermute | solution.py:240
  11.7 1.5 %collective-permute-start.2 = (bf16[4,32,128]{2,1,0:T(8,128)(2,1)S(1)}, bf16[4,32,128]{2,1,0:T(8,128)(2,1)S(1)}, u32[]{:S(2)}, u32[]{:S(2)}) collective-permute-start(bf16[4,32,128]{2,1,0:T(8,128)(2,1)S(1)} %maximum_bitcast_fusion.refs_3_), channel_id=1, source_target_pairs={{0,4},{4,0},{8,12},{12,8},{16,20},{20,16},{24,28},{28,24},{1,5},{5... | collective-permute-start | bytes 98312 | tf_op jit(solution)/shard_map/ppermute | solution.py:240
  13.2 0.0 collective-permute-done.3
  13.2 0.0 collective-permute-done.4
  13.2 0.0 collective-permute-done.5
  13.2 0.0 copy-start.4
  13.2 0.0 copy-start.5
  13.3 2.3 %collective-permute-done.2.refs_4_ = bf16[4,32,128]{2,1,0:T(8,128)(2,1)S(1)} collective-permute-done((bf16[4,32,128]{2,1,0:T(8,128)(2,1)S(1)}, bf16[4,32,128]{2,1,0:T(8,128)(2,1)S(1)}, u32[]{:S(2)}, u32[]{:S(2)}) %collective-permute-start.2) | collective-permute-done | bytes 32800 | tf_op jit(solution)/shard_map/ppermute | solution.py:240
  15.6 0.6 shard_map.87
  16.2 0.7 collective-permute-start.7
  16.9 4.3 %collective-permute-start.6 = (bf16[4,32,512]{2,1,0:T(8,128)(2,1)S(1)}, bf16[4,32,512]{2,1,0:T(8,128)(2,1)S(1)}, u32[]{:S(2)}, u32[]{:S(2)}) collective-permute-start(bf16[4,32,512]{2,1,0:T(8,128)(2,1)S(1)} %pad_maximum_fusion.1.refs_1_), channel_id=1, source_target_pairs={{0,4},{4,0},{8,12},{12,8},{16,20},{20,16},{24,28},{28,24},{1,5},{5... | collective-permute-start | bytes 393224 | tf_op jit(solution)/shard_map/ppermute | solution.py:240
  21.2 0.0 collective-permute-start.10
  21.2 1.5 %collective-permute-start.9 = (bf16[512,128]{1,0:T(8,128)(2,1)S(1)}, bf16[512,128]{1,0:T(8,128)(2,1)S(1)}, u32[]{:S(2)}, u32[]{:S(2)}) collective-permute-start(bf16[512,128]{1,0:T(8,128)(2,1)S(1)} %get-tuple-element.59.refs_3_), channel_id=1, source_target_pairs={{0,2},{1,3},{2,0},{3,1},{4,6},{5,7},{6,4},{7,5},{8,10},{9,11},{10,... | collective-permute-start | bytes 393224 | tf_op jit(solution)/shard_map/ppermute | solution.py:240
  22.8 0.3 collective-permute-start.8
  23.1 0.0 collective-permute-done.7.refs_2_
  23.1 1.3 %collective-permute-done.6.refs_0_ = bf16[4,32,512]{2,1,0:T(8,128)(2,1)S(1)} collective-permute-done((bf16[4,32,512]{2,1,0:T(8,128)(2,1)S(1)}, bf16[4,32,512]{2,1,0:T(8,128)(2,1)S(1)}, u32[]{:S(2)}, u32[]{:S(2)}) %collective-permute-start.6) | collective-permute-done | bytes 131104 | tf_op jit(solution)/shard_map/ppermute | solution.py:240
  24.5 0.0 collective-permute-start.12
  24.5 2.5 %collective-permute-done.10.refs_6_ = bf16[512,128]{1,0:T(8,128)(2,1)S(1)} collective-permute-done((bf16[512,128]{1,0:T(8,128)(2,1)S(1)}, bf16[512,128]{1,0:T(8,128)(2,1)S(1)}, u32[]{:S(2)}, u32[]{:S(2)}) %collective-permute-start.10) | collective-permute-done | bytes 131104 | tf_op jit(solution)/shard_map/ppermute | solution.py:240
  27.0 2.9 %collective-permute-done.9.refs_5_ = bf16[512,128]{1,0:T(8,128)(2,1)S(1)} collective-permute-done((bf16[512,128]{1,0:T(8,128)(2,1)S(1)}, bf16[512,128]{1,0:T(8,128)(2,1)S(1)}, u32[]{:S(2)}, u32[]{:S(2)}) %collective-permute-start.9) | collective-permute-done | bytes 131104 | tf_op jit(solution)/shard_map/ppermute | solution.py:240
  29.9 0.0 collective-permute-done.8.refs_4_
  29.9 1.5 %shard_map.88 = (f32[432,128]{1,0:T(8,128)S(1)}, bf16[432,128]{1,0:T(8,128)(2,1)S(1)}, bf16[10,64,128]{2,1,0:T(8,128)(2,1)S(1)}) custom-call(bf16[4,32,512]{2,1,0:T(8,128)(2,1)S(1)} %collective-permute-done.6.refs_0_, bf16[4,32,512]{2,1,0:T(8,128)(2,1)S(1)} %pad_maximum_fusion.1.refs_1_, bf16[4,32,512]{2,1,0:T(8,128)(2,1)S(1)} %collective-permute-done.7.refs_2_, ...), custom_call_target="tpu_custom_call" | custom-call | tf_op jit(solution)/shard_map/pallas_call | solution.py:16
  31.4 0.1 collective-permute-start.11
  31.5 0.0 collective-permute-start.13
  31.5 1.4 %collective-permute-start.14 = (bf16[256,128]{1,0:T(8,128)(2,1)S(1)}, bf16[256,128]{1,0:T(8,128)(2,1)S(1)}, u32[]{:S(2)}, u32[]{:S(2)}) collective-permute-start(bf16[256,128]{1,0:T(8,128)(2,1)S(1)} %get-tuple-element.65), channel_id=1, source_target_pairs={{0,3},{1,2},{2,1},{3,0},{4,7},{5,6},{6,5},{7,4},{8,11},{9,10},{10,... | collective-permute-start | bytes 196616 | tf_op jit(solution)/shard_map/ppermute | solution.py:240
  32.9 0.7 collective-permute-start.19
  33.6 4.4 %collective-permute-start.18 = (bf16[10,64,128]{2,1,0:T(8,128)(2,1)S(1)}, bf16[10,64,128]{2,1,0:T(8,128)(2,1)S(1)}, u32[]{:S(2)}, u32[]{:S(2)}) collective-permute-start(bf16[10,64,128]{2,1,0:T(8,128)(2,1)S(1)} %get-tuple-element.70.own), channel_id=1, source_target_pairs={{0,4},{4,0},{8,12},{12,8},{16,20},{20,16},{24,28},{28,24},{1,5},{5... | collective-permute-start | bytes 491528 | tf_op jit(solution)/shard_map/ppermute | solution.py:240
  38.0 0.0 collective-permute-done.13.rest_2_
  38.0 0.1 shard_map.89
  38.1 1.6 %collective-permute-start.15 = (bf16[176,128]{1,0:T(8,128)(2,1)S(1)}, bf16[176,128]{1,0:T(8,128)(2,1)S(1)}, u32[]{:S(2)}, u32[]{:S(2)}) collective-permute-start(bf16[176,128]{1,0:T(8,128)(2,1)S(1)} %get-tuple-element.67), channel_id=1, source_target_pairs={{0,8},{4,12},{8,0},{12,4},{16,24},{20,28},{24,16},{28,20},{1,9},{5... | collective-permute-start | bytes 135176 | tf_op jit(solution)/shard_map/ppermute | solution.py:240
  39.7 1.1 %collective-permute-start.16 = (bf16[176,128]{1,0:T(8,128)(2,1)S(1)}, bf16[176,128]{1,0:T(8,128)(2,1)S(1)}, u32[]{:S(2)}, u32[]{:S(2)}) collective-permute-start(bf16[176,128]{1,0:T(8,128)(2,1)S(1)} %get-tuple-element.68), channel_id=1, source_target_pairs={{0,16},{4,20},{8,24},{12,28},{16,0},{20,4},{24,8},{28,12},{1,17},{... | collective-permute-start | bytes 135176 | tf_op jit(solution)/shard_map/ppermute | solution.py:240
  40.8 1.7 %collective-permute-start.17 = (bf16[176,128]{1,0:T(8,128)(2,1)S(1)}, bf16[176,128]{1,0:T(8,128)(2,1)S(1)}, u32[]{:S(2)}, u32[]{:S(2)}) collective-permute-start(bf16[176,128]{1,0:T(8,128)(2,1)S(1)} %get-tuple-element.69), channel_id=1, source_target_pairs={{0,24},{4,28},{8,16},{12,20},{16,8},{20,12},{24,0},{28,4},{1,25},{... | collective-permute-start | bytes 135176 | tf_op jit(solution)/shard_map/ppermute | solution.py:240
  42.5 1.4 %collective-permute-done.15 = bf16[176,128]{1,0:T(8,128)(2,1)S(1)} collective-permute-done((bf16[176,128]{1,0:T(8,128)(2,1)S(1)}, bf16[176,128]{1,0:T(8,128)(2,1)S(1)}, u32[]{:S(2)}, u32[]{:S(2)}) %collective-permute-start.15) | collective-permute-done | bytes 45088 | tf_op jit(solution)/shard_map/ppermute | solution.py:240
  44.0 1.3 %collective-permute-done.16 = bf16[176,128]{1,0:T(8,128)(2,1)S(1)} collective-permute-done((bf16[176,128]{1,0:T(8,128)(2,1)S(1)}, bf16[176,128]{1,0:T(8,128)(2,1)S(1)}, u32[]{:S(2)}, u32[]{:S(2)}) %collective-permute-start.16) | collective-permute-done | bytes 45088 | tf_op jit(solution)/shard_map/ppermute | solution.py:240
  45.2 2.8 %collective-permute-done.17 = bf16[176,128]{1,0:T(8,128)(2,1)S(1)} collective-permute-done((bf16[176,128]{1,0:T(8,128)(2,1)S(1)}, bf16[176,128]{1,0:T(8,128)(2,1)S(1)}, u32[]{:S(2)}, u32[]{:S(2)}) %collective-permute-start.17) | collective-permute-done | bytes 45088 | tf_op jit(solution)/shard_map/ppermute | solution.py:240
  48.0 0.0 collective-permute-done.19.odd
  48.0 0.1 multiply_convert_fusion
  48.1 1.9 %collective-permute-start.22 = (bf16[176,128]{1,0:T(8,128)(2,1)S(1)}, bf16[176,128]{1,0:T(8,128)(2,1)S(1)}, u32[]{:S(2)}, u32[]{:S(2)}) collective-permute-start(bf16[176,128]{1,0:T(8,128)(2,1)S(1)} %multiply_convert_fusion), channel_id=1, source_target_pairs={{0,24},{4,28},{8,16},{12,20},{16,8},{20,12},{24,0},{28,4},{1,25},{... | collective-permute-start | bytes 135176 | tf_op jit(solution)/shard_map/ppermute | solution.py:240
  50.0 0.3 collective-permute-start.21
  50.3 2.2 %collective-permute-start.20 = (bf16[176,128]{1,0:T(8,128)(2,1)S(1)}, bf16[176,128]{1,0:T(8,128)(2,1)S(1)}, u32[]{:S(2)}, u32[]{:S(2)}) collective-permute-start(bf16[176,128]{1,0:T(8,128)(2,1)S(1)} %multiply_convert_fusion), channel_id=1, source_target_pairs={{0,8},{4,12},{8,0},{12,4},{16,24},{20,28},{24,16},{28,20},{1,9},{5... | collective-permute-start | bytes 135176 | tf_op jit(solution)/shard_map/ppermute | solution.py:240
  52.5 1.7 %shard_map.90 = bf16[8,64,128]{2,1,0:T(8,128)(2,1)} custom-call(bf16[10,64,128]{2,1,0:T(8,128)(2,1)S(1)} %collective-permute-done.18.even, bf16[10,64,128]{2,1,0:T(8,128)(2,1)S(1)} %get-tuple-element.70.own, bf16[10,64,128]{2,1,0:T(8,128)(2,1)S(1)} %collective-permute-done.19.odd, bf16[3,3,3,128,128]{4,3,2,1,0:T(8,128)(2,1)S(1)} %copy-done.1), custom_call_target="tpu_custom_call" | custom-call | tf_op jit(solution)/shard_map/pallas_call | solution.py:16
  54.3 0.0 collective-permute-done.22
  54.3 1.2 %collective-permute-done.21 = bf16[176,128]{1,0:T(8,128)(2,1)S(1)} collective-permute-done((bf16[176,128]{1,0:T(8,128)(2,1)S(1)}, bf16[176,128]{1,0:T(8,128)(2,1)S(1)}, u32[]{:S(2)}, u32[]{:S(2)}) %collective-permute-start.21) | collective-permute-done | bytes 45088 | tf_op jit(solution)/shard_map/ppermute | solution.py:240
  55.5 0.0 collective-permute-done.20
  55.5 0.6 collective-permute-start.26
  56.1 0.5 collective-permute-start.24
  56.6 5.5 %collective-permute-done.26.refs_4_ = bf16[4,176,128]{2,1,0:T(8,128)(2,1)S(1)} collective-permute-done((bf16[4,176,128]{2,1,0:T(8,128)(2,1)S(1)}, bf16[4,176,128]{2,1,0:T(8,128)(2,1)S(1)}, u32[]{:S(2)}, u32[]{:S(2)}) %collective-permute-start.26) | collective-permute-done | bytes 180256 | tf_op jit(solution)/shard_map/ppermute | solution.py:240
  62.1 0.0 collective-permute-start.28
  62.1 0.5 collective-permute-start.27
  62.6 0.0 collective-permute-start.25
  62.6 5.1 %collective-permute-done.28.refs_6_ = bf16[4,176,128]{2,1,0:T(8,128)(2,1)S(1)} collective-permute-done((bf16[4,176,128]{2,1,0:T(8,128)(2,1)S(1)}, bf16[4,176,128]{2,1,0:T(8,128)(2,1)S(1)}, u32[]{:S(2)}, u32[]{:S(2)}) %collective-permute-start.28) | collective-permute-done | bytes 180256 | tf_op jit(solution)/shard_map/ppermute | solution.py:240
  67.7 0.0 collective-permute-done.27.refs_5_
  67.7 0.0 collective-permute-done.25.refs_3_
  67.7 1.4 %collective-permute-done.29.refs_7_ = bf16[4,176,128]{2,1,0:T(8,128)(2,1)S(1)} collective-permute-done((bf16[4,176,128]{2,1,0:T(8,128)(2,1)S(1)}, bf16[4,176,128]{2,1,0:T(8,128)(2,1)S(1)}, u32[]{:S(2)}, u32[]{:S(2)}) %collective-permute-start.29) | collective-permute-done | bytes 180256 | tf_op jit(solution)/shard_map/ppermute | solution.py:240
  69.1 1.3 %shard_map.91 = (bf16[27,4,2,16,128]{4,3,2,1,0:T(8,128)(2,1)}, bf16[2,4,128,256]{3,2,1,0:T(8,128)(2,1)}) custom-call(bf16[4,176,128]{2,1,0:T(8,128)(2,1)S(1)} %pad_maximum_fusion.refs_0_, bf16[4,176,128]{2,1,0:T(8,128)(2,1)S(1)} %collective-permute-done.23.refs_1_, bf16[4,176,128]{2,1,0:T(8,128)(2,1)S(1)} %collective-permute-done.24.refs_2_, ...), custom_call_target="tpu_custom_call" | custom-call | tf_op jit(solution)/shard_map/pallas_call | solution.py:16
  (22 shorter events, 0.1 us)
Async XLA Ops:
  0.6 8.9 %copy-start = (bf16[2,2,2,128,256]{4,3,2,1,0:T(8,128)(2,1)S(1)}, bf16[2,2,2,128,256]{4,3,2,1,0:T(8,128)(2,1)}, u32[]{:S(2)}) copy-start(bf16[2,2,2,128,256]{4,3,2,1,0:T(8,128)(2,1)} %param.9) | copy-start | bytes 1572868
  0.6 1.0 %copy-start.2 = (bf16[4,4,32,32]{3,2,1,0:T(8,128)(2,1)S(1)}, bf16[4,4,32,32]{3,2,1,0:T(8,128)(2,1)}, u32[]{:S(2)}) copy-start(bf16[4,4,32,32]{3,2,1,0:T(8,128)(2,1)} %param.11) | copy-start | bytes 98308
  1.6 4.2 %copy-start.3 = (bf16[1,8,64,128]{3,2,1,0:T(8,128)(2,1)S(1)}, bf16[1,8,64,128]{3,2,1,0:T(8,128)(2,1)}, u32[]{:S(2)}) copy-start(bf16[1,8,64,128]{3,2,1,0:T(8,128)(2,1)} %param.6) | copy-start | bytes 393220
  1.7 6.2 %collective-permute-start = (bf16[2,32,128]{2,1,0:T(8,128)(2,1)S(1)}, bf16[2,32,128]{2,1,0:T(8,128)(2,1)S(1)}, u32[]{:S(2)}, u32[]{:S(2)}) collective-permute-start(bf16[2,32,128]{2,1,0:T(8,128)(2,1)S(1)} %get-tuple-element.44), channel_id=1, source_target_pairs={{0,16},{4,20},{8,24},{12,28},{16,0},{20,4},{24,8},{28,12},{1,17},{... | collective-permute-start | bytes 49160 | tf_op jit(solution)/shard_map/ppermute | solution.py:240
  5.9 7.3 %collective-permute-start.3 = (bf16[32,512]{1,0:T(8,128)(2,1)S(1)}, bf16[32,512]{1,0:T(8,128)(2,1)S(1)}, u32[]{:S(2)}, u32[]{:S(2)}) collective-permute-start(bf16[32,512]{1,0:T(8,128)(2,1)S(1)} %get-tuple-element.46), channel_id=1, source_target_pairs={{0,1},{1,0},{2,3},{3,2},{4,5},{5,4},{6,7},{7,6},{8,9},{9,8},{10,11... | collective-permute-start | bytes 98312 | tf_op jit(solution)/shard_map/ppermute | solution.py:240
  6.0 7.2 %collective-permute-start.4 = (bf16[32,512]{1,0:T(8,128)(2,1)S(1)}, bf16[32,512]{1,0:T(8,128)(2,1)S(1)}, u32[]{:S(2)}, u32[]{:S(2)}) collective-permute-start(bf16[32,512]{1,0:T(8,128)(2,1)S(1)} %get-tuple-element.47), channel_id=1, source_target_pairs={{0,2},{1,3},{2,0},{3,1},{4,6},{5,7},{6,4},{7,5},{8,10},{9,11},{10,... | collective-permute-start | bytes 98312 | tf_op jit(solution)/shard_map/ppermute | solution.py:240
  7.6 5.7 %collective-permute-start.5 = (bf16[32,512]{1,0:T(8,128)(2,1)S(1)}, bf16[32,512]{1,0:T(8,128)(2,1)S(1)}, u32[]{:S(2)}, u32[]{:S(2)}) collective-permute-start(bf16[32,512]{1,0:T(8,128)(2,1)S(1)} %get-tuple-element.48), channel_id=1, source_target_pairs={{0,3},{1,2},{2,1},{3,0},{4,7},{5,6},{6,5},{7,4},{8,11},{9,10},{10,... | collective-permute-start | bytes 98312 | tf_op jit(solution)/shard_map/ppermute | solution.py:240
  7.9 3.8 %collective-permute-start.1 = (bf16[1,2,32,128]{3,2,1,0:T(8,128)(2,1)S(1)}, bf16[1,2,32,128]{3,2,1,0:T(8,128)(2,1)S(1)}, u32[]{:S(2)}, u32[]{:S(2)}) collective-permute-start(bf16[1,2,32,128]{3,2,1,0:T(8,128)(2,1)S(1)} %get-tuple-element.84), channel_id=1, source_target_pairs={{0,8},{4,12},{8,0},{12,4},{16,24},{20,28},{24,16},{28,20},{1,9},{5... | collective-permute-start | bytes 49160 | tf_op jit(solution)/shard_map/ppermute | solution.py:240
  11.7 3.9 %collective-permute-start.2 = (bf16[4,32,128]{2,1,0:T(8,128)(2,1)S(1)}, bf16[4,32,128]{2,1,0:T(8,128)(2,1)S(1)}, u32[]{:S(2)}, u32[]{:S(2)}) collective-permute-start(bf16[4,32,128]{2,1,0:T(8,128)(2,1)S(1)} %maximum_bitcast_fusion.refs_3_), channel_id=1, source_target_pairs={{0,4},{4,0},{8,12},{12,8},{16,20},{20,16},{24,28},{28,24},{1,5},{5... | collective-permute-start | bytes 98312 | tf_op jit(solution)/shard_map/ppermute | solution.py:240
  13.2 2.4 %copy-start.4 = (bf16[1,8,64,128]{3,2,1,0:T(8,128)(2,1)S(1)}, bf16[1,8,64,128]{3,2,1,0:T(8,128)(2,1)}, u32[]{:S(2)}) copy-start(bf16[1,8,64,128]{3,2,1,0:T(8,128)(2,1)} %param.7) | copy-start | bytes 393220
  13.2 2.4 %copy-start.5 = (bf16[1,8,64,128]{3,2,1,0:T(8,128)(2,1)S(1)}, bf16[1,8,64,128]{3,2,1,0:T(8,128)(2,1)}, u32[]{:S(2)}) copy-start(bf16[1,8,64,128]{3,2,1,0:T(8,128)(2,1)} %param.10) | copy-start | bytes 393220
  16.2 6.9 %collective-permute-start.7 = (bf16[4,32,512]{2,1,0:T(8,128)(2,1)S(1)}, bf16[4,32,512]{2,1,0:T(8,128)(2,1)S(1)}, u32[]{:S(2)}, u32[]{:S(2)}) collective-permute-start(bf16[4,32,512]{2,1,0:T(8,128)(2,1)S(1)} %pad_maximum_fusion.1.refs_1_), channel_id=1, source_target_pairs={{4,8},{8,4},{12,16},{16,12},{20,24},{24,20},{5,9},{9,5},{13,17},{1... | collective-permute-start | bytes 393224 | tf_op jit(solution)/shard_map/ppermute | solution.py:246
  16.9 7.5 %collective-permute-start.6 = (bf16[4,32,512]{2,1,0:T(8,128)(2,1)S(1)}, bf16[4,32,512]{2,1,0:T(8,128)(2,1)S(1)}, u32[]{:S(2)}, u32[]{:S(2)}) collective-permute-start(bf16[4,32,512]{2,1,0:T(8,128)(2,1)S(1)} %pad_maximum_fusion.1.refs_1_), channel_id=1, source_target_pairs={{0,4},{4,0},{8,12},{12,8},{16,20},{20,16},{24,28},{28,24},{1,5},{5... | collective-permute-start | bytes 393224 | tf_op jit(solution)/shard_map/ppermute | solution.py:240
  21.2 5.7 %collective-permute-start.10 = (bf16[512,128]{1,0:T(8,128)(2,1)S(1)}, bf16[512,128]{1,0:T(8,128)(2,1)S(1)}, u32[]{:S(2)}, u32[]{:S(2)}) collective-permute-start(bf16[512,128]{1,0:T(8,128)(2,1)S(1)} %get-tuple-element.59.refs_3_), channel_id=1, source_target_pairs={{0,3},{1,2},{2,1},{3,0},{4,7},{5,6},{6,5},{7,4},{8,11},{9,10},{10,... | collective-permute-start | bytes 393224 | tf_op jit(solution)/shard_map/ppermute | solution.py:240
  21.2 8.6 %collective-permute-start.9 = (bf16[512,128]{1,0:T(8,128)(2,1)S(1)}, bf16[512,128]{1,0:T(8,128)(2,1)S(1)}, u32[]{:S(2)}, u32[]{:S(2)}) collective-permute-start(bf16[512,128]{1,0:T(8,128)(2,1)S(1)} %get-tuple-element.59.refs_3_), channel_id=1, source_target_pairs={{0,2},{1,3},{2,0},{3,1},{4,6},{5,7},{6,4},{7,5},{8,10},{9,11},{10,... | collective-permute-start | bytes 393224 | tf_op jit(solution)/shard_map/ppermute | solution.py:240
  22.8 7.1 %collective-permute-start.8 = (bf16[512,128]{1,0:T(8,128)(2,1)S(1)}, bf16[512,128]{1,0:T(8,128)(2,1)S(1)}, u32[]{:S(2)}, u32[]{:S(2)}) collective-permute-start(bf16[512,128]{1,0:T(8,128)(2,1)S(1)} %get-tuple-element.59.refs_3_), channel_id=1, source_target_pairs={{0,1},{1,0},{2,3},{3,2},{4,5},{5,4},{6,7},{7,6},{8,9},{9,8},{10,11... | collective-permute-start | bytes 393224 | tf_op jit(solution)/shard_map/ppermute | solution.py:240
  24.5 28.1 %copy-start.1 = (bf16[3,3,3,128,128]{4,3,2,1,0:T(8,128)(2,1)S(1)}, bf16[3,3,3,128,128]{4,3,2,1,0:T(8,128)(2,1)}, u32[]{:S(2)}) copy-start(bf16[3,3,3,128,128]{4,3,2,1,0:T(8,128)(2,1)} %weight.1) | copy-start | bytes 2654212
  24.5 9.1 %collective-permute-start.12 = (bf16[256,128]{1,0:T(8,128)(2,1)S(1)}, bf16[256,128]{1,0:T(8,128)(2,1)S(1)}, u32[]{:S(2)}, u32[]{:S(2)}) collective-permute-start(bf16[256,128]{1,0:T(8,128)(2,1)S(1)} %get-tuple-element.63), channel_id=1, source_target_pairs={{0,1},{1,0},{2,3},{3,2},{4,5},{5,4},{6,7},{7,6},{8,9},{9,8},{10,11... | collective-permute-start | bytes 196616 | tf_op jit(solution)/shard_map/ppermute | solution.py:240
  31.4 6.6 %collective-permute-start.11 = (bf16[432,128]{1,0:T(8,128)(2,1)S(1)}, bf16[432,128]{1,0:T(8,128)(2,1)S(1)}, u32[]{:S(2)}, u32[]{:S(2)}) collective-permute-start(bf16[432,128]{1,0:T(8,128)(2,1)S(1)} %get-tuple-element.61), channel_id=1, source_target_pairs={{0,4},{4,0},{8,12},{12,8},{16,20},{20,16},{24,28},{28,24},{1,5},{5... | collective-permute-start | bytes 331784 | tf_op jit(solution)/shard_map/ppermute | solution.py:240
  31.5 6.5 %collective-permute-start.13 = (bf16[256,128]{1,0:T(8,128)(2,1)S(1)}, bf16[256,128]{1,0:T(8,128)(2,1)S(1)}, u32[]{:S(2)}, u32[]{:S(2)}) collective-permute-start(bf16[256,128]{1,0:T(8,128)(2,1)S(1)} %get-tuple-element.64), channel_id=1, source_target_pairs={{0,2},{1,3},{2,0},{3,1},{4,6},{5,7},{6,4},{7,5},{8,10},{9,11},{10,... | collective-permute-start | bytes 196616 | tf_op jit(solution)/shard_map/ppermute | solution.py:240
  31.5 6.5 %collective-permute-start.14 = (bf16[256,128]{1,0:T(8,128)(2,1)S(1)}, bf16[256,128]{1,0:T(8,128)(2,1)S(1)}, u32[]{:S(2)}, u32[]{:S(2)}) collective-permute-start(bf16[256,128]{1,0:T(8,128)(2,1)S(1)} %get-tuple-element.65), channel_id=1, source_target_pairs={{0,3},{1,2},{2,1},{3,0},{4,7},{5,6},{6,5},{7,4},{8,11},{9,10},{10,... | collective-permute-start | bytes 196616 | tf_op jit(solution)/shard_map/ppermute | solution.py:240
  32.9 15.1 %collective-permute-start.19 = (bf16[10,64,128]{2,1,0:T(8,128)(2,1)S(1)}, bf16[10,64,128]{2,1,0:T(8,128)(2,1)S(1)}, u32[]{:S(2)}, u32[]{:S(2)}) collective-permute-start(bf16[10,64,128]{2,1,0:T(8,128)(2,1)S(1)} %get-tuple-element.70.own), channel_id=1, source_target_pairs={{4,8},{8,4},{12,16},{16,12},{20,24},{24,20},{5,9},{9,5},{13,17},{1... | collective-permute-start | bytes 491528 | tf_op jit(solution)/shard_map/ppermute | solution.py:246
  33.6 14.4 %collective-permute-start.18 = (bf16[10,64,128]{2,1,0:T(8,128)(2,1)S(1)}, bf16[10,64,128]{2,1,0:T(8,128)(2,1)S(1)}, u32[]{:S(2)}, u32[]{:S(2)}) collective-permute-start(bf16[10,64,128]{2,1,0:T(8,128)(2,1)S(1)} %get-tuple-element.70.own), channel_id=1, source_target_pairs={{0,4},{4,0},{8,12},{12,8},{16,20},{20,16},{24,28},{28,24},{1,5},{5... | collective-permute-start | bytes 491528 | tf_op jit(solution)/shard_map/ppermute | solution.py:240
  38.1 5.9 %collective-permute-start.15 = (bf16[176,128]{1,0:T(8,128)(2,1)S(1)}, bf16[176,128]{1,0:T(8,128)(2,1)S(1)}, u32[]{:S(2)}, u32[]{:S(2)}) collective-permute-start(bf16[176,128]{1,0:T(8,128)(2,1)S(1)} %get-tuple-element.67), channel_id=1, source_target_pairs={{0,8},{4,12},{8,0},{12,4},{16,24},{20,28},{24,16},{28,20},{1,9},{5... | collective-permute-start | bytes 135176 | tf_op jit(solution)/shard_map/ppermute | solution.py:240
  39.7 5.5 %collective-permute-start.16 = (bf16[176,128]{1,0:T(8,128)(2,1)S(1)}, bf16[176,128]{1,0:T(8,128)(2,1)S(1)}, u32[]{:S(2)}, u32[]{:S(2)}) collective-permute-start(bf16[176,128]{1,0:T(8,128)(2,1)S(1)} %get-tuple-element.68), channel_id=1, source_target_pairs={{0,16},{4,20},{8,24},{12,28},{16,0},{20,4},{24,8},{28,12},{1,17},{... | collective-permute-start | bytes 135176 | tf_op jit(solution)/shard_map/ppermute | solution.py:240
  40.8 7.2 %collective-permute-start.17 = (bf16[176,128]{1,0:T(8,128)(2,1)S(1)}, bf16[176,128]{1,0:T(8,128)(2,1)S(1)}, u32[]{:S(2)}, u32[]{:S(2)}) collective-permute-start(bf16[176,128]{1,0:T(8,128)(2,1)S(1)} %get-tuple-element.69), channel_id=1, source_target_pairs={{0,24},{4,28},{8,16},{12,20},{16,8},{20,12},{24,0},{28,4},{1,25},{... | collective-permute-start | bytes 135176 | tf_op jit(solution)/shard_map/ppermute | solution.py:240
  48.1 6.2 %collective-permute-start.22 = (bf16[176,128]{1,0:T(8,128)(2,1)S(1)}, bf16[176,128]{1,0:T(8,128)(2,1)S(1)}, u32[]{:S(2)}, u32[]{:S(2)}) collective-permute-start(bf16[176,128]{1,0:T(8,128)(2,1)S(1)} %multiply_convert_fusion), channel_id=1, source_target_pairs={{0,24},{4,28},{8,16},{12,20},{16,8},{20,12},{24,0},{28,4},{1,25},{... | collective-permute-start | bytes 135176 | tf_op jit(solution)/shard_map/ppermute | solution.py:240
  50.0 5.5 %collective-permute-start.21 = (bf16[176,128]{1,0:T(8,128)(2,1)S(1)}, bf16[176,128]{1,0:T(8,128)(2,1)S(1)}, u32[]{:S(2)}, u32[]{:S(2)}) collective-permute-start(bf16[176,128]{1,0:T(8,128)(2,1)S(1)} %multiply_convert_fusion), channel_id=1, source_target_pairs={{0,16},{4,20},{8,24},{12,28},{16,0},{20,4},{24,8},{28,12},{1,17},{... | collective-permute-start | bytes 135176 | tf_op jit(solution)/shard_map/ppermute | solution.py:240
  50.3 5.2 %collective-permute-start.20 = (bf16[176,128]{1,0:T(8,128)(2,1)S(1)}, bf16[176,128]{1,0:T(8,128)(2,1)S(1)}, u32[]{:S(2)}, u32[]{:S(2)}) collective-permute-start(bf16[176,128]{1,0:T(8,128)(2,1)S(1)} %multiply_convert_fusion), channel_id=1, source_target_pairs={{0,8},{4,12},{8,0},{12,4},{16,24},{20,28},{24,16},{28,20},{1,9},{5... | collective-permute-start | bytes 135176 | tf_op jit(solution)/shard_map/ppermute | solution.py:240
  55.5 6.5 %collective-permute-start.26 = (bf16[4,176,128]{2,1,0:T(8,128)(2,1)S(1)}, bf16[4,176,128]{2,1,0:T(8,128)(2,1)S(1)}, u32[]{:S(2)}, u32[]{:S(2)}) collective-permute-start(bf16[4,176,128]{2,1,0:T(8,128)(2,1)S(1)} %pad_maximum_fusion.refs_0_), channel_id=1, source_target_pairs={{0,4},{4,0},{8,12},{12,8},{16,20},{20,16},{24,28},{28,24},{1,5},{5... | collective-permute-start | bytes 540680 | tf_op jit(solution)/shard_map/ppermute | solution.py:240
  56.1 6.5 %collective-permute-start.24 = (bf16[4,176,128]{2,1,0:T(8,128)(2,1)S(1)}, bf16[4,176,128]{2,1,0:T(8,128)(2,1)S(1)}, u32[]{:S(2)}, u32[]{:S(2)}) collective-permute-start(bf16[4,176,128]{2,1,0:T(8,128)(2,1)S(1)} %pad_maximum_fusion.refs_0_), channel_id=1, source_target_pairs={{0,2},{1,3},{2,0},{3,1},{4,6},{5,7},{6,4},{7,5},{8,10},{9,11},{10,... | collective-permute-start | bytes 540680 | tf_op jit(solution)/shard_map/ppermute | solution.py:240
  62.1 5.6 %collective-permute-start.28 = (bf16[4,176,128]{2,1,0:T(8,128)(2,1)S(1)}, bf16[4,176,128]{2,1,0:T(8,128)(2,1)S(1)}, u32[]{:S(2)}, u32[]{:S(2)}) collective-permute-start(bf16[4,176,128]{2,1,0:T(8,128)(2,1)S(1)} %collective-permute-done.26.refs_4_), channel_id=1, source_target_pairs={{0,2},{1,3},{2,0},{3,1},{4,6},{5,7},{6,4},{7,5},{8,10},{9,11},{10,... | collective-permute-start | bytes 540680 | tf_op jit(solution)/shard_map/ppermute | solution.py:240
  62.1 5.6 %collective-permute-start.23 = (bf16[4,176,128]{2,1,0:T(8,128)(2,1)S(1)}, bf16[4,176,128]{2,1,0:T(8,128)(2,1)S(1)}, u32[]{:S(2)}, u32[]{:S(2)}) collective-permute-start(bf16[4,176,128]{2,1,0:T(8,128)(2,1)S(1)} %pad_maximum_fusion.refs_0_), channel_id=1, source_target_pairs={{0,1},{1,0},{2,3},{3,2},{4,5},{5,4},{6,7},{7,6},{8,9},{9,8},{10,11... | collective-permute-start | bytes 540680 | tf_op jit(solution)/shard_map/ppermute | solution.py:240
  62.1 5.6 %collective-permute-start.27 = (bf16[4,176,128]{2,1,0:T(8,128)(2,1)S(1)}, bf16[4,176,128]{2,1,0:T(8,128)(2,1)S(1)}, u32[]{:S(2)}, u32[]{:S(2)}) collective-permute-start(bf16[4,176,128]{2,1,0:T(8,128)(2,1)S(1)} %collective-permute-done.26.refs_4_), channel_id=1, source_target_pairs={{0,1},{1,0},{2,3},{3,2},{4,5},{5,4},{6,7},{7,6},{8,9},{9,8},{10,11... | collective-permute-start | bytes 540680 | tf_op jit(solution)/shard_map/ppermute | solution.py:240
  62.6 5.1 %collective-permute-start.25 = (bf16[4,176,128]{2,1,0:T(8,128)(2,1)S(1)}, bf16[4,176,128]{2,1,0:T(8,128)(2,1)S(1)}, u32[]{:S(2)}, u32[]{:S(2)}) collective-permute-start(bf16[4,176,128]{2,1,0:T(8,128)(2,1)S(1)} %collective-permute-done.24.refs_2_), channel_id=1, source_target_pairs={{0,1},{1,0},{2,3},{3,2},{4,5},{5,4},{6,7},{7,6},{8,9},{9,8},{10,11... | collective-permute-start | bytes 540680 | tf_op jit(solution)/shard_map/ppermute | solution.py:240
  67.7 1.4 %collective-permute-start.29 = (bf16[4,176,128]{2,1,0:T(8,128)(2,1)S(1)}, bf16[4,176,128]{2,1,0:T(8,128)(2,1)S(1)}, u32[]{:S(2)}, u32[]{:S(2)}) collective-permute-start(bf16[4,176,128]{2,1,0:T(8,128)(2,1)S(1)} %collective-permute-done.28.refs_6_), channel_id=1, source_target_pairs={{0,1},{1,0},{2,3},{3,2},{4,5},{5,4},{6,7},{7,6},{8,9},{9,8},{10,11... | collective-permute-start | bytes 540680 | tf_op jit(solution)/shard_map/ppermute | solution.py:240

commit v13 on v12

--- a/solution.py
+++ b/solution.py
@@ -313,11 +313,9 @@
             pltpu.VMEM((n_gy, 4 * channels // n_gy, deep_channels), F32),
         ],
     )
-    grad, level_t = lax.optimization_barrier((grad, level_t))
+    shared = [swapped(grad, "gy", code) if code else grad for code in range(n_gy)]
+    shared[1], level_t = lax.optimization_barrier((shared[1], level_t))
     even, odd = neighbours(level_t)
-    shared = [swapped(grad, "gy", code) if code else grad for code in range(n_gy)]
-    even, odd, *others = lax.optimization_barrier((even, odd, *others))
-    downs = [down] + [swapped(value, "gy", code + 1) for code, value in enumerate(others)]
     keep, send, near = call(
         lambda *refs: weight_kernel(n_gy, (rows, cols, channels), *refs),
         (
@@ -335,8 +333,10 @@
             pltpu.VMEM((2, 27 * half, channels), F32),
         ],
     )
+    send, *others = lax.optimization_barrier((send, *others))
+    downs = [down] + [swapped(value, "gy", code + 1) for code, value in enumerate(others)]
+    send, near = lax.optimization_barrier((swapped(send, "gz", 1), near))
     near_even, near_odd = neighbours(near)
-    send = swapped(send, "gz", 1)
 
     def input_part(near_even, near_odd):
         return call(

time: 70.6 us -> 70.8 us (level)
  starting transfers between devices: 33.1 us -> 39.6 us
  waiting for transfers between devices: 29.9 us -> 23.6 us
    ppermute x28, starting transfers between devices: 31.8 us -> 38.3 us  [swapped(): lax.ppermute(value, axis, [(i, i ^ code) for i in range(lax.axis_size(axi...]
    ppermute x28, waiting for transfers between devices: 29.9 us -> 23.5 us  [swapped(): lax.ppermute(value, axis, [(i, i ^ code) for i in range(lax.axis_size(axi...]
  transfers between devices with their start and end apart: 30 -> 30, of which waited for: 12 -> 12; matrix products, arithmetic and copies ran while one was open for 0% -> 0% of each run, Pallas kernels for 5% -> 3%
where the time goes in v13:
time: 70.8 us; the launch traced here: 70.6 us
  starting transfers between devices  39.6 us (56%)
  waiting for transfers between devices  23.6 us (33%)
  Pallas kernels  5.43 us (8%)
  local copies, waits for them, and re-layouts  1 us (1%)
  between operations  0.81 us (1%)
    ppermute x28, starting transfers between devices, swapped(): lax.ppermute(value, axis, [(i, i ^ code) for i in range(lax.axis_size(axi...  38.3 us
    ppermute x28, waiting for transfers between devices, swapped(): lax.ppermute(value, axis, [(i, i ^ code) for i in range(lax.axis_size(axi...  23.5 us
    pallas_call x7, Pallas kernels, call(): pl.pallas_call(kernel, out_shape=out_shape, scratch_shapes=list(scratch),...  5.43 us
  transfers between devices with their start and end apart: 30, of which 12 were waited for; matrix products, arithmetic and copies ran while one was open for 0% of the time, Pallas kernels for 3%

profile of v13, /device:TPU:0, one launch (start us, length us, event | category | flops | bytes accessed | tf_op | source)
XLA Modules:
  0.0 70.6 jit_solution(464628289498648058)
XLA Ops:
  0.6 0.0 copy-start
  0.7 1.0 %copy-done.2 = bf16[4,4,32,32]{3,2,1,0:T(8,128)(2,1)S(1)} copy-done((bf16[4,4,32,32]{3,2,1,0:T(8,128)(2,1)S(1)}, bf16[4,4,32,32]{3,2,1,0:T(8,128)(2,1)}, u32[]{:S(2)}) %copy-start.2) | copy-done | bytes 32792
  1.6 0.1 shard_map.85
  1.7 4.1 %collective-permute-start = (bf16[2,32,128]{2,1,0:T(8,128)(2,1)S(1)}, bf16[2,32,128]{2,1,0:T(8,128)(2,1)S(1)}, u32[]{:S(2)}, u32[]{:S(2)}) collective-permute-start(bf16[2,32,128]{2,1,0:T(8,128)(2,1)S(1)} %get-tuple-element.45), channel_id=1, source_target_pairs={{0,16},{4,20},{8,24},{12,28},{16,0},{20,4},{24,8},{28,12},{1,17},{... | collective-permute-start | bytes 49160 | tf_op jit(solution)/shard_map/ppermute | solution.py:240
  5.8 0.1 shard_map.86
  5.9 0.1 collective-permute-start.3
  6.0 1.6 %collective-permute-start.4 = (bf16[32,512]{1,0:T(8,128)(2,1)S(1)}, bf16[32,512]{1,0:T(8,128)(2,1)S(1)}, u32[]{:S(2)}, u32[]{:S(2)}) collective-permute-start(bf16[32,512]{1,0:T(8,128)(2,1)S(1)} %get-tuple-element.48), channel_id=1, source_target_pairs={{0,2},{1,3},{2,0},{3,1},{4,6},{5,7},{6,4},{7,5},{8,10},{9,11},{10,... | collective-permute-start | bytes 98312 | tf_op jit(solution)/shard_map/ppermute | solution.py:240
  7.6 0.3 collective-permute-start.5
  7.9 1.6 %collective-permute-start.1 = (bf16[1,2,32,128]{3,2,1,0:T(8,128)(2,1)S(1)}, bf16[1,2,32,128]{3,2,1,0:T(8,128)(2,1)S(1)}, u32[]{:S(2)}, u32[]{:S(2)}) collective-permute-start(bf16[1,2,32,128]{3,2,1,0:T(8,128)(2,1)S(1)} %get-tuple-element.86), channel_id=1, source_target_pairs={{0,8},{4,12},{8,0},{12,4},{16,24},{20,28},{24,16},{28,20},{1,9},{5... | collective-permute-start | bytes 49160 | tf_op jit(solution)/shard_map/ppermute | solution.py:240
  9.5 2.1 %collective-permute-done.1 = bf16[1,2,32,128]{3,2,1,0:T(8,128)(2,1)S(1)} collective-permute-done((bf16[1,2,32,128]{3,2,1,0:T(8,128)(2,1)S(1)}, bf16[1,2,32,128]{3,2,1,0:T(8,128)(2,1)S(1)}, u32[]{:S(2)}, u32[]{:S(2)}) %collective-permute-start.1) | collective-permute-done | bytes 16416 | tf_op jit(solution)/shard_map/ppermute | solution.py:240
  11.7 1.5 %collective-permute-start.2 = (bf16[4,32,128]{2,1,0:T(8,128)(2,1)S(1)}, bf16[4,32,128]{2,1,0:T(8,128)(2,1)S(1)}, u32[]{:S(2)}, u32[]{:S(2)}) collective-permute-start(bf16[4,32,128]{2,1,0:T(8,128)(2,1)S(1)} %maximum_bitcast_fusion.refs_3_), channel_id=1, source_target_pairs={{0,4},{4,0},{8,12},{12,8},{16,20},{20,16},{24,28},{28,24},{1,5},{5... | collective-permute-start | bytes 98312 | tf_op jit(solution)/shard_map/ppermute | solution.py:240
  13.2 0.0 collective-permute-done.4
  13.2 0.0 collective-permute-done.5
  13.2 0.0 copy-start.4
  13.2 0.0 copy-start.5
  13.3 2.3 %collective-permute-done.2.refs_4_ = bf16[4,32,128]{2,1,0:T(8,128)(2,1)S(1)} collective-permute-done((bf16[4,32,128]{2,1,0:T(8,128)(2,1)S(1)}, bf16[4,32,128]{2,1,0:T(8,128)(2,1)S(1)}, u32[]{:S(2)}, u32[]{:S(2)}) %collective-permute-start.2) | collective-permute-done | bytes 32800 | tf_op jit(solution)/shard_map/ppermute | solution.py:240
  15.6 0.6 shard_map.87
  16.2 0.0 copy-start.1
  16.2 0.1 collective-permute-start.6
  16.3 1.6 %collective-permute-start.10 = (bf16[512,128]{1,0:T(8,128)(2,1)S(1)}, bf16[512,128]{1,0:T(8,128)(2,1)S(1)}, u32[]{:S(2)}, u32[]{:S(2)}) collective-permute-start(bf16[512,128]{1,0:T(8,128)(2,1)S(1)} %get-tuple-element.52.refs_3_), channel_id=1, source_target_pairs={{0,3},{1,2},{2,1},{3,0},{4,7},{5,6},{6,5},{7,4},{8,11},{9,10},{10,... | collective-permute-start | bytes 393224 | tf_op jit(solution)/shard_map/ppermute | solution.py:240
  17.9 0.5 collective-permute-start.9
  18.5 0.7 collective-permute-start.8
  19.1 4.3 %collective-permute-start.7 = (bf16[4,32,512]{2,1,0:T(8,128)(2,1)S(1)}, bf16[4,32,512]{2,1,0:T(8,128)(2,1)S(1)}, u32[]{:S(2)}, u32[]{:S(2)}) collective-permute-start(bf16[4,32,512]{2,1,0:T(8,128)(2,1)S(1)} %pad_maximum_fusion.1.refs_1_), channel_id=1, source_target_pairs={{0,4},{4,0},{8,12},{12,8},{16,20},{20,16},{24,28},{28,24},{1,5},{5... | collective-permute-start | bytes 393224 | tf_op jit(solution)/shard_map/ppermute | solution.py:240
  23.5 1.5 %collective-permute-done.9.refs_5_ = bf16[512,128]{1,0:T(8,128)(2,1)S(1)} collective-permute-done((bf16[512,128]{1,0:T(8,128)(2,1)S(1)}, bf16[512,128]{1,0:T(8,128)(2,1)S(1)}, u32[]{:S(2)}, u32[]{:S(2)}) %collective-permute-start.9) | collective-permute-done | bytes 131104 | tf_op jit(solution)/shard_map/ppermute | solution.py:240
  25.0 0.0 collective-permute-done.8.refs_2_
  25.0 3.3 %collective-permute-done.7.refs_0_ = bf16[4,32,512]{2,1,0:T(8,128)(2,1)S(1)} collective-permute-done((bf16[4,32,512]{2,1,0:T(8,128)(2,1)S(1)}, bf16[4,32,512]{2,1,0:T(8,128)(2,1)S(1)}, u32[]{:S(2)}, u32[]{:S(2)}) %collective-permute-start.7) | collective-permute-done | bytes 131104 | tf_op jit(solution)/shard_map/ppermute | solution.py:240
  28.3 1.5 %shard_map.88 = (f32[432,128]{1,0:T(8,128)S(1)}, bf16[432,128]{1,0:T(8,128)(2,1)S(1)}, bf16[10,64,128]{2,1,0:T(8,128)(2,1)S(1)}) custom-call(bf16[4,32,512]{2,1,0:T(8,128)(2,1)S(1)} %collective-permute-done.7.refs_0_, bf16[4,32,512]{2,1,0:T(8,128)(2,1)S(1)} %pad_maximum_fusion.1.refs_1_, bf16[4,32,512]{2,1,0:T(8,128)(2,1)S(1)} %collective-permute-done.8.refs_2_, ...), custom_call_target="tpu_custom_call" | custom-call | tf_op jit(solution)/shard_map/pallas_call | solution.py:16
  29.8 2.5 %collective-permute-start.11 = (bf16[432,128]{1,0:T(8,128)(2,1)S(1)}, bf16[432,128]{1,0:T(8,128)(2,1)S(1)}, u32[]{:S(2)}, u32[]{:S(2)}) collective-permute-start(bf16[432,128]{1,0:T(8,128)(2,1)S(1)} %get-tuple-element.61), channel_id=1, source_target_pairs={{0,4},{4,0},{8,12},{12,8},{16,20},{20,16},{24,28},{28,24},{1,5},{5... | collective-permute-start | bytes 331784 | tf_op jit(solution)/shard_map/ppermute | solution.py:240
  32.3 0.0 collective-permute-start.12
  32.4 1.5 %collective-permute-start.13 = (bf16[256,128]{1,0:T(8,128)(2,1)S(1)}, bf16[256,128]{1,0:T(8,128)(2,1)S(1)}, u32[]{:S(2)}, u32[]{:S(2)}) collective-permute-start(bf16[256,128]{1,0:T(8,128)(2,1)S(1)} %get-tuple-element.66), channel_id=1, source_target_pairs={{0,2},{1,3},{2,0},{3,1},{4,6},{5,7},{6,4},{7,5},{8,10},{9,11},{10,... | collective-permute-start | bytes 196616 | tf_op jit(solution)/shard_map/ppermute | solution.py:240
  33.8 0.4 collective-permute-start.14
  34.2 1.4 %collective-permute-done.11.other = bf16[432,128]{1,0:T(8,128)(2,1)S(1)} collective-permute-done((bf16[432,128]{1,0:T(8,128)(2,1)S(1)}, bf16[432,128]{1,0:T(8,128)(2,1)S(1)}, u32[]{:S(2)}, u32[]{:S(2)}) %collective-permute-start.11) | collective-permute-done | bytes 110624 | tf_op jit(solution)/shard_map/ppermute | solution.py:240
  35.6 0.7 collective-permute-start.19
  36.3 4.6 %collective-permute-start.18 = (bf16[10,64,128]{2,1,0:T(8,128)(2,1)S(1)}, bf16[10,64,128]{2,1,0:T(8,128)(2,1)S(1)}, u32[]{:S(2)}, u32[]{:S(2)}) collective-permute-start(bf16[10,64,128]{2,1,0:T(8,128)(2,1)S(1)} %get-tuple-element.72.own), channel_id=1, source_target_pairs={{0,4},{4,0},{8,12},{12,8},{16,20},{20,16},{24,28},{28,24},{1,5},{5... | collective-permute-start | bytes 491528 | tf_op jit(solution)/shard_map/ppermute | solution.py:240
  40.8 0.0 collective-permute-done.13.rest_2_
  40.8 0.0 collective-permute-done.14.rest_3_
  40.8 0.1 shard_map.89
  40.9 1.6 %collective-permute-start.15 = (bf16[176,128]{1,0:T(8,128)(2,1)S(1)}, bf16[176,128]{1,0:T(8,128)(2,1)S(1)}, u32[]{:S(2)}, u32[]{:S(2)}) collective-permute-start(bf16[176,128]{1,0:T(8,128)(2,1)S(1)} %get-tuple-element.69), channel_id=1, source_target_pairs={{0,8},{4,12},{8,0},{12,4},{16,24},{20,28},{24,16},{28,20},{1,9},{5... | collective-permute-start | bytes 135176 | tf_op jit(solution)/shard_map/ppermute | solution.py:240
  42.5 1.2 %collective-permute-start.16 = (bf16[176,128]{1,0:T(8,128)(2,1)S(1)}, bf16[176,128]{1,0:T(8,128)(2,1)S(1)}, u32[]{:S(2)}, u32[]{:S(2)}) collective-permute-start(bf16[176,128]{1,0:T(8,128)(2,1)S(1)} %get-tuple-element.70), channel_id=1, source_target_pairs={{0,16},{4,20},{8,24},{12,28},{16,0},{20,4},{24,8},{28,12},{1,17},{... | collective-permute-start | bytes 135176 | tf_op jit(solution)/shard_map/ppermute | solution.py:240
  43.6 1.7 %collective-permute-start.17 = (bf16[176,128]{1,0:T(8,128)(2,1)S(1)}, bf16[176,128]{1,0:T(8,128)(2,1)S(1)}, u32[]{:S(2)}, u32[]{:S(2)}) collective-permute-start(bf16[176,128]{1,0:T(8,128)(2,1)S(1)} %get-tuple-element.71), channel_id=1, source_target_pairs={{0,24},{4,28},{8,16},{12,20},{16,8},{20,12},{24,0},{28,4},{1,25},{... | collective-permute-start | bytes 135176 | tf_op jit(solution)/shard_map/ppermute | solution.py:240
  45.4 0.0 collective-permute-done.15
  45.4 2.3 %collective-permute-done.16 = bf16[176,128]{1,0:T(8,128)(2,1)S(1)} collective-permute-done((bf16[176,128]{1,0:T(8,128)(2,1)S(1)}, bf16[176,128]{1,0:T(8,128)(2,1)S(1)}, u32[]{:S(2)}, u32[]{:S(2)}) %collective-permute-start.16) | collective-permute-done | bytes 45088 | tf_op jit(solution)/shard_map/ppermute | solution.py:240
  47.7 1.9 %collective-permute-done.17 = bf16[176,128]{1,0:T(8,128)(2,1)S(1)} collective-permute-done((bf16[176,128]{1,0:T(8,128)(2,1)S(1)}, bf16[176,128]{1,0:T(8,128)(2,1)S(1)}, u32[]{:S(2)}, u32[]{:S(2)}) %collective-permute-start.17) | collective-permute-done | bytes 45088 | tf_op jit(solution)/shard_map/ppermute | solution.py:240
  49.5 0.0 collective-permute-done.19.odd
  49.6 0.0 collective-permute-done.18.even
  49.6 0.1 multiply_convert_fusion
  49.7 1.7 %collective-permute-start.22 = (bf16[176,128]{1,0:T(8,128)(2,1)S(1)}, bf16[176,128]{1,0:T(8,128)(2,1)S(1)}, u32[]{:S(2)}, u32[]{:S(2)}) collective-permute-start(bf16[176,128]{1,0:T(8,128)(2,1)S(1)} %multiply_convert_fusion), channel_id=1, source_target_pairs={{0,24},{4,28},{8,16},{12,20},{16,8},{20,12},{24,0},{28,4},{1,25},{... | collective-permute-start | bytes 135176 | tf_op jit(solution)/shard_map/ppermute | solution.py:240
  51.4 2.7 %collective-permute-start.20 = (bf16[176,128]{1,0:T(8,128)(2,1)S(1)}, bf16[176,128]{1,0:T(8,128)(2,1)S(1)}, u32[]{:S(2)}, u32[]{:S(2)}) collective-permute-start(bf16[176,128]{1,0:T(8,128)(2,1)S(1)} %multiply_convert_fusion), channel_id=1, source_target_pairs={{0,8},{4,12},{8,0},{12,4},{16,24},{20,28},{24,16},{28,20},{1,9},{5... | collective-permute-start | bytes 135176 | tf_op jit(solution)/shard_map/ppermute | solution.py:240
  54.1 1.8 %shard_map.90 = bf16[8,64,128]{2,1,0:T(8,128)(2,1)} custom-call(bf16[10,64,128]{2,1,0:T(8,128)(2,1)S(1)} %collective-permute-done.18.even, bf16[10,64,128]{2,1,0:T(8,128)(2,1)S(1)} %get-tuple-element.72.own, bf16[10,64,128]{2,1,0:T(8,128)(2,1)S(1)} %collective-permute-done.19.odd, bf16[3,3,3,128,128]{4,3,2,1,0:T(8,128)(2,1)S(1)} %copy-done.1), custom_call_target="tpu_custom_call" | custom-call | tf_op jit(solution)/shard_map/pallas_call | solution.py:16
  55.9 0.0 collective-permute-done.22
  55.9 0.9 %collective-permute-done.21 = bf16[176,128]{1,0:T(8,128)(2,1)S(1)} collective-permute-done((bf16[176,128]{1,0:T(8,128)(2,1)S(1)}, bf16[176,128]{1,0:T(8,128)(2,1)S(1)}, u32[]{:S(2)}, u32[]{:S(2)}) %collective-permute-start.21) | collective-permute-done | bytes 45088 | tf_op jit(solution)/shard_map/ppermute | solution.py:240
  56.8 0.0 collective-permute-done.20
  56.8 1.2 %collective-permute-start.26 = (bf16[4,176,128]{2,1,0:T(8,128)(2,1)S(1)}, bf16[4,176,128]{2,1,0:T(8,128)(2,1)S(1)}, u32[]{:S(2)}, u32[]{:S(2)}) collective-permute-start(bf16[4,176,128]{2,1,0:T(8,128)(2,1)S(1)} %pad_maximum_fusion.refs_0_), channel_id=1, source_target_pairs={{0,4},{4,0},{8,12},{12,8},{16,20},{20,16},{24,28},{28,24},{1,5},{5... | collective-permute-start | bytes 540680 | tf_op jit(solution)/shard_map/ppermute | solution.py:240
  58.0 1.5 %collective-permute-start.24 = (bf16[4,176,128]{2,1,0:T(8,128)(2,1)S(1)}, bf16[4,176,128]{2,1,0:T(8,128)(2,1)S(1)}, u32[]{:S(2)}, u32[]{:S(2)}) collective-permute-start(bf16[4,176,128]{2,1,0:T(8,128)(2,1)S(1)} %pad_maximum_fusion.refs_0_), channel_id=1, source_target_pairs={{0,2},{1,3},{2,0},{3,1},{4,6},{5,7},{6,4},{7,5},{8,10},{9,11},{10,... | collective-permute-start | bytes 540680 | tf_op jit(solution)/shard_map/ppermute | solution.py:240
  59.5 2.9 %collective-permute-done.26.refs_4_ = bf16[4,176,128]{2,1,0:T(8,128)(2,1)S(1)} collective-permute-done((bf16[4,176,128]{2,1,0:T(8,128)(2,1)S(1)}, bf16[4,176,128]{2,1,0:T(8,128)(2,1)S(1)}, u32[]{:S(2)}, u32[]{:S(2)}) %collective-permute-start.26) | collective-permute-done | bytes 180256 | tf_op jit(solution)/shard_map/ppermute | solution.py:240
  62.4 1.5 %collective-permute-start.28 = (bf16[4,176,128]{2,1,0:T(8,128)(2,1)S(1)}, bf16[4,176,128]{2,1,0:T(8,128)(2,1)S(1)}, u32[]{:S(2)}, u32[]{:S(2)}) collective-permute-start(bf16[4,176,128]{2,1,0:T(8,128)(2,1)S(1)} %collective-permute-done.26.refs_4_), channel_id=1, source_target_pairs={{0,2},{1,3},{2,0},{3,1},{4,6},{5,7},{6,4},{7,5},{8,10},{9,11},{10,... | collective-permute-start | bytes 540680 | tf_op jit(solution)/shard_map/ppermute | solution.py:240
  63.9 0.5 collective-permute-start.27
  64.4 0.9 %collective-permute-done.24.refs_2_ = bf16[4,176,128]{2,1,0:T(8,128)(2,1)S(1)} collective-permute-done((bf16[4,176,128]{2,1,0:T(8,128)(2,1)S(1)}, bf16[4,176,128]{2,1,0:T(8,128)(2,1)S(1)}, u32[]{:S(2)}, u32[]{:S(2)}) %collective-permute-start.24) | collective-permute-done | bytes 180256 | tf_op jit(solution)/shard_map/ppermute | solution.py:240
  65.3 0.0 collective-permute-start.25
  65.3 2.6 %collective-permute-done.28.refs_6_ = bf16[4,176,128]{2,1,0:T(8,128)(2,1)S(1)} collective-permute-done((bf16[4,176,128]{2,1,0:T(8,128)(2,1)S(1)}, bf16[4,176,128]{2,1,0:T(8,128)(2,1)S(1)}, u32[]{:S(2)}, u32[]{:S(2)}) %collective-permute-start.28) | collective-permute-done | bytes 180256 | tf_op jit(solution)/shard_map/ppermute | solution.py:240
  67.9 0.0 collective-permute-done.27.refs_5_
  67.9 0.0 collective-permute-done.25.refs_3_
  67.9 1.4 %collective-permute-done.29.refs_7_ = bf16[4,176,128]{2,1,0:T(8,128)(2,1)S(1)} collective-permute-done((bf16[4,176,128]{2,1,0:T(8,128)(2,1)S(1)}, bf16[4,176,128]{2,1,0:T(8,128)(2,1)S(1)}, u32[]{:S(2)}, u32[]{:S(2)}) %collective-permute-start.29) | collective-permute-done | bytes 180256 | tf_op jit(solution)/shard_map/ppermute | solution.py:240
  69.3 1.3 %shard_map.91 = (bf16[27,4,2,16,128]{4,3,2,1,0:T(8,128)(2,1)}, bf16[2,4,128,256]{3,2,1,0:T(8,128)(2,1)}) custom-call(bf16[4,176,128]{2,1,0:T(8,128)(2,1)S(1)} %pad_maximum_fusion.refs_0_, bf16[4,176,128]{2,1,0:T(8,128)(2,1)S(1)} %collective-permute-done.23.refs_1_, bf16[4,176,128]{2,1,0:T(8,128)(2,1)S(1)} %collective-permute-done.24.refs_2_, ...), custom_call_target="tpu_custom_call" | custom-call | tf_op jit(solution)/shard_map/pallas_call | solution.py:16
  (22 shorter events, 0.1 us)
Async XLA Ops:
  0.6 8.9 %copy-start = (bf16[2,2,2,128,256]{4,3,2,1,0:T(8,128)(2,1)S(1)}, bf16[2,2,2,128,256]{4,3,2,1,0:T(8,128)(2,1)}, u32[]{:S(2)}) copy-start(bf16[2,2,2,128,256]{4,3,2,1,0:T(8,128)(2,1)} %param.9) | copy-start | bytes 1572868
  0.6 1.0 %copy-start.2 = (bf16[4,4,32,32]{3,2,1,0:T(8,128)(2,1)S(1)}, bf16[4,4,32,32]{3,2,1,0:T(8,128)(2,1)}, u32[]{:S(2)}) copy-start(bf16[4,4,32,32]{3,2,1,0:T(8,128)(2,1)} %param.11) | copy-start | bytes 98308
  1.6 4.2 %copy-start.3 = (bf16[1,8,64,128]{3,2,1,0:T(8,128)(2,1)S(1)}, bf16[1,8,64,128]{3,2,1,0:T(8,128)(2,1)}, u32[]{:S(2)}) copy-start(bf16[1,8,64,128]{3,2,1,0:T(8,128)(2,1)} %param.6) | copy-start | bytes 393220
  1.7 6.2 %collective-permute-start = (bf16[2,32,128]{2,1,0:T(8,128)(2,1)S(1)}, bf16[2,32,128]{2,1,0:T(8,128)(2,1)S(1)}, u32[]{:S(2)}, u32[]{:S(2)}) collective-permute-start(bf16[2,32,128]{2,1,0:T(8,128)(2,1)S(1)} %get-tuple-element.45), channel_id=1, source_target_pairs={{0,16},{4,20},{8,24},{12,28},{16,0},{20,4},{24,8},{28,12},{1,17},{... | collective-permute-start | bytes 49160 | tf_op jit(solution)/shard_map/ppermute | solution.py:240
  5.9 7.3 %collective-permute-start.3 = (bf16[32,512]{1,0:T(8,128)(2,1)S(1)}, bf16[32,512]{1,0:T(8,128)(2,1)S(1)}, u32[]{:S(2)}, u32[]{:S(2)}) collective-permute-start(bf16[32,512]{1,0:T(8,128)(2,1)S(1)} %get-tuple-element.47), channel_id=1, source_target_pairs={{0,1},{1,0},{2,3},{3,2},{4,5},{5,4},{6,7},{7,6},{8,9},{9,8},{10,11... | collective-permute-start | bytes 98312 | tf_op jit(solution)/shard_map/ppermute | solution.py:240
  6.0 7.2 %collective-permute-start.4 = (bf16[32,512]{1,0:T(8,128)(2,1)S(1)}, bf16[32,512]{1,0:T(8,128)(2,1)S(1)}, u32[]{:S(2)}, u32[]{:S(2)}) collective-permute-start(bf16[32,512]{1,0:T(8,128)(2,1)S(1)} %get-tuple-element.48), channel_id=1, source_target_pairs={{0,2},{1,3},{2,0},{3,1},{4,6},{5,7},{6,4},{7,5},{8,10},{9,11},{10,... | collective-permute-start | bytes 98312 | tf_op jit(solution)/shard_map/ppermute | solution.py:240
  7.6 5.7 %collective-permute-start.5 = (bf16[32,512]{1,0:T(8,128)(2,1)S(1)}, bf16[32,512]{1,0:T(8,128)(2,1)S(1)}, u32[]{:S(2)}, u32[]{:S(2)}) collective-permute-start(bf16[32,512]{1,0:T(8,128)(2,1)S(1)} %get-tuple-element.49), channel_id=1, source_target_pairs={{0,3},{1,2},{2,1},{3,0},{4,7},{5,6},{6,5},{7,4},{8,11},{9,10},{10,... | collective-permute-start | bytes 98312 | tf_op jit(solution)/shard_map/ppermute | solution.py:240
  7.9 3.8 %collective-permute-start.1 = (bf16[1,2,32,128]{3,2,1,0:T(8,128)(2,1)S(1)}, bf16[1,2,32,128]{3,2,1,0:T(8,128)(2,1)S(1)}, u32[]{:S(2)}, u32[]{:S(2)}) collective-permute-start(bf16[1,2,32,128]{3,2,1,0:T(8,128)(2,1)S(1)} %get-tuple-element.86), channel_id=1, source_target_pairs={{0,8},{4,12},{8,0},{12,4},{16,24},{20,28},{24,16},{28,20},{1,9},{5... | collective-permute-start | bytes 49160 | tf_op jit(solution)/shard_map/ppermute | solution.py:240
  11.7 3.9 %collective-permute-start.2 = (bf16[4,32,128]{2,1,0:T(8,128)(2,1)S(1)}, bf16[4,32,128]{2,1,0:T(8,128)(2,1)S(1)}, u32[]{:S(2)}, u32[]{:S(2)}) collective-permute-start(bf16[4,32,128]{2,1,0:T(8,128)(2,1)S(1)} %maximum_bitcast_fusion.refs_3_), channel_id=1, source_target_pairs={{0,4},{4,0},{8,12},{12,8},{16,20},{20,16},{24,28},{28,24},{1,5},{5... | collective-permute-start | bytes 98312 | tf_op jit(solution)/shard_map/ppermute | solution.py:240
  13.2 2.4 %copy-start.4 = (bf16[1,8,64,128]{3,2,1,0:T(8,128)(2,1)S(1)}, bf16[1,8,64,128]{3,2,1,0:T(8,128)(2,1)}, u32[]{:S(2)}) copy-start(bf16[1,8,64,128]{3,2,1,0:T(8,128)(2,1)} %param.7) | copy-start | bytes 393220
  13.2 2.4 %copy-start.5 = (bf16[1,8,64,128]{3,2,1,0:T(8,128)(2,1)S(1)}, bf16[1,8,64,128]{3,2,1,0:T(8,128)(2,1)}, u32[]{:S(2)}) copy-start(bf16[1,8,64,128]{3,2,1,0:T(8,128)(2,1)} %param.10) | copy-start | bytes 393220
  16.2 37.9 %copy-start.1 = (bf16[3,3,3,128,128]{4,3,2,1,0:T(8,128)(2,1)S(1)}, bf16[3,3,3,128,128]{4,3,2,1,0:T(8,128)(2,1)}, u32[]{:S(2)}) copy-start(bf16[3,3,3,128,128]{4,3,2,1,0:T(8,128)(2,1)} %weight.1) | copy-start | bytes 2654212
  16.2 2.2 %collective-permute-start.6 = (bf16[512,128]{1,0:T(8,128)(2,1)S(1)}, bf16[512,128]{1,0:T(8,128)(2,1)S(1)}, u32[]{:S(2)}, u32[]{:S(2)}) collective-permute-start(bf16[512,128]{1,0:T(8,128)(2,1)S(1)} %get-tuple-element.52.refs_3_), channel_id=1, source_target_pairs={{0,1},{1,0},{2,3},{3,2},{4,5},{5,4},{6,7},{7,6},{8,9},{9,8},{10,11... | collective-permute-start | bytes 393224 | tf_op jit(solution)/shard_map/ppermute | solution.py:240
  16.3 7.2 %collective-permute-start.10 = (bf16[512,128]{1,0:T(8,128)(2,1)S(1)}, bf16[512,128]{1,0:T(8,128)(2,1)S(1)}, u32[]{:S(2)}, u32[]{:S(2)}) collective-permute-start(bf16[512,128]{1,0:T(8,128)(2,1)S(1)} %get-tuple-element.52.refs_3_), channel_id=1, source_target_pairs={{0,3},{1,2},{2,1},{3,0},{4,7},{5,6},{6,5},{7,4},{8,11},{9,10},{10,... | collective-permute-start | bytes 393224 | tf_op jit(solution)/shard_map/ppermute | solution.py:240
  17.9 7.1 %collective-permute-start.9 = (bf16[512,128]{1,0:T(8,128)(2,1)S(1)}, bf16[512,128]{1,0:T(8,128)(2,1)S(1)}, u32[]{:S(2)}, u32[]{:S(2)}) collective-permute-start(bf16[512,128]{1,0:T(8,128)(2,1)S(1)} %get-tuple-element.52.refs_3_), channel_id=1, source_target_pairs={{0,2},{1,3},{2,0},{3,1},{4,6},{5,7},{6,4},{7,5},{8,10},{9,11},{10,... | collective-permute-start | bytes 393224 | tf_op jit(solution)/shard_map/ppermute | solution.py:240
  18.5 6.5 %collective-permute-start.8 = (bf16[4,32,512]{2,1,0:T(8,128)(2,1)S(1)}, bf16[4,32,512]{2,1,0:T(8,128)(2,1)S(1)}, u32[]{:S(2)}, u32[]{:S(2)}) collective-permute-start(bf16[4,32,512]{2,1,0:T(8,128)(2,1)S(1)} %pad_maximum_fusion.1.refs_1_), channel_id=1, source_target_pairs={{4,8},{8,4},{12,16},{16,12},{20,24},{24,20},{5,9},{9,5},{13,17},{1... | collective-permute-start | bytes 393224 | tf_op jit(solution)/shard_map/ppermute | solution.py:246
  19.1 9.1 %collective-permute-start.7 = (bf16[4,32,512]{2,1,0:T(8,128)(2,1)S(1)}, bf16[4,32,512]{2,1,0:T(8,128)(2,1)S(1)}, u32[]{:S(2)}, u32[]{:S(2)}) collective-permute-start(bf16[4,32,512]{2,1,0:T(8,128)(2,1)S(1)} %pad_maximum_fusion.1.refs_1_), channel_id=1, source_target_pairs={{0,4},{4,0},{8,12},{12,8},{16,20},{20,16},{24,28},{28,24},{1,5},{5... | collective-permute-start | bytes 393224 | tf_op jit(solution)/shard_map/ppermute | solution.py:240
  29.8 5.8 %collective-permute-start.11 = (bf16[432,128]{1,0:T(8,128)(2,1)S(1)}, bf16[432,128]{1,0:T(8,128)(2,1)S(1)}, u32[]{:S(2)}, u32[]{:S(2)}) collective-permute-start(bf16[432,128]{1,0:T(8,128)(2,1)S(1)} %get-tuple-element.61), channel_id=1, source_target_pairs={{0,4},{4,0},{8,12},{12,8},{16,20},{20,16},{24,28},{28,24},{1,5},{5... | collective-permute-start | bytes 331784 | tf_op jit(solution)/shard_map/ppermute | solution.py:240
  32.3 8.5 %collective-permute-start.12 = (bf16[256,128]{1,0:T(8,128)(2,1)S(1)}, bf16[256,128]{1,0:T(8,128)(2,1)S(1)}, u32[]{:S(2)}, u32[]{:S(2)}) collective-permute-start(bf16[256,128]{1,0:T(8,128)(2,1)S(1)} %get-tuple-element.65), channel_id=1, source_target_pairs={{0,1},{1,0},{2,3},{3,2},{4,5},{5,4},{6,7},{7,6},{8,9},{9,8},{10,11... | collective-permute-start | bytes 196616 | tf_op jit(solution)/shard_map/ppermute | solution.py:240
  32.4 8.5 %collective-permute-start.13 = (bf16[256,128]{1,0:T(8,128)(2,1)S(1)}, bf16[256,128]{1,0:T(8,128)(2,1)S(1)}, u32[]{:S(2)}, u32[]{:S(2)}) collective-permute-start(bf16[256,128]{1,0:T(8,128)(2,1)S(1)} %get-tuple-element.66), channel_id=1, source_target_pairs={{0,2},{1,3},{2,0},{3,1},{4,6},{5,7},{6,4},{7,5},{8,10},{9,11},{10,... | collective-permute-start | bytes 196616 | tf_op jit(solution)/shard_map/ppermute | solution.py:240
  33.8 7.0 %collective-permute-start.14 = (bf16[256,128]{1,0:T(8,128)(2,1)S(1)}, bf16[256,128]{1,0:T(8,128)(2,1)S(1)}, u32[]{:S(2)}, u32[]{:S(2)}) collective-permute-start(bf16[256,128]{1,0:T(8,128)(2,1)S(1)} %get-tuple-element.67), channel_id=1, source_target_pairs={{0,3},{1,2},{2,1},{3,0},{4,7},{5,6},{6,5},{7,4},{8,11},{9,10},{10,... | collective-permute-start | bytes 196616 | tf_op jit(solution)/shard_map/ppermute | solution.py:240
  35.6 14.0 %collective-permute-start.19 = (bf16[10,64,128]{2,1,0:T(8,128)(2,1)S(1)}, bf16[10,64,128]{2,1,0:T(8,128)(2,1)S(1)}, u32[]{:S(2)}, u32[]{:S(2)}) collective-permute-start(bf16[10,64,128]{2,1,0:T(8,128)(2,1)S(1)} %get-tuple-element.72.own), channel_id=1, source_target_pairs={{4,8},{8,4},{12,16},{16,12},{20,24},{24,20},{5,9},{9,5},{13,17},{1... | collective-permute-start | bytes 491528 | tf_op jit(solution)/shard_map/ppermute | solution.py:246
  36.3 13.3 %collective-permute-start.18 = (bf16[10,64,128]{2,1,0:T(8,128)(2,1)S(1)}, bf16[10,64,128]{2,1,0:T(8,128)(2,1)S(1)}, u32[]{:S(2)}, u32[]{:S(2)}) collective-permute-start(bf16[10,64,128]{2,1,0:T(8,128)(2,1)S(1)} %get-tuple-element.72.own), channel_id=1, source_target_pairs={{0,4},{4,0},{8,12},{12,8},{16,20},{20,16},{24,28},{28,24},{1,5},{5... | collective-permute-start | bytes 491528 | tf_op jit(solution)/shard_map/ppermute | solution.py:240
  40.9 4.5 %collective-permute-start.15 = (bf16[176,128]{1,0:T(8,128)(2,1)S(1)}, bf16[176,128]{1,0:T(8,128)(2,1)S(1)}, u32[]{:S(2)}, u32[]{:S(2)}) collective-permute-start(bf16[176,128]{1,0:T(8,128)(2,1)S(1)} %get-tuple-element.69), channel_id=1, source_target_pairs={{0,8},{4,12},{8,0},{12,4},{16,24},{20,28},{24,16},{28,20},{1,9},{5... | collective-permute-start | bytes 135176 | tf_op jit(solution)/shard_map/ppermute | solution.py:240
  42.5 5.2 %collective-permute-start.16 = (bf16[176,128]{1,0:T(8,128)(2,1)S(1)}, bf16[176,128]{1,0:T(8,128)(2,1)S(1)}, u32[]{:S(2)}, u32[]{:S(2)}) collective-permute-start(bf16[176,128]{1,0:T(8,128)(2,1)S(1)} %get-tuple-element.70), channel_id=1, source_target_pairs={{0,16},{4,20},{8,24},{12,28},{16,0},{20,4},{24,8},{28,12},{1,17},{... | collective-permute-start | bytes 135176 | tf_op jit(solution)/shard_map/ppermute | solution.py:240
  43.6 5.9 %collective-permute-start.17 = (bf16[176,128]{1,0:T(8,128)(2,1)S(1)}, bf16[176,128]{1,0:T(8,128)(2,1)S(1)}, u32[]{:S(2)}, u32[]{:S(2)}) collective-permute-start(bf16[176,128]{1,0:T(8,128)(2,1)S(1)} %get-tuple-element.71), channel_id=1, source_target_pairs={{0,24},{4,28},{8,16},{12,20},{16,8},{20,12},{24,0},{28,4},{1,25},{... | collective-permute-start | bytes 135176 | tf_op jit(solution)/shard_map/ppermute | solution.py:240
  49.7 6.2 %collective-permute-start.22 = (bf16[176,128]{1,0:T(8,128)(2,1)S(1)}, bf16[176,128]{1,0:T(8,128)(2,1)S(1)}, u32[]{:S(2)}, u32[]{:S(2)}) collective-permute-start(bf16[176,128]{1,0:T(8,128)(2,1)S(1)} %multiply_convert_fusion), channel_id=1, source_target_pairs={{0,24},{4,28},{8,16},{12,20},{16,8},{20,12},{24,0},{28,4},{1,25},{... | collective-permute-start | bytes 135176 | tf_op jit(solution)/shard_map/ppermute | solution.py:240
  51.4 5.4 %collective-permute-start.21 = (bf16[176,128]{1,0:T(8,128)(2,1)S(1)}, bf16[176,128]{1,0:T(8,128)(2,1)S(1)}, u32[]{:S(2)}, u32[]{:S(2)}) collective-permute-start(bf16[176,128]{1,0:T(8,128)(2,1)S(1)} %multiply_convert_fusion), channel_id=1, source_target_pairs={{0,16},{4,20},{8,24},{12,28},{16,0},{20,4},{24,8},{28,12},{1,17},{... | collective-permute-start | bytes 135176 | tf_op jit(solution)/shard_map/ppermute | solution.py:240
  51.4 5.4 %collective-permute-start.20 = (bf16[176,128]{1,0:T(8,128)(2,1)S(1)}, bf16[176,128]{1,0:T(8,128)(2,1)S(1)}, u32[]{:S(2)}, u32[]{:S(2)}) collective-permute-start(bf16[176,128]{1,0:T(8,128)(2,1)S(1)} %multiply_convert_fusion), channel_id=1, source_target_pairs={{0,8},{4,12},{8,0},{12,4},{16,24},{20,28},{24,16},{28,20},{1,9},{5... | collective-permute-start | bytes 135176 | tf_op jit(solution)/shard_map/ppermute | solution.py:240
  56.8 5.6 %collective-permute-start.26 = (bf16[4,176,128]{2,1,0:T(8,128)(2,1)S(1)}, bf16[4,176,128]{2,1,0:T(8,128)(2,1)S(1)}, u32[]{:S(2)}, u32[]{:S(2)}) collective-permute-start(bf16[4,176,128]{2,1,0:T(8,128)(2,1)S(1)} %pad_maximum_fusion.refs_0_), channel_id=1, source_target_pairs={{0,4},{4,0},{8,12},{12,8},{16,20},{20,16},{24,28},{28,24},{1,5},{5... | collective-permute-start | bytes 540680 | tf_op jit(solution)/shard_map/ppermute | solution.py:240
  58.0 7.3 %collective-permute-start.24 = (bf16[4,176,128]{2,1,0:T(8,128)(2,1)S(1)}, bf16[4,176,128]{2,1,0:T(8,128)(2,1)S(1)}, u32[]{:S(2)}, u32[]{:S(2)}) collective-permute-start(bf16[4,176,128]{2,1,0:T(8,128)(2,1)S(1)} %pad_maximum_fusion.refs_0_), channel_id=1, source_target_pairs={{0,2},{1,3},{2,0},{3,1},{4,6},{5,7},{6,4},{7,5},{8,10},{9,11},{10,... | collective-permute-start | bytes 540680 | tf_op jit(solution)/shard_map/ppermute | solution.py:240
  62.4 5.5 %collective-permute-start.28 = (bf16[4,176,128]{2,1,0:T(8,128)(2,1)S(1)}, bf16[4,176,128]{2,1,0:T(8,128)(2,1)S(1)}, u32[]{:S(2)}, u32[]{:S(2)}) collective-permute-start(bf16[4,176,128]{2,1,0:T(8,128)(2,1)S(1)} %collective-permute-done.26.refs_4_), channel_id=1, source_target_pairs={{0,2},{1,3},{2,0},{3,1},{4,6},{5,7},{6,4},{7,5},{8,10},{9,11},{10,... | collective-permute-start | bytes 540680 | tf_op jit(solution)/shard_map/ppermute | solution.py:240
  63.9 4.0 %collective-permute-start.23 = (bf16[4,176,128]{2,1,0:T(8,128)(2,1)S(1)}, bf16[4,176,128]{2,1,0:T(8,128)(2,1)S(1)}, u32[]{:S(2)}, u32[]{:S(2)}) collective-permute-start(bf16[4,176,128]{2,1,0:T(8,128)(2,1)S(1)} %pad_maximum_fusion.refs_0_), channel_id=1, source_target_pairs={{0,1},{1,0},{2,3},{3,2},{4,5},{5,4},{6,7},{7,6},{8,9},{9,8},{10,11... | collective-permute-start | bytes 540680 | tf_op jit(solution)/shard_map/ppermute | solution.py:240
  63.9 4.0 %collective-permute-start.27 = (bf16[4,176,128]{2,1,0:T(8,128)(2,1)S(1)}, bf16[4,176,128]{2,1,0:T(8,128)(2,1)S(1)}, u32[]{:S(2)}, u32[]{:S(2)}) collective-permute-start(bf16[4,176,128]{2,1,0:T(8,128)(2,1)S(1)} %collective-permute-done.26.refs_4_), channel_id=1, source_target_pairs={{0,1},{1,0},{2,3},{3,2},{4,5},{5,4},{6,7},{7,6},{8,9},{9,8},{10,11... | collective-permute-start | bytes 540680 | tf_op jit(solution)/shard_map/ppermute | solution.py:240
  65.3 2.6 %collective-permute-start.25 = (bf16[4,176,128]{2,1,0:T(8,128)(2,1)S(1)}, bf16[4,176,128]{2,1,0:T(8,128)(2,1)S(1)}, u32[]{:S(2)}, u32[]{:S(2)}) collective-permute-start(bf16[4,176,128]{2,1,0:T(8,128)(2,1)S(1)} %collective-permute-done.24.refs_2_), channel_id=1, source_target_pairs={{0,1},{1,0},{2,3},{3,2},{4,5},{5,4},{6,7},{7,6},{8,9},{9,8},{10,11... | collective-permute-start | bytes 540680 | tf_op jit(solution)/shard_map/ppermute | solution.py:240
  67.9 1.4 %collective-permute-start.29 = (bf16[4,176,128]{2,1,0:T(8,128)(2,1)S(1)}, bf16[4,176,128]{2,1,0:T(8,128)(2,1)S(1)}, u32[]{:S(2)}, u32[]{:S(2)}) collective-permute-start(bf16[4,176,128]{2,1,0:T(8,128)(2,1)S(1)} %collective-permute-done.28.refs_6_), channel_id=1, source_target_pairs={{0,1},{1,0},{2,3},{3,2},{4,5},{5,4},{6,7},{7,6},{8,9},{9,8},{10,11... | collective-permute-start | bytes 540680 | tf_op jit(solution)/shard_map/ppermute | solution.py:240

commit v14 on v12

--- a/solution.py
+++ b/solution.py
@@ -298,6 +298,7 @@
     )
     level_t = [swapped(value, "gy", code) if code else value for code, value in enumerate(level_t)]
     level_t = jnp.stack(level_t)
+    even, odd = neighbours(level_t)
     *deep_t, level_t = lax.optimization_barrier((*deep_t, level_t))
     down_slice = lax.dynamic_index_in_dim(down_weight, parity, 0, keepdims=False)
     grad, down, *others = call(
@@ -313,8 +314,6 @@
             pltpu.VMEM((n_gy, 4 * channels // n_gy, deep_channels), F32),
         ],
     )
-    grad, level_t = lax.optimization_barrier((grad, level_t))
-    even, odd = neighbours(level_t)
     shared = [swapped(grad, "gy", code) if code else grad for code in range(n_gy)]
     even, odd, *others = lax.optimization_barrier((even, odd, *others))
     downs = [down] + [swapped(value, "gy", code + 1) for code, value in enumerate(others)]
@@ -335,7 +334,6 @@
             pltpu.VMEM((2, 27 * half, channels), F32),
         ],
     )
-    near_even, near_odd = neighbours(near)
     send = swapped(send, "gz", 1)
 
     def input_part(near_even, near_odd):
@@ -361,6 +359,8 @@
             *downs,
             scratch=[pltpu.VMEM((n_z, piece, channels), F32)],
         )
+        own, near, *pieces = lax.optimization_barrier((own, near, *pieces))
+        near_even, near_odd = neighbours(near)
         pieces = [swapped(value, "gz", 2 * code + 2) for code, value in enumerate(pieces)]
         *pieces, near_even, near_odd = lax.optimization_barrier((*pieces, near_even, near_odd))
         total = own + sum(value.astype(F32) for value in pieces)
@@ -373,6 +373,7 @@
             total = total + swapped(total, "gz", code)
             code //= 2
         first = 0
+        near_even, near_odd = neighbours(near)
     row = first + lax.broadcasted_iota(jnp.int32, total.shape, 0)
     scale = jnp.where(
         row < 27 * half, 1 / math.sqrt(cell_total), 1 / math.sqrt(cell_total // 8)

time: 70.6 us -> 70.5 us (level)
  starting transfers between devices: 33.1 us -> 34.9 us
  waiting for transfers between devices: 29.9 us -> 28.1 us
    ppermute x28, waiting for transfers between devices: 29.9 us -> 28 us  [swapped(): lax.ppermute(value, axis, [(i, i ^ code) for i in range(lax.axis_size(axi...]
    ppermute x28, starting transfers between devices: 31.8 us -> 33.4 us  [swapped(): lax.ppermute(value, axis, [(i, i ^ code) for i in range(lax.axis_size(axi...]
  transfers between devices with their start and end apart: 30 -> 30, of which waited for: 12 -> 15; matrix products, arithmetic and copies ran while one was open for 0% -> 0% of each run, Pallas kernels for 5% -> 4%
where the time goes in v14:
time: 70.5 us; the launch traced here: 70.3 us
  starting transfers between devices  34.9 us (50%)
  waiting for transfers between devices  28.1 us (40%)
  Pallas kernels  5.43 us (8%)
  local copies, waits for them, and re-layouts  1 us (1%)
  between operations  0.8 us (1%)
    ppermute x28, starting transfers between devices, swapped(): lax.ppermute(value, axis, [(i, i ^ code) for i in range(lax.axis_size(axi...  33.4 us
    ppermute x28, waiting for transfers between devices, swapped(): lax.ppermute(value, axis, [(i, i ^ code) for i in range(lax.axis_size(axi...  28 us
    pallas_call x7, Pallas kernels, call(): pl.pallas_call(kernel, out_shape=out_shape, scratch_shapes=list(scratch),...  5.43 us
    ppermute x2, starting transfers between devices, neighbours(): return (swapped(value, 'gz', 1), lax.ppermute(value, 'gz', odd))  1.47 us
  transfers between devices with their start and end apart: 30, of which 15 were waited for; matrix products, arithmetic and copies ran while one was open for 0% of the time, Pallas kernels for 4%

profile of v14, /device:TPU:0, one launch (start us, length us, event | category | flops | bytes accessed | tf_op | source)
XLA Modules:
  0.0 70.3 jit_solution(17209395659253353751)
XLA Ops:
  0.6 0.0 copy-start
  0.7 1.0 %copy-done.2 = bf16[4,4,32,32]{3,2,1,0:T(8,128)(2,1)S(1)} copy-done((bf16[4,4,32,32]{3,2,1,0:T(8,128)(2,1)S(1)}, bf16[4,4,32,32]{3,2,1,0:T(8,128)(2,1)}, u32[]{:S(2)}) %copy-start.2) | copy-done | bytes 32792
  1.6 0.1 shard_map.86
  1.7 4.1 %collective-permute-start.5 = (bf16[2,32,128]{2,1,0:T(8,128)(2,1)S(1)}, bf16[2,32,128]{2,1,0:T(8,128)(2,1)S(1)}, u32[]{:S(2)}, u32[]{:S(2)}) collective-permute-start(bf16[2,32,128]{2,1,0:T(8,128)(2,1)S(1)} %get-tuple-element.51), channel_id=1, source_target_pairs={{0,16},{4,20},{8,24},{12,28},{16,0},{20,4},{24,8},{28,12},{1,17},{... | collective-permute-start | bytes 49160 | tf_op jit(solution)/shard_map/ppermute | solution.py:240
  5.8 0.1 shard_map.85
  5.9 0.1 collective-permute-start
  6.0 1.6 %collective-permute-start.1 = (bf16[32,512]{1,0:T(8,128)(2,1)S(1)}, bf16[32,512]{1,0:T(8,128)(2,1)S(1)}, u32[]{:S(2)}, u32[]{:S(2)}) collective-permute-start(bf16[32,512]{1,0:T(8,128)(2,1)S(1)} %get-tuple-element.48), channel_id=1, source_target_pairs={{0,2},{1,3},{2,0},{3,1},{4,6},{5,7},{6,4},{7,5},{8,10},{9,11},{10,... | collective-permute-start | bytes 98312 | tf_op jit(solution)/shard_map/ppermute | solution.py:240
  7.6 0.3 collective-permute-start.2
  7.9 1.6 %collective-permute-start.6 = (bf16[1,2,32,128]{3,2,1,0:T(8,128)(2,1)S(1)}, bf16[1,2,32,128]{3,2,1,0:T(8,128)(2,1)S(1)}, u32[]{:S(2)}, u32[]{:S(2)}) collective-permute-start(bf16[1,2,32,128]{3,2,1,0:T(8,128)(2,1)S(1)} %get-tuple-element.90), channel_id=1, source_target_pairs={{0,8},{4,12},{8,0},{12,4},{16,24},{20,28},{24,16},{28,20},{1,9},{5... | collective-permute-start | bytes 49160 | tf_op jit(solution)/shard_map/ppermute | solution.py:240
  9.5 2.1 %collective-permute-done.6 = bf16[1,2,32,128]{3,2,1,0:T(8,128)(2,1)S(1)} collective-permute-done((bf16[1,2,32,128]{3,2,1,0:T(8,128)(2,1)S(1)}, bf16[1,2,32,128]{3,2,1,0:T(8,128)(2,1)S(1)}, u32[]{:S(2)}, u32[]{:S(2)}) %collective-permute-start.6) | collective-permute-done | bytes 16416 | tf_op jit(solution)/shard_map/ppermute | solution.py:240
  11.7 1.5 %collective-permute-start.7 = (bf16[4,32,128]{2,1,0:T(8,128)(2,1)S(1)}, bf16[4,32,128]{2,1,0:T(8,128)(2,1)S(1)}, u32[]{:S(2)}, u32[]{:S(2)}) collective-permute-start(bf16[4,32,128]{2,1,0:T(8,128)(2,1)S(1)} %maximum_bitcast_fusion.refs_3_), channel_id=1, source_target_pairs={{0,4},{4,0},{8,12},{12,8},{16,20},{20,16},{24,28},{28,24},{1,5},{5... | collective-permute-start | bytes 98312 | tf_op jit(solution)/shard_map/ppermute | solution.py:240
  13.2 0.0 collective-permute-done
  13.2 0.0 collective-permute-done.1
  13.2 0.0 collective-permute-done.2
  13.2 0.0 copy-start.4
  13.2 0.0 copy-start.5
  13.3 0.8 %collective-permute-start.4 = (bf16[4,32,512]{2,1,0:T(8,128)(2,1)S(1)}, bf16[4,32,512]{2,1,0:T(8,128)(2,1)S(1)}, u32[]{:S(2)}, u32[]{:S(2)}) collective-permute-start(bf16[4,32,512]{2,1,0:T(8,128)(2,1)S(1)} %pad_maximum_fusion.1.refs_1_), channel_id=1, source_target_pairs={{4,8},{8,4},{12,16},{16,12},{20,24},{24,20},{5,9},{9,5},{13,17},{1... | collective-permute-start | bytes 393224 | tf_op jit(solution)/shard_map/ppermute | solution.py:246
  14.1 4.3 %collective-permute-start.3 = (bf16[4,32,512]{2,1,0:T(8,128)(2,1)S(1)}, bf16[4,32,512]{2,1,0:T(8,128)(2,1)S(1)}, u32[]{:S(2)}, u32[]{:S(2)}) collective-permute-start(bf16[4,32,512]{2,1,0:T(8,128)(2,1)S(1)} %pad_maximum_fusion.1.refs_1_), channel_id=1, source_target_pairs={{0,4},{4,0},{8,12},{12,8},{16,20},{20,16},{24,28},{28,24},{1,5},{5... | collective-permute-start | bytes 393224 | tf_op jit(solution)/shard_map/ppermute | solution.py:240
  18.4 0.6 shard_map.87
  19.1 0.1 collective-permute-start.10
  19.1 1.6 %collective-permute-start.9 = (bf16[512,128]{1,0:T(8,128)(2,1)S(1)}, bf16[512,128]{1,0:T(8,128)(2,1)S(1)}, u32[]{:S(2)}, u32[]{:S(2)}) collective-permute-start(bf16[512,128]{1,0:T(8,128)(2,1)S(1)} %get-tuple-element.60.refs_3_), channel_id=1, source_target_pairs={{0,2},{1,3},{2,0},{3,1},{4,6},{5,7},{6,4},{7,5},{8,10},{9,11},{10,... | collective-permute-start | bytes 393224 | tf_op jit(solution)/shard_map/ppermute | solution.py:240
  20.7 0.3 collective-permute-start.8
  21.0 0.5 collective-permute-done.3.refs_0_
  21.5 3.3 %collective-permute-done.10.refs_6_ = bf16[512,128]{1,0:T(8,128)(2,1)S(1)} collective-permute-done((bf16[512,128]{1,0:T(8,128)(2,1)S(1)}, bf16[512,128]{1,0:T(8,128)(2,1)S(1)}, u32[]{:S(2)}, u32[]{:S(2)}) %collective-permute-start.10) | collective-permute-done | bytes 131104 | tf_op jit(solution)/shard_map/ppermute | solution.py:240
  24.9 2.9 %collective-permute-done.9.refs_5_ = bf16[512,128]{1,0:T(8,128)(2,1)S(1)} collective-permute-done((bf16[512,128]{1,0:T(8,128)(2,1)S(1)}, bf16[512,128]{1,0:T(8,128)(2,1)S(1)}, u32[]{:S(2)}, u32[]{:S(2)}) %collective-permute-start.9) | collective-permute-done | bytes 131104 | tf_op jit(solution)/shard_map/ppermute | solution.py:240
  27.7 0.0 collective-permute-done.8.refs_4_
  27.7 1.5 %shard_map.88 = (f32[432,128]{1,0:T(8,128)S(1)}, bf16[432,128]{1,0:T(8,128)(2,1)S(1)}, bf16[10,64,128]{2,1,0:T(8,128)(2,1)S(1)}) custom-call(bf16[4,32,512]{2,1,0:T(8,128)(2,1)S(1)} %collective-permute-done.3.refs_0_, bf16[4,32,512]{2,1,0:T(8,128)(2,1)S(1)} %pad_maximum_fusion.1.refs_1_, bf16[4,32,512]{2,1,0:T(8,128)(2,1)S(1)} %collective-permute-done.4.refs_2_, ...), custom_call_target="tpu_custom_call" | custom-call | tf_op jit(solution)/shard_map/pallas_call | solution.py:16
  29.3 0.1 collective-permute-start.11
  29.4 0.1 collective-permute-start.12
  29.5 0.3 collective-permute-start.13
  29.8 1.5 %collective-permute-start.14 = (bf16[256,128]{1,0:T(8,128)(2,1)S(1)}, bf16[256,128]{1,0:T(8,128)(2,1)S(1)}, u32[]{:S(2)}, u32[]{:S(2)}) collective-permute-start(bf16[256,128]{1,0:T(8,128)(2,1)S(1)} %get-tuple-element.66), channel_id=1, source_target_pairs={{0,3},{1,2},{2,1},{3,0},{4,7},{5,6},{6,5},{7,4},{8,11},{9,10},{10,... | collective-permute-start | bytes 196616 | tf_op jit(solution)/shard_map/ppermute | solution.py:240
  31.3 3.1 %collective-permute-done.13.rest_2_ = bf16[256,128]{1,0:T(8,128)(2,1)S(1)} collective-permute-done((bf16[256,128]{1,0:T(8,128)(2,1)S(1)}, bf16[256,128]{1,0:T(8,128)(2,1)S(1)}, u32[]{:S(2)}, u32[]{:S(2)}) %collective-permute-start.13) | collective-permute-done | bytes 65568 | tf_op jit(solution)/shard_map/ppermute | solution.py:240
  34.4 0.5 collective-permute-done.14.rest_3_
  34.9 0.0 collective-permute-done.11.other
  34.9 0.1 shard_map.89
  35.0 0.7 collective-permute-start.19
  35.6 4.3 %collective-permute-start.18 = (bf16[10,64,128]{2,1,0:T(8,128)(2,1)S(1)}, bf16[10,64,128]{2,1,0:T(8,128)(2,1)S(1)}, u32[]{:S(2)}, u32[]{:S(2)}) collective-permute-start(bf16[10,64,128]{2,1,0:T(8,128)(2,1)S(1)} %get-tuple-element.76.own), channel_id=1, source_target_pairs={{0,4},{4,0},{8,12},{12,8},{16,20},{20,16},{24,28},{28,24},{1,5},{5... | collective-permute-start | bytes 491528 | tf_op jit(solution)/shard_map/ppermute | solution.py:240
  39.9 1.7 %collective-permute-start.15 = (bf16[176,128]{1,0:T(8,128)(2,1)S(1)}, bf16[176,128]{1,0:T(8,128)(2,1)S(1)}, u32[]{:S(2)}, u32[]{:S(2)}) collective-permute-start(bf16[176,128]{1,0:T(8,128)(2,1)S(1)} %get-tuple-element.73), channel_id=1, source_target_pairs={{0,8},{4,12},{8,0},{12,4},{16,24},{20,28},{24,16},{28,20},{1,9},{5... | collective-permute-start | bytes 135176 | tf_op jit(solution)/shard_map/ppermute | solution.py:240
  41.6 1.5 %collective-permute-start.16 = (bf16[176,128]{1,0:T(8,128)(2,1)S(1)}, bf16[176,128]{1,0:T(8,128)(2,1)S(1)}, u32[]{:S(2)}, u32[]{:S(2)}) collective-permute-start(bf16[176,128]{1,0:T(8,128)(2,1)S(1)} %get-tuple-element.74), channel_id=1, source_target_pairs={{0,16},{4,20},{8,24},{12,28},{16,0},{20,4},{24,8},{28,12},{1,17},{... | collective-permute-start | bytes 135176 | tf_op jit(solution)/shard_map/ppermute | solution.py:240
  43.0 1.2 %collective-permute-start.17 = (bf16[176,128]{1,0:T(8,128)(2,1)S(1)}, bf16[176,128]{1,0:T(8,128)(2,1)S(1)}, u32[]{:S(2)}, u32[]{:S(2)}) collective-permute-start(bf16[176,128]{1,0:T(8,128)(2,1)S(1)} %get-tuple-element.75), channel_id=1, source_target_pairs={{0,24},{4,28},{8,16},{12,20},{16,8},{20,12},{24,0},{28,4},{1,25},{... | collective-permute-start | bytes 135176 | tf_op jit(solution)/shard_map/ppermute | solution.py:240
  44.3 1.8 %collective-permute-done.15 = bf16[176,128]{1,0:T(8,128)(2,1)S(1)} collective-permute-done((bf16[176,128]{1,0:T(8,128)(2,1)S(1)}, bf16[176,128]{1,0:T(8,128)(2,1)S(1)}, u32[]{:S(2)}, u32[]{:S(2)}) %collective-permute-start.15) | collective-permute-done | bytes 45088 | tf_op jit(solution)/shard_map/ppermute | solution.py:240
  46.1 1.1 %collective-permute-done.16 = bf16[176,128]{1,0:T(8,128)(2,1)S(1)} collective-permute-done((bf16[176,128]{1,0:T(8,128)(2,1)S(1)}, bf16[176,128]{1,0:T(8,128)(2,1)S(1)}, u32[]{:S(2)}, u32[]{:S(2)}) %collective-permute-start.16) | collective-permute-done | bytes 45088 | tf_op jit(solution)/shard_map/ppermute | solution.py:240
  47.2 2.4 %collective-permute-done.17 = bf16[176,128]{1,0:T(8,128)(2,1)S(1)} collective-permute-done((bf16[176,128]{1,0:T(8,128)(2,1)S(1)}, bf16[176,128]{1,0:T(8,128)(2,1)S(1)}, u32[]{:S(2)}, u32[]{:S(2)}) %collective-permute-start.17) | collective-permute-done | bytes 45088 | tf_op jit(solution)/shard_map/ppermute | solution.py:240
  49.6 0.1 multiply_convert_fusion
  49.7 1.0 %collective-permute-start.22 = (bf16[176,128]{1,0:T(8,128)(2,1)S(1)}, bf16[176,128]{1,0:T(8,128)(2,1)S(1)}, u32[]{:S(2)}, u32[]{:S(2)}) collective-permute-start(bf16[176,128]{1,0:T(8,128)(2,1)S(1)} %multiply_convert_fusion), channel_id=1, source_target_pairs={{0,24},{4,28},{8,16},{12,20},{16,8},{20,12},{24,0},{28,4},{1,25},{... | collective-permute-start | bytes 135176 | tf_op jit(solution)/shard_map/ppermute | solution.py:240
  50.6 0.7 collective-permute-start.21
  51.3 2.8 %collective-permute-start.20 = (bf16[176,128]{1,0:T(8,128)(2,1)S(1)}, bf16[176,128]{1,0:T(8,128)(2,1)S(1)}, u32[]{:S(2)}, u32[]{:S(2)}) collective-permute-start(bf16[176,128]{1,0:T(8,128)(2,1)S(1)} %multiply_convert_fusion), channel_id=1, source_target_pairs={{0,8},{4,12},{8,0},{12,4},{16,24},{20,28},{24,16},{28,20},{1,9},{5... | collective-permute-start | bytes 135176 | tf_op jit(solution)/shard_map/ppermute | solution.py:240
  54.1 1.7 %shard_map.90 = bf16[8,64,128]{2,1,0:T(8,128)(2,1)} custom-call(bf16[10,64,128]{2,1,0:T(8,128)(2,1)S(1)} %collective-permute-done.18.even, bf16[10,64,128]{2,1,0:T(8,128)(2,1)S(1)} %get-tuple-element.76.own, bf16[10,64,128]{2,1,0:T(8,128)(2,1)S(1)} %collective-permute-done.19.odd, bf16[3,3,3,128,128]{4,3,2,1,0:T(8,128)(2,1)S(1)} %copy-done.1), custom_call_target="tpu_custom_call" | custom-call | tf_op jit(solution)/shard_map/pallas_call | solution.py:16
  55.9 0.2 collective-permute-done.22
  56.1 0.4 collective-permute-done.20
  56.6 1.2 %collective-permute-start.26 = (bf16[4,176,128]{2,1,0:T(8,128)(2,1)S(1)}, bf16[4,176,128]{2,1,0:T(8,128)(2,1)S(1)}, u32[]{:S(2)}, u32[]{:S(2)}) collective-permute-start(bf16[4,176,128]{2,1,0:T(8,128)(2,1)S(1)} %pad_maximum_fusion.refs_0_), channel_id=1, source_target_pairs={{0,4},{4,0},{8,12},{12,8},{16,20},{20,16},{24,28},{28,24},{1,5},{5... | collective-permute-start | bytes 540680 | tf_op jit(solution)/shard_map/ppermute | solution.py:240
  57.8 0.6 collective-permute-start.24
  58.4 3.8 %collective-permute-done.26.refs_4_ = bf16[4,176,128]{2,1,0:T(8,128)(2,1)S(1)} collective-permute-done((bf16[4,176,128]{2,1,0:T(8,128)(2,1)S(1)}, bf16[4,176,128]{2,1,0:T(8,128)(2,1)S(1)}, u32[]{:S(2)}, u32[]{:S(2)}) %collective-permute-start.26) | collective-permute-done | bytes 180256 | tf_op jit(solution)/shard_map/ppermute | solution.py:240
  62.1 0.5 collective-permute-start.28
  62.6 0.5 collective-permute-start.27
  63.1 1.8 %collective-permute-done.24.refs_2_ = bf16[4,176,128]{2,1,0:T(8,128)(2,1)S(1)} collective-permute-done((bf16[4,176,128]{2,1,0:T(8,128)(2,1)S(1)}, bf16[4,176,128]{2,1,0:T(8,128)(2,1)S(1)}, u32[]{:S(2)}, u32[]{:S(2)}) %collective-permute-start.24) | collective-permute-done | bytes 180256 | tf_op jit(solution)/shard_map/ppermute | solution.py:240
  65.0 0.0 collective-permute-start.25
  65.0 2.6 %collective-permute-done.28.refs_6_ = bf16[4,176,128]{2,1,0:T(8,128)(2,1)S(1)} collective-permute-done((bf16[4,176,128]{2,1,0:T(8,128)(2,1)S(1)}, bf16[4,176,128]{2,1,0:T(8,128)(2,1)S(1)}, u32[]{:S(2)}, u32[]{:S(2)}) %collective-permute-start.28) | collective-permute-done | bytes 180256 | tf_op jit(solution)/shard_map/ppermute | solution.py:240
  67.6 0.0 collective-permute-start.29
  67.6 0.0 collective-permute-done.23.refs_1_
  67.6 0.0 collective-permute-done.27.refs_5_
  67.6 0.0 collective-permute-done.25.refs_3_
  67.6 1.4 %collective-permute-done.29.refs_7_ = bf16[4,176,128]{2,1,0:T(8,128)(2,1)S(1)} collective-permute-done((bf16[4,176,128]{2,1,0:T(8,128)(2,1)S(1)}, bf16[4,176,128]{2,1,0:T(8,128)(2,1)S(1)}, u32[]{:S(2)}, u32[]{:S(2)}) %collective-permute-start.29) | collective-permute-done | bytes 180256 | tf_op jit(solution)/shard_map/ppermute | solution.py:240
  69.0 1.3 %shard_map.91 = (bf16[27,4,2,16,128]{4,3,2,1,0:T(8,128)(2,1)}, bf16[2,4,128,256]{3,2,1,0:T(8,128)(2,1)}) custom-call(bf16[4,176,128]{2,1,0:T(8,128)(2,1)S(1)} %pad_maximum_fusion.refs_0_, bf16[4,176,128]{2,1,0:T(8,128)(2,1)S(1)} %collective-permute-done.23.refs_1_, bf16[4,176,128]{2,1,0:T(8,128)(2,1)S(1)} %collective-permute-done.24.refs_2_, ...), custom_call_target="tpu_custom_call" | custom-call | tf_op jit(solution)/shard_map/pallas_call | solution.py:16
  (22 shorter events, 0.1 us)
Async XLA Ops:
  0.6 8.9 %copy-start = (bf16[2,2,2,128,256]{4,3,2,1,0:T(8,128)(2,1)S(1)}, bf16[2,2,2,128,256]{4,3,2,1,0:T(8,128)(2,1)}, u32[]{:S(2)}) copy-start(bf16[2,2,2,128,256]{4,3,2,1,0:T(8,128)(2,1)} %param.9) | copy-start | bytes 1572868
  0.6 1.0 %copy-start.2 = (bf16[4,4,32,32]{3,2,1,0:T(8,128)(2,1)S(1)}, bf16[4,4,32,32]{3,2,1,0:T(8,128)(2,1)}, u32[]{:S(2)}) copy-start(bf16[4,4,32,32]{3,2,1,0:T(8,128)(2,1)} %param.11) | copy-start | bytes 98308
  1.6 4.2 %copy-start.3 = (bf16[1,8,64,128]{3,2,1,0:T(8,128)(2,1)S(1)}, bf16[1,8,64,128]{3,2,1,0:T(8,128)(2,1)}, u32[]{:S(2)}) copy-start(bf16[1,8,64,128]{3,2,1,0:T(8,128)(2,1)} %param.6) | copy-start | bytes 393220
  1.7 6.2 %collective-permute-start.5 = (bf16[2,32,128]{2,1,0:T(8,128)(2,1)S(1)}, bf16[2,32,128]{2,1,0:T(8,128)(2,1)S(1)}, u32[]{:S(2)}, u32[]{:S(2)}) collective-permute-start(bf16[2,32,128]{2,1,0:T(8,128)(2,1)S(1)} %get-tuple-element.51), channel_id=1, source_target_pairs={{0,16},{4,20},{8,24},{12,28},{16,0},{20,4},{24,8},{28,12},{1,17},{... | collective-permute-start | bytes 49160 | tf_op jit(solution)/shard_map/ppermute | solution.py:240
  5.9 7.3 %collective-permute-start = (bf16[32,512]{1,0:T(8,128)(2,1)S(1)}, bf16[32,512]{1,0:T(8,128)(2,1)S(1)}, u32[]{:S(2)}, u32[]{:S(2)}) collective-permute-start(bf16[32,512]{1,0:T(8,128)(2,1)S(1)} %get-tuple-element.47), channel_id=1, source_target_pairs={{0,1},{1,0},{2,3},{3,2},{4,5},{5,4},{6,7},{7,6},{8,9},{9,8},{10,11... | collective-permute-start | bytes 98312 | tf_op jit(solution)/shard_map/ppermute | solution.py:240
  6.0 7.2 %collective-permute-start.1 = (bf16[32,512]{1,0:T(8,128)(2,1)S(1)}, bf16[32,512]{1,0:T(8,128)(2,1)S(1)}, u32[]{:S(2)}, u32[]{:S(2)}) collective-permute-start(bf16[32,512]{1,0:T(8,128)(2,1)S(1)} %get-tuple-element.48), channel_id=1, source_target_pairs={{0,2},{1,3},{2,0},{3,1},{4,6},{5,7},{6,4},{7,5},{8,10},{9,11},{10,... | collective-permute-start | bytes 98312 | tf_op jit(solution)/shard_map/ppermute | solution.py:240
  7.6 5.7 %collective-permute-start.2 = (bf16[32,512]{1,0:T(8,128)(2,1)S(1)}, bf16[32,512]{1,0:T(8,128)(2,1)S(1)}, u32[]{:S(2)}, u32[]{:S(2)}) collective-permute-start(bf16[32,512]{1,0:T(8,128)(2,1)S(1)} %get-tuple-element.49), channel_id=1, source_target_pairs={{0,3},{1,2},{2,1},{3,0},{4,7},{5,6},{6,5},{7,4},{8,11},{9,10},{10,... | collective-permute-start | bytes 98312 | tf_op jit(solution)/shard_map/ppermute | solution.py:240
  7.9 3.8 %collective-permute-start.6 = (bf16[1,2,32,128]{3,2,1,0:T(8,128)(2,1)S(1)}, bf16[1,2,32,128]{3,2,1,0:T(8,128)(2,1)S(1)}, u32[]{:S(2)}, u32[]{:S(2)}) collective-permute-start(bf16[1,2,32,128]{3,2,1,0:T(8,128)(2,1)S(1)} %get-tuple-element.90), channel_id=1, source_target_pairs={{0,8},{4,12},{8,0},{12,4},{16,24},{20,28},{24,16},{28,20},{1,9},{5... | collective-permute-start | bytes 49160 | tf_op jit(solution)/shard_map/ppermute | solution.py:240
  11.7 6.7 %collective-permute-start.7 = (bf16[4,32,128]{2,1,0:T(8,128)(2,1)S(1)}, bf16[4,32,128]{2,1,0:T(8,128)(2,1)S(1)}, u32[]{:S(2)}, u32[]{:S(2)}) collective-permute-start(bf16[4,32,128]{2,1,0:T(8,128)(2,1)S(1)} %maximum_bitcast_fusion.refs_3_), channel_id=1, source_target_pairs={{0,4},{4,0},{8,12},{12,8},{16,20},{20,16},{24,28},{28,24},{1,5},{5... | collective-permute-start | bytes 98312 | tf_op jit(solution)/shard_map/ppermute | solution.py:240
  13.2 5.2 %copy-start.4 = (bf16[1,8,64,128]{3,2,1,0:T(8,128)(2,1)S(1)}, bf16[1,8,64,128]{3,2,1,0:T(8,128)(2,1)}, u32[]{:S(2)}) copy-start(bf16[1,8,64,128]{3,2,1,0:T(8,128)(2,1)} %param.7) | copy-start | bytes 393220
  13.2 5.2 %copy-start.5 = (bf16[1,8,64,128]{3,2,1,0:T(8,128)(2,1)S(1)}, bf16[1,8,64,128]{3,2,1,0:T(8,128)(2,1)}, u32[]{:S(2)}) copy-start(bf16[1,8,64,128]{3,2,1,0:T(8,128)(2,1)} %param.10) | copy-start | bytes 393220
  13.3 7.7 %collective-permute-start.4 = (bf16[4,32,512]{2,1,0:T(8,128)(2,1)S(1)}, bf16[4,32,512]{2,1,0:T(8,128)(2,1)S(1)}, u32[]{:S(2)}, u32[]{:S(2)}) collective-permute-start(bf16[4,32,512]{2,1,0:T(8,128)(2,1)S(1)} %pad_maximum_fusion.1.refs_1_), channel_id=1, source_target_pairs={{4,8},{8,4},{12,16},{16,12},{20,24},{24,20},{5,9},{9,5},{13,17},{1... | collective-permute-start | bytes 393224 | tf_op jit(solution)/shard_map/ppermute | solution.py:246
  14.1 7.4 %collective-permute-start.3 = (bf16[4,32,512]{2,1,0:T(8,128)(2,1)S(1)}, bf16[4,32,512]{2,1,0:T(8,128)(2,1)S(1)}, u32[]{:S(2)}, u32[]{:S(2)}) collective-permute-start(bf16[4,32,512]{2,1,0:T(8,128)(2,1)S(1)} %pad_maximum_fusion.1.refs_1_), channel_id=1, source_target_pairs={{0,4},{4,0},{8,12},{12,8},{16,20},{20,16},{24,28},{28,24},{1,5},{5... | collective-permute-start | bytes 393224 | tf_op jit(solution)/shard_map/ppermute | solution.py:240
  19.1 5.8 %collective-permute-start.10 = (bf16[512,128]{1,0:T(8,128)(2,1)S(1)}, bf16[512,128]{1,0:T(8,128)(2,1)S(1)}, u32[]{:S(2)}, u32[]{:S(2)}) collective-permute-start(bf16[512,128]{1,0:T(8,128)(2,1)S(1)} %get-tuple-element.60.refs_3_), channel_id=1, source_target_pairs={{0,3},{1,2},{2,1},{3,0},{4,7},{5,6},{6,5},{7,4},{8,11},{9,10},{10,... | collective-permute-start | bytes 393224 | tf_op jit(solution)/shard_map/ppermute | solution.py:240
  19.1 8.6 %collective-permute-start.9 = (bf16[512,128]{1,0:T(8,128)(2,1)S(1)}, bf16[512,128]{1,0:T(8,128)(2,1)S(1)}, u32[]{:S(2)}, u32[]{:S(2)}) collective-permute-start(bf16[512,128]{1,0:T(8,128)(2,1)S(1)} %get-tuple-element.60.refs_3_), channel_id=1, source_target_pairs={{0,2},{1,3},{2,0},{3,1},{4,6},{5,7},{6,4},{7,5},{8,10},{9,11},{10,... | collective-permute-start | bytes 393224 | tf_op jit(solution)/shard_map/ppermute | solution.py:240
  20.7 7.0 %collective-permute-start.8 = (bf16[512,128]{1,0:T(8,128)(2,1)S(1)}, bf16[512,128]{1,0:T(8,128)(2,1)S(1)}, u32[]{:S(2)}, u32[]{:S(2)}) collective-permute-start(bf16[512,128]{1,0:T(8,128)(2,1)S(1)} %get-tuple-element.60.refs_3_), channel_id=1, source_target_pairs={{0,1},{1,0},{2,3},{3,2},{4,5},{5,4},{6,7},{7,6},{8,9},{9,8},{10,11... | collective-permute-start | bytes 393224 | tf_op jit(solution)/shard_map/ppermute | solution.py:240
  21.5 32.6 %copy-start.1 = (bf16[3,3,3,128,128]{4,3,2,1,0:T(8,128)(2,1)S(1)}, bf16[3,3,3,128,128]{4,3,2,1,0:T(8,128)(2,1)}, u32[]{:S(2)}) copy-start(bf16[3,3,3,128,128]{4,3,2,1,0:T(8,128)(2,1)} %weight.1) | copy-start | bytes 2654212
  29.3 5.6 %collective-permute-start.11 = (bf16[432,128]{1,0:T(8,128)(2,1)S(1)}, bf16[432,128]{1,0:T(8,128)(2,1)S(1)}, u32[]{:S(2)}, u32[]{:S(2)}) collective-permute-start(bf16[432,128]{1,0:T(8,128)(2,1)S(1)} %get-tuple-element.62), channel_id=1, source_target_pairs={{0,4},{4,0},{8,12},{12,8},{16,20},{20,16},{24,28},{28,24},{1,5},{5... | collective-permute-start | bytes 331784 | tf_op jit(solution)/shard_map/ppermute | solution.py:240
  29.4 1.9 %collective-permute-start.12 = (bf16[256,128]{1,0:T(8,128)(2,1)S(1)}, bf16[256,128]{1,0:T(8,128)(2,1)S(1)}, u32[]{:S(2)}, u32[]{:S(2)}) collective-permute-start(bf16[256,128]{1,0:T(8,128)(2,1)S(1)} %get-tuple-element.64), channel_id=1, source_target_pairs={{0,1},{1,0},{2,3},{3,2},{4,5},{5,4},{6,7},{7,6},{8,9},{9,8},{10,11... | collective-permute-start | bytes 196616 | tf_op jit(solution)/shard_map/ppermute | solution.py:240
  29.5 4.9 %collective-permute-start.13 = (bf16[256,128]{1,0:T(8,128)(2,1)S(1)}, bf16[256,128]{1,0:T(8,128)(2,1)S(1)}, u32[]{:S(2)}, u32[]{:S(2)}) collective-permute-start(bf16[256,128]{1,0:T(8,128)(2,1)S(1)} %get-tuple-element.65), channel_id=1, source_target_pairs={{0,2},{1,3},{2,0},{3,1},{4,6},{5,7},{6,4},{7,5},{8,10},{9,11},{10,... | collective-permute-start | bytes 196616 | tf_op jit(solution)/shard_map/ppermute | solution.py:240
  29.8 5.1 %collective-permute-start.14 = (bf16[256,128]{1,0:T(8,128)(2,1)S(1)}, bf16[256,128]{1,0:T(8,128)(2,1)S(1)}, u32[]{:S(2)}, u32[]{:S(2)}) collective-permute-start(bf16[256,128]{1,0:T(8,128)(2,1)S(1)} %get-tuple-element.66), channel_id=1, source_target_pairs={{0,3},{1,2},{2,1},{3,0},{4,7},{5,6},{6,5},{7,4},{8,11},{9,10},{10,... | collective-permute-start | bytes 196616 | tf_op jit(solution)/shard_map/ppermute | solution.py:240
  35.0 14.6 %collective-permute-start.19 = (bf16[10,64,128]{2,1,0:T(8,128)(2,1)S(1)}, bf16[10,64,128]{2,1,0:T(8,128)(2,1)S(1)}, u32[]{:S(2)}, u32[]{:S(2)}) collective-permute-start(bf16[10,64,128]{2,1,0:T(8,128)(2,1)S(1)} %get-tuple-element.76.own), channel_id=1, source_target_pairs={{4,8},{8,4},{12,16},{16,12},{20,24},{24,20},{5,9},{9,5},{13,17},{1... | collective-permute-start | bytes 491528 | tf_op jit(solution)/shard_map/ppermute | solution.py:246
  35.6 13.9 %collective-permute-start.18 = (bf16[10,64,128]{2,1,0:T(8,128)(2,1)S(1)}, bf16[10,64,128]{2,1,0:T(8,128)(2,1)S(1)}, u32[]{:S(2)}, u32[]{:S(2)}) collective-permute-start(bf16[10,64,128]{2,1,0:T(8,128)(2,1)S(1)} %get-tuple-element.76.own), channel_id=1, source_target_pairs={{0,4},{4,0},{8,12},{12,8},{16,20},{20,16},{24,28},{28,24},{1,5},{5... | collective-permute-start | bytes 491528 | tf_op jit(solution)/shard_map/ppermute | solution.py:240
  39.9 6.2 %collective-permute-start.15 = (bf16[176,128]{1,0:T(8,128)(2,1)S(1)}, bf16[176,128]{1,0:T(8,128)(2,1)S(1)}, u32[]{:S(2)}, u32[]{:S(2)}) collective-permute-start(bf16[176,128]{1,0:T(8,128)(2,1)S(1)} %get-tuple-element.73), channel_id=1, source_target_pairs={{0,8},{4,12},{8,0},{12,4},{16,24},{20,28},{24,16},{28,20},{1,9},{5... | collective-permute-start | bytes 135176 | tf_op jit(solution)/shard_map/ppermute | solution.py:240
  41.6 5.6 %collective-permute-start.16 = (bf16[176,128]{1,0:T(8,128)(2,1)S(1)}, bf16[176,128]{1,0:T(8,128)(2,1)S(1)}, u32[]{:S(2)}, u32[]{:S(2)}) collective-permute-start(bf16[176,128]{1,0:T(8,128)(2,1)S(1)} %get-tuple-element.74), channel_id=1, source_target_pairs={{0,16},{4,20},{8,24},{12,28},{16,0},{20,4},{24,8},{28,12},{1,17},{... | collective-permute-start | bytes 135176 | tf_op jit(solution)/shard_map/ppermute | solution.py:240
  43.0 6.5 %collective-permute-start.17 = (bf16[176,128]{1,0:T(8,128)(2,1)S(1)}, bf16[176,128]{1,0:T(8,128)(2,1)S(1)}, u32[]{:S(2)}, u32[]{:S(2)}) collective-permute-start(bf16[176,128]{1,0:T(8,128)(2,1)S(1)} %get-tuple-element.75), channel_id=1, source_target_pairs={{0,24},{4,28},{8,16},{12,20},{16,8},{20,12},{24,0},{28,4},{1,25},{... | collective-permute-start | bytes 135176 | tf_op jit(solution)/shard_map/ppermute | solution.py:240
  49.7 6.4 %collective-permute-start.22 = (bf16[176,128]{1,0:T(8,128)(2,1)S(1)}, bf16[176,128]{1,0:T(8,128)(2,1)S(1)}, u32[]{:S(2)}, u32[]{:S(2)}) collective-permute-start(bf16[176,128]{1,0:T(8,128)(2,1)S(1)} %multiply_convert_fusion), channel_id=1, source_target_pairs={{0,24},{4,28},{8,16},{12,20},{16,8},{20,12},{24,0},{28,4},{1,25},{... | collective-permute-start | bytes 135176 | tf_op jit(solution)/shard_map/ppermute | solution.py:240
  50.6 5.5 %collective-permute-start.21 = (bf16[176,128]{1,0:T(8,128)(2,1)S(1)}, bf16[176,128]{1,0:T(8,128)(2,1)S(1)}, u32[]{:S(2)}, u32[]{:S(2)}) collective-permute-start(bf16[176,128]{1,0:T(8,128)(2,1)S(1)} %multiply_convert_fusion), channel_id=1, source_target_pairs={{0,16},{4,20},{8,24},{12,28},{16,0},{20,4},{24,8},{28,12},{1,17},{... | collective-permute-start | bytes 135176 | tf_op jit(solution)/shard_map/ppermute | solution.py:240
  51.3 5.3 %collective-permute-start.20 = (bf16[176,128]{1,0:T(8,128)(2,1)S(1)}, bf16[176,128]{1,0:T(8,128)(2,1)S(1)}, u32[]{:S(2)}, u32[]{:S(2)}) collective-permute-start(bf16[176,128]{1,0:T(8,128)(2,1)S(1)} %multiply_convert_fusion), channel_id=1, source_target_pairs={{0,8},{4,12},{8,0},{12,4},{16,24},{20,28},{24,16},{28,20},{1,9},{5... | collective-permute-start | bytes 135176 | tf_op jit(solution)/shard_map/ppermute | solution.py:240
  56.6 5.6 %collective-permute-start.26 = (bf16[4,176,128]{2,1,0:T(8,128)(2,1)S(1)}, bf16[4,176,128]{2,1,0:T(8,128)(2,1)S(1)}, u32[]{:S(2)}, u32[]{:S(2)}) collective-permute-start(bf16[4,176,128]{2,1,0:T(8,128)(2,1)S(1)} %pad_maximum_fusion.refs_0_), channel_id=1, source_target_pairs={{0,4},{4,0},{8,12},{12,8},{16,20},{20,16},{24,28},{28,24},{1,5},{5... | collective-permute-start | bytes 540680 | tf_op jit(solution)/shard_map/ppermute | solution.py:240
  57.8 7.2 %collective-permute-start.24 = (bf16[4,176,128]{2,1,0:T(8,128)(2,1)S(1)}, bf16[4,176,128]{2,1,0:T(8,128)(2,1)S(1)}, u32[]{:S(2)}, u32[]{:S(2)}) collective-permute-start(bf16[4,176,128]{2,1,0:T(8,128)(2,1)S(1)} %pad_maximum_fusion.refs_0_), channel_id=1, source_target_pairs={{0,2},{1,3},{2,0},{3,1},{4,6},{5,7},{6,4},{7,5},{8,10},{9,11},{10,... | collective-permute-start | bytes 540680 | tf_op jit(solution)/shard_map/ppermute | solution.py:240
  62.1 5.5 %collective-permute-start.28 = (bf16[4,176,128]{2,1,0:T(8,128)(2,1)S(1)}, bf16[4,176,128]{2,1,0:T(8,128)(2,1)S(1)}, u32[]{:S(2)}, u32[]{:S(2)}) collective-permute-start(bf16[4,176,128]{2,1,0:T(8,128)(2,1)S(1)} %collective-permute-done.26.refs_4_), channel_id=1, source_target_pairs={{0,2},{1,3},{2,0},{3,1},{4,6},{5,7},{6,4},{7,5},{8,10},{9,11},{10,... | collective-permute-start | bytes 540680 | tf_op jit(solution)/shard_map/ppermute | solution.py:240
  62.6 5.0 %collective-permute-start.23 = (bf16[4,176,128]{2,1,0:T(8,128)(2,1)S(1)}, bf16[4,176,128]{2,1,0:T(8,128)(2,1)S(1)}, u32[]{:S(2)}, u32[]{:S(2)}) collective-permute-start(bf16[4,176,128]{2,1,0:T(8,128)(2,1)S(1)} %pad_maximum_fusion.refs_0_), channel_id=1, source_target_pairs={{0,1},{1,0},{2,3},{3,2},{4,5},{5,4},{6,7},{7,6},{8,9},{9,8},{10,11... | collective-permute-start | bytes 540680 | tf_op jit(solution)/shard_map/ppermute | solution.py:240
  62.6 5.0 %collective-permute-start.27 = (bf16[4,176,128]{2,1,0:T(8,128)(2,1)S(1)}, bf16[4,176,128]{2,1,0:T(8,128)(2,1)S(1)}, u32[]{:S(2)}, u32[]{:S(2)}) collective-permute-start(bf16[4,176,128]{2,1,0:T(8,128)(2,1)S(1)} %collective-permute-done.26.refs_4_), channel_id=1, source_target_pairs={{0,1},{1,0},{2,3},{3,2},{4,5},{5,4},{6,7},{7,6},{8,9},{9,8},{10,11... | collective-permute-start | bytes 540680 | tf_op jit(solution)/shard_map/ppermute | solution.py:240
  65.0 2.6 %collective-permute-start.25 = (bf16[4,176,128]{2,1,0:T(8,128)(2,1)S(1)}, bf16[4,176,128]{2,1,0:T(8,128)(2,1)S(1)}, u32[]{:S(2)}, u32[]{:S(2)}) collective-permute-start(bf16[4,176,128]{2,1,0:T(8,128)(2,1)S(1)} %collective-permute-done.24.refs_2_), channel_id=1, source_target_pairs={{0,1},{1,0},{2,3},{3,2},{4,5},{5,4},{6,7},{7,6},{8,9},{9,8},{10,11... | collective-permute-start | bytes 540680 | tf_op jit(solution)/shard_map/ppermute | solution.py:240
  67.6 1.4 %collective-permute-start.29 = (bf16[4,176,128]{2,1,0:T(8,128)(2,1)S(1)}, bf16[4,176,128]{2,1,0:T(8,128)(2,1)S(1)}, u32[]{:S(2)}, u32[]{:S(2)}) collective-permute-start(bf16[4,176,128]{2,1,0:T(8,128)(2,1)S(1)} %collective-permute-done.28.refs_6_), channel_id=1, source_target_pairs={{0,1},{1,0},{2,3},{3,2},{4,5},{5,4},{6,7},{7,6},{8,9},{9,8},{10,11... | collective-permute-start | bytes 540680 | tf_op jit(solution)/shard_map/ppermute | solution.py:240

commit v15 on v13

--- a/solution.py
+++ b/solution.py
@@ -240,10 +240,14 @@
     return lax.ppermute(value, axis, [(i, i ^ code) for i in range(lax.axis_size(axis))])
 
 
-def neighbours(value):
+def even_pairs(value):
+    return swapped(value, "gz", 1)
+
+
+def odd_pairs(value):
     last = lax.axis_size("gz") - 1
-    odd = [(i + d, i + 1 - d) for i in range(1, last, 2) for d in range(2)]
-    return swapped(value, "gz", 1), lax.ppermute(value, "gz", odd)
+    pairs = [(i + d, i + 1 - d) for i in range(1, last, 2) for d in range(2)]
+    return lax.ppermute(value, "gz", pairs)
 
 
 def exchanged(value, axis):
@@ -298,6 +302,7 @@
     )
     level_t = [swapped(value, "gy", code) if code else value for code, value in enumerate(level_t)]
     level_t = jnp.stack(level_t)
+    even = even_pairs(level_t)
     *deep_t, level_t = lax.optimization_barrier((*deep_t, level_t))
     down_slice = lax.dynamic_index_in_dim(down_weight, parity, 0, keepdims=False)
     grad, down, *others = call(
@@ -315,7 +320,7 @@
     )
     shared = [swapped(grad, "gy", code) if code else grad for code in range(n_gy)]
     shared[1], level_t = lax.optimization_barrier((shared[1], level_t))
-    even, odd = neighbours(level_t)
+    odd = odd_pairs(level_t)
     keep, send, near = call(
         lambda *refs: weight_kernel(n_gy, (rows, cols, channels), *refs),
         (
@@ -335,8 +340,7 @@
     )
     send, *others = lax.optimization_barrier((send, *others))
     downs = [down] + [swapped(value, "gy", code + 1) for code, value in enumerate(others)]
-    send, near = lax.optimization_barrier((swapped(send, "gz", 1), near))
-    near_even, near_odd = neighbours(near)
+    send = swapped(send, "gz", 1)
 
     def input_part(near_even, near_odd):
         return call(
@@ -361,8 +365,10 @@
             *downs,
             scratch=[pltpu.VMEM((n_z, piece, channels), F32)],
         )
+        own, near, *pieces = lax.optimization_barrier((own, near, *pieces))
+        near_even = even_pairs(near)
         pieces = [swapped(value, "gz", 2 * code + 2) for code, value in enumerate(pieces)]
-        *pieces, near_even, near_odd = lax.optimization_barrier((*pieces, near_even, near_odd))
+        *pieces, near_even = lax.optimization_barrier((*pieces, near_even))
         total = own + sum(value.astype(F32) for value in pieces)
         first = lax.axis_index("gz") // 2 * piece
     else:
@@ -373,15 +379,17 @@
             total = total + swapped(total, "gz", code)
             code //= 2
         first = 0
+        near_even = even_pairs(near)
     row = first + lax.broadcasted_iota(jnp.int32, total.shape, 0)
     scale = jnp.where(
         row < 27 * half, 1 / math.sqrt(cell_total), 1 / math.sqrt(cell_total // 8)
     )
     total = (total * scale).astype(BF16)
+    total, near = lax.optimization_barrier((total, near))
+    near_odd = odd_pairs(near)
     input_grad = input_part(near_even, near_odd)
     if n_z <= 4:
         pieces = [swapped(total, "gz", 2 * code) if code else total for code in range(n_z)]
-        *pieces, input_grad = lax.optimization_barrier((*pieces, input_grad))
         total = jnp.stack(pieces)
     else:
         total = total[None]
@@ -391,6 +399,8 @@
         line = [block]
         code = n_gy // 2
         while code:
+            if code == 1 and index == 1:
+                input_grad, *line = lax.optimization_barrier((input_grad, *line))
             line = line + [swapped(value, "gy", code) for value in line]
             code //= 2
         blocks += [line[reversed_bits(place, n_gy)] for place in range(n_gy)]

time: 70.8 us -> 73.6 us (1.040)
  the two profiles are of different devices: /device:TPU:0 before, /device:TPU:9 now
where the time goes in v15:
time: 73.6 us; the launch traced here: 73.4 us
  starting transfers between devices  42.1 us (57%)
  waiting for transfers between devices  23.9 us (32%)
  Pallas kernels  5.42 us (7%)
  local copies, waits for them, and re-layouts  1 us (1%)
  between operations  0.78 us (1%)
    ppermute x28, starting transfers between devices, swapped(): lax.ppermute(value, axis, [(i, i ^ code) for i in range(lax.axis_size(axi...  38.1 us
    ppermute x28, waiting for transfers between devices, swapped(): lax.ppermute(value, axis, [(i, i ^ code) for i in range(lax.axis_size(axi...  23 us
    pallas_call x7, Pallas kernels, call(): pl.pallas_call(kernel, out_shape=out_shape, scratch_shapes=list(scratch),...  5.42 us
    ppermute x2, starting transfers between devices, odd_pairs(): return lax.ppermute(value, 'gz', pairs)  3.98 us
  transfers between devices with their start and end apart: 30, of which 17 were waited for; matrix products, arithmetic and copies ran while one was open for 0% of the time, Pallas kernels for 3%

profile of v15, /device:TPU:9, one launch (start us, length us, event | category | flops | bytes accessed | tf_op | source)
XLA Modules:
  0.0 73.4 jit_solution(3090050952232081532)
XLA Ops:
  0.6 0.0 copy-start
  0.7 1.0 %copy-done.2 = bf16[4,4,32,32]{3,2,1,0:T(8,128)(2,1)S(1)} copy-done((bf16[4,4,32,32]{3,2,1,0:T(8,128)(2,1)S(1)}, bf16[4,4,32,32]{3,2,1,0:T(8,128)(2,1)}, u32[]{:S(2)}) %copy-start.2) | copy-done | bytes 32792
  1.6 0.1 shard_map.86
  1.7 2.4 %collective-permute-start.4 = (bf16[2,32,128]{2,1,0:T(8,128)(2,1)S(1)}, bf16[2,32,128]{2,1,0:T(8,128)(2,1)S(1)}, u32[]{:S(2)}, u32[]{:S(2)}) collective-permute-start(bf16[2,32,128]{2,1,0:T(8,128)(2,1)S(1)} %get-tuple-element.51), channel_id=1, source_target_pairs={{0,16},{4,20},{8,24},{12,28},{16,0},{20,4},{24,8},{28,12},{1,17},{... | collective-permute-start | bytes 49160 | tf_op jit(solution)/shard_map/ppermute | solution.py:240
  4.1 0.1 shard_map.85
  4.2 1.0 %collective-permute-start = (bf16[32,512]{1,0:T(8,128)(2,1)S(1)}, bf16[32,512]{1,0:T(8,128)(2,1)S(1)}, u32[]{:S(2)}, u32[]{:S(2)}) collective-permute-start(bf16[32,512]{1,0:T(8,128)(2,1)S(1)} %get-tuple-element.47), channel_id=1, source_target_pairs={{0,1},{1,0},{2,3},{3,2},{4,5},{5,4},{6,7},{7,6},{8,9},{9,8},{10,11... | collective-permute-start | bytes 98312 | tf_op jit(solution)/shard_map/ppermute | solution.py:240
  5.2 1.2 %collective-permute-start.1 = (bf16[32,512]{1,0:T(8,128)(2,1)S(1)}, bf16[32,512]{1,0:T(8,128)(2,1)S(1)}, u32[]{:S(2)}, u32[]{:S(2)}) collective-permute-start(bf16[32,512]{1,0:T(8,128)(2,1)S(1)} %get-tuple-element.48), channel_id=1, source_target_pairs={{0,2},{1,3},{2,0},{3,1},{4,6},{5,7},{6,4},{7,5},{8,10},{9,11},{10,... | collective-permute-start | bytes 98312 | tf_op jit(solution)/shard_map/ppermute | solution.py:240
  6.4 0.5 collective-permute-start.2
  6.9 0.0 collective-permute-done.4
  6.9 0.2 collective-permute-start.5
  7.2 2.5 %collective-permute-done.5 = bf16[1,2,32,128]{3,2,1,0:T(8,128)(2,1)S(1)} collective-permute-done((bf16[1,2,32,128]{3,2,1,0:T(8,128)(2,1)S(1)}, bf16[1,2,32,128]{3,2,1,0:T(8,128)(2,1)S(1)}, u32[]{:S(2)}, u32[]{:S(2)}) %collective-permute-start.5) | collective-permute-done | bytes 16416 | tf_op jit(solution)/shard_map/ppermute | solution.py:240
  9.7 1.2 %collective-permute-start.6 = (bf16[4,32,128]{2,1,0:T(8,128)(2,1)S(1)}, bf16[4,32,128]{2,1,0:T(8,128)(2,1)S(1)}, u32[]{:S(2)}, u32[]{:S(2)}) collective-permute-start(bf16[4,32,128]{2,1,0:T(8,128)(2,1)S(1)} %maximum_bitcast_fusion.refs_3_), channel_id=1, source_target_pairs={{0,4},{4,0},{8,12},{12,8},{16,20},{20,16},{24,28},{28,24},{1,5},{5... | collective-permute-start | bytes 98312 | tf_op jit(solution)/shard_map/ppermute | solution.py:240
  11.0 0.0 collective-permute-done.1
  11.0 0.0 collective-permute-done.2
  11.0 0.0 copy-start.4
  11.0 0.0 copy-start.5
  11.0 1.5 %collective-permute-done.6.refs_4_ = bf16[4,32,128]{2,1,0:T(8,128)(2,1)S(1)} collective-permute-done((bf16[4,32,128]{2,1,0:T(8,128)(2,1)S(1)}, bf16[4,32,128]{2,1,0:T(8,128)(2,1)S(1)}, u32[]{:S(2)}, u32[]{:S(2)}) %collective-permute-start.6) | collective-permute-done | bytes 32800 | tf_op jit(solution)/shard_map/ppermute | solution.py:240
  12.5 0.6 shard_map.87
  13.1 2.4 %collective-permute-start.7 = (bf16[512,128]{1,0:T(8,128)(2,1)S(1)}, bf16[512,128]{1,0:T(8,128)(2,1)S(1)}, u32[]{:S(2)}, u32[]{:S(2)}) collective-permute-start(bf16[512,128]{1,0:T(8,128)(2,1)S(1)} %get-tuple-element.54.refs_3_), channel_id=1, source_target_pairs={{0,1},{1,0},{2,3},{3,2},{4,5},{5,4},{6,7},{7,6},{8,9},{9,8},{10,11... | collective-permute-start | bytes 393224 | tf_op jit(solution)/shard_map/ppermute | solution.py:240
  15.5 1.3 %collective-permute-start.3 = (bf16[4,32,512]{2,1,0:T(8,128)(2,1)S(1)}, bf16[4,32,512]{2,1,0:T(8,128)(2,1)S(1)}, u32[]{:S(2)}, u32[]{:S(2)}) collective-permute-start(bf16[4,32,512]{2,1,0:T(8,128)(2,1)S(1)} %pad_maximum_fusion.1.refs_1_), channel_id=1, source_target_pairs={{0,4},{4,0},{8,12},{12,8},{16,20},{20,16},{24,28},{28,24},{1,5},{5... | collective-permute-start | bytes 393224 | tf_op jit(solution)/shard_map/ppermute | solution.py:240
  16.8 1.5 %collective-permute-start.10 = (bf16[512,128]{1,0:T(8,128)(2,1)S(1)}, bf16[512,128]{1,0:T(8,128)(2,1)S(1)}, u32[]{:S(2)}, u32[]{:S(2)}) collective-permute-start(bf16[512,128]{1,0:T(8,128)(2,1)S(1)} %get-tuple-element.54.refs_3_), channel_id=1, source_target_pairs={{0,3},{1,2},{2,1},{3,0},{4,7},{5,6},{6,5},{7,4},{8,11},{9,10},{10,... | collective-permute-start | bytes 393224 | tf_op jit(solution)/shard_map/ppermute | solution.py:240
  18.2 0.2 collective-permute-start.9
  18.5 2.0 %collective-permute-start.8 = (bf16[4,32,512]{2,1,0:T(8,128)(2,1)S(1)}, bf16[4,32,512]{2,1,0:T(8,128)(2,1)S(1)}, u32[]{:S(2)}, u32[]{:S(2)}) collective-permute-start(bf16[4,32,512]{2,1,0:T(8,128)(2,1)S(1)} %pad_maximum_fusion.1.refs_1_), channel_id=1, source_target_pairs={{4,8},{8,4},{12,16},{16,12},{20,24},{24,20},{5,9},{9,5},{13,17},{1... | collective-permute-start | bytes 393224 | tf_op jit(solution)/shard_map/ppermute | solution.py:250
  20.5 0.1 collective-permute-done.3.refs_0_
  20.6 2.0 %collective-permute-done.10.refs_6_ = bf16[512,128]{1,0:T(8,128)(2,1)S(1)} collective-permute-done((bf16[512,128]{1,0:T(8,128)(2,1)S(1)}, bf16[512,128]{1,0:T(8,128)(2,1)S(1)}, u32[]{:S(2)}, u32[]{:S(2)}) %collective-permute-start.10) | collective-permute-done | bytes 131104 | tf_op jit(solution)/shard_map/ppermute | solution.py:240
  22.6 2.4 %collective-permute-done.9.refs_5_ = bf16[512,128]{1,0:T(8,128)(2,1)S(1)} collective-permute-done((bf16[512,128]{1,0:T(8,128)(2,1)S(1)}, bf16[512,128]{1,0:T(8,128)(2,1)S(1)}, u32[]{:S(2)}, u32[]{:S(2)}) %collective-permute-start.9) | collective-permute-done | bytes 131104 | tf_op jit(solution)/shard_map/ppermute | solution.py:240
  25.0 0.9 %collective-permute-done.8.refs_2_ = bf16[4,32,512]{2,1,0:T(8,128)(2,1)S(1)} collective-permute-done((bf16[4,32,512]{2,1,0:T(8,128)(2,1)S(1)}, bf16[4,32,512]{2,1,0:T(8,128)(2,1)S(1)}, u32[]{:S(2)}, u32[]{:S(2)}) %collective-permute-start.8) | collective-permute-done | bytes 131104 | tf_op jit(solution)/shard_map/ppermute | solution.py:250
  25.9 1.5 %shard_map.88 = (f32[432,128]{1,0:T(8,128)S(1)}, bf16[432,128]{1,0:T(8,128)(2,1)S(1)}, bf16[10,64,128]{2,1,0:T(8,128)(2,1)S(1)}) custom-call(bf16[4,32,512]{2,1,0:T(8,128)(2,1)S(1)} %collective-permute-done.3.refs_0_, bf16[4,32,512]{2,1,0:T(8,128)(2,1)S(1)} %pad_maximum_fusion.1.refs_1_, bf16[4,32,512]{2,1,0:T(8,128)(2,1)S(1)} %collective-permute-done.8.refs_2_, ...), custom_call_target="tpu_custom_call" | custom-call | tf_op jit(solution)/shard_map/pallas_call | solution.py:16
  27.4 0.0 copy-start.1
  27.4 0.3 collective-permute-start.11
  27.7 1.6 %collective-permute-start.12 = (bf16[256,128]{1,0:T(8,128)(2,1)S(1)}, bf16[256,128]{1,0:T(8,128)(2,1)S(1)}, u32[]{:S(2)}, u32[]{:S(2)}) collective-permute-start(bf16[256,128]{1,0:T(8,128)(2,1)S(1)} %get-tuple-element.65), channel_id=1, source_target_pairs={{0,1},{1,0},{2,3},{3,2},{4,5},{5,4},{6,7},{7,6},{8,9},{9,8},{10,11... | collective-permute-start | bytes 196616 | tf_op jit(solution)/shard_map/ppermute | solution.py:240
  29.3 1.2 %collective-permute-start.13 = (bf16[256,128]{1,0:T(8,128)(2,1)S(1)}, bf16[256,128]{1,0:T(8,128)(2,1)S(1)}, u32[]{:S(2)}, u32[]{:S(2)}) collective-permute-start(bf16[256,128]{1,0:T(8,128)(2,1)S(1)} %get-tuple-element.66), channel_id=1, source_target_pairs={{0,2},{1,3},{2,0},{3,1},{4,6},{5,7},{6,4},{7,5},{8,10},{9,11},{10,... | collective-permute-start | bytes 196616 | tf_op jit(solution)/shard_map/ppermute | solution.py:240
  30.5 0.4 collective-permute-start.14
  30.9 2.1 %collective-permute-done.13.rest_2_ = bf16[256,128]{1,0:T(8,128)(2,1)S(1)} collective-permute-done((bf16[256,128]{1,0:T(8,128)(2,1)S(1)}, bf16[256,128]{1,0:T(8,128)(2,1)S(1)}, u32[]{:S(2)}, u32[]{:S(2)}) %collective-permute-start.13) | collective-permute-done | bytes 65568 | tf_op jit(solution)/shard_map/ppermute | solution.py:240
  33.0 1.5 %collective-permute-done.14.rest_3_ = bf16[256,128]{1,0:T(8,128)(2,1)S(1)} collective-permute-done((bf16[256,128]{1,0:T(8,128)(2,1)S(1)}, bf16[256,128]{1,0:T(8,128)(2,1)S(1)}, u32[]{:S(2)}, u32[]{:S(2)}) %collective-permute-start.14) | collective-permute-done | bytes 65568 | tf_op jit(solution)/shard_map/ppermute | solution.py:240
  34.5 0.1 shard_map.89
  34.6 1.3 %collective-permute-start.18 = (bf16[10,64,128]{2,1,0:T(8,128)(2,1)S(1)}, bf16[10,64,128]{2,1,0:T(8,128)(2,1)S(1)}, u32[]{:S(2)}, u32[]{:S(2)}) collective-permute-start(bf16[10,64,128]{2,1,0:T(8,128)(2,1)S(1)} %get-tuple-element.82.own), channel_id=1, source_target_pairs={{0,4},{4,0},{8,12},{12,8},{16,20},{20,16},{24,28},{28,24},{1,5},{5... | collective-permute-start | bytes 491528 | tf_op jit(solution)/shard_map/ppermute | solution.py:240
  35.9 2.4 %collective-permute-start.16 = (bf16[176,128]{1,0:T(8,128)(2,1)S(1)}, bf16[176,128]{1,0:T(8,128)(2,1)S(1)}, u32[]{:S(2)}, u32[]{:S(2)}) collective-permute-start(bf16[176,128]{1,0:T(8,128)(2,1)S(1)} %get-tuple-element.74), channel_id=1, source_target_pairs={{0,16},{4,20},{8,24},{12,28},{16,0},{20,4},{24,8},{28,12},{1,17},{... | collective-permute-start | bytes 135176 | tf_op jit(solution)/shard_map/ppermute | solution.py:240
  38.3 0.2 collective-permute-start.17
  38.5 0.5 collective-permute-done.15
  39.1 1.2 %collective-permute-done.16 = bf16[176,128]{1,0:T(8,128)(2,1)S(1)} collective-permute-done((bf16[176,128]{1,0:T(8,128)(2,1)S(1)}, bf16[176,128]{1,0:T(8,128)(2,1)S(1)}, u32[]{:S(2)}, u32[]{:S(2)}) %collective-permute-start.16) | collective-permute-done | bytes 45088 | tf_op jit(solution)/shard_map/ppermute | solution.py:240
  40.3 1.7 %collective-permute-done.17 = bf16[176,128]{1,0:T(8,128)(2,1)S(1)} collective-permute-done((bf16[176,128]{1,0:T(8,128)(2,1)S(1)}, bf16[176,128]{1,0:T(8,128)(2,1)S(1)}, u32[]{:S(2)}, u32[]{:S(2)}) %collective-permute-start.17) | collective-permute-done | bytes 45088 | tf_op jit(solution)/shard_map/ppermute | solution.py:240
  42.0 0.1 multiply_convert_fusion
  42.1 0.3 collective-permute-start.22
  42.4 4.3 %collective-permute-start.21 = (bf16[176,128]{1,0:T(8,128)(2,1)S(1)}, bf16[176,128]{1,0:T(8,128)(2,1)S(1)}, u32[]{:S(2)}, u32[]{:S(2)}) collective-permute-start(bf16[176,128]{1,0:T(8,128)(2,1)S(1)} %multiply_convert_fusion), channel_id=1, source_target_pairs={{0,16},{4,20},{8,24},{12,28},{16,0},{20,4},{24,8},{28,12},{1,17},{... | collective-permute-start | bytes 135176 | tf_op jit(solution)/shard_map/ppermute | solution.py:240
  46.7 0.0 collective-permute-done.22
  46.7 2.0 %collective-permute-done.21 = bf16[176,128]{1,0:T(8,128)(2,1)S(1)} collective-permute-done((bf16[176,128]{1,0:T(8,128)(2,1)S(1)}, bf16[176,128]{1,0:T(8,128)(2,1)S(1)}, u32[]{:S(2)}, u32[]{:S(2)}) %collective-permute-start.21) | collective-permute-done | bytes 45088 | tf_op jit(solution)/shard_map/ppermute | solution.py:240
  48.7 1.3 %collective-permute-done.20 = bf16[176,128]{1,0:T(8,128)(2,1)S(1)} collective-permute-done((bf16[176,128]{1,0:T(8,128)(2,1)S(1)}, bf16[176,128]{1,0:T(8,128)(2,1)S(1)}, u32[]{:S(2)}, u32[]{:S(2)}) %collective-permute-start.20) | collective-permute-done | bytes 45088 | tf_op jit(solution)/shard_map/ppermute | solution.py:240
  50.0 0.2 collective-permute-start.23
  50.2 1.2 %collective-permute-start.26 = (bf16[4,176,128]{2,1,0:T(8,128)(2,1)S(1)}, bf16[4,176,128]{2,1,0:T(8,128)(2,1)S(1)}, u32[]{:S(2)}, u32[]{:S(2)}) collective-permute-start(bf16[4,176,128]{2,1,0:T(8,128)(2,1)S(1)} %pad_maximum_fusion.refs_0_), channel_id=1, source_target_pairs={{0,2},{1,3},{2,0},{3,1},{4,6},{5,7},{6,4},{7,5},{8,10},{9,11},{10,... | collective-permute-start | bytes 540680 | tf_op jit(solution)/shard_map/ppermute | solution.py:240
  51.4 3.0 %collective-permute-done.23.refs_4_ = bf16[4,176,128]{2,1,0:T(8,128)(2,1)S(1)} collective-permute-done((bf16[4,176,128]{2,1,0:T(8,128)(2,1)S(1)}, bf16[4,176,128]{2,1,0:T(8,128)(2,1)S(1)}, u32[]{:S(2)}, u32[]{:S(2)}) %collective-permute-start.23) | collective-permute-done | bytes 180256 | tf_op jit(solution)/shard_map/ppermute | solution.py:240
  54.4 1.2 %collective-permute-start.24 = (bf16[4,176,128]{2,1,0:T(8,128)(2,1)S(1)}, bf16[4,176,128]{2,1,0:T(8,128)(2,1)S(1)}, u32[]{:S(2)}, u32[]{:S(2)}) collective-permute-start(bf16[4,176,128]{2,1,0:T(8,128)(2,1)S(1)} %collective-permute-done.23.refs_4_), channel_id=1, source_target_pairs={{0,2},{1,3},{2,0},{3,1},{4,6},{5,7},{6,4},{7,5},{8,10},{9,11},{10,... | collective-permute-start | bytes 540680 | tf_op jit(solution)/shard_map/ppermute | solution.py:240
  55.6 2.0 %collective-permute-start.19 = (bf16[10,64,128]{2,1,0:T(8,128)(2,1)S(1)}, bf16[10,64,128]{2,1,0:T(8,128)(2,1)S(1)}, u32[]{:S(2)}, u32[]{:S(2)}) collective-permute-start(bf16[10,64,128]{2,1,0:T(8,128)(2,1)S(1)} %get-tuple-element.82.own), channel_id=1, source_target_pairs={{4,8},{8,4},{12,16},{16,12},{20,24},{24,20},{5,9},{9,5},{13,17},{1... | collective-permute-start | bytes 491528 | tf_op jit(solution)/shard_map/ppermute | solution.py:250
  57.6 4.9 %collective-permute-start.25 = (bf16[4,176,128]{2,1,0:T(8,128)(2,1)S(1)}, bf16[4,176,128]{2,1,0:T(8,128)(2,1)S(1)}, u32[]{:S(2)}, u32[]{:S(2)}) collective-permute-start(bf16[4,176,128]{2,1,0:T(8,128)(2,1)S(1)} %pad_maximum_fusion.refs_0_), channel_id=1, source_target_pairs={{0,1},{1,0},{2,3},{3,2},{4,5},{5,4},{6,7},{7,6},{8,9},{9,8},{10,11... | collective-permute-start | bytes 540680 | tf_op jit(solution)/shard_map/ppermute | solution.py:240
  62.6 0.0 collective-permute-done.19.odd
  62.6 1.7 %shard_map.90 = bf16[8,64,128]{2,1,0:T(8,128)(2,1)} custom-call(bf16[10,64,128]{2,1,0:T(8,128)(2,1)S(1)} %collective-permute-done.18.even, bf16[10,64,128]{2,1,0:T(8,128)(2,1)S(1)} %get-tuple-element.82.own, bf16[10,64,128]{2,1,0:T(8,128)(2,1)S(1)} %collective-permute-done.19.odd, bf16[3,3,3,128,128]{4,3,2,1,0:T(8,128)(2,1)S(1)} %copy-done.1), custom_call_target="tpu_custom_call" | custom-call | tf_op jit(solution)/shard_map/pallas_call | solution.py:16
  64.3 0.0 collective-permute-done.26.refs_2_
  64.4 6.1 %collective-permute-start.27 = (bf16[4,176,128]{2,1,0:T(8,128)(2,1)S(1)}, bf16[4,176,128]{2,1,0:T(8,128)(2,1)S(1)}, u32[]{:S(2)}, u32[]{:S(2)}) collective-permute-start(bf16[4,176,128]{2,1,0:T(8,128)(2,1)S(1)} %collective-permute-done.26.refs_2_), channel_id=1, source_target_pairs={{0,1},{1,0},{2,3},{3,2},{4,5},{5,4},{6,7},{7,6},{8,9},{9,8},{10,11... | collective-permute-start | bytes 540680 | tf_op jit(solution)/shard_map/ppermute | solution.py:240
  70.4 0.1 collective-permute-start.28
  70.5 0.4 collective-permute-start.29
  71.0 0.5 collective-permute-done.27.refs_3_
  71.5 0.4 collective-permute-done.28.refs_5_
  71.9 0.3 collective-permute-done.29.refs_7_
  72.1 1.3 %shard_map.91 = (bf16[27,4,2,16,128]{4,3,2,1,0:T(8,128)(2,1)}, bf16[2,4,128,256]{3,2,1,0:T(8,128)(2,1)}) custom-call(bf16[4,176,128]{2,1,0:T(8,128)(2,1)S(1)} %pad_maximum_fusion.refs_0_, bf16[4,176,128]{2,1,0:T(8,128)(2,1)S(1)} %collective-permute-done.25.refs_1_, bf16[4,176,128]{2,1,0:T(8,128)(2,1)S(1)} %collective-permute-done.26.refs_2_, ...), custom_call_target="tpu_custom_call" | custom-call | tf_op jit(solution)/shard_map/pallas_call | solution.py:16
  (22 shorter events, 0.1 us)
Async XLA Ops:
  0.6 6.5 %copy-start = (bf16[2,2,2,128,256]{4,3,2,1,0:T(8,128)(2,1)S(1)}, bf16[2,2,2,128,256]{4,3,2,1,0:T(8,128)(2,1)}, u32[]{:S(2)}) copy-start(bf16[2,2,2,128,256]{4,3,2,1,0:T(8,128)(2,1)} %param.9) | copy-start | bytes 1572868
  0.6 1.0 %copy-start.2 = (bf16[4,4,32,32]{3,2,1,0:T(8,128)(2,1)S(1)}, bf16[4,4,32,32]{3,2,1,0:T(8,128)(2,1)}, u32[]{:S(2)}) copy-start(bf16[4,4,32,32]{3,2,1,0:T(8,128)(2,1)} %param.11) | copy-start | bytes 98308
  1.6 2.5 %copy-start.3 = (bf16[1,8,64,128]{3,2,1,0:T(8,128)(2,1)S(1)}, bf16[1,8,64,128]{3,2,1,0:T(8,128)(2,1)}, u32[]{:S(2)}) copy-start(bf16[1,8,64,128]{3,2,1,0:T(8,128)(2,1)} %param.6) | copy-start | bytes 393220
  1.7 5.2 %collective-permute-start.4 = (bf16[2,32,128]{2,1,0:T(8,128)(2,1)S(1)}, bf16[2,32,128]{2,1,0:T(8,128)(2,1)S(1)}, u32[]{:S(2)}, u32[]{:S(2)}) collective-permute-start(bf16[2,32,128]{2,1,0:T(8,128)(2,1)S(1)} %get-tuple-element.51), channel_id=1, source_target_pairs={{0,16},{4,20},{8,24},{12,28},{16,0},{20,4},{24,8},{28,12},{1,17},{... | collective-permute-start | bytes 49160 | tf_op jit(solution)/shard_map/ppermute | solution.py:240
  4.2 6.8 %collective-permute-start = (bf16[32,512]{1,0:T(8,128)(2,1)S(1)}, bf16[32,512]{1,0:T(8,128)(2,1)S(1)}, u32[]{:S(2)}, u32[]{:S(2)}) collective-permute-start(bf16[32,512]{1,0:T(8,128)(2,1)S(1)} %get-tuple-element.47), channel_id=1, source_target_pairs={{0,1},{1,0},{2,3},{3,2},{4,5},{5,4},{6,7},{7,6},{8,9},{9,8},{10,11... | collective-permute-start | bytes 98312 | tf_op jit(solution)/shard_map/ppermute | solution.py:240
  5.2 5.8 %collective-permute-start.1 = (bf16[32,512]{1,0:T(8,128)(2,1)S(1)}, bf16[32,512]{1,0:T(8,128)(2,1)S(1)}, u32[]{:S(2)}, u32[]{:S(2)}) collective-permute-start(bf16[32,512]{1,0:T(8,128)(2,1)S(1)} %get-tuple-element.48), channel_id=1, source_target_pairs={{0,2},{1,3},{2,0},{3,1},{4,6},{5,7},{6,4},{7,5},{8,10},{9,11},{10,... | collective-permute-start | bytes 98312 | tf_op jit(solution)/shard_map/ppermute | solution.py:240
  6.4 4.5 %collective-permute-start.2 = (bf16[32,512]{1,0:T(8,128)(2,1)S(1)}, bf16[32,512]{1,0:T(8,128)(2,1)S(1)}, u32[]{:S(2)}, u32[]{:S(2)}) collective-permute-start(bf16[32,512]{1,0:T(8,128)(2,1)S(1)} %get-tuple-element.49), channel_id=1, source_target_pairs={{0,3},{1,2},{2,1},{3,0},{4,7},{5,6},{6,5},{7,4},{8,11},{9,10},{10,... | collective-permute-start | bytes 98312 | tf_op jit(solution)/shard_map/ppermute | solution.py:240
  6.9 2.8 %collective-permute-start.5 = (bf16[1,2,32,128]{3,2,1,0:T(8,128)(2,1)S(1)}, bf16[1,2,32,128]{3,2,1,0:T(8,128)(2,1)S(1)}, u32[]{:S(2)}, u32[]{:S(2)}) collective-permute-start(bf16[1,2,32,128]{3,2,1,0:T(8,128)(2,1)S(1)} %get-tuple-element.90), channel_id=1, source_target_pairs={{0,8},{4,12},{8,0},{12,4},{16,24},{20,28},{24,16},{28,20},{1,9},{5... | collective-permute-start | bytes 49160 | tf_op jit(solution)/shard_map/ppermute | solution.py:240
  9.7 2.8 %collective-permute-start.6 = (bf16[4,32,128]{2,1,0:T(8,128)(2,1)S(1)}, bf16[4,32,128]{2,1,0:T(8,128)(2,1)S(1)}, u32[]{:S(2)}, u32[]{:S(2)}) collective-permute-start(bf16[4,32,128]{2,1,0:T(8,128)(2,1)S(1)} %maximum_bitcast_fusion.refs_3_), channel_id=1, source_target_pairs={{0,4},{4,0},{8,12},{12,8},{16,20},{20,16},{24,28},{28,24},{1,5},{5... | collective-permute-start | bytes 98312 | tf_op jit(solution)/shard_map/ppermute | solution.py:240
  11.0 1.5 %copy-start.4 = (bf16[1,8,64,128]{3,2,1,0:T(8,128)(2,1)S(1)}, bf16[1,8,64,128]{3,2,1,0:T(8,128)(2,1)}, u32[]{:S(2)}) copy-start(bf16[1,8,64,128]{3,2,1,0:T(8,128)(2,1)} %param.7) | copy-start | bytes 393220
  11.0 1.5 %copy-start.5 = (bf16[1,8,64,128]{3,2,1,0:T(8,128)(2,1)S(1)}, bf16[1,8,64,128]{3,2,1,0:T(8,128)(2,1)}, u32[]{:S(2)}) copy-start(bf16[1,8,64,128]{3,2,1,0:T(8,128)(2,1)} %param.10) | copy-start | bytes 393220
  13.1 5.3 %collective-permute-start.7 = (bf16[512,128]{1,0:T(8,128)(2,1)S(1)}, bf16[512,128]{1,0:T(8,128)(2,1)S(1)}, u32[]{:S(2)}, u32[]{:S(2)}) collective-permute-start(bf16[512,128]{1,0:T(8,128)(2,1)S(1)} %get-tuple-element.54.refs_3_), channel_id=1, source_target_pairs={{0,1},{1,0},{2,3},{3,2},{4,5},{5,4},{6,7},{7,6},{8,9},{9,8},{10,11... | collective-permute-start | bytes 393224 | tf_op jit(solution)/shard_map/ppermute | solution.py:240
  15.5 5.1 %collective-permute-start.3 = (bf16[4,32,512]{2,1,0:T(8,128)(2,1)S(1)}, bf16[4,32,512]{2,1,0:T(8,128)(2,1)S(1)}, u32[]{:S(2)}, u32[]{:S(2)}) collective-permute-start(bf16[4,32,512]{2,1,0:T(8,128)(2,1)S(1)} %pad_maximum_fusion.1.refs_1_), channel_id=1, source_target_pairs={{0,4},{4,0},{8,12},{12,8},{16,20},{20,16},{24,28},{28,24},{1,5},{5... | collective-permute-start | bytes 393224 | tf_op jit(solution)/shard_map/ppermute | solution.py:240
  16.8 5.8 %collective-permute-start.10 = (bf16[512,128]{1,0:T(8,128)(2,1)S(1)}, bf16[512,128]{1,0:T(8,128)(2,1)S(1)}, u32[]{:S(2)}, u32[]{:S(2)}) collective-permute-start(bf16[512,128]{1,0:T(8,128)(2,1)S(1)} %get-tuple-element.54.refs_3_), channel_id=1, source_target_pairs={{0,3},{1,2},{2,1},{3,0},{4,7},{5,6},{6,5},{7,4},{8,11},{9,10},{10,... | collective-permute-start | bytes 393224 | tf_op jit(solution)/shard_map/ppermute | solution.py:240
  18.2 6.8 %collective-permute-start.9 = (bf16[512,128]{1,0:T(8,128)(2,1)S(1)}, bf16[512,128]{1,0:T(8,128)(2,1)S(1)}, u32[]{:S(2)}, u32[]{:S(2)}) collective-permute-start(bf16[512,128]{1,0:T(8,128)(2,1)S(1)} %get-tuple-element.54.refs_3_), channel_id=1, source_target_pairs={{0,2},{1,3},{2,0},{3,1},{4,6},{5,7},{6,4},{7,5},{8,10},{9,11},{10,... | collective-permute-start | bytes 393224 | tf_op jit(solution)/shard_map/ppermute | solution.py:240
  18.5 7.4 %collective-permute-start.8 = (bf16[4,32,512]{2,1,0:T(8,128)(2,1)S(1)}, bf16[4,32,512]{2,1,0:T(8,128)(2,1)S(1)}, u32[]{:S(2)}, u32[]{:S(2)}) collective-permute-start(bf16[4,32,512]{2,1,0:T(8,128)(2,1)S(1)} %pad_maximum_fusion.1.refs_1_), channel_id=1, source_target_pairs={{4,8},{8,4},{12,16},{16,12},{20,24},{24,20},{5,9},{9,5},{13,17},{1... | collective-permute-start | bytes 393224 | tf_op jit(solution)/shard_map/ppermute | solution.py:250
  27.4 35.2 %copy-start.1 = (bf16[3,3,3,128,128]{4,3,2,1,0:T(8,128)(2,1)S(1)}, bf16[3,3,3,128,128]{4,3,2,1,0:T(8,128)(2,1)}, u32[]{:S(2)}) copy-start(bf16[3,3,3,128,128]{4,3,2,1,0:T(8,128)(2,1)} %weight.1) | copy-start | bytes 2654212
  27.4 7.1 %collective-permute-start.11 = (bf16[432,128]{1,0:T(8,128)(2,1)S(1)}, bf16[432,128]{1,0:T(8,128)(2,1)S(1)}, u32[]{:S(2)}, u32[]{:S(2)}) collective-permute-start(bf16[432,128]{1,0:T(8,128)(2,1)S(1)} %get-tuple-element.63), channel_id=1, source_target_pairs={{0,4},{4,0},{8,12},{12,8},{16,20},{20,16},{24,28},{28,24},{1,5},{5... | collective-permute-start | bytes 331784 | tf_op jit(solution)/shard_map/ppermute | solution.py:240
  27.7 3.2 %collective-permute-start.12 = (bf16[256,128]{1,0:T(8,128)(2,1)S(1)}, bf16[256,128]{1,0:T(8,128)(2,1)S(1)}, u32[]{:S(2)}, u32[]{:S(2)}) collective-permute-start(bf16[256,128]{1,0:T(8,128)(2,1)S(1)} %get-tuple-element.65), channel_id=1, source_target_pairs={{0,1},{1,0},{2,3},{3,2},{4,5},{5,4},{6,7},{7,6},{8,9},{9,8},{10,11... | collective-permute-start | bytes 196616 | tf_op jit(solution)/shard_map/ppermute | solution.py:240
  29.3 3.7 %collective-permute-start.13 = (bf16[256,128]{1,0:T(8,128)(2,1)S(1)}, bf16[256,128]{1,0:T(8,128)(2,1)S(1)}, u32[]{:S(2)}, u32[]{:S(2)}) collective-permute-start(bf16[256,128]{1,0:T(8,128)(2,1)S(1)} %get-tuple-element.66), channel_id=1, source_target_pairs={{0,2},{1,3},{2,0},{3,1},{4,6},{5,7},{6,4},{7,5},{8,10},{9,11},{10,... | collective-permute-start | bytes 196616 | tf_op jit(solution)/shard_map/ppermute | solution.py:240
  30.5 4.0 %collective-permute-start.14 = (bf16[256,128]{1,0:T(8,128)(2,1)S(1)}, bf16[256,128]{1,0:T(8,128)(2,1)S(1)}, u32[]{:S(2)}, u32[]{:S(2)}) collective-permute-start(bf16[256,128]{1,0:T(8,128)(2,1)S(1)} %get-tuple-element.67), channel_id=1, source_target_pairs={{0,3},{1,2},{2,1},{3,0},{4,7},{5,6},{6,5},{7,4},{8,11},{9,10},{10,... | collective-permute-start | bytes 196616 | tf_op jit(solution)/shard_map/ppermute | solution.py:240
  34.6 7.4 %collective-permute-start.18 = (bf16[10,64,128]{2,1,0:T(8,128)(2,1)S(1)}, bf16[10,64,128]{2,1,0:T(8,128)(2,1)S(1)}, u32[]{:S(2)}, u32[]{:S(2)}) collective-permute-start(bf16[10,64,128]{2,1,0:T(8,128)(2,1)S(1)} %get-tuple-element.82.own), channel_id=1, source_target_pairs={{0,4},{4,0},{8,12},{12,8},{16,20},{20,16},{24,28},{28,24},{1,5},{5... | collective-permute-start | bytes 491528 | tf_op jit(solution)/shard_map/ppermute | solution.py:240
  35.9 3.2 %collective-permute-start.15 = (bf16[176,128]{1,0:T(8,128)(2,1)S(1)}, bf16[176,128]{1,0:T(8,128)(2,1)S(1)}, u32[]{:S(2)}, u32[]{:S(2)}) collective-permute-start(bf16[176,128]{1,0:T(8,128)(2,1)S(1)} %get-tuple-element.73), channel_id=1, source_target_pairs={{0,8},{4,12},{8,0},{12,4},{16,24},{20,28},{24,16},{28,20},{1,9},{5... | collective-permute-start | bytes 135176 | tf_op jit(solution)/shard_map/ppermute | solution.py:240
  35.9 4.4 %collective-permute-start.16 = (bf16[176,128]{1,0:T(8,128)(2,1)S(1)}, bf16[176,128]{1,0:T(8,128)(2,1)S(1)}, u32[]{:S(2)}, u32[]{:S(2)}) collective-permute-start(bf16[176,128]{1,0:T(8,128)(2,1)S(1)} %get-tuple-element.74), channel_id=1, source_target_pairs={{0,16},{4,20},{8,24},{12,28},{16,0},{20,4},{24,8},{28,12},{1,17},{... | collective-permute-start | bytes 135176 | tf_op jit(solution)/shard_map/ppermute | solution.py:240
  38.3 3.7 %collective-permute-start.17 = (bf16[176,128]{1,0:T(8,128)(2,1)S(1)}, bf16[176,128]{1,0:T(8,128)(2,1)S(1)}, u32[]{:S(2)}, u32[]{:S(2)}) collective-permute-start(bf16[176,128]{1,0:T(8,128)(2,1)S(1)} %get-tuple-element.75), channel_id=1, source_target_pairs={{0,24},{4,28},{8,16},{12,20},{16,8},{20,12},{24,0},{28,4},{1,25},{... | collective-permute-start | bytes 135176 | tf_op jit(solution)/shard_map/ppermute | solution.py:240
  42.1 4.6 %collective-permute-start.22 = (bf16[176,128]{1,0:T(8,128)(2,1)S(1)}, bf16[176,128]{1,0:T(8,128)(2,1)S(1)}, u32[]{:S(2)}, u32[]{:S(2)}) collective-permute-start(bf16[176,128]{1,0:T(8,128)(2,1)S(1)} %multiply_convert_fusion), channel_id=1, source_target_pairs={{0,24},{4,28},{8,16},{12,20},{16,8},{20,12},{24,0},{28,4},{1,25},{... | collective-permute-start | bytes 135176 | tf_op jit(solution)/shard_map/ppermute | solution.py:240
  42.4 6.3 %collective-permute-start.21 = (bf16[176,128]{1,0:T(8,128)(2,1)S(1)}, bf16[176,128]{1,0:T(8,128)(2,1)S(1)}, u32[]{:S(2)}, u32[]{:S(2)}) collective-permute-start(bf16[176,128]{1,0:T(8,128)(2,1)S(1)} %multiply_convert_fusion), channel_id=1, source_target_pairs={{0,16},{4,20},{8,24},{12,28},{16,0},{20,4},{24,8},{28,12},{1,17},{... | collective-permute-start | bytes 135176 | tf_op jit(solution)/shard_map/ppermute | solution.py:240
  46.7 3.3 %collective-permute-start.20 = (bf16[176,128]{1,0:T(8,128)(2,1)S(1)}, bf16[176,128]{1,0:T(8,128)(2,1)S(1)}, u32[]{:S(2)}, u32[]{:S(2)}) collective-permute-start(bf16[176,128]{1,0:T(8,128)(2,1)S(1)} %multiply_convert_fusion), channel_id=1, source_target_pairs={{0,8},{4,12},{8,0},{12,4},{16,24},{20,28},{24,16},{28,20},{1,9},{5... | collective-permute-start | bytes 135176 | tf_op jit(solution)/shard_map/ppermute | solution.py:240
  50.0 4.4 %collective-permute-start.23 = (bf16[4,176,128]{2,1,0:T(8,128)(2,1)S(1)}, bf16[4,176,128]{2,1,0:T(8,128)(2,1)S(1)}, u32[]{:S(2)}, u32[]{:S(2)}) collective-permute-start(bf16[4,176,128]{2,1,0:T(8,128)(2,1)S(1)} %pad_maximum_fusion.refs_0_), channel_id=1, source_target_pairs={{0,4},{4,0},{8,12},{12,8},{16,20},{20,16},{24,28},{28,24},{1,5},{5... | collective-permute-start | bytes 540680 | tf_op jit(solution)/shard_map/ppermute | solution.py:240
  50.2 14.2 %collective-permute-start.26 = (bf16[4,176,128]{2,1,0:T(8,128)(2,1)S(1)}, bf16[4,176,128]{2,1,0:T(8,128)(2,1)S(1)}, u32[]{:S(2)}, u32[]{:S(2)}) collective-permute-start(bf16[4,176,128]{2,1,0:T(8,128)(2,1)S(1)} %pad_maximum_fusion.refs_0_), channel_id=1, source_target_pairs={{0,2},{1,3},{2,0},{3,1},{4,6},{5,7},{6,4},{7,5},{8,10},{9,11},{10,... | collective-permute-start | bytes 540680 | tf_op jit(solution)/shard_map/ppermute | solution.py:240
  54.4 16.0 %collective-permute-start.24 = (bf16[4,176,128]{2,1,0:T(8,128)(2,1)S(1)}, bf16[4,176,128]{2,1,0:T(8,128)(2,1)S(1)}, u32[]{:S(2)}, u32[]{:S(2)}) collective-permute-start(bf16[4,176,128]{2,1,0:T(8,128)(2,1)S(1)} %collective-permute-done.23.refs_4_), channel_id=1, source_target_pairs={{0,2},{1,3},{2,0},{3,1},{4,6},{5,7},{6,4},{7,5},{8,10},{9,11},{10,... | collective-permute-start | bytes 540680 | tf_op jit(solution)/shard_map/ppermute | solution.py:240
  55.6 7.0 %collective-permute-start.19 = (bf16[10,64,128]{2,1,0:T(8,128)(2,1)S(1)}, bf16[10,64,128]{2,1,0:T(8,128)(2,1)S(1)}, u32[]{:S(2)}, u32[]{:S(2)}) collective-permute-start(bf16[10,64,128]{2,1,0:T(8,128)(2,1)S(1)} %get-tuple-element.82.own), channel_id=1, source_target_pairs={{4,8},{8,4},{12,16},{16,12},{20,24},{24,20},{5,9},{9,5},{13,17},{1... | collective-permute-start | bytes 491528 | tf_op jit(solution)/shard_map/ppermute | solution.py:250
  57.6 13.3 %collective-permute-start.25 = (bf16[4,176,128]{2,1,0:T(8,128)(2,1)S(1)}, bf16[4,176,128]{2,1,0:T(8,128)(2,1)S(1)}, u32[]{:S(2)}, u32[]{:S(2)}) collective-permute-start(bf16[4,176,128]{2,1,0:T(8,128)(2,1)S(1)} %pad_maximum_fusion.refs_0_), channel_id=1, source_target_pairs={{0,1},{1,0},{2,3},{3,2},{4,5},{5,4},{6,7},{7,6},{8,9},{9,8},{10,11... | collective-permute-start | bytes 540680 | tf_op jit(solution)/shard_map/ppermute | solution.py:240
  64.4 7.1 %collective-permute-start.27 = (bf16[4,176,128]{2,1,0:T(8,128)(2,1)S(1)}, bf16[4,176,128]{2,1,0:T(8,128)(2,1)S(1)}, u32[]{:S(2)}, u32[]{:S(2)}) collective-permute-start(bf16[4,176,128]{2,1,0:T(8,128)(2,1)S(1)} %collective-permute-done.26.refs_2_), channel_id=1, source_target_pairs={{0,1},{1,0},{2,3},{3,2},{4,5},{5,4},{6,7},{7,6},{8,9},{9,8},{10,11... | collective-permute-start | bytes 540680 | tf_op jit(solution)/shard_map/ppermute | solution.py:240
  70.4 1.4 %collective-permute-start.28 = (bf16[4,176,128]{2,1,0:T(8,128)(2,1)S(1)}, bf16[4,176,128]{2,1,0:T(8,128)(2,1)S(1)}, u32[]{:S(2)}, u32[]{:S(2)}) collective-permute-start(bf16[4,176,128]{2,1,0:T(8,128)(2,1)S(1)} %collective-permute-done.23.refs_4_), channel_id=1, source_target_pairs={{0,1},{1,0},{2,3},{3,2},{4,5},{5,4},{6,7},{7,6},{8,9},{9,8},{10,11... | collective-permute-start | bytes 540680 | tf_op jit(solution)/shard_map/ppermute | solution.py:240
  70.5 1.6 %collective-permute-start.29 = (bf16[4,176,128]{2,1,0:T(8,128)(2,1)S(1)}, bf16[4,176,128]{2,1,0:T(8,128)(2,1)S(1)}, u32[]{:S(2)}, u32[]{:S(2)}) collective-permute-start(bf16[4,176,128]{2,1,0:T(8,128)(2,1)S(1)} %collective-permute-done.24.refs_6_), channel_id=1, source_target_pairs={{0,1},{1,0},{2,3},{3,2},{4,5},{5,4},{6,7},{7,6},{8,9},{9,8},{10,11... | collective-permute-start | bytes 540680 | tf_op jit(solution)/shard_map/ppermute | solution.py:240

commit v16 on v11

--- a/solution.py
+++ b/solution.py
@@ -215,10 +215,14 @@
     return lax.ppermute(value, axis, [(i, i ^ code) for i in range(lax.axis_size(axis))])
 
 
-def neighbours(value):
+def even_pairs(value):
+    return swapped(value, "gz", 1)
+
+
+def odd_pairs(value):
     last = lax.axis_size("gz") - 1
-    odd = [(i + d, i + 1 - d) for i in range(1, last, 2) for d in range(2)]
-    return swapped(value, "gz", 1), lax.ppermute(value, "gz", odd)
+    pairs = [(i + d, i + 1 - d) for i in range(1, last, 2) for d in range(2)]
+    return lax.ppermute(value, "gz", pairs)
 
 
 def exchanged(value, axis):
@@ -273,7 +277,7 @@
     )
     level_t = [swapped(value, "gy", code) if code else value for code, value in enumerate(level_t)]
     level_t = jnp.stack(level_t)
-    even, odd = neighbours(level_t)
+    even = even_pairs(level_t)
     *deep_t, level_t = lax.optimization_barrier((*deep_t, level_t))
     down_slice = lax.dynamic_index_in_dim(down_weight, parity, 0, keepdims=False)
     grad, down, *others = call(
@@ -290,7 +294,9 @@
         ],
     )
     shared = [swapped(grad, "gy", code) if code else grad for code in range(n_gy)]
-    even, odd, *others = lax.optimization_barrier((even, odd, *others))
+    shared[1], level_t = lax.optimization_barrier((shared[1], level_t))
+    odd = odd_pairs(level_t)
+    even, *others = lax.optimization_barrier((even, *others))
     for code, value in enumerate(others):
         down = down + swapped(value, "gy", code + 1).astype(F32)
     keep, send, near = call(
@@ -310,7 +316,7 @@
             pltpu.VMEM((2, 27 * half, channels), F32),
         ],
     )
-    near_even, near_odd = neighbours(near)
+    near_even, near_odd = even_pairs(near), odd_pairs(near)
     conv = (keep + swapped(send, "gz", 1).astype(F32)).astype(wire)
     total = jnp.concatenate([conv, down.astype(wire)], axis=0)
     total = lax.optimization_barrier(total)

time: 66.5 us -> 66.3 us (level)
  waiting for transfers between devices: 26.5 us -> 24.2 us
  starting transfers between devices: 32.3 us -> 34.4 us
    ppermute x24, waiting for transfers between devices: 26.5 us -> 24.2 us  [swapped(): lax.ppermute(value, axis, [(i, i ^ code) for i in range(lax.axis_size(axi...]
    ppermute x24, starting transfers between devices: 30.8 us -> 33 us  [swapped(): lax.ppermute(value, axis, [(i, i ^ code) for i in range(lax.axis_size(axi...]
  transfers between devices with their start and end apart: 26 -> 26, of which waited for: 12 -> 11; matrix products, arithmetic and copies ran while one was open for 0% -> 0% of each run, Pallas kernels for 6% -> 5%
where the time goes in v16:
time: 66.3 us; the launch traced here: 66.1 us
  starting transfers between devices  34.4 us (52%)
  waiting for transfers between devices  24.2 us (37%)
  Pallas kernels  5.34 us (8%)
  local copies, waits for them, and re-layouts  1 us (2%)
  between operations  0.82 us (1%)
    ppermute x24, starting transfers between devices, swapped(): lax.ppermute(value, axis, [(i, i ^ code) for i in range(lax.axis_size(axi...  33 us
    ppermute x24, waiting for transfers between devices, swapped(): lax.ppermute(value, axis, [(i, i ^ code) for i in range(lax.axis_size(axi...  24.2 us
    pallas_call x6, Pallas kernels, call(): pl.pallas_call(kernel, out_shape=out_shape, scratch_shapes=list(scratch),...  5.34 us
  transfers between devices with their start and end apart: 26, of which 11 were waited for; matrix products, arithmetic and copies ran while one was open for 0% of the time, Pallas kernels for 5%

profile of v16, /device:TPU:0, one launch (start us, length us, event | category | flops | bytes accessed | tf_op | source)
XLA Modules:
  0.0 66.1 jit_solution(3977856202905894303)
XLA Ops:
  0.6 0.0 copy-start
  0.7 1.0 %copy-done.2 = bf16[4,4,32,32]{3,2,1,0:T(8,128)(2,1)S(1)} copy-done((bf16[4,4,32,32]{3,2,1,0:T(8,128)(2,1)S(1)}, bf16[4,4,32,32]{3,2,1,0:T(8,128)(2,1)}, u32[]{:S(2)}) %copy-start.2) | copy-done | bytes 32792
  1.6 0.1 shard_map.86
  1.7 4.1 %collective-permute-start.4 = (bf16[2,32,128]{2,1,0:T(8,128)(2,1)S(1)}, bf16[2,32,128]{2,1,0:T(8,128)(2,1)S(1)}, u32[]{:S(2)}, u32[]{:S(2)}) collective-permute-start(bf16[2,32,128]{2,1,0:T(8,128)(2,1)S(1)} %get-tuple-element.38), channel_id=1, source_target_pairs={{0,16},{4,20},{8,24},{12,28},{16,0},{20,4},{24,8},{28,12},{1,17},{... | collective-permute-start | bytes 49160 | tf_op jit(solution)/shard_map/ppermute | solution.py:215
  5.8 0.1 shard_map.85
  5.9 0.1 collective-permute-start
  6.0 1.6 %collective-permute-start.1 = (bf16[32,512]{1,0:T(8,128)(2,1)S(1)}, bf16[32,512]{1,0:T(8,128)(2,1)S(1)}, u32[]{:S(2)}, u32[]{:S(2)}) collective-permute-start(bf16[32,512]{1,0:T(8,128)(2,1)S(1)} %get-tuple-element.35), channel_id=1, source_target_pairs={{0,2},{1,3},{2,0},{3,1},{4,6},{5,7},{6,4},{7,5},{8,10},{9,11},{10,... | collective-permute-start | bytes 98312 | tf_op jit(solution)/shard_map/ppermute | solution.py:215
  7.6 0.3 collective-permute-start.2
  7.9 0.0 collective-permute-done.4
  7.9 1.6 %collective-permute-start.5 = (bf16[1,2,32,128]{3,2,1,0:T(8,128)(2,1)S(1)}, bf16[1,2,32,128]{3,2,1,0:T(8,128)(2,1)S(1)}, u32[]{:S(2)}, u32[]{:S(2)}) collective-permute-start(bf16[1,2,32,128]{3,2,1,0:T(8,128)(2,1)S(1)} %get-tuple-element.64), channel_id=1, source_target_pairs={{0,8},{4,12},{8,0},{12,4},{16,24},{20,28},{24,16},{28,20},{1,9},{5... | collective-permute-start | bytes 49160 | tf_op jit(solution)/shard_map/ppermute | solution.py:215
  9.5 2.1 %collective-permute-done.5 = bf16[1,2,32,128]{3,2,1,0:T(8,128)(2,1)S(1)} collective-permute-done((bf16[1,2,32,128]{3,2,1,0:T(8,128)(2,1)S(1)}, bf16[1,2,32,128]{3,2,1,0:T(8,128)(2,1)S(1)}, u32[]{:S(2)}, u32[]{:S(2)}) %collective-permute-start.5) | collective-permute-done | bytes 16416 | tf_op jit(solution)/shard_map/ppermute | solution.py:215
  11.7 1.5 %collective-permute-start.6 = (bf16[4,32,128]{2,1,0:T(8,128)(2,1)S(1)}, bf16[4,32,128]{2,1,0:T(8,128)(2,1)S(1)}, u32[]{:S(2)}, u32[]{:S(2)}) collective-permute-start(bf16[4,32,128]{2,1,0:T(8,128)(2,1)S(1)} %maximum_bitcast_fusion.refs_3_), channel_id=1, source_target_pairs={{0,4},{4,0},{8,12},{12,8},{16,20},{20,16},{24,28},{28,24},{1,5},{5... | collective-permute-start | bytes 98312 | tf_op jit(solution)/shard_map/ppermute | solution.py:215
  13.2 0.0 collective-permute-done
  13.2 0.0 collective-permute-done.1
  13.2 0.0 collective-permute-done.2
  13.2 0.0 copy-start.4
  13.2 0.0 copy-start.5
  13.3 2.3 %collective-permute-done.6.refs_4_ = bf16[4,32,128]{2,1,0:T(8,128)(2,1)S(1)} collective-permute-done((bf16[4,32,128]{2,1,0:T(8,128)(2,1)S(1)}, bf16[4,32,128]{2,1,0:T(8,128)(2,1)S(1)}, u32[]{:S(2)}, u32[]{:S(2)}) %collective-permute-start.6) | collective-permute-done | bytes 32800 | tf_op jit(solution)/shard_map/ppermute | solution.py:215
  15.6 0.6 shard_map.87
  16.2 0.1 collective-permute-start.7
  16.3 1.6 %collective-permute-start.3 = (bf16[4,32,512]{2,1,0:T(8,128)(2,1)S(1)}, bf16[4,32,512]{2,1,0:T(8,128)(2,1)S(1)}, u32[]{:S(2)}, u32[]{:S(2)}) collective-permute-start(bf16[4,32,512]{2,1,0:T(8,128)(2,1)S(1)} %pad_maximum_fusion.1.refs_1_), channel_id=1, source_target_pairs={{0,4},{4,0},{8,12},{12,8},{16,20},{20,16},{24,28},{28,24},{1,5},{5... | collective-permute-start | bytes 393224 | tf_op jit(solution)/shard_map/ppermute | solution.py:215
  17.9 1.3 %collective-permute-start.10 = (bf16[512,128]{1,0:T(8,128)(2,1)S(1)}, bf16[512,128]{1,0:T(8,128)(2,1)S(1)}, u32[]{:S(2)}, u32[]{:S(2)}) collective-permute-start(bf16[512,128]{1,0:T(8,128)(2,1)S(1)} %get-tuple-element.45.refs_3_), channel_id=1, source_target_pairs={{0,3},{1,2},{2,1},{3,0},{4,7},{5,6},{6,5},{7,4},{8,11},{9,10},{10,... | collective-permute-start | bytes 393224 | tf_op jit(solution)/shard_map/ppermute | solution.py:215
  19.2 0.5 collective-permute-start.9
  19.7 0.0 collective-permute-done.7.refs_4_
  19.7 0.7 collective-permute-start.8
  20.4 1.9 %collective-permute-done.3.refs_0_ = bf16[4,32,512]{2,1,0:T(8,128)(2,1)S(1)} collective-permute-done((bf16[4,32,512]{2,1,0:T(8,128)(2,1)S(1)}, bf16[4,32,512]{2,1,0:T(8,128)(2,1)S(1)}, u32[]{:S(2)}, u32[]{:S(2)}) %collective-permute-start.3) | collective-permute-done | bytes 131104 | tf_op jit(solution)/shard_map/ppermute | solution.py:215
  22.2 0.0 collective-permute-start.12
  22.2 1.5 %collective-permute-start.13 = (bf16[256,128]{1,0:T(8,128)(2,1)S(1)}, bf16[256,128]{1,0:T(8,128)(2,1)S(1)}, u32[]{:S(2)}, u32[]{:S(2)}) collective-permute-start(bf16[256,128]{1,0:T(8,128)(2,1)S(1)} %get-tuple-element.53), channel_id=1, source_target_pairs={{0,2},{1,3},{2,0},{3,1},{4,6},{5,7},{6,4},{7,5},{8,10},{9,11},{10,... | collective-permute-start | bytes 196616 | tf_op jit(solution)/shard_map/ppermute | solution.py:215
  23.7 0.0 collective-permute-done.10.refs_6_
  23.7 1.2 %collective-permute-start.14 = (bf16[256,128]{1,0:T(8,128)(2,1)S(1)}, bf16[256,128]{1,0:T(8,128)(2,1)S(1)}, u32[]{:S(2)}, u32[]{:S(2)}) collective-permute-start(bf16[256,128]{1,0:T(8,128)(2,1)S(1)} %get-tuple-element.54), channel_id=1, source_target_pairs={{0,3},{1,2},{2,1},{3,0},{4,7},{5,6},{6,5},{7,4},{8,11},{9,10},{10,... | collective-permute-start | bytes 196616 | tf_op jit(solution)/shard_map/ppermute | solution.py:215
  25.0 1.9 %collective-permute-done.9.refs_5_ = bf16[512,128]{1,0:T(8,128)(2,1)S(1)} collective-permute-done((bf16[512,128]{1,0:T(8,128)(2,1)S(1)}, bf16[512,128]{1,0:T(8,128)(2,1)S(1)}, u32[]{:S(2)}, u32[]{:S(2)}) %collective-permute-start.9) | collective-permute-done | bytes 131104 | tf_op jit(solution)/shard_map/ppermute | solution.py:215
  26.8 0.0 collective-permute-done.8.refs_2_
  26.8 1.5 %shard_map.88 = (f32[432,128]{1,0:T(8,128)S(1)}, bf16[432,128]{1,0:T(8,128)(2,1)S(1)}, bf16[10,64,128]{2,1,0:T(8,128)(2,1)S(1)}) custom-call(bf16[4,32,512]{2,1,0:T(8,128)(2,1)S(1)} %collective-permute-done.3.refs_0_, bf16[4,32,512]{2,1,0:T(8,128)(2,1)S(1)} %pad_maximum_fusion.1.refs_1_, bf16[4,32,512]{2,1,0:T(8,128)(2,1)S(1)} %collective-permute-done.8.refs_2_, ...), custom_call_target="tpu_custom_call" | custom-call | tf_op jit(solution)/shard_map/pallas_call | solution.py:16
  28.3 0.0 copy-start.1
  28.4 1.7 %collective-permute-start.11 = (bf16[432,128]{1,0:T(8,128)(2,1)S(1)}, bf16[432,128]{1,0:T(8,128)(2,1)S(1)}, u32[]{:S(2)}, u32[]{:S(2)}) collective-permute-start(bf16[432,128]{1,0:T(8,128)(2,1)S(1)} %get-tuple-element.50), channel_id=1, source_target_pairs={{0,4},{4,0},{8,12},{12,8},{16,20},{20,16},{24,28},{28,24},{1,5},{5... | collective-permute-start | bytes 331784 | tf_op jit(solution)/shard_map/ppermute | solution.py:215
  30.0 0.0 collective-permute-done.12
  30.1 0.0 collective-permute-done.13
  30.1 0.0 collective-permute-done.14
  30.1 3.1 %collective-permute-done.11 = bf16[432,128]{1,0:T(8,128)(2,1)S(1)} collective-permute-done((bf16[432,128]{1,0:T(8,128)(2,1)S(1)}, bf16[432,128]{1,0:T(8,128)(2,1)S(1)}, u32[]{:S(2)}, u32[]{:S(2)}) %collective-permute-start.11) | collective-permute-done | bytes 110624 | tf_op jit(solution)/shard_map/ppermute | solution.py:215
  33.2 3.7 %collective-permute-start.15 = (bf16[688,128]{1,0:T(8,128)(2,1)S(1)}, bf16[688,128]{1,0:T(8,128)(2,1)S(1)}, u32[]{:S(2)}, u32[]{:S(2)}) collective-permute-start(bf16[688,128]{1,0:T(8,128)(2,1)S(1)} %pad_maximum_fusion), channel_id=1, source_target_pairs={{0,16},{4,20},{8,24},{12,28},{16,0},{20,4},{24,8},{28,12},{1,17},{... | collective-permute-start | bytes 528392 | tf_op jit(solution)/shard_map/ppermute | solution.py:215
  36.9 0.7 collective-permute-start.17
  37.6 4.4 %collective-permute-start.16 = (bf16[10,64,128]{2,1,0:T(8,128)(2,1)S(1)}, bf16[10,64,128]{2,1,0:T(8,128)(2,1)S(1)}, u32[]{:S(2)}, u32[]{:S(2)}) collective-permute-start(bf16[10,64,128]{2,1,0:T(8,128)(2,1)S(1)} %get-tuple-element.55.own), channel_id=1, source_target_pairs={{0,4},{4,0},{8,12},{12,8},{16,20},{20,16},{24,28},{28,24},{1,5},{5... | collective-permute-start | bytes 491528 | tf_op jit(solution)/shard_map/ppermute | solution.py:215
  42.0 0.0 collective-permute-done.17.odd
  42.0 4.2 %collective-permute-done.16.even = bf16[10,64,128]{2,1,0:T(8,128)(2,1)S(1)} collective-permute-done((bf16[10,64,128]{2,1,0:T(8,128)(2,1)S(1)}, bf16[10,64,128]{2,1,0:T(8,128)(2,1)S(1)}, u32[]{:S(2)}, u32[]{:S(2)}) %collective-permute-start.16) | collective-permute-done | bytes 163872 | tf_op jit(solution)/shard_map/ppermute | solution.py:215
  46.2 0.0 collective-permute-done.15
  46.3 1.8 %collective-permute-start.18 = (bf16[688,128]{1,0:T(8,128)(2,1)S(1)}, bf16[688,128]{1,0:T(8,128)(2,1)S(1)}, u32[]{:S(2)}, u32[]{:S(2)}) collective-permute-start(bf16[688,128]{1,0:T(8,128)(2,1)S(1)} %add_convert_fusion), channel_id=1, source_target_pairs={{0,8},{4,12},{8,0},{12,4},{16,24},{20,28},{24,16},{28,20},{1,9},{5... | collective-permute-start | bytes 528392 | tf_op jit(solution)/shard_map/ppermute | solution.py:215
  48.1 1.7 %shard_map.89 = bf16[8,64,128]{2,1,0:T(8,128)(2,1)} custom-call(bf16[10,64,128]{2,1,0:T(8,128)(2,1)S(1)} %collective-permute-done.16.even, bf16[10,64,128]{2,1,0:T(8,128)(2,1)S(1)} %get-tuple-element.55.own, bf16[10,64,128]{2,1,0:T(8,128)(2,1)S(1)} %collective-permute-done.17.odd, bf16[3,3,3,128,128]{4,3,2,1,0:T(8,128)(2,1)S(1)} %copy-done.1), custom_call_target="tpu_custom_call" | custom-call | tf_op jit(solution)/shard_map/pallas_call | solution.py:16
  49.9 1.9 %collective-permute-done.18 = bf16[688,128]{1,0:T(8,128)(2,1)S(1)} collective-permute-done((bf16[688,128]{1,0:T(8,128)(2,1)S(1)}, bf16[688,128]{1,0:T(8,128)(2,1)S(1)}, u32[]{:S(2)}, u32[]{:S(2)}) %collective-permute-start.18) | collective-permute-done | bytes 176160 | tf_op jit(solution)/shard_map/ppermute | solution.py:215
  51.8 0.2 multiply_convert_fusion.refs_0_
  52.0 2.5 %collective-permute-start.22 = (bf16[688,128]{1,0:T(8,128)(2,1)S(1)}, bf16[688,128]{1,0:T(8,128)(2,1)S(1)}, u32[]{:S(2)}, u32[]{:S(2)}) collective-permute-start(bf16[688,128]{1,0:T(8,128)(2,1)S(1)} %multiply_convert_fusion.refs_0_), channel_id=1, source_target_pairs={{0,4},{4,0},{8,12},{12,8},{16,20},{20,16},{24,28},{28,24},{1,5},{5... | collective-permute-start | bytes 528392 | tf_op jit(solution)/shard_map/ppermute | solution.py:215
  54.5 1.5 %collective-permute-start.20 = (bf16[688,128]{1,0:T(8,128)(2,1)S(1)}, bf16[688,128]{1,0:T(8,128)(2,1)S(1)}, u32[]{:S(2)}, u32[]{:S(2)}) collective-permute-start(bf16[688,128]{1,0:T(8,128)(2,1)S(1)} %multiply_convert_fusion.refs_0_), channel_id=1, source_target_pairs={{0,2},{1,3},{2,0},{3,1},{4,6},{5,7},{6,4},{7,5},{8,10},{9,11},{10,... | collective-permute-start | bytes 528392 | tf_op jit(solution)/shard_map/ppermute | solution.py:215
  56.0 1.9 %collective-permute-done.22.refs_4_ = bf16[688,128]{1,0:T(8,128)(2,1)S(1)} collective-permute-done((bf16[688,128]{1,0:T(8,128)(2,1)S(1)}, bf16[688,128]{1,0:T(8,128)(2,1)S(1)}, u32[]{:S(2)}, u32[]{:S(2)}) %collective-permute-start.22) | collective-permute-done | bytes 176160 | tf_op jit(solution)/shard_map/ppermute | solution.py:215
  57.9 1.5 %collective-permute-start.24 = (bf16[688,128]{1,0:T(8,128)(2,1)S(1)}, bf16[688,128]{1,0:T(8,128)(2,1)S(1)}, u32[]{:S(2)}, u32[]{:S(2)}) collective-permute-start(bf16[688,128]{1,0:T(8,128)(2,1)S(1)} %collective-permute-done.22.refs_4_), channel_id=1, source_target_pairs={{0,2},{1,3},{2,0},{3,1},{4,6},{5,7},{6,4},{7,5},{8,10},{9,11},{10,... | collective-permute-start | bytes 528392 | tf_op jit(solution)/shard_map/ppermute | solution.py:215
  59.4 0.0 collective-permute-start.19
  59.4 0.5 collective-permute-start.23
  59.9 1.4 %collective-permute-done.20.refs_2_ = bf16[688,128]{1,0:T(8,128)(2,1)S(1)} collective-permute-done((bf16[688,128]{1,0:T(8,128)(2,1)S(1)}, bf16[688,128]{1,0:T(8,128)(2,1)S(1)}, u32[]{:S(2)}, u32[]{:S(2)}) %collective-permute-start.20) | collective-permute-done | bytes 176160 | tf_op jit(solution)/shard_map/ppermute | solution.py:215
  61.3 0.0 collective-permute-start.21
  61.3 2.1 %collective-permute-done.24.refs_6_ = bf16[688,128]{1,0:T(8,128)(2,1)S(1)} collective-permute-done((bf16[688,128]{1,0:T(8,128)(2,1)S(1)}, bf16[688,128]{1,0:T(8,128)(2,1)S(1)}, u32[]{:S(2)}, u32[]{:S(2)}) %collective-permute-start.24) | collective-permute-done | bytes 176160 | tf_op jit(solution)/shard_map/ppermute | solution.py:215
  63.4 0.0 collective-permute-start.25
  63.4 0.0 collective-permute-done.19.refs_1_
  63.4 0.0 collective-permute-done.23.refs_5_
  63.4 0.0 collective-permute-done.21.refs_3_
  63.4 1.4 %collective-permute-done.25.refs_7_ = bf16[688,128]{1,0:T(8,128)(2,1)S(1)} collective-permute-done((bf16[688,128]{1,0:T(8,128)(2,1)S(1)}, bf16[688,128]{1,0:T(8,128)(2,1)S(1)}, u32[]{:S(2)}, u32[]{:S(2)}) %collective-permute-start.25) | collective-permute-done | bytes 176160 | tf_op jit(solution)/shard_map/ppermute | solution.py:215
  64.8 1.3 %shard_map.90 = (bf16[27,4,2,16,128]{4,3,2,1,0:T(8,128)(2,1)}, bf16[2,4,128,256]{3,2,1,0:T(8,128)(2,1)}) custom-call(bf16[688,128]{1,0:T(8,128)(2,1)S(1)} %multiply_convert_fusion.refs_0_, bf16[688,128]{1,0:T(8,128)(2,1)S(1)} %collective-permute-done.19.refs_1_, bf16[688,128]{1,0:T(8,128)(2,1)S(1)} %collective-permute-done.20.refs_2_, ...), custom_call_target="tpu_custom_call" | custom-call | tf_op jit(solution)/shard_map/pallas_call | solution.py:16
  (16 shorter events, 0.2 us)
Async XLA Ops:
  0.6 8.9 %copy-start = (bf16[2,2,2,128,256]{4,3,2,1,0:T(8,128)(2,1)S(1)}, bf16[2,2,2,128,256]{4,3,2,1,0:T(8,128)(2,1)}, u32[]{:S(2)}) copy-start(bf16[2,2,2,128,256]{4,3,2,1,0:T(8,128)(2,1)} %param.9) | copy-start | bytes 1572868
  0.6 1.0 %copy-start.2 = (bf16[4,4,32,32]{3,2,1,0:T(8,128)(2,1)S(1)}, bf16[4,4,32,32]{3,2,1,0:T(8,128)(2,1)}, u32[]{:S(2)}) copy-start(bf16[4,4,32,32]{3,2,1,0:T(8,128)(2,1)} %param.11) | copy-start | bytes 98308
  1.6 4.2 %copy-start.3 = (bf16[1,8,64,128]{3,2,1,0:T(8,128)(2,1)S(1)}, bf16[1,8,64,128]{3,2,1,0:T(8,128)(2,1)}, u32[]{:S(2)}) copy-start(bf16[1,8,64,128]{3,2,1,0:T(8,128)(2,1)} %param.6) | copy-start | bytes 393220
  1.7 6.2 %collective-permute-start.4 = (bf16[2,32,128]{2,1,0:T(8,128)(2,1)S(1)}, bf16[2,32,128]{2,1,0:T(8,128)(2,1)S(1)}, u32[]{:S(2)}, u32[]{:S(2)}) collective-permute-start(bf16[2,32,128]{2,1,0:T(8,128)(2,1)S(1)} %get-tuple-element.38), channel_id=1, source_target_pairs={{0,16},{4,20},{8,24},{12,28},{16,0},{20,4},{24,8},{28,12},{1,17},{... | collective-permute-start | bytes 49160 | tf_op jit(solution)/shard_map/ppermute | solution.py:215
  5.9 7.3 %collective-permute-start = (bf16[32,512]{1,0:T(8,128)(2,1)S(1)}, bf16[32,512]{1,0:T(8,128)(2,1)S(1)}, u32[]{:S(2)}, u32[]{:S(2)}) collective-permute-start(bf16[32,512]{1,0:T(8,128)(2,1)S(1)} %get-tuple-element.34), channel_id=1, source_target_pairs={{0,1},{1,0},{2,3},{3,2},{4,5},{5,4},{6,7},{7,6},{8,9},{9,8},{10,11... | collective-permute-start | bytes 98312 | tf_op jit(solution)/shard_map/ppermute | solution.py:215
  6.0 7.2 %collective-permute-start.1 = (bf16[32,512]{1,0:T(8,128)(2,1)S(1)}, bf16[32,512]{1,0:T(8,128)(2,1)S(1)}, u32[]{:S(2)}, u32[]{:S(2)}) collective-permute-start(bf16[32,512]{1,0:T(8,128)(2,1)S(1)} %get-tuple-element.35), channel_id=1, source_target_pairs={{0,2},{1,3},{2,0},{3,1},{4,6},{5,7},{6,4},{7,5},{8,10},{9,11},{10,... | collective-permute-start | bytes 98312 | tf_op jit(solution)/shard_map/ppermute | solution.py:215
  7.6 5.7 %collective-permute-start.2 = (bf16[32,512]{1,0:T(8,128)(2,1)S(1)}, bf16[32,512]{1,0:T(8,128)(2,1)S(1)}, u32[]{:S(2)}, u32[]{:S(2)}) collective-permute-start(bf16[32,512]{1,0:T(8,128)(2,1)S(1)} %get-tuple-element.36), channel_id=1, source_target_pairs={{0,3},{1,2},{2,1},{3,0},{4,7},{5,6},{6,5},{7,4},{8,11},{9,10},{10,... | collective-permute-start | bytes 98312 | tf_op jit(solution)/shard_map/ppermute | solution.py:215
  7.9 3.8 %collective-permute-start.5 = (bf16[1,2,32,128]{3,2,1,0:T(8,128)(2,1)S(1)}, bf16[1,2,32,128]{3,2,1,0:T(8,128)(2,1)S(1)}, u32[]{:S(2)}, u32[]{:S(2)}) collective-permute-start(bf16[1,2,32,128]{3,2,1,0:T(8,128)(2,1)S(1)} %get-tuple-element.64), channel_id=1, source_target_pairs={{0,8},{4,12},{8,0},{12,4},{16,24},{20,28},{24,16},{28,20},{1,9},{5... | collective-permute-start | bytes 49160 | tf_op jit(solution)/shard_map/ppermute | solution.py:215
  11.7 3.9 %collective-permute-start.6 = (bf16[4,32,128]{2,1,0:T(8,128)(2,1)S(1)}, bf16[4,32,128]{2,1,0:T(8,128)(2,1)S(1)}, u32[]{:S(2)}, u32[]{:S(2)}) collective-permute-start(bf16[4,32,128]{2,1,0:T(8,128)(2,1)S(1)} %maximum_bitcast_fusion.refs_3_), channel_id=1, source_target_pairs={{0,4},{4,0},{8,12},{12,8},{16,20},{20,16},{24,28},{28,24},{1,5},{5... | collective-permute-start | bytes 98312 | tf_op jit(solution)/shard_map/ppermute | solution.py:215
  13.2 2.4 %copy-start.4 = (bf16[1,8,64,128]{3,2,1,0:T(8,128)(2,1)S(1)}, bf16[1,8,64,128]{3,2,1,0:T(8,128)(2,1)}, u32[]{:S(2)}) copy-start(bf16[1,8,64,128]{3,2,1,0:T(8,128)(2,1)} %param.7) | copy-start | bytes 393220
  13.2 2.4 %copy-start.5 = (bf16[1,8,64,128]{3,2,1,0:T(8,128)(2,1)S(1)}, bf16[1,8,64,128]{3,2,1,0:T(8,128)(2,1)}, u32[]{:S(2)}) copy-start(bf16[1,8,64,128]{3,2,1,0:T(8,128)(2,1)} %param.10) | copy-start | bytes 393220
  16.2 3.5 %collective-permute-start.7 = (bf16[512,128]{1,0:T(8,128)(2,1)S(1)}, bf16[512,128]{1,0:T(8,128)(2,1)S(1)}, u32[]{:S(2)}, u32[]{:S(2)}) collective-permute-start(bf16[512,128]{1,0:T(8,128)(2,1)S(1)} %get-tuple-element.45.refs_3_), channel_id=1, source_target_pairs={{0,1},{1,0},{2,3},{3,2},{4,5},{5,4},{6,7},{7,6},{8,9},{9,8},{10,11... | collective-permute-start | bytes 393224 | tf_op jit(solution)/shard_map/ppermute | solution.py:215
  16.3 5.9 %collective-permute-start.3 = (bf16[4,32,512]{2,1,0:T(8,128)(2,1)S(1)}, bf16[4,32,512]{2,1,0:T(8,128)(2,1)S(1)}, u32[]{:S(2)}, u32[]{:S(2)}) collective-permute-start(bf16[4,32,512]{2,1,0:T(8,128)(2,1)S(1)} %pad_maximum_fusion.1.refs_1_), channel_id=1, source_target_pairs={{0,4},{4,0},{8,12},{12,8},{16,20},{20,16},{24,28},{28,24},{1,5},{5... | collective-permute-start | bytes 393224 | tf_op jit(solution)/shard_map/ppermute | solution.py:215
  17.9 5.8 %collective-permute-start.10 = (bf16[512,128]{1,0:T(8,128)(2,1)S(1)}, bf16[512,128]{1,0:T(8,128)(2,1)S(1)}, u32[]{:S(2)}, u32[]{:S(2)}) collective-permute-start(bf16[512,128]{1,0:T(8,128)(2,1)S(1)} %get-tuple-element.45.refs_3_), channel_id=1, source_target_pairs={{0,3},{1,2},{2,1},{3,0},{4,7},{5,6},{6,5},{7,4},{8,11},{9,10},{10,... | collective-permute-start | bytes 393224 | tf_op jit(solution)/shard_map/ppermute | solution.py:215
  19.2 7.7 %collective-permute-start.9 = (bf16[512,128]{1,0:T(8,128)(2,1)S(1)}, bf16[512,128]{1,0:T(8,128)(2,1)S(1)}, u32[]{:S(2)}, u32[]{:S(2)}) collective-permute-start(bf16[512,128]{1,0:T(8,128)(2,1)S(1)} %get-tuple-element.45.refs_3_), channel_id=1, source_target_pairs={{0,2},{1,3},{2,0},{3,1},{4,6},{5,7},{6,4},{7,5},{8,10},{9,11},{10,... | collective-permute-start | bytes 393224 | tf_op jit(solution)/shard_map/ppermute | solution.py:215
  19.7 7.1 %collective-permute-start.8 = (bf16[4,32,512]{2,1,0:T(8,128)(2,1)S(1)}, bf16[4,32,512]{2,1,0:T(8,128)(2,1)S(1)}, u32[]{:S(2)}, u32[]{:S(2)}) collective-permute-start(bf16[4,32,512]{2,1,0:T(8,128)(2,1)S(1)} %pad_maximum_fusion.1.refs_1_), channel_id=1, source_target_pairs={{4,8},{8,4},{12,16},{16,12},{20,24},{24,20},{5,9},{9,5},{13,17},{1... | collective-permute-start | bytes 393224 | tf_op jit(solution)/shard_map/ppermute | solution.py:225
  22.2 7.8 %collective-permute-start.12 = (bf16[256,128]{1,0:T(8,128)(2,1)S(1)}, bf16[256,128]{1,0:T(8,128)(2,1)S(1)}, u32[]{:S(2)}, u32[]{:S(2)}) collective-permute-start(bf16[256,128]{1,0:T(8,128)(2,1)S(1)} %get-tuple-element.52), channel_id=1, source_target_pairs={{0,1},{1,0},{2,3},{3,2},{4,5},{5,4},{6,7},{7,6},{8,9},{9,8},{10,11... | collective-permute-start | bytes 196616 | tf_op jit(solution)/shard_map/ppermute | solution.py:215
  22.2 7.8 %collective-permute-start.13 = (bf16[256,128]{1,0:T(8,128)(2,1)S(1)}, bf16[256,128]{1,0:T(8,128)(2,1)S(1)}, u32[]{:S(2)}, u32[]{:S(2)}) collective-permute-start(bf16[256,128]{1,0:T(8,128)(2,1)S(1)} %get-tuple-element.53), channel_id=1, source_target_pairs={{0,2},{1,3},{2,0},{3,1},{4,6},{5,7},{6,4},{7,5},{8,10},{9,11},{10,... | collective-permute-start | bytes 196616 | tf_op jit(solution)/shard_map/ppermute | solution.py:215
  23.7 6.3 %collective-permute-start.14 = (bf16[256,128]{1,0:T(8,128)(2,1)S(1)}, bf16[256,128]{1,0:T(8,128)(2,1)S(1)}, u32[]{:S(2)}, u32[]{:S(2)}) collective-permute-start(bf16[256,128]{1,0:T(8,128)(2,1)S(1)} %get-tuple-element.54), channel_id=1, source_target_pairs={{0,3},{1,2},{2,1},{3,0},{4,7},{5,6},{6,5},{7,4},{8,11},{9,10},{10,... | collective-permute-start | bytes 196616 | tf_op jit(solution)/shard_map/ppermute | solution.py:215
  28.3 19.8 %copy-start.1 = (bf16[3,3,3,128,128]{4,3,2,1,0:T(8,128)(2,1)S(1)}, bf16[3,3,3,128,128]{4,3,2,1,0:T(8,128)(2,1)}, u32[]{:S(2)}) copy-start(bf16[3,3,3,128,128]{4,3,2,1,0:T(8,128)(2,1)} %weight.1) | copy-start | bytes 2654212
  28.4 4.8 %collective-permute-start.11 = (bf16[432,128]{1,0:T(8,128)(2,1)S(1)}, bf16[432,128]{1,0:T(8,128)(2,1)S(1)}, u32[]{:S(2)}, u32[]{:S(2)}) collective-permute-start(bf16[432,128]{1,0:T(8,128)(2,1)S(1)} %get-tuple-element.50), channel_id=1, source_target_pairs={{0,4},{4,0},{8,12},{12,8},{16,20},{20,16},{24,28},{28,24},{1,5},{5... | collective-permute-start | bytes 331784 | tf_op jit(solution)/shard_map/ppermute | solution.py:215
  33.2 13.0 %collective-permute-start.15 = (bf16[688,128]{1,0:T(8,128)(2,1)S(1)}, bf16[688,128]{1,0:T(8,128)(2,1)S(1)}, u32[]{:S(2)}, u32[]{:S(2)}) collective-permute-start(bf16[688,128]{1,0:T(8,128)(2,1)S(1)} %pad_maximum_fusion), channel_id=1, source_target_pairs={{0,16},{4,20},{8,24},{12,28},{16,0},{20,4},{24,8},{28,12},{1,17},{... | collective-permute-start | bytes 528392 | tf_op jit(solution)/shard_map/ppermute | solution.py:215
  36.9 5.1 %collective-permute-start.17 = (bf16[10,64,128]{2,1,0:T(8,128)(2,1)S(1)}, bf16[10,64,128]{2,1,0:T(8,128)(2,1)S(1)}, u32[]{:S(2)}, u32[]{:S(2)}) collective-permute-start(bf16[10,64,128]{2,1,0:T(8,128)(2,1)S(1)} %get-tuple-element.55.own), channel_id=1, source_target_pairs={{4,8},{8,4},{12,16},{16,12},{20,24},{24,20},{5,9},{9,5},{13,17},{1... | collective-permute-start | bytes 491528 | tf_op jit(solution)/shard_map/ppermute | solution.py:225
  37.6 8.6 %collective-permute-start.16 = (bf16[10,64,128]{2,1,0:T(8,128)(2,1)S(1)}, bf16[10,64,128]{2,1,0:T(8,128)(2,1)S(1)}, u32[]{:S(2)}, u32[]{:S(2)}) collective-permute-start(bf16[10,64,128]{2,1,0:T(8,128)(2,1)S(1)} %get-tuple-element.55.own), channel_id=1, source_target_pairs={{0,4},{4,0},{8,12},{12,8},{16,20},{20,16},{24,28},{28,24},{1,5},{5... | collective-permute-start | bytes 491528 | tf_op jit(solution)/shard_map/ppermute | solution.py:215
  46.3 5.5 %collective-permute-start.18 = (bf16[688,128]{1,0:T(8,128)(2,1)S(1)}, bf16[688,128]{1,0:T(8,128)(2,1)S(1)}, u32[]{:S(2)}, u32[]{:S(2)}) collective-permute-start(bf16[688,128]{1,0:T(8,128)(2,1)S(1)} %add_convert_fusion), channel_id=1, source_target_pairs={{0,8},{4,12},{8,0},{12,4},{16,24},{20,28},{24,16},{28,20},{1,9},{5... | collective-permute-start | bytes 528392 | tf_op jit(solution)/shard_map/ppermute | solution.py:215
  52.0 6.0 %collective-permute-start.22 = (bf16[688,128]{1,0:T(8,128)(2,1)S(1)}, bf16[688,128]{1,0:T(8,128)(2,1)S(1)}, u32[]{:S(2)}, u32[]{:S(2)}) collective-permute-start(bf16[688,128]{1,0:T(8,128)(2,1)S(1)} %multiply_convert_fusion.refs_0_), channel_id=1, source_target_pairs={{0,4},{4,0},{8,12},{12,8},{16,20},{20,16},{24,28},{28,24},{1,5},{5... | collective-permute-start | bytes 528392 | tf_op jit(solution)/shard_map/ppermute | solution.py:215
  54.5 6.8 %collective-permute-start.20 = (bf16[688,128]{1,0:T(8,128)(2,1)S(1)}, bf16[688,128]{1,0:T(8,128)(2,1)S(1)}, u32[]{:S(2)}, u32[]{:S(2)}) collective-permute-start(bf16[688,128]{1,0:T(8,128)(2,1)S(1)} %multiply_convert_fusion.refs_0_), channel_id=1, source_target_pairs={{0,2},{1,3},{2,0},{3,1},{4,6},{5,7},{6,4},{7,5},{8,10},{9,11},{10,... | collective-permute-start | bytes 528392 | tf_op jit(solution)/shard_map/ppermute | solution.py:215
  57.9 5.5 %collective-permute-start.24 = (bf16[688,128]{1,0:T(8,128)(2,1)S(1)}, bf16[688,128]{1,0:T(8,128)(2,1)S(1)}, u32[]{:S(2)}, u32[]{:S(2)}) collective-permute-start(bf16[688,128]{1,0:T(8,128)(2,1)S(1)} %collective-permute-done.22.refs_4_), channel_id=1, source_target_pairs={{0,2},{1,3},{2,0},{3,1},{4,6},{5,7},{6,4},{7,5},{8,10},{9,11},{10,... | collective-permute-start | bytes 528392 | tf_op jit(solution)/shard_map/ppermute | solution.py:215
  59.4 4.0 %collective-permute-start.19 = (bf16[688,128]{1,0:T(8,128)(2,1)S(1)}, bf16[688,128]{1,0:T(8,128)(2,1)S(1)}, u32[]{:S(2)}, u32[]{:S(2)}) collective-permute-start(bf16[688,128]{1,0:T(8,128)(2,1)S(1)} %multiply_convert_fusion.refs_0_), channel_id=1, source_target_pairs={{0,1},{1,0},{2,3},{3,2},{4,5},{5,4},{6,7},{7,6},{8,9},{9,8},{10,11... | collective-permute-start | bytes 528392 | tf_op jit(solution)/shard_map/ppermute | solution.py:215
  59.4 4.0 %collective-permute-start.23 = (bf16[688,128]{1,0:T(8,128)(2,1)S(1)}, bf16[688,128]{1,0:T(8,128)(2,1)S(1)}, u32[]{:S(2)}, u32[]{:S(2)}) collective-permute-start(bf16[688,128]{1,0:T(8,128)(2,1)S(1)} %collective-permute-done.22.refs_4_), channel_id=1, source_target_pairs={{0,1},{1,0},{2,3},{3,2},{4,5},{5,4},{6,7},{7,6},{8,9},{9,8},{10,11... | collective-permute-start | bytes 528392 | tf_op jit(solution)/shard_map/ppermute | solution.py:215
  61.3 2.1 %collective-permute-start.21 = (bf16[688,128]{1,0:T(8,128)(2,1)S(1)}, bf16[688,128]{1,0:T(8,128)(2,1)S(1)}, u32[]{:S(2)}, u32[]{:S(2)}) collective-permute-start(bf16[688,128]{1,0:T(8,128)(2,1)S(1)} %collective-permute-done.20.refs_2_), channel_id=1, source_target_pairs={{0,1},{1,0},{2,3},{3,2},{4,5},{5,4},{6,7},{7,6},{8,9},{9,8},{10,11... | collective-permute-start | bytes 528392 | tf_op jit(solution)/shard_map/ppermute | solution.py:215
  63.4 1.4 %collective-permute-start.25 = (bf16[688,128]{1,0:T(8,128)(2,1)S(1)}, bf16[688,128]{1,0:T(8,128)(2,1)S(1)}, u32[]{:S(2)}, u32[]{:S(2)}) collective-permute-start(bf16[688,128]{1,0:T(8,128)(2,1)S(1)} %collective-permute-done.24.refs_6_), channel_id=1, source_target_pairs={{0,1},{1,0},{2,3},{3,2},{4,5},{5,4},{6,7},{7,6},{8,9},{9,8},{10,11... | collective-permute-start | bytes 528392 | tf_op jit(solution)/shard_map/ppermute | solution.py:215

commit v17 on v16

--- a/solution.py
+++ b/solution.py
@@ -215,6 +215,16 @@
     return lax.ppermute(value, axis, [(i, i ^ code) for i in range(lax.axis_size(axis))])
 
 
+def crossed(value, code_gz, code_gy):
+    count = lax.axis_size("gy")
+    pairs = [
+        (i * count + j, (i ^ code_gz) * count + (j ^ code_gy))
+        for i in range(lax.axis_size("gz"))
+        for j in range(count)
+    ]
+    return lax.ppermute(value, ("gz", "gy"), pairs)
+
+
 def even_pairs(value):
     return swapped(value, "gz", 1)
 
@@ -345,15 +355,21 @@
         row < 27 * half, 1 / math.sqrt(cell_total), 1 / math.sqrt(cell_total // 8)
     )
     total = (total * scale).astype(BF16)
-    pair = [total, swapped(total, "gz", 1)]
-    blocks = []
-    for index, block in enumerate(pair):
-        line = [block]
-        code = n_gy // 2
-        while code:
-            line = line + [swapped(value, "gy", code) for value in line]
-            code //= 2
-        blocks += [line[reversed_bits(place, n_gy)] for place in range(n_gy)]
+    if n_gy == 4:
+        lines = [
+            [total, swapped(total, "gy", 2)],
+            [swapped(total, "gz", 1), crossed(total, 1, 2)],
+        ]
+        blocks = []
+        for near_block, far_block in lines:
+            blocks += [near_block, swapped(near_block, "gy", 1)]
+            blocks += [far_block, swapped(far_block, "gy", 1)]
+    else:
+        blocks = [
+            swapped(block, "gy", code) if code else block
+            for block in (total, swapped(total, "gz", 1))
+            for code in range(n_gy)
+        ]
     conv_grad, down_grad = call(
         lambda *refs: place_kernel(n_gy, *refs),
         (

time: 66.3 us -> 64.9 us (0.979)
  starting transfers between devices: 34.4 us -> 32.7 us
    ppermute x24 -> x23, starting transfers between devices: 33 us -> 27.9 us  [swapped(): lax.ppermute(value, axis, [(i, i ^ code) for i in range(lax.axis_size(axi...]
    ppermute x0 -> x1, waiting for transfers between devices: none -> 4.56 us  [crossed(): return lax.ppermute(value, ('gz', 'gy'), pairs)]
    ppermute x24 -> x23, waiting for transfers between devices: 24.2 us -> 20 us  [swapped(): lax.ppermute(value, axis, [(i, i ^ code) for i in range(lax.axis_size(axi...]
    ppermute x0 -> x1, starting transfers between devices: none -> 3.47 us  [crossed(): return lax.ppermute(value, ('gz', 'gy'), pairs)]
  transfers between devices with their start and end apart: 26 -> 26, of which waited for: 11 -> 12; matrix products, arithmetic and copies ran while one was open for 0% -> 0% of each run, Pallas kernels for 5% -> 5%
where the time goes in v17:
time: 64.9 us; the launch traced here: 64.7 us
  starting transfers between devices  32.7 us (50%)
  waiting for transfers between devices  24.6 us (38%)
  Pallas kernels  5.34 us (8%)
  local copies, waits for them, and re-layouts  1 us (2%)
  between operations  0.81 us (1%)
    ppermute x23, starting transfers between devices, swapped(): lax.ppermute(value, axis, [(i, i ^ code) for i in range(lax.axis_size(axi...  27.9 us
    ppermute x23, waiting for transfers between devices, swapped(): lax.ppermute(value, axis, [(i, i ^ code) for i in range(lax.axis_size(axi...  20 us
    pallas_call x6, Pallas kernels, call(): pl.pallas_call(kernel, out_shape=out_shape, scratch_shapes=list(scratch),...  5.34 us
    ppermute x1, waiting for transfers between devices, crossed(): return lax.ppermute(value, ('gz', 'gy'), pairs)  4.56 us
    ppermute x1, starting transfers between devices, crossed(): return lax.ppermute(value, ('gz', 'gy'), pairs)  3.47 us
    ppermute x2, starting transfers between devices, odd_pairs(): return lax.ppermute(value, 'gz', pairs)  1.32 us
  transfers between devices with their start and end apart: 26, of which 12 were waited for; matrix products, arithmetic and copies ran while one was open for 0% of the time, Pallas kernels for 5%

profile of v17, /device:TPU:0, one launch (start us, length us, event | category | flops | bytes accessed | tf_op | source)
XLA Modules:
  0.0 64.7 jit_solution(7624115545588609037)
XLA Ops:
  0.6 0.0 copy-start
  0.7 1.0 %copy-done.2 = bf16[4,4,32,32]{3,2,1,0:T(8,128)(2,1)S(1)} copy-done((bf16[4,4,32,32]{3,2,1,0:T(8,128)(2,1)S(1)}, bf16[4,4,32,32]{3,2,1,0:T(8,128)(2,1)}, u32[]{:S(2)}) %copy-start.2) | copy-done | bytes 32792
  1.6 0.1 shard_map.86
  1.7 4.1 %collective-permute-start.4 = (bf16[2,32,128]{2,1,0:T(8,128)(2,1)S(1)}, bf16[2,32,128]{2,1,0:T(8,128)(2,1)S(1)}, u32[]{:S(2)}, u32[]{:S(2)}) collective-permute-start(bf16[2,32,128]{2,1,0:T(8,128)(2,1)S(1)} %get-tuple-element.38), channel_id=1, source_target_pairs={{0,16},{4,20},{8,24},{12,28},{16,0},{20,4},{24,8},{28,12},{1,17},{... | collective-permute-start | bytes 49160 | tf_op jit(solution)/shard_map/ppermute | solution.py:215
  5.8 0.1 shard_map.85
  5.9 0.1 collective-permute-start
  6.0 1.6 %collective-permute-start.1 = (bf16[32,512]{1,0:T(8,128)(2,1)S(1)}, bf16[32,512]{1,0:T(8,128)(2,1)S(1)}, u32[]{:S(2)}, u32[]{:S(2)}) collective-permute-start(bf16[32,512]{1,0:T(8,128)(2,1)S(1)} %get-tuple-element.35), channel_id=1, source_target_pairs={{0,2},{1,3},{2,0},{3,1},{4,6},{5,7},{6,4},{7,5},{8,10},{9,11},{10,... | collective-permute-start | bytes 98312 | tf_op jit(solution)/shard_map/ppermute | solution.py:215
  7.6 0.3 collective-permute-start.2
  7.9 0.0 collective-permute-done.4
  7.9 1.6 %collective-permute-start.5 = (bf16[1,2,32,128]{3,2,1,0:T(8,128)(2,1)S(1)}, bf16[1,2,32,128]{3,2,1,0:T(8,128)(2,1)S(1)}, u32[]{:S(2)}, u32[]{:S(2)}) collective-permute-start(bf16[1,2,32,128]{3,2,1,0:T(8,128)(2,1)S(1)} %get-tuple-element.64), channel_id=1, source_target_pairs={{0,8},{4,12},{8,0},{12,4},{16,24},{20,28},{24,16},{28,20},{1,9},{5... | collective-permute-start | bytes 49160 | tf_op jit(solution)/shard_map/ppermute | solution.py:215
  9.5 2.1 %collective-permute-done.5 = bf16[1,2,32,128]{3,2,1,0:T(8,128)(2,1)S(1)} collective-permute-done((bf16[1,2,32,128]{3,2,1,0:T(8,128)(2,1)S(1)}, bf16[1,2,32,128]{3,2,1,0:T(8,128)(2,1)S(1)}, u32[]{:S(2)}, u32[]{:S(2)}) %collective-permute-start.5) | collective-permute-done | bytes 16416 | tf_op jit(solution)/shard_map/ppermute | solution.py:215
  11.7 1.5 %collective-permute-start.6 = (bf16[4,32,128]{2,1,0:T(8,128)(2,1)S(1)}, bf16[4,32,128]{2,1,0:T(8,128)(2,1)S(1)}, u32[]{:S(2)}, u32[]{:S(2)}) collective-permute-start(bf16[4,32,128]{2,1,0:T(8,128)(2,1)S(1)} %maximum_bitcast_fusion.refs_3_), channel_id=1, source_target_pairs={{0,4},{4,0},{8,12},{12,8},{16,20},{20,16},{24,28},{28,24},{1,5},{5... | collective-permute-start | bytes 98312 | tf_op jit(solution)/shard_map/ppermute | solution.py:215
  13.2 0.0 collective-permute-done
  13.2 0.0 collective-permute-done.1
  13.2 0.0 collective-permute-done.2
  13.2 0.0 copy-start.4
  13.2 0.0 copy-start.5
  13.3 2.3 %collective-permute-done.6.refs_4_ = bf16[4,32,128]{2,1,0:T(8,128)(2,1)S(1)} collective-permute-done((bf16[4,32,128]{2,1,0:T(8,128)(2,1)S(1)}, bf16[4,32,128]{2,1,0:T(8,128)(2,1)S(1)}, u32[]{:S(2)}, u32[]{:S(2)}) %collective-permute-start.6) | collective-permute-done | bytes 32800 | tf_op jit(solution)/shard_map/ppermute | solution.py:215
  15.6 0.6 shard_map.87
  16.2 0.1 collective-permute-start.7
  16.3 1.6 %collective-permute-start.3 = (bf16[4,32,512]{2,1,0:T(8,128)(2,1)S(1)}, bf16[4,32,512]{2,1,0:T(8,128)(2,1)S(1)}, u32[]{:S(2)}, u32[]{:S(2)}) collective-permute-start(bf16[4,32,512]{2,1,0:T(8,128)(2,1)S(1)} %pad_maximum_fusion.1.refs_1_), channel_id=1, source_target_pairs={{0,4},{4,0},{8,12},{12,8},{16,20},{20,16},{24,28},{28,24},{1,5},{5... | collective-permute-start | bytes 393224 | tf_op jit(solution)/shard_map/ppermute | solution.py:215
  17.9 1.3 %collective-permute-start.10 = (bf16[512,128]{1,0:T(8,128)(2,1)S(1)}, bf16[512,128]{1,0:T(8,128)(2,1)S(1)}, u32[]{:S(2)}, u32[]{:S(2)}) collective-permute-start(bf16[512,128]{1,0:T(8,128)(2,1)S(1)} %get-tuple-element.45.refs_3_), channel_id=1, source_target_pairs={{0,3},{1,2},{2,1},{3,0},{4,7},{5,6},{6,5},{7,4},{8,11},{9,10},{10,... | collective-permute-start | bytes 393224 | tf_op jit(solution)/shard_map/ppermute | solution.py:215
  19.2 0.5 collective-permute-start.9
  19.7 0.0 collective-permute-done.7.refs_4_
  19.7 0.7 %collective-permute-start.8 = (bf16[4,32,512]{2,1,0:T(8,128)(2,1)S(1)}, bf16[4,32,512]{2,1,0:T(8,128)(2,1)S(1)}, u32[]{:S(2)}, u32[]{:S(2)}) collective-permute-start(bf16[4,32,512]{2,1,0:T(8,128)(2,1)S(1)} %pad_maximum_fusion.1.refs_1_), channel_id=1, source_target_pairs={{4,8},{8,4},{12,16},{16,12},{20,24},{24,20},{5,9},{9,5},{13,17},{1... | collective-permute-start | bytes 393224 | tf_op jit(solution)/shard_map/ppermute | solution.py:235
  20.4 1.9 %collective-permute-done.3.refs_0_ = bf16[4,32,512]{2,1,0:T(8,128)(2,1)S(1)} collective-permute-done((bf16[4,32,512]{2,1,0:T(8,128)(2,1)S(1)}, bf16[4,32,512]{2,1,0:T(8,128)(2,1)S(1)}, u32[]{:S(2)}, u32[]{:S(2)}) %collective-permute-start.3) | collective-permute-done | bytes 131104 | tf_op jit(solution)/shard_map/ppermute | solution.py:215
  22.2 0.0 collective-permute-start.12
  22.2 1.5 %collective-permute-start.13 = (bf16[256,128]{1,0:T(8,128)(2,1)S(1)}, bf16[256,128]{1,0:T(8,128)(2,1)S(1)}, u32[]{:S(2)}, u32[]{:S(2)}) collective-permute-start(bf16[256,128]{1,0:T(8,128)(2,1)S(1)} %get-tuple-element.53), channel_id=1, source_target_pairs={{0,2},{1,3},{2,0},{3,1},{4,6},{5,7},{6,4},{7,5},{8,10},{9,11},{10,... | collective-permute-start | bytes 196616 | tf_op jit(solution)/shard_map/ppermute | solution.py:215
  23.7 0.0 collective-permute-done.10.refs_6_
  23.7 1.2 %collective-permute-start.14 = (bf16[256,128]{1,0:T(8,128)(2,1)S(1)}, bf16[256,128]{1,0:T(8,128)(2,1)S(1)}, u32[]{:S(2)}, u32[]{:S(2)}) collective-permute-start(bf16[256,128]{1,0:T(8,128)(2,1)S(1)} %get-tuple-element.54), channel_id=1, source_target_pairs={{0,3},{1,2},{2,1},{3,0},{4,7},{5,6},{6,5},{7,4},{8,11},{9,10},{10,... | collective-permute-start | bytes 196616 | tf_op jit(solution)/shard_map/ppermute | solution.py:215
  25.0 1.9 %collective-permute-done.9.refs_5_ = bf16[512,128]{1,0:T(8,128)(2,1)S(1)} collective-permute-done((bf16[512,128]{1,0:T(8,128)(2,1)S(1)}, bf16[512,128]{1,0:T(8,128)(2,1)S(1)}, u32[]{:S(2)}, u32[]{:S(2)}) %collective-permute-start.9) | collective-permute-done | bytes 131104 | tf_op jit(solution)/shard_map/ppermute | solution.py:215
  26.8 0.0 collective-permute-done.8.refs_2_
  26.8 1.5 %shard_map.88 = (f32[432,128]{1,0:T(8,128)S(1)}, bf16[432,128]{1,0:T(8,128)(2,1)S(1)}, bf16[10,64,128]{2,1,0:T(8,128)(2,1)S(1)}) custom-call(bf16[4,32,512]{2,1,0:T(8,128)(2,1)S(1)} %collective-permute-done.3.refs_0_, bf16[4,32,512]{2,1,0:T(8,128)(2,1)S(1)} %pad_maximum_fusion.1.refs_1_, bf16[4,32,512]{2,1,0:T(8,128)(2,1)S(1)} %collective-permute-done.8.refs_2_, ...), custom_call_target="tpu_custom_call" | custom-call | tf_op jit(solution)/shard_map/pallas_call | solution.py:16
  28.3 0.0 copy-start.1
  28.4 1.7 %collective-permute-start.11 = (bf16[432,128]{1,0:T(8,128)(2,1)S(1)}, bf16[432,128]{1,0:T(8,128)(2,1)S(1)}, u32[]{:S(2)}, u32[]{:S(2)}) collective-permute-start(bf16[432,128]{1,0:T(8,128)(2,1)S(1)} %get-tuple-element.50), channel_id=1, source_target_pairs={{0,4},{4,0},{8,12},{12,8},{16,20},{20,16},{24,28},{28,24},{1,5},{5... | collective-permute-start | bytes 331784 | tf_op jit(solution)/shard_map/ppermute | solution.py:215
  30.0 0.0 collective-permute-done.12
  30.1 0.0 collective-permute-done.13
  30.1 0.0 collective-permute-done.14
  30.1 3.1 %collective-permute-done.11 = bf16[432,128]{1,0:T(8,128)(2,1)S(1)} collective-permute-done((bf16[432,128]{1,0:T(8,128)(2,1)S(1)}, bf16[432,128]{1,0:T(8,128)(2,1)S(1)}, u32[]{:S(2)}, u32[]{:S(2)}) %collective-permute-start.11) | collective-permute-done | bytes 110624 | tf_op jit(solution)/shard_map/ppermute | solution.py:215
  33.2 3.7 %collective-permute-start.15 = (bf16[688,128]{1,0:T(8,128)(2,1)S(1)}, bf16[688,128]{1,0:T(8,128)(2,1)S(1)}, u32[]{:S(2)}, u32[]{:S(2)}) collective-permute-start(bf16[688,128]{1,0:T(8,128)(2,1)S(1)} %pad_maximum_fusion), channel_id=1, source_target_pairs={{0,16},{4,20},{8,24},{12,28},{16,0},{20,4},{24,8},{28,12},{1,17},{... | collective-permute-start | bytes 528392 | tf_op jit(solution)/shard_map/ppermute | solution.py:215
  36.9 0.7 %collective-permute-start.17 = (bf16[10,64,128]{2,1,0:T(8,128)(2,1)S(1)}, bf16[10,64,128]{2,1,0:T(8,128)(2,1)S(1)}, u32[]{:S(2)}, u32[]{:S(2)}) collective-permute-start(bf16[10,64,128]{2,1,0:T(8,128)(2,1)S(1)} %get-tuple-element.55.own), channel_id=1, source_target_pairs={{4,8},{8,4},{12,16},{16,12},{20,24},{24,20},{5,9},{9,5},{13,17},{1... | collective-permute-start | bytes 491528 | tf_op jit(solution)/shard_map/ppermute | solution.py:235
  37.6 4.4 %collective-permute-start.16 = (bf16[10,64,128]{2,1,0:T(8,128)(2,1)S(1)}, bf16[10,64,128]{2,1,0:T(8,128)(2,1)S(1)}, u32[]{:S(2)}, u32[]{:S(2)}) collective-permute-start(bf16[10,64,128]{2,1,0:T(8,128)(2,1)S(1)} %get-tuple-element.55.own), channel_id=1, source_target_pairs={{0,4},{4,0},{8,12},{12,8},{16,20},{20,16},{24,28},{28,24},{1,5},{5... | collective-permute-start | bytes 491528 | tf_op jit(solution)/shard_map/ppermute | solution.py:215
  42.0 0.0 collective-permute-done.17.odd
  42.0 4.2 %collective-permute-done.16.even = bf16[10,64,128]{2,1,0:T(8,128)(2,1)S(1)} collective-permute-done((bf16[10,64,128]{2,1,0:T(8,128)(2,1)S(1)}, bf16[10,64,128]{2,1,0:T(8,128)(2,1)S(1)}, u32[]{:S(2)}, u32[]{:S(2)}) %collective-permute-start.16) | collective-permute-done | bytes 163872 | tf_op jit(solution)/shard_map/ppermute | solution.py:215
  46.2 0.0 collective-permute-done.15
  46.3 1.8 %collective-permute-start.18 = (bf16[688,128]{1,0:T(8,128)(2,1)S(1)}, bf16[688,128]{1,0:T(8,128)(2,1)S(1)}, u32[]{:S(2)}, u32[]{:S(2)}) collective-permute-start(bf16[688,128]{1,0:T(8,128)(2,1)S(1)} %add_convert_fusion), channel_id=1, source_target_pairs={{0,8},{4,12},{8,0},{12,4},{16,24},{20,28},{24,16},{28,20},{1,9},{5... | collective-permute-start | bytes 528392 | tf_op jit(solution)/shard_map/ppermute | solution.py:215
  48.1 1.7 %shard_map.89 = bf16[8,64,128]{2,1,0:T(8,128)(2,1)} custom-call(bf16[10,64,128]{2,1,0:T(8,128)(2,1)S(1)} %collective-permute-done.16.even, bf16[10,64,128]{2,1,0:T(8,128)(2,1)S(1)} %get-tuple-element.55.own, bf16[10,64,128]{2,1,0:T(8,128)(2,1)S(1)} %collective-permute-done.17.odd, bf16[3,3,3,128,128]{4,3,2,1,0:T(8,128)(2,1)S(1)} %copy-done.1), custom_call_target="tpu_custom_call" | custom-call | tf_op jit(solution)/shard_map/pallas_call | solution.py:16
  49.9 1.9 %collective-permute-done.18 = bf16[688,128]{1,0:T(8,128)(2,1)S(1)} collective-permute-done((bf16[688,128]{1,0:T(8,128)(2,1)S(1)}, bf16[688,128]{1,0:T(8,128)(2,1)S(1)}, u32[]{:S(2)}, u32[]{:S(2)}) %collective-permute-start.18) | collective-permute-done | bytes 176160 | tf_op jit(solution)/shard_map/ppermute | solution.py:215
  51.8 0.2 multiply_convert_fusion.refs_0_
  52.0 3.5 %collective-permute-start.24 = (bf16[688,128]{1,0:T(8,128)(2,1)S(1)}, bf16[688,128]{1,0:T(8,128)(2,1)S(1)}, u32[]{:S(2)}, u32[]{:S(2)}) collective-permute-start(bf16[688,128]{1,0:T(8,128)(2,1)S(1)} %multiply_convert_fusion.refs_0_), channel_id=1, source_target_pairs={{0,6},{1,7},{2,4},{3,5},{4,2},{5,3},{6,0},{7,1},{8,14},{9,15},{10,... | collective-permute-start | bytes 528392 | tf_op jit(solution)/shard_map/ppermute | solution.py:225
  55.4 0.0 collective-permute-start.22
  55.4 0.6 collective-permute-start.20
  56.1 0.0 collective-permute-start.19
  56.1 4.6 %collective-permute-done.24.refs_6_ = bf16[688,128]{1,0:T(8,128)(2,1)S(1)} collective-permute-done((bf16[688,128]{1,0:T(8,128)(2,1)S(1)}, bf16[688,128]{1,0:T(8,128)(2,1)S(1)}, u32[]{:S(2)}, u32[]{:S(2)}) %collective-permute-start.24) | collective-permute-done | bytes 176160 | tf_op jit(solution)/shard_map/ppermute | solution.py:225
  60.6 0.0 collective-permute-start.25
  60.6 1.1 %collective-permute-done.22.refs_4_ = bf16[688,128]{1,0:T(8,128)(2,1)S(1)} collective-permute-done((bf16[688,128]{1,0:T(8,128)(2,1)S(1)}, bf16[688,128]{1,0:T(8,128)(2,1)S(1)}, u32[]{:S(2)}, u32[]{:S(2)}) %collective-permute-start.22) | collective-permute-done | bytes 176160 | tf_op jit(solution)/shard_map/ppermute | solution.py:215
  61.8 0.0 collective-permute-start.23
  61.8 0.3 collective-permute-done.20.refs_2_
  62.0 0.3 collective-permute-start.21
  62.3 0.0 collective-permute-done.19.refs_1_
  62.3 0.0 collective-permute-done.25.refs_7_
  62.3 0.9 %collective-permute-done.23.refs_5_ = bf16[688,128]{1,0:T(8,128)(2,1)S(1)} collective-permute-done((bf16[688,128]{1,0:T(8,128)(2,1)S(1)}, bf16[688,128]{1,0:T(8,128)(2,1)S(1)}, u32[]{:S(2)}, u32[]{:S(2)}) %collective-permute-start.23) | collective-permute-done | bytes 176160 | tf_op jit(solution)/shard_map/ppermute | solution.py:215
  63.2 0.3 collective-permute-done.21.refs_3_
  63.4 1.3 %shard_map.90 = (bf16[27,4,2,16,128]{4,3,2,1,0:T(8,128)(2,1)}, bf16[2,4,128,256]{3,2,1,0:T(8,128)(2,1)}) custom-call(bf16[688,128]{1,0:T(8,128)(2,1)S(1)} %multiply_convert_fusion.refs_0_, bf16[688,128]{1,0:T(8,128)(2,1)S(1)} %collective-permute-done.19.refs_1_, bf16[688,128]{1,0:T(8,128)(2,1)S(1)} %collective-permute-done.20.refs_2_, ...), custom_call_target="tpu_custom_call" | custom-call | tf_op jit(solution)/shard_map/pallas_call | solution.py:16
  (16 shorter events, 0.2 us)
Async XLA Ops:
  0.6 8.9 %copy-start = (bf16[2,2,2,128,256]{4,3,2,1,0:T(8,128)(2,1)S(1)}, bf16[2,2,2,128,256]{4,3,2,1,0:T(8,128)(2,1)}, u32[]{:S(2)}) copy-start(bf16[2,2,2,128,256]{4,3,2,1,0:T(8,128)(2,1)} %param.9) | copy-start | bytes 1572868
  0.6 1.0 %copy-start.2 = (bf16[4,4,32,32]{3,2,1,0:T(8,128)(2,1)S(1)}, bf16[4,4,32,32]{3,2,1,0:T(8,128)(2,1)}, u32[]{:S(2)}) copy-start(bf16[4,4,32,32]{3,2,1,0:T(8,128)(2,1)} %param.11) | copy-start | bytes 98308
  1.6 4.2 %copy-start.3 = (bf16[1,8,64,128]{3,2,1,0:T(8,128)(2,1)S(1)}, bf16[1,8,64,128]{3,2,1,0:T(8,128)(2,1)}, u32[]{:S(2)}) copy-start(bf16[1,8,64,128]{3,2,1,0:T(8,128)(2,1)} %param.6) | copy-start | bytes 393220
  1.7 6.2 %collective-permute-start.4 = (bf16[2,32,128]{2,1,0:T(8,128)(2,1)S(1)}, bf16[2,32,128]{2,1,0:T(8,128)(2,1)S(1)}, u32[]{:S(2)}, u32[]{:S(2)}) collective-permute-start(bf16[2,32,128]{2,1,0:T(8,128)(2,1)S(1)} %get-tuple-element.38), channel_id=1, source_target_pairs={{0,16},{4,20},{8,24},{12,28},{16,0},{20,4},{24,8},{28,12},{1,17},{... | collective-permute-start | bytes 49160 | tf_op jit(solution)/shard_map/ppermute | solution.py:215
  5.9 7.3 %collective-permute-start = (bf16[32,512]{1,0:T(8,128)(2,1)S(1)}, bf16[32,512]{1,0:T(8,128)(2,1)S(1)}, u32[]{:S(2)}, u32[]{:S(2)}) collective-permute-start(bf16[32,512]{1,0:T(8,128)(2,1)S(1)} %get-tuple-element.34), channel_id=1, source_target_pairs={{0,1},{1,0},{2,3},{3,2},{4,5},{5,4},{6,7},{7,6},{8,9},{9,8},{10,11... | collective-permute-start | bytes 98312 | tf_op jit(solution)/shard_map/ppermute | solution.py:215
  6.0 7.2 %collective-permute-start.1 = (bf16[32,512]{1,0:T(8,128)(2,1)S(1)}, bf16[32,512]{1,0:T(8,128)(2,1)S(1)}, u32[]{:S(2)}, u32[]{:S(2)}) collective-permute-start(bf16[32,512]{1,0:T(8,128)(2,1)S(1)} %get-tuple-element.35), channel_id=1, source_target_pairs={{0,2},{1,3},{2,0},{3,1},{4,6},{5,7},{6,4},{7,5},{8,10},{9,11},{10,... | collective-permute-start | bytes 98312 | tf_op jit(solution)/shard_map/ppermute | solution.py:215
  7.6 5.7 %collective-permute-start.2 = (bf16[32,512]{1,0:T(8,128)(2,1)S(1)}, bf16[32,512]{1,0:T(8,128)(2,1)S(1)}, u32[]{:S(2)}, u32[]{:S(2)}) collective-permute-start(bf16[32,512]{1,0:T(8,128)(2,1)S(1)} %get-tuple-element.36), channel_id=1, source_target_pairs={{0,3},{1,2},{2,1},{3,0},{4,7},{5,6},{6,5},{7,4},{8,11},{9,10},{10,... | collective-permute-start | bytes 98312 | tf_op jit(solution)/shard_map/ppermute | solution.py:215
  7.9 3.8 %collective-permute-start.5 = (bf16[1,2,32,128]{3,2,1,0:T(8,128)(2,1)S(1)}, bf16[1,2,32,128]{3,2,1,0:T(8,128)(2,1)S(1)}, u32[]{:S(2)}, u32[]{:S(2)}) collective-permute-start(bf16[1,2,32,128]{3,2,1,0:T(8,128)(2,1)S(1)} %get-tuple-element.64), channel_id=1, source_target_pairs={{0,8},{4,12},{8,0},{12,4},{16,24},{20,28},{24,16},{28,20},{1,9},{5... | collective-permute-start | bytes 49160 | tf_op jit(solution)/shard_map/ppermute | solution.py:215
  11.7 3.9 %collective-permute-start.6 = (bf16[4,32,128]{2,1,0:T(8,128)(2,1)S(1)}, bf16[4,32,128]{2,1,0:T(8,128)(2,1)S(1)}, u32[]{:S(2)}, u32[]{:S(2)}) collective-permute-start(bf16[4,32,128]{2,1,0:T(8,128)(2,1)S(1)} %maximum_bitcast_fusion.refs_3_), channel_id=1, source_target_pairs={{0,4},{4,0},{8,12},{12,8},{16,20},{20,16},{24,28},{28,24},{1,5},{5... | collective-permute-start | bytes 98312 | tf_op jit(solution)/shard_map/ppermute | solution.py:215
  13.2 2.4 %copy-start.4 = (bf16[1,8,64,128]{3,2,1,0:T(8,128)(2,1)S(1)}, bf16[1,8,64,128]{3,2,1,0:T(8,128)(2,1)}, u32[]{:S(2)}) copy-start(bf16[1,8,64,128]{3,2,1,0:T(8,128)(2,1)} %param.7) | copy-start | bytes 393220
  13.2 2.4 %copy-start.5 = (bf16[1,8,64,128]{3,2,1,0:T(8,128)(2,1)S(1)}, bf16[1,8,64,128]{3,2,1,0:T(8,128)(2,1)}, u32[]{:S(2)}) copy-start(bf16[1,8,64,128]{3,2,1,0:T(8,128)(2,1)} %param.10) | copy-start | bytes 393220
  16.2 3.5 %collective-permute-start.7 = (bf16[512,128]{1,0:T(8,128)(2,1)S(1)}, bf16[512,128]{1,0:T(8,128)(2,1)S(1)}, u32[]{:S(2)}, u32[]{:S(2)}) collective-permute-start(bf16[512,128]{1,0:T(8,128)(2,1)S(1)} %get-tuple-element.45.refs_3_), channel_id=1, source_target_pairs={{0,1},{1,0},{2,3},{3,2},{4,5},{5,4},{6,7},{7,6},{8,9},{9,8},{10,11... | collective-permute-start | bytes 393224 | tf_op jit(solution)/shard_map/ppermute | solution.py:215
  16.3 5.9 %collective-permute-start.3 = (bf16[4,32,512]{2,1,0:T(8,128)(2,1)S(1)}, bf16[4,32,512]{2,1,0:T(8,128)(2,1)S(1)}, u32[]{:S(2)}, u32[]{:S(2)}) collective-permute-start(bf16[4,32,512]{2,1,0:T(8,128)(2,1)S(1)} %pad_maximum_fusion.1.refs_1_), channel_id=1, source_target_pairs={{0,4},{4,0},{8,12},{12,8},{16,20},{20,16},{24,28},{28,24},{1,5},{5... | collective-permute-start | bytes 393224 | tf_op jit(solution)/shard_map/ppermute | solution.py:215
  17.9 5.8 %collective-permute-start.10 = (bf16[512,128]{1,0:T(8,128)(2,1)S(1)}, bf16[512,128]{1,0:T(8,128)(2,1)S(1)}, u32[]{:S(2)}, u32[]{:S(2)}) collective-permute-start(bf16[512,128]{1,0:T(8,128)(2,1)S(1)} %get-tuple-element.45.refs_3_), channel_id=1, source_target_pairs={{0,3},{1,2},{2,1},{3,0},{4,7},{5,6},{6,5},{7,4},{8,11},{9,10},{10,... | collective-permute-start | bytes 393224 | tf_op jit(solution)/shard_map/ppermute | solution.py:215
  19.2 7.7 %collective-permute-start.9 = (bf16[512,128]{1,0:T(8,128)(2,1)S(1)}, bf16[512,128]{1,0:T(8,128)(2,1)S(1)}, u32[]{:S(2)}, u32[]{:S(2)}) collective-permute-start(bf16[512,128]{1,0:T(8,128)(2,1)S(1)} %get-tuple-element.45.refs_3_), channel_id=1, source_target_pairs={{0,2},{1,3},{2,0},{3,1},{4,6},{5,7},{6,4},{7,5},{8,10},{9,11},{10,... | collective-permute-start | bytes 393224 | tf_op jit(solution)/shard_map/ppermute | solution.py:215
  19.7 7.1 %collective-permute-start.8 = (bf16[4,32,512]{2,1,0:T(8,128)(2,1)S(1)}, bf16[4,32,512]{2,1,0:T(8,128)(2,1)S(1)}, u32[]{:S(2)}, u32[]{:S(2)}) collective-permute-start(bf16[4,32,512]{2,1,0:T(8,128)(2,1)S(1)} %pad_maximum_fusion.1.refs_1_), channel_id=1, source_target_pairs={{4,8},{8,4},{12,16},{16,12},{20,24},{24,20},{5,9},{9,5},{13,17},{1... | collective-permute-start | bytes 393224 | tf_op jit(solution)/shard_map/ppermute | solution.py:235
  22.2 7.8 %collective-permute-start.12 = (bf16[256,128]{1,0:T(8,128)(2,1)S(1)}, bf16[256,128]{1,0:T(8,128)(2,1)S(1)}, u32[]{:S(2)}, u32[]{:S(2)}) collective-permute-start(bf16[256,128]{1,0:T(8,128)(2,1)S(1)} %get-tuple-element.52), channel_id=1, source_target_pairs={{0,1},{1,0},{2,3},{3,2},{4,5},{5,4},{6,7},{7,6},{8,9},{9,8},{10,11... | collective-permute-start | bytes 196616 | tf_op jit(solution)/shard_map/ppermute | solution.py:215
  22.2 7.8 %collective-permute-start.13 = (bf16[256,128]{1,0:T(8,128)(2,1)S(1)}, bf16[256,128]{1,0:T(8,128)(2,1)S(1)}, u32[]{:S(2)}, u32[]{:S(2)}) collective-permute-start(bf16[256,128]{1,0:T(8,128)(2,1)S(1)} %get-tuple-element.53), channel_id=1, source_target_pairs={{0,2},{1,3},{2,0},{3,1},{4,6},{5,7},{6,4},{7,5},{8,10},{9,11},{10,... | collective-permute-start | bytes 196616 | tf_op jit(solution)/shard_map/ppermute | solution.py:215
  23.7 6.3 %collective-permute-start.14 = (bf16[256,128]{1,0:T(8,128)(2,1)S(1)}, bf16[256,128]{1,0:T(8,128)(2,1)S(1)}, u32[]{:S(2)}, u32[]{:S(2)}) collective-permute-start(bf16[256,128]{1,0:T(8,128)(2,1)S(1)} %get-tuple-element.54), channel_id=1, source_target_pairs={{0,3},{1,2},{2,1},{3,0},{4,7},{5,6},{6,5},{7,4},{8,11},{9,10},{10,... | collective-permute-start | bytes 196616 | tf_op jit(solution)/shard_map/ppermute | solution.py:215
  28.3 19.8 %copy-start.1 = (bf16[3,3,3,128,128]{4,3,2,1,0:T(8,128)(2,1)S(1)}, bf16[3,3,3,128,128]{4,3,2,1,0:T(8,128)(2,1)}, u32[]{:S(2)}) copy-start(bf16[3,3,3,128,128]{4,3,2,1,0:T(8,128)(2,1)} %weight.1) | copy-start | bytes 2654212
  28.4 4.8 %collective-permute-start.11 = (bf16[432,128]{1,0:T(8,128)(2,1)S(1)}, bf16[432,128]{1,0:T(8,128)(2,1)S(1)}, u32[]{:S(2)}, u32[]{:S(2)}) collective-permute-start(bf16[432,128]{1,0:T(8,128)(2,1)S(1)} %get-tuple-element.50), channel_id=1, source_target_pairs={{0,4},{4,0},{8,12},{12,8},{16,20},{20,16},{24,28},{28,24},{1,5},{5... | collective-permute-start | bytes 331784 | tf_op jit(solution)/shard_map/ppermute | solution.py:215
  33.2 13.0 %collective-permute-start.15 = (bf16[688,128]{1,0:T(8,128)(2,1)S(1)}, bf16[688,128]{1,0:T(8,128)(2,1)S(1)}, u32[]{:S(2)}, u32[]{:S(2)}) collective-permute-start(bf16[688,128]{1,0:T(8,128)(2,1)S(1)} %pad_maximum_fusion), channel_id=1, source_target_pairs={{0,16},{4,20},{8,24},{12,28},{16,0},{20,4},{24,8},{28,12},{1,17},{... | collective-permute-start | bytes 528392 | tf_op jit(solution)/shard_map/ppermute | solution.py:215
  36.9 5.1 %collective-permute-start.17 = (bf16[10,64,128]{2,1,0:T(8,128)(2,1)S(1)}, bf16[10,64,128]{2,1,0:T(8,128)(2,1)S(1)}, u32[]{:S(2)}, u32[]{:S(2)}) collective-permute-start(bf16[10,64,128]{2,1,0:T(8,128)(2,1)S(1)} %get-tuple-element.55.own), channel_id=1, source_target_pairs={{4,8},{8,4},{12,16},{16,12},{20,24},{24,20},{5,9},{9,5},{13,17},{1... | collective-permute-start | bytes 491528 | tf_op jit(solution)/shard_map/ppermute | solution.py:235
  37.6 8.6 %collective-permute-start.16 = (bf16[10,64,128]{2,1,0:T(8,128)(2,1)S(1)}, bf16[10,64,128]{2,1,0:T(8,128)(2,1)S(1)}, u32[]{:S(2)}, u32[]{:S(2)}) collective-permute-start(bf16[10,64,128]{2,1,0:T(8,128)(2,1)S(1)} %get-tuple-element.55.own), channel_id=1, source_target_pairs={{0,4},{4,0},{8,12},{12,8},{16,20},{20,16},{24,28},{28,24},{1,5},{5... | collective-permute-start | bytes 491528 | tf_op jit(solution)/shard_map/ppermute | solution.py:215
  46.3 5.5 %collective-permute-start.18 = (bf16[688,128]{1,0:T(8,128)(2,1)S(1)}, bf16[688,128]{1,0:T(8,128)(2,1)S(1)}, u32[]{:S(2)}, u32[]{:S(2)}) collective-permute-start(bf16[688,128]{1,0:T(8,128)(2,1)S(1)} %add_convert_fusion), channel_id=1, source_target_pairs={{0,8},{4,12},{8,0},{12,4},{16,24},{20,28},{24,16},{28,20},{1,9},{5... | collective-permute-start | bytes 528392 | tf_op jit(solution)/shard_map/ppermute | solution.py:215
  52.0 8.7 %collective-permute-start.24 = (bf16[688,128]{1,0:T(8,128)(2,1)S(1)}, bf16[688,128]{1,0:T(8,128)(2,1)S(1)}, u32[]{:S(2)}, u32[]{:S(2)}) collective-permute-start(bf16[688,128]{1,0:T(8,128)(2,1)S(1)} %multiply_convert_fusion.refs_0_), channel_id=1, source_target_pairs={{0,6},{1,7},{2,4},{3,5},{4,2},{5,3},{6,0},{7,1},{8,14},{9,15},{10,... | collective-permute-start | bytes 528392 | tf_op jit(solution)/shard_map/ppermute | solution.py:225
  55.4 6.3 %collective-permute-start.22 = (bf16[688,128]{1,0:T(8,128)(2,1)S(1)}, bf16[688,128]{1,0:T(8,128)(2,1)S(1)}, u32[]{:S(2)}, u32[]{:S(2)}) collective-permute-start(bf16[688,128]{1,0:T(8,128)(2,1)S(1)} %multiply_convert_fusion.refs_0_), channel_id=1, source_target_pairs={{0,4},{4,0},{8,12},{12,8},{16,20},{20,16},{24,28},{28,24},{1,5},{5... | collective-permute-start | bytes 528392 | tf_op jit(solution)/shard_map/ppermute | solution.py:215
  55.4 6.6 %collective-permute-start.20 = (bf16[688,128]{1,0:T(8,128)(2,1)S(1)}, bf16[688,128]{1,0:T(8,128)(2,1)S(1)}, u32[]{:S(2)}, u32[]{:S(2)}) collective-permute-start(bf16[688,128]{1,0:T(8,128)(2,1)S(1)} %multiply_convert_fusion.refs_0_), channel_id=1, source_target_pairs={{0,2},{1,3},{2,0},{3,1},{4,6},{5,7},{6,4},{7,5},{8,10},{9,11},{10,... | collective-permute-start | bytes 528392 | tf_op jit(solution)/shard_map/ppermute | solution.py:215
  56.1 6.2 %collective-permute-start.19 = (bf16[688,128]{1,0:T(8,128)(2,1)S(1)}, bf16[688,128]{1,0:T(8,128)(2,1)S(1)}, u32[]{:S(2)}, u32[]{:S(2)}) collective-permute-start(bf16[688,128]{1,0:T(8,128)(2,1)S(1)} %multiply_convert_fusion.refs_0_), channel_id=1, source_target_pairs={{0,1},{1,0},{2,3},{3,2},{4,5},{5,4},{6,7},{7,6},{8,9},{9,8},{10,11... | collective-permute-start | bytes 528392 | tf_op jit(solution)/shard_map/ppermute | solution.py:215
  60.6 1.6 %collective-permute-start.25 = (bf16[688,128]{1,0:T(8,128)(2,1)S(1)}, bf16[688,128]{1,0:T(8,128)(2,1)S(1)}, u32[]{:S(2)}, u32[]{:S(2)}) collective-permute-start(bf16[688,128]{1,0:T(8,128)(2,1)S(1)} %collective-permute-done.24.refs_6_), channel_id=1, source_target_pairs={{0,1},{1,0},{2,3},{3,2},{4,5},{5,4},{6,7},{7,6},{8,9},{9,8},{10,11... | collective-permute-start | bytes 528392 | tf_op jit(solution)/shard_map/ppermute | solution.py:215
  61.8 1.4 %collective-permute-start.23 = (bf16[688,128]{1,0:T(8,128)(2,1)S(1)}, bf16[688,128]{1,0:T(8,128)(2,1)S(1)}, u32[]{:S(2)}, u32[]{:S(2)}) collective-permute-start(bf16[688,128]{1,0:T(8,128)(2,1)S(1)} %collective-permute-done.22.refs_4_), channel_id=1, source_target_pairs={{0,1},{1,0},{2,3},{3,2},{4,5},{5,4},{6,7},{7,6},{8,9},{9,8},{10,11... | collective-permute-start | bytes 528392 | tf_op jit(solution)/shard_map/ppermute | solution.py:215
  62.0 1.4 %collective-permute-start.21 = (bf16[688,128]{1,0:T(8,128)(2,1)S(1)}, bf16[688,128]{1,0:T(8,128)(2,1)S(1)}, u32[]{:S(2)}, u32[]{:S(2)}) collective-permute-start(bf16[688,128]{1,0:T(8,128)(2,1)S(1)} %collective-permute-done.20.refs_2_), channel_id=1, source_target_pairs={{0,1},{1,0},{2,3},{3,2},{4,5},{5,4},{6,7},{7,6},{8,9},{9,8},{10,11... | collective-permute-start | bytes 528392 | tf_op jit(solution)/shard_map/ppermute | solution.py:215

commit v18 on v17

--- a/solution.py
+++ b/solution.py
@@ -326,35 +326,48 @@
             pltpu.VMEM((2, 27 * half, channels), F32),
         ],
     )
-    near_even, near_odd = even_pairs(near), odd_pairs(near)
-    conv = (keep + swapped(send, "gz", 1).astype(F32)).astype(wire)
-    total = jnp.concatenate([conv, down.astype(wire)], axis=0)
-    total = lax.optimization_barrier(total)
+    near_odd, near_even = odd_pairs(near), even_pairs(near)
+    def rounded(value):
+        return lax.optimization_barrier(value.astype(wire))
+
+    def added(value, other):
+        return value.astype(F32) + other.astype(F32)
+
+    cell_total = devices * cells
+    down = rounded(down)
+    codes = []
     code = n_gz // 2
     while code > 1:
-        other = swapped(total, "gz", code)
-        if code == 4:
-            other, near_even, near_odd = lax.optimization_barrier((other, near_even, near_odd))
-        if code == 2:
-            input_grad = call(
-                input_kernel,
-                shape((rows, cols, channels), BF16),
-                near_even,
-                near,
-                near_odd,
-                conv_weight,
-            )
-            other, input_grad = lax.optimization_barrier((other, input_grad))
-        total = total.astype(F32) + other.astype(F32)
-        if code > 2:
-            total = lax.optimization_barrier(total.astype(wire))
+        codes.append(code)
         code //= 2
-    cell_total = devices * cells
-    row = lax.broadcasted_iota(jnp.int32, total.shape, 0)
-    scale = jnp.where(
-        row < 27 * half, 1 / math.sqrt(cell_total), 1 / math.sqrt(cell_total // 8)
-    )
-    total = (total * scale).astype(BF16)
+    send = swapped(send, "gz", 1)
+    for index, code in enumerate(codes):
+        down_other = swapped(down, "gz", code)
+        if index == 0:
+            send, down_other = lax.optimization_barrier((send, down_other))
+            conv = rounded(keep + send.astype(F32))
+        else:
+            conv_other = swapped(conv, "gz", codes[index - 1])
+            if index == 1:
+                tied = (conv_other, down_other, near_odd, near_even)
+                conv_other, down_other, near_odd, near_even = lax.optimization_barrier(tied)
+            conv = rounded(added(conv, conv_other))
+        down = added(down, down_other)
+        if index < len(codes) - 1:
+            down = rounded(down)
+    conv_other = swapped(conv, "gz", codes[-1])
+    input_grad = call(
+        input_kernel,
+        shape((rows, cols, channels), BF16),
+        near_even,
+        near,
+        near_odd,
+        conv_weight,
+    )
+    conv_other, input_grad = lax.optimization_barrier((conv_other, input_grad))
+    conv = added(conv, conv_other) * (1 / math.sqrt(cell_total))
+    down = down * (1 / math.sqrt(cell_total // 8))
+    total = jnp.concatenate([conv.astype(BF16), down.astype(BF16)], axis=0)
     if n_gy == 4:
         lines = [
             [total, swapped(total, "gy", 2)],

time: 64.9 us -> 62.8 us (0.968)
  starting transfers between devices: 32.7 us -> 30.9 us
    ppermute x1, starting transfers between devices: 3.47 us -> 0.35 us  [crossed(): return lax.ppermute(value, ('gz', 'gy'), pairs)]
    ppermute x1, waiting for transfers between devices: 4.56 us -> 2.96 us  [crossed(): return lax.ppermute(value, ('gz', 'gy'), pairs)]
    ppermute x23 -> x25, starting transfers between devices: 27.9 us -> 29.3 us  [swapped(): lax.ppermute(value, axis, [(i, i ^ code) for i in range(lax.axis_size(axi...]
    ppermute x23 -> x25, waiting for transfers between devices: 20 us -> 21.3 us  [swapped(): lax.ppermute(value, axis, [(i, i ^ code) for i in range(lax.axis_size(axi...]
  transfers between devices with their start and end apart: 26 -> 28, of which waited for: 12 -> 13; matrix products, arithmetic and copies ran while one was open for 0% -> 0% of each run, Pallas kernels for 5% -> 5%
where the time goes in v18:
time: 62.8 us; the launch traced here: 62.7 us
  starting transfers between devices  30.9 us (49%)
  waiting for transfers between devices  24.3 us (39%)
  Pallas kernels  5.34 us (9%)
  local copies, waits for them, and re-layouts  1 us (2%)
  between operations  0.83 us (1%)
    ppermute x25, starting transfers between devices, swapped(): lax.ppermute(value, axis, [(i, i ^ code) for i in range(lax.axis_size(axi...  29.3 us
    ppermute x25, waiting for transfers between devices, swapped(): lax.ppermute(value, axis, [(i, i ^ code) for i in range(lax.axis_size(axi...  21.3 us
    pallas_call x6, Pallas kernels, call(): pl.pallas_call(kernel, out_shape=out_shape, scratch_shapes=list(scratch),...  5.34 us
    ppermute x1, waiting for transfers between devices, crossed(): return lax.ppermute(value, ('gz', 'gy'), pairs)  2.96 us
    ppermute x2, starting transfers between devices, odd_pairs(): return lax.ppermute(value, 'gz', pairs)  1.32 us
  transfers between devices with their start and end apart: 28, of which 13 were waited for; matrix products, arithmetic and copies ran while one was open for 0% of the time, Pallas kernels for 5%

profile of v18, /device:TPU:0, one launch (start us, length us, event | category | flops | bytes accessed | tf_op | source)
XLA Modules:
  0.0 62.7 jit_solution(1814374615445247275)
XLA Ops:
  0.6 0.0 copy-start
  0.7 1.0 %copy-done.2 = bf16[4,4,32,32]{3,2,1,0:T(8,128)(2,1)S(1)} copy-done((bf16[4,4,32,32]{3,2,1,0:T(8,128)(2,1)S(1)}, bf16[4,4,32,32]{3,2,1,0:T(8,128)(2,1)}, u32[]{:S(2)}) %copy-start.2) | copy-done | bytes 32792
  1.6 0.1 shard_map.86
  1.7 4.1 %collective-permute-start.4 = (bf16[2,32,128]{2,1,0:T(8,128)(2,1)S(1)}, bf16[2,32,128]{2,1,0:T(8,128)(2,1)S(1)}, u32[]{:S(2)}, u32[]{:S(2)}) collective-permute-start(bf16[2,32,128]{2,1,0:T(8,128)(2,1)S(1)} %get-tuple-element.41), channel_id=1, source_target_pairs={{0,16},{4,20},{8,24},{12,28},{16,0},{20,4},{24,8},{28,12},{1,17},{... | collective-permute-start | bytes 49160 | tf_op jit(solution)/shard_map/ppermute | solution.py:215
  5.8 0.1 shard_map.85
  5.9 0.1 collective-permute-start
  6.0 1.6 %collective-permute-start.1 = (bf16[32,512]{1,0:T(8,128)(2,1)S(1)}, bf16[32,512]{1,0:T(8,128)(2,1)S(1)}, u32[]{:S(2)}, u32[]{:S(2)}) collective-permute-start(bf16[32,512]{1,0:T(8,128)(2,1)S(1)} %get-tuple-element.38), channel_id=1, source_target_pairs={{0,2},{1,3},{2,0},{3,1},{4,6},{5,7},{6,4},{7,5},{8,10},{9,11},{10,... | collective-permute-start | bytes 98312 | tf_op jit(solution)/shard_map/ppermute | solution.py:215
  7.6 0.3 collective-permute-start.2
  7.9 0.0 collective-permute-done.4
  7.9 1.6 %collective-permute-start.5 = (bf16[1,2,32,128]{3,2,1,0:T(8,128)(2,1)S(1)}, bf16[1,2,32,128]{3,2,1,0:T(8,128)(2,1)S(1)}, u32[]{:S(2)}, u32[]{:S(2)}) collective-permute-start(bf16[1,2,32,128]{3,2,1,0:T(8,128)(2,1)S(1)} %get-tuple-element.70), channel_id=1, source_target_pairs={{0,8},{4,12},{8,0},{12,4},{16,24},{20,28},{24,16},{28,20},{1,9},{5... | collective-permute-start | bytes 49160 | tf_op jit(solution)/shard_map/ppermute | solution.py:215
  9.5 2.1 %collective-permute-done.5 = bf16[1,2,32,128]{3,2,1,0:T(8,128)(2,1)S(1)} collective-permute-done((bf16[1,2,32,128]{3,2,1,0:T(8,128)(2,1)S(1)}, bf16[1,2,32,128]{3,2,1,0:T(8,128)(2,1)S(1)}, u32[]{:S(2)}, u32[]{:S(2)}) %collective-permute-start.5) | collective-permute-done | bytes 16416 | tf_op jit(solution)/shard_map/ppermute | solution.py:215
  11.7 1.5 %collective-permute-start.6 = (bf16[4,32,128]{2,1,0:T(8,128)(2,1)S(1)}, bf16[4,32,128]{2,1,0:T(8,128)(2,1)S(1)}, u32[]{:S(2)}, u32[]{:S(2)}) collective-permute-start(bf16[4,32,128]{2,1,0:T(8,128)(2,1)S(1)} %maximum_bitcast_fusion.refs_3_), channel_id=1, source_target_pairs={{0,4},{4,0},{8,12},{12,8},{16,20},{20,16},{24,28},{28,24},{1,5},{5... | collective-permute-start | bytes 98312 | tf_op jit(solution)/shard_map/ppermute | solution.py:215
  13.2 0.0 collective-permute-done
  13.2 0.0 collective-permute-done.1
  13.2 0.0 collective-permute-done.2
  13.2 0.0 copy-start.4
  13.2 0.0 copy-start.5
  13.3 2.3 %collective-permute-done.6.refs_4_ = bf16[4,32,128]{2,1,0:T(8,128)(2,1)S(1)} collective-permute-done((bf16[4,32,128]{2,1,0:T(8,128)(2,1)S(1)}, bf16[4,32,128]{2,1,0:T(8,128)(2,1)S(1)}, u32[]{:S(2)}, u32[]{:S(2)}) %collective-permute-start.6) | collective-permute-done | bytes 32800 | tf_op jit(solution)/shard_map/ppermute | solution.py:215
  15.6 0.6 shard_map.87
  16.2 0.1 collective-permute-start.7
  16.3 1.6 %collective-permute-start.3 = (bf16[4,32,512]{2,1,0:T(8,128)(2,1)S(1)}, bf16[4,32,512]{2,1,0:T(8,128)(2,1)S(1)}, u32[]{:S(2)}, u32[]{:S(2)}) collective-permute-start(bf16[4,32,512]{2,1,0:T(8,128)(2,1)S(1)} %pad_maximum_fusion.1.refs_1_), channel_id=1, source_target_pairs={{0,4},{4,0},{8,12},{12,8},{16,20},{20,16},{24,28},{28,24},{1,5},{5... | collective-permute-start | bytes 393224 | tf_op jit(solution)/shard_map/ppermute | solution.py:215
  17.9 1.3 %collective-permute-start.10 = (bf16[512,128]{1,0:T(8,128)(2,1)S(1)}, bf16[512,128]{1,0:T(8,128)(2,1)S(1)}, u32[]{:S(2)}, u32[]{:S(2)}) collective-permute-start(bf16[512,128]{1,0:T(8,128)(2,1)S(1)} %get-tuple-element.48.refs_3_), channel_id=1, source_target_pairs={{0,3},{1,2},{2,1},{3,0},{4,7},{5,6},{6,5},{7,4},{8,11},{9,10},{10,... | collective-permute-start | bytes 393224 | tf_op jit(solution)/shard_map/ppermute | solution.py:215
  19.2 0.5 collective-permute-start.9
  19.7 0.0 collective-permute-done.7.refs_4_
  19.7 0.7 %collective-permute-start.8 = (bf16[4,32,512]{2,1,0:T(8,128)(2,1)S(1)}, bf16[4,32,512]{2,1,0:T(8,128)(2,1)S(1)}, u32[]{:S(2)}, u32[]{:S(2)}) collective-permute-start(bf16[4,32,512]{2,1,0:T(8,128)(2,1)S(1)} %pad_maximum_fusion.1.refs_1_), channel_id=1, source_target_pairs={{4,8},{8,4},{12,16},{16,12},{20,24},{24,20},{5,9},{9,5},{13,17},{1... | collective-permute-start | bytes 393224 | tf_op jit(solution)/shard_map/ppermute | solution.py:235
  20.4 1.9 %collective-permute-done.3.refs_0_ = bf16[4,32,512]{2,1,0:T(8,128)(2,1)S(1)} collective-permute-done((bf16[4,32,512]{2,1,0:T(8,128)(2,1)S(1)}, bf16[4,32,512]{2,1,0:T(8,128)(2,1)S(1)}, u32[]{:S(2)}, u32[]{:S(2)}) %collective-permute-start.3) | collective-permute-done | bytes 131104 | tf_op jit(solution)/shard_map/ppermute | solution.py:215
  22.2 0.0 collective-permute-start.12
  22.2 1.5 %collective-permute-start.13 = (bf16[256,128]{1,0:T(8,128)(2,1)S(1)}, bf16[256,128]{1,0:T(8,128)(2,1)S(1)}, u32[]{:S(2)}, u32[]{:S(2)}) collective-permute-start(bf16[256,128]{1,0:T(8,128)(2,1)S(1)} %get-tuple-element.56), channel_id=1, source_target_pairs={{0,2},{1,3},{2,0},{3,1},{4,6},{5,7},{6,4},{7,5},{8,10},{9,11},{10,... | collective-permute-start | bytes 196616 | tf_op jit(solution)/shard_map/ppermute | solution.py:215
  23.7 0.0 collective-permute-done.10.refs_6_
  23.7 1.2 %collective-permute-start.14 = (bf16[256,128]{1,0:T(8,128)(2,1)S(1)}, bf16[256,128]{1,0:T(8,128)(2,1)S(1)}, u32[]{:S(2)}, u32[]{:S(2)}) collective-permute-start(bf16[256,128]{1,0:T(8,128)(2,1)S(1)} %get-tuple-element.57), channel_id=1, source_target_pairs={{0,3},{1,2},{2,1},{3,0},{4,7},{5,6},{6,5},{7,4},{8,11},{9,10},{10,... | collective-permute-start | bytes 196616 | tf_op jit(solution)/shard_map/ppermute | solution.py:215
  25.0 1.9 %collective-permute-done.9.refs_5_ = bf16[512,128]{1,0:T(8,128)(2,1)S(1)} collective-permute-done((bf16[512,128]{1,0:T(8,128)(2,1)S(1)}, bf16[512,128]{1,0:T(8,128)(2,1)S(1)}, u32[]{:S(2)}, u32[]{:S(2)}) %collective-permute-start.9) | collective-permute-done | bytes 131104 | tf_op jit(solution)/shard_map/ppermute | solution.py:215
  26.8 0.0 collective-permute-done.8.refs_2_
  26.8 1.5 %shard_map.88 = (f32[432,128]{1,0:T(8,128)S(1)}, bf16[432,128]{1,0:T(8,128)(2,1)S(1)}, bf16[10,64,128]{2,1,0:T(8,128)(2,1)S(1)}) custom-call(bf16[4,32,512]{2,1,0:T(8,128)(2,1)S(1)} %collective-permute-done.3.refs_0_, bf16[4,32,512]{2,1,0:T(8,128)(2,1)S(1)} %pad_maximum_fusion.1.refs_1_, bf16[4,32,512]{2,1,0:T(8,128)(2,1)S(1)} %collective-permute-done.8.refs_2_, ...), custom_call_target="tpu_custom_call" | custom-call | tf_op jit(solution)/shard_map/pallas_call | solution.py:16
  28.3 0.0 copy-start.1
  28.4 1.7 %collective-permute-start.11 = (bf16[432,128]{1,0:T(8,128)(2,1)S(1)}, bf16[432,128]{1,0:T(8,128)(2,1)S(1)}, u32[]{:S(2)}, u32[]{:S(2)}) collective-permute-start(bf16[432,128]{1,0:T(8,128)(2,1)S(1)} %get-tuple-element.53), channel_id=1, source_target_pairs={{0,4},{4,0},{8,12},{12,8},{16,20},{20,16},{24,28},{28,24},{1,5},{5... | collective-permute-start | bytes 331784 | tf_op jit(solution)/shard_map/ppermute | solution.py:215
  30.0 0.0 collective-permute-done.12
  30.1 0.0 collective-permute-done.13
  30.1 0.0 collective-permute-done.14
  30.1 2.6 %collective-permute-start.15 = (bf16[256,128]{1,0:T(8,128)(2,1)S(1)}, bf16[256,128]{1,0:T(8,128)(2,1)S(1)}, u32[]{:S(2)}, u32[]{:S(2)}) collective-permute-start(bf16[256,128]{1,0:T(8,128)(2,1)S(1)} %add_convert_fusion.3), channel_id=1, source_target_pairs={{0,16},{4,20},{8,24},{12,28},{16,0},{20,4},{24,8},{28,12},{1,17},{... | collective-permute-start | bytes 196616 | tf_op jit(solution)/shard_map/ppermute | solution.py:215
  32.7 1.5 %collective-permute-start.19 = (bf16[10,64,128]{2,1,0:T(8,128)(2,1)S(1)}, bf16[10,64,128]{2,1,0:T(8,128)(2,1)S(1)}, u32[]{:S(2)}, u32[]{:S(2)}) collective-permute-start(bf16[10,64,128]{2,1,0:T(8,128)(2,1)S(1)} %get-tuple-element.60.own), channel_id=1, source_target_pairs={{0,4},{4,0},{8,12},{12,8},{16,20},{20,16},{24,28},{28,24},{1,5},{5... | collective-permute-start | bytes 491528 | tf_op jit(solution)/shard_map/ppermute | solution.py:215
  34.2 0.7 %collective-permute-start.18 = (bf16[10,64,128]{2,1,0:T(8,128)(2,1)S(1)}, bf16[10,64,128]{2,1,0:T(8,128)(2,1)S(1)}, u32[]{:S(2)}, u32[]{:S(2)}) collective-permute-start(bf16[10,64,128]{2,1,0:T(8,128)(2,1)S(1)} %get-tuple-element.60.own), channel_id=1, source_target_pairs={{4,8},{8,4},{12,16},{16,12},{20,24},{24,20},{5,9},{9,5},{13,17},{1... | collective-permute-start | bytes 491528 | tf_op jit(solution)/shard_map/ppermute | solution.py:235
  34.9 0.5 collective-permute-done.15
  35.3 0.0 collective-permute-done.11
  35.4 3.4 %collective-permute-start.16 = (bf16[432,128]{1,0:T(8,128)(2,1)S(1)}, bf16[432,128]{1,0:T(8,128)(2,1)S(1)}, u32[]{:S(2)}, u32[]{:S(2)}) collective-permute-start(bf16[432,128]{1,0:T(8,128)(2,1)S(1)} %add_convert_fusion.1), channel_id=1, source_target_pairs={{0,16},{4,20},{8,24},{12,28},{16,0},{20,4},{24,8},{28,12},{1,17},{... | collective-permute-start | bytes 331784 | tf_op jit(solution)/shard_map/ppermute | solution.py:215
  38.8 1.1 %collective-permute-start.17 = (bf16[256,128]{1,0:T(8,128)(2,1)S(1)}, bf16[256,128]{1,0:T(8,128)(2,1)S(1)}, u32[]{:S(2)}, u32[]{:S(2)}) collective-permute-start(bf16[256,128]{1,0:T(8,128)(2,1)S(1)} %add_convert_fusion.2), channel_id=1, source_target_pairs={{0,8},{4,12},{8,0},{12,4},{16,24},{20,28},{24,16},{28,20},{1,9},{5... | collective-permute-start | bytes 196616 | tf_op jit(solution)/shard_map/ppermute | solution.py:215
  39.9 0.0 collective-permute-done.19.even
  39.9 0.0 collective-permute-done.18.odd
  39.9 3.7 %collective-permute-done.17 = bf16[256,128]{1,0:T(8,128)(2,1)S(1)} collective-permute-done((bf16[256,128]{1,0:T(8,128)(2,1)S(1)}, bf16[256,128]{1,0:T(8,128)(2,1)S(1)}, u32[]{:S(2)}, u32[]{:S(2)}) %collective-permute-start.17) | collective-permute-done | bytes 65568 | tf_op jit(solution)/shard_map/ppermute | solution.py:215
  43.6 2.9 %collective-permute-done.16 = bf16[432,128]{1,0:T(8,128)(2,1)S(1)} collective-permute-done((bf16[432,128]{1,0:T(8,128)(2,1)S(1)}, bf16[432,128]{1,0:T(8,128)(2,1)S(1)}, u32[]{:S(2)}, u32[]{:S(2)}) %collective-permute-start.16) | collective-permute-done | bytes 110624 | tf_op jit(solution)/shard_map/ppermute | solution.py:215
  46.5 0.1 collective-permute-start.20
  46.6 1.7 %shard_map.89 = bf16[8,64,128]{2,1,0:T(8,128)(2,1)} custom-call(bf16[10,64,128]{2,1,0:T(8,128)(2,1)S(1)} %collective-permute-done.19.even, bf16[10,64,128]{2,1,0:T(8,128)(2,1)S(1)} %get-tuple-element.60.own, bf16[10,64,128]{2,1,0:T(8,128)(2,1)S(1)} %collective-permute-done.18.odd, bf16[3,3,3,128,128]{4,3,2,1,0:T(8,128)(2,1)S(1)} %copy-done.1), custom_call_target="tpu_custom_call" | custom-call | tf_op jit(solution)/shard_map/pallas_call | solution.py:16
  48.4 2.9 %collective-permute-done.20 = bf16[432,128]{1,0:T(8,128)(2,1)S(1)} collective-permute-done((bf16[432,128]{1,0:T(8,128)(2,1)S(1)}, bf16[432,128]{1,0:T(8,128)(2,1)S(1)}, u32[]{:S(2)}, u32[]{:S(2)}) %collective-permute-start.20) | collective-permute-done | bytes 110624 | tf_op jit(solution)/shard_map/ppermute | solution.py:215
  51.4 0.3 collective-permute-start.26
  51.7 2.7 %collective-permute-start.24 = (bf16[688,128]{1,0:T(8,128)(2,1)S(1)}, bf16[688,128]{1,0:T(8,128)(2,1)S(1)}, u32[]{:S(2)}, u32[]{:S(2)}) collective-permute-start(bf16[688,128]{1,0:T(8,128)(2,1)S(1)} %pad_maximum_fusion.refs_0_), channel_id=1, source_target_pairs={{0,4},{4,0},{8,12},{12,8},{16,20},{20,16},{24,28},{28,24},{1,5},{5... | collective-permute-start | bytes 528392 | tf_op jit(solution)/shard_map/ppermute | solution.py:215
  54.4 0.5 collective-permute-start.22
  55.0 3.0 %collective-permute-done.26.refs_6_ = bf16[688,128]{1,0:T(8,128)(2,1)S(1)} collective-permute-done((bf16[688,128]{1,0:T(8,128)(2,1)S(1)}, bf16[688,128]{1,0:T(8,128)(2,1)S(1)}, u32[]{:S(2)}, u32[]{:S(2)}) %collective-permute-start.26) | collective-permute-done | bytes 176160 | tf_op jit(solution)/shard_map/ppermute | solution.py:225
  57.9 0.0 collective-permute-start.27
  57.9 1.8 %collective-permute-done.24.refs_4_ = bf16[688,128]{1,0:T(8,128)(2,1)S(1)} collective-permute-done((bf16[688,128]{1,0:T(8,128)(2,1)S(1)}, bf16[688,128]{1,0:T(8,128)(2,1)S(1)}, u32[]{:S(2)}, u32[]{:S(2)}) %collective-permute-start.24) | collective-permute-done | bytes 176160 | tf_op jit(solution)/shard_map/ppermute | solution.py:215
  59.7 0.0 collective-permute-start.25
  59.7 0.2 collective-permute-done.22.refs_2_
  59.9 0.3 collective-permute-start.23
  60.2 0.9 %collective-permute-done.25.refs_5_ = bf16[688,128]{1,0:T(8,128)(2,1)S(1)} collective-permute-done((bf16[688,128]{1,0:T(8,128)(2,1)S(1)}, bf16[688,128]{1,0:T(8,128)(2,1)S(1)}, u32[]{:S(2)}, u32[]{:S(2)}) %collective-permute-start.25) | collective-permute-done | bytes 176160 | tf_op jit(solution)/shard_map/ppermute | solution.py:215
  61.1 0.3 collective-permute-done.23.refs_3_
  61.4 1.3 %shard_map.90 = (bf16[27,4,2,16,128]{4,3,2,1,0:T(8,128)(2,1)}, bf16[2,4,128,256]{3,2,1,0:T(8,128)(2,1)}) custom-call(bf16[688,128]{1,0:T(8,128)(2,1)S(1)} %pad_maximum_fusion.refs_0_, bf16[688,128]{1,0:T(8,128)(2,1)S(1)} %collective-permute-done.21.refs_1_, bf16[688,128]{1,0:T(8,128)(2,1)S(1)} %collective-permute-done.22.refs_2_, ...), custom_call_target="tpu_custom_call" | custom-call | tf_op jit(solution)/shard_map/pallas_call | solution.py:16
  (21 shorter events, 0.3 us)
Async XLA Ops:
  0.6 8.9 %copy-start = (bf16[2,2,2,128,256]{4,3,2,1,0:T(8,128)(2,1)S(1)}, bf16[2,2,2,128,256]{4,3,2,1,0:T(8,128)(2,1)}, u32[]{:S(2)}) copy-start(bf16[2,2,2,128,256]{4,3,2,1,0:T(8,128)(2,1)} %param.9) | copy-start | bytes 1572868
  0.6 1.0 %copy-start.2 = (bf16[4,4,32,32]{3,2,1,0:T(8,128)(2,1)S(1)}, bf16[4,4,32,32]{3,2,1,0:T(8,128)(2,1)}, u32[]{:S(2)}) copy-start(bf16[4,4,32,32]{3,2,1,0:T(8,128)(2,1)} %param.11) | copy-start | bytes 98308
  1.6 4.2 %copy-start.3 = (bf16[1,8,64,128]{3,2,1,0:T(8,128)(2,1)S(1)}, bf16[1,8,64,128]{3,2,1,0:T(8,128)(2,1)}, u32[]{:S(2)}) copy-start(bf16[1,8,64,128]{3,2,1,0:T(8,128)(2,1)} %param.6) | copy-start | bytes 393220
  1.7 6.2 %collective-permute-start.4 = (bf16[2,32,128]{2,1,0:T(8,128)(2,1)S(1)}, bf16[2,32,128]{2,1,0:T(8,128)(2,1)S(1)}, u32[]{:S(2)}, u32[]{:S(2)}) collective-permute-start(bf16[2,32,128]{2,1,0:T(8,128)(2,1)S(1)} %get-tuple-element.41), channel_id=1, source_target_pairs={{0,16},{4,20},{8,24},{12,28},{16,0},{20,4},{24,8},{28,12},{1,17},{... | collective-permute-start | bytes 49160 | tf_op jit(solution)/shard_map/ppermute | solution.py:215
  5.9 7.3 %collective-permute-start = (bf16[32,512]{1,0:T(8,128)(2,1)S(1)}, bf16[32,512]{1,0:T(8,128)(2,1)S(1)}, u32[]{:S(2)}, u32[]{:S(2)}) collective-permute-start(bf16[32,512]{1,0:T(8,128)(2,1)S(1)} %get-tuple-element.37), channel_id=1, source_target_pairs={{0,1},{1,0},{2,3},{3,2},{4,5},{5,4},{6,7},{7,6},{8,9},{9,8},{10,11... | collective-permute-start | bytes 98312 | tf_op jit(solution)/shard_map/ppermute | solution.py:215
  6.0 7.2 %collective-permute-start.1 = (bf16[32,512]{1,0:T(8,128)(2,1)S(1)}, bf16[32,512]{1,0:T(8,128)(2,1)S(1)}, u32[]{:S(2)}, u32[]{:S(2)}) collective-permute-start(bf16[32,512]{1,0:T(8,128)(2,1)S(1)} %get-tuple-element.38), channel_id=1, source_target_pairs={{0,2},{1,3},{2,0},{3,1},{4,6},{5,7},{6,4},{7,5},{8,10},{9,11},{10,... | collective-permute-start | bytes 98312 | tf_op jit(solution)/shard_map/ppermute | solution.py:215
  7.6 5.7 %collective-permute-start.2 = (bf16[32,512]{1,0:T(8,128)(2,1)S(1)}, bf16[32,512]{1,0:T(8,128)(2,1)S(1)}, u32[]{:S(2)}, u32[]{:S(2)}) collective-permute-start(bf16[32,512]{1,0:T(8,128)(2,1)S(1)} %get-tuple-element.39), channel_id=1, source_target_pairs={{0,3},{1,2},{2,1},{3,0},{4,7},{5,6},{6,5},{7,4},{8,11},{9,10},{10,... | collective-permute-start | bytes 98312 | tf_op jit(solution)/shard_map/ppermute | solution.py:215
  7.9 3.8 %collective-permute-start.5 = (bf16[1,2,32,128]{3,2,1,0:T(8,128)(2,1)S(1)}, bf16[1,2,32,128]{3,2,1,0:T(8,128)(2,1)S(1)}, u32[]{:S(2)}, u32[]{:S(2)}) collective-permute-start(bf16[1,2,32,128]{3,2,1,0:T(8,128)(2,1)S(1)} %get-tuple-element.70), channel_id=1, source_target_pairs={{0,8},{4,12},{8,0},{12,4},{16,24},{20,28},{24,16},{28,20},{1,9},{5... | collective-permute-start | bytes 49160 | tf_op jit(solution)/shard_map/ppermute | solution.py:215
  11.7 3.9 %collective-permute-start.6 = (bf16[4,32,128]{2,1,0:T(8,128)(2,1)S(1)}, bf16[4,32,128]{2,1,0:T(8,128)(2,1)S(1)}, u32[]{:S(2)}, u32[]{:S(2)}) collective-permute-start(bf16[4,32,128]{2,1,0:T(8,128)(2,1)S(1)} %maximum_bitcast_fusion.refs_3_), channel_id=1, source_target_pairs={{0,4},{4,0},{8,12},{12,8},{16,20},{20,16},{24,28},{28,24},{1,5},{5... | collective-permute-start | bytes 98312 | tf_op jit(solution)/shard_map/ppermute | solution.py:215
  13.2 2.4 %copy-start.4 = (bf16[1,8,64,128]{3,2,1,0:T(8,128)(2,1)S(1)}, bf16[1,8,64,128]{3,2,1,0:T(8,128)(2,1)}, u32[]{:S(2)}) copy-start(bf16[1,8,64,128]{3,2,1,0:T(8,128)(2,1)} %param.7) | copy-start | bytes 393220
  13.2 2.4 %copy-start.5 = (bf16[1,8,64,128]{3,2,1,0:T(8,128)(2,1)S(1)}, bf16[1,8,64,128]{3,2,1,0:T(8,128)(2,1)}, u32[]{:S(2)}) copy-start(bf16[1,8,64,128]{3,2,1,0:T(8,128)(2,1)} %param.10) | copy-start | bytes 393220
  16.2 3.5 %collective-permute-start.7 = (bf16[512,128]{1,0:T(8,128)(2,1)S(1)}, bf16[512,128]{1,0:T(8,128)(2,1)S(1)}, u32[]{:S(2)}, u32[]{:S(2)}) collective-permute-start(bf16[512,128]{1,0:T(8,128)(2,1)S(1)} %get-tuple-element.48.refs_3_), channel_id=1, source_target_pairs={{0,1},{1,0},{2,3},{3,2},{4,5},{5,4},{6,7},{7,6},{8,9},{9,8},{10,11... | collective-permute-start | bytes 393224 | tf_op jit(solution)/shard_map/ppermute | solution.py:215
  16.3 5.9 %collective-permute-start.3 = (bf16[4,32,512]{2,1,0:T(8,128)(2,1)S(1)}, bf16[4,32,512]{2,1,0:T(8,128)(2,1)S(1)}, u32[]{:S(2)}, u32[]{:S(2)}) collective-permute-start(bf16[4,32,512]{2,1,0:T(8,128)(2,1)S(1)} %pad_maximum_fusion.1.refs_1_), channel_id=1, source_target_pairs={{0,4},{4,0},{8,12},{12,8},{16,20},{20,16},{24,28},{28,24},{1,5},{5... | collective-permute-start | bytes 393224 | tf_op jit(solution)/shard_map/ppermute | solution.py:215
  17.9 5.8 %collective-permute-start.10 = (bf16[512,128]{1,0:T(8,128)(2,1)S(1)}, bf16[512,128]{1,0:T(8,128)(2,1)S(1)}, u32[]{:S(2)}, u32[]{:S(2)}) collective-permute-start(bf16[512,128]{1,0:T(8,128)(2,1)S(1)} %get-tuple-element.48.refs_3_), channel_id=1, source_target_pairs={{0,3},{1,2},{2,1},{3,0},{4,7},{5,6},{6,5},{7,4},{8,11},{9,10},{10,... | collective-permute-start | bytes 393224 | tf_op jit(solution)/shard_map/ppermute | solution.py:215
  19.2 7.7 %collective-permute-start.9 = (bf16[512,128]{1,0:T(8,128)(2,1)S(1)}, bf16[512,128]{1,0:T(8,128)(2,1)S(1)}, u32[]{:S(2)}, u32[]{:S(2)}) collective-permute-start(bf16[512,128]{1,0:T(8,128)(2,1)S(1)} %get-tuple-element.48.refs_3_), channel_id=1, source_target_pairs={{0,2},{1,3},{2,0},{3,1},{4,6},{5,7},{6,4},{7,5},{8,10},{9,11},{10,... | collective-permute-start | bytes 393224 | tf_op jit(solution)/shard_map/ppermute | solution.py:215
  19.7 7.1 %collective-permute-start.8 = (bf16[4,32,512]{2,1,0:T(8,128)(2,1)S(1)}, bf16[4,32,512]{2,1,0:T(8,128)(2,1)S(1)}, u32[]{:S(2)}, u32[]{:S(2)}) collective-permute-start(bf16[4,32,512]{2,1,0:T(8,128)(2,1)S(1)} %pad_maximum_fusion.1.refs_1_), channel_id=1, source_target_pairs={{4,8},{8,4},{12,16},{16,12},{20,24},{24,20},{5,9},{9,5},{13,17},{1... | collective-permute-start | bytes 393224 | tf_op jit(solution)/shard_map/ppermute | solution.py:235
  22.2 7.8 %collective-permute-start.12 = (bf16[256,128]{1,0:T(8,128)(2,1)S(1)}, bf16[256,128]{1,0:T(8,128)(2,1)S(1)}, u32[]{:S(2)}, u32[]{:S(2)}) collective-permute-start(bf16[256,128]{1,0:T(8,128)(2,1)S(1)} %get-tuple-element.55), channel_id=1, source_target_pairs={{0,1},{1,0},{2,3},{3,2},{4,5},{5,4},{6,7},{7,6},{8,9},{9,8},{10,11... | collective-permute-start | bytes 196616 | tf_op jit(solution)/shard_map/ppermute | solution.py:215
  22.2 7.8 %collective-permute-start.13 = (bf16[256,128]{1,0:T(8,128)(2,1)S(1)}, bf16[256,128]{1,0:T(8,128)(2,1)S(1)}, u32[]{:S(2)}, u32[]{:S(2)}) collective-permute-start(bf16[256,128]{1,0:T(8,128)(2,1)S(1)} %get-tuple-element.56), channel_id=1, source_target_pairs={{0,2},{1,3},{2,0},{3,1},{4,6},{5,7},{6,4},{7,5},{8,10},{9,11},{10,... | collective-permute-start | bytes 196616 | tf_op jit(solution)/shard_map/ppermute | solution.py:215
  23.7 6.3 %collective-permute-start.14 = (bf16[256,128]{1,0:T(8,128)(2,1)S(1)}, bf16[256,128]{1,0:T(8,128)(2,1)S(1)}, u32[]{:S(2)}, u32[]{:S(2)}) collective-permute-start(bf16[256,128]{1,0:T(8,128)(2,1)S(1)} %get-tuple-element.57), channel_id=1, source_target_pairs={{0,3},{1,2},{2,1},{3,0},{4,7},{5,6},{6,5},{7,4},{8,11},{9,10},{10,... | collective-permute-start | bytes 196616 | tf_op jit(solution)/shard_map/ppermute | solution.py:215
  28.3 18.3 %copy-start.1 = (bf16[3,3,3,128,128]{4,3,2,1,0:T(8,128)(2,1)S(1)}, bf16[3,3,3,128,128]{4,3,2,1,0:T(8,128)(2,1)}, u32[]{:S(2)}) copy-start(bf16[3,3,3,128,128]{4,3,2,1,0:T(8,128)(2,1)} %weight.1) | copy-start | bytes 2654212
  28.4 7.0 %collective-permute-start.11 = (bf16[432,128]{1,0:T(8,128)(2,1)S(1)}, bf16[432,128]{1,0:T(8,128)(2,1)S(1)}, u32[]{:S(2)}, u32[]{:S(2)}) collective-permute-start(bf16[432,128]{1,0:T(8,128)(2,1)S(1)} %get-tuple-element.53), channel_id=1, source_target_pairs={{0,4},{4,0},{8,12},{12,8},{16,20},{20,16},{24,28},{28,24},{1,5},{5... | collective-permute-start | bytes 331784 | tf_op jit(solution)/shard_map/ppermute | solution.py:215
  30.1 5.2 %collective-permute-start.15 = (bf16[256,128]{1,0:T(8,128)(2,1)S(1)}, bf16[256,128]{1,0:T(8,128)(2,1)S(1)}, u32[]{:S(2)}, u32[]{:S(2)}) collective-permute-start(bf16[256,128]{1,0:T(8,128)(2,1)S(1)} %add_convert_fusion.3), channel_id=1, source_target_pairs={{0,16},{4,20},{8,24},{12,28},{16,0},{20,4},{24,8},{28,12},{1,17},{... | collective-permute-start | bytes 196616 | tf_op jit(solution)/shard_map/ppermute | solution.py:215
  32.7 7.2 %collective-permute-start.19 = (bf16[10,64,128]{2,1,0:T(8,128)(2,1)S(1)}, bf16[10,64,128]{2,1,0:T(8,128)(2,1)S(1)}, u32[]{:S(2)}, u32[]{:S(2)}) collective-permute-start(bf16[10,64,128]{2,1,0:T(8,128)(2,1)S(1)} %get-tuple-element.60.own), channel_id=1, source_target_pairs={{0,4},{4,0},{8,12},{12,8},{16,20},{20,16},{24,28},{28,24},{1,5},{5... | collective-permute-start | bytes 491528 | tf_op jit(solution)/shard_map/ppermute | solution.py:215
  34.2 5.7 %collective-permute-start.18 = (bf16[10,64,128]{2,1,0:T(8,128)(2,1)S(1)}, bf16[10,64,128]{2,1,0:T(8,128)(2,1)S(1)}, u32[]{:S(2)}, u32[]{:S(2)}) collective-permute-start(bf16[10,64,128]{2,1,0:T(8,128)(2,1)S(1)} %get-tuple-element.60.own), channel_id=1, source_target_pairs={{4,8},{8,4},{12,16},{16,12},{20,24},{24,20},{5,9},{9,5},{13,17},{1... | collective-permute-start | bytes 491528 | tf_op jit(solution)/shard_map/ppermute | solution.py:235
  35.4 11.1 %collective-permute-start.16 = (bf16[432,128]{1,0:T(8,128)(2,1)S(1)}, bf16[432,128]{1,0:T(8,128)(2,1)S(1)}, u32[]{:S(2)}, u32[]{:S(2)}) collective-permute-start(bf16[432,128]{1,0:T(8,128)(2,1)S(1)} %add_convert_fusion.1), channel_id=1, source_target_pairs={{0,16},{4,20},{8,24},{12,28},{16,0},{20,4},{24,8},{28,12},{1,17},{... | collective-permute-start | bytes 331784 | tf_op jit(solution)/shard_map/ppermute | solution.py:215
  38.8 4.8 %collective-permute-start.17 = (bf16[256,128]{1,0:T(8,128)(2,1)S(1)}, bf16[256,128]{1,0:T(8,128)(2,1)S(1)}, u32[]{:S(2)}, u32[]{:S(2)}) collective-permute-start(bf16[256,128]{1,0:T(8,128)(2,1)S(1)} %add_convert_fusion.2), channel_id=1, source_target_pairs={{0,8},{4,12},{8,0},{12,4},{16,24},{20,28},{24,16},{28,20},{1,9},{5... | collective-permute-start | bytes 196616 | tf_op jit(solution)/shard_map/ppermute | solution.py:215
  46.5 4.8 %collective-permute-start.20 = (bf16[432,128]{1,0:T(8,128)(2,1)S(1)}, bf16[432,128]{1,0:T(8,128)(2,1)S(1)}, u32[]{:S(2)}, u32[]{:S(2)}) collective-permute-start(bf16[432,128]{1,0:T(8,128)(2,1)S(1)} %add_convert_fusion), channel_id=1, source_target_pairs={{0,8},{4,12},{8,0},{12,4},{16,24},{20,28},{24,16},{28,20},{1,9},{5... | collective-permute-start | bytes 331784 | tf_op jit(solution)/shard_map/ppermute | solution.py:215
  51.4 6.5 %collective-permute-start.26 = (bf16[688,128]{1,0:T(8,128)(2,1)S(1)}, bf16[688,128]{1,0:T(8,128)(2,1)S(1)}, u32[]{:S(2)}, u32[]{:S(2)}) collective-permute-start(bf16[688,128]{1,0:T(8,128)(2,1)S(1)} %pad_maximum_fusion.refs_0_), channel_id=1, source_target_pairs={{0,6},{1,7},{2,4},{3,5},{4,2},{5,3},{6,0},{7,1},{8,14},{9,15},{10,... | collective-permute-start | bytes 528392 | tf_op jit(solution)/shard_map/ppermute | solution.py:225
  51.7 8.0 %collective-permute-start.24 = (bf16[688,128]{1,0:T(8,128)(2,1)S(1)}, bf16[688,128]{1,0:T(8,128)(2,1)S(1)}, u32[]{:S(2)}, u32[]{:S(2)}) collective-permute-start(bf16[688,128]{1,0:T(8,128)(2,1)S(1)} %pad_maximum_fusion.refs_0_), channel_id=1, source_target_pairs={{0,4},{4,0},{8,12},{12,8},{16,20},{20,16},{24,28},{28,24},{1,5},{5... | collective-permute-start | bytes 528392 | tf_op jit(solution)/shard_map/ppermute | solution.py:215
  54.4 5.5 %collective-permute-start.22 = (bf16[688,128]{1,0:T(8,128)(2,1)S(1)}, bf16[688,128]{1,0:T(8,128)(2,1)S(1)}, u32[]{:S(2)}, u32[]{:S(2)}) collective-permute-start(bf16[688,128]{1,0:T(8,128)(2,1)S(1)} %pad_maximum_fusion.refs_0_), channel_id=1, source_target_pairs={{0,2},{1,3},{2,0},{3,1},{4,6},{5,7},{6,4},{7,5},{8,10},{9,11},{10,... | collective-permute-start | bytes 528392 | tf_op jit(solution)/shard_map/ppermute | solution.py:215
  55.0 5.3 %collective-permute-start.21 = (bf16[688,128]{1,0:T(8,128)(2,1)S(1)}, bf16[688,128]{1,0:T(8,128)(2,1)S(1)}, u32[]{:S(2)}, u32[]{:S(2)}) collective-permute-start(bf16[688,128]{1,0:T(8,128)(2,1)S(1)} %pad_maximum_fusion.refs_0_), channel_id=1, source_target_pairs={{0,1},{1,0},{2,3},{3,2},{4,5},{5,4},{6,7},{7,6},{8,9},{9,8},{10,11... | collective-permute-start | bytes 528392 | tf_op jit(solution)/shard_map/ppermute | solution.py:215
  57.9 2.3 %collective-permute-start.27 = (bf16[688,128]{1,0:T(8,128)(2,1)S(1)}, bf16[688,128]{1,0:T(8,128)(2,1)S(1)}, u32[]{:S(2)}, u32[]{:S(2)}) collective-permute-start(bf16[688,128]{1,0:T(8,128)(2,1)S(1)} %collective-permute-done.26.refs_6_), channel_id=1, source_target_pairs={{0,1},{1,0},{2,3},{3,2},{4,5},{5,4},{6,7},{7,6},{8,9},{9,8},{10,11... | collective-permute-start | bytes 528392 | tf_op jit(solution)/shard_map/ppermute | solution.py:215
  59.7 1.4 %collective-permute-start.25 = (bf16[688,128]{1,0:T(8,128)(2,1)S(1)}, bf16[688,128]{1,0:T(8,128)(2,1)S(1)}, u32[]{:S(2)}, u32[]{:S(2)}) collective-permute-start(bf16[688,128]{1,0:T(8,128)(2,1)S(1)} %collective-permute-done.24.refs_4_), channel_id=1, source_target_pairs={{0,1},{1,0},{2,3},{3,2},{4,5},{5,4},{6,7},{7,6},{8,9},{9,8},{10,11... | collective-permute-start | bytes 528392 | tf_op jit(solution)/shard_map/ppermute | solution.py:215
  59.9 1.5 %collective-permute-start.23 = (bf16[688,128]{1,0:T(8,128)(2,1)S(1)}, bf16[688,128]{1,0:T(8,128)(2,1)S(1)}, u32[]{:S(2)}, u32[]{:S(2)}) collective-permute-start(bf16[688,128]{1,0:T(8,128)(2,1)S(1)} %collective-permute-done.22.refs_2_), channel_id=1, source_target_pairs={{0,1},{1,0},{2,3},{3,2},{4,5},{5,4},{6,7},{7,6},{8,9},{9,8},{10,11... | collective-permute-start | bytes 528392 | tf_op jit(solution)/shard_map/ppermute | solution.py:215

commit v19 on v18

--- a/solution.py
+++ b/solution.py
@@ -364,25 +364,25 @@
         near_odd,
         conv_weight,
     )
-    conv_other, input_grad = lax.optimization_barrier((conv_other, input_grad))
-    conv = added(conv, conv_other) * (1 / math.sqrt(cell_total))
-    down = down * (1 / math.sqrt(cell_total // 8))
-    total = jnp.concatenate([conv.astype(BF16), down.astype(BF16)], axis=0)
-    if n_gy == 4:
-        lines = [
-            [total, swapped(total, "gy", 2)],
-            [swapped(total, "gz", 1), crossed(total, 1, 2)],
+    down = (down * (1 / math.sqrt(cell_total // 8))).astype(BF16)
+
+    def spread(value):
+        return [
+            value,
+            swapped(value, "gy", 2),
+            swapped(value, "gz", 1),
+            crossed(value, 1, 2),
         ]
-        blocks = []
-        for near_block, far_block in lines:
-            blocks += [near_block, swapped(near_block, "gy", 1)]
-            blocks += [far_block, swapped(far_block, "gy", 1)]
-    else:
-        blocks = [
-            swapped(block, "gy", code) if code else block
-            for block in (total, swapped(total, "gz", 1))
-            for code in range(n_gy)
-        ]
+
+    downs = spread(down)
+    conv_other, *downs = lax.optimization_barrier((conv_other, *downs))
+    conv = (added(conv, conv_other) * (1 / math.sqrt(cell_total))).astype(BF16)
+    convs = spread(conv)
+    convs[3], input_grad = lax.optimization_barrier((convs[3], input_grad))
+    blocks = []
+    for pieces in zip(convs, downs):
+        block = jnp.concatenate(pieces, axis=0)
+        blocks += [block, swapped(block, "gy", 1)]
     conv_grad, down_grad = call(
         lambda *refs: place_kernel(n_gy, *refs),
         (

time: 62.8 us -> 65.6 us (1.045)
  starting transfers between devices: 30.9 us -> 34.9 us
  waiting for transfers between devices: 24.3 us -> 22.9 us
    ppermute x1 -> x2, starting transfers between devices: 0.35 us -> 4.42 us  [crossed(): return lax.ppermute(value, ('gz', 'gy'), pairs)]
    ppermute x25 -> x27, waiting for transfers between devices: 21.3 us -> 19.1 us  [swapped(): lax.ppermute(value, axis, [(i, i ^ code) for i in range(lax.axis_size(axi...]
    ppermute x1 -> x2, waiting for transfers between devices: 2.96 us -> 3.81 us  [crossed(): return lax.ppermute(value, ('gz', 'gy'), pairs)]
    ppermute x25 -> x27, starting transfers between devices: 29.3 us -> 29.2 us  [swapped(): lax.ppermute(value, axis, [(i, i ^ code) for i in range(lax.axis_size(axi...]
  transfers between devices with their start and end apart: 28 -> 31, of which waited for: 13 -> 13; matrix products, arithmetic and copies ran while one was open for 0% -> 0% of each run, Pallas kernels for 5% -> 5%
where the time goes in v19:
time: 65.6 us; the launch traced here: 65.4 us
  starting transfers between devices  34.9 us (53%)
  waiting for transfers between devices  22.9 us (35%)
  Pallas kernels  5.34 us (8%)
  local copies, waits for them, and re-layouts  1.07 us (2%)
  between operations  0.88 us (1%)
    ppermute x27, starting transfers between devices, swapped(): lax.ppermute(value, axis, [(i, i ^ code) for i in range(lax.axis_size(axi...  29.2 us
    ppermute x27, waiting for transfers between devices, swapped(): lax.ppermute(value, axis, [(i, i ^ code) for i in range(lax.axis_size(axi...  19.1 us
    pallas_call x6, Pallas kernels, call(): pl.pallas_call(kernel, out_shape=out_shape, scratch_shapes=list(scratch),...  5.34 us
    ppermute x2, starting transfers between devices, crossed(): return lax.ppermute(value, ('gz', 'gy'), pairs)  4.42 us
    ppermute x2, waiting for transfers between devices, crossed(): return lax.ppermute(value, ('gz', 'gy'), pairs)  3.81 us
    ppermute x2, starting transfers between devices, odd_pairs(): return lax.ppermute(value, 'gz', pairs)  1.32 us
  transfers between devices with their start and end apart: 31, of which 13 were waited for; matrix products, arithmetic and copies ran while one was open for 0% of the time, Pallas kernels for 5%

profile of v19, /device:TPU:0, one launch (start us, length us, event | category | flops | bytes accessed | tf_op | source)
XLA Modules:
  0.0 65.4 jit_solution(8992255552162618927)
XLA Ops:
  0.6 0.0 copy-start
  0.7 1.0 %copy-done.2 = bf16[4,4,32,32]{3,2,1,0:T(8,128)(2,1)S(1)} copy-done((bf16[4,4,32,32]{3,2,1,0:T(8,128)(2,1)S(1)}, bf16[4,4,32,32]{3,2,1,0:T(8,128)(2,1)}, u32[]{:S(2)}) %copy-start.2) | copy-done | bytes 32792
  1.6 0.1 shard_map.86
  1.7 4.1 %collective-permute-start.4 = (bf16[2,32,128]{2,1,0:T(8,128)(2,1)S(1)}, bf16[2,32,128]{2,1,0:T(8,128)(2,1)S(1)}, u32[]{:S(2)}, u32[]{:S(2)}) collective-permute-start(bf16[2,32,128]{2,1,0:T(8,128)(2,1)S(1)} %get-tuple-element.46), channel_id=1, source_target_pairs={{0,16},{4,20},{8,24},{12,28},{16,0},{20,4},{24,8},{28,12},{1,17},{... | collective-permute-start | bytes 49160 | tf_op jit(solution)/shard_map/ppermute | solution.py:215
  5.8 0.1 shard_map.85
  5.9 0.1 collective-permute-start
  6.0 1.6 %collective-permute-start.1 = (bf16[32,512]{1,0:T(8,128)(2,1)S(1)}, bf16[32,512]{1,0:T(8,128)(2,1)S(1)}, u32[]{:S(2)}, u32[]{:S(2)}) collective-permute-start(bf16[32,512]{1,0:T(8,128)(2,1)S(1)} %get-tuple-element.43), channel_id=1, source_target_pairs={{0,2},{1,3},{2,0},{3,1},{4,6},{5,7},{6,4},{7,5},{8,10},{9,11},{10,... | collective-permute-start | bytes 98312 | tf_op jit(solution)/shard_map/ppermute | solution.py:215
  7.6 0.3 collective-permute-start.2
  7.9 0.0 collective-permute-done.4
  7.9 1.6 %collective-permute-start.5 = (bf16[1,2,32,128]{3,2,1,0:T(8,128)(2,1)S(1)}, bf16[1,2,32,128]{3,2,1,0:T(8,128)(2,1)S(1)}, u32[]{:S(2)}, u32[]{:S(2)}) collective-permute-start(bf16[1,2,32,128]{3,2,1,0:T(8,128)(2,1)S(1)} %get-tuple-element.80), channel_id=1, source_target_pairs={{0,8},{4,12},{8,0},{12,4},{16,24},{20,28},{24,16},{28,20},{1,9},{5... | collective-permute-start | bytes 49160 | tf_op jit(solution)/shard_map/ppermute | solution.py:215
  9.5 2.1 %collective-permute-done.5 = bf16[1,2,32,128]{3,2,1,0:T(8,128)(2,1)S(1)} collective-permute-done((bf16[1,2,32,128]{3,2,1,0:T(8,128)(2,1)S(1)}, bf16[1,2,32,128]{3,2,1,0:T(8,128)(2,1)S(1)}, u32[]{:S(2)}, u32[]{:S(2)}) %collective-permute-start.5) | collective-permute-done | bytes 16416 | tf_op jit(solution)/shard_map/ppermute | solution.py:215
  11.7 1.5 %collective-permute-start.6 = (bf16[4,32,128]{2,1,0:T(8,128)(2,1)S(1)}, bf16[4,32,128]{2,1,0:T(8,128)(2,1)S(1)}, u32[]{:S(2)}, u32[]{:S(2)}) collective-permute-start(bf16[4,32,128]{2,1,0:T(8,128)(2,1)S(1)} %maximum_bitcast_fusion.refs_3_), channel_id=1, source_target_pairs={{0,4},{4,0},{8,12},{12,8},{16,20},{20,16},{24,28},{28,24},{1,5},{5... | collective-permute-start | bytes 98312 | tf_op jit(solution)/shard_map/ppermute | solution.py:215
  13.2 0.0 collective-permute-done
  13.2 0.0 collective-permute-done.1
  13.2 0.0 copy-start.4
  13.2 0.0 copy-start.5
  13.3 2.3 %collective-permute-done.6.refs_4_ = bf16[4,32,128]{2,1,0:T(8,128)(2,1)S(1)} collective-permute-done((bf16[4,32,128]{2,1,0:T(8,128)(2,1)S(1)}, bf16[4,32,128]{2,1,0:T(8,128)(2,1)S(1)}, u32[]{:S(2)}, u32[]{:S(2)}) %collective-permute-start.6) | collective-permute-done | bytes 32800 | tf_op jit(solution)/shard_map/ppermute | solution.py:215
  15.6 0.6 shard_map.87
  16.2 0.1 collective-permute-start.7
  16.3 1.6 %collective-permute-start.3 = (bf16[4,32,512]{2,1,0:T(8,128)(2,1)S(1)}, bf16[4,32,512]{2,1,0:T(8,128)(2,1)S(1)}, u32[]{:S(2)}, u32[]{:S(2)}) collective-permute-start(bf16[4,32,512]{2,1,0:T(8,128)(2,1)S(1)} %pad_maximum_fusion.1.refs_1_), channel_id=1, source_target_pairs={{0,4},{4,0},{8,12},{12,8},{16,20},{20,16},{24,28},{28,24},{1,5},{5... | collective-permute-start | bytes 393224 | tf_op jit(solution)/shard_map/ppermute | solution.py:215
  17.9 1.3 %collective-permute-start.10 = (bf16[512,128]{1,0:T(8,128)(2,1)S(1)}, bf16[512,128]{1,0:T(8,128)(2,1)S(1)}, u32[]{:S(2)}, u32[]{:S(2)}) collective-permute-start(bf16[512,128]{1,0:T(8,128)(2,1)S(1)} %get-tuple-element.53.refs_3_), channel_id=1, source_target_pairs={{0,3},{1,2},{2,1},{3,0},{4,7},{5,6},{6,5},{7,4},{8,11},{9,10},{10,... | collective-permute-start | bytes 393224 | tf_op jit(solution)/shard_map/ppermute | solution.py:215
  19.2 0.5 collective-permute-start.9
  19.7 0.7 %collective-permute-start.8 = (bf16[4,32,512]{2,1,0:T(8,128)(2,1)S(1)}, bf16[4,32,512]{2,1,0:T(8,128)(2,1)S(1)}, u32[]{:S(2)}, u32[]{:S(2)}) collective-permute-start(bf16[4,32,512]{2,1,0:T(8,128)(2,1)S(1)} %pad_maximum_fusion.1.refs_1_), channel_id=1, source_target_pairs={{4,8},{8,4},{12,16},{16,12},{20,24},{24,20},{5,9},{9,5},{13,17},{1... | collective-permute-start | bytes 393224 | tf_op jit(solution)/shard_map/ppermute | solution.py:235
  20.4 1.9 %collective-permute-done.3.refs_0_ = bf16[4,32,512]{2,1,0:T(8,128)(2,1)S(1)} collective-permute-done((bf16[4,32,512]{2,1,0:T(8,128)(2,1)S(1)}, bf16[4,32,512]{2,1,0:T(8,128)(2,1)S(1)}, u32[]{:S(2)}, u32[]{:S(2)}) %collective-permute-start.3) | collective-permute-done | bytes 131104 | tf_op jit(solution)/shard_map/ppermute | solution.py:215
  22.2 1.5 %collective-permute-start.13 = (bf16[256,128]{1,0:T(8,128)(2,1)S(1)}, bf16[256,128]{1,0:T(8,128)(2,1)S(1)}, u32[]{:S(2)}, u32[]{:S(2)}) collective-permute-start(bf16[256,128]{1,0:T(8,128)(2,1)S(1)} %get-tuple-element.61), channel_id=1, source_target_pairs={{0,2},{1,3},{2,0},{3,1},{4,6},{5,7},{6,4},{7,5},{8,10},{9,11},{10,... | collective-permute-start | bytes 196616 | tf_op jit(solution)/shard_map/ppermute | solution.py:215
  23.7 1.2 %collective-permute-start.14 = (bf16[256,128]{1,0:T(8,128)(2,1)S(1)}, bf16[256,128]{1,0:T(8,128)(2,1)S(1)}, u32[]{:S(2)}, u32[]{:S(2)}) collective-permute-start(bf16[256,128]{1,0:T(8,128)(2,1)S(1)} %get-tuple-element.62), channel_id=1, source_target_pairs={{0,3},{1,2},{2,1},{3,0},{4,7},{5,6},{6,5},{7,4},{8,11},{9,10},{10,... | collective-permute-start | bytes 196616 | tf_op jit(solution)/shard_map/ppermute | solution.py:215
  25.0 1.9 %collective-permute-done.9.refs_5_ = bf16[512,128]{1,0:T(8,128)(2,1)S(1)} collective-permute-done((bf16[512,128]{1,0:T(8,128)(2,1)S(1)}, bf16[512,128]{1,0:T(8,128)(2,1)S(1)}, u32[]{:S(2)}, u32[]{:S(2)}) %collective-permute-start.9) | collective-permute-done | bytes 131104 | tf_op jit(solution)/shard_map/ppermute | solution.py:215
  26.8 0.0 collective-permute-done.8.refs_2_
  26.8 1.5 %shard_map.88 = (f32[432,128]{1,0:T(8,128)S(1)}, bf16[432,128]{1,0:T(8,128)(2,1)S(1)}, bf16[10,64,128]{2,1,0:T(8,128)(2,1)S(1)}) custom-call(bf16[4,32,512]{2,1,0:T(8,128)(2,1)S(1)} %collective-permute-done.3.refs_0_, bf16[4,32,512]{2,1,0:T(8,128)(2,1)S(1)} %pad_maximum_fusion.1.refs_1_, bf16[4,32,512]{2,1,0:T(8,128)(2,1)S(1)} %collective-permute-done.8.refs_2_, ...), custom_call_target="tpu_custom_call" | custom-call | tf_op jit(solution)/shard_map/pallas_call | solution.py:16
  28.3 0.0 copy-start.1
  28.4 1.7 %collective-permute-start.11 = (bf16[432,128]{1,0:T(8,128)(2,1)S(1)}, bf16[432,128]{1,0:T(8,128)(2,1)S(1)}, u32[]{:S(2)}, u32[]{:S(2)}) collective-permute-start(bf16[432,128]{1,0:T(8,128)(2,1)S(1)} %get-tuple-element.58), channel_id=1, source_target_pairs={{0,4},{4,0},{8,12},{12,8},{16,20},{20,16},{24,28},{28,24},{1,5},{5... | collective-permute-start | bytes 331784 | tf_op jit(solution)/shard_map/ppermute | solution.py:215
  30.0 0.0 collective-permute-done.12
  30.1 0.0 collective-permute-done.13
  30.1 0.0 collective-permute-done.14
  30.1 2.6 %collective-permute-start.15 = (bf16[256,128]{1,0:T(8,128)(2,1)S(1)}, bf16[256,128]{1,0:T(8,128)(2,1)S(1)}, u32[]{:S(2)}, u32[]{:S(2)}) collective-permute-start(bf16[256,128]{1,0:T(8,128)(2,1)S(1)} %add_convert_fusion.3), channel_id=1, source_target_pairs={{0,16},{4,20},{8,24},{12,28},{16,0},{20,4},{24,8},{28,12},{1,17},{... | collective-permute-start | bytes 196616 | tf_op jit(solution)/shard_map/ppermute | solution.py:215
  32.7 1.5 %collective-permute-start.19 = (bf16[10,64,128]{2,1,0:T(8,128)(2,1)S(1)}, bf16[10,64,128]{2,1,0:T(8,128)(2,1)S(1)}, u32[]{:S(2)}, u32[]{:S(2)}) collective-permute-start(bf16[10,64,128]{2,1,0:T(8,128)(2,1)S(1)} %get-tuple-element.65.own), channel_id=1, source_target_pairs={{0,4},{4,0},{8,12},{12,8},{16,20},{20,16},{24,28},{28,24},{1,5},{5... | collective-permute-start | bytes 491528 | tf_op jit(solution)/shard_map/ppermute | solution.py:215
  34.2 0.7 %collective-permute-start.18 = (bf16[10,64,128]{2,1,0:T(8,128)(2,1)S(1)}, bf16[10,64,128]{2,1,0:T(8,128)(2,1)S(1)}, u32[]{:S(2)}, u32[]{:S(2)}) collective-permute-start(bf16[10,64,128]{2,1,0:T(8,128)(2,1)S(1)} %get-tuple-element.65.own), channel_id=1, source_target_pairs={{4,8},{8,4},{12,16},{16,12},{20,24},{24,20},{5,9},{9,5},{13,17},{1... | collective-permute-start | bytes 491528 | tf_op jit(solution)/shard_map/ppermute | solution.py:235
  34.9 0.5 collective-permute-done.15
  35.3 0.0 collective-permute-done.11
  35.4 3.4 %collective-permute-start.16 = (bf16[432,128]{1,0:T(8,128)(2,1)S(1)}, bf16[432,128]{1,0:T(8,128)(2,1)S(1)}, u32[]{:S(2)}, u32[]{:S(2)}) collective-permute-start(bf16[432,128]{1,0:T(8,128)(2,1)S(1)} %add_convert_fusion.1), channel_id=1, source_target_pairs={{0,16},{4,20},{8,24},{12,28},{16,0},{20,4},{24,8},{28,12},{1,17},{... | collective-permute-start | bytes 331784 | tf_op jit(solution)/shard_map/ppermute | solution.py:215
  38.8 1.1 %collective-permute-start.17 = (bf16[256,128]{1,0:T(8,128)(2,1)S(1)}, bf16[256,128]{1,0:T(8,128)(2,1)S(1)}, u32[]{:S(2)}, u32[]{:S(2)}) collective-permute-start(bf16[256,128]{1,0:T(8,128)(2,1)S(1)} %add_convert_fusion.2), channel_id=1, source_target_pairs={{0,8},{4,12},{8,0},{12,4},{16,24},{20,28},{24,16},{28,20},{1,9},{5... | collective-permute-start | bytes 196616 | tf_op jit(solution)/shard_map/ppermute | solution.py:215
  39.9 3.7 %collective-permute-done.17 = bf16[256,128]{1,0:T(8,128)(2,1)S(1)} collective-permute-done((bf16[256,128]{1,0:T(8,128)(2,1)S(1)}, bf16[256,128]{1,0:T(8,128)(2,1)S(1)}, u32[]{:S(2)}, u32[]{:S(2)}) %collective-permute-start.17) | collective-permute-done | bytes 65568 | tf_op jit(solution)/shard_map/ppermute | solution.py:215
  43.6 2.9 %collective-permute-done.16 = bf16[432,128]{1,0:T(8,128)(2,1)S(1)} collective-permute-done((bf16[432,128]{1,0:T(8,128)(2,1)S(1)}, bf16[432,128]{1,0:T(8,128)(2,1)S(1)}, u32[]{:S(2)}, u32[]{:S(2)}) %collective-permute-start.16) | collective-permute-done | bytes 110624 | tf_op jit(solution)/shard_map/ppermute | solution.py:215
  46.5 0.1 collective-permute-start.20
  46.6 2.0 %collective-permute-start.23 = (bf16[256,128]{1,0:T(8,128)(2,1)S(1)}, bf16[256,128]{1,0:T(8,128)(2,1)S(1)}, u32[]{:S(2)}, u32[]{:S(2)}) collective-permute-start(bf16[256,128]{1,0:T(8,128)(2,1)S(1)} %multiply_convert_fusion.1), channel_id=1, source_target_pairs={{0,6},{1,7},{2,4},{3,5},{4,2},{5,3},{6,0},{7,1},{8,14},{9,15},{10,... | collective-permute-start | bytes 196616 | tf_op jit(solution)/shard_map/ppermute | solution.py:225
  48.6 1.0 %collective-permute-start.22 = (bf16[256,128]{1,0:T(8,128)(2,1)S(1)}, bf16[256,128]{1,0:T(8,128)(2,1)S(1)}, u32[]{:S(2)}, u32[]{:S(2)}) collective-permute-start(bf16[256,128]{1,0:T(8,128)(2,1)S(1)} %multiply_convert_fusion.1), channel_id=1, source_target_pairs={{0,4},{4,0},{8,12},{12,8},{16,20},{20,16},{24,28},{28,24},{1,5},{5... | collective-permute-start | bytes 196616 | tf_op jit(solution)/shard_map/ppermute | solution.py:215
  49.7 0.5 collective-permute-start.21
  50.2 1.7 %shard_map.89 = bf16[8,64,128]{2,1,0:T(8,128)(2,1)} custom-call(bf16[10,64,128]{2,1,0:T(8,128)(2,1)S(1)} %collective-permute-done.19.even, bf16[10,64,128]{2,1,0:T(8,128)(2,1)S(1)} %get-tuple-element.65.own, bf16[10,64,128]{2,1,0:T(8,128)(2,1)S(1)} %collective-permute-done.18.odd, bf16[3,3,3,128,128]{4,3,2,1,0:T(8,128)(2,1)S(1)} %copy-done.1), custom_call_target="tpu_custom_call" | custom-call | tf_op jit(solution)/shard_map/pallas_call | solution.py:16
  51.9 0.9 %collective-permute-done.22 = bf16[256,128]{1,0:T(8,128)(2,1)S(1)} collective-permute-done((bf16[256,128]{1,0:T(8,128)(2,1)S(1)}, bf16[256,128]{1,0:T(8,128)(2,1)S(1)}, u32[]{:S(2)}, u32[]{:S(2)}) %collective-permute-start.22) | collective-permute-done | bytes 65568 | tf_op jit(solution)/shard_map/ppermute | solution.py:215
  52.9 1.5 %collective-permute-done.21 = bf16[256,128]{1,0:T(8,128)(2,1)S(1)} collective-permute-done((bf16[256,128]{1,0:T(8,128)(2,1)S(1)}, bf16[256,128]{1,0:T(8,128)(2,1)S(1)}, u32[]{:S(2)}, u32[]{:S(2)}) %collective-permute-start.21) | collective-permute-done | bytes 65568 | tf_op jit(solution)/shard_map/ppermute | solution.py:215
  54.4 0.6 collective-permute-start.28
  55.0 0.5 collective-permute-start.26
  55.6 2.4 %collective-permute-start.24 = (bf16[432,128]{1,0:T(8,128)(2,1)S(1)}, bf16[432,128]{1,0:T(8,128)(2,1)S(1)}, u32[]{:S(2)}, u32[]{:S(2)}) collective-permute-start(bf16[432,128]{1,0:T(8,128)(2,1)S(1)} %multiply_convert_fusion), channel_id=1, source_target_pairs={{0,6},{1,7},{2,4},{3,5},{4,2},{5,3},{6,0},{7,1},{8,14},{9,15},{10,... | collective-permute-start | bytes 331784 | tf_op jit(solution)/shard_map/ppermute | solution.py:225
  58.0 0.1 collective-permute-start.25
  58.1 3.8 %collective-permute-done.24 = bf16[432,128]{1,0:T(8,128)(2,1)S(1)} collective-permute-done((bf16[432,128]{1,0:T(8,128)(2,1)S(1)}, bf16[432,128]{1,0:T(8,128)(2,1)S(1)}, u32[]{:S(2)}, u32[]{:S(2)}) %collective-permute-start.24) | collective-permute-done | bytes 110624 | tf_op jit(solution)/shard_map/ppermute | solution.py:225
  61.9 0.1 collective-permute-start.30
  62.0 0.6 collective-permute-start.27
  62.6 0.0 collective-permute-done.28
  62.6 0.1 collective-permute-start.29
  62.7 0.0 collective-permute-done.25.refs_1_
  62.7 0.7 %collective-permute-done.30.refs_7_ = bf16[688,128]{1,0:T(8,128)(2,1)S(1)} collective-permute-done((bf16[688,128]{1,0:T(8,128)(2,1)S(1)}, bf16[688,128]{1,0:T(8,128)(2,1)S(1)}, u32[]{:S(2)}, u32[]{:S(2)}) %collective-permute-start.30) | collective-permute-done | bytes 176160 | tf_op jit(solution)/shard_map/ppermute | solution.py:215
  63.4 0.3 collective-permute-done.27.refs_3_
  63.7 0.5 collective-permute-done.29.refs_5_
  64.1 1.3 %shard_map.90 = (bf16[27,4,2,16,128]{4,3,2,1,0:T(8,128)(2,1)}, bf16[2,4,128,256]{3,2,1,0:T(8,128)(2,1)}) custom-call(bf16[688,128]{1,0:T(8,128)(2,1)S(1)} %pad_maximum_fusion.refs_0_, bf16[688,128]{1,0:T(8,128)(2,1)S(1)} %collective-permute-done.25.refs_1_, bf16[688,128]{1,0:T(8,128)(2,1)S(1)} %constant_dynamic-update-slice_fusion.refs_2_, ...), custom_call_target="tpu_custom_call" | custom-call | tf_op jit(solution)/shard_map/pallas_call | solution.py:16
  (33 shorter events, 0.4 us)
Async XLA Ops:
  0.6 8.9 %copy-start = (bf16[2,2,2,128,256]{4,3,2,1,0:T(8,128)(2,1)S(1)}, bf16[2,2,2,128,256]{4,3,2,1,0:T(8,128)(2,1)}, u32[]{:S(2)}) copy-start(bf16[2,2,2,128,256]{4,3,2,1,0:T(8,128)(2,1)} %param.9) | copy-start | bytes 1572868
  0.6 1.0 %copy-start.2 = (bf16[4,4,32,32]{3,2,1,0:T(8,128)(2,1)S(1)}, bf16[4,4,32,32]{3,2,1,0:T(8,128)(2,1)}, u32[]{:S(2)}) copy-start(bf16[4,4,32,32]{3,2,1,0:T(8,128)(2,1)} %param.11) | copy-start | bytes 98308
  1.6 4.2 %copy-start.3 = (bf16[1,8,64,128]{3,2,1,0:T(8,128)(2,1)S(1)}, bf16[1,8,64,128]{3,2,1,0:T(8,128)(2,1)}, u32[]{:S(2)}) copy-start(bf16[1,8,64,128]{3,2,1,0:T(8,128)(2,1)} %param.6) | copy-start | bytes 393220
  1.7 6.2 %collective-permute-start.4 = (bf16[2,32,128]{2,1,0:T(8,128)(2,1)S(1)}, bf16[2,32,128]{2,1,0:T(8,128)(2,1)S(1)}, u32[]{:S(2)}, u32[]{:S(2)}) collective-permute-start(bf16[2,32,128]{2,1,0:T(8,128)(2,1)S(1)} %get-tuple-element.46), channel_id=1, source_target_pairs={{0,16},{4,20},{8,24},{12,28},{16,0},{20,4},{24,8},{28,12},{1,17},{... | collective-permute-start | bytes 49160 | tf_op jit(solution)/shard_map/ppermute | solution.py:215
  5.9 7.3 %collective-permute-start = (bf16[32,512]{1,0:T(8,128)(2,1)S(1)}, bf16[32,512]{1,0:T(8,128)(2,1)S(1)}, u32[]{:S(2)}, u32[]{:S(2)}) collective-permute-start(bf16[32,512]{1,0:T(8,128)(2,1)S(1)} %get-tuple-element.42), channel_id=1, source_target_pairs={{0,1},{1,0},{2,3},{3,2},{4,5},{5,4},{6,7},{7,6},{8,9},{9,8},{10,11... | collective-permute-start | bytes 98312 | tf_op jit(solution)/shard_map/ppermute | solution.py:215
  6.0 7.2 %collective-permute-start.1 = (bf16[32,512]{1,0:T(8,128)(2,1)S(1)}, bf16[32,512]{1,0:T(8,128)(2,1)S(1)}, u32[]{:S(2)}, u32[]{:S(2)}) collective-permute-start(bf16[32,512]{1,0:T(8,128)(2,1)S(1)} %get-tuple-element.43), channel_id=1, source_target_pairs={{0,2},{1,3},{2,0},{3,1},{4,6},{5,7},{6,4},{7,5},{8,10},{9,11},{10,... | collective-permute-start | bytes 98312 | tf_op jit(solution)/shard_map/ppermute | solution.py:215
  7.6 5.7 %collective-permute-start.2 = (bf16[32,512]{1,0:T(8,128)(2,1)S(1)}, bf16[32,512]{1,0:T(8,128)(2,1)S(1)}, u32[]{:S(2)}, u32[]{:S(2)}) collective-permute-start(bf16[32,512]{1,0:T(8,128)(2,1)S(1)} %get-tuple-element.44), channel_id=1, source_target_pairs={{0,3},{1,2},{2,1},{3,0},{4,7},{5,6},{6,5},{7,4},{8,11},{9,10},{10,... | collective-permute-start | bytes 98312 | tf_op jit(solution)/shard_map/ppermute | solution.py:215
  7.9 3.8 %collective-permute-start.5 = (bf16[1,2,32,128]{3,2,1,0:T(8,128)(2,1)S(1)}, bf16[1,2,32,128]{3,2,1,0:T(8,128)(2,1)S(1)}, u32[]{:S(2)}, u32[]{:S(2)}) collective-permute-start(bf16[1,2,32,128]{3,2,1,0:T(8,128)(2,1)S(1)} %get-tuple-element.80), channel_id=1, source_target_pairs={{0,8},{4,12},{8,0},{12,4},{16,24},{20,28},{24,16},{28,20},{1,9},{5... | collective-permute-start | bytes 49160 | tf_op jit(solution)/shard_map/ppermute | solution.py:215
  11.7 3.9 %collective-permute-start.6 = (bf16[4,32,128]{2,1,0:T(8,128)(2,1)S(1)}, bf16[4,32,128]{2,1,0:T(8,128)(2,1)S(1)}, u32[]{:S(2)}, u32[]{:S(2)}) collective-permute-start(bf16[4,32,128]{2,1,0:T(8,128)(2,1)S(1)} %maximum_bitcast_fusion.refs_3_), channel_id=1, source_target_pairs={{0,4},{4,0},{8,12},{12,8},{16,20},{20,16},{24,28},{28,24},{1,5},{5... | collective-permute-start | bytes 98312 | tf_op jit(solution)/shard_map/ppermute | solution.py:215
  13.2 2.4 %copy-start.4 = (bf16[1,8,64,128]{3,2,1,0:T(8,128)(2,1)S(1)}, bf16[1,8,64,128]{3,2,1,0:T(8,128)(2,1)}, u32[]{:S(2)}) copy-start(bf16[1,8,64,128]{3,2,1,0:T(8,128)(2,1)} %param.7) | copy-start | bytes 393220
  13.2 2.4 %copy-start.5 = (bf16[1,8,64,128]{3,2,1,0:T(8,128)(2,1)S(1)}, bf16[1,8,64,128]{3,2,1,0:T(8,128)(2,1)}, u32[]{:S(2)}) copy-start(bf16[1,8,64,128]{3,2,1,0:T(8,128)(2,1)} %param.10) | copy-start | bytes 393220
  16.2 3.5 %collective-permute-start.7 = (bf16[512,128]{1,0:T(8,128)(2,1)S(1)}, bf16[512,128]{1,0:T(8,128)(2,1)S(1)}, u32[]{:S(2)}, u32[]{:S(2)}) collective-permute-start(bf16[512,128]{1,0:T(8,128)(2,1)S(1)} %get-tuple-element.53.refs_3_), channel_id=1, source_target_pairs={{0,1},{1,0},{2,3},{3,2},{4,5},{5,4},{6,7},{7,6},{8,9},{9,8},{10,11... | collective-permute-start | bytes 393224 | tf_op jit(solution)/shard_map/ppermute | solution.py:215
  16.3 5.9 %collective-permute-start.3 = (bf16[4,32,512]{2,1,0:T(8,128)(2,1)S(1)}, bf16[4,32,512]{2,1,0:T(8,128)(2,1)S(1)}, u32[]{:S(2)}, u32[]{:S(2)}) collective-permute-start(bf16[4,32,512]{2,1,0:T(8,128)(2,1)S(1)} %pad_maximum_fusion.1.refs_1_), channel_id=1, source_target_pairs={{0,4},{4,0},{8,12},{12,8},{16,20},{20,16},{24,28},{28,24},{1,5},{5... | collective-permute-start | bytes 393224 | tf_op jit(solution)/shard_map/ppermute | solution.py:215
  17.9 5.8 %collective-permute-start.10 = (bf16[512,128]{1,0:T(8,128)(2,1)S(1)}, bf16[512,128]{1,0:T(8,128)(2,1)S(1)}, u32[]{:S(2)}, u32[]{:S(2)}) collective-permute-start(bf16[512,128]{1,0:T(8,128)(2,1)S(1)} %get-tuple-element.53.refs_3_), channel_id=1, source_target_pairs={{0,3},{1,2},{2,1},{3,0},{4,7},{5,6},{6,5},{7,4},{8,11},{9,10},{10,... | collective-permute-start | bytes 393224 | tf_op jit(solution)/shard_map/ppermute | solution.py:215
  19.2 7.7 %collective-permute-start.9 = (bf16[512,128]{1,0:T(8,128)(2,1)S(1)}, bf16[512,128]{1,0:T(8,128)(2,1)S(1)}, u32[]{:S(2)}, u32[]{:S(2)}) collective-permute-start(bf16[512,128]{1,0:T(8,128)(2,1)S(1)} %get-tuple-element.53.refs_3_), channel_id=1, source_target_pairs={{0,2},{1,3},{2,0},{3,1},{4,6},{5,7},{6,4},{7,5},{8,10},{9,11},{10,... | collective-permute-start | bytes 393224 | tf_op jit(solution)/shard_map/ppermute | solution.py:215
  19.7 7.1 %collective-permute-start.8 = (bf16[4,32,512]{2,1,0:T(8,128)(2,1)S(1)}, bf16[4,32,512]{2,1,0:T(8,128)(2,1)S(1)}, u32[]{:S(2)}, u32[]{:S(2)}) collective-permute-start(bf16[4,32,512]{2,1,0:T(8,128)(2,1)S(1)} %pad_maximum_fusion.1.refs_1_), channel_id=1, source_target_pairs={{4,8},{8,4},{12,16},{16,12},{20,24},{24,20},{5,9},{9,5},{13,17},{1... | collective-permute-start | bytes 393224 | tf_op jit(solution)/shard_map/ppermute | solution.py:235
  22.2 7.8 %collective-permute-start.12 = (bf16[256,128]{1,0:T(8,128)(2,1)S(1)}, bf16[256,128]{1,0:T(8,128)(2,1)S(1)}, u32[]{:S(2)}, u32[]{:S(2)}) collective-permute-start(bf16[256,128]{1,0:T(8,128)(2,1)S(1)} %get-tuple-element.60), channel_id=1, source_target_pairs={{0,1},{1,0},{2,3},{3,2},{4,5},{5,4},{6,7},{7,6},{8,9},{9,8},{10,11... | collective-permute-start | bytes 196616 | tf_op jit(solution)/shard_map/ppermute | solution.py:215
  22.2 7.8 %collective-permute-start.13 = (bf16[256,128]{1,0:T(8,128)(2,1)S(1)}, bf16[256,128]{1,0:T(8,128)(2,1)S(1)}, u32[]{:S(2)}, u32[]{:S(2)}) collective-permute-start(bf16[256,128]{1,0:T(8,128)(2,1)S(1)} %get-tuple-element.61), channel_id=1, source_target_pairs={{0,2},{1,3},{2,0},{3,1},{4,6},{5,7},{6,4},{7,5},{8,10},{9,11},{10,... | collective-permute-start | bytes 196616 | tf_op jit(solution)/shard_map/ppermute | solution.py:215
  23.7 6.3 %collective-permute-start.14 = (bf16[256,128]{1,0:T(8,128)(2,1)S(1)}, bf16[256,128]{1,0:T(8,128)(2,1)S(1)}, u32[]{:S(2)}, u32[]{:S(2)}) collective-permute-start(bf16[256,128]{1,0:T(8,128)(2,1)S(1)} %get-tuple-element.62), channel_id=1, source_target_pairs={{0,3},{1,2},{2,1},{3,0},{4,7},{5,6},{6,5},{7,4},{8,11},{9,10},{10,... | collective-permute-start | bytes 196616 | tf_op jit(solution)/shard_map/ppermute | solution.py:215
  28.3 21.8 %copy-start.1 = (bf16[3,3,3,128,128]{4,3,2,1,0:T(8,128)(2,1)S(1)}, bf16[3,3,3,128,128]{4,3,2,1,0:T(8,128)(2,1)}, u32[]{:S(2)}) copy-start(bf16[3,3,3,128,128]{4,3,2,1,0:T(8,128)(2,1)} %weight.1) | copy-start | bytes 2654212
  28.4 7.0 %collective-permute-start.11 = (bf16[432,128]{1,0:T(8,128)(2,1)S(1)}, bf16[432,128]{1,0:T(8,128)(2,1)S(1)}, u32[]{:S(2)}, u32[]{:S(2)}) collective-permute-start(bf16[432,128]{1,0:T(8,128)(2,1)S(1)} %get-tuple-element.58), channel_id=1, source_target_pairs={{0,4},{4,0},{8,12},{12,8},{16,20},{20,16},{24,28},{28,24},{1,5},{5... | collective-permute-start | bytes 331784 | tf_op jit(solution)/shard_map/ppermute | solution.py:215
  30.1 5.2 %collective-permute-start.15 = (bf16[256,128]{1,0:T(8,128)(2,1)S(1)}, bf16[256,128]{1,0:T(8,128)(2,1)S(1)}, u32[]{:S(2)}, u32[]{:S(2)}) collective-permute-start(bf16[256,128]{1,0:T(8,128)(2,1)S(1)} %add_convert_fusion.3), channel_id=1, source_target_pairs={{0,16},{4,20},{8,24},{12,28},{16,0},{20,4},{24,8},{28,12},{1,17},{... | collective-permute-start | bytes 196616 | tf_op jit(solution)/shard_map/ppermute | solution.py:215
  32.7 7.2 %collective-permute-start.19 = (bf16[10,64,128]{2,1,0:T(8,128)(2,1)S(1)}, bf16[10,64,128]{2,1,0:T(8,128)(2,1)S(1)}, u32[]{:S(2)}, u32[]{:S(2)}) collective-permute-start(bf16[10,64,128]{2,1,0:T(8,128)(2,1)S(1)} %get-tuple-element.65.own), channel_id=1, source_target_pairs={{0,4},{4,0},{8,12},{12,8},{16,20},{20,16},{24,28},{28,24},{1,5},{5... | collective-permute-start | bytes 491528 | tf_op jit(solution)/shard_map/ppermute | solution.py:215
  34.2 5.7 %collective-permute-start.18 = (bf16[10,64,128]{2,1,0:T(8,128)(2,1)S(1)}, bf16[10,64,128]{2,1,0:T(8,128)(2,1)S(1)}, u32[]{:S(2)}, u32[]{:S(2)}) collective-permute-start(bf16[10,64,128]{2,1,0:T(8,128)(2,1)S(1)} %get-tuple-element.65.own), channel_id=1, source_target_pairs={{4,8},{8,4},{12,16},{16,12},{20,24},{24,20},{5,9},{9,5},{13,17},{1... | collective-permute-start | bytes 491528 | tf_op jit(solution)/shard_map/ppermute | solution.py:235
  35.4 11.1 %collective-permute-start.16 = (bf16[432,128]{1,0:T(8,128)(2,1)S(1)}, bf16[432,128]{1,0:T(8,128)(2,1)S(1)}, u32[]{:S(2)}, u32[]{:S(2)}) collective-permute-start(bf16[432,128]{1,0:T(8,128)(2,1)S(1)} %add_convert_fusion.1), channel_id=1, source_target_pairs={{0,16},{4,20},{8,24},{12,28},{16,0},{20,4},{24,8},{28,12},{1,17},{... | collective-permute-start | bytes 331784 | tf_op jit(solution)/shard_map/ppermute | solution.py:215
  38.8 4.8 %collective-permute-start.17 = (bf16[256,128]{1,0:T(8,128)(2,1)S(1)}, bf16[256,128]{1,0:T(8,128)(2,1)S(1)}, u32[]{:S(2)}, u32[]{:S(2)}) collective-permute-start(bf16[256,128]{1,0:T(8,128)(2,1)S(1)} %add_convert_fusion.2), channel_id=1, source_target_pairs={{0,8},{4,12},{8,0},{12,4},{16,24},{20,28},{24,16},{28,20},{1,9},{5... | collective-permute-start | bytes 196616 | tf_op jit(solution)/shard_map/ppermute | solution.py:215
  46.5 7.9 %collective-permute-start.20 = (bf16[432,128]{1,0:T(8,128)(2,1)S(1)}, bf16[432,128]{1,0:T(8,128)(2,1)S(1)}, u32[]{:S(2)}, u32[]{:S(2)}) collective-permute-start(bf16[432,128]{1,0:T(8,128)(2,1)S(1)} %add_convert_fusion), channel_id=1, source_target_pairs={{0,8},{4,12},{8,0},{12,4},{16,24},{20,28},{24,16},{28,20},{1,9},{5... | collective-permute-start | bytes 331784 | tf_op jit(solution)/shard_map/ppermute | solution.py:215
  46.6 5.3 %collective-permute-start.23 = (bf16[256,128]{1,0:T(8,128)(2,1)S(1)}, bf16[256,128]{1,0:T(8,128)(2,1)S(1)}, u32[]{:S(2)}, u32[]{:S(2)}) collective-permute-start(bf16[256,128]{1,0:T(8,128)(2,1)S(1)} %multiply_convert_fusion.1), channel_id=1, source_target_pairs={{0,6},{1,7},{2,4},{3,5},{4,2},{5,3},{6,0},{7,1},{8,14},{9,15},{10,... | collective-permute-start | bytes 196616 | tf_op jit(solution)/shard_map/ppermute | solution.py:225
  48.6 4.3 %collective-permute-start.22 = (bf16[256,128]{1,0:T(8,128)(2,1)S(1)}, bf16[256,128]{1,0:T(8,128)(2,1)S(1)}, u32[]{:S(2)}, u32[]{:S(2)}) collective-permute-start(bf16[256,128]{1,0:T(8,128)(2,1)S(1)} %multiply_convert_fusion.1), channel_id=1, source_target_pairs={{0,4},{4,0},{8,12},{12,8},{16,20},{20,16},{24,28},{28,24},{1,5},{5... | collective-permute-start | bytes 196616 | tf_op jit(solution)/shard_map/ppermute | solution.py:215
  49.7 4.7 %collective-permute-start.21 = (bf16[256,128]{1,0:T(8,128)(2,1)S(1)}, bf16[256,128]{1,0:T(8,128)(2,1)S(1)}, u32[]{:S(2)}, u32[]{:S(2)}) collective-permute-start(bf16[256,128]{1,0:T(8,128)(2,1)S(1)} %multiply_convert_fusion.1), channel_id=1, source_target_pairs={{0,2},{1,3},{2,0},{3,1},{4,6},{5,7},{6,4},{7,5},{8,10},{9,11},{10,... | collective-permute-start | bytes 196616 | tf_op jit(solution)/shard_map/ppermute | solution.py:215
  54.4 8.2 %collective-permute-start.28 = (bf16[432,128]{1,0:T(8,128)(2,1)S(1)}, bf16[432,128]{1,0:T(8,128)(2,1)S(1)}, u32[]{:S(2)}, u32[]{:S(2)}) collective-permute-start(bf16[432,128]{1,0:T(8,128)(2,1)S(1)} %multiply_convert_fusion), channel_id=1, source_target_pairs={{0,4},{4,0},{8,12},{12,8},{16,20},{20,16},{24,28},{28,24},{1,5},{5... | collective-permute-start | bytes 331784 | tf_op jit(solution)/shard_map/ppermute | solution.py:215
  55.0 7.0 %collective-permute-start.26 = (bf16[432,128]{1,0:T(8,128)(2,1)S(1)}, bf16[432,128]{1,0:T(8,128)(2,1)S(1)}, u32[]{:S(2)}, u32[]{:S(2)}) collective-permute-start(bf16[432,128]{1,0:T(8,128)(2,1)S(1)} %multiply_convert_fusion), channel_id=1, source_target_pairs={{0,2},{1,3},{2,0},{3,1},{4,6},{5,7},{6,4},{7,5},{8,10},{9,11},{10,... | collective-permute-start | bytes 331784 | tf_op jit(solution)/shard_map/ppermute | solution.py:215
  55.6 6.3 %collective-permute-start.24 = (bf16[432,128]{1,0:T(8,128)(2,1)S(1)}, bf16[432,128]{1,0:T(8,128)(2,1)S(1)}, u32[]{:S(2)}, u32[]{:S(2)}) collective-permute-start(bf16[432,128]{1,0:T(8,128)(2,1)S(1)} %multiply_convert_fusion), channel_id=1, source_target_pairs={{0,6},{1,7},{2,4},{3,5},{4,2},{5,3},{6,0},{7,1},{8,14},{9,15},{10,... | collective-permute-start | bytes 331784 | tf_op jit(solution)/shard_map/ppermute | solution.py:225
  58.0 4.7 %collective-permute-start.25 = (bf16[688,128]{1,0:T(8,128)(2,1)S(1)}, bf16[688,128]{1,0:T(8,128)(2,1)S(1)}, u32[]{:S(2)}, u32[]{:S(2)}) collective-permute-start(bf16[688,128]{1,0:T(8,128)(2,1)S(1)} %pad_maximum_fusion.refs_0_), channel_id=1, source_target_pairs={{0,1},{1,0},{2,3},{3,2},{4,5},{5,4},{6,7},{7,6},{8,9},{9,8},{10,11... | collective-permute-start | bytes 528392 | tf_op jit(solution)/shard_map/ppermute | solution.py:215
  61.9 1.5 %collective-permute-start.30 = (bf16[688,128]{1,0:T(8,128)(2,1)S(1)}, bf16[688,128]{1,0:T(8,128)(2,1)S(1)}, u32[]{:S(2)}, u32[]{:S(2)}) collective-permute-start(bf16[688,128]{1,0:T(8,128)(2,1)S(1)} %constant_dynamic-update-slice_fusion.4.refs_6_), channel_id=1, source_target_pairs={{0,1},{1,0},{2,3},{3,2},{4,5},{5,4},{6,7},{7,6},{8,9},{9,8},{10,11... | collective-permute-start | bytes 528392 | tf_op jit(solution)/shard_map/ppermute | solution.py:215
  62.0 1.6 %collective-permute-start.27 = (bf16[688,128]{1,0:T(8,128)(2,1)S(1)}, bf16[688,128]{1,0:T(8,128)(2,1)S(1)}, u32[]{:S(2)}, u32[]{:S(2)}) collective-permute-start(bf16[688,128]{1,0:T(8,128)(2,1)S(1)} %constant_dynamic-update-slice_fusion.refs_2_), channel_id=1, source_target_pairs={{0,1},{1,0},{2,3},{3,2},{4,5},{5,4},{6,7},{7,6},{8,9},{9,8},{10,11... | collective-permute-start | bytes 528392 | tf_op jit(solution)/shard_map/ppermute | solution.py:215
  62.6 1.5 %collective-permute-start.29 = (bf16[688,128]{1,0:T(8,128)(2,1)S(1)}, bf16[688,128]{1,0:T(8,128)(2,1)S(1)}, u32[]{:S(2)}, u32[]{:S(2)}) collective-permute-start(bf16[688,128]{1,0:T(8,128)(2,1)S(1)} %constant_dynamic-update-slice_fusion.2.refs_4_), channel_id=1, source_target_pairs={{0,1},{1,0},{2,3},{3,2},{4,5},{5,4},{6,7},{7,6},{8,9},{9,8},{10,11... | collective-permute-start | bytes 528392 | tf_op jit(solution)/shard_map/ppermute | solution.py:215

commit v20 on v18

--- a/solution.py
+++ b/solution.py
@@ -326,7 +326,7 @@
             pltpu.VMEM((2, 27 * half, channels), F32),
         ],
     )
-    near_odd, near_even = odd_pairs(near), even_pairs(near)
+    near_odd = odd_pairs(near)
     def rounded(value):
         return lax.optimization_barrier(value.astype(wire))
 
@@ -345,12 +345,15 @@
         down_other = swapped(down, "gz", code)
         if index == 0:
             send, down_other = lax.optimization_barrier((send, down_other))
-            conv = rounded(keep + send.astype(F32))
+            conv = (keep + send.astype(F32)).astype(wire)
+            conv, late = lax.optimization_barrier((conv, near))
+            cut = late.shape[0] // 2
+            evens = even_pairs(late[:cut]), even_pairs(late[cut:])
         else:
             conv_other = swapped(conv, "gz", codes[index - 1])
             if index == 1:
-                tied = (conv_other, down_other, near_odd, near_even)
-                conv_other, down_other, near_odd, near_even = lax.optimization_barrier(tied)
+                tied = (conv_other, down_other, near_odd, *evens)
+                conv_other, down_other, near_odd, *evens = lax.optimization_barrier(tied)
             conv = rounded(added(conv, conv_other))
         down = added(down, down_other)
         if index < len(codes) - 1:
@@ -359,7 +362,7 @@
     input_grad = call(
         input_kernel,
         shape((rows, cols, channels), BF16),
-        near_even,
+        jnp.concatenate(evens, axis=0),
         near,
         near_odd,
         conv_weight,

time: 62.8 us -> 62.8 us (level)
  starting transfers between devices: 30.9 us -> 32.5 us
  waiting for transfers between devices: 24.3 us -> 22.7 us
    ppermute x25 -> x26, waiting for transfers between devices: 21.3 us -> 19.7 us  [swapped(): lax.ppermute(value, axis, [(i, i ^ code) for i in range(lax.axis_size(axi...]
    ppermute x1, starting transfers between devices: 0.35 us -> 1.71 us  [crossed(): return lax.ppermute(value, ('gz', 'gy'), pairs)]
    ppermute x25 -> x26, starting transfers between devices: 29.3 us -> 29.5 us  [swapped(): lax.ppermute(value, axis, [(i, i ^ code) for i in range(lax.axis_size(axi...]
  transfers between devices with their start and end apart: 28 -> 29, of which waited for: 13 -> 12; matrix products, arithmetic and copies ran while one was open for 0% -> 0% of each run, Pallas kernels for 5% -> 5%
where the time goes in v20:
time: 62.8 us; the launch traced here: 62.6 us
  starting transfers between devices  32.5 us (52%)
  waiting for transfers between devices  22.7 us (36%)
  Pallas kernels  5.35 us (9%)
  local copies, waits for them, and re-layouts  1.01 us (2%)
  between operations  0.83 us (1%)
    ppermute x26, starting transfers between devices, swapped(): lax.ppermute(value, axis, [(i, i ^ code) for i in range(lax.axis_size(axi...  29.5 us
    ppermute x26, waiting for transfers between devices, swapped(): lax.ppermute(value, axis, [(i, i ^ code) for i in range(lax.axis_size(axi...  19.7 us
    pallas_call x6, Pallas kernels, call(): pl.pallas_call(kernel, out_shape=out_shape, scratch_shapes=list(scratch),...  5.35 us
    ppermute x1, waiting for transfers between devices, crossed(): return lax.ppermute(value, ('gz', 'gy'), pairs)  2.96 us
    ppermute x1, starting transfers between devices, crossed(): return lax.ppermute(value, ('gz', 'gy'), pairs)  1.71 us
    ppermute x2, starting transfers between devices, odd_pairs(): return lax.ppermute(value, 'gz', pairs)  1.32 us
  transfers between devices with their start and end apart: 29, of which 12 were waited for; matrix products, arithmetic and copies ran while one was open for 0% of the time, Pallas kernels for 5%

profile of v20, /device:TPU:0, one launch (start us, length us, event | category | flops | bytes accessed | tf_op | source)
XLA Modules:
  0.0 62.6 jit_solution(2504254480839452965)
XLA Ops:
  0.6 0.0 copy-start
  0.7 1.0 %copy-done.2 = bf16[4,4,32,32]{3,2,1,0:T(8,128)(2,1)S(1)} copy-done((bf16[4,4,32,32]{3,2,1,0:T(8,128)(2,1)S(1)}, bf16[4,4,32,32]{3,2,1,0:T(8,128)(2,1)}, u32[]{:S(2)}) %copy-start.2) | copy-done | bytes 32792
  1.6 0.1 shard_map.86
  1.7 4.1 %collective-permute-start.4 = (bf16[2,32,128]{2,1,0:T(8,128)(2,1)S(1)}, bf16[2,32,128]{2,1,0:T(8,128)(2,1)S(1)}, u32[]{:S(2)}, u32[]{:S(2)}) collective-permute-start(bf16[2,32,128]{2,1,0:T(8,128)(2,1)S(1)} %get-tuple-element.44), channel_id=1, source_target_pairs={{0,16},{4,20},{8,24},{12,28},{16,0},{20,4},{24,8},{28,12},{1,17},{... | collective-permute-start | bytes 49160 | tf_op jit(solution)/shard_map/ppermute | solution.py:215
  5.8 0.1 shard_map.85
  5.9 0.1 collective-permute-start
  6.0 1.6 %collective-permute-start.1 = (bf16[32,512]{1,0:T(8,128)(2,1)S(1)}, bf16[32,512]{1,0:T(8,128)(2,1)S(1)}, u32[]{:S(2)}, u32[]{:S(2)}) collective-permute-start(bf16[32,512]{1,0:T(8,128)(2,1)S(1)} %get-tuple-element.41), channel_id=1, source_target_pairs={{0,2},{1,3},{2,0},{3,1},{4,6},{5,7},{6,4},{7,5},{8,10},{9,11},{10,... | collective-permute-start | bytes 98312 | tf_op jit(solution)/shard_map/ppermute | solution.py:215
  7.6 0.3 collective-permute-start.2
  7.9 0.0 collective-permute-done.4
  7.9 1.6 %collective-permute-start.5 = (bf16[1,2,32,128]{3,2,1,0:T(8,128)(2,1)S(1)}, bf16[1,2,32,128]{3,2,1,0:T(8,128)(2,1)S(1)}, u32[]{:S(2)}, u32[]{:S(2)}) collective-permute-start(bf16[1,2,32,128]{3,2,1,0:T(8,128)(2,1)S(1)} %get-tuple-element.78), channel_id=1, source_target_pairs={{0,8},{4,12},{8,0},{12,4},{16,24},{20,28},{24,16},{28,20},{1,9},{5... | collective-permute-start | bytes 49160 | tf_op jit(solution)/shard_map/ppermute | solution.py:215
  9.5 2.1 %collective-permute-done.5 = bf16[1,2,32,128]{3,2,1,0:T(8,128)(2,1)S(1)} collective-permute-done((bf16[1,2,32,128]{3,2,1,0:T(8,128)(2,1)S(1)}, bf16[1,2,32,128]{3,2,1,0:T(8,128)(2,1)S(1)}, u32[]{:S(2)}, u32[]{:S(2)}) %collective-permute-start.5) | collective-permute-done | bytes 16416 | tf_op jit(solution)/shard_map/ppermute | solution.py:215
  11.7 1.5 %collective-permute-start.6 = (bf16[4,32,128]{2,1,0:T(8,128)(2,1)S(1)}, bf16[4,32,128]{2,1,0:T(8,128)(2,1)S(1)}, u32[]{:S(2)}, u32[]{:S(2)}) collective-permute-start(bf16[4,32,128]{2,1,0:T(8,128)(2,1)S(1)} %maximum_bitcast_fusion.refs_3_), channel_id=1, source_target_pairs={{0,4},{4,0},{8,12},{12,8},{16,20},{20,16},{24,28},{28,24},{1,5},{5... | collective-permute-start | bytes 98312 | tf_op jit(solution)/shard_map/ppermute | solution.py:215
  13.2 0.0 collective-permute-done
  13.2 0.0 collective-permute-done.1
  13.2 0.0 collective-permute-done.2
  13.2 0.0 copy-start.4
  13.2 0.0 copy-start.5
  13.3 2.3 %collective-permute-done.6.refs_4_ = bf16[4,32,128]{2,1,0:T(8,128)(2,1)S(1)} collective-permute-done((bf16[4,32,128]{2,1,0:T(8,128)(2,1)S(1)}, bf16[4,32,128]{2,1,0:T(8,128)(2,1)S(1)}, u32[]{:S(2)}, u32[]{:S(2)}) %collective-permute-start.6) | collective-permute-done | bytes 32800 | tf_op jit(solution)/shard_map/ppermute | solution.py:215
  15.6 0.6 shard_map.87
  16.2 0.1 collective-permute-start.7
  16.3 1.6 %collective-permute-start.3 = (bf16[4,32,512]{2,1,0:T(8,128)(2,1)S(1)}, bf16[4,32,512]{2,1,0:T(8,128)(2,1)S(1)}, u32[]{:S(2)}, u32[]{:S(2)}) collective-permute-start(bf16[4,32,512]{2,1,0:T(8,128)(2,1)S(1)} %pad_maximum_fusion.2.refs_1_), channel_id=1, source_target_pairs={{0,4},{4,0},{8,12},{12,8},{16,20},{20,16},{24,28},{28,24},{1,5},{5... | collective-permute-start | bytes 393224 | tf_op jit(solution)/shard_map/ppermute | solution.py:215
  17.9 1.3 %collective-permute-start.10 = (bf16[512,128]{1,0:T(8,128)(2,1)S(1)}, bf16[512,128]{1,0:T(8,128)(2,1)S(1)}, u32[]{:S(2)}, u32[]{:S(2)}) collective-permute-start(bf16[512,128]{1,0:T(8,128)(2,1)S(1)} %get-tuple-element.51.refs_3_), channel_id=1, source_target_pairs={{0,3},{1,2},{2,1},{3,0},{4,7},{5,6},{6,5},{7,4},{8,11},{9,10},{10,... | collective-permute-start | bytes 393224 | tf_op jit(solution)/shard_map/ppermute | solution.py:215
  19.2 0.5 collective-permute-start.9
  19.7 0.0 collective-permute-done.7.refs_4_
  19.7 0.7 %collective-permute-start.8 = (bf16[4,32,512]{2,1,0:T(8,128)(2,1)S(1)}, bf16[4,32,512]{2,1,0:T(8,128)(2,1)S(1)}, u32[]{:S(2)}, u32[]{:S(2)}) collective-permute-start(bf16[4,32,512]{2,1,0:T(8,128)(2,1)S(1)} %pad_maximum_fusion.2.refs_1_), channel_id=1, source_target_pairs={{4,8},{8,4},{12,16},{16,12},{20,24},{24,20},{5,9},{9,5},{13,17},{1... | collective-permute-start | bytes 393224 | tf_op jit(solution)/shard_map/ppermute | solution.py:235
  20.4 1.9 %collective-permute-done.3.refs_0_ = bf16[4,32,512]{2,1,0:T(8,128)(2,1)S(1)} collective-permute-done((bf16[4,32,512]{2,1,0:T(8,128)(2,1)S(1)}, bf16[4,32,512]{2,1,0:T(8,128)(2,1)S(1)}, u32[]{:S(2)}, u32[]{:S(2)}) %collective-permute-start.3) | collective-permute-done | bytes 131104 | tf_op jit(solution)/shard_map/ppermute | solution.py:215
  22.2 0.0 collective-permute-start.12
  22.2 1.5 %collective-permute-start.13 = (bf16[256,128]{1,0:T(8,128)(2,1)S(1)}, bf16[256,128]{1,0:T(8,128)(2,1)S(1)}, u32[]{:S(2)}, u32[]{:S(2)}) collective-permute-start(bf16[256,128]{1,0:T(8,128)(2,1)S(1)} %get-tuple-element.59), channel_id=1, source_target_pairs={{0,2},{1,3},{2,0},{3,1},{4,6},{5,7},{6,4},{7,5},{8,10},{9,11},{10,... | collective-permute-start | bytes 196616 | tf_op jit(solution)/shard_map/ppermute | solution.py:215
  23.7 0.0 collective-permute-done.10.refs_6_
  23.7 1.2 %collective-permute-start.14 = (bf16[256,128]{1,0:T(8,128)(2,1)S(1)}, bf16[256,128]{1,0:T(8,128)(2,1)S(1)}, u32[]{:S(2)}, u32[]{:S(2)}) collective-permute-start(bf16[256,128]{1,0:T(8,128)(2,1)S(1)} %get-tuple-element.60), channel_id=1, source_target_pairs={{0,3},{1,2},{2,1},{3,0},{4,7},{5,6},{6,5},{7,4},{8,11},{9,10},{10,... | collective-permute-start | bytes 196616 | tf_op jit(solution)/shard_map/ppermute | solution.py:215
  25.0 1.9 %collective-permute-done.9.refs_5_ = bf16[512,128]{1,0:T(8,128)(2,1)S(1)} collective-permute-done((bf16[512,128]{1,0:T(8,128)(2,1)S(1)}, bf16[512,128]{1,0:T(8,128)(2,1)S(1)}, u32[]{:S(2)}, u32[]{:S(2)}) %collective-permute-start.9) | collective-permute-done | bytes 131104 | tf_op jit(solution)/shard_map/ppermute | solution.py:215
  26.8 0.0 collective-permute-done.8.refs_2_
  26.8 1.5 %shard_map.88 = (f32[432,128]{1,0:T(8,128)S(1)}, bf16[432,128]{1,0:T(8,128)(2,1)S(1)}, bf16[10,64,128]{2,1,0:T(8,128)(2,1)S(1)}) custom-call(bf16[4,32,512]{2,1,0:T(8,128)(2,1)S(1)} %collective-permute-done.3.refs_0_, bf16[4,32,512]{2,1,0:T(8,128)(2,1)S(1)} %pad_maximum_fusion.2.refs_1_, bf16[4,32,512]{2,1,0:T(8,128)(2,1)S(1)} %collective-permute-done.8.refs_2_, ...), custom_call_target="tpu_custom_call" | custom-call | tf_op jit(solution)/shard_map/pallas_call | solution.py:16
  28.4 1.7 %collective-permute-start.11 = (bf16[432,128]{1,0:T(8,128)(2,1)S(1)}, bf16[432,128]{1,0:T(8,128)(2,1)S(1)}, u32[]{:S(2)}, u32[]{:S(2)}) collective-permute-start(bf16[432,128]{1,0:T(8,128)(2,1)S(1)} %get-tuple-element.56), channel_id=1, source_target_pairs={{0,4},{4,0},{8,12},{12,8},{16,20},{20,16},{24,28},{28,24},{1,5},{5... | collective-permute-start | bytes 331784 | tf_op jit(solution)/shard_map/ppermute | solution.py:215
  30.0 0.0 collective-permute-done.12
  30.0 0.0 collective-permute-done.13
  30.0 0.0 collective-permute-done.14
  30.1 2.6 %collective-permute-start.15 = (bf16[256,128]{1,0:T(8,128)(2,1)S(1)}, bf16[256,128]{1,0:T(8,128)(2,1)S(1)}, u32[]{:S(2)}, u32[]{:S(2)}) collective-permute-start(bf16[256,128]{1,0:T(8,128)(2,1)S(1)} %add_convert_fusion.3), channel_id=1, source_target_pairs={{0,16},{4,20},{8,24},{12,28},{16,0},{20,4},{24,8},{28,12},{1,17},{... | collective-permute-start | bytes 196616 | tf_op jit(solution)/shard_map/ppermute | solution.py:215
  32.7 0.7 %collective-permute-start.18 = (bf16[10,64,128]{2,1,0:T(8,128)(2,1)S(1)}, bf16[10,64,128]{2,1,0:T(8,128)(2,1)S(1)}, u32[]{:S(2)}, u32[]{:S(2)}) collective-permute-start(bf16[10,64,128]{2,1,0:T(8,128)(2,1)S(1)} %get-tuple-element.65.own), channel_id=1, source_target_pairs={{4,8},{8,4},{12,16},{16,12},{20,24},{24,20},{5,9},{9,5},{13,17},{1... | collective-permute-start | bytes 491528 | tf_op jit(solution)/shard_map/ppermute | solution.py:235
  33.3 2.0 %collective-permute-done.15 = bf16[256,128]{1,0:T(8,128)(2,1)S(1)} collective-permute-done((bf16[256,128]{1,0:T(8,128)(2,1)S(1)}, bf16[256,128]{1,0:T(8,128)(2,1)S(1)}, u32[]{:S(2)}, u32[]{:S(2)}) %collective-permute-start.15) | collective-permute-done | bytes 65568 | tf_op jit(solution)/shard_map/ppermute | solution.py:215
  35.3 0.0 collective-permute-done.11
  35.4 3.4 %collective-permute-start.16 = (bf16[432,128]{1,0:T(8,128)(2,1)S(1)}, bf16[432,128]{1,0:T(8,128)(2,1)S(1)}, u32[]{:S(2)}, u32[]{:S(2)}) collective-permute-start(bf16[432,128]{1,0:T(8,128)(2,1)S(1)} %add_convert_fusion.1), channel_id=1, source_target_pairs={{0,16},{4,20},{8,24},{12,28},{16,0},{20,4},{24,8},{28,12},{1,17},{... | collective-permute-start | bytes 331784 | tf_op jit(solution)/shard_map/ppermute | solution.py:215
  38.8 0.8 %collective-permute-start.20 = (bf16[5,64,128]{2,1,0:T(8,128)(2,1)S(1)}, bf16[5,64,128]{2,1,0:T(8,128)(2,1)S(1)}, u32[]{:S(2)}, u32[]{:S(2)}) collective-permute-start(bf16[5,64,128]{2,1,0:T(8,128)(2,1)S(1)} %get-tuple-element.75), channel_id=1, source_target_pairs={{0,4},{4,0},{8,12},{12,8},{16,20},{20,16},{24,28},{28,24},{1,5},{5... | collective-permute-start | bytes 245768 | tf_op jit(solution)/shard_map/ppermute | solution.py:215
  39.6 1.3 %collective-permute-start.19 = (bf16[5,64,128]{2,1,0:T(8,128)(2,1)S(1)}, bf16[5,64,128]{2,1,0:T(8,128)(2,1)S(1)}, u32[]{:S(2)}, u32[]{:S(2)}) collective-permute-start(bf16[5,64,128]{2,1,0:T(8,128)(2,1)S(1)} %get-tuple-element.76), channel_id=1, source_target_pairs={{0,4},{4,0},{8,12},{12,8},{16,20},{20,16},{24,28},{28,24},{1,5},{5... | collective-permute-start | bytes 245768 | tf_op jit(solution)/shard_map/ppermute | solution.py:215
  40.9 1.7 %collective-permute-start.17 = (bf16[256,128]{1,0:T(8,128)(2,1)S(1)}, bf16[256,128]{1,0:T(8,128)(2,1)S(1)}, u32[]{:S(2)}, u32[]{:S(2)}) collective-permute-start(bf16[256,128]{1,0:T(8,128)(2,1)S(1)} %add_convert_fusion.2), channel_id=1, source_target_pairs={{0,8},{4,12},{8,0},{12,4},{16,24},{20,28},{24,16},{28,20},{1,9},{5... | collective-permute-start | bytes 196616 | tf_op jit(solution)/shard_map/ppermute | solution.py:215
  42.6 3.8 %collective-permute-done.17 = bf16[256,128]{1,0:T(8,128)(2,1)S(1)} collective-permute-done((bf16[256,128]{1,0:T(8,128)(2,1)S(1)}, bf16[256,128]{1,0:T(8,128)(2,1)S(1)}, u32[]{:S(2)}, u32[]{:S(2)}) %collective-permute-start.17) | collective-permute-done | bytes 65568 | tf_op jit(solution)/shard_map/ppermute | solution.py:215
  46.4 0.0 collective-permute-done.19
  46.4 0.0 collective-permute-done.16
  46.5 0.5 collective-permute-start.21
  47.0 1.7 %shard_map.89 = bf16[8,64,128]{2,1,0:T(8,128)(2,1)} custom-call(bf16[10,64,128]{2,1,0:T(8,128)(2,1)S(1)} %pad_maximum_fusion.1.even, bf16[10,64,128]{2,1,0:T(8,128)(2,1)S(1)} %get-tuple-element.65.own, bf16[10,64,128]{2,1,0:T(8,128)(2,1)S(1)} %collective-permute-done.18.odd, bf16[3,3,3,128,128]{4,3,2,1,0:T(8,128)(2,1)S(1)} %copy-done.1), custom_call_target="tpu_custom_call" | custom-call | tf_op jit(solution)/shard_map/pallas_call | solution.py:16
  48.8 2.5 %collective-permute-done.21 = bf16[432,128]{1,0:T(8,128)(2,1)S(1)} collective-permute-done((bf16[432,128]{1,0:T(8,128)(2,1)S(1)}, bf16[432,128]{1,0:T(8,128)(2,1)S(1)}, u32[]{:S(2)}, u32[]{:S(2)}) %collective-permute-start.21) | collective-permute-done | bytes 110624 | tf_op jit(solution)/shard_map/ppermute | solution.py:215
  51.4 1.7 %collective-permute-start.27 = (bf16[688,128]{1,0:T(8,128)(2,1)S(1)}, bf16[688,128]{1,0:T(8,128)(2,1)S(1)}, u32[]{:S(2)}, u32[]{:S(2)}) collective-permute-start(bf16[688,128]{1,0:T(8,128)(2,1)S(1)} %pad_maximum_fusion.refs_0_), channel_id=1, source_target_pairs={{0,6},{1,7},{2,4},{3,5},{4,2},{5,3},{6,0},{7,1},{8,14},{9,15},{10,... | collective-permute-start | bytes 528392 | tf_op jit(solution)/shard_map/ppermute | solution.py:225
  53.1 1.3 %collective-permute-start.25 = (bf16[688,128]{1,0:T(8,128)(2,1)S(1)}, bf16[688,128]{1,0:T(8,128)(2,1)S(1)}, u32[]{:S(2)}, u32[]{:S(2)}) collective-permute-start(bf16[688,128]{1,0:T(8,128)(2,1)S(1)} %pad_maximum_fusion.refs_0_), channel_id=1, source_target_pairs={{0,4},{4,0},{8,12},{12,8},{16,20},{20,16},{24,28},{28,24},{1,5},{5... | collective-permute-start | bytes 528392 | tf_op jit(solution)/shard_map/ppermute | solution.py:215
  54.4 0.5 collective-permute-start.23
  54.9 3.0 %collective-permute-done.27.refs_6_ = bf16[688,128]{1,0:T(8,128)(2,1)S(1)} collective-permute-done((bf16[688,128]{1,0:T(8,128)(2,1)S(1)}, bf16[688,128]{1,0:T(8,128)(2,1)S(1)}, u32[]{:S(2)}, u32[]{:S(2)}) %collective-permute-start.27) | collective-permute-done | bytes 176160 | tf_op jit(solution)/shard_map/ppermute | solution.py:225
  57.9 0.0 collective-permute-start.28
  57.9 1.8 %collective-permute-done.25.refs_4_ = bf16[688,128]{1,0:T(8,128)(2,1)S(1)} collective-permute-done((bf16[688,128]{1,0:T(8,128)(2,1)S(1)}, bf16[688,128]{1,0:T(8,128)(2,1)S(1)}, u32[]{:S(2)}, u32[]{:S(2)}) %collective-permute-start.25) | collective-permute-done | bytes 176160 | tf_op jit(solution)/shard_map/ppermute | solution.py:215
  59.7 0.0 collective-permute-start.26
  59.7 0.2 collective-permute-done.23.refs_2_
  59.9 0.3 collective-permute-start.24
  60.2 0.0 collective-permute-done.22.refs_1_
  60.2 0.9 %collective-permute-done.26.refs_5_ = bf16[688,128]{1,0:T(8,128)(2,1)S(1)} collective-permute-done((bf16[688,128]{1,0:T(8,128)(2,1)S(1)}, bf16[688,128]{1,0:T(8,128)(2,1)S(1)}, u32[]{:S(2)}, u32[]{:S(2)}) %collective-permute-start.26) | collective-permute-done | bytes 176160 | tf_op jit(solution)/shard_map/ppermute | solution.py:215
  61.1 0.3 collective-permute-done.24.refs_3_
  61.3 1.3 %shard_map.90 = (bf16[27,4,2,16,128]{4,3,2,1,0:T(8,128)(2,1)}, bf16[2,4,128,256]{3,2,1,0:T(8,128)(2,1)}) custom-call(bf16[688,128]{1,0:T(8,128)(2,1)S(1)} %pad_maximum_fusion.refs_0_, bf16[688,128]{1,0:T(8,128)(2,1)S(1)} %collective-permute-done.22.refs_1_, bf16[688,128]{1,0:T(8,128)(2,1)S(1)} %collective-permute-done.23.refs_2_, ...), custom_call_target="tpu_custom_call" | custom-call | tf_op jit(solution)/shard_map/pallas_call | solution.py:16
  (25 shorter events, 0.3 us)
Async XLA Ops:
  0.6 8.9 %copy-start = (bf16[2,2,2,128,256]{4,3,2,1,0:T(8,128)(2,1)S(1)}, bf16[2,2,2,128,256]{4,3,2,1,0:T(8,128)(2,1)}, u32[]{:S(2)}) copy-start(bf16[2,2,2,128,256]{4,3,2,1,0:T(8,128)(2,1)} %param.9) | copy-start | bytes 1572868
  0.6 1.0 %copy-start.2 = (bf16[4,4,32,32]{3,2,1,0:T(8,128)(2,1)S(1)}, bf16[4,4,32,32]{3,2,1,0:T(8,128)(2,1)}, u32[]{:S(2)}) copy-start(bf16[4,4,32,32]{3,2,1,0:T(8,128)(2,1)} %param.11) | copy-start | bytes 98308
  1.6 4.2 %copy-start.3 = (bf16[1,8,64,128]{3,2,1,0:T(8,128)(2,1)S(1)}, bf16[1,8,64,128]{3,2,1,0:T(8,128)(2,1)}, u32[]{:S(2)}) copy-start(bf16[1,8,64,128]{3,2,1,0:T(8,128)(2,1)} %param.6) | copy-start | bytes 393220
  1.7 6.2 %collective-permute-start.4 = (bf16[2,32,128]{2,1,0:T(8,128)(2,1)S(1)}, bf16[2,32,128]{2,1,0:T(8,128)(2,1)S(1)}, u32[]{:S(2)}, u32[]{:S(2)}) collective-permute-start(bf16[2,32,128]{2,1,0:T(8,128)(2,1)S(1)} %get-tuple-element.44), channel_id=1, source_target_pairs={{0,16},{4,20},{8,24},{12,28},{16,0},{20,4},{24,8},{28,12},{1,17},{... | collective-permute-start | bytes 49160 | tf_op jit(solution)/shard_map/ppermute | solution.py:215
  5.9 7.3 %collective-permute-start = (bf16[32,512]{1,0:T(8,128)(2,1)S(1)}, bf16[32,512]{1,0:T(8,128)(2,1)S(1)}, u32[]{:S(2)}, u32[]{:S(2)}) collective-permute-start(bf16[32,512]{1,0:T(8,128)(2,1)S(1)} %get-tuple-element.40), channel_id=1, source_target_pairs={{0,1},{1,0},{2,3},{3,2},{4,5},{5,4},{6,7},{7,6},{8,9},{9,8},{10,11... | collective-permute-start | bytes 98312 | tf_op jit(solution)/shard_map/ppermute | solution.py:215
  6.0 7.2 %collective-permute-start.1 = (bf16[32,512]{1,0:T(8,128)(2,1)S(1)}, bf16[32,512]{1,0:T(8,128)(2,1)S(1)}, u32[]{:S(2)}, u32[]{:S(2)}) collective-permute-start(bf16[32,512]{1,0:T(8,128)(2,1)S(1)} %get-tuple-element.41), channel_id=1, source_target_pairs={{0,2},{1,3},{2,0},{3,1},{4,6},{5,7},{6,4},{7,5},{8,10},{9,11},{10,... | collective-permute-start | bytes 98312 | tf_op jit(solution)/shard_map/ppermute | solution.py:215
  7.6 5.7 %collective-permute-start.2 = (bf16[32,512]{1,0:T(8,128)(2,1)S(1)}, bf16[32,512]{1,0:T(8,128)(2,1)S(1)}, u32[]{:S(2)}, u32[]{:S(2)}) collective-permute-start(bf16[32,512]{1,0:T(8,128)(2,1)S(1)} %get-tuple-element.42), channel_id=1, source_target_pairs={{0,3},{1,2},{2,1},{3,0},{4,7},{5,6},{6,5},{7,4},{8,11},{9,10},{10,... | collective-permute-start | bytes 98312 | tf_op jit(solution)/shard_map/ppermute | solution.py:215
  7.9 3.8 %collective-permute-start.5 = (bf16[1,2,32,128]{3,2,1,0:T(8,128)(2,1)S(1)}, bf16[1,2,32,128]{3,2,1,0:T(8,128)(2,1)S(1)}, u32[]{:S(2)}, u32[]{:S(2)}) collective-permute-start(bf16[1,2,32,128]{3,2,1,0:T(8,128)(2,1)S(1)} %get-tuple-element.78), channel_id=1, source_target_pairs={{0,8},{4,12},{8,0},{12,4},{16,24},{20,28},{24,16},{28,20},{1,9},{5... | collective-permute-start | bytes 49160 | tf_op jit(solution)/shard_map/ppermute | solution.py:215
  11.7 3.9 %collective-permute-start.6 = (bf16[4,32,128]{2,1,0:T(8,128)(2,1)S(1)}, bf16[4,32,128]{2,1,0:T(8,128)(2,1)S(1)}, u32[]{:S(2)}, u32[]{:S(2)}) collective-permute-start(bf16[4,32,128]{2,1,0:T(8,128)(2,1)S(1)} %maximum_bitcast_fusion.refs_3_), channel_id=1, source_target_pairs={{0,4},{4,0},{8,12},{12,8},{16,20},{20,16},{24,28},{28,24},{1,5},{5... | collective-permute-start | bytes 98312 | tf_op jit(solution)/shard_map/ppermute | solution.py:215
  13.2 2.4 %copy-start.4 = (bf16[1,8,64,128]{3,2,1,0:T(8,128)(2,1)S(1)}, bf16[1,8,64,128]{3,2,1,0:T(8,128)(2,1)}, u32[]{:S(2)}) copy-start(bf16[1,8,64,128]{3,2,1,0:T(8,128)(2,1)} %param.7) | copy-start | bytes 393220
  13.2 2.4 %copy-start.5 = (bf16[1,8,64,128]{3,2,1,0:T(8,128)(2,1)S(1)}, bf16[1,8,64,128]{3,2,1,0:T(8,128)(2,1)}, u32[]{:S(2)}) copy-start(bf16[1,8,64,128]{3,2,1,0:T(8,128)(2,1)} %param.10) | copy-start | bytes 393220
  16.2 3.5 %collective-permute-start.7 = (bf16[512,128]{1,0:T(8,128)(2,1)S(1)}, bf16[512,128]{1,0:T(8,128)(2,1)S(1)}, u32[]{:S(2)}, u32[]{:S(2)}) collective-permute-start(bf16[512,128]{1,0:T(8,128)(2,1)S(1)} %get-tuple-element.51.refs_3_), channel_id=1, source_target_pairs={{0,1},{1,0},{2,3},{3,2},{4,5},{5,4},{6,7},{7,6},{8,9},{9,8},{10,11... | collective-permute-start | bytes 393224 | tf_op jit(solution)/shard_map/ppermute | solution.py:215
  16.3 5.9 %collective-permute-start.3 = (bf16[4,32,512]{2,1,0:T(8,128)(2,1)S(1)}, bf16[4,32,512]{2,1,0:T(8,128)(2,1)S(1)}, u32[]{:S(2)}, u32[]{:S(2)}) collective-permute-start(bf16[4,32,512]{2,1,0:T(8,128)(2,1)S(1)} %pad_maximum_fusion.2.refs_1_), channel_id=1, source_target_pairs={{0,4},{4,0},{8,12},{12,8},{16,20},{20,16},{24,28},{28,24},{1,5},{5... | collective-permute-start | bytes 393224 | tf_op jit(solution)/shard_map/ppermute | solution.py:215
  17.9 5.8 %collective-permute-start.10 = (bf16[512,128]{1,0:T(8,128)(2,1)S(1)}, bf16[512,128]{1,0:T(8,128)(2,1)S(1)}, u32[]{:S(2)}, u32[]{:S(2)}) collective-permute-start(bf16[512,128]{1,0:T(8,128)(2,1)S(1)} %get-tuple-element.51.refs_3_), channel_id=1, source_target_pairs={{0,3},{1,2},{2,1},{3,0},{4,7},{5,6},{6,5},{7,4},{8,11},{9,10},{10,... | collective-permute-start | bytes 393224 | tf_op jit(solution)/shard_map/ppermute | solution.py:215
  19.2 7.7 %collective-permute-start.9 = (bf16[512,128]{1,0:T(8,128)(2,1)S(1)}, bf16[512,128]{1,0:T(8,128)(2,1)S(1)}, u32[]{:S(2)}, u32[]{:S(2)}) collective-permute-start(bf16[512,128]{1,0:T(8,128)(2,1)S(1)} %get-tuple-element.51.refs_3_), channel_id=1, source_target_pairs={{0,2},{1,3},{2,0},{3,1},{4,6},{5,7},{6,4},{7,5},{8,10},{9,11},{10,... | collective-permute-start | bytes 393224 | tf_op jit(solution)/shard_map/ppermute | solution.py:215
  19.7 7.1 %collective-permute-start.8 = (bf16[4,32,512]{2,1,0:T(8,128)(2,1)S(1)}, bf16[4,32,512]{2,1,0:T(8,128)(2,1)S(1)}, u32[]{:S(2)}, u32[]{:S(2)}) collective-permute-start(bf16[4,32,512]{2,1,0:T(8,128)(2,1)S(1)} %pad_maximum_fusion.2.refs_1_), channel_id=1, source_target_pairs={{4,8},{8,4},{12,16},{16,12},{20,24},{24,20},{5,9},{9,5},{13,17},{1... | collective-permute-start | bytes 393224 | tf_op jit(solution)/shard_map/ppermute | solution.py:235
  22.2 7.8 %collective-permute-start.12 = (bf16[256,128]{1,0:T(8,128)(2,1)S(1)}, bf16[256,128]{1,0:T(8,128)(2,1)S(1)}, u32[]{:S(2)}, u32[]{:S(2)}) collective-permute-start(bf16[256,128]{1,0:T(8,128)(2,1)S(1)} %get-tuple-element.58), channel_id=1, source_target_pairs={{0,1},{1,0},{2,3},{3,2},{4,5},{5,4},{6,7},{7,6},{8,9},{9,8},{10,11... | collective-permute-start | bytes 196616 | tf_op jit(solution)/shard_map/ppermute | solution.py:215
  22.2 7.8 %collective-permute-start.13 = (bf16[256,128]{1,0:T(8,128)(2,1)S(1)}, bf16[256,128]{1,0:T(8,128)(2,1)S(1)}, u32[]{:S(2)}, u32[]{:S(2)}) collective-permute-start(bf16[256,128]{1,0:T(8,128)(2,1)S(1)} %get-tuple-element.59), channel_id=1, source_target_pairs={{0,2},{1,3},{2,0},{3,1},{4,6},{5,7},{6,4},{7,5},{8,10},{9,11},{10,... | collective-permute-start | bytes 196616 | tf_op jit(solution)/shard_map/ppermute | solution.py:215
  23.7 6.3 %collective-permute-start.14 = (bf16[256,128]{1,0:T(8,128)(2,1)S(1)}, bf16[256,128]{1,0:T(8,128)(2,1)S(1)}, u32[]{:S(2)}, u32[]{:S(2)}) collective-permute-start(bf16[256,128]{1,0:T(8,128)(2,1)S(1)} %get-tuple-element.60), channel_id=1, source_target_pairs={{0,3},{1,2},{2,1},{3,0},{4,7},{5,6},{6,5},{7,4},{8,11},{9,10},{10,... | collective-permute-start | bytes 196616 | tf_op jit(solution)/shard_map/ppermute | solution.py:215
  28.4 7.0 %collective-permute-start.11 = (bf16[432,128]{1,0:T(8,128)(2,1)S(1)}, bf16[432,128]{1,0:T(8,128)(2,1)S(1)}, u32[]{:S(2)}, u32[]{:S(2)}) collective-permute-start(bf16[432,128]{1,0:T(8,128)(2,1)S(1)} %get-tuple-element.56), channel_id=1, source_target_pairs={{0,4},{4,0},{8,12},{12,8},{16,20},{20,16},{24,28},{28,24},{1,5},{5... | collective-permute-start | bytes 331784 | tf_op jit(solution)/shard_map/ppermute | solution.py:215
  30.1 5.2 %collective-permute-start.15 = (bf16[256,128]{1,0:T(8,128)(2,1)S(1)}, bf16[256,128]{1,0:T(8,128)(2,1)S(1)}, u32[]{:S(2)}, u32[]{:S(2)}) collective-permute-start(bf16[256,128]{1,0:T(8,128)(2,1)S(1)} %add_convert_fusion.3), channel_id=1, source_target_pairs={{0,16},{4,20},{8,24},{12,28},{16,0},{20,4},{24,8},{28,12},{1,17},{... | collective-permute-start | bytes 196616 | tf_op jit(solution)/shard_map/ppermute | solution.py:215
  32.7 9.9 %collective-permute-start.18 = (bf16[10,64,128]{2,1,0:T(8,128)(2,1)S(1)}, bf16[10,64,128]{2,1,0:T(8,128)(2,1)S(1)}, u32[]{:S(2)}, u32[]{:S(2)}) collective-permute-start(bf16[10,64,128]{2,1,0:T(8,128)(2,1)S(1)} %get-tuple-element.65.own), channel_id=1, source_target_pairs={{4,8},{8,4},{12,16},{16,12},{20,24},{24,20},{5,9},{9,5},{13,17},{1... | collective-permute-start | bytes 491528 | tf_op jit(solution)/shard_map/ppermute | solution.py:235
  35.3 11.7 %copy-start.1 = (bf16[3,3,3,128,128]{4,3,2,1,0:T(8,128)(2,1)S(1)}, bf16[3,3,3,128,128]{4,3,2,1,0:T(8,128)(2,1)}, u32[]{:S(2)}) copy-start(bf16[3,3,3,128,128]{4,3,2,1,0:T(8,128)(2,1)} %weight.1) | copy-start | bytes 2654212
  35.4 11.0 %collective-permute-start.16 = (bf16[432,128]{1,0:T(8,128)(2,1)S(1)}, bf16[432,128]{1,0:T(8,128)(2,1)S(1)}, u32[]{:S(2)}, u32[]{:S(2)}) collective-permute-start(bf16[432,128]{1,0:T(8,128)(2,1)S(1)} %add_convert_fusion.1), channel_id=1, source_target_pairs={{0,16},{4,20},{8,24},{12,28},{16,0},{20,4},{24,8},{28,12},{1,17},{... | collective-permute-start | bytes 331784 | tf_op jit(solution)/shard_map/ppermute | solution.py:215
  38.8 7.6 %collective-permute-start.20 = (bf16[5,64,128]{2,1,0:T(8,128)(2,1)S(1)}, bf16[5,64,128]{2,1,0:T(8,128)(2,1)S(1)}, u32[]{:S(2)}, u32[]{:S(2)}) collective-permute-start(bf16[5,64,128]{2,1,0:T(8,128)(2,1)S(1)} %get-tuple-element.75), channel_id=1, source_target_pairs={{0,4},{4,0},{8,12},{12,8},{16,20},{20,16},{24,28},{28,24},{1,5},{5... | collective-permute-start | bytes 245768 | tf_op jit(solution)/shard_map/ppermute | solution.py:215
  39.6 6.8 %collective-permute-start.19 = (bf16[5,64,128]{2,1,0:T(8,128)(2,1)S(1)}, bf16[5,64,128]{2,1,0:T(8,128)(2,1)S(1)}, u32[]{:S(2)}, u32[]{:S(2)}) collective-permute-start(bf16[5,64,128]{2,1,0:T(8,128)(2,1)S(1)} %get-tuple-element.76), channel_id=1, source_target_pairs={{0,4},{4,0},{8,12},{12,8},{16,20},{20,16},{24,28},{28,24},{1,5},{5... | collective-permute-start | bytes 245768 | tf_op jit(solution)/shard_map/ppermute | solution.py:215
  40.9 5.5 %collective-permute-start.17 = (bf16[256,128]{1,0:T(8,128)(2,1)S(1)}, bf16[256,128]{1,0:T(8,128)(2,1)S(1)}, u32[]{:S(2)}, u32[]{:S(2)}) collective-permute-start(bf16[256,128]{1,0:T(8,128)(2,1)S(1)} %add_convert_fusion.2), channel_id=1, source_target_pairs={{0,8},{4,12},{8,0},{12,4},{16,24},{20,28},{24,16},{28,20},{1,9},{5... | collective-permute-start | bytes 196616 | tf_op jit(solution)/shard_map/ppermute | solution.py:215
  46.5 4.8 %collective-permute-start.21 = (bf16[432,128]{1,0:T(8,128)(2,1)S(1)}, bf16[432,128]{1,0:T(8,128)(2,1)S(1)}, u32[]{:S(2)}, u32[]{:S(2)}) collective-permute-start(bf16[432,128]{1,0:T(8,128)(2,1)S(1)} %add_convert_fusion), channel_id=1, source_target_pairs={{0,8},{4,12},{8,0},{12,4},{16,24},{20,28},{24,16},{28,20},{1,9},{5... | collective-permute-start | bytes 331784 | tf_op jit(solution)/shard_map/ppermute | solution.py:215
  51.4 6.5 %collective-permute-start.27 = (bf16[688,128]{1,0:T(8,128)(2,1)S(1)}, bf16[688,128]{1,0:T(8,128)(2,1)S(1)}, u32[]{:S(2)}, u32[]{:S(2)}) collective-permute-start(bf16[688,128]{1,0:T(8,128)(2,1)S(1)} %pad_maximum_fusion.refs_0_), channel_id=1, source_target_pairs={{0,6},{1,7},{2,4},{3,5},{4,2},{5,3},{6,0},{7,1},{8,14},{9,15},{10,... | collective-permute-start | bytes 528392 | tf_op jit(solution)/shard_map/ppermute | solution.py:225
  53.1 6.6 %collective-permute-start.25 = (bf16[688,128]{1,0:T(8,128)(2,1)S(1)}, bf16[688,128]{1,0:T(8,128)(2,1)S(1)}, u32[]{:S(2)}, u32[]{:S(2)}) collective-permute-start(bf16[688,128]{1,0:T(8,128)(2,1)S(1)} %pad_maximum_fusion.refs_0_), channel_id=1, source_target_pairs={{0,4},{4,0},{8,12},{12,8},{16,20},{20,16},{24,28},{28,24},{1,5},{5... | collective-permute-start | bytes 528392 | tf_op jit(solution)/shard_map/ppermute | solution.py:215
  54.4 5.5 %collective-permute-start.23 = (bf16[688,128]{1,0:T(8,128)(2,1)S(1)}, bf16[688,128]{1,0:T(8,128)(2,1)S(1)}, u32[]{:S(2)}, u32[]{:S(2)}) collective-permute-start(bf16[688,128]{1,0:T(8,128)(2,1)S(1)} %pad_maximum_fusion.refs_0_), channel_id=1, source_target_pairs={{0,2},{1,3},{2,0},{3,1},{4,6},{5,7},{6,4},{7,5},{8,10},{9,11},{10,... | collective-permute-start | bytes 528392 | tf_op jit(solution)/shard_map/ppermute | solution.py:215
  54.9 5.3 %collective-permute-start.22 = (bf16[688,128]{1,0:T(8,128)(2,1)S(1)}, bf16[688,128]{1,0:T(8,128)(2,1)S(1)}, u32[]{:S(2)}, u32[]{:S(2)}) collective-permute-start(bf16[688,128]{1,0:T(8,128)(2,1)S(1)} %pad_maximum_fusion.refs_0_), channel_id=1, source_target_pairs={{0,1},{1,0},{2,3},{3,2},{4,5},{5,4},{6,7},{7,6},{8,9},{9,8},{10,11... | collective-permute-start | bytes 528392 | tf_op jit(solution)/shard_map/ppermute | solution.py:215
  57.9 2.3 %collective-permute-start.28 = (bf16[688,128]{1,0:T(8,128)(2,1)S(1)}, bf16[688,128]{1,0:T(8,128)(2,1)S(1)}, u32[]{:S(2)}, u32[]{:S(2)}) collective-permute-start(bf16[688,128]{1,0:T(8,128)(2,1)S(1)} %collective-permute-done.27.refs_6_), channel_id=1, source_target_pairs={{0,1},{1,0},{2,3},{3,2},{4,5},{5,4},{6,7},{7,6},{8,9},{9,8},{10,11... | collective-permute-start | bytes 528392 | tf_op jit(solution)/shard_map/ppermute | solution.py:215
  59.7 1.4 %collective-permute-start.26 = (bf16[688,128]{1,0:T(8,128)(2,1)S(1)}, bf16[688,128]{1,0:T(8,128)(2,1)S(1)}, u32[]{:S(2)}, u32[]{:S(2)}) collective-permute-start(bf16[688,128]{1,0:T(8,128)(2,1)S(1)} %collective-permute-done.25.refs_4_), channel_id=1, source_target_pairs={{0,1},{1,0},{2,3},{3,2},{4,5},{5,4},{6,7},{7,6},{8,9},{9,8},{10,11... | collective-permute-start | bytes 528392 | tf_op jit(solution)/shard_map/ppermute | solution.py:215
  59.9 1.5 %collective-permute-start.24 = (bf16[688,128]{1,0:T(8,128)(2,1)S(1)}, bf16[688,128]{1,0:T(8,128)(2,1)S(1)}, u32[]{:S(2)}, u32[]{:S(2)}) collective-permute-start(bf16[688,128]{1,0:T(8,128)(2,1)S(1)} %collective-permute-done.23.refs_2_), channel_id=1, source_target_pairs={{0,1},{1,0},{2,3},{3,2},{4,5},{5,4},{6,7},{7,6},{8,9},{9,8},{10,11... | collective-permute-start | bytes 528392 | tf_op jit(solution)/shard_map/ppermute | solution.py:215

commit v21 on v20

--- a/solution.py
+++ b/solution.py
@@ -344,7 +344,6 @@
     for index, code in enumerate(codes):
         down_other = swapped(down, "gz", code)
         if index == 0:
-            send, down_other = lax.optimization_barrier((send, down_other))
             conv = (keep + send.astype(F32)).astype(wire)
             conv, late = lax.optimization_barrier((conv, near))
             cut = late.shape[0] // 2

time: 62.8 us -> 62.8 us (level)
    ppermute x1, starting transfers between devices: 1.71 us -> 0.07 us  [crossed(): return lax.ppermute(value, ('gz', 'gy'), pairs)]
    ppermute x26, starting transfers between devices: 29.5 us -> 31 us  [swapped(): lax.ppermute(value, axis, [(i, i ^ code) for i in range(lax.axis_size(axi...]
  transfers between devices with their start and end apart: 29 -> 29, of which waited for: 12 -> 11; matrix products, arithmetic and copies ran while one was open for 0% -> 0% of each run, Pallas kernels for 5% -> 5%
where the time goes in v21:
time: 62.8 us; the launch traced here: 62.6 us
  starting transfers between devices  32.4 us (52%)
  waiting for transfers between devices  22.7 us (36%)
  Pallas kernels  5.35 us (9%)
  local copies, waits for them, and re-layouts  1.02 us (2%)
  between operations  0.89 us (1%)
    ppermute x26, starting transfers between devices, swapped(): lax.ppermute(value, axis, [(i, i ^ code) for i in range(lax.axis_size(axi...  31 us
    ppermute x26, waiting for transfers between devices, swapped(): lax.ppermute(value, axis, [(i, i ^ code) for i in range(lax.axis_size(axi...  19.7 us
    pallas_call x6, Pallas kernels, call(): pl.pallas_call(kernel, out_shape=out_shape, scratch_shapes=list(scratch),...  5.35 us
    ppermute x1, waiting for transfers between devices, crossed(): return lax.ppermute(value, ('gz', 'gy'), pairs)  2.96 us
    ppermute x2, starting transfers between devices, odd_pairs(): return lax.ppermute(value, 'gz', pairs)  1.32 us
  transfers between devices with their start and end apart: 29, of which 11 were waited for; matrix products, arithmetic and copies ran while one was open for 0% of the time, Pallas kernels for 5%

profile of v21, /device:TPU:0, one launch (start us, length us, event | category | flops | bytes accessed | tf_op | source)
XLA Modules:
  0.0 62.6 jit_solution(9486888477831274341)
XLA Ops:
  0.6 0.0 copy-start
  0.7 1.0 %copy-done.2 = bf16[4,4,32,32]{3,2,1,0:T(8,128)(2,1)S(1)} copy-done((bf16[4,4,32,32]{3,2,1,0:T(8,128)(2,1)S(1)}, bf16[4,4,32,32]{3,2,1,0:T(8,128)(2,1)}, u32[]{:S(2)}) %copy-start.2) | copy-done | bytes 32792
  1.6 0.1 shard_map.86
  1.7 4.1 %collective-permute-start.4 = (bf16[2,32,128]{2,1,0:T(8,128)(2,1)S(1)}, bf16[2,32,128]{2,1,0:T(8,128)(2,1)S(1)}, u32[]{:S(2)}, u32[]{:S(2)}) collective-permute-start(bf16[2,32,128]{2,1,0:T(8,128)(2,1)S(1)} %get-tuple-element.42), channel_id=1, source_target_pairs={{0,16},{4,20},{8,24},{12,28},{16,0},{20,4},{24,8},{28,12},{1,17},{... | collective-permute-start | bytes 49160 | tf_op jit(solution)/shard_map/ppermute | solution.py:215
  5.8 0.1 shard_map.85
  5.9 0.1 collective-permute-start
  6.0 1.6 %collective-permute-start.1 = (bf16[32,512]{1,0:T(8,128)(2,1)S(1)}, bf16[32,512]{1,0:T(8,128)(2,1)S(1)}, u32[]{:S(2)}, u32[]{:S(2)}) collective-permute-start(bf16[32,512]{1,0:T(8,128)(2,1)S(1)} %get-tuple-element.39), channel_id=1, source_target_pairs={{0,2},{1,3},{2,0},{3,1},{4,6},{5,7},{6,4},{7,5},{8,10},{9,11},{10,... | collective-permute-start | bytes 98312 | tf_op jit(solution)/shard_map/ppermute | solution.py:215
  7.6 0.3 collective-permute-start.2
  7.9 0.0 collective-permute-done.4
  7.9 1.6 %collective-permute-start.5 = (bf16[1,2,32,128]{3,2,1,0:T(8,128)(2,1)S(1)}, bf16[1,2,32,128]{3,2,1,0:T(8,128)(2,1)S(1)}, u32[]{:S(2)}, u32[]{:S(2)}) collective-permute-start(bf16[1,2,32,128]{3,2,1,0:T(8,128)(2,1)S(1)} %get-tuple-element.74), channel_id=1, source_target_pairs={{0,8},{4,12},{8,0},{12,4},{16,24},{20,28},{24,16},{28,20},{1,9},{5... | collective-permute-start | bytes 49160 | tf_op jit(solution)/shard_map/ppermute | solution.py:215
  9.5 2.1 %collective-permute-done.5 = bf16[1,2,32,128]{3,2,1,0:T(8,128)(2,1)S(1)} collective-permute-done((bf16[1,2,32,128]{3,2,1,0:T(8,128)(2,1)S(1)}, bf16[1,2,32,128]{3,2,1,0:T(8,128)(2,1)S(1)}, u32[]{:S(2)}, u32[]{:S(2)}) %collective-permute-start.5) | collective-permute-done | bytes 16416 | tf_op jit(solution)/shard_map/ppermute | solution.py:215
  11.7 1.5 %collective-permute-start.6 = (bf16[4,32,128]{2,1,0:T(8,128)(2,1)S(1)}, bf16[4,32,128]{2,1,0:T(8,128)(2,1)S(1)}, u32[]{:S(2)}, u32[]{:S(2)}) collective-permute-start(bf16[4,32,128]{2,1,0:T(8,128)(2,1)S(1)} %maximum_bitcast_fusion.refs_3_), channel_id=1, source_target_pairs={{0,4},{4,0},{8,12},{12,8},{16,20},{20,16},{24,28},{28,24},{1,5},{5... | collective-permute-start | bytes 98312 | tf_op jit(solution)/shard_map/ppermute | solution.py:215
  13.2 0.0 collective-permute-done
  13.2 0.0 collective-permute-done.1
  13.2 0.0 collective-permute-done.2
  13.2 0.0 copy-start.4
  13.2 0.0 copy-start.5
  13.3 2.3 %collective-permute-done.6.refs_4_ = bf16[4,32,128]{2,1,0:T(8,128)(2,1)S(1)} collective-permute-done((bf16[4,32,128]{2,1,0:T(8,128)(2,1)S(1)}, bf16[4,32,128]{2,1,0:T(8,128)(2,1)S(1)}, u32[]{:S(2)}, u32[]{:S(2)}) %collective-permute-start.6) | collective-permute-done | bytes 32800 | tf_op jit(solution)/shard_map/ppermute | solution.py:215
  15.6 0.6 shard_map.87
  16.2 0.1 collective-permute-start.7
  16.3 1.6 %collective-permute-start.3 = (bf16[4,32,512]{2,1,0:T(8,128)(2,1)S(1)}, bf16[4,32,512]{2,1,0:T(8,128)(2,1)S(1)}, u32[]{:S(2)}, u32[]{:S(2)}) collective-permute-start(bf16[4,32,512]{2,1,0:T(8,128)(2,1)S(1)} %pad_maximum_fusion.2.refs_1_), channel_id=1, source_target_pairs={{0,4},{4,0},{8,12},{12,8},{16,20},{20,16},{24,28},{28,24},{1,5},{5... | collective-permute-start | bytes 393224 | tf_op jit(solution)/shard_map/ppermute | solution.py:215
  17.9 1.3 %collective-permute-start.10 = (bf16[512,128]{1,0:T(8,128)(2,1)S(1)}, bf16[512,128]{1,0:T(8,128)(2,1)S(1)}, u32[]{:S(2)}, u32[]{:S(2)}) collective-permute-start(bf16[512,128]{1,0:T(8,128)(2,1)S(1)} %get-tuple-element.49.refs_3_), channel_id=1, source_target_pairs={{0,3},{1,2},{2,1},{3,0},{4,7},{5,6},{6,5},{7,4},{8,11},{9,10},{10,... | collective-permute-start | bytes 393224 | tf_op jit(solution)/shard_map/ppermute | solution.py:215
  19.2 0.5 collective-permute-start.9
  19.7 0.0 collective-permute-done.7.refs_4_
  19.7 0.7 %collective-permute-start.8 = (bf16[4,32,512]{2,1,0:T(8,128)(2,1)S(1)}, bf16[4,32,512]{2,1,0:T(8,128)(2,1)S(1)}, u32[]{:S(2)}, u32[]{:S(2)}) collective-permute-start(bf16[4,32,512]{2,1,0:T(8,128)(2,1)S(1)} %pad_maximum_fusion.2.refs_1_), channel_id=1, source_target_pairs={{4,8},{8,4},{12,16},{16,12},{20,24},{24,20},{5,9},{9,5},{13,17},{1... | collective-permute-start | bytes 393224 | tf_op jit(solution)/shard_map/ppermute | solution.py:235
  20.4 1.9 %collective-permute-done.3.refs_0_ = bf16[4,32,512]{2,1,0:T(8,128)(2,1)S(1)} collective-permute-done((bf16[4,32,512]{2,1,0:T(8,128)(2,1)S(1)}, bf16[4,32,512]{2,1,0:T(8,128)(2,1)S(1)}, u32[]{:S(2)}, u32[]{:S(2)}) %collective-permute-start.3) | collective-permute-done | bytes 131104 | tf_op jit(solution)/shard_map/ppermute | solution.py:215
  22.2 0.0 collective-permute-start.13
  22.2 1.5 %collective-permute-start.14 = (bf16[256,128]{1,0:T(8,128)(2,1)S(1)}, bf16[256,128]{1,0:T(8,128)(2,1)S(1)}, u32[]{:S(2)}, u32[]{:S(2)}) collective-permute-start(bf16[256,128]{1,0:T(8,128)(2,1)S(1)} %get-tuple-element.59), channel_id=1, source_target_pairs={{0,2},{1,3},{2,0},{3,1},{4,6},{5,7},{6,4},{7,5},{8,10},{9,11},{10,... | collective-permute-start | bytes 196616 | tf_op jit(solution)/shard_map/ppermute | solution.py:215
  23.7 0.0 collective-permute-done.10.refs_6_
  23.7 1.2 %collective-permute-start.15 = (bf16[256,128]{1,0:T(8,128)(2,1)S(1)}, bf16[256,128]{1,0:T(8,128)(2,1)S(1)}, u32[]{:S(2)}, u32[]{:S(2)}) collective-permute-start(bf16[256,128]{1,0:T(8,128)(2,1)S(1)} %get-tuple-element.60), channel_id=1, source_target_pairs={{0,3},{1,2},{2,1},{3,0},{4,7},{5,6},{6,5},{7,4},{8,11},{9,10},{10,... | collective-permute-start | bytes 196616 | tf_op jit(solution)/shard_map/ppermute | solution.py:215
  25.0 1.9 %collective-permute-done.9.refs_5_ = bf16[512,128]{1,0:T(8,128)(2,1)S(1)} collective-permute-done((bf16[512,128]{1,0:T(8,128)(2,1)S(1)}, bf16[512,128]{1,0:T(8,128)(2,1)S(1)}, u32[]{:S(2)}, u32[]{:S(2)}) %collective-permute-start.9) | collective-permute-done | bytes 131104 | tf_op jit(solution)/shard_map/ppermute | solution.py:215
  26.8 1.5 %shard_map.88 = (f32[432,128]{1,0:T(8,128)S(1)}, bf16[432,128]{1,0:T(8,128)(2,1)S(1)}, bf16[10,64,128]{2,1,0:T(8,128)(2,1)S(1)}) custom-call(bf16[4,32,512]{2,1,0:T(8,128)(2,1)S(1)} %collective-permute-done.3.refs_0_, bf16[4,32,512]{2,1,0:T(8,128)(2,1)S(1)} %pad_maximum_fusion.2.refs_1_, bf16[4,32,512]{2,1,0:T(8,128)(2,1)S(1)} %collective-permute-done.8.refs_2_, ...), custom_call_target="tpu_custom_call" | custom-call | tf_op jit(solution)/shard_map/pallas_call | solution.py:16
  28.4 1.7 %collective-permute-start.11 = (bf16[432,128]{1,0:T(8,128)(2,1)S(1)}, bf16[432,128]{1,0:T(8,128)(2,1)S(1)}, u32[]{:S(2)}, u32[]{:S(2)}) collective-permute-start(bf16[432,128]{1,0:T(8,128)(2,1)S(1)} %get-tuple-element.54), channel_id=1, source_target_pairs={{0,4},{4,0},{8,12},{12,8},{16,20},{20,16},{24,28},{28,24},{1,5},{5... | collective-permute-start | bytes 331784 | tf_op jit(solution)/shard_map/ppermute | solution.py:215
  30.0 0.0 collective-permute-done.14
  30.0 0.0 collective-permute-done.15
  30.1 2.6 %collective-permute-start.16 = (bf16[256,128]{1,0:T(8,128)(2,1)S(1)}, bf16[256,128]{1,0:T(8,128)(2,1)S(1)}, u32[]{:S(2)}, u32[]{:S(2)}) collective-permute-start(bf16[256,128]{1,0:T(8,128)(2,1)S(1)} %add_convert_fusion.3), channel_id=1, source_target_pairs={{0,16},{4,20},{8,24},{12,28},{16,0},{20,4},{24,8},{28,12},{1,17},{... | collective-permute-start | bytes 196616 | tf_op jit(solution)/shard_map/ppermute | solution.py:215
  32.7 0.7 %collective-permute-start.18 = (bf16[10,64,128]{2,1,0:T(8,128)(2,1)S(1)}, bf16[10,64,128]{2,1,0:T(8,128)(2,1)S(1)}, u32[]{:S(2)}, u32[]{:S(2)}) collective-permute-start(bf16[10,64,128]{2,1,0:T(8,128)(2,1)S(1)} %get-tuple-element.61.own), channel_id=1, source_target_pairs={{4,8},{8,4},{12,16},{16,12},{20,24},{24,20},{5,9},{9,5},{13,17},{1... | collective-permute-start | bytes 491528 | tf_op jit(solution)/shard_map/ppermute | solution.py:235
  33.3 0.0 collective-permute-done.11
  33.3 0.0 copy-start.1
  33.4 5.4 %collective-permute-start.12 = (bf16[432,128]{1,0:T(8,128)(2,1)S(1)}, bf16[432,128]{1,0:T(8,128)(2,1)S(1)}, u32[]{:S(2)}, u32[]{:S(2)}) collective-permute-start(bf16[432,128]{1,0:T(8,128)(2,1)S(1)} %add_convert_fusion.1), channel_id=1, source_target_pairs={{0,16},{4,20},{8,24},{12,28},{16,0},{20,4},{24,8},{28,12},{1,17},{... | collective-permute-start | bytes 331784 | tf_op jit(solution)/shard_map/ppermute | solution.py:215
  38.8 0.1 collective-permute-start.20
  38.8 2.0 %collective-permute-start.19 = (bf16[5,64,128]{2,1,0:T(8,128)(2,1)S(1)}, bf16[5,64,128]{2,1,0:T(8,128)(2,1)S(1)}, u32[]{:S(2)}, u32[]{:S(2)}) collective-permute-start(bf16[5,64,128]{2,1,0:T(8,128)(2,1)S(1)} %get-tuple-element.72), channel_id=1, source_target_pairs={{0,4},{4,0},{8,12},{12,8},{16,20},{20,16},{24,28},{28,24},{1,5},{5... | collective-permute-start | bytes 245768 | tf_op jit(solution)/shard_map/ppermute | solution.py:215
  40.8 0.0 collective-permute-done.16
  40.9 0.1 collective-permute-start.17
  41.0 5.4 %collective-permute-done.17 = bf16[256,128]{1,0:T(8,128)(2,1)S(1)} collective-permute-done((bf16[256,128]{1,0:T(8,128)(2,1)S(1)}, bf16[256,128]{1,0:T(8,128)(2,1)S(1)}, u32[]{:S(2)}, u32[]{:S(2)}) %collective-permute-start.17) | collective-permute-done | bytes 65568 | tf_op jit(solution)/shard_map/ppermute | solution.py:215
  46.4 0.0 collective-permute-done.18.odd
  46.4 0.0 collective-permute-done.20
  46.4 0.0 collective-permute-done.19
  46.5 0.1 collective-permute-start.21
  46.6 1.7 %shard_map.89 = bf16[8,64,128]{2,1,0:T(8,128)(2,1)} custom-call(bf16[10,64,128]{2,1,0:T(8,128)(2,1)S(1)} %pad_maximum_fusion.1.even, bf16[10,64,128]{2,1,0:T(8,128)(2,1)S(1)} %get-tuple-element.61.own, bf16[10,64,128]{2,1,0:T(8,128)(2,1)S(1)} %collective-permute-done.18.odd, bf16[3,3,3,128,128]{4,3,2,1,0:T(8,128)(2,1)S(1)} %copy-done.1), custom_call_target="tpu_custom_call" | custom-call | tf_op jit(solution)/shard_map/pallas_call | solution.py:16
  48.4 3.0 %collective-permute-done.21 = bf16[432,128]{1,0:T(8,128)(2,1)S(1)} collective-permute-done((bf16[432,128]{1,0:T(8,128)(2,1)S(1)}, bf16[432,128]{1,0:T(8,128)(2,1)S(1)}, u32[]{:S(2)}, u32[]{:S(2)}) %collective-permute-start.21) | collective-permute-done | bytes 110624 | tf_op jit(solution)/shard_map/ppermute | solution.py:215
  51.4 0.1 collective-permute-start.27
  51.5 3.0 %collective-permute-start.25 = (bf16[688,128]{1,0:T(8,128)(2,1)S(1)}, bf16[688,128]{1,0:T(8,128)(2,1)S(1)}, u32[]{:S(2)}, u32[]{:S(2)}) collective-permute-start(bf16[688,128]{1,0:T(8,128)(2,1)S(1)} %pad_maximum_fusion.refs_0_), channel_id=1, source_target_pairs={{0,4},{4,0},{8,12},{12,8},{16,20},{20,16},{24,28},{28,24},{1,5},{5... | collective-permute-start | bytes 528392 | tf_op jit(solution)/shard_map/ppermute | solution.py:215
  54.4 0.5 collective-permute-start.23
  54.9 3.0 %collective-permute-done.27.refs_6_ = bf16[688,128]{1,0:T(8,128)(2,1)S(1)} collective-permute-done((bf16[688,128]{1,0:T(8,128)(2,1)S(1)}, bf16[688,128]{1,0:T(8,128)(2,1)S(1)}, u32[]{:S(2)}, u32[]{:S(2)}) %collective-permute-start.27) | collective-permute-done | bytes 176160 | tf_op jit(solution)/shard_map/ppermute | solution.py:225
  57.9 0.0 collective-permute-start.28
  57.9 1.8 %collective-permute-done.25.refs_4_ = bf16[688,128]{1,0:T(8,128)(2,1)S(1)} collective-permute-done((bf16[688,128]{1,0:T(8,128)(2,1)S(1)}, bf16[688,128]{1,0:T(8,128)(2,1)S(1)}, u32[]{:S(2)}, u32[]{:S(2)}) %collective-permute-start.25) | collective-permute-done | bytes 176160 | tf_op jit(solution)/shard_map/ppermute | solution.py:215
  59.7 0.0 collective-permute-start.26
  59.7 0.2 collective-permute-done.23.refs_2_
  59.9 0.3 collective-permute-start.24
  60.2 0.0 collective-permute-done.22.refs_1_
  60.2 0.9 %collective-permute-done.26.refs_5_ = bf16[688,128]{1,0:T(8,128)(2,1)S(1)} collective-permute-done((bf16[688,128]{1,0:T(8,128)(2,1)S(1)}, bf16[688,128]{1,0:T(8,128)(2,1)S(1)}, u32[]{:S(2)}, u32[]{:S(2)}) %collective-permute-start.26) | collective-permute-done | bytes 176160 | tf_op jit(solution)/shard_map/ppermute | solution.py:215
  61.1 0.3 collective-permute-done.24.refs_3_
  61.3 1.3 %shard_map.90 = (bf16[27,4,2,16,128]{4,3,2,1,0:T(8,128)(2,1)}, bf16[2,4,128,256]{3,2,1,0:T(8,128)(2,1)}) custom-call(bf16[688,128]{1,0:T(8,128)(2,1)S(1)} %pad_maximum_fusion.refs_0_, bf16[688,128]{1,0:T(8,128)(2,1)S(1)} %collective-permute-done.22.refs_1_, bf16[688,128]{1,0:T(8,128)(2,1)S(1)} %collective-permute-done.23.refs_2_, ...), custom_call_target="tpu_custom_call" | custom-call | tf_op jit(solution)/shard_map/pallas_call | solution.py:16
  (25 shorter events, 0.3 us)
Async XLA Ops:
  0.6 8.9 %copy-start = (bf16[2,2,2,128,256]{4,3,2,1,0:T(8,128)(2,1)S(1)}, bf16[2,2,2,128,256]{4,3,2,1,0:T(8,128)(2,1)}, u32[]{:S(2)}) copy-start(bf16[2,2,2,128,256]{4,3,2,1,0:T(8,128)(2,1)} %param.9) | copy-start | bytes 1572868
  0.6 1.0 %copy-start.2 = (bf16[4,4,32,32]{3,2,1,0:T(8,128)(2,1)S(1)}, bf16[4,4,32,32]{3,2,1,0:T(8,128)(2,1)}, u32[]{:S(2)}) copy-start(bf16[4,4,32,32]{3,2,1,0:T(8,128)(2,1)} %param.11) | copy-start | bytes 98308
  1.6 4.2 %copy-start.3 = (bf16[1,8,64,128]{3,2,1,0:T(8,128)(2,1)S(1)}, bf16[1,8,64,128]{3,2,1,0:T(8,128)(2,1)}, u32[]{:S(2)}) copy-start(bf16[1,8,64,128]{3,2,1,0:T(8,128)(2,1)} %param.6) | copy-start | bytes 393220
  1.7 6.2 %collective-permute-start.4 = (bf16[2,32,128]{2,1,0:T(8,128)(2,1)S(1)}, bf16[2,32,128]{2,1,0:T(8,128)(2,1)S(1)}, u32[]{:S(2)}, u32[]{:S(2)}) collective-permute-start(bf16[2,32,128]{2,1,0:T(8,128)(2,1)S(1)} %get-tuple-element.42), channel_id=1, source_target_pairs={{0,16},{4,20},{8,24},{12,28},{16,0},{20,4},{24,8},{28,12},{1,17},{... | collective-permute-start | bytes 49160 | tf_op jit(solution)/shard_map/ppermute | solution.py:215
  5.9 7.3 %collective-permute-start = (bf16[32,512]{1,0:T(8,128)(2,1)S(1)}, bf16[32,512]{1,0:T(8,128)(2,1)S(1)}, u32[]{:S(2)}, u32[]{:S(2)}) collective-permute-start(bf16[32,512]{1,0:T(8,128)(2,1)S(1)} %get-tuple-element.38), channel_id=1, source_target_pairs={{0,1},{1,0},{2,3},{3,2},{4,5},{5,4},{6,7},{7,6},{8,9},{9,8},{10,11... | collective-permute-start | bytes 98312 | tf_op jit(solution)/shard_map/ppermute | solution.py:215
  6.0 7.2 %collective-permute-start.1 = (bf16[32,512]{1,0:T(8,128)(2,1)S(1)}, bf16[32,512]{1,0:T(8,128)(2,1)S(1)}, u32[]{:S(2)}, u32[]{:S(2)}) collective-permute-start(bf16[32,512]{1,0:T(8,128)(2,1)S(1)} %get-tuple-element.39), channel_id=1, source_target_pairs={{0,2},{1,3},{2,0},{3,1},{4,6},{5,7},{6,4},{7,5},{8,10},{9,11},{10,... | collective-permute-start | bytes 98312 | tf_op jit(solution)/shard_map/ppermute | solution.py:215
  7.6 5.7 %collective-permute-start.2 = (bf16[32,512]{1,0:T(8,128)(2,1)S(1)}, bf16[32,512]{1,0:T(8,128)(2,1)S(1)}, u32[]{:S(2)}, u32[]{:S(2)}) collective-permute-start(bf16[32,512]{1,0:T(8,128)(2,1)S(1)} %get-tuple-element.40), channel_id=1, source_target_pairs={{0,3},{1,2},{2,1},{3,0},{4,7},{5,6},{6,5},{7,4},{8,11},{9,10},{10,... | collective-permute-start | bytes 98312 | tf_op jit(solution)/shard_map/ppermute | solution.py:215
  7.9 3.8 %collective-permute-start.5 = (bf16[1,2,32,128]{3,2,1,0:T(8,128)(2,1)S(1)}, bf16[1,2,32,128]{3,2,1,0:T(8,128)(2,1)S(1)}, u32[]{:S(2)}, u32[]{:S(2)}) collective-permute-start(bf16[1,2,32,128]{3,2,1,0:T(8,128)(2,1)S(1)} %get-tuple-element.74), channel_id=1, source_target_pairs={{0,8},{4,12},{8,0},{12,4},{16,24},{20,28},{24,16},{28,20},{1,9},{5... | collective-permute-start | bytes 49160 | tf_op jit(solution)/shard_map/ppermute | solution.py:215
  11.7 3.9 %collective-permute-start.6 = (bf16[4,32,128]{2,1,0:T(8,128)(2,1)S(1)}, bf16[4,32,128]{2,1,0:T(8,128)(2,1)S(1)}, u32[]{:S(2)}, u32[]{:S(2)}) collective-permute-start(bf16[4,32,128]{2,1,0:T(8,128)(2,1)S(1)} %maximum_bitcast_fusion.refs_3_), channel_id=1, source_target_pairs={{0,4},{4,0},{8,12},{12,8},{16,20},{20,16},{24,28},{28,24},{1,5},{5... | collective-permute-start | bytes 98312 | tf_op jit(solution)/shard_map/ppermute | solution.py:215
  13.2 2.4 %copy-start.4 = (bf16[1,8,64,128]{3,2,1,0:T(8,128)(2,1)S(1)}, bf16[1,8,64,128]{3,2,1,0:T(8,128)(2,1)}, u32[]{:S(2)}) copy-start(bf16[1,8,64,128]{3,2,1,0:T(8,128)(2,1)} %param.7) | copy-start | bytes 393220
  13.2 2.4 %copy-start.5 = (bf16[1,8,64,128]{3,2,1,0:T(8,128)(2,1)S(1)}, bf16[1,8,64,128]{3,2,1,0:T(8,128)(2,1)}, u32[]{:S(2)}) copy-start(bf16[1,8,64,128]{3,2,1,0:T(8,128)(2,1)} %param.10) | copy-start | bytes 393220
  16.2 3.5 %collective-permute-start.7 = (bf16[512,128]{1,0:T(8,128)(2,1)S(1)}, bf16[512,128]{1,0:T(8,128)(2,1)S(1)}, u32[]{:S(2)}, u32[]{:S(2)}) collective-permute-start(bf16[512,128]{1,0:T(8,128)(2,1)S(1)} %get-tuple-element.49.refs_3_), channel_id=1, source_target_pairs={{0,1},{1,0},{2,3},{3,2},{4,5},{5,4},{6,7},{7,6},{8,9},{9,8},{10,11... | collective-permute-start | bytes 393224 | tf_op jit(solution)/shard_map/ppermute | solution.py:215
  16.3 5.9 %collective-permute-start.3 = (bf16[4,32,512]{2,1,0:T(8,128)(2,1)S(1)}, bf16[4,32,512]{2,1,0:T(8,128)(2,1)S(1)}, u32[]{:S(2)}, u32[]{:S(2)}) collective-permute-start(bf16[4,32,512]{2,1,0:T(8,128)(2,1)S(1)} %pad_maximum_fusion.2.refs_1_), channel_id=1, source_target_pairs={{0,4},{4,0},{8,12},{12,8},{16,20},{20,16},{24,28},{28,24},{1,5},{5... | collective-permute-start | bytes 393224 | tf_op jit(solution)/shard_map/ppermute | solution.py:215
  17.9 5.8 %collective-permute-start.10 = (bf16[512,128]{1,0:T(8,128)(2,1)S(1)}, bf16[512,128]{1,0:T(8,128)(2,1)S(1)}, u32[]{:S(2)}, u32[]{:S(2)}) collective-permute-start(bf16[512,128]{1,0:T(8,128)(2,1)S(1)} %get-tuple-element.49.refs_3_), channel_id=1, source_target_pairs={{0,3},{1,2},{2,1},{3,0},{4,7},{5,6},{6,5},{7,4},{8,11},{9,10},{10,... | collective-permute-start | bytes 393224 | tf_op jit(solution)/shard_map/ppermute | solution.py:215
  19.2 7.7 %collective-permute-start.9 = (bf16[512,128]{1,0:T(8,128)(2,1)S(1)}, bf16[512,128]{1,0:T(8,128)(2,1)S(1)}, u32[]{:S(2)}, u32[]{:S(2)}) collective-permute-start(bf16[512,128]{1,0:T(8,128)(2,1)S(1)} %get-tuple-element.49.refs_3_), channel_id=1, source_target_pairs={{0,2},{1,3},{2,0},{3,1},{4,6},{5,7},{6,4},{7,5},{8,10},{9,11},{10,... | collective-permute-start | bytes 393224 | tf_op jit(solution)/shard_map/ppermute | solution.py:215
  19.7 7.1 %collective-permute-start.8 = (bf16[4,32,512]{2,1,0:T(8,128)(2,1)S(1)}, bf16[4,32,512]{2,1,0:T(8,128)(2,1)S(1)}, u32[]{:S(2)}, u32[]{:S(2)}) collective-permute-start(bf16[4,32,512]{2,1,0:T(8,128)(2,1)S(1)} %pad_maximum_fusion.2.refs_1_), channel_id=1, source_target_pairs={{4,8},{8,4},{12,16},{16,12},{20,24},{24,20},{5,9},{9,5},{13,17},{1... | collective-permute-start | bytes 393224 | tf_op jit(solution)/shard_map/ppermute | solution.py:235
  22.2 7.8 %collective-permute-start.13 = (bf16[256,128]{1,0:T(8,128)(2,1)S(1)}, bf16[256,128]{1,0:T(8,128)(2,1)S(1)}, u32[]{:S(2)}, u32[]{:S(2)}) collective-permute-start(bf16[256,128]{1,0:T(8,128)(2,1)S(1)} %get-tuple-element.58), channel_id=1, source_target_pairs={{0,1},{1,0},{2,3},{3,2},{4,5},{5,4},{6,7},{7,6},{8,9},{9,8},{10,11... | collective-permute-start | bytes 196616 | tf_op jit(solution)/shard_map/ppermute | solution.py:215
  22.2 7.8 %collective-permute-start.14 = (bf16[256,128]{1,0:T(8,128)(2,1)S(1)}, bf16[256,128]{1,0:T(8,128)(2,1)S(1)}, u32[]{:S(2)}, u32[]{:S(2)}) collective-permute-start(bf16[256,128]{1,0:T(8,128)(2,1)S(1)} %get-tuple-element.59), channel_id=1, source_target_pairs={{0,2},{1,3},{2,0},{3,1},{4,6},{5,7},{6,4},{7,5},{8,10},{9,11},{10,... | collective-permute-start | bytes 196616 | tf_op jit(solution)/shard_map/ppermute | solution.py:215
  23.7 6.3 %collective-permute-start.15 = (bf16[256,128]{1,0:T(8,128)(2,1)S(1)}, bf16[256,128]{1,0:T(8,128)(2,1)S(1)}, u32[]{:S(2)}, u32[]{:S(2)}) collective-permute-start(bf16[256,128]{1,0:T(8,128)(2,1)S(1)} %get-tuple-element.60), channel_id=1, source_target_pairs={{0,3},{1,2},{2,1},{3,0},{4,7},{5,6},{6,5},{7,4},{8,11},{9,10},{10,... | collective-permute-start | bytes 196616 | tf_op jit(solution)/shard_map/ppermute | solution.py:215
  28.4 5.0 %collective-permute-start.11 = (bf16[432,128]{1,0:T(8,128)(2,1)S(1)}, bf16[432,128]{1,0:T(8,128)(2,1)S(1)}, u32[]{:S(2)}, u32[]{:S(2)}) collective-permute-start(bf16[432,128]{1,0:T(8,128)(2,1)S(1)} %get-tuple-element.54), channel_id=1, source_target_pairs={{0,4},{4,0},{8,12},{12,8},{16,20},{20,16},{24,28},{28,24},{1,5},{5... | collective-permute-start | bytes 331784 | tf_op jit(solution)/shard_map/ppermute | solution.py:215
  30.1 10.8 %collective-permute-start.16 = (bf16[256,128]{1,0:T(8,128)(2,1)S(1)}, bf16[256,128]{1,0:T(8,128)(2,1)S(1)}, u32[]{:S(2)}, u32[]{:S(2)}) collective-permute-start(bf16[256,128]{1,0:T(8,128)(2,1)S(1)} %add_convert_fusion.3), channel_id=1, source_target_pairs={{0,16},{4,20},{8,24},{12,28},{16,0},{20,4},{24,8},{28,12},{1,17},{... | collective-permute-start | bytes 196616 | tf_op jit(solution)/shard_map/ppermute | solution.py:215
  32.7 13.7 %collective-permute-start.18 = (bf16[10,64,128]{2,1,0:T(8,128)(2,1)S(1)}, bf16[10,64,128]{2,1,0:T(8,128)(2,1)S(1)}, u32[]{:S(2)}, u32[]{:S(2)}) collective-permute-start(bf16[10,64,128]{2,1,0:T(8,128)(2,1)S(1)} %get-tuple-element.61.own), channel_id=1, source_target_pairs={{4,8},{8,4},{12,16},{16,12},{20,24},{24,20},{5,9},{9,5},{13,17},{1... | collective-permute-start | bytes 491528 | tf_op jit(solution)/shard_map/ppermute | solution.py:235
  33.3 13.3 %copy-start.1 = (bf16[3,3,3,128,128]{4,3,2,1,0:T(8,128)(2,1)S(1)}, bf16[3,3,3,128,128]{4,3,2,1,0:T(8,128)(2,1)}, u32[]{:S(2)}) copy-start(bf16[3,3,3,128,128]{4,3,2,1,0:T(8,128)(2,1)} %weight.1) | copy-start | bytes 2654212
  33.4 13.0 %collective-permute-start.12 = (bf16[432,128]{1,0:T(8,128)(2,1)S(1)}, bf16[432,128]{1,0:T(8,128)(2,1)S(1)}, u32[]{:S(2)}, u32[]{:S(2)}) collective-permute-start(bf16[432,128]{1,0:T(8,128)(2,1)S(1)} %add_convert_fusion.1), channel_id=1, source_target_pairs={{0,16},{4,20},{8,24},{12,28},{16,0},{20,4},{24,8},{28,12},{1,17},{... | collective-permute-start | bytes 331784 | tf_op jit(solution)/shard_map/ppermute | solution.py:215
  38.8 7.6 %collective-permute-start.20 = (bf16[5,64,128]{2,1,0:T(8,128)(2,1)S(1)}, bf16[5,64,128]{2,1,0:T(8,128)(2,1)S(1)}, u32[]{:S(2)}, u32[]{:S(2)}) collective-permute-start(bf16[5,64,128]{2,1,0:T(8,128)(2,1)S(1)} %get-tuple-element.71), channel_id=1, source_target_pairs={{0,4},{4,0},{8,12},{12,8},{16,20},{20,16},{24,28},{28,24},{1,5},{5... | collective-permute-start | bytes 245768 | tf_op jit(solution)/shard_map/ppermute | solution.py:215
  38.8 7.6 %collective-permute-start.19 = (bf16[5,64,128]{2,1,0:T(8,128)(2,1)S(1)}, bf16[5,64,128]{2,1,0:T(8,128)(2,1)S(1)}, u32[]{:S(2)}, u32[]{:S(2)}) collective-permute-start(bf16[5,64,128]{2,1,0:T(8,128)(2,1)S(1)} %get-tuple-element.72), channel_id=1, source_target_pairs={{0,4},{4,0},{8,12},{12,8},{16,20},{20,16},{24,28},{28,24},{1,5},{5... | collective-permute-start | bytes 245768 | tf_op jit(solution)/shard_map/ppermute | solution.py:215
  40.9 5.5 %collective-permute-start.17 = (bf16[256,128]{1,0:T(8,128)(2,1)S(1)}, bf16[256,128]{1,0:T(8,128)(2,1)S(1)}, u32[]{:S(2)}, u32[]{:S(2)}) collective-permute-start(bf16[256,128]{1,0:T(8,128)(2,1)S(1)} %add_convert_fusion.2), channel_id=1, source_target_pairs={{0,8},{4,12},{8,0},{12,4},{16,24},{20,28},{24,16},{28,20},{1,9},{5... | collective-permute-start | bytes 196616 | tf_op jit(solution)/shard_map/ppermute | solution.py:215
  46.5 4.8 %collective-permute-start.21 = (bf16[432,128]{1,0:T(8,128)(2,1)S(1)}, bf16[432,128]{1,0:T(8,128)(2,1)S(1)}, u32[]{:S(2)}, u32[]{:S(2)}) collective-permute-start(bf16[432,128]{1,0:T(8,128)(2,1)S(1)} %add_convert_fusion), channel_id=1, source_target_pairs={{0,8},{4,12},{8,0},{12,4},{16,24},{20,28},{24,16},{28,20},{1,9},{5... | collective-permute-start | bytes 331784 | tf_op jit(solution)/shard_map/ppermute | solution.py:215
  51.4 6.5 %collective-permute-start.27 = (bf16[688,128]{1,0:T(8,128)(2,1)S(1)}, bf16[688,128]{1,0:T(8,128)(2,1)S(1)}, u32[]{:S(2)}, u32[]{:S(2)}) collective-permute-start(bf16[688,128]{1,0:T(8,128)(2,1)S(1)} %pad_maximum_fusion.refs_0_), channel_id=1, source_target_pairs={{0,6},{1,7},{2,4},{3,5},{4,2},{5,3},{6,0},{7,1},{8,14},{9,15},{10,... | collective-permute-start | bytes 528392 | tf_op jit(solution)/shard_map/ppermute | solution.py:225
  51.5 8.2 %collective-permute-start.25 = (bf16[688,128]{1,0:T(8,128)(2,1)S(1)}, bf16[688,128]{1,0:T(8,128)(2,1)S(1)}, u32[]{:S(2)}, u32[]{:S(2)}) collective-permute-start(bf16[688,128]{1,0:T(8,128)(2,1)S(1)} %pad_maximum_fusion.refs_0_), channel_id=1, source_target_pairs={{0,4},{4,0},{8,12},{12,8},{16,20},{20,16},{24,28},{28,24},{1,5},{5... | collective-permute-start | bytes 528392 | tf_op jit(solution)/shard_map/ppermute | solution.py:215
  54.4 5.5 %collective-permute-start.23 = (bf16[688,128]{1,0:T(8,128)(2,1)S(1)}, bf16[688,128]{1,0:T(8,128)(2,1)S(1)}, u32[]{:S(2)}, u32[]{:S(2)}) collective-permute-start(bf16[688,128]{1,0:T(8,128)(2,1)S(1)} %pad_maximum_fusion.refs_0_), channel_id=1, source_target_pairs={{0,2},{1,3},{2,0},{3,1},{4,6},{5,7},{6,4},{7,5},{8,10},{9,11},{10,... | collective-permute-start | bytes 528392 | tf_op jit(solution)/shard_map/ppermute | solution.py:215
  54.9 5.3 %collective-permute-start.22 = (bf16[688,128]{1,0:T(8,128)(2,1)S(1)}, bf16[688,128]{1,0:T(8,128)(2,1)S(1)}, u32[]{:S(2)}, u32[]{:S(2)}) collective-permute-start(bf16[688,128]{1,0:T(8,128)(2,1)S(1)} %pad_maximum_fusion.refs_0_), channel_id=1, source_target_pairs={{0,1},{1,0},{2,3},{3,2},{4,5},{5,4},{6,7},{7,6},{8,9},{9,8},{10,11... | collective-permute-start | bytes 528392 | tf_op jit(solution)/shard_map/ppermute | solution.py:215
  57.9 2.3 %collective-permute-start.28 = (bf16[688,128]{1,0:T(8,128)(2,1)S(1)}, bf16[688,128]{1,0:T(8,128)(2,1)S(1)}, u32[]{:S(2)}, u32[]{:S(2)}) collective-permute-start(bf16[688,128]{1,0:T(8,128)(2,1)S(1)} %collective-permute-done.27.refs_6_), channel_id=1, source_target_pairs={{0,1},{1,0},{2,3},{3,2},{4,5},{5,4},{6,7},{7,6},{8,9},{9,8},{10,11... | collective-permute-start | bytes 528392 | tf_op jit(solution)/shard_map/ppermute | solution.py:215
  59.7 1.4 %collective-permute-start.26 = (bf16[688,128]{1,0:T(8,128)(2,1)S(1)}, bf16[688,128]{1,0:T(8,128)(2,1)S(1)}, u32[]{:S(2)}, u32[]{:S(2)}) collective-permute-start(bf16[688,128]{1,0:T(8,128)(2,1)S(1)} %collective-permute-done.25.refs_4_), channel_id=1, source_target_pairs={{0,1},{1,0},{2,3},{3,2},{4,5},{5,4},{6,7},{7,6},{8,9},{9,8},{10,11... | collective-permute-start | bytes 528392 | tf_op jit(solution)/shard_map/ppermute | solution.py:215
  59.9 1.5 %collective-permute-start.24 = (bf16[688,128]{1,0:T(8,128)(2,1)S(1)}, bf16[688,128]{1,0:T(8,128)(2,1)S(1)}, u32[]{:S(2)}, u32[]{:S(2)}) collective-permute-start(bf16[688,128]{1,0:T(8,128)(2,1)S(1)} %collective-permute-done.23.refs_2_), channel_id=1, source_target_pairs={{0,1},{1,0},{2,3},{3,2},{4,5},{5,4},{6,7},{7,6},{8,9},{9,8},{10,11... | collective-permute-start | bytes 528392 | tf_op jit(solution)/shard_map/ppermute | solution.py:215

commit v22 on v21

--- a/solution.py
+++ b/solution.py
@@ -326,7 +326,6 @@
             pltpu.VMEM((2, 27 * half, channels), F32),
         ],
     )
-    near_odd = odd_pairs(near)
     def rounded(value):
         return lax.optimization_barrier(value.astype(wire))
 
@@ -351,9 +350,14 @@
         else:
             conv_other = swapped(conv, "gz", codes[index - 1])
             if index == 1:
-                tied = (conv_other, down_other, near_odd, *evens)
-                conv_other, down_other, near_odd, *evens = lax.optimization_barrier(tied)
-            conv = rounded(added(conv, conv_other))
+                tied = (conv_other, down_other, *evens)
+                conv_other, down_other, *evens = lax.optimization_barrier(tied)
+            conv = added(conv, conv_other).astype(wire)
+            if index == 1:
+                conv, late = lax.optimization_barrier((conv, near))
+                odds = odd_pairs(late[:cut]), odd_pairs(late[cut:])
+            else:
+                conv = lax.optimization_barrier(conv)
         down = added(down, down_other)
         if index < len(codes) - 1:
             down = rounded(down)
@@ -363,10 +367,9 @@
         shape((rows, cols, channels), BF16),
         jnp.concatenate(evens, axis=0),
         near,
-        near_odd,
+        jnp.concatenate(odds, axis=0),
         conv_weight,
     )
-    conv_other, input_grad = lax.optimization_barrier((conv_other, input_grad))
     conv = added(conv, conv_other) * (1 / math.sqrt(cell_total))
     down = down * (1 / math.sqrt(cell_total // 8))
     total = jnp.concatenate([conv.astype(BF16), down.astype(BF16)], axis=0)
@@ -375,6 +378,7 @@
             [total, swapped(total, "gy", 2)],
             [swapped(total, "gz", 1), crossed(total, 1, 2)],
         ]
+        lines[1][1], input_grad = lax.optimization_barrier((lines[1][1], input_grad))
         blocks = []
         for near_block, far_block in lines:
             blocks += [near_block, swapped(near_block, "gy", 1)]

time: 62.8 us -> 63.4 us (level)
  starting transfers between devices: 32.4 us -> 37.2 us
  waiting for transfers between devices: 22.7 us -> 18.5 us
    ppermute x26, waiting for transfers between devices: 19.7 us -> 14 us  [swapped(): lax.ppermute(value, axis, [(i, i ^ code) for i in range(lax.axis_size(axi...]
    ppermute x26, starting transfers between devices: 31 us -> 35.1 us  [swapped(): lax.ppermute(value, axis, [(i, i ^ code) for i in range(lax.axis_size(axi...]
    ppermute x1, waiting for transfers between devices: 2.96 us -> 4.48 us  [crossed(): return lax.ppermute(value, ('gz', 'gy'), pairs)]
    ppermute x2 -> x3, starting transfers between devices: 1.32 us -> 1.99 us  [odd_pairs(): return lax.ppermute(value, 'gz', pairs)]
  transfers between devices with their start and end apart: 29 -> 30, of which waited for: 11 -> 11; matrix products, arithmetic and copies ran while one was open for 0% -> 0% of each run, Pallas kernels for 5% -> 5%
where the time goes in v22:
time: 63.4 us; the launch traced here: 63.2 us
  starting transfers between devices  37.2 us (59%)
  waiting for transfers between devices  18.5 us (29%)
  Pallas kernels  5.34 us (8%)
  local copies, waits for them, and re-layouts  1.03 us (2%)
  between operations  0.88 us (1%)
    ppermute x26, starting transfers between devices, swapped(): lax.ppermute(value, axis, [(i, i ^ code) for i in range(lax.axis_size(axi...  35.1 us
    ppermute x26, waiting for transfers between devices, swapped(): lax.ppermute(value, axis, [(i, i ^ code) for i in range(lax.axis_size(axi...  14 us
    pallas_call x6, Pallas kernels, call(): pl.pallas_call(kernel, out_shape=out_shape, scratch_shapes=list(scratch),...  5.34 us
    ppermute x1, waiting for transfers between devices, crossed(): return lax.ppermute(value, ('gz', 'gy'), pairs)  4.48 us
    ppermute x3, starting transfers between devices, odd_pairs(): return lax.ppermute(value, 'gz', pairs)  1.99 us
  transfers between devices with their start and end apart: 30, of which 11 were waited for; matrix products, arithmetic and copies ran while one was open for 0% of the time, Pallas kernels for 5%

profile of v22, /device:TPU:0, one launch (start us, length us, event | category | flops | bytes accessed | tf_op | source)
XLA Modules:
  0.0 63.2 jit_solution(4299873715331740677)
XLA Ops:
  0.6 0.0 copy-start
  0.7 1.0 %copy-done.2 = bf16[4,4,32,32]{3,2,1,0:T(8,128)(2,1)S(1)} copy-done((bf16[4,4,32,32]{3,2,1,0:T(8,128)(2,1)S(1)}, bf16[4,4,32,32]{3,2,1,0:T(8,128)(2,1)}, u32[]{:S(2)}) %copy-start.2) | copy-done | bytes 32792
  1.6 0.1 shard_map.86
  1.7 4.1 %collective-permute-start.4 = (bf16[2,32,128]{2,1,0:T(8,128)(2,1)S(1)}, bf16[2,32,128]{2,1,0:T(8,128)(2,1)S(1)}, u32[]{:S(2)}, u32[]{:S(2)}) collective-permute-start(bf16[2,32,128]{2,1,0:T(8,128)(2,1)S(1)} %get-tuple-element.43), channel_id=1, source_target_pairs={{0,16},{4,20},{8,24},{12,28},{16,0},{20,4},{24,8},{28,12},{1,17},{... | collective-permute-start | bytes 49160 | tf_op jit(solution)/shard_map/ppermute | solution.py:215
  5.8 0.1 shard_map.85
  5.9 0.1 collective-permute-start
  6.0 1.6 %collective-permute-start.1 = (bf16[32,512]{1,0:T(8,128)(2,1)S(1)}, bf16[32,512]{1,0:T(8,128)(2,1)S(1)}, u32[]{:S(2)}, u32[]{:S(2)}) collective-permute-start(bf16[32,512]{1,0:T(8,128)(2,1)S(1)} %get-tuple-element.40), channel_id=1, source_target_pairs={{0,2},{1,3},{2,0},{3,1},{4,6},{5,7},{6,4},{7,5},{8,10},{9,11},{10,... | collective-permute-start | bytes 98312 | tf_op jit(solution)/shard_map/ppermute | solution.py:215
  7.6 0.3 collective-permute-start.2
  7.9 0.0 collective-permute-done.4
  7.9 1.6 %collective-permute-start.5 = (bf16[1,2,32,128]{3,2,1,0:T(8,128)(2,1)S(1)}, bf16[1,2,32,128]{3,2,1,0:T(8,128)(2,1)S(1)}, u32[]{:S(2)}, u32[]{:S(2)}) collective-permute-start(bf16[1,2,32,128]{3,2,1,0:T(8,128)(2,1)S(1)} %get-tuple-element.78), channel_id=1, source_target_pairs={{0,8},{4,12},{8,0},{12,4},{16,24},{20,28},{24,16},{28,20},{1,9},{5... | collective-permute-start | bytes 49160 | tf_op jit(solution)/shard_map/ppermute | solution.py:215
  9.5 2.1 %collective-permute-done.5 = bf16[1,2,32,128]{3,2,1,0:T(8,128)(2,1)S(1)} collective-permute-done((bf16[1,2,32,128]{3,2,1,0:T(8,128)(2,1)S(1)}, bf16[1,2,32,128]{3,2,1,0:T(8,128)(2,1)S(1)}, u32[]{:S(2)}, u32[]{:S(2)}) %collective-permute-start.5) | collective-permute-done | bytes 16416 | tf_op jit(solution)/shard_map/ppermute | solution.py:215
  11.7 1.5 %collective-permute-start.6 = (bf16[4,32,128]{2,1,0:T(8,128)(2,1)S(1)}, bf16[4,32,128]{2,1,0:T(8,128)(2,1)S(1)}, u32[]{:S(2)}, u32[]{:S(2)}) collective-permute-start(bf16[4,32,128]{2,1,0:T(8,128)(2,1)S(1)} %maximum_bitcast_fusion.refs_3_), channel_id=1, source_target_pairs={{0,4},{4,0},{8,12},{12,8},{16,20},{20,16},{24,28},{28,24},{1,5},{5... | collective-permute-start | bytes 98312 | tf_op jit(solution)/shard_map/ppermute | solution.py:215
  13.2 0.0 copy-start.4
  13.2 0.0 copy-start.5
  13.3 2.3 %collective-permute-done.6.refs_4_ = bf16[4,32,128]{2,1,0:T(8,128)(2,1)S(1)} collective-permute-done((bf16[4,32,128]{2,1,0:T(8,128)(2,1)S(1)}, bf16[4,32,128]{2,1,0:T(8,128)(2,1)S(1)}, u32[]{:S(2)}, u32[]{:S(2)}) %collective-permute-start.6) | collective-permute-done | bytes 32800 | tf_op jit(solution)/shard_map/ppermute | solution.py:215
  15.6 0.6 shard_map.87
  16.2 0.1 collective-permute-start.7
  16.3 1.6 %collective-permute-start.3 = (bf16[4,32,512]{2,1,0:T(8,128)(2,1)S(1)}, bf16[4,32,512]{2,1,0:T(8,128)(2,1)S(1)}, u32[]{:S(2)}, u32[]{:S(2)}) collective-permute-start(bf16[4,32,512]{2,1,0:T(8,128)(2,1)S(1)} %pad_maximum_fusion.3.refs_1_), channel_id=1, source_target_pairs={{0,4},{4,0},{8,12},{12,8},{16,20},{20,16},{24,28},{28,24},{1,5},{5... | collective-permute-start | bytes 393224 | tf_op jit(solution)/shard_map/ppermute | solution.py:215
  17.9 1.3 %collective-permute-start.10 = (bf16[512,128]{1,0:T(8,128)(2,1)S(1)}, bf16[512,128]{1,0:T(8,128)(2,1)S(1)}, u32[]{:S(2)}, u32[]{:S(2)}) collective-permute-start(bf16[512,128]{1,0:T(8,128)(2,1)S(1)} %get-tuple-element.50.refs_3_), channel_id=1, source_target_pairs={{0,3},{1,2},{2,1},{3,0},{4,7},{5,6},{6,5},{7,4},{8,11},{9,10},{10,... | collective-permute-start | bytes 393224 | tf_op jit(solution)/shard_map/ppermute | solution.py:215
  19.2 0.5 collective-permute-start.9
  19.7 0.0 collective-permute-done.7.refs_4_
  19.7 0.7 %collective-permute-start.8 = (bf16[4,32,512]{2,1,0:T(8,128)(2,1)S(1)}, bf16[4,32,512]{2,1,0:T(8,128)(2,1)S(1)}, u32[]{:S(2)}, u32[]{:S(2)}) collective-permute-start(bf16[4,32,512]{2,1,0:T(8,128)(2,1)S(1)} %pad_maximum_fusion.3.refs_1_), channel_id=1, source_target_pairs={{4,8},{8,4},{12,16},{16,12},{20,24},{24,20},{5,9},{9,5},{13,17},{1... | collective-permute-start | bytes 393224 | tf_op jit(solution)/shard_map/ppermute | solution.py:235
  20.4 1.9 %collective-permute-done.3.refs_0_ = bf16[4,32,512]{2,1,0:T(8,128)(2,1)S(1)} collective-permute-done((bf16[4,32,512]{2,1,0:T(8,128)(2,1)S(1)}, bf16[4,32,512]{2,1,0:T(8,128)(2,1)S(1)}, u32[]{:S(2)}, u32[]{:S(2)}) %collective-permute-start.3) | collective-permute-done | bytes 131104 | tf_op jit(solution)/shard_map/ppermute | solution.py:215
  22.2 0.0 collective-permute-start.13
  22.2 1.5 %collective-permute-start.14 = (bf16[256,128]{1,0:T(8,128)(2,1)S(1)}, bf16[256,128]{1,0:T(8,128)(2,1)S(1)}, u32[]{:S(2)}, u32[]{:S(2)}) collective-permute-start(bf16[256,128]{1,0:T(8,128)(2,1)S(1)} %get-tuple-element.60), channel_id=1, source_target_pairs={{0,2},{1,3},{2,0},{3,1},{4,6},{5,7},{6,4},{7,5},{8,10},{9,11},{10,... | collective-permute-start | bytes 196616 | tf_op jit(solution)/shard_map/ppermute | solution.py:215
  23.7 0.0 collective-permute-done.10.refs_6_
  23.7 1.2 %collective-permute-start.15 = (bf16[256,128]{1,0:T(8,128)(2,1)S(1)}, bf16[256,128]{1,0:T(8,128)(2,1)S(1)}, u32[]{:S(2)}, u32[]{:S(2)}) collective-permute-start(bf16[256,128]{1,0:T(8,128)(2,1)S(1)} %get-tuple-element.61), channel_id=1, source_target_pairs={{0,3},{1,2},{2,1},{3,0},{4,7},{5,6},{6,5},{7,4},{8,11},{9,10},{10,... | collective-permute-start | bytes 196616 | tf_op jit(solution)/shard_map/ppermute | solution.py:215
  25.0 1.9 %collective-permute-done.9.refs_5_ = bf16[512,128]{1,0:T(8,128)(2,1)S(1)} collective-permute-done((bf16[512,128]{1,0:T(8,128)(2,1)S(1)}, bf16[512,128]{1,0:T(8,128)(2,1)S(1)}, u32[]{:S(2)}, u32[]{:S(2)}) %collective-permute-start.9) | collective-permute-done | bytes 131104 | tf_op jit(solution)/shard_map/ppermute | solution.py:215
  26.8 0.0 collective-permute-done.8.refs_2_
  26.8 1.5 %shard_map.88 = (f32[432,128]{1,0:T(8,128)S(1)}, bf16[432,128]{1,0:T(8,128)(2,1)S(1)}, bf16[10,64,128]{2,1,0:T(8,128)(2,1)S(1)}) custom-call(bf16[4,32,512]{2,1,0:T(8,128)(2,1)S(1)} %collective-permute-done.3.refs_0_, bf16[4,32,512]{2,1,0:T(8,128)(2,1)S(1)} %pad_maximum_fusion.3.refs_1_, bf16[4,32,512]{2,1,0:T(8,128)(2,1)S(1)} %collective-permute-done.8.refs_2_, ...), custom_call_target="tpu_custom_call" | custom-call | tf_op jit(solution)/shard_map/pallas_call | solution.py:16
  28.4 1.7 %collective-permute-start.11 = (bf16[432,128]{1,0:T(8,128)(2,1)S(1)}, bf16[432,128]{1,0:T(8,128)(2,1)S(1)}, u32[]{:S(2)}, u32[]{:S(2)}) collective-permute-start(bf16[432,128]{1,0:T(8,128)(2,1)S(1)} %get-tuple-element.55), channel_id=1, source_target_pairs={{0,4},{4,0},{8,12},{12,8},{16,20},{20,16},{24,28},{28,24},{1,5},{5... | collective-permute-start | bytes 331784 | tf_op jit(solution)/shard_map/ppermute | solution.py:215
  30.0 0.0 collective-permute-done.13
  30.0 0.0 collective-permute-done.14
  30.0 0.0 collective-permute-done.15
  30.1 2.6 %collective-permute-start.16 = (bf16[256,128]{1,0:T(8,128)(2,1)S(1)}, bf16[256,128]{1,0:T(8,128)(2,1)S(1)}, u32[]{:S(2)}, u32[]{:S(2)}) collective-permute-start(bf16[256,128]{1,0:T(8,128)(2,1)S(1)} %add_convert_fusion.3), channel_id=1, source_target_pairs={{0,16},{4,20},{8,24},{12,28},{16,0},{20,4},{24,8},{28,12},{1,17},{... | collective-permute-start | bytes 196616 | tf_op jit(solution)/shard_map/ppermute | solution.py:215
  32.7 0.5 collective-permute-done.11
  33.2 3.7 %collective-permute-start.12 = (bf16[432,128]{1,0:T(8,128)(2,1)S(1)}, bf16[432,128]{1,0:T(8,128)(2,1)S(1)}, u32[]{:S(2)}, u32[]{:S(2)}) collective-permute-start(bf16[432,128]{1,0:T(8,128)(2,1)S(1)} %add_convert_fusion.1), channel_id=1, source_target_pairs={{0,16},{4,20},{8,24},{12,28},{16,0},{20,4},{24,8},{28,12},{1,17},{... | collective-permute-start | bytes 331784 | tf_op jit(solution)/shard_map/ppermute | solution.py:215
  36.9 0.6 collective-permute-start.19
  37.5 1.5 %collective-permute-start.18 = (bf16[5,64,128]{2,1,0:T(8,128)(2,1)S(1)}, bf16[5,64,128]{2,1,0:T(8,128)(2,1)S(1)}, u32[]{:S(2)}, u32[]{:S(2)}) collective-permute-start(bf16[5,64,128]{2,1,0:T(8,128)(2,1)S(1)} %get-tuple-element.76), channel_id=1, source_target_pairs={{0,4},{4,0},{8,12},{12,8},{16,20},{20,16},{24,28},{28,24},{1,5},{5... | collective-permute-start | bytes 245768 | tf_op jit(solution)/shard_map/ppermute | solution.py:215
  39.0 0.0 collective-permute-done.16
  39.0 1.7 %collective-permute-start.17 = (bf16[256,128]{1,0:T(8,128)(2,1)S(1)}, bf16[256,128]{1,0:T(8,128)(2,1)S(1)}, u32[]{:S(2)}, u32[]{:S(2)}) collective-permute-start(bf16[256,128]{1,0:T(8,128)(2,1)S(1)} %add_convert_fusion.2), channel_id=1, source_target_pairs={{0,8},{4,12},{8,0},{12,4},{16,24},{20,28},{24,16},{28,20},{1,9},{5... | collective-permute-start | bytes 196616 | tf_op jit(solution)/shard_map/ppermute | solution.py:215
  40.7 2.6 %collective-permute-done.17 = bf16[256,128]{1,0:T(8,128)(2,1)S(1)} collective-permute-done((bf16[256,128]{1,0:T(8,128)(2,1)S(1)}, bf16[256,128]{1,0:T(8,128)(2,1)S(1)}, u32[]{:S(2)}, u32[]{:S(2)}) %collective-permute-start.17) | collective-permute-done | bytes 65568 | tf_op jit(solution)/shard_map/ppermute | solution.py:215
  43.3 0.0 collective-permute-done.19
  43.4 0.0 copy-start.1
  43.4 2.2 %collective-permute-start.20 = (bf16[432,128]{1,0:T(8,128)(2,1)S(1)}, bf16[432,128]{1,0:T(8,128)(2,1)S(1)}, u32[]{:S(2)}, u32[]{:S(2)}) collective-permute-start(bf16[432,128]{1,0:T(8,128)(2,1)S(1)} %add_convert_fusion), channel_id=1, source_target_pairs={{0,8},{4,12},{8,0},{12,4},{16,24},{20,28},{24,16},{28,20},{1,9},{5... | collective-permute-start | bytes 331784 | tf_op jit(solution)/shard_map/ppermute | solution.py:215
  45.7 0.7 %collective-permute-start.22 = (bf16[5,64,128]{2,1,0:T(8,128)(2,1)S(1)}, bf16[5,64,128]{2,1,0:T(8,128)(2,1)S(1)}, u32[]{:S(2)}, u32[]{:S(2)}) collective-permute-start(bf16[5,64,128]{2,1,0:T(8,128)(2,1)S(1)} %get-tuple-element.73), channel_id=1, source_target_pairs={{4,8},{8,4},{12,16},{16,12},{20,24},{24,20},{5,9},{9,5},{13,17},{1... | collective-permute-start | bytes 245768 | tf_op jit(solution)/shard_map/ppermute | solution.py:235
  46.3 0.7 %collective-permute-start.23 = (bf16[5,64,128]{2,1,0:T(8,128)(2,1)S(1)}, bf16[5,64,128]{2,1,0:T(8,128)(2,1)S(1)}, u32[]{:S(2)}, u32[]{:S(2)}) collective-permute-start(bf16[5,64,128]{2,1,0:T(8,128)(2,1)S(1)} %get-tuple-element.74), channel_id=1, source_target_pairs={{4,8},{8,4},{12,16},{16,12},{20,24},{24,20},{5,9},{9,5},{13,17},{1... | collective-permute-start | bytes 245768 | tf_op jit(solution)/shard_map/ppermute | solution.py:235
  47.0 1.3 %collective-permute-done.20 = bf16[432,128]{1,0:T(8,128)(2,1)S(1)} collective-permute-done((bf16[432,128]{1,0:T(8,128)(2,1)S(1)}, bf16[432,128]{1,0:T(8,128)(2,1)S(1)}, u32[]{:S(2)}, u32[]{:S(2)}) %collective-permute-start.20) | collective-permute-done | bytes 110624 | tf_op jit(solution)/shard_map/ppermute | solution.py:215
  48.4 3.7 %collective-permute-start.27 = (bf16[688,128]{1,0:T(8,128)(2,1)S(1)}, bf16[688,128]{1,0:T(8,128)(2,1)S(1)}, u32[]{:S(2)}, u32[]{:S(2)}) collective-permute-start(bf16[688,128]{1,0:T(8,128)(2,1)S(1)} %pad_maximum_fusion.refs_0_), channel_id=1, source_target_pairs={{0,4},{4,0},{8,12},{12,8},{16,20},{20,16},{24,28},{28,24},{1,5},{5... | collective-permute-start | bytes 528392 | tf_op jit(solution)/shard_map/ppermute | solution.py:215
  52.1 1.5 %collective-permute-start.25 = (bf16[688,128]{1,0:T(8,128)(2,1)S(1)}, bf16[688,128]{1,0:T(8,128)(2,1)S(1)}, u32[]{:S(2)}, u32[]{:S(2)}) collective-permute-start(bf16[688,128]{1,0:T(8,128)(2,1)S(1)} %pad_maximum_fusion.refs_0_), channel_id=1, source_target_pairs={{0,2},{1,3},{2,0},{3,1},{4,6},{5,7},{6,4},{7,5},{8,10},{9,11},{10,... | collective-permute-start | bytes 528392 | tf_op jit(solution)/shard_map/ppermute | solution.py:215
  53.6 0.0 collective-permute-start.21
  53.7 0.0 collective-permute-done.22
  53.8 1.7 %shard_map.89 = bf16[8,64,128]{2,1,0:T(8,128)(2,1)} custom-call(bf16[10,64,128]{2,1,0:T(8,128)(2,1)S(1)} %pad_maximum_fusion.1.even, bf16[10,64,128]{2,1,0:T(8,128)(2,1)S(1)} %get-tuple-element.68.own, bf16[10,64,128]{2,1,0:T(8,128)(2,1)S(1)} %pad_maximum_fusion.2.odd, bf16[3,3,3,128,128]{4,3,2,1,0:T(8,128)(2,1)S(1)} %copy-done.1), custom_call_target="tpu_custom_call" | custom-call | tf_op jit(solution)/shard_map/pallas_call | solution.py:16
  55.5 0.0 collective-permute-start.24
  55.5 4.5 %collective-permute-done.21.refs_6_ = bf16[688,128]{1,0:T(8,128)(2,1)S(1)} collective-permute-done((bf16[688,128]{1,0:T(8,128)(2,1)S(1)}, bf16[688,128]{1,0:T(8,128)(2,1)S(1)}, u32[]{:S(2)}, u32[]{:S(2)}) %collective-permute-start.21) | collective-permute-done | bytes 176160 | tf_op jit(solution)/shard_map/ppermute | solution.py:225
  60.0 0.0 collective-permute-done.27.refs_4_
  60.0 0.0 collective-permute-start.28
  60.0 0.5 collective-permute-start.26
  60.5 0.1 collective-permute-start.29
  60.6 0.0 collective-permute-done.24.refs_1_
  60.6 0.8 %collective-permute-done.28.refs_5_ = bf16[688,128]{1,0:T(8,128)(2,1)S(1)} collective-permute-done((bf16[688,128]{1,0:T(8,128)(2,1)S(1)}, bf16[688,128]{1,0:T(8,128)(2,1)S(1)}, u32[]{:S(2)}, u32[]{:S(2)}) %collective-permute-start.28) | collective-permute-done | bytes 176160 | tf_op jit(solution)/shard_map/ppermute | solution.py:215
  61.4 0.3 collective-permute-done.26.refs_3_
  61.7 0.3 collective-permute-done.29.refs_7_
  61.9 1.3 %shard_map.90 = (bf16[27,4,2,16,128]{4,3,2,1,0:T(8,128)(2,1)}, bf16[2,4,128,256]{3,2,1,0:T(8,128)(2,1)}) custom-call(bf16[688,128]{1,0:T(8,128)(2,1)S(1)} %pad_maximum_fusion.refs_0_, bf16[688,128]{1,0:T(8,128)(2,1)S(1)} %collective-permute-done.24.refs_1_, bf16[688,128]{1,0:T(8,128)(2,1)S(1)} %collective-permute-done.25.refs_2_, ...), custom_call_target="tpu_custom_call" | custom-call | tf_op jit(solution)/shard_map/pallas_call | solution.py:16
  (29 shorter events, 0.3 us)
Async XLA Ops:
  0.6 8.9 %copy-start = (bf16[2,2,2,128,256]{4,3,2,1,0:T(8,128)(2,1)S(1)}, bf16[2,2,2,128,256]{4,3,2,1,0:T(8,128)(2,1)}, u32[]{:S(2)}) copy-start(bf16[2,2,2,128,256]{4,3,2,1,0:T(8,128)(2,1)} %param.9) | copy-start | bytes 1572868
  0.6 1.0 %copy-start.2 = (bf16[4,4,32,32]{3,2,1,0:T(8,128)(2,1)S(1)}, bf16[4,4,32,32]{3,2,1,0:T(8,128)(2,1)}, u32[]{:S(2)}) copy-start(bf16[4,4,32,32]{3,2,1,0:T(8,128)(2,1)} %param.11) | copy-start | bytes 98308
  1.6 4.2 %copy-start.3 = (bf16[1,8,64,128]{3,2,1,0:T(8,128)(2,1)S(1)}, bf16[1,8,64,128]{3,2,1,0:T(8,128)(2,1)}, u32[]{:S(2)}) copy-start(bf16[1,8,64,128]{3,2,1,0:T(8,128)(2,1)} %param.6) | copy-start | bytes 393220
  1.7 6.2 %collective-permute-start.4 = (bf16[2,32,128]{2,1,0:T(8,128)(2,1)S(1)}, bf16[2,32,128]{2,1,0:T(8,128)(2,1)S(1)}, u32[]{:S(2)}, u32[]{:S(2)}) collective-permute-start(bf16[2,32,128]{2,1,0:T(8,128)(2,1)S(1)} %get-tuple-element.43), channel_id=1, source_target_pairs={{0,16},{4,20},{8,24},{12,28},{16,0},{20,4},{24,8},{28,12},{1,17},{... | collective-permute-start | bytes 49160 | tf_op jit(solution)/shard_map/ppermute | solution.py:215
  5.9 7.3 %collective-permute-start = (bf16[32,512]{1,0:T(8,128)(2,1)S(1)}, bf16[32,512]{1,0:T(8,128)(2,1)S(1)}, u32[]{:S(2)}, u32[]{:S(2)}) collective-permute-start(bf16[32,512]{1,0:T(8,128)(2,1)S(1)} %get-tuple-element.39), channel_id=1, source_target_pairs={{0,1},{1,0},{2,3},{3,2},{4,5},{5,4},{6,7},{7,6},{8,9},{9,8},{10,11... | collective-permute-start | bytes 98312 | tf_op jit(solution)/shard_map/ppermute | solution.py:215
  6.0 7.2 %collective-permute-start.1 = (bf16[32,512]{1,0:T(8,128)(2,1)S(1)}, bf16[32,512]{1,0:T(8,128)(2,1)S(1)}, u32[]{:S(2)}, u32[]{:S(2)}) collective-permute-start(bf16[32,512]{1,0:T(8,128)(2,1)S(1)} %get-tuple-element.40), channel_id=1, source_target_pairs={{0,2},{1,3},{2,0},{3,1},{4,6},{5,7},{6,4},{7,5},{8,10},{9,11},{10,... | collective-permute-start | bytes 98312 | tf_op jit(solution)/shard_map/ppermute | solution.py:215
  7.6 5.7 %collective-permute-start.2 = (bf16[32,512]{1,0:T(8,128)(2,1)S(1)}, bf16[32,512]{1,0:T(8,128)(2,1)S(1)}, u32[]{:S(2)}, u32[]{:S(2)}) collective-permute-start(bf16[32,512]{1,0:T(8,128)(2,1)S(1)} %get-tuple-element.41), channel_id=1, source_target_pairs={{0,3},{1,2},{2,1},{3,0},{4,7},{5,6},{6,5},{7,4},{8,11},{9,10},{10,... | collective-permute-start | bytes 98312 | tf_op jit(solution)/shard_map/ppermute | solution.py:215
  7.9 3.8 %collective-permute-start.5 = (bf16[1,2,32,128]{3,2,1,0:T(8,128)(2,1)S(1)}, bf16[1,2,32,128]{3,2,1,0:T(8,128)(2,1)S(1)}, u32[]{:S(2)}, u32[]{:S(2)}) collective-permute-start(bf16[1,2,32,128]{3,2,1,0:T(8,128)(2,1)S(1)} %get-tuple-element.78), channel_id=1, source_target_pairs={{0,8},{4,12},{8,0},{12,4},{16,24},{20,28},{24,16},{28,20},{1,9},{5... | collective-permute-start | bytes 49160 | tf_op jit(solution)/shard_map/ppermute | solution.py:215
  11.7 3.9 %collective-permute-start.6 = (bf16[4,32,128]{2,1,0:T(8,128)(2,1)S(1)}, bf16[4,32,128]{2,1,0:T(8,128)(2,1)S(1)}, u32[]{:S(2)}, u32[]{:S(2)}) collective-permute-start(bf16[4,32,128]{2,1,0:T(8,128)(2,1)S(1)} %maximum_bitcast_fusion.refs_3_), channel_id=1, source_target_pairs={{0,4},{4,0},{8,12},{12,8},{16,20},{20,16},{24,28},{28,24},{1,5},{5... | collective-permute-start | bytes 98312 | tf_op jit(solution)/shard_map/ppermute | solution.py:215
  13.2 2.4 %copy-start.4 = (bf16[1,8,64,128]{3,2,1,0:T(8,128)(2,1)S(1)}, bf16[1,8,64,128]{3,2,1,0:T(8,128)(2,1)}, u32[]{:S(2)}) copy-start(bf16[1,8,64,128]{3,2,1,0:T(8,128)(2,1)} %param.7) | copy-start | bytes 393220
  13.2 2.4 %copy-start.5 = (bf16[1,8,64,128]{3,2,1,0:T(8,128)(2,1)S(1)}, bf16[1,8,64,128]{3,2,1,0:T(8,128)(2,1)}, u32[]{:S(2)}) copy-start(bf16[1,8,64,128]{3,2,1,0:T(8,128)(2,1)} %param.10) | copy-start | bytes 393220
  16.2 3.5 %collective-permute-start.7 = (bf16[512,128]{1,0:T(8,128)(2,1)S(1)}, bf16[512,128]{1,0:T(8,128)(2,1)S(1)}, u32[]{:S(2)}, u32[]{:S(2)}) collective-permute-start(bf16[512,128]{1,0:T(8,128)(2,1)S(1)} %get-tuple-element.50.refs_3_), channel_id=1, source_target_pairs={{0,1},{1,0},{2,3},{3,2},{4,5},{5,4},{6,7},{7,6},{8,9},{9,8},{10,11... | collective-permute-start | bytes 393224 | tf_op jit(solution)/shard_map/ppermute | solution.py:215
  16.3 5.9 %collective-permute-start.3 = (bf16[4,32,512]{2,1,0:T(8,128)(2,1)S(1)}, bf16[4,32,512]{2,1,0:T(8,128)(2,1)S(1)}, u32[]{:S(2)}, u32[]{:S(2)}) collective-permute-start(bf16[4,32,512]{2,1,0:T(8,128)(2,1)S(1)} %pad_maximum_fusion.3.refs_1_), channel_id=1, source_target_pairs={{0,4},{4,0},{8,12},{12,8},{16,20},{20,16},{24,28},{28,24},{1,5},{5... | collective-permute-start | bytes 393224 | tf_op jit(solution)/shard_map/ppermute | solution.py:215
  17.9 5.8 %collective-permute-start.10 = (bf16[512,128]{1,0:T(8,128)(2,1)S(1)}, bf16[512,128]{1,0:T(8,128)(2,1)S(1)}, u32[]{:S(2)}, u32[]{:S(2)}) collective-permute-start(bf16[512,128]{1,0:T(8,128)(2,1)S(1)} %get-tuple-element.50.refs_3_), channel_id=1, source_target_pairs={{0,3},{1,2},{2,1},{3,0},{4,7},{5,6},{6,5},{7,4},{8,11},{9,10},{10,... | collective-permute-start | bytes 393224 | tf_op jit(solution)/shard_map/ppermute | solution.py:215
  19.2 7.7 %collective-permute-start.9 = (bf16[512,128]{1,0:T(8,128)(2,1)S(1)}, bf16[512,128]{1,0:T(8,128)(2,1)S(1)}, u32[]{:S(2)}, u32[]{:S(2)}) collective-permute-start(bf16[512,128]{1,0:T(8,128)(2,1)S(1)} %get-tuple-element.50.refs_3_), channel_id=1, source_target_pairs={{0,2},{1,3},{2,0},{3,1},{4,6},{5,7},{6,4},{7,5},{8,10},{9,11},{10,... | collective-permute-start | bytes 393224 | tf_op jit(solution)/shard_map/ppermute | solution.py:215
  19.7 7.1 %collective-permute-start.8 = (bf16[4,32,512]{2,1,0:T(8,128)(2,1)S(1)}, bf16[4,32,512]{2,1,0:T(8,128)(2,1)S(1)}, u32[]{:S(2)}, u32[]{:S(2)}) collective-permute-start(bf16[4,32,512]{2,1,0:T(8,128)(2,1)S(1)} %pad_maximum_fusion.3.refs_1_), channel_id=1, source_target_pairs={{4,8},{8,4},{12,16},{16,12},{20,24},{24,20},{5,9},{9,5},{13,17},{1... | collective-permute-start | bytes 393224 | tf_op jit(solution)/shard_map/ppermute | solution.py:235
  22.2 7.8 %collective-permute-start.13 = (bf16[256,128]{1,0:T(8,128)(2,1)S(1)}, bf16[256,128]{1,0:T(8,128)(2,1)S(1)}, u32[]{:S(2)}, u32[]{:S(2)}) collective-permute-start(bf16[256,128]{1,0:T(8,128)(2,1)S(1)} %get-tuple-element.59), channel_id=1, source_target_pairs={{0,1},{1,0},{2,3},{3,2},{4,5},{5,4},{6,7},{7,6},{8,9},{9,8},{10,11... | collective-permute-start | bytes 196616 | tf_op jit(solution)/shard_map/ppermute | solution.py:215
  22.2 7.8 %collective-permute-start.14 = (bf16[256,128]{1,0:T(8,128)(2,1)S(1)}, bf16[256,128]{1,0:T(8,128)(2,1)S(1)}, u32[]{:S(2)}, u32[]{:S(2)}) collective-permute-start(bf16[256,128]{1,0:T(8,128)(2,1)S(1)} %get-tuple-element.60), channel_id=1, source_target_pairs={{0,2},{1,3},{2,0},{3,1},{4,6},{5,7},{6,4},{7,5},{8,10},{9,11},{10,... | collective-permute-start | bytes 196616 | tf_op jit(solution)/shard_map/ppermute | solution.py:215
  23.7 6.3 %collective-permute-start.15 = (bf16[256,128]{1,0:T(8,128)(2,1)S(1)}, bf16[256,128]{1,0:T(8,128)(2,1)S(1)}, u32[]{:S(2)}, u32[]{:S(2)}) collective-permute-start(bf16[256,128]{1,0:T(8,128)(2,1)S(1)} %get-tuple-element.61), channel_id=1, source_target_pairs={{0,3},{1,2},{2,1},{3,0},{4,7},{5,6},{6,5},{7,4},{8,11},{9,10},{10,... | collective-permute-start | bytes 196616 | tf_op jit(solution)/shard_map/ppermute | solution.py:215
  28.4 4.8 %collective-permute-start.11 = (bf16[432,128]{1,0:T(8,128)(2,1)S(1)}, bf16[432,128]{1,0:T(8,128)(2,1)S(1)}, u32[]{:S(2)}, u32[]{:S(2)}) collective-permute-start(bf16[432,128]{1,0:T(8,128)(2,1)S(1)} %get-tuple-element.55), channel_id=1, source_target_pairs={{0,4},{4,0},{8,12},{12,8},{16,20},{20,16},{24,28},{28,24},{1,5},{5... | collective-permute-start | bytes 331784 | tf_op jit(solution)/shard_map/ppermute | solution.py:215
  30.1 8.9 %collective-permute-start.16 = (bf16[256,128]{1,0:T(8,128)(2,1)S(1)}, bf16[256,128]{1,0:T(8,128)(2,1)S(1)}, u32[]{:S(2)}, u32[]{:S(2)}) collective-permute-start(bf16[256,128]{1,0:T(8,128)(2,1)S(1)} %add_convert_fusion.3), channel_id=1, source_target_pairs={{0,16},{4,20},{8,24},{12,28},{16,0},{20,4},{24,8},{28,12},{1,17},{... | collective-permute-start | bytes 196616 | tf_op jit(solution)/shard_map/ppermute | solution.py:215
  33.2 10.1 %collective-permute-start.12 = (bf16[432,128]{1,0:T(8,128)(2,1)S(1)}, bf16[432,128]{1,0:T(8,128)(2,1)S(1)}, u32[]{:S(2)}, u32[]{:S(2)}) collective-permute-start(bf16[432,128]{1,0:T(8,128)(2,1)S(1)} %add_convert_fusion.1), channel_id=1, source_target_pairs={{0,16},{4,20},{8,24},{12,28},{16,0},{20,4},{24,8},{28,12},{1,17},{... | collective-permute-start | bytes 331784 | tf_op jit(solution)/shard_map/ppermute | solution.py:215
  36.9 6.5 %collective-permute-start.19 = (bf16[5,64,128]{2,1,0:T(8,128)(2,1)S(1)}, bf16[5,64,128]{2,1,0:T(8,128)(2,1)S(1)}, u32[]{:S(2)}, u32[]{:S(2)}) collective-permute-start(bf16[5,64,128]{2,1,0:T(8,128)(2,1)S(1)} %get-tuple-element.75), channel_id=1, source_target_pairs={{0,4},{4,0},{8,12},{12,8},{16,20},{20,16},{24,28},{28,24},{1,5},{5... | collective-permute-start | bytes 245768 | tf_op jit(solution)/shard_map/ppermute | solution.py:215
  37.5 5.9 %collective-permute-start.18 = (bf16[5,64,128]{2,1,0:T(8,128)(2,1)S(1)}, bf16[5,64,128]{2,1,0:T(8,128)(2,1)S(1)}, u32[]{:S(2)}, u32[]{:S(2)}) collective-permute-start(bf16[5,64,128]{2,1,0:T(8,128)(2,1)S(1)} %get-tuple-element.76), channel_id=1, source_target_pairs={{0,4},{4,0},{8,12},{12,8},{16,20},{20,16},{24,28},{28,24},{1,5},{5... | collective-permute-start | bytes 245768 | tf_op jit(solution)/shard_map/ppermute | solution.py:215
  39.0 4.3 %collective-permute-start.17 = (bf16[256,128]{1,0:T(8,128)(2,1)S(1)}, bf16[256,128]{1,0:T(8,128)(2,1)S(1)}, u32[]{:S(2)}, u32[]{:S(2)}) collective-permute-start(bf16[256,128]{1,0:T(8,128)(2,1)S(1)} %add_convert_fusion.2), channel_id=1, source_target_pairs={{0,8},{4,12},{8,0},{12,4},{16,24},{20,28},{24,16},{28,20},{1,9},{5... | collective-permute-start | bytes 196616 | tf_op jit(solution)/shard_map/ppermute | solution.py:215
  43.4 10.4 %copy-start.1 = (bf16[3,3,3,128,128]{4,3,2,1,0:T(8,128)(2,1)S(1)}, bf16[3,3,3,128,128]{4,3,2,1,0:T(8,128)(2,1)}, u32[]{:S(2)}) copy-start(bf16[3,3,3,128,128]{4,3,2,1,0:T(8,128)(2,1)} %weight.1) | copy-start | bytes 2654212
  43.4 4.9 %collective-permute-start.20 = (bf16[432,128]{1,0:T(8,128)(2,1)S(1)}, bf16[432,128]{1,0:T(8,128)(2,1)S(1)}, u32[]{:S(2)}, u32[]{:S(2)}) collective-permute-start(bf16[432,128]{1,0:T(8,128)(2,1)S(1)} %add_convert_fusion), channel_id=1, source_target_pairs={{0,8},{4,12},{8,0},{12,4},{16,24},{20,28},{24,16},{28,20},{1,9},{5... | collective-permute-start | bytes 331784 | tf_op jit(solution)/shard_map/ppermute | solution.py:215
  45.7 8.1 %collective-permute-start.22 = (bf16[5,64,128]{2,1,0:T(8,128)(2,1)S(1)}, bf16[5,64,128]{2,1,0:T(8,128)(2,1)S(1)}, u32[]{:S(2)}, u32[]{:S(2)}) collective-permute-start(bf16[5,64,128]{2,1,0:T(8,128)(2,1)S(1)} %get-tuple-element.73), channel_id=1, source_target_pairs={{4,8},{8,4},{12,16},{16,12},{20,24},{24,20},{5,9},{9,5},{13,17},{1... | collective-permute-start | bytes 245768 | tf_op jit(solution)/shard_map/ppermute | solution.py:235
  46.3 7.4 %collective-permute-start.23 = (bf16[5,64,128]{2,1,0:T(8,128)(2,1)S(1)}, bf16[5,64,128]{2,1,0:T(8,128)(2,1)S(1)}, u32[]{:S(2)}, u32[]{:S(2)}) collective-permute-start(bf16[5,64,128]{2,1,0:T(8,128)(2,1)S(1)} %get-tuple-element.74), channel_id=1, source_target_pairs={{4,8},{8,4},{12,16},{16,12},{20,24},{24,20},{5,9},{9,5},{13,17},{1... | collective-permute-start | bytes 245768 | tf_op jit(solution)/shard_map/ppermute | solution.py:235
  48.4 11.6 %collective-permute-start.27 = (bf16[688,128]{1,0:T(8,128)(2,1)S(1)}, bf16[688,128]{1,0:T(8,128)(2,1)S(1)}, u32[]{:S(2)}, u32[]{:S(2)}) collective-permute-start(bf16[688,128]{1,0:T(8,128)(2,1)S(1)} %pad_maximum_fusion.refs_0_), channel_id=1, source_target_pairs={{0,4},{4,0},{8,12},{12,8},{16,20},{20,16},{24,28},{28,24},{1,5},{5... | collective-permute-start | bytes 528392 | tf_op jit(solution)/shard_map/ppermute | solution.py:215
  52.1 7.9 %collective-permute-start.25 = (bf16[688,128]{1,0:T(8,128)(2,1)S(1)}, bf16[688,128]{1,0:T(8,128)(2,1)S(1)}, u32[]{:S(2)}, u32[]{:S(2)}) collective-permute-start(bf16[688,128]{1,0:T(8,128)(2,1)S(1)} %pad_maximum_fusion.refs_0_), channel_id=1, source_target_pairs={{0,2},{1,3},{2,0},{3,1},{4,6},{5,7},{6,4},{7,5},{8,10},{9,11},{10,... | collective-permute-start | bytes 528392 | tf_op jit(solution)/shard_map/ppermute | solution.py:215
  53.6 6.3 %collective-permute-start.21 = (bf16[688,128]{1,0:T(8,128)(2,1)S(1)}, bf16[688,128]{1,0:T(8,128)(2,1)S(1)}, u32[]{:S(2)}, u32[]{:S(2)}) collective-permute-start(bf16[688,128]{1,0:T(8,128)(2,1)S(1)} %pad_maximum_fusion.refs_0_), channel_id=1, source_target_pairs={{0,6},{1,7},{2,4},{3,5},{4,2},{5,3},{6,0},{7,1},{8,14},{9,15},{10,... | collective-permute-start | bytes 528392 | tf_op jit(solution)/shard_map/ppermute | solution.py:225
  55.5 5.1 %collective-permute-start.24 = (bf16[688,128]{1,0:T(8,128)(2,1)S(1)}, bf16[688,128]{1,0:T(8,128)(2,1)S(1)}, u32[]{:S(2)}, u32[]{:S(2)}) collective-permute-start(bf16[688,128]{1,0:T(8,128)(2,1)S(1)} %pad_maximum_fusion.refs_0_), channel_id=1, source_target_pairs={{0,1},{1,0},{2,3},{3,2},{4,5},{5,4},{6,7},{7,6},{8,9},{9,8},{10,11... | collective-permute-start | bytes 528392 | tf_op jit(solution)/shard_map/ppermute | solution.py:215
  60.0 1.4 %collective-permute-start.28 = (bf16[688,128]{1,0:T(8,128)(2,1)S(1)}, bf16[688,128]{1,0:T(8,128)(2,1)S(1)}, u32[]{:S(2)}, u32[]{:S(2)}) collective-permute-start(bf16[688,128]{1,0:T(8,128)(2,1)S(1)} %collective-permute-done.27.refs_4_), channel_id=1, source_target_pairs={{0,1},{1,0},{2,3},{3,2},{4,5},{5,4},{6,7},{7,6},{8,9},{9,8},{10,11... | collective-permute-start | bytes 528392 | tf_op jit(solution)/shard_map/ppermute | solution.py:215
  60.0 1.7 %collective-permute-start.26 = (bf16[688,128]{1,0:T(8,128)(2,1)S(1)}, bf16[688,128]{1,0:T(8,128)(2,1)S(1)}, u32[]{:S(2)}, u32[]{:S(2)}) collective-permute-start(bf16[688,128]{1,0:T(8,128)(2,1)S(1)} %collective-permute-done.25.refs_2_), channel_id=1, source_target_pairs={{0,1},{1,0},{2,3},{3,2},{4,5},{5,4},{6,7},{7,6},{8,9},{9,8},{10,11... | collective-permute-start | bytes 528392 | tf_op jit(solution)/shard_map/ppermute | solution.py:215
  60.5 1.4 %collective-permute-start.29 = (bf16[688,128]{1,0:T(8,128)(2,1)S(1)}, bf16[688,128]{1,0:T(8,128)(2,1)S(1)}, u32[]{:S(2)}, u32[]{:S(2)}) collective-permute-start(bf16[688,128]{1,0:T(8,128)(2,1)S(1)} %collective-permute-done.21.refs_6_), channel_id=1, source_target_pairs={{0,1},{1,0},{2,3},{3,2},{4,5},{5,4},{6,7},{7,6},{8,9},{9,8},{10,11... | collective-permute-start | bytes 528392 | tf_op jit(solution)/shard_map/ppermute | solution.py:215

commit v23 on v18

--- a/solution.py
+++ b/solution.py
@@ -344,7 +344,6 @@
     for index, code in enumerate(codes):
         down_other = swapped(down, "gz", code)
         if index == 0:
-            send, down_other = lax.optimization_barrier((send, down_other))
             conv = rounded(keep + send.astype(F32))
         else:
             conv_other = swapped(conv, "gz", codes[index - 1])

time: 62.8 us -> 62.8 us (level)
    ppermute x25, starting transfers between devices: 29.3 us -> 29.9 us  [swapped(): lax.ppermute(value, axis, [(i, i ^ code) for i in range(lax.axis_size(axi...]
  transfers between devices with their start and end apart: 28 -> 28, of which waited for: 13 -> 12; matrix products, arithmetic and copies ran while one was open for 0% -> 0% of each run, Pallas kernels for 5% -> 5%
where the time goes in v23:
time: 62.8 us; the launch traced here: 62.7 us
  starting transfers between devices  31.3 us (50%)
  waiting for transfers between devices  23.9 us (38%)
  Pallas kernels  5.34 us (9%)
  local copies, waits for them, and re-layouts  1 us (2%)
  between operations  0.85 us (1%)
    ppermute x25, starting transfers between devices, swapped(): lax.ppermute(value, axis, [(i, i ^ code) for i in range(lax.axis_size(axi...  29.9 us
    ppermute x25, waiting for transfers between devices, swapped(): lax.ppermute(value, axis, [(i, i ^ code) for i in range(lax.axis_size(axi...  21 us
    pallas_call x6, Pallas kernels, call(): pl.pallas_call(kernel, out_shape=out_shape, scratch_shapes=list(scratch),...  5.34 us
    ppermute x1, waiting for transfers between devices, crossed(): return lax.ppermute(value, ('gz', 'gy'), pairs)  2.96 us
    ppermute x2, starting transfers between devices, odd_pairs(): return lax.ppermute(value, 'gz', pairs)  1.32 us
  transfers between devices with their start and end apart: 28, of which 12 were waited for; matrix products, arithmetic and copies ran while one was open for 0% of the time, Pallas kernels for 5%

profile of v23, /device:TPU:0, one launch (start us, length us, event | category | flops | bytes accessed | tf_op | source)
XLA Modules:
  0.0 62.7 jit_solution(1655698466570488466)
XLA Ops:
  0.6 0.0 copy-start
  0.7 1.0 %copy-done.2 = bf16[4,4,32,32]{3,2,1,0:T(8,128)(2,1)S(1)} copy-done((bf16[4,4,32,32]{3,2,1,0:T(8,128)(2,1)S(1)}, bf16[4,4,32,32]{3,2,1,0:T(8,128)(2,1)}, u32[]{:S(2)}) %copy-start.2) | copy-done | bytes 32792
  1.6 0.1 shard_map.86
  1.7 4.1 %collective-permute-start.4 = (bf16[2,32,128]{2,1,0:T(8,128)(2,1)S(1)}, bf16[2,32,128]{2,1,0:T(8,128)(2,1)S(1)}, u32[]{:S(2)}, u32[]{:S(2)}) collective-permute-start(bf16[2,32,128]{2,1,0:T(8,128)(2,1)S(1)} %get-tuple-element.39), channel_id=1, source_target_pairs={{0,16},{4,20},{8,24},{12,28},{16,0},{20,4},{24,8},{28,12},{1,17},{... | collective-permute-start | bytes 49160 | tf_op jit(solution)/shard_map/ppermute | solution.py:215
  5.8 0.1 shard_map.85
  5.9 0.1 collective-permute-start
  6.0 1.6 %collective-permute-start.1 = (bf16[32,512]{1,0:T(8,128)(2,1)S(1)}, bf16[32,512]{1,0:T(8,128)(2,1)S(1)}, u32[]{:S(2)}, u32[]{:S(2)}) collective-permute-start(bf16[32,512]{1,0:T(8,128)(2,1)S(1)} %get-tuple-element.36), channel_id=1, source_target_pairs={{0,2},{1,3},{2,0},{3,1},{4,6},{5,7},{6,4},{7,5},{8,10},{9,11},{10,... | collective-permute-start | bytes 98312 | tf_op jit(solution)/shard_map/ppermute | solution.py:215
  7.6 0.3 collective-permute-start.2
  7.9 0.0 collective-permute-done.4
  7.9 1.6 %collective-permute-start.5 = (bf16[1,2,32,128]{3,2,1,0:T(8,128)(2,1)S(1)}, bf16[1,2,32,128]{3,2,1,0:T(8,128)(2,1)S(1)}, u32[]{:S(2)}, u32[]{:S(2)}) collective-permute-start(bf16[1,2,32,128]{3,2,1,0:T(8,128)(2,1)S(1)} %get-tuple-element.66), channel_id=1, source_target_pairs={{0,8},{4,12},{8,0},{12,4},{16,24},{20,28},{24,16},{28,20},{1,9},{5... | collective-permute-start | bytes 49160 | tf_op jit(solution)/shard_map/ppermute | solution.py:215
  9.5 2.1 %collective-permute-done.5 = bf16[1,2,32,128]{3,2,1,0:T(8,128)(2,1)S(1)} collective-permute-done((bf16[1,2,32,128]{3,2,1,0:T(8,128)(2,1)S(1)}, bf16[1,2,32,128]{3,2,1,0:T(8,128)(2,1)S(1)}, u32[]{:S(2)}, u32[]{:S(2)}) %collective-permute-start.5) | collective-permute-done | bytes 16416 | tf_op jit(solution)/shard_map/ppermute | solution.py:215
  11.7 1.5 %collective-permute-start.6 = (bf16[4,32,128]{2,1,0:T(8,128)(2,1)S(1)}, bf16[4,32,128]{2,1,0:T(8,128)(2,1)S(1)}, u32[]{:S(2)}, u32[]{:S(2)}) collective-permute-start(bf16[4,32,128]{2,1,0:T(8,128)(2,1)S(1)} %maximum_bitcast_fusion.refs_3_), channel_id=1, source_target_pairs={{0,4},{4,0},{8,12},{12,8},{16,20},{20,16},{24,28},{28,24},{1,5},{5... | collective-permute-start | bytes 98312 | tf_op jit(solution)/shard_map/ppermute | solution.py:215
  13.2 0.0 collective-permute-done
  13.2 0.0 collective-permute-done.1
  13.2 0.0 collective-permute-done.2
  13.2 0.0 copy-start.4
  13.2 0.0 copy-start.5
  13.3 2.3 %collective-permute-done.6.refs_4_ = bf16[4,32,128]{2,1,0:T(8,128)(2,1)S(1)} collective-permute-done((bf16[4,32,128]{2,1,0:T(8,128)(2,1)S(1)}, bf16[4,32,128]{2,1,0:T(8,128)(2,1)S(1)}, u32[]{:S(2)}, u32[]{:S(2)}) %collective-permute-start.6) | collective-permute-done | bytes 32800 | tf_op jit(solution)/shard_map/ppermute | solution.py:215
  15.6 0.6 shard_map.87
  16.2 0.1 collective-permute-start.7
  16.3 1.6 %collective-permute-start.3 = (bf16[4,32,512]{2,1,0:T(8,128)(2,1)S(1)}, bf16[4,32,512]{2,1,0:T(8,128)(2,1)S(1)}, u32[]{:S(2)}, u32[]{:S(2)}) collective-permute-start(bf16[4,32,512]{2,1,0:T(8,128)(2,1)S(1)} %pad_maximum_fusion.1.refs_1_), channel_id=1, source_target_pairs={{0,4},{4,0},{8,12},{12,8},{16,20},{20,16},{24,28},{28,24},{1,5},{5... | collective-permute-start | bytes 393224 | tf_op jit(solution)/shard_map/ppermute | solution.py:215
  17.9 1.3 %collective-permute-start.10 = (bf16[512,128]{1,0:T(8,128)(2,1)S(1)}, bf16[512,128]{1,0:T(8,128)(2,1)S(1)}, u32[]{:S(2)}, u32[]{:S(2)}) collective-permute-start(bf16[512,128]{1,0:T(8,128)(2,1)S(1)} %get-tuple-element.46.refs_3_), channel_id=1, source_target_pairs={{0,3},{1,2},{2,1},{3,0},{4,7},{5,6},{6,5},{7,4},{8,11},{9,10},{10,... | collective-permute-start | bytes 393224 | tf_op jit(solution)/shard_map/ppermute | solution.py:215
  19.2 0.5 collective-permute-start.9
  19.7 0.0 collective-permute-done.7.refs_4_
  19.7 0.7 %collective-permute-start.8 = (bf16[4,32,512]{2,1,0:T(8,128)(2,1)S(1)}, bf16[4,32,512]{2,1,0:T(8,128)(2,1)S(1)}, u32[]{:S(2)}, u32[]{:S(2)}) collective-permute-start(bf16[4,32,512]{2,1,0:T(8,128)(2,1)S(1)} %pad_maximum_fusion.1.refs_1_), channel_id=1, source_target_pairs={{4,8},{8,4},{12,16},{16,12},{20,24},{24,20},{5,9},{9,5},{13,17},{1... | collective-permute-start | bytes 393224 | tf_op jit(solution)/shard_map/ppermute | solution.py:235
  20.4 1.9 %collective-permute-done.3.refs_0_ = bf16[4,32,512]{2,1,0:T(8,128)(2,1)S(1)} collective-permute-done((bf16[4,32,512]{2,1,0:T(8,128)(2,1)S(1)}, bf16[4,32,512]{2,1,0:T(8,128)(2,1)S(1)}, u32[]{:S(2)}, u32[]{:S(2)}) %collective-permute-start.3) | collective-permute-done | bytes 131104 | tf_op jit(solution)/shard_map/ppermute | solution.py:215
  22.2 0.0 collective-permute-start.13
  22.2 1.5 %collective-permute-start.14 = (bf16[256,128]{1,0:T(8,128)(2,1)S(1)}, bf16[256,128]{1,0:T(8,128)(2,1)S(1)}, u32[]{:S(2)}, u32[]{:S(2)}) collective-permute-start(bf16[256,128]{1,0:T(8,128)(2,1)S(1)} %get-tuple-element.54), channel_id=1, source_target_pairs={{0,2},{1,3},{2,0},{3,1},{4,6},{5,7},{6,4},{7,5},{8,10},{9,11},{10,... | collective-permute-start | bytes 196616 | tf_op jit(solution)/shard_map/ppermute | solution.py:215
  23.7 0.0 collective-permute-done.10.refs_6_
  23.7 1.2 %collective-permute-start.15 = (bf16[256,128]{1,0:T(8,128)(2,1)S(1)}, bf16[256,128]{1,0:T(8,128)(2,1)S(1)}, u32[]{:S(2)}, u32[]{:S(2)}) collective-permute-start(bf16[256,128]{1,0:T(8,128)(2,1)S(1)} %get-tuple-element.55), channel_id=1, source_target_pairs={{0,3},{1,2},{2,1},{3,0},{4,7},{5,6},{6,5},{7,4},{8,11},{9,10},{10,... | collective-permute-start | bytes 196616 | tf_op jit(solution)/shard_map/ppermute | solution.py:215
  25.0 1.9 %collective-permute-done.9.refs_5_ = bf16[512,128]{1,0:T(8,128)(2,1)S(1)} collective-permute-done((bf16[512,128]{1,0:T(8,128)(2,1)S(1)}, bf16[512,128]{1,0:T(8,128)(2,1)S(1)}, u32[]{:S(2)}, u32[]{:S(2)}) %collective-permute-start.9) | collective-permute-done | bytes 131104 | tf_op jit(solution)/shard_map/ppermute | solution.py:215
  26.8 0.0 collective-permute-done.8.refs_2_
  26.8 1.5 %shard_map.88 = (f32[432,128]{1,0:T(8,128)S(1)}, bf16[432,128]{1,0:T(8,128)(2,1)S(1)}, bf16[10,64,128]{2,1,0:T(8,128)(2,1)S(1)}) custom-call(bf16[4,32,512]{2,1,0:T(8,128)(2,1)S(1)} %collective-permute-done.3.refs_0_, bf16[4,32,512]{2,1,0:T(8,128)(2,1)S(1)} %pad_maximum_fusion.1.refs_1_, bf16[4,32,512]{2,1,0:T(8,128)(2,1)S(1)} %collective-permute-done.8.refs_2_, ...), custom_call_target="tpu_custom_call" | custom-call | tf_op jit(solution)/shard_map/pallas_call | solution.py:16
  28.3 0.0 copy-start.1
  28.4 1.7 %collective-permute-start.11 = (bf16[432,128]{1,0:T(8,128)(2,1)S(1)}, bf16[432,128]{1,0:T(8,128)(2,1)S(1)}, u32[]{:S(2)}, u32[]{:S(2)}) collective-permute-start(bf16[432,128]{1,0:T(8,128)(2,1)S(1)} %get-tuple-element.51), channel_id=1, source_target_pairs={{0,4},{4,0},{8,12},{12,8},{16,20},{20,16},{24,28},{28,24},{1,5},{5... | collective-permute-start | bytes 331784 | tf_op jit(solution)/shard_map/ppermute | solution.py:215
  30.0 0.0 collective-permute-done.13
  30.1 0.0 collective-permute-done.14
  30.1 0.0 collective-permute-done.15
  30.1 2.6 %collective-permute-start.16 = (bf16[256,128]{1,0:T(8,128)(2,1)S(1)}, bf16[256,128]{1,0:T(8,128)(2,1)S(1)}, u32[]{:S(2)}, u32[]{:S(2)}) collective-permute-start(bf16[256,128]{1,0:T(8,128)(2,1)S(1)} %add_convert_fusion.3), channel_id=1, source_target_pairs={{0,16},{4,20},{8,24},{12,28},{16,0},{20,4},{24,8},{28,12},{1,17},{... | collective-permute-start | bytes 196616 | tf_op jit(solution)/shard_map/ppermute | solution.py:215
  32.7 1.5 %collective-permute-start.19 = (bf16[10,64,128]{2,1,0:T(8,128)(2,1)S(1)}, bf16[10,64,128]{2,1,0:T(8,128)(2,1)S(1)}, u32[]{:S(2)}, u32[]{:S(2)}) collective-permute-start(bf16[10,64,128]{2,1,0:T(8,128)(2,1)S(1)} %get-tuple-element.56.own), channel_id=1, source_target_pairs={{0,4},{4,0},{8,12},{12,8},{16,20},{20,16},{24,28},{28,24},{1,5},{5... | collective-permute-start | bytes 491528 | tf_op jit(solution)/shard_map/ppermute | solution.py:215
  34.2 0.7 %collective-permute-start.18 = (bf16[10,64,128]{2,1,0:T(8,128)(2,1)S(1)}, bf16[10,64,128]{2,1,0:T(8,128)(2,1)S(1)}, u32[]{:S(2)}, u32[]{:S(2)}) collective-permute-start(bf16[10,64,128]{2,1,0:T(8,128)(2,1)S(1)} %get-tuple-element.56.own), channel_id=1, source_target_pairs={{4,8},{8,4},{12,16},{16,12},{20,24},{24,20},{5,9},{9,5},{13,17},{1... | collective-permute-start | bytes 491528 | tf_op jit(solution)/shard_map/ppermute | solution.py:235
  34.9 0.0 collective-permute-done.11
  34.9 3.9 %collective-permute-start.12 = (bf16[432,128]{1,0:T(8,128)(2,1)S(1)}, bf16[432,128]{1,0:T(8,128)(2,1)S(1)}, u32[]{:S(2)}, u32[]{:S(2)}) collective-permute-start(bf16[432,128]{1,0:T(8,128)(2,1)S(1)} %add_convert_fusion.1), channel_id=1, source_target_pairs={{0,16},{4,20},{8,24},{12,28},{16,0},{20,4},{24,8},{28,12},{1,17},{... | collective-permute-start | bytes 331784 | tf_op jit(solution)/shard_map/ppermute | solution.py:215
  38.8 1.0 %collective-permute-start.17 = (bf16[256,128]{1,0:T(8,128)(2,1)S(1)}, bf16[256,128]{1,0:T(8,128)(2,1)S(1)}, u32[]{:S(2)}, u32[]{:S(2)}) collective-permute-start(bf16[256,128]{1,0:T(8,128)(2,1)S(1)} %add_convert_fusion.2), channel_id=1, source_target_pairs={{0,8},{4,12},{8,0},{12,4},{16,24},{20,28},{24,16},{28,20},{1,9},{5... | collective-permute-start | bytes 196616 | tf_op jit(solution)/shard_map/ppermute | solution.py:215
  39.8 3.8 %collective-permute-done.17 = bf16[256,128]{1,0:T(8,128)(2,1)S(1)} collective-permute-done((bf16[256,128]{1,0:T(8,128)(2,1)S(1)}, bf16[256,128]{1,0:T(8,128)(2,1)S(1)}, u32[]{:S(2)}, u32[]{:S(2)}) %collective-permute-start.17) | collective-permute-done | bytes 65568 | tf_op jit(solution)/shard_map/ppermute | solution.py:215
  43.6 0.0 collective-permute-done.19.even
  43.6 2.9 %collective-permute-done.12 = bf16[432,128]{1,0:T(8,128)(2,1)S(1)} collective-permute-done((bf16[432,128]{1,0:T(8,128)(2,1)S(1)}, bf16[432,128]{1,0:T(8,128)(2,1)S(1)}, u32[]{:S(2)}, u32[]{:S(2)}) %collective-permute-start.12) | collective-permute-done | bytes 110624 | tf_op jit(solution)/shard_map/ppermute | solution.py:215
  46.5 0.1 collective-permute-start.20
  46.6 1.7 %shard_map.89 = bf16[8,64,128]{2,1,0:T(8,128)(2,1)} custom-call(bf16[10,64,128]{2,1,0:T(8,128)(2,1)S(1)} %collective-permute-done.19.even, bf16[10,64,128]{2,1,0:T(8,128)(2,1)S(1)} %get-tuple-element.56.own, bf16[10,64,128]{2,1,0:T(8,128)(2,1)S(1)} %collective-permute-done.18.odd, bf16[3,3,3,128,128]{4,3,2,1,0:T(8,128)(2,1)S(1)} %copy-done.1), custom_call_target="tpu_custom_call" | custom-call | tf_op jit(solution)/shard_map/pallas_call | solution.py:16
  48.4 2.9 %collective-permute-done.20 = bf16[432,128]{1,0:T(8,128)(2,1)S(1)} collective-permute-done((bf16[432,128]{1,0:T(8,128)(2,1)S(1)}, bf16[432,128]{1,0:T(8,128)(2,1)S(1)}, u32[]{:S(2)}, u32[]{:S(2)}) %collective-permute-start.20) | collective-permute-done | bytes 110624 | tf_op jit(solution)/shard_map/ppermute | solution.py:215
  51.4 0.1 collective-permute-start.26
  51.5 3.0 %collective-permute-start.24 = (bf16[688,128]{1,0:T(8,128)(2,1)S(1)}, bf16[688,128]{1,0:T(8,128)(2,1)S(1)}, u32[]{:S(2)}, u32[]{:S(2)}) collective-permute-start(bf16[688,128]{1,0:T(8,128)(2,1)S(1)} %pad_maximum_fusion.refs_0_), channel_id=1, source_target_pairs={{0,4},{4,0},{8,12},{12,8},{16,20},{20,16},{24,28},{28,24},{1,5},{5... | collective-permute-start | bytes 528392 | tf_op jit(solution)/shard_map/ppermute | solution.py:215
  54.4 0.5 collective-permute-start.22
  55.0 3.0 %collective-permute-done.26.refs_6_ = bf16[688,128]{1,0:T(8,128)(2,1)S(1)} collective-permute-done((bf16[688,128]{1,0:T(8,128)(2,1)S(1)}, bf16[688,128]{1,0:T(8,128)(2,1)S(1)}, u32[]{:S(2)}, u32[]{:S(2)}) %collective-permute-start.26) | collective-permute-done | bytes 176160 | tf_op jit(solution)/shard_map/ppermute | solution.py:225
  57.9 0.0 collective-permute-start.27
  57.9 1.8 %collective-permute-done.24.refs_4_ = bf16[688,128]{1,0:T(8,128)(2,1)S(1)} collective-permute-done((bf16[688,128]{1,0:T(8,128)(2,1)S(1)}, bf16[688,128]{1,0:T(8,128)(2,1)S(1)}, u32[]{:S(2)}, u32[]{:S(2)}) %collective-permute-start.24) | collective-permute-done | bytes 176160 | tf_op jit(solution)/shard_map/ppermute | solution.py:215
  59.7 0.0 collective-permute-start.25
  59.7 0.2 collective-permute-done.22.refs_2_
  59.9 0.3 collective-permute-start.23
  60.2 0.0 collective-permute-done.21.refs_1_
  60.2 0.0 collective-permute-done.27.refs_7_
  60.2 0.9 %collective-permute-done.25.refs_5_ = bf16[688,128]{1,0:T(8,128)(2,1)S(1)} collective-permute-done((bf16[688,128]{1,0:T(8,128)(2,1)S(1)}, bf16[688,128]{1,0:T(8,128)(2,1)S(1)}, u32[]{:S(2)}, u32[]{:S(2)}) %collective-permute-start.25) | collective-permute-done | bytes 176160 | tf_op jit(solution)/shard_map/ppermute | solution.py:215
  61.1 0.3 collective-permute-done.23.refs_3_
  61.4 1.3 %shard_map.90 = (bf16[27,4,2,16,128]{4,3,2,1,0:T(8,128)(2,1)}, bf16[2,4,128,256]{3,2,1,0:T(8,128)(2,1)}) custom-call(bf16[688,128]{1,0:T(8,128)(2,1)S(1)} %pad_maximum_fusion.refs_0_, bf16[688,128]{1,0:T(8,128)(2,1)S(1)} %collective-permute-done.21.refs_1_, bf16[688,128]{1,0:T(8,128)(2,1)S(1)} %collective-permute-done.22.refs_2_, ...), custom_call_target="tpu_custom_call" | custom-call | tf_op jit(solution)/shard_map/pallas_call | solution.py:16
  (21 shorter events, 0.3 us)
Async XLA Ops:
  0.6 8.9 %copy-start = (bf16[2,2,2,128,256]{4,3,2,1,0:T(8,128)(2,1)S(1)}, bf16[2,2,2,128,256]{4,3,2,1,0:T(8,128)(2,1)}, u32[]{:S(2)}) copy-start(bf16[2,2,2,128,256]{4,3,2,1,0:T(8,128)(2,1)} %param.9) | copy-start | bytes 1572868
  0.6 1.0 %copy-start.2 = (bf16[4,4,32,32]{3,2,1,0:T(8,128)(2,1)S(1)}, bf16[4,4,32,32]{3,2,1,0:T(8,128)(2,1)}, u32[]{:S(2)}) copy-start(bf16[4,4,32,32]{3,2,1,0:T(8,128)(2,1)} %param.11) | copy-start | bytes 98308
  1.6 4.2 %copy-start.3 = (bf16[1,8,64,128]{3,2,1,0:T(8,128)(2,1)S(1)}, bf16[1,8,64,128]{3,2,1,0:T(8,128)(2,1)}, u32[]{:S(2)}) copy-start(bf16[1,8,64,128]{3,2,1,0:T(8,128)(2,1)} %param.6) | copy-start | bytes 393220
  1.7 6.2 %collective-permute-start.4 = (bf16[2,32,128]{2,1,0:T(8,128)(2,1)S(1)}, bf16[2,32,128]{2,1,0:T(8,128)(2,1)S(1)}, u32[]{:S(2)}, u32[]{:S(2)}) collective-permute-start(bf16[2,32,128]{2,1,0:T(8,128)(2,1)S(1)} %get-tuple-element.39), channel_id=1, source_target_pairs={{0,16},{4,20},{8,24},{12,28},{16,0},{20,4},{24,8},{28,12},{1,17},{... | collective-permute-start | bytes 49160 | tf_op jit(solution)/shard_map/ppermute | solution.py:215
  5.9 7.3 %collective-permute-start = (bf16[32,512]{1,0:T(8,128)(2,1)S(1)}, bf16[32,512]{1,0:T(8,128)(2,1)S(1)}, u32[]{:S(2)}, u32[]{:S(2)}) collective-permute-start(bf16[32,512]{1,0:T(8,128)(2,1)S(1)} %get-tuple-element.35), channel_id=1, source_target_pairs={{0,1},{1,0},{2,3},{3,2},{4,5},{5,4},{6,7},{7,6},{8,9},{9,8},{10,11... | collective-permute-start | bytes 98312 | tf_op jit(solution)/shard_map/ppermute | solution.py:215
  6.0 7.2 %collective-permute-start.1 = (bf16[32,512]{1,0:T(8,128)(2,1)S(1)}, bf16[32,512]{1,0:T(8,128)(2,1)S(1)}, u32[]{:S(2)}, u32[]{:S(2)}) collective-permute-start(bf16[32,512]{1,0:T(8,128)(2,1)S(1)} %get-tuple-element.36), channel_id=1, source_target_pairs={{0,2},{1,3},{2,0},{3,1},{4,6},{5,7},{6,4},{7,5},{8,10},{9,11},{10,... | collective-permute-start | bytes 98312 | tf_op jit(solution)/shard_map/ppermute | solution.py:215
  7.6 5.7 %collective-permute-start.2 = (bf16[32,512]{1,0:T(8,128)(2,1)S(1)}, bf16[32,512]{1,0:T(8,128)(2,1)S(1)}, u32[]{:S(2)}, u32[]{:S(2)}) collective-permute-start(bf16[32,512]{1,0:T(8,128)(2,1)S(1)} %get-tuple-element.37), channel_id=1, source_target_pairs={{0,3},{1,2},{2,1},{3,0},{4,7},{5,6},{6,5},{7,4},{8,11},{9,10},{10,... | collective-permute-start | bytes 98312 | tf_op jit(solution)/shard_map/ppermute | solution.py:215
  7.9 3.8 %collective-permute-start.5 = (bf16[1,2,32,128]{3,2,1,0:T(8,128)(2,1)S(1)}, bf16[1,2,32,128]{3,2,1,0:T(8,128)(2,1)S(1)}, u32[]{:S(2)}, u32[]{:S(2)}) collective-permute-start(bf16[1,2,32,128]{3,2,1,0:T(8,128)(2,1)S(1)} %get-tuple-element.66), channel_id=1, source_target_pairs={{0,8},{4,12},{8,0},{12,4},{16,24},{20,28},{24,16},{28,20},{1,9},{5... | collective-permute-start | bytes 49160 | tf_op jit(solution)/shard_map/ppermute | solution.py:215
  11.7 3.9 %collective-permute-start.6 = (bf16[4,32,128]{2,1,0:T(8,128)(2,1)S(1)}, bf16[4,32,128]{2,1,0:T(8,128)(2,1)S(1)}, u32[]{:S(2)}, u32[]{:S(2)}) collective-permute-start(bf16[4,32,128]{2,1,0:T(8,128)(2,1)S(1)} %maximum_bitcast_fusion.refs_3_), channel_id=1, source_target_pairs={{0,4},{4,0},{8,12},{12,8},{16,20},{20,16},{24,28},{28,24},{1,5},{5... | collective-permute-start | bytes 98312 | tf_op jit(solution)/shard_map/ppermute | solution.py:215
  13.2 2.4 %copy-start.4 = (bf16[1,8,64,128]{3,2,1,0:T(8,128)(2,1)S(1)}, bf16[1,8,64,128]{3,2,1,0:T(8,128)(2,1)}, u32[]{:S(2)}) copy-start(bf16[1,8,64,128]{3,2,1,0:T(8,128)(2,1)} %param.7) | copy-start | bytes 393220
  13.2 2.4 %copy-start.5 = (bf16[1,8,64,128]{3,2,1,0:T(8,128)(2,1)S(1)}, bf16[1,8,64,128]{3,2,1,0:T(8,128)(2,1)}, u32[]{:S(2)}) copy-start(bf16[1,8,64,128]{3,2,1,0:T(8,128)(2,1)} %param.10) | copy-start | bytes 393220
  16.2 3.5 %collective-permute-start.7 = (bf16[512,128]{1,0:T(8,128)(2,1)S(1)}, bf16[512,128]{1,0:T(8,128)(2,1)S(1)}, u32[]{:S(2)}, u32[]{:S(2)}) collective-permute-start(bf16[512,128]{1,0:T(8,128)(2,1)S(1)} %get-tuple-element.46.refs_3_), channel_id=1, source_target_pairs={{0,1},{1,0},{2,3},{3,2},{4,5},{5,4},{6,7},{7,6},{8,9},{9,8},{10,11... | collective-permute-start | bytes 393224 | tf_op jit(solution)/shard_map/ppermute | solution.py:215
  16.3 5.9 %collective-permute-start.3 = (bf16[4,32,512]{2,1,0:T(8,128)(2,1)S(1)}, bf16[4,32,512]{2,1,0:T(8,128)(2,1)S(1)}, u32[]{:S(2)}, u32[]{:S(2)}) collective-permute-start(bf16[4,32,512]{2,1,0:T(8,128)(2,1)S(1)} %pad_maximum_fusion.1.refs_1_), channel_id=1, source_target_pairs={{0,4},{4,0},{8,12},{12,8},{16,20},{20,16},{24,28},{28,24},{1,5},{5... | collective-permute-start | bytes 393224 | tf_op jit(solution)/shard_map/ppermute | solution.py:215
  17.9 5.8 %collective-permute-start.10 = (bf16[512,128]{1,0:T(8,128)(2,1)S(1)}, bf16[512,128]{1,0:T(8,128)(2,1)S(1)}, u32[]{:S(2)}, u32[]{:S(2)}) collective-permute-start(bf16[512,128]{1,0:T(8,128)(2,1)S(1)} %get-tuple-element.46.refs_3_), channel_id=1, source_target_pairs={{0,3},{1,2},{2,1},{3,0},{4,7},{5,6},{6,5},{7,4},{8,11},{9,10},{10,... | collective-permute-start | bytes 393224 | tf_op jit(solution)/shard_map/ppermute | solution.py:215
  19.2 7.7 %collective-permute-start.9 = (bf16[512,128]{1,0:T(8,128)(2,1)S(1)}, bf16[512,128]{1,0:T(8,128)(2,1)S(1)}, u32[]{:S(2)}, u32[]{:S(2)}) collective-permute-start(bf16[512,128]{1,0:T(8,128)(2,1)S(1)} %get-tuple-element.46.refs_3_), channel_id=1, source_target_pairs={{0,2},{1,3},{2,0},{3,1},{4,6},{5,7},{6,4},{7,5},{8,10},{9,11},{10,... | collective-permute-start | bytes 393224 | tf_op jit(solution)/shard_map/ppermute | solution.py:215
  19.7 7.1 %collective-permute-start.8 = (bf16[4,32,512]{2,1,0:T(8,128)(2,1)S(1)}, bf16[4,32,512]{2,1,0:T(8,128)(2,1)S(1)}, u32[]{:S(2)}, u32[]{:S(2)}) collective-permute-start(bf16[4,32,512]{2,1,0:T(8,128)(2,1)S(1)} %pad_maximum_fusion.1.refs_1_), channel_id=1, source_target_pairs={{4,8},{8,4},{12,16},{16,12},{20,24},{24,20},{5,9},{9,5},{13,17},{1... | collective-permute-start | bytes 393224 | tf_op jit(solution)/shard_map/ppermute | solution.py:235
  22.2 7.8 %collective-permute-start.13 = (bf16[256,128]{1,0:T(8,128)(2,1)S(1)}, bf16[256,128]{1,0:T(8,128)(2,1)S(1)}, u32[]{:S(2)}, u32[]{:S(2)}) collective-permute-start(bf16[256,128]{1,0:T(8,128)(2,1)S(1)} %get-tuple-element.53), channel_id=1, source_target_pairs={{0,1},{1,0},{2,3},{3,2},{4,5},{5,4},{6,7},{7,6},{8,9},{9,8},{10,11... | collective-permute-start | bytes 196616 | tf_op jit(solution)/shard_map/ppermute | solution.py:215
  22.2 7.8 %collective-permute-start.14 = (bf16[256,128]{1,0:T(8,128)(2,1)S(1)}, bf16[256,128]{1,0:T(8,128)(2,1)S(1)}, u32[]{:S(2)}, u32[]{:S(2)}) collective-permute-start(bf16[256,128]{1,0:T(8,128)(2,1)S(1)} %get-tuple-element.54), channel_id=1, source_target_pairs={{0,2},{1,3},{2,0},{3,1},{4,6},{5,7},{6,4},{7,5},{8,10},{9,11},{10,... | collective-permute-start | bytes 196616 | tf_op jit(solution)/shard_map/ppermute | solution.py:215
  23.7 6.3 %collective-permute-start.15 = (bf16[256,128]{1,0:T(8,128)(2,1)S(1)}, bf16[256,128]{1,0:T(8,128)(2,1)S(1)}, u32[]{:S(2)}, u32[]{:S(2)}) collective-permute-start(bf16[256,128]{1,0:T(8,128)(2,1)S(1)} %get-tuple-element.55), channel_id=1, source_target_pairs={{0,3},{1,2},{2,1},{3,0},{4,7},{5,6},{6,5},{7,4},{8,11},{9,10},{10,... | collective-permute-start | bytes 196616 | tf_op jit(solution)/shard_map/ppermute | solution.py:215
  28.3 18.3 %copy-start.1 = (bf16[3,3,3,128,128]{4,3,2,1,0:T(8,128)(2,1)S(1)}, bf16[3,3,3,128,128]{4,3,2,1,0:T(8,128)(2,1)}, u32[]{:S(2)}) copy-start(bf16[3,3,3,128,128]{4,3,2,1,0:T(8,128)(2,1)} %weight.1) | copy-start | bytes 2654212
  28.4 6.5 %collective-permute-start.11 = (bf16[432,128]{1,0:T(8,128)(2,1)S(1)}, bf16[432,128]{1,0:T(8,128)(2,1)S(1)}, u32[]{:S(2)}, u32[]{:S(2)}) collective-permute-start(bf16[432,128]{1,0:T(8,128)(2,1)S(1)} %get-tuple-element.51), channel_id=1, source_target_pairs={{0,4},{4,0},{8,12},{12,8},{16,20},{20,16},{24,28},{28,24},{1,5},{5... | collective-permute-start | bytes 331784 | tf_op jit(solution)/shard_map/ppermute | solution.py:215
  30.1 8.7 %collective-permute-start.16 = (bf16[256,128]{1,0:T(8,128)(2,1)S(1)}, bf16[256,128]{1,0:T(8,128)(2,1)S(1)}, u32[]{:S(2)}, u32[]{:S(2)}) collective-permute-start(bf16[256,128]{1,0:T(8,128)(2,1)S(1)} %add_convert_fusion.3), channel_id=1, source_target_pairs={{0,16},{4,20},{8,24},{12,28},{16,0},{20,4},{24,8},{28,12},{1,17},{... | collective-permute-start | bytes 196616 | tf_op jit(solution)/shard_map/ppermute | solution.py:215
  32.7 10.9 %collective-permute-start.19 = (bf16[10,64,128]{2,1,0:T(8,128)(2,1)S(1)}, bf16[10,64,128]{2,1,0:T(8,128)(2,1)S(1)}, u32[]{:S(2)}, u32[]{:S(2)}) collective-permute-start(bf16[10,64,128]{2,1,0:T(8,128)(2,1)S(1)} %get-tuple-element.56.own), channel_id=1, source_target_pairs={{0,4},{4,0},{8,12},{12,8},{16,20},{20,16},{24,28},{28,24},{1,5},{5... | collective-permute-start | bytes 491528 | tf_op jit(solution)/shard_map/ppermute | solution.py:215
  34.2 9.4 %collective-permute-start.18 = (bf16[10,64,128]{2,1,0:T(8,128)(2,1)S(1)}, bf16[10,64,128]{2,1,0:T(8,128)(2,1)S(1)}, u32[]{:S(2)}, u32[]{:S(2)}) collective-permute-start(bf16[10,64,128]{2,1,0:T(8,128)(2,1)S(1)} %get-tuple-element.56.own), channel_id=1, source_target_pairs={{4,8},{8,4},{12,16},{16,12},{20,24},{24,20},{5,9},{9,5},{13,17},{1... | collective-permute-start | bytes 491528 | tf_op jit(solution)/shard_map/ppermute | solution.py:235
  34.9 11.6 %collective-permute-start.12 = (bf16[432,128]{1,0:T(8,128)(2,1)S(1)}, bf16[432,128]{1,0:T(8,128)(2,1)S(1)}, u32[]{:S(2)}, u32[]{:S(2)}) collective-permute-start(bf16[432,128]{1,0:T(8,128)(2,1)S(1)} %add_convert_fusion.1), channel_id=1, source_target_pairs={{0,16},{4,20},{8,24},{12,28},{16,0},{20,4},{24,8},{28,12},{1,17},{... | collective-permute-start | bytes 331784 | tf_op jit(solution)/shard_map/ppermute | solution.py:215
  38.8 4.8 %collective-permute-start.17 = (bf16[256,128]{1,0:T(8,128)(2,1)S(1)}, bf16[256,128]{1,0:T(8,128)(2,1)S(1)}, u32[]{:S(2)}, u32[]{:S(2)}) collective-permute-start(bf16[256,128]{1,0:T(8,128)(2,1)S(1)} %add_convert_fusion.2), channel_id=1, source_target_pairs={{0,8},{4,12},{8,0},{12,4},{16,24},{20,28},{24,16},{28,20},{1,9},{5... | collective-permute-start | bytes 196616 | tf_op jit(solution)/shard_map/ppermute | solution.py:215
  46.5 4.8 %collective-permute-start.20 = (bf16[432,128]{1,0:T(8,128)(2,1)S(1)}, bf16[432,128]{1,0:T(8,128)(2,1)S(1)}, u32[]{:S(2)}, u32[]{:S(2)}) collective-permute-start(bf16[432,128]{1,0:T(8,128)(2,1)S(1)} %add_convert_fusion), channel_id=1, source_target_pairs={{0,8},{4,12},{8,0},{12,4},{16,24},{20,28},{24,16},{28,20},{1,9},{5... | collective-permute-start | bytes 331784 | tf_op jit(solution)/shard_map/ppermute | solution.py:215
  51.4 6.5 %collective-permute-start.26 = (bf16[688,128]{1,0:T(8,128)(2,1)S(1)}, bf16[688,128]{1,0:T(8,128)(2,1)S(1)}, u32[]{:S(2)}, u32[]{:S(2)}) collective-permute-start(bf16[688,128]{1,0:T(8,128)(2,1)S(1)} %pad_maximum_fusion.refs_0_), channel_id=1, source_target_pairs={{0,6},{1,7},{2,4},{3,5},{4,2},{5,3},{6,0},{7,1},{8,14},{9,15},{10,... | collective-permute-start | bytes 528392 | tf_op jit(solution)/shard_map/ppermute | solution.py:225
  51.5 8.2 %collective-permute-start.24 = (bf16[688,128]{1,0:T(8,128)(2,1)S(1)}, bf16[688,128]{1,0:T(8,128)(2,1)S(1)}, u32[]{:S(2)}, u32[]{:S(2)}) collective-permute-start(bf16[688,128]{1,0:T(8,128)(2,1)S(1)} %pad_maximum_fusion.refs_0_), channel_id=1, source_target_pairs={{0,4},{4,0},{8,12},{12,8},{16,20},{20,16},{24,28},{28,24},{1,5},{5... | collective-permute-start | bytes 528392 | tf_op jit(solution)/shard_map/ppermute | solution.py:215
  54.4 5.5 %collective-permute-start.22 = (bf16[688,128]{1,0:T(8,128)(2,1)S(1)}, bf16[688,128]{1,0:T(8,128)(2,1)S(1)}, u32[]{:S(2)}, u32[]{:S(2)}) collective-permute-start(bf16[688,128]{1,0:T(8,128)(2,1)S(1)} %pad_maximum_fusion.refs_0_), channel_id=1, source_target_pairs={{0,2},{1,3},{2,0},{3,1},{4,6},{5,7},{6,4},{7,5},{8,10},{9,11},{10,... | collective-permute-start | bytes 528392 | tf_op jit(solution)/shard_map/ppermute | solution.py:215
  55.0 5.3 %collective-permute-start.21 = (bf16[688,128]{1,0:T(8,128)(2,1)S(1)}, bf16[688,128]{1,0:T(8,128)(2,1)S(1)}, u32[]{:S(2)}, u32[]{:S(2)}) collective-permute-start(bf16[688,128]{1,0:T(8,128)(2,1)S(1)} %pad_maximum_fusion.refs_0_), channel_id=1, source_target_pairs={{0,1},{1,0},{2,3},{3,2},{4,5},{5,4},{6,7},{7,6},{8,9},{9,8},{10,11... | collective-permute-start | bytes 528392 | tf_op jit(solution)/shard_map/ppermute | solution.py:215
  57.9 2.3 %collective-permute-start.27 = (bf16[688,128]{1,0:T(8,128)(2,1)S(1)}, bf16[688,128]{1,0:T(8,128)(2,1)S(1)}, u32[]{:S(2)}, u32[]{:S(2)}) collective-permute-start(bf16[688,128]{1,0:T(8,128)(2,1)S(1)} %collective-permute-done.26.refs_6_), channel_id=1, source_target_pairs={{0,1},{1,0},{2,3},{3,2},{4,5},{5,4},{6,7},{7,6},{8,9},{9,8},{10,11... | collective-permute-start | bytes 528392 | tf_op jit(solution)/shard_map/ppermute | solution.py:215
  59.7 1.4 %collective-permute-start.25 = (bf16[688,128]{1,0:T(8,128)(2,1)S(1)}, bf16[688,128]{1,0:T(8,128)(2,1)S(1)}, u32[]{:S(2)}, u32[]{:S(2)}) collective-permute-start(bf16[688,128]{1,0:T(8,128)(2,1)S(1)} %collective-permute-done.24.refs_4_), channel_id=1, source_target_pairs={{0,1},{1,0},{2,3},{3,2},{4,5},{5,4},{6,7},{7,6},{8,9},{9,8},{10,11... | collective-permute-start | bytes 528392 | tf_op jit(solution)/shard_map/ppermute | solution.py:215
  59.9 1.5 %collective-permute-start.23 = (bf16[688,128]{1,0:T(8,128)(2,1)S(1)}, bf16[688,128]{1,0:T(8,128)(2,1)S(1)}, u32[]{:S(2)}, u32[]{:S(2)}) collective-permute-start(bf16[688,128]{1,0:T(8,128)(2,1)S(1)} %collective-permute-done.22.refs_2_), channel_id=1, source_target_pairs={{0,1},{1,0},{2,3},{3,2},{4,5},{5,4},{6,7},{7,6},{8,9},{9,8},{10,11... | collective-permute-start | bytes 528392 | tf_op jit(solution)/shard_map/ppermute | solution.py:215

commit v24 on v18

--- a/solution.py
+++ b/solution.py
@@ -326,7 +326,7 @@
             pltpu.VMEM((2, 27 * half, channels), F32),
         ],
     )
-    near_odd, near_even = odd_pairs(near), even_pairs(near)
+    near_even, near_odd = even_pairs(near), odd_pairs(near)
     def rounded(value):
         return lax.optimization_barrier(value.astype(wire))
 
@@ -349,8 +349,8 @@
         else:
             conv_other = swapped(conv, "gz", codes[index - 1])
             if index == 1:
-                tied = (conv_other, down_other, near_odd, near_even)
-                conv_other, down_other, near_odd, near_even = lax.optimization_barrier(tied)
+                tied = (conv_other, down_other, near_even, near_odd)
+                conv_other, down_other, near_even, near_odd = lax.optimization_barrier(tied)
             conv = rounded(added(conv, conv_other))
         down = added(down, down_other)
         if index < len(codes) - 1:

time: 62.8 us -> 62.5 us (level)
  waiting for transfers between devices: 24.3 us -> 23.5 us
    ppermute x25, waiting for transfers between devices: 21.3 us -> 20.5 us  [swapped(): lax.ppermute(value, axis, [(i, i ^ code) for i in range(lax.axis_size(axi...]
    ppermute x25, starting transfers between devices: 29.3 us -> 30 us  [swapped(): lax.ppermute(value, axis, [(i, i ^ code) for i in range(lax.axis_size(axi...]
where the time goes in v24:
time: 62.5 us; the launch traced here: 62.3 us
  starting transfers between devices  31.4 us (50%)
  waiting for transfers between devices  23.5 us (38%)
  Pallas kernels  5.34 us (9%)
  local copies, waits for them, and re-layouts  1 us (2%)
  between operations  0.83 us (1%)
    ppermute x25, starting transfers between devices, swapped(): lax.ppermute(value, axis, [(i, i ^ code) for i in range(lax.axis_size(axi...  30 us
    ppermute x25, waiting for transfers between devices, swapped(): lax.ppermute(value, axis, [(i, i ^ code) for i in range(lax.axis_size(axi...  20.5 us
    pallas_call x6, Pallas kernels, call(): pl.pallas_call(kernel, out_shape=out_shape, scratch_shapes=list(scratch),...  5.34 us
    ppermute x1, waiting for transfers between devices, crossed(): return lax.ppermute(value, ('gz', 'gy'), pairs)  2.96 us
    ppermute x2, starting transfers between devices, odd_pairs(): return lax.ppermute(value, 'gz', pairs)  1.32 us
  transfers between devices with their start and end apart: 28, of which 13 were waited for; matrix products, arithmetic and copies ran while one was open for 0% of the time, Pallas kernels for 5%

profile of v24, /device:TPU:0, one launch (start us, length us, event | category | flops | bytes accessed | tf_op | source)
XLA Modules:
  0.0 62.3 jit_solution(2087910882933790988)
XLA Ops:
  0.6 0.0 copy-start
  0.7 1.0 %copy-done.2 = bf16[4,4,32,32]{3,2,1,0:T(8,128)(2,1)S(1)} copy-done((bf16[4,4,32,32]{3,2,1,0:T(8,128)(2,1)S(1)}, bf16[4,4,32,32]{3,2,1,0:T(8,128)(2,1)}, u32[]{:S(2)}) %copy-start.2) | copy-done | bytes 32792
  1.6 0.1 shard_map.86
  1.7 4.1 %collective-permute-start.4 = (bf16[2,32,128]{2,1,0:T(8,128)(2,1)S(1)}, bf16[2,32,128]{2,1,0:T(8,128)(2,1)S(1)}, u32[]{:S(2)}, u32[]{:S(2)}) collective-permute-start(bf16[2,32,128]{2,1,0:T(8,128)(2,1)S(1)} %get-tuple-element.41), channel_id=1, source_target_pairs={{0,16},{4,20},{8,24},{12,28},{16,0},{20,4},{24,8},{28,12},{1,17},{... | collective-permute-start | bytes 49160 | tf_op jit(solution)/shard_map/ppermute | solution.py:215
  5.8 0.1 shard_map.85
  5.9 0.1 collective-permute-start
  6.0 1.6 %collective-permute-start.1 = (bf16[32,512]{1,0:T(8,128)(2,1)S(1)}, bf16[32,512]{1,0:T(8,128)(2,1)S(1)}, u32[]{:S(2)}, u32[]{:S(2)}) collective-permute-start(bf16[32,512]{1,0:T(8,128)(2,1)S(1)} %get-tuple-element.38), channel_id=1, source_target_pairs={{0,2},{1,3},{2,0},{3,1},{4,6},{5,7},{6,4},{7,5},{8,10},{9,11},{10,... | collective-permute-start | bytes 98312 | tf_op jit(solution)/shard_map/ppermute | solution.py:215
  7.6 0.3 collective-permute-start.2
  7.9 0.0 collective-permute-done.4
  7.9 1.6 %collective-permute-start.5 = (bf16[1,2,32,128]{3,2,1,0:T(8,128)(2,1)S(1)}, bf16[1,2,32,128]{3,2,1,0:T(8,128)(2,1)S(1)}, u32[]{:S(2)}, u32[]{:S(2)}) collective-permute-start(bf16[1,2,32,128]{3,2,1,0:T(8,128)(2,1)S(1)} %get-tuple-element.70), channel_id=1, source_target_pairs={{0,8},{4,12},{8,0},{12,4},{16,24},{20,28},{24,16},{28,20},{1,9},{5... | collective-permute-start | bytes 49160 | tf_op jit(solution)/shard_map/ppermute | solution.py:215
  9.5 2.1 %collective-permute-done.5 = bf16[1,2,32,128]{3,2,1,0:T(8,128)(2,1)S(1)} collective-permute-done((bf16[1,2,32,128]{3,2,1,0:T(8,128)(2,1)S(1)}, bf16[1,2,32,128]{3,2,1,0:T(8,128)(2,1)S(1)}, u32[]{:S(2)}, u32[]{:S(2)}) %collective-permute-start.5) | collective-permute-done | bytes 16416 | tf_op jit(solution)/shard_map/ppermute | solution.py:215
  11.7 1.5 %collective-permute-start.6 = (bf16[4,32,128]{2,1,0:T(8,128)(2,1)S(1)}, bf16[4,32,128]{2,1,0:T(8,128)(2,1)S(1)}, u32[]{:S(2)}, u32[]{:S(2)}) collective-permute-start(bf16[4,32,128]{2,1,0:T(8,128)(2,1)S(1)} %maximum_bitcast_fusion.refs_3_), channel_id=1, source_target_pairs={{0,4},{4,0},{8,12},{12,8},{16,20},{20,16},{24,28},{28,24},{1,5},{5... | collective-permute-start | bytes 98312 | tf_op jit(solution)/shard_map/ppermute | solution.py:215
  13.2 0.0 collective-permute-done
  13.2 0.0 collective-permute-done.1
  13.2 0.0 collective-permute-done.2
  13.2 0.0 copy-start.4
  13.2 0.0 copy-start.5
  13.3 2.3 %collective-permute-done.6.refs_4_ = bf16[4,32,128]{2,1,0:T(8,128)(2,1)S(1)} collective-permute-done((bf16[4,32,128]{2,1,0:T(8,128)(2,1)S(1)}, bf16[4,32,128]{2,1,0:T(8,128)(2,1)S(1)}, u32[]{:S(2)}, u32[]{:S(2)}) %collective-permute-start.6) | collective-permute-done | bytes 32800 | tf_op jit(solution)/shard_map/ppermute | solution.py:215
  15.6 0.6 shard_map.87
  16.2 0.1 collective-permute-start.7
  16.3 1.6 %collective-permute-start.3 = (bf16[4,32,512]{2,1,0:T(8,128)(2,1)S(1)}, bf16[4,32,512]{2,1,0:T(8,128)(2,1)S(1)}, u32[]{:S(2)}, u32[]{:S(2)}) collective-permute-start(bf16[4,32,512]{2,1,0:T(8,128)(2,1)S(1)} %pad_maximum_fusion.1.refs_1_), channel_id=1, source_target_pairs={{0,4},{4,0},{8,12},{12,8},{16,20},{20,16},{24,28},{28,24},{1,5},{5... | collective-permute-start | bytes 393224 | tf_op jit(solution)/shard_map/ppermute | solution.py:215
  17.9 1.3 %collective-permute-start.10 = (bf16[512,128]{1,0:T(8,128)(2,1)S(1)}, bf16[512,128]{1,0:T(8,128)(2,1)S(1)}, u32[]{:S(2)}, u32[]{:S(2)}) collective-permute-start(bf16[512,128]{1,0:T(8,128)(2,1)S(1)} %get-tuple-element.48.refs_3_), channel_id=1, source_target_pairs={{0,3},{1,2},{2,1},{3,0},{4,7},{5,6},{6,5},{7,4},{8,11},{9,10},{10,... | collective-permute-start | bytes 393224 | tf_op jit(solution)/shard_map/ppermute | solution.py:215
  19.2 0.5 collective-permute-start.9
  19.7 0.0 collective-permute-done.7.refs_4_
  19.7 0.7 %collective-permute-start.8 = (bf16[4,32,512]{2,1,0:T(8,128)(2,1)S(1)}, bf16[4,32,512]{2,1,0:T(8,128)(2,1)S(1)}, u32[]{:S(2)}, u32[]{:S(2)}) collective-permute-start(bf16[4,32,512]{2,1,0:T(8,128)(2,1)S(1)} %pad_maximum_fusion.1.refs_1_), channel_id=1, source_target_pairs={{4,8},{8,4},{12,16},{16,12},{20,24},{24,20},{5,9},{9,5},{13,17},{1... | collective-permute-start | bytes 393224 | tf_op jit(solution)/shard_map/ppermute | solution.py:235
  20.4 1.9 %collective-permute-done.3.refs_0_ = bf16[4,32,512]{2,1,0:T(8,128)(2,1)S(1)} collective-permute-done((bf16[4,32,512]{2,1,0:T(8,128)(2,1)S(1)}, bf16[4,32,512]{2,1,0:T(8,128)(2,1)S(1)}, u32[]{:S(2)}, u32[]{:S(2)}) %collective-permute-start.3) | collective-permute-done | bytes 131104 | tf_op jit(solution)/shard_map/ppermute | solution.py:215
  22.2 0.0 collective-permute-start.12
  22.2 1.5 %collective-permute-start.13 = (bf16[256,128]{1,0:T(8,128)(2,1)S(1)}, bf16[256,128]{1,0:T(8,128)(2,1)S(1)}, u32[]{:S(2)}, u32[]{:S(2)}) collective-permute-start(bf16[256,128]{1,0:T(8,128)(2,1)S(1)} %get-tuple-element.56), channel_id=1, source_target_pairs={{0,2},{1,3},{2,0},{3,1},{4,6},{5,7},{6,4},{7,5},{8,10},{9,11},{10,... | collective-permute-start | bytes 196616 | tf_op jit(solution)/shard_map/ppermute | solution.py:215
  23.7 0.0 collective-permute-done.10.refs_6_
  23.7 1.2 %collective-permute-start.14 = (bf16[256,128]{1,0:T(8,128)(2,1)S(1)}, bf16[256,128]{1,0:T(8,128)(2,1)S(1)}, u32[]{:S(2)}, u32[]{:S(2)}) collective-permute-start(bf16[256,128]{1,0:T(8,128)(2,1)S(1)} %get-tuple-element.57), channel_id=1, source_target_pairs={{0,3},{1,2},{2,1},{3,0},{4,7},{5,6},{6,5},{7,4},{8,11},{9,10},{10,... | collective-permute-start | bytes 196616 | tf_op jit(solution)/shard_map/ppermute | solution.py:215
  25.0 1.9 %collective-permute-done.9.refs_5_ = bf16[512,128]{1,0:T(8,128)(2,1)S(1)} collective-permute-done((bf16[512,128]{1,0:T(8,128)(2,1)S(1)}, bf16[512,128]{1,0:T(8,128)(2,1)S(1)}, u32[]{:S(2)}, u32[]{:S(2)}) %collective-permute-start.9) | collective-permute-done | bytes 131104 | tf_op jit(solution)/shard_map/ppermute | solution.py:215
  26.8 0.0 collective-permute-done.8.refs_2_
  26.8 1.5 %shard_map.88 = (f32[432,128]{1,0:T(8,128)S(1)}, bf16[432,128]{1,0:T(8,128)(2,1)S(1)}, bf16[10,64,128]{2,1,0:T(8,128)(2,1)S(1)}) custom-call(bf16[4,32,512]{2,1,0:T(8,128)(2,1)S(1)} %collective-permute-done.3.refs_0_, bf16[4,32,512]{2,1,0:T(8,128)(2,1)S(1)} %pad_maximum_fusion.1.refs_1_, bf16[4,32,512]{2,1,0:T(8,128)(2,1)S(1)} %collective-permute-done.8.refs_2_, ...), custom_call_target="tpu_custom_call" | custom-call | tf_op jit(solution)/shard_map/pallas_call | solution.py:16
  28.3 0.0 copy-start.1
  28.4 1.7 %collective-permute-start.11 = (bf16[432,128]{1,0:T(8,128)(2,1)S(1)}, bf16[432,128]{1,0:T(8,128)(2,1)S(1)}, u32[]{:S(2)}, u32[]{:S(2)}) collective-permute-start(bf16[432,128]{1,0:T(8,128)(2,1)S(1)} %get-tuple-element.53), channel_id=1, source_target_pairs={{0,4},{4,0},{8,12},{12,8},{16,20},{20,16},{24,28},{28,24},{1,5},{5... | collective-permute-start | bytes 331784 | tf_op jit(solution)/shard_map/ppermute | solution.py:215
  30.0 0.0 collective-permute-done.12
  30.1 0.0 collective-permute-done.13
  30.1 2.6 %collective-permute-start.15 = (bf16[256,128]{1,0:T(8,128)(2,1)S(1)}, bf16[256,128]{1,0:T(8,128)(2,1)S(1)}, u32[]{:S(2)}, u32[]{:S(2)}) collective-permute-start(bf16[256,128]{1,0:T(8,128)(2,1)S(1)} %add_convert_fusion.3), channel_id=1, source_target_pairs={{0,16},{4,20},{8,24},{12,28},{16,0},{20,4},{24,8},{28,12},{1,17},{... | collective-permute-start | bytes 196616 | tf_op jit(solution)/shard_map/ppermute | solution.py:215
  32.7 0.7 %collective-permute-start.19 = (bf16[10,64,128]{2,1,0:T(8,128)(2,1)S(1)}, bf16[10,64,128]{2,1,0:T(8,128)(2,1)S(1)}, u32[]{:S(2)}, u32[]{:S(2)}) collective-permute-start(bf16[10,64,128]{2,1,0:T(8,128)(2,1)S(1)} %get-tuple-element.60.own), channel_id=1, source_target_pairs={{4,8},{8,4},{12,16},{16,12},{20,24},{24,20},{5,9},{9,5},{13,17},{1... | collective-permute-start | bytes 491528 | tf_op jit(solution)/shard_map/ppermute | solution.py:235
  33.3 3.9 %collective-permute-start.18 = (bf16[10,64,128]{2,1,0:T(8,128)(2,1)S(1)}, bf16[10,64,128]{2,1,0:T(8,128)(2,1)S(1)}, u32[]{:S(2)}, u32[]{:S(2)}) collective-permute-start(bf16[10,64,128]{2,1,0:T(8,128)(2,1)S(1)} %get-tuple-element.60.own), channel_id=1, source_target_pairs={{0,4},{4,0},{8,12},{12,8},{16,20},{20,16},{24,28},{28,24},{1,5},{5... | collective-permute-start | bytes 491528 | tf_op jit(solution)/shard_map/ppermute | solution.py:215
  37.3 0.0 collective-permute-done.15
  37.3 0.0 collective-permute-done.11
  37.3 1.5 %collective-permute-start.16 = (bf16[432,128]{1,0:T(8,128)(2,1)S(1)}, bf16[432,128]{1,0:T(8,128)(2,1)S(1)}, u32[]{:S(2)}, u32[]{:S(2)}) collective-permute-start(bf16[432,128]{1,0:T(8,128)(2,1)S(1)} %add_convert_fusion.1), channel_id=1, source_target_pairs={{0,16},{4,20},{8,24},{12,28},{16,0},{20,4},{24,8},{28,12},{1,17},{... | collective-permute-start | bytes 331784 | tf_op jit(solution)/shard_map/ppermute | solution.py:215
  38.9 1.0 %collective-permute-start.17 = (bf16[256,128]{1,0:T(8,128)(2,1)S(1)}, bf16[256,128]{1,0:T(8,128)(2,1)S(1)}, u32[]{:S(2)}, u32[]{:S(2)}) collective-permute-start(bf16[256,128]{1,0:T(8,128)(2,1)S(1)} %add_convert_fusion.2), channel_id=1, source_target_pairs={{0,8},{4,12},{8,0},{12,4},{16,24},{20,28},{24,16},{28,20},{1,9},{5... | collective-permute-start | bytes 196616 | tf_op jit(solution)/shard_map/ppermute | solution.py:215
  39.9 0.0 collective-permute-done.19.odd
  39.9 2.9 %collective-permute-done.18.even = bf16[10,64,128]{2,1,0:T(8,128)(2,1)S(1)} collective-permute-done((bf16[10,64,128]{2,1,0:T(8,128)(2,1)S(1)}, bf16[10,64,128]{2,1,0:T(8,128)(2,1)S(1)}, u32[]{:S(2)}, u32[]{:S(2)}) %collective-permute-start.18) | collective-permute-done | bytes 163872 | tf_op jit(solution)/shard_map/ppermute | solution.py:215
  42.8 0.4 collective-permute-done.17
  43.2 2.9 %collective-permute-done.16 = bf16[432,128]{1,0:T(8,128)(2,1)S(1)} collective-permute-done((bf16[432,128]{1,0:T(8,128)(2,1)S(1)}, bf16[432,128]{1,0:T(8,128)(2,1)S(1)}, u32[]{:S(2)}, u32[]{:S(2)}) %collective-permute-start.16) | collective-permute-done | bytes 110624 | tf_op jit(solution)/shard_map/ppermute | solution.py:215
  46.2 0.1 collective-permute-start.20
  46.3 1.7 %shard_map.89 = bf16[8,64,128]{2,1,0:T(8,128)(2,1)} custom-call(bf16[10,64,128]{2,1,0:T(8,128)(2,1)S(1)} %collective-permute-done.18.even, bf16[10,64,128]{2,1,0:T(8,128)(2,1)S(1)} %get-tuple-element.60.own, bf16[10,64,128]{2,1,0:T(8,128)(2,1)S(1)} %collective-permute-done.19.odd, bf16[3,3,3,128,128]{4,3,2,1,0:T(8,128)(2,1)S(1)} %copy-done.1), custom_call_target="tpu_custom_call" | custom-call | tf_op jit(solution)/shard_map/pallas_call | solution.py:16
  48.0 2.9 %collective-permute-done.20 = bf16[432,128]{1,0:T(8,128)(2,1)S(1)} collective-permute-done((bf16[432,128]{1,0:T(8,128)(2,1)S(1)}, bf16[432,128]{1,0:T(8,128)(2,1)S(1)}, u32[]{:S(2)}, u32[]{:S(2)}) %collective-permute-start.20) | collective-permute-done | bytes 110624 | tf_op jit(solution)/shard_map/ppermute | solution.py:215
  51.1 0.1 collective-permute-start.26
  51.2 2.9 %collective-permute-start.24 = (bf16[688,128]{1,0:T(8,128)(2,1)S(1)}, bf16[688,128]{1,0:T(8,128)(2,1)S(1)}, u32[]{:S(2)}, u32[]{:S(2)}) collective-permute-start(bf16[688,128]{1,0:T(8,128)(2,1)S(1)} %pad_maximum_fusion.refs_0_), channel_id=1, source_target_pairs={{0,4},{4,0},{8,12},{12,8},{16,20},{20,16},{24,28},{28,24},{1,5},{5... | collective-permute-start | bytes 528392 | tf_op jit(solution)/shard_map/ppermute | solution.py:215
  54.1 0.5 collective-permute-start.22
  54.6 0.0 collective-permute-start.21
  54.6 3.0 %collective-permute-done.26.refs_6_ = bf16[688,128]{1,0:T(8,128)(2,1)S(1)} collective-permute-done((bf16[688,128]{1,0:T(8,128)(2,1)S(1)}, bf16[688,128]{1,0:T(8,128)(2,1)S(1)}, u32[]{:S(2)}, u32[]{:S(2)}) %collective-permute-start.26) | collective-permute-done | bytes 176160 | tf_op jit(solution)/shard_map/ppermute | solution.py:225
  57.6 1.8 %collective-permute-done.24.refs_4_ = bf16[688,128]{1,0:T(8,128)(2,1)S(1)} collective-permute-done((bf16[688,128]{1,0:T(8,128)(2,1)S(1)}, bf16[688,128]{1,0:T(8,128)(2,1)S(1)}, u32[]{:S(2)}, u32[]{:S(2)}) %collective-permute-start.24) | collective-permute-done | bytes 176160 | tf_op jit(solution)/shard_map/ppermute | solution.py:215
  59.4 0.2 collective-permute-done.22.refs_2_
  59.5 0.3 collective-permute-start.23
  59.9 0.0 collective-permute-done.21.refs_1_
  59.9 0.0 collective-permute-done.27.refs_7_
  59.9 0.9 %collective-permute-done.25.refs_5_ = bf16[688,128]{1,0:T(8,128)(2,1)S(1)} collective-permute-done((bf16[688,128]{1,0:T(8,128)(2,1)S(1)}, bf16[688,128]{1,0:T(8,128)(2,1)S(1)}, u32[]{:S(2)}, u32[]{:S(2)}) %collective-permute-start.25) | collective-permute-done | bytes 176160 | tf_op jit(solution)/shard_map/ppermute | solution.py:215
  60.8 0.3 collective-permute-done.23.refs_3_
  61.0 1.3 %shard_map.90 = (bf16[27,4,2,16,128]{4,3,2,1,0:T(8,128)(2,1)}, bf16[2,4,128,256]{3,2,1,0:T(8,128)(2,1)}) custom-call(bf16[688,128]{1,0:T(8,128)(2,1)S(1)} %pad_maximum_fusion.refs_0_, bf16[688,128]{1,0:T(8,128)(2,1)S(1)} %collective-permute-done.21.refs_1_, bf16[688,128]{1,0:T(8,128)(2,1)S(1)} %collective-permute-done.22.refs_2_, ...), custom_call_target="tpu_custom_call" | custom-call | tf_op jit(solution)/shard_map/pallas_call | solution.py:16
  (21 shorter events, 0.3 us)
Async XLA Ops:
  0.6 8.9 %copy-start = (bf16[2,2,2,128,256]{4,3,2,1,0:T(8,128)(2,1)S(1)}, bf16[2,2,2,128,256]{4,3,2,1,0:T(8,128)(2,1)}, u32[]{:S(2)}) copy-start(bf16[2,2,2,128,256]{4,3,2,1,0:T(8,128)(2,1)} %param.9) | copy-start | bytes 1572868
  0.6 1.0 %copy-start.2 = (bf16[4,4,32,32]{3,2,1,0:T(8,128)(2,1)S(1)}, bf16[4,4,32,32]{3,2,1,0:T(8,128)(2,1)}, u32[]{:S(2)}) copy-start(bf16[4,4,32,32]{3,2,1,0:T(8,128)(2,1)} %param.11) | copy-start | bytes 98308
  1.6 4.2 %copy-start.3 = (bf16[1,8,64,128]{3,2,1,0:T(8,128)(2,1)S(1)}, bf16[1,8,64,128]{3,2,1,0:T(8,128)(2,1)}, u32[]{:S(2)}) copy-start(bf16[1,8,64,128]{3,2,1,0:T(8,128)(2,1)} %param.6) | copy-start | bytes 393220
  1.7 6.2 %collective-permute-start.4 = (bf16[2,32,128]{2,1,0:T(8,128)(2,1)S(1)}, bf16[2,32,128]{2,1,0:T(8,128)(2,1)S(1)}, u32[]{:S(2)}, u32[]{:S(2)}) collective-permute-start(bf16[2,32,128]{2,1,0:T(8,128)(2,1)S(1)} %get-tuple-element.41), channel_id=1, source_target_pairs={{0,16},{4,20},{8,24},{12,28},{16,0},{20,4},{24,8},{28,12},{1,17},{... | collective-permute-start | bytes 49160 | tf_op jit(solution)/shard_map/ppermute | solution.py:215
  5.9 7.3 %collective-permute-start = (bf16[32,512]{1,0:T(8,128)(2,1)S(1)}, bf16[32,512]{1,0:T(8,128)(2,1)S(1)}, u32[]{:S(2)}, u32[]{:S(2)}) collective-permute-start(bf16[32,512]{1,0:T(8,128)(2,1)S(1)} %get-tuple-element.37), channel_id=1, source_target_pairs={{0,1},{1,0},{2,3},{3,2},{4,5},{5,4},{6,7},{7,6},{8,9},{9,8},{10,11... | collective-permute-start | bytes 98312 | tf_op jit(solution)/shard_map/ppermute | solution.py:215
  6.0 7.2 %collective-permute-start.1 = (bf16[32,512]{1,0:T(8,128)(2,1)S(1)}, bf16[32,512]{1,0:T(8,128)(2,1)S(1)}, u32[]{:S(2)}, u32[]{:S(2)}) collective-permute-start(bf16[32,512]{1,0:T(8,128)(2,1)S(1)} %get-tuple-element.38), channel_id=1, source_target_pairs={{0,2},{1,3},{2,0},{3,1},{4,6},{5,7},{6,4},{7,5},{8,10},{9,11},{10,... | collective-permute-start | bytes 98312 | tf_op jit(solution)/shard_map/ppermute | solution.py:215
  7.6 5.7 %collective-permute-start.2 = (bf16[32,512]{1,0:T(8,128)(2,1)S(1)}, bf16[32,512]{1,0:T(8,128)(2,1)S(1)}, u32[]{:S(2)}, u32[]{:S(2)}) collective-permute-start(bf16[32,512]{1,0:T(8,128)(2,1)S(1)} %get-tuple-element.39), channel_id=1, source_target_pairs={{0,3},{1,2},{2,1},{3,0},{4,7},{5,6},{6,5},{7,4},{8,11},{9,10},{10,... | collective-permute-start | bytes 98312 | tf_op jit(solution)/shard_map/ppermute | solution.py:215
  7.9 3.8 %collective-permute-start.5 = (bf16[1,2,32,128]{3,2,1,0:T(8,128)(2,1)S(1)}, bf16[1,2,32,128]{3,2,1,0:T(8,128)(2,1)S(1)}, u32[]{:S(2)}, u32[]{:S(2)}) collective-permute-start(bf16[1,2,32,128]{3,2,1,0:T(8,128)(2,1)S(1)} %get-tuple-element.70), channel_id=1, source_target_pairs={{0,8},{4,12},{8,0},{12,4},{16,24},{20,28},{24,16},{28,20},{1,9},{5... | collective-permute-start | bytes 49160 | tf_op jit(solution)/shard_map/ppermute | solution.py:215
  11.7 3.9 %collective-permute-start.6 = (bf16[4,32,128]{2,1,0:T(8,128)(2,1)S(1)}, bf16[4,32,128]{2,1,0:T(8,128)(2,1)S(1)}, u32[]{:S(2)}, u32[]{:S(2)}) collective-permute-start(bf16[4,32,128]{2,1,0:T(8,128)(2,1)S(1)} %maximum_bitcast_fusion.refs_3_), channel_id=1, source_target_pairs={{0,4},{4,0},{8,12},{12,8},{16,20},{20,16},{24,28},{28,24},{1,5},{5... | collective-permute-start | bytes 98312 | tf_op jit(solution)/shard_map/ppermute | solution.py:215
  13.2 2.4 %copy-start.4 = (bf16[1,8,64,128]{3,2,1,0:T(8,128)(2,1)S(1)}, bf16[1,8,64,128]{3,2,1,0:T(8,128)(2,1)}, u32[]{:S(2)}) copy-start(bf16[1,8,64,128]{3,2,1,0:T(8,128)(2,1)} %param.7) | copy-start | bytes 393220
  13.2 2.4 %copy-start.5 = (bf16[1,8,64,128]{3,2,1,0:T(8,128)(2,1)S(1)}, bf16[1,8,64,128]{3,2,1,0:T(8,128)(2,1)}, u32[]{:S(2)}) copy-start(bf16[1,8,64,128]{3,2,1,0:T(8,128)(2,1)} %param.10) | copy-start | bytes 393220
  16.2 3.5 %collective-permute-start.7 = (bf16[512,128]{1,0:T(8,128)(2,1)S(1)}, bf16[512,128]{1,0:T(8,128)(2,1)S(1)}, u32[]{:S(2)}, u32[]{:S(2)}) collective-permute-start(bf16[512,128]{1,0:T(8,128)(2,1)S(1)} %get-tuple-element.48.refs_3_), channel_id=1, source_target_pairs={{0,1},{1,0},{2,3},{3,2},{4,5},{5,4},{6,7},{7,6},{8,9},{9,8},{10,11... | collective-permute-start | bytes 393224 | tf_op jit(solution)/shard_map/ppermute | solution.py:215
  16.3 5.9 %collective-permute-start.3 = (bf16[4,32,512]{2,1,0:T(8,128)(2,1)S(1)}, bf16[4,32,512]{2,1,0:T(8,128)(2,1)S(1)}, u32[]{:S(2)}, u32[]{:S(2)}) collective-permute-start(bf16[4,32,512]{2,1,0:T(8,128)(2,1)S(1)} %pad_maximum_fusion.1.refs_1_), channel_id=1, source_target_pairs={{0,4},{4,0},{8,12},{12,8},{16,20},{20,16},{24,28},{28,24},{1,5},{5... | collective-permute-start | bytes 393224 | tf_op jit(solution)/shard_map/ppermute | solution.py:215
  17.9 5.8 %collective-permute-start.10 = (bf16[512,128]{1,0:T(8,128)(2,1)S(1)}, bf16[512,128]{1,0:T(8,128)(2,1)S(1)}, u32[]{:S(2)}, u32[]{:S(2)}) collective-permute-start(bf16[512,128]{1,0:T(8,128)(2,1)S(1)} %get-tuple-element.48.refs_3_), channel_id=1, source_target_pairs={{0,3},{1,2},{2,1},{3,0},{4,7},{5,6},{6,5},{7,4},{8,11},{9,10},{10,... | collective-permute-start | bytes 393224 | tf_op jit(solution)/shard_map/ppermute | solution.py:215
  19.2 7.7 %collective-permute-start.9 = (bf16[512,128]{1,0:T(8,128)(2,1)S(1)}, bf16[512,128]{1,0:T(8,128)(2,1)S(1)}, u32[]{:S(2)}, u32[]{:S(2)}) collective-permute-start(bf16[512,128]{1,0:T(8,128)(2,1)S(1)} %get-tuple-element.48.refs_3_), channel_id=1, source_target_pairs={{0,2},{1,3},{2,0},{3,1},{4,6},{5,7},{6,4},{7,5},{8,10},{9,11},{10,... | collective-permute-start | bytes 393224 | tf_op jit(solution)/shard_map/ppermute | solution.py:215
  19.7 7.1 %collective-permute-start.8 = (bf16[4,32,512]{2,1,0:T(8,128)(2,1)S(1)}, bf16[4,32,512]{2,1,0:T(8,128)(2,1)S(1)}, u32[]{:S(2)}, u32[]{:S(2)}) collective-permute-start(bf16[4,32,512]{2,1,0:T(8,128)(2,1)S(1)} %pad_maximum_fusion.1.refs_1_), channel_id=1, source_target_pairs={{4,8},{8,4},{12,16},{16,12},{20,24},{24,20},{5,9},{9,5},{13,17},{1... | collective-permute-start | bytes 393224 | tf_op jit(solution)/shard_map/ppermute | solution.py:235
  22.2 7.8 %collective-permute-start.12 = (bf16[256,128]{1,0:T(8,128)(2,1)S(1)}, bf16[256,128]{1,0:T(8,128)(2,1)S(1)}, u32[]{:S(2)}, u32[]{:S(2)}) collective-permute-start(bf16[256,128]{1,0:T(8,128)(2,1)S(1)} %get-tuple-element.55), channel_id=1, source_target_pairs={{0,1},{1,0},{2,3},{3,2},{4,5},{5,4},{6,7},{7,6},{8,9},{9,8},{10,11... | collective-permute-start | bytes 196616 | tf_op jit(solution)/shard_map/ppermute | solution.py:215
  22.2 7.8 %collective-permute-start.13 = (bf16[256,128]{1,0:T(8,128)(2,1)S(1)}, bf16[256,128]{1,0:T(8,128)(2,1)S(1)}, u32[]{:S(2)}, u32[]{:S(2)}) collective-permute-start(bf16[256,128]{1,0:T(8,128)(2,1)S(1)} %get-tuple-element.56), channel_id=1, source_target_pairs={{0,2},{1,3},{2,0},{3,1},{4,6},{5,7},{6,4},{7,5},{8,10},{9,11},{10,... | collective-permute-start | bytes 196616 | tf_op jit(solution)/shard_map/ppermute | solution.py:215
  23.7 6.3 %collective-permute-start.14 = (bf16[256,128]{1,0:T(8,128)(2,1)S(1)}, bf16[256,128]{1,0:T(8,128)(2,1)S(1)}, u32[]{:S(2)}, u32[]{:S(2)}) collective-permute-start(bf16[256,128]{1,0:T(8,128)(2,1)S(1)} %get-tuple-element.57), channel_id=1, source_target_pairs={{0,3},{1,2},{2,1},{3,0},{4,7},{5,6},{6,5},{7,4},{8,11},{9,10},{10,... | collective-permute-start | bytes 196616 | tf_op jit(solution)/shard_map/ppermute | solution.py:215
  28.3 17.9 %copy-start.1 = (bf16[3,3,3,128,128]{4,3,2,1,0:T(8,128)(2,1)S(1)}, bf16[3,3,3,128,128]{4,3,2,1,0:T(8,128)(2,1)}, u32[]{:S(2)}) copy-start(bf16[3,3,3,128,128]{4,3,2,1,0:T(8,128)(2,1)} %weight.1) | copy-start | bytes 2654212
  28.4 8.9 %collective-permute-start.11 = (bf16[432,128]{1,0:T(8,128)(2,1)S(1)}, bf16[432,128]{1,0:T(8,128)(2,1)S(1)}, u32[]{:S(2)}, u32[]{:S(2)}) collective-permute-start(bf16[432,128]{1,0:T(8,128)(2,1)S(1)} %get-tuple-element.53), channel_id=1, source_target_pairs={{0,4},{4,0},{8,12},{12,8},{16,20},{20,16},{24,28},{28,24},{1,5},{5... | collective-permute-start | bytes 331784 | tf_op jit(solution)/shard_map/ppermute | solution.py:215
  30.1 7.2 %collective-permute-start.15 = (bf16[256,128]{1,0:T(8,128)(2,1)S(1)}, bf16[256,128]{1,0:T(8,128)(2,1)S(1)}, u32[]{:S(2)}, u32[]{:S(2)}) collective-permute-start(bf16[256,128]{1,0:T(8,128)(2,1)S(1)} %add_convert_fusion.3), channel_id=1, source_target_pairs={{0,16},{4,20},{8,24},{12,28},{16,0},{20,4},{24,8},{28,12},{1,17},{... | collective-permute-start | bytes 196616 | tf_op jit(solution)/shard_map/ppermute | solution.py:215
  32.7 7.2 %collective-permute-start.19 = (bf16[10,64,128]{2,1,0:T(8,128)(2,1)S(1)}, bf16[10,64,128]{2,1,0:T(8,128)(2,1)S(1)}, u32[]{:S(2)}, u32[]{:S(2)}) collective-permute-start(bf16[10,64,128]{2,1,0:T(8,128)(2,1)S(1)} %get-tuple-element.60.own), channel_id=1, source_target_pairs={{4,8},{8,4},{12,16},{16,12},{20,24},{24,20},{5,9},{9,5},{13,17},{1... | collective-permute-start | bytes 491528 | tf_op jit(solution)/shard_map/ppermute | solution.py:235
  33.3 9.5 %collective-permute-start.18 = (bf16[10,64,128]{2,1,0:T(8,128)(2,1)S(1)}, bf16[10,64,128]{2,1,0:T(8,128)(2,1)S(1)}, u32[]{:S(2)}, u32[]{:S(2)}) collective-permute-start(bf16[10,64,128]{2,1,0:T(8,128)(2,1)S(1)} %get-tuple-element.60.own), channel_id=1, source_target_pairs={{0,4},{4,0},{8,12},{12,8},{16,20},{20,16},{24,28},{28,24},{1,5},{5... | collective-permute-start | bytes 491528 | tf_op jit(solution)/shard_map/ppermute | solution.py:215
  37.3 8.8 %collective-permute-start.16 = (bf16[432,128]{1,0:T(8,128)(2,1)S(1)}, bf16[432,128]{1,0:T(8,128)(2,1)S(1)}, u32[]{:S(2)}, u32[]{:S(2)}) collective-permute-start(bf16[432,128]{1,0:T(8,128)(2,1)S(1)} %add_convert_fusion.1), channel_id=1, source_target_pairs={{0,16},{4,20},{8,24},{12,28},{16,0},{20,4},{24,8},{28,12},{1,17},{... | collective-permute-start | bytes 331784 | tf_op jit(solution)/shard_map/ppermute | solution.py:215
  38.9 4.3 %collective-permute-start.17 = (bf16[256,128]{1,0:T(8,128)(2,1)S(1)}, bf16[256,128]{1,0:T(8,128)(2,1)S(1)}, u32[]{:S(2)}, u32[]{:S(2)}) collective-permute-start(bf16[256,128]{1,0:T(8,128)(2,1)S(1)} %add_convert_fusion.2), channel_id=1, source_target_pairs={{0,8},{4,12},{8,0},{12,4},{16,24},{20,28},{24,16},{28,20},{1,9},{5... | collective-permute-start | bytes 196616 | tf_op jit(solution)/shard_map/ppermute | solution.py:215
  46.2 4.8 %collective-permute-start.20 = (bf16[432,128]{1,0:T(8,128)(2,1)S(1)}, bf16[432,128]{1,0:T(8,128)(2,1)S(1)}, u32[]{:S(2)}, u32[]{:S(2)}) collective-permute-start(bf16[432,128]{1,0:T(8,128)(2,1)S(1)} %add_convert_fusion), channel_id=1, source_target_pairs={{0,8},{4,12},{8,0},{12,4},{16,24},{20,28},{24,16},{28,20},{1,9},{5... | collective-permute-start | bytes 331784 | tf_op jit(solution)/shard_map/ppermute | solution.py:215
  51.1 6.5 %collective-permute-start.26 = (bf16[688,128]{1,0:T(8,128)(2,1)S(1)}, bf16[688,128]{1,0:T(8,128)(2,1)S(1)}, u32[]{:S(2)}, u32[]{:S(2)}) collective-permute-start(bf16[688,128]{1,0:T(8,128)(2,1)S(1)} %pad_maximum_fusion.refs_0_), channel_id=1, source_target_pairs={{0,6},{1,7},{2,4},{3,5},{4,2},{5,3},{6,0},{7,1},{8,14},{9,15},{10,... | collective-permute-start | bytes 528392 | tf_op jit(solution)/shard_map/ppermute | solution.py:225
  51.2 8.2 %collective-permute-start.24 = (bf16[688,128]{1,0:T(8,128)(2,1)S(1)}, bf16[688,128]{1,0:T(8,128)(2,1)S(1)}, u32[]{:S(2)}, u32[]{:S(2)}) collective-permute-start(bf16[688,128]{1,0:T(8,128)(2,1)S(1)} %pad_maximum_fusion.refs_0_), channel_id=1, source_target_pairs={{0,4},{4,0},{8,12},{12,8},{16,20},{20,16},{24,28},{28,24},{1,5},{5... | collective-permute-start | bytes 528392 | tf_op jit(solution)/shard_map/ppermute | solution.py:215
  54.1 5.5 %collective-permute-start.22 = (bf16[688,128]{1,0:T(8,128)(2,1)S(1)}, bf16[688,128]{1,0:T(8,128)(2,1)S(1)}, u32[]{:S(2)}, u32[]{:S(2)}) collective-permute-start(bf16[688,128]{1,0:T(8,128)(2,1)S(1)} %pad_maximum_fusion.refs_0_), channel_id=1, source_target_pairs={{0,2},{1,3},{2,0},{3,1},{4,6},{5,7},{6,4},{7,5},{8,10},{9,11},{10,... | collective-permute-start | bytes 528392 | tf_op jit(solution)/shard_map/ppermute | solution.py:215
  54.6 5.3 %collective-permute-start.21 = (bf16[688,128]{1,0:T(8,128)(2,1)S(1)}, bf16[688,128]{1,0:T(8,128)(2,1)S(1)}, u32[]{:S(2)}, u32[]{:S(2)}) collective-permute-start(bf16[688,128]{1,0:T(8,128)(2,1)S(1)} %pad_maximum_fusion.refs_0_), channel_id=1, source_target_pairs={{0,1},{1,0},{2,3},{3,2},{4,5},{5,4},{6,7},{7,6},{8,9},{9,8},{10,11... | collective-permute-start | bytes 528392 | tf_op jit(solution)/shard_map/ppermute | solution.py:215
  57.6 2.3 %collective-permute-start.27 = (bf16[688,128]{1,0:T(8,128)(2,1)S(1)}, bf16[688,128]{1,0:T(8,128)(2,1)S(1)}, u32[]{:S(2)}, u32[]{:S(2)}) collective-permute-start(bf16[688,128]{1,0:T(8,128)(2,1)S(1)} %collective-permute-done.26.refs_6_), channel_id=1, source_target_pairs={{0,1},{1,0},{2,3},{3,2},{4,5},{5,4},{6,7},{7,6},{8,9},{9,8},{10,11... | collective-permute-start | bytes 528392 | tf_op jit(solution)/shard_map/ppermute | solution.py:215
  59.4 1.4 %collective-permute-start.25 = (bf16[688,128]{1,0:T(8,128)(2,1)S(1)}, bf16[688,128]{1,0:T(8,128)(2,1)S(1)}, u32[]{:S(2)}, u32[]{:S(2)}) collective-permute-start(bf16[688,128]{1,0:T(8,128)(2,1)S(1)} %collective-permute-done.24.refs_4_), channel_id=1, source_target_pairs={{0,1},{1,0},{2,3},{3,2},{4,5},{5,4},{6,7},{7,6},{8,9},{9,8},{10,11... | collective-permute-start | bytes 528392 | tf_op jit(solution)/shard_map/ppermute | solution.py:215
  59.5 1.5 %collective-permute-start.23 = (bf16[688,128]{1,0:T(8,128)(2,1)S(1)}, bf16[688,128]{1,0:T(8,128)(2,1)S(1)}, u32[]{:S(2)}, u32[]{:S(2)}) collective-permute-start(bf16[688,128]{1,0:T(8,128)(2,1)S(1)} %collective-permute-done.22.refs_2_), channel_id=1, source_target_pairs={{0,1},{1,0},{2,3},{3,2},{4,5},{5,4},{6,7},{7,6},{8,9},{9,8},{10,11... | collective-permute-start | bytes 528392 | tf_op jit(solution)/shard_map/ppermute | solution.py:215

commit v25 on v24

--- a/solution.py
+++ b/solution.py
@@ -344,7 +344,6 @@
     for index, code in enumerate(codes):
         down_other = swapped(down, "gz", code)
         if index == 0:
-            send, down_other = lax.optimization_barrier((send, down_other))
             conv = rounded(keep + send.astype(F32))
         else:
             conv_other = swapped(conv, "gz", codes[index - 1])

time: 62.5 us -> 62.5 us (level)
  starting transfers between devices: 31.4 us -> 30.4 us
  waiting for transfers between devices: 23.5 us -> 24.5 us
    ppermute x25, starting transfers between devices: 30 us -> 29 us  [swapped(): lax.ppermute(value, axis, [(i, i ^ code) for i in range(lax.axis_size(axi...]
    ppermute x25, waiting for transfers between devices: 20.5 us -> 21.5 us  [swapped(): lax.ppermute(value, axis, [(i, i ^ code) for i in range(lax.axis_size(axi...]
  transfers between devices with their start and end apart: 28 -> 28, of which waited for: 13 -> 12; matrix products, arithmetic and copies ran while one was open for 0% -> 0% of each run, Pallas kernels for 5% -> 5%
where the time goes in v25:
time: 62.5 us; the launch traced here: 62.3 us
  starting transfers between devices  30.4 us (49%)
  waiting for transfers between devices  24.5 us (39%)
  Pallas kernels  5.34 us (9%)
  local copies, waits for them, and re-layouts  1 us (2%)
  between operations  0.84 us (1%)
    ppermute x25, starting transfers between devices, swapped(): lax.ppermute(value, axis, [(i, i ^ code) for i in range(lax.axis_size(axi...  29 us
    ppermute x25, waiting for transfers between devices, swapped(): lax.ppermute(value, axis, [(i, i ^ code) for i in range(lax.axis_size(axi...  21.5 us
    pallas_call x6, Pallas kernels, call(): pl.pallas_call(kernel, out_shape=out_shape, scratch_shapes=list(scratch),...  5.34 us
    ppermute x1, waiting for transfers between devices, crossed(): return lax.ppermute(value, ('gz', 'gy'), pairs)  2.96 us
    ppermute x2, starting transfers between devices, odd_pairs(): return lax.ppermute(value, 'gz', pairs)  1.32 us
  transfers between devices with their start and end apart: 28, of which 12 were waited for; matrix products, arithmetic and copies ran while one was open for 0% of the time, Pallas kernels for 5%

profile of v25, /device:TPU:0, one launch (start us, length us, event | category | flops | bytes accessed | tf_op | source)
XLA Modules:
  0.0 62.3 jit_solution(16717577845052351357)
XLA Ops:
  0.6 0.0 copy-start
  0.7 1.0 %copy-done.2 = bf16[4,4,32,32]{3,2,1,0:T(8,128)(2,1)S(1)} copy-done((bf16[4,4,32,32]{3,2,1,0:T(8,128)(2,1)S(1)}, bf16[4,4,32,32]{3,2,1,0:T(8,128)(2,1)}, u32[]{:S(2)}) %copy-start.2) | copy-done | bytes 32792
  1.6 0.1 shard_map.86
  1.7 4.1 %collective-permute-start.4 = (bf16[2,32,128]{2,1,0:T(8,128)(2,1)S(1)}, bf16[2,32,128]{2,1,0:T(8,128)(2,1)S(1)}, u32[]{:S(2)}, u32[]{:S(2)}) collective-permute-start(bf16[2,32,128]{2,1,0:T(8,128)(2,1)S(1)} %get-tuple-element.39), channel_id=1, source_target_pairs={{0,16},{4,20},{8,24},{12,28},{16,0},{20,4},{24,8},{28,12},{1,17},{... | collective-permute-start | bytes 49160 | tf_op jit(solution)/shard_map/ppermute | solution.py:215
  5.8 0.1 shard_map.85
  5.9 0.1 collective-permute-start
  6.0 1.6 %collective-permute-start.1 = (bf16[32,512]{1,0:T(8,128)(2,1)S(1)}, bf16[32,512]{1,0:T(8,128)(2,1)S(1)}, u32[]{:S(2)}, u32[]{:S(2)}) collective-permute-start(bf16[32,512]{1,0:T(8,128)(2,1)S(1)} %get-tuple-element.36), channel_id=1, source_target_pairs={{0,2},{1,3},{2,0},{3,1},{4,6},{5,7},{6,4},{7,5},{8,10},{9,11},{10,... | collective-permute-start | bytes 98312 | tf_op jit(solution)/shard_map/ppermute | solution.py:215
  7.6 0.3 collective-permute-start.2
  7.9 0.0 collective-permute-done.4
  7.9 1.6 %collective-permute-start.5 = (bf16[1,2,32,128]{3,2,1,0:T(8,128)(2,1)S(1)}, bf16[1,2,32,128]{3,2,1,0:T(8,128)(2,1)S(1)}, u32[]{:S(2)}, u32[]{:S(2)}) collective-permute-start(bf16[1,2,32,128]{3,2,1,0:T(8,128)(2,1)S(1)} %get-tuple-element.66), channel_id=1, source_target_pairs={{0,8},{4,12},{8,0},{12,4},{16,24},{20,28},{24,16},{28,20},{1,9},{5... | collective-permute-start | bytes 49160 | tf_op jit(solution)/shard_map/ppermute | solution.py:215
  9.5 2.1 %collective-permute-done.5 = bf16[1,2,32,128]{3,2,1,0:T(8,128)(2,1)S(1)} collective-permute-done((bf16[1,2,32,128]{3,2,1,0:T(8,128)(2,1)S(1)}, bf16[1,2,32,128]{3,2,1,0:T(8,128)(2,1)S(1)}, u32[]{:S(2)}, u32[]{:S(2)}) %collective-permute-start.5) | collective-permute-done | bytes 16416 | tf_op jit(solution)/shard_map/ppermute | solution.py:215
  11.7 1.5 %collective-permute-start.6 = (bf16[4,32,128]{2,1,0:T(8,128)(2,1)S(1)}, bf16[4,32,128]{2,1,0:T(8,128)(2,1)S(1)}, u32[]{:S(2)}, u32[]{:S(2)}) collective-permute-start(bf16[4,32,128]{2,1,0:T(8,128)(2,1)S(1)} %maximum_bitcast_fusion.refs_3_), channel_id=1, source_target_pairs={{0,4},{4,0},{8,12},{12,8},{16,20},{20,16},{24,28},{28,24},{1,5},{5... | collective-permute-start | bytes 98312 | tf_op jit(solution)/shard_map/ppermute | solution.py:215
  13.2 0.0 collective-permute-done
  13.2 0.0 collective-permute-done.1
  13.2 0.0 collective-permute-done.2
  13.2 0.0 copy-start.4
  13.2 0.0 copy-start.5
  13.3 2.3 %collective-permute-done.6.refs_4_ = bf16[4,32,128]{2,1,0:T(8,128)(2,1)S(1)} collective-permute-done((bf16[4,32,128]{2,1,0:T(8,128)(2,1)S(1)}, bf16[4,32,128]{2,1,0:T(8,128)(2,1)S(1)}, u32[]{:S(2)}, u32[]{:S(2)}) %collective-permute-start.6) | collective-permute-done | bytes 32800 | tf_op jit(solution)/shard_map/ppermute | solution.py:215
  15.6 0.6 shard_map.87
  16.2 0.1 collective-permute-start.7
  16.3 1.6 %collective-permute-start.3 = (bf16[4,32,512]{2,1,0:T(8,128)(2,1)S(1)}, bf16[4,32,512]{2,1,0:T(8,128)(2,1)S(1)}, u32[]{:S(2)}, u32[]{:S(2)}) collective-permute-start(bf16[4,32,512]{2,1,0:T(8,128)(2,1)S(1)} %pad_maximum_fusion.1.refs_1_), channel_id=1, source_target_pairs={{0,4},{4,0},{8,12},{12,8},{16,20},{20,16},{24,28},{28,24},{1,5},{5... | collective-permute-start | bytes 393224 | tf_op jit(solution)/shard_map/ppermute | solution.py:215
  17.9 1.3 %collective-permute-start.10 = (bf16[512,128]{1,0:T(8,128)(2,1)S(1)}, bf16[512,128]{1,0:T(8,128)(2,1)S(1)}, u32[]{:S(2)}, u32[]{:S(2)}) collective-permute-start(bf16[512,128]{1,0:T(8,128)(2,1)S(1)} %get-tuple-element.46.refs_3_), channel_id=1, source_target_pairs={{0,3},{1,2},{2,1},{3,0},{4,7},{5,6},{6,5},{7,4},{8,11},{9,10},{10,... | collective-permute-start | bytes 393224 | tf_op jit(solution)/shard_map/ppermute | solution.py:215
  19.2 0.5 collective-permute-start.9
  19.7 0.0 collective-permute-done.7.refs_4_
  19.7 0.7 %collective-permute-start.8 = (bf16[4,32,512]{2,1,0:T(8,128)(2,1)S(1)}, bf16[4,32,512]{2,1,0:T(8,128)(2,1)S(1)}, u32[]{:S(2)}, u32[]{:S(2)}) collective-permute-start(bf16[4,32,512]{2,1,0:T(8,128)(2,1)S(1)} %pad_maximum_fusion.1.refs_1_), channel_id=1, source_target_pairs={{4,8},{8,4},{12,16},{16,12},{20,24},{24,20},{5,9},{9,5},{13,17},{1... | collective-permute-start | bytes 393224 | tf_op jit(solution)/shard_map/ppermute | solution.py:235
  20.4 1.9 %collective-permute-done.3.refs_0_ = bf16[4,32,512]{2,1,0:T(8,128)(2,1)S(1)} collective-permute-done((bf16[4,32,512]{2,1,0:T(8,128)(2,1)S(1)}, bf16[4,32,512]{2,1,0:T(8,128)(2,1)S(1)}, u32[]{:S(2)}, u32[]{:S(2)}) %collective-permute-start.3) | collective-permute-done | bytes 131104 | tf_op jit(solution)/shard_map/ppermute | solution.py:215
  22.2 0.0 collective-permute-start.13
  22.2 1.5 %collective-permute-start.14 = (bf16[256,128]{1,0:T(8,128)(2,1)S(1)}, bf16[256,128]{1,0:T(8,128)(2,1)S(1)}, u32[]{:S(2)}, u32[]{:S(2)}) collective-permute-start(bf16[256,128]{1,0:T(8,128)(2,1)S(1)} %get-tuple-element.54), channel_id=1, source_target_pairs={{0,2},{1,3},{2,0},{3,1},{4,6},{5,7},{6,4},{7,5},{8,10},{9,11},{10,... | collective-permute-start | bytes 196616 | tf_op jit(solution)/shard_map/ppermute | solution.py:215
  23.7 0.0 collective-permute-done.10.refs_6_
  23.7 1.2 %collective-permute-start.15 = (bf16[256,128]{1,0:T(8,128)(2,1)S(1)}, bf16[256,128]{1,0:T(8,128)(2,1)S(1)}, u32[]{:S(2)}, u32[]{:S(2)}) collective-permute-start(bf16[256,128]{1,0:T(8,128)(2,1)S(1)} %get-tuple-element.55), channel_id=1, source_target_pairs={{0,3},{1,2},{2,1},{3,0},{4,7},{5,6},{6,5},{7,4},{8,11},{9,10},{10,... | collective-permute-start | bytes 196616 | tf_op jit(solution)/shard_map/ppermute | solution.py:215
  25.0 1.9 %collective-permute-done.9.refs_5_ = bf16[512,128]{1,0:T(8,128)(2,1)S(1)} collective-permute-done((bf16[512,128]{1,0:T(8,128)(2,1)S(1)}, bf16[512,128]{1,0:T(8,128)(2,1)S(1)}, u32[]{:S(2)}, u32[]{:S(2)}) %collective-permute-start.9) | collective-permute-done | bytes 131104 | tf_op jit(solution)/shard_map/ppermute | solution.py:215
  26.8 0.0 collective-permute-done.8.refs_2_
  26.8 1.5 %shard_map.88 = (f32[432,128]{1,0:T(8,128)S(1)}, bf16[432,128]{1,0:T(8,128)(2,1)S(1)}, bf16[10,64,128]{2,1,0:T(8,128)(2,1)S(1)}) custom-call(bf16[4,32,512]{2,1,0:T(8,128)(2,1)S(1)} %collective-permute-done.3.refs_0_, bf16[4,32,512]{2,1,0:T(8,128)(2,1)S(1)} %pad_maximum_fusion.1.refs_1_, bf16[4,32,512]{2,1,0:T(8,128)(2,1)S(1)} %collective-permute-done.8.refs_2_, ...), custom_call_target="tpu_custom_call" | custom-call | tf_op jit(solution)/shard_map/pallas_call | solution.py:16
  28.3 0.0 copy-start.1
  28.4 1.7 %collective-permute-start.11 = (bf16[432,128]{1,0:T(8,128)(2,1)S(1)}, bf16[432,128]{1,0:T(8,128)(2,1)S(1)}, u32[]{:S(2)}, u32[]{:S(2)}) collective-permute-start(bf16[432,128]{1,0:T(8,128)(2,1)S(1)} %get-tuple-element.51), channel_id=1, source_target_pairs={{0,4},{4,0},{8,12},{12,8},{16,20},{20,16},{24,28},{28,24},{1,5},{5... | collective-permute-start | bytes 331784 | tf_op jit(solution)/shard_map/ppermute | solution.py:215
  30.0 0.0 collective-permute-done.13
  30.1 0.0 collective-permute-done.14
  30.1 2.6 %collective-permute-start.16 = (bf16[256,128]{1,0:T(8,128)(2,1)S(1)}, bf16[256,128]{1,0:T(8,128)(2,1)S(1)}, u32[]{:S(2)}, u32[]{:S(2)}) collective-permute-start(bf16[256,128]{1,0:T(8,128)(2,1)S(1)} %add_convert_fusion.3), channel_id=1, source_target_pairs={{0,16},{4,20},{8,24},{12,28},{16,0},{20,4},{24,8},{28,12},{1,17},{... | collective-permute-start | bytes 196616 | tf_op jit(solution)/shard_map/ppermute | solution.py:215
  32.7 0.7 %collective-permute-start.19 = (bf16[10,64,128]{2,1,0:T(8,128)(2,1)S(1)}, bf16[10,64,128]{2,1,0:T(8,128)(2,1)S(1)}, u32[]{:S(2)}, u32[]{:S(2)}) collective-permute-start(bf16[10,64,128]{2,1,0:T(8,128)(2,1)S(1)} %get-tuple-element.56.own), channel_id=1, source_target_pairs={{4,8},{8,4},{12,16},{16,12},{20,24},{24,20},{5,9},{9,5},{13,17},{1... | collective-permute-start | bytes 491528 | tf_op jit(solution)/shard_map/ppermute | solution.py:235
  33.3 3.9 %collective-permute-start.18 = (bf16[10,64,128]{2,1,0:T(8,128)(2,1)S(1)}, bf16[10,64,128]{2,1,0:T(8,128)(2,1)S(1)}, u32[]{:S(2)}, u32[]{:S(2)}) collective-permute-start(bf16[10,64,128]{2,1,0:T(8,128)(2,1)S(1)} %get-tuple-element.56.own), channel_id=1, source_target_pairs={{0,4},{4,0},{8,12},{12,8},{16,20},{20,16},{24,28},{28,24},{1,5},{5... | collective-permute-start | bytes 491528 | tf_op jit(solution)/shard_map/ppermute | solution.py:215
  37.3 0.0 collective-permute-done.11
  37.3 1.5 %collective-permute-start.12 = (bf16[432,128]{1,0:T(8,128)(2,1)S(1)}, bf16[432,128]{1,0:T(8,128)(2,1)S(1)}, u32[]{:S(2)}, u32[]{:S(2)}) collective-permute-start(bf16[432,128]{1,0:T(8,128)(2,1)S(1)} %add_convert_fusion.1), channel_id=1, source_target_pairs={{0,16},{4,20},{8,24},{12,28},{16,0},{20,4},{24,8},{28,12},{1,17},{... | collective-permute-start | bytes 331784 | tf_op jit(solution)/shard_map/ppermute | solution.py:215
  38.8 0.0 collective-permute-done.16
  38.9 0.1 collective-permute-start.17
  38.9 4.3 %collective-permute-done.17 = bf16[256,128]{1,0:T(8,128)(2,1)S(1)} collective-permute-done((bf16[256,128]{1,0:T(8,128)(2,1)S(1)}, bf16[256,128]{1,0:T(8,128)(2,1)S(1)}, u32[]{:S(2)}, u32[]{:S(2)}) %collective-permute-start.17) | collective-permute-done | bytes 65568 | tf_op jit(solution)/shard_map/ppermute | solution.py:215
  43.2 0.0 collective-permute-done.19.odd
  43.2 0.0 collective-permute-done.18.even
  43.2 2.9 %collective-permute-done.12 = bf16[432,128]{1,0:T(8,128)(2,1)S(1)} collective-permute-done((bf16[432,128]{1,0:T(8,128)(2,1)S(1)}, bf16[432,128]{1,0:T(8,128)(2,1)S(1)}, u32[]{:S(2)}, u32[]{:S(2)}) %collective-permute-start.12) | collective-permute-done | bytes 110624 | tf_op jit(solution)/shard_map/ppermute | solution.py:215
  46.2 0.1 collective-permute-start.20
  46.3 1.7 %shard_map.89 = bf16[8,64,128]{2,1,0:T(8,128)(2,1)} custom-call(bf16[10,64,128]{2,1,0:T(8,128)(2,1)S(1)} %collective-permute-done.18.even, bf16[10,64,128]{2,1,0:T(8,128)(2,1)S(1)} %get-tuple-element.56.own, bf16[10,64,128]{2,1,0:T(8,128)(2,1)S(1)} %collective-permute-done.19.odd, bf16[3,3,3,128,128]{4,3,2,1,0:T(8,128)(2,1)S(1)} %copy-done.1), custom_call_target="tpu_custom_call" | custom-call | tf_op jit(solution)/shard_map/pallas_call | solution.py:16
  48.0 2.9 %collective-permute-done.20 = bf16[432,128]{1,0:T(8,128)(2,1)S(1)} collective-permute-done((bf16[432,128]{1,0:T(8,128)(2,1)S(1)}, bf16[432,128]{1,0:T(8,128)(2,1)S(1)}, u32[]{:S(2)}, u32[]{:S(2)}) %collective-permute-start.20) | collective-permute-done | bytes 110624 | tf_op jit(solution)/shard_map/ppermute | solution.py:215
  51.1 0.1 collective-permute-start.26
  51.2 2.9 %collective-permute-start.24 = (bf16[688,128]{1,0:T(8,128)(2,1)S(1)}, bf16[688,128]{1,0:T(8,128)(2,1)S(1)}, u32[]{:S(2)}, u32[]{:S(2)}) collective-permute-start(bf16[688,128]{1,0:T(8,128)(2,1)S(1)} %pad_maximum_fusion.refs_0_), channel_id=1, source_target_pairs={{0,4},{4,0},{8,12},{12,8},{16,20},{20,16},{24,28},{28,24},{1,5},{5... | collective-permute-start | bytes 528392 | tf_op jit(solution)/shard_map/ppermute | solution.py:215
  54.1 0.5 collective-permute-start.22
  54.6 0.0 collective-permute-start.21
  54.6 3.0 %collective-permute-done.26.refs_6_ = bf16[688,128]{1,0:T(8,128)(2,1)S(1)} collective-permute-done((bf16[688,128]{1,0:T(8,128)(2,1)S(1)}, bf16[688,128]{1,0:T(8,128)(2,1)S(1)}, u32[]{:S(2)}, u32[]{:S(2)}) %collective-permute-start.26) | collective-permute-done | bytes 176160 | tf_op jit(solution)/shard_map/ppermute | solution.py:225
  57.6 1.8 %collective-permute-done.24.refs_4_ = bf16[688,128]{1,0:T(8,128)(2,1)S(1)} collective-permute-done((bf16[688,128]{1,0:T(8,128)(2,1)S(1)}, bf16[688,128]{1,0:T(8,128)(2,1)S(1)}, u32[]{:S(2)}, u32[]{:S(2)}) %collective-permute-start.24) | collective-permute-done | bytes 176160 | tf_op jit(solution)/shard_map/ppermute | solution.py:215
  59.4 0.2 collective-permute-done.22.refs_2_
  59.5 0.3 collective-permute-start.23
  59.9 0.0 collective-permute-done.21.refs_1_
  59.9 0.0 collective-permute-done.27.refs_7_
  59.9 0.9 %collective-permute-done.25.refs_5_ = bf16[688,128]{1,0:T(8,128)(2,1)S(1)} collective-permute-done((bf16[688,128]{1,0:T(8,128)(2,1)S(1)}, bf16[688,128]{1,0:T(8,128)(2,1)S(1)}, u32[]{:S(2)}, u32[]{:S(2)}) %collective-permute-start.25) | collective-permute-done | bytes 176160 | tf_op jit(solution)/shard_map/ppermute | solution.py:215
  60.8 0.3 collective-permute-done.23.refs_3_
  61.0 1.3 %shard_map.90 = (bf16[27,4,2,16,128]{4,3,2,1,0:T(8,128)(2,1)}, bf16[2,4,128,256]{3,2,1,0:T(8,128)(2,1)}) custom-call(bf16[688,128]{1,0:T(8,128)(2,1)S(1)} %pad_maximum_fusion.refs_0_, bf16[688,128]{1,0:T(8,128)(2,1)S(1)} %collective-permute-done.21.refs_1_, bf16[688,128]{1,0:T(8,128)(2,1)S(1)} %collective-permute-done.22.refs_2_, ...), custom_call_target="tpu_custom_call" | custom-call | tf_op jit(solution)/shard_map/pallas_call | solution.py:16
  (21 shorter events, 0.3 us)
Async XLA Ops:
  0.6 8.9 %copy-start = (bf16[2,2,2,128,256]{4,3,2,1,0:T(8,128)(2,1)S(1)}, bf16[2,2,2,128,256]{4,3,2,1,0:T(8,128)(2,1)}, u32[]{:S(2)}) copy-start(bf16[2,2,2,128,256]{4,3,2,1,0:T(8,128)(2,1)} %param.9) | copy-start | bytes 1572868
  0.6 1.0 %copy-start.2 = (bf16[4,4,32,32]{3,2,1,0:T(8,128)(2,1)S(1)}, bf16[4,4,32,32]{3,2,1,0:T(8,128)(2,1)}, u32[]{:S(2)}) copy-start(bf16[4,4,32,32]{3,2,1,0:T(8,128)(2,1)} %param.11) | copy-start | bytes 98308
  1.6 4.2 %copy-start.3 = (bf16[1,8,64,128]{3,2,1,0:T(8,128)(2,1)S(1)}, bf16[1,8,64,128]{3,2,1,0:T(8,128)(2,1)}, u32[]{:S(2)}) copy-start(bf16[1,8,64,128]{3,2,1,0:T(8,128)(2,1)} %param.6) | copy-start | bytes 393220
  1.7 6.2 %collective-permute-start.4 = (bf16[2,32,128]{2,1,0:T(8,128)(2,1)S(1)}, bf16[2,32,128]{2,1,0:T(8,128)(2,1)S(1)}, u32[]{:S(2)}, u32[]{:S(2)}) collective-permute-start(bf16[2,32,128]{2,1,0:T(8,128)(2,1)S(1)} %get-tuple-element.39), channel_id=1, source_target_pairs={{0,16},{4,20},{8,24},{12,28},{16,0},{20,4},{24,8},{28,12},{1,17},{... | collective-permute-start | bytes 49160 | tf_op jit(solution)/shard_map/ppermute | solution.py:215
  5.9 7.3 %collective-permute-start = (bf16[32,512]{1,0:T(8,128)(2,1)S(1)}, bf16[32,512]{1,0:T(8,128)(2,1)S(1)}, u32[]{:S(2)}, u32[]{:S(2)}) collective-permute-start(bf16[32,512]{1,0:T(8,128)(2,1)S(1)} %get-tuple-element.35), channel_id=1, source_target_pairs={{0,1},{1,0},{2,3},{3,2},{4,5},{5,4},{6,7},{7,6},{8,9},{9,8},{10,11... | collective-permute-start | bytes 98312 | tf_op jit(solution)/shard_map/ppermute | solution.py:215
  6.0 7.2 %collective-permute-start.1 = (bf16[32,512]{1,0:T(8,128)(2,1)S(1)}, bf16[32,512]{1,0:T(8,128)(2,1)S(1)}, u32[]{:S(2)}, u32[]{:S(2)}) collective-permute-start(bf16[32,512]{1,0:T(8,128)(2,1)S(1)} %get-tuple-element.36), channel_id=1, source_target_pairs={{0,2},{1,3},{2,0},{3,1},{4,6},{5,7},{6,4},{7,5},{8,10},{9,11},{10,... | collective-permute-start | bytes 98312 | tf_op jit(solution)/shard_map/ppermute | solution.py:215
  7.6 5.7 %collective-permute-start.2 = (bf16[32,512]{1,0:T(8,128)(2,1)S(1)}, bf16[32,512]{1,0:T(8,128)(2,1)S(1)}, u32[]{:S(2)}, u32[]{:S(2)}) collective-permute-start(bf16[32,512]{1,0:T(8,128)(2,1)S(1)} %get-tuple-element.37), channel_id=1, source_target_pairs={{0,3},{1,2},{2,1},{3,0},{4,7},{5,6},{6,5},{7,4},{8,11},{9,10},{10,... | collective-permute-start | bytes 98312 | tf_op jit(solution)/shard_map/ppermute | solution.py:215
  7.9 3.8 %collective-permute-start.5 = (bf16[1,2,32,128]{3,2,1,0:T(8,128)(2,1)S(1)}, bf16[1,2,32,128]{3,2,1,0:T(8,128)(2,1)S(1)}, u32[]{:S(2)}, u32[]{:S(2)}) collective-permute-start(bf16[1,2,32,128]{3,2,1,0:T(8,128)(2,1)S(1)} %get-tuple-element.66), channel_id=1, source_target_pairs={{0,8},{4,12},{8,0},{12,4},{16,24},{20,28},{24,16},{28,20},{1,9},{5... | collective-permute-start | bytes 49160 | tf_op jit(solution)/shard_map/ppermute | solution.py:215
  11.7 3.9 %collective-permute-start.6 = (bf16[4,32,128]{2,1,0:T(8,128)(2,1)S(1)}, bf16[4,32,128]{2,1,0:T(8,128)(2,1)S(1)}, u32[]{:S(2)}, u32[]{:S(2)}) collective-permute-start(bf16[4,32,128]{2,1,0:T(8,128)(2,1)S(1)} %maximum_bitcast_fusion.refs_3_), channel_id=1, source_target_pairs={{0,4},{4,0},{8,12},{12,8},{16,20},{20,16},{24,28},{28,24},{1,5},{5... | collective-permute-start | bytes 98312 | tf_op jit(solution)/shard_map/ppermute | solution.py:215
  13.2 2.4 %copy-start.4 = (bf16[1,8,64,128]{3,2,1,0:T(8,128)(2,1)S(1)}, bf16[1,8,64,128]{3,2,1,0:T(8,128)(2,1)}, u32[]{:S(2)}) copy-start(bf16[1,8,64,128]{3,2,1,0:T(8,128)(2,1)} %param.7) | copy-start | bytes 393220
  13.2 2.4 %copy-start.5 = (bf16[1,8,64,128]{3,2,1,0:T(8,128)(2,1)S(1)}, bf16[1,8,64,128]{3,2,1,0:T(8,128)(2,1)}, u32[]{:S(2)}) copy-start(bf16[1,8,64,128]{3,2,1,0:T(8,128)(2,1)} %param.10) | copy-start | bytes 393220
  16.2 3.5 %collective-permute-start.7 = (bf16[512,128]{1,0:T(8,128)(2,1)S(1)}, bf16[512,128]{1,0:T(8,128)(2,1)S(1)}, u32[]{:S(2)}, u32[]{:S(2)}) collective-permute-start(bf16[512,128]{1,0:T(8,128)(2,1)S(1)} %get-tuple-element.46.refs_3_), channel_id=1, source_target_pairs={{0,1},{1,0},{2,3},{3,2},{4,5},{5,4},{6,7},{7,6},{8,9},{9,8},{10,11... | collective-permute-start | bytes 393224 | tf_op jit(solution)/shard_map/ppermute | solution.py:215
  16.3 5.9 %collective-permute-start.3 = (bf16[4,32,512]{2,1,0:T(8,128)(2,1)S(1)}, bf16[4,32,512]{2,1,0:T(8,128)(2,1)S(1)}, u32[]{:S(2)}, u32[]{:S(2)}) collective-permute-start(bf16[4,32,512]{2,1,0:T(8,128)(2,1)S(1)} %pad_maximum_fusion.1.refs_1_), channel_id=1, source_target_pairs={{0,4},{4,0},{8,12},{12,8},{16,20},{20,16},{24,28},{28,24},{1,5},{5... | collective-permute-start | bytes 393224 | tf_op jit(solution)/shard_map/ppermute | solution.py:215
  17.9 5.8 %collective-permute-start.10 = (bf16[512,128]{1,0:T(8,128)(2,1)S(1)}, bf16[512,128]{1,0:T(8,128)(2,1)S(1)}, u32[]{:S(2)}, u32[]{:S(2)}) collective-permute-start(bf16[512,128]{1,0:T(8,128)(2,1)S(1)} %get-tuple-element.46.refs_3_), channel_id=1, source_target_pairs={{0,3},{1,2},{2,1},{3,0},{4,7},{5,6},{6,5},{7,4},{8,11},{9,10},{10,... | collective-permute-start | bytes 393224 | tf_op jit(solution)/shard_map/ppermute | solution.py:215
  19.2 7.7 %collective-permute-start.9 = (bf16[512,128]{1,0:T(8,128)(2,1)S(1)}, bf16[512,128]{1,0:T(8,128)(2,1)S(1)}, u32[]{:S(2)}, u32[]{:S(2)}) collective-permute-start(bf16[512,128]{1,0:T(8,128)(2,1)S(1)} %get-tuple-element.46.refs_3_), channel_id=1, source_target_pairs={{0,2},{1,3},{2,0},{3,1},{4,6},{5,7},{6,4},{7,5},{8,10},{9,11},{10,... | collective-permute-start | bytes 393224 | tf_op jit(solution)/shard_map/ppermute | solution.py:215
  19.7 7.1 %collective-permute-start.8 = (bf16[4,32,512]{2,1,0:T(8,128)(2,1)S(1)}, bf16[4,32,512]{2,1,0:T(8,128)(2,1)S(1)}, u32[]{:S(2)}, u32[]{:S(2)}) collective-permute-start(bf16[4,32,512]{2,1,0:T(8,128)(2,1)S(1)} %pad_maximum_fusion.1.refs_1_), channel_id=1, source_target_pairs={{4,8},{8,4},{12,16},{16,12},{20,24},{24,20},{5,9},{9,5},{13,17},{1... | collective-permute-start | bytes 393224 | tf_op jit(solution)/shard_map/ppermute | solution.py:235
  22.2 7.8 %collective-permute-start.13 = (bf16[256,128]{1,0:T(8,128)(2,1)S(1)}, bf16[256,128]{1,0:T(8,128)(2,1)S(1)}, u32[]{:S(2)}, u32[]{:S(2)}) collective-permute-start(bf16[256,128]{1,0:T(8,128)(2,1)S(1)} %get-tuple-element.53), channel_id=1, source_target_pairs={{0,1},{1,0},{2,3},{3,2},{4,5},{5,4},{6,7},{7,6},{8,9},{9,8},{10,11... | collective-permute-start | bytes 196616 | tf_op jit(solution)/shard_map/ppermute | solution.py:215
  22.2 7.8 %collective-permute-start.14 = (bf16[256,128]{1,0:T(8,128)(2,1)S(1)}, bf16[256,128]{1,0:T(8,128)(2,1)S(1)}, u32[]{:S(2)}, u32[]{:S(2)}) collective-permute-start(bf16[256,128]{1,0:T(8,128)(2,1)S(1)} %get-tuple-element.54), channel_id=1, source_target_pairs={{0,2},{1,3},{2,0},{3,1},{4,6},{5,7},{6,4},{7,5},{8,10},{9,11},{10,... | collective-permute-start | bytes 196616 | tf_op jit(solution)/shard_map/ppermute | solution.py:215
  23.7 6.3 %collective-permute-start.15 = (bf16[256,128]{1,0:T(8,128)(2,1)S(1)}, bf16[256,128]{1,0:T(8,128)(2,1)S(1)}, u32[]{:S(2)}, u32[]{:S(2)}) collective-permute-start(bf16[256,128]{1,0:T(8,128)(2,1)S(1)} %get-tuple-element.55), channel_id=1, source_target_pairs={{0,3},{1,2},{2,1},{3,0},{4,7},{5,6},{6,5},{7,4},{8,11},{9,10},{10,... | collective-permute-start | bytes 196616 | tf_op jit(solution)/shard_map/ppermute | solution.py:215
  28.3 17.9 %copy-start.1 = (bf16[3,3,3,128,128]{4,3,2,1,0:T(8,128)(2,1)S(1)}, bf16[3,3,3,128,128]{4,3,2,1,0:T(8,128)(2,1)}, u32[]{:S(2)}) copy-start(bf16[3,3,3,128,128]{4,3,2,1,0:T(8,128)(2,1)} %weight.1) | copy-start | bytes 2654212
  28.4 8.9 %collective-permute-start.11 = (bf16[432,128]{1,0:T(8,128)(2,1)S(1)}, bf16[432,128]{1,0:T(8,128)(2,1)S(1)}, u32[]{:S(2)}, u32[]{:S(2)}) collective-permute-start(bf16[432,128]{1,0:T(8,128)(2,1)S(1)} %get-tuple-element.51), channel_id=1, source_target_pairs={{0,4},{4,0},{8,12},{12,8},{16,20},{20,16},{24,28},{28,24},{1,5},{5... | collective-permute-start | bytes 331784 | tf_op jit(solution)/shard_map/ppermute | solution.py:215
  30.1 8.7 %collective-permute-start.16 = (bf16[256,128]{1,0:T(8,128)(2,1)S(1)}, bf16[256,128]{1,0:T(8,128)(2,1)S(1)}, u32[]{:S(2)}, u32[]{:S(2)}) collective-permute-start(bf16[256,128]{1,0:T(8,128)(2,1)S(1)} %add_convert_fusion.3), channel_id=1, source_target_pairs={{0,16},{4,20},{8,24},{12,28},{16,0},{20,4},{24,8},{28,12},{1,17},{... | collective-permute-start | bytes 196616 | tf_op jit(solution)/shard_map/ppermute | solution.py:215
  32.7 10.5 %collective-permute-start.19 = (bf16[10,64,128]{2,1,0:T(8,128)(2,1)S(1)}, bf16[10,64,128]{2,1,0:T(8,128)(2,1)S(1)}, u32[]{:S(2)}, u32[]{:S(2)}) collective-permute-start(bf16[10,64,128]{2,1,0:T(8,128)(2,1)S(1)} %get-tuple-element.56.own), channel_id=1, source_target_pairs={{4,8},{8,4},{12,16},{16,12},{20,24},{24,20},{5,9},{9,5},{13,17},{1... | collective-permute-start | bytes 491528 | tf_op jit(solution)/shard_map/ppermute | solution.py:235
  33.3 9.9 %collective-permute-start.18 = (bf16[10,64,128]{2,1,0:T(8,128)(2,1)S(1)}, bf16[10,64,128]{2,1,0:T(8,128)(2,1)S(1)}, u32[]{:S(2)}, u32[]{:S(2)}) collective-permute-start(bf16[10,64,128]{2,1,0:T(8,128)(2,1)S(1)} %get-tuple-element.56.own), channel_id=1, source_target_pairs={{0,4},{4,0},{8,12},{12,8},{16,20},{20,16},{24,28},{28,24},{1,5},{5... | collective-permute-start | bytes 491528 | tf_op jit(solution)/shard_map/ppermute | solution.py:215
  37.3 8.8 %collective-permute-start.12 = (bf16[432,128]{1,0:T(8,128)(2,1)S(1)}, bf16[432,128]{1,0:T(8,128)(2,1)S(1)}, u32[]{:S(2)}, u32[]{:S(2)}) collective-permute-start(bf16[432,128]{1,0:T(8,128)(2,1)S(1)} %add_convert_fusion.1), channel_id=1, source_target_pairs={{0,16},{4,20},{8,24},{12,28},{16,0},{20,4},{24,8},{28,12},{1,17},{... | collective-permute-start | bytes 331784 | tf_op jit(solution)/shard_map/ppermute | solution.py:215
  38.9 4.3 %collective-permute-start.17 = (bf16[256,128]{1,0:T(8,128)(2,1)S(1)}, bf16[256,128]{1,0:T(8,128)(2,1)S(1)}, u32[]{:S(2)}, u32[]{:S(2)}) collective-permute-start(bf16[256,128]{1,0:T(8,128)(2,1)S(1)} %add_convert_fusion.2), channel_id=1, source_target_pairs={{0,8},{4,12},{8,0},{12,4},{16,24},{20,28},{24,16},{28,20},{1,9},{5... | collective-permute-start | bytes 196616 | tf_op jit(solution)/shard_map/ppermute | solution.py:215
  46.2 4.8 %collective-permute-start.20 = (bf16[432,128]{1,0:T(8,128)(2,1)S(1)}, bf16[432,128]{1,0:T(8,128)(2,1)S(1)}, u32[]{:S(2)}, u32[]{:S(2)}) collective-permute-start(bf16[432,128]{1,0:T(8,128)(2,1)S(1)} %add_convert_fusion), channel_id=1, source_target_pairs={{0,8},{4,12},{8,0},{12,4},{16,24},{20,28},{24,16},{28,20},{1,9},{5... | collective-permute-start | bytes 331784 | tf_op jit(solution)/shard_map/ppermute | solution.py:215
  51.1 6.5 %collective-permute-start.26 = (bf16[688,128]{1,0:T(8,128)(2,1)S(1)}, bf16[688,128]{1,0:T(8,128)(2,1)S(1)}, u32[]{:S(2)}, u32[]{:S(2)}) collective-permute-start(bf16[688,128]{1,0:T(8,128)(2,1)S(1)} %pad_maximum_fusion.refs_0_), channel_id=1, source_target_pairs={{0,6},{1,7},{2,4},{3,5},{4,2},{5,3},{6,0},{7,1},{8,14},{9,15},{10,... | collective-permute-start | bytes 528392 | tf_op jit(solution)/shard_map/ppermute | solution.py:225
  51.2 8.2 %collective-permute-start.24 = (bf16[688,128]{1,0:T(8,128)(2,1)S(1)}, bf16[688,128]{1,0:T(8,128)(2,1)S(1)}, u32[]{:S(2)}, u32[]{:S(2)}) collective-permute-start(bf16[688,128]{1,0:T(8,128)(2,1)S(1)} %pad_maximum_fusion.refs_0_), channel_id=1, source_target_pairs={{0,4},{4,0},{8,12},{12,8},{16,20},{20,16},{24,28},{28,24},{1,5},{5... | collective-permute-start | bytes 528392 | tf_op jit(solution)/shard_map/ppermute | solution.py:215
  54.1 5.5 %collective-permute-start.22 = (bf16[688,128]{1,0:T(8,128)(2,1)S(1)}, bf16[688,128]{1,0:T(8,128)(2,1)S(1)}, u32[]{:S(2)}, u32[]{:S(2)}) collective-permute-start(bf16[688,128]{1,0:T(8,128)(2,1)S(1)} %pad_maximum_fusion.refs_0_), channel_id=1, source_target_pairs={{0,2},{1,3},{2,0},{3,1},{4,6},{5,7},{6,4},{7,5},{8,10},{9,11},{10,... | collective-permute-start | bytes 528392 | tf_op jit(solution)/shard_map/ppermute | solution.py:215
  54.6 5.3 %collective-permute-start.21 = (bf16[688,128]{1,0:T(8,128)(2,1)S(1)}, bf16[688,128]{1,0:T(8,128)(2,1)S(1)}, u32[]{:S(2)}, u32[]{:S(2)}) collective-permute-start(bf16[688,128]{1,0:T(8,128)(2,1)S(1)} %pad_maximum_fusion.refs_0_), channel_id=1, source_target_pairs={{0,1},{1,0},{2,3},{3,2},{4,5},{5,4},{6,7},{7,6},{8,9},{9,8},{10,11... | collective-permute-start | bytes 528392 | tf_op jit(solution)/shard_map/ppermute | solution.py:215
  57.6 2.3 %collective-permute-start.27 = (bf16[688,128]{1,0:T(8,128)(2,1)S(1)}, bf16[688,128]{1,0:T(8,128)(2,1)S(1)}, u32[]{:S(2)}, u32[]{:S(2)}) collective-permute-start(bf16[688,128]{1,0:T(8,128)(2,1)S(1)} %collective-permute-done.26.refs_6_), channel_id=1, source_target_pairs={{0,1},{1,0},{2,3},{3,2},{4,5},{5,4},{6,7},{7,6},{8,9},{9,8},{10,11... | collective-permute-start | bytes 528392 | tf_op jit(solution)/shard_map/ppermute | solution.py:215
  59.4 1.4 %collective-permute-start.25 = (bf16[688,128]{1,0:T(8,128)(2,1)S(1)}, bf16[688,128]{1,0:T(8,128)(2,1)S(1)}, u32[]{:S(2)}, u32[]{:S(2)}) collective-permute-start(bf16[688,128]{1,0:T(8,128)(2,1)S(1)} %collective-permute-done.24.refs_4_), channel_id=1, source_target_pairs={{0,1},{1,0},{2,3},{3,2},{4,5},{5,4},{6,7},{7,6},{8,9},{9,8},{10,11... | collective-permute-start | bytes 528392 | tf_op jit(solution)/shard_map/ppermute | solution.py:215
  59.5 1.5 %collective-permute-start.23 = (bf16[688,128]{1,0:T(8,128)(2,1)S(1)}, bf16[688,128]{1,0:T(8,128)(2,1)S(1)}, u32[]{:S(2)}, u32[]{:S(2)}) collective-permute-start(bf16[688,128]{1,0:T(8,128)(2,1)S(1)} %collective-permute-done.22.refs_2_), channel_id=1, source_target_pairs={{0,1},{1,0},{2,3},{3,2},{4,5},{5,4},{6,7},{7,6},{8,9},{9,8},{10,11... | collective-permute-start | bytes 528392 | tf_op jit(solution)/shard_map/ppermute | solution.py:215
